TPU v7x, 32 devices: a whole 2x2x4 slice. The times are simulated.
32 devices in a mesh: rep: 4 (over z), fsdp: 8 (over y, x, core).
Axes of the slice: x: 2, y: 2, z: 4, core: 2. Of those that a mesh axis runs over, the one named last changes fastest.
Arguments:
- tokens: bfloat16 [4, 2048, 12288], P('rep', 'fsdp'), may hold values from -8 to 8, as said below
- cotangent: bfloat16 [4, 2048, 1024], P('rep', 'fsdp'), may hold values from -1 to 1, as said below
- weights: float32 [4, 12288, 1024], P('rep', 'fsdp'), may hold values from -0.0546875 to 0.0546875
- first_moment: float32 [4, 12288, 1024], P('rep', 'fsdp'), may hold values from -0.00390625 to 0.00390625
- second_moment: float32 [4, 12288, 1024], P('rep', 'fsdp'), may hold values from 3.973643e-08 to 7.947286e-07
- anchor: float32 [12288, 1024], P(('fsdp', 'rep')), may hold values from -0.0546875 to 0.0546875
- momentum: float32 [12288, 1024], P(('fsdp', 'rep')), may hold values from -0.15625 to 0.15625
- due_fragment: int32 [1], replicated, may hold values from 0 to 7
- step_count: int32 [1], replicated, may hold values from 1 to 100000
Outputs:
- weights_out: float32 [4, 12288, 1024], P('rep', 'fsdp')
- first_out: float32 [4, 12288, 1024], P('rep', 'fsdp')
- second_out: float32 [4, 12288, 1024], P('rep', 'fsdp')
- anchor_out: float32 [12288, 1024], P(('fsdp', 'rep'))
- momentum_out: float32 [12288, 1024], P(('fsdp', 'rep'))
- plan_out: float32 [1], replicated
Inputs may be any that keep to these rules, and one draw needn't show every extreme that they name: `tokens`: activations of order one. `cotangent`: each replica's entries carry a scale of its own.
All inputs are finite; a program needn't handle non-finite values.
Results may differ from a plain program's by a relative error of at most 0.0009.
Values may be sent and summed in bfloat16 or wider, within the bound.
No kernel may reach another device: no remote copies, remote signals or barrier semaphores. Data moves between devices by JAX's collectives and lax.ppermute only.
A program may use at most 192 MiB of HBM per device.

v0:
```python
import jax
import jax.numpy as jnp
from jax import lax
from jax.sharding import PartitionSpec as P

HEAD = 128
WARMUP = 2000
STEPS_TOTAL = 100000
FRAG_COLS = 128


BETA_ONE = 0.9
BETA_TWO = 0.95
ADAM_EPS = 1e-08
DECAY = 0.1
PEAK_RATE = 0.0003
CLIP_NORM = 1.0
OUTER_MU = 0.9
OUTER_RATE = 0.7
MIX_LOCAL = 0.5


def key_backward(raw_keys, incoming):
    count = raw_keys.shape[0]
    heads = raw_keys.reshape(count, -1, HEAD)
    inverse = lax.rsqrt(jnp.mean(heads * heads, axis=2, keepdims=True) + 1e-06)
    normed = heads * inverse
    upper = incoming.astype(jnp.float32).reshape(heads.shape)
    back = inverse * (upper - normed * jnp.mean(upper * normed, axis=2, keepdims=True))
    return back.reshape(count, -1).astype(jnp.bfloat16)


def token_columns(inputs):
    return lax.all_to_all(inputs, "fsdp", split_axis=1, concat_axis=0, tiled=True)


def nesterov(anchor_cols, moment_cols, mean_inner):
    pseudo = anchor_cols - mean_inner
    new_moment = OUTER_MU * moment_cols + pseudo
    new_anchor = anchor_cols - OUTER_RATE * (OUTER_MU * new_moment + pseudo)
    return (new_anchor, new_moment)


def body(
    tokens,
    cotangent,
    weights,
    first_moment,
    second_moment,
    anchor,
    momentum,
    due_fragment,
    step_count,
):
    inputs = tokens[0]
    incoming = cotangent[0]
    params = weights[0]
    tok_rows = inputs.shape[0]
    kv_width = incoming.shape[1] // 2
    replicas = lax.axis_size("rep")
    key_weights = params[:, :kv_width].astype(jnp.bfloat16)
    columns = None
    picked = inputs
    raw_keys = jnp.dot(
        picked,
        lax.all_gather(key_weights, "fsdp", axis=0, tiled=True),
        preferred_element_type=jnp.float32,
    )
    upstream = jnp.concatenate(
        [key_backward(raw_keys, incoming[:, :kv_width]), incoming[:, kv_width:]], axis=1
    )
    columns = token_columns(inputs)
    piece = lax.all_gather(upstream, "fsdp", axis=0, tiled=True)
    blocks = piece.shape[0] // tok_rows

    def one_block(index, carried):
        first = index * tok_rows
        picked = lax.dynamic_slice_in_dim(columns, first, tok_rows, 0)
        shaped = lax.dynamic_slice_in_dim(piece, first, tok_rows, 0)
        partial_sum = lax.dot_general(
            picked, shaped, (((0,), (0,)), ((), ())), preferred_element_type=jnp.float32
        )
        partial_sum = lax.optimization_barrier(partial_sum.astype(jnp.bfloat16))
        return carried + partial_sum.astype(jnp.float32)

    gradient = lax.fori_loop(
        0, blocks, one_block, jnp.zeros((params.shape[0], 2 * kv_width), jnp.float32)
    )
    square = lax.psum(jnp.sum(gradient * gradient), "fsdp")
    factor = jnp.minimum(1.0, CLIP_NORM / (jnp.sqrt(square) + 1e-06))
    clipped = gradient * factor
    steps_now = step_count[0].astype(jnp.float32)
    plan = jnp.minimum(1.0, steps_now / WARMUP) * (
        0.55 + 0.45 * jnp.cos(jnp.pi * steps_now / STEPS_TOTAL)
    )
    rate = PEAK_RATE * plan
    first_out = BETA_ONE * first_moment[0] + (1.0 - BETA_ONE) * clipped
    second_out = BETA_TWO * second_moment[0] + (1.0 - BETA_TWO) * clipped * clipped
    correct_one = 1.0 - jnp.power(BETA_ONE, steps_now)
    correct_two = 1.0 - jnp.power(BETA_TWO, steps_now)
    inner = params - rate * (
        first_out / correct_one / (jnp.sqrt(second_out / correct_two) + ADAM_EPS) + DECAY * params
    )
    offset = due_fragment[0] * FRAG_COLS
    own_cols = lax.dynamic_slice_in_dim(inner, offset, FRAG_COLS, 1)
    anchor_cols = lax.dynamic_slice_in_dim(anchor, offset, FRAG_COLS, 1)
    moment_cols = lax.dynamic_slice_in_dim(momentum, offset, FRAG_COLS, 1)
    summed = lax.psum_scatter(own_cols, "rep", scatter_dimension=0, tiled=True)
    new_anchor, new_moment = nesterov(anchor_cols, moment_cols, summed / replicas)
    fresh = lax.all_gather(new_anchor, "rep", axis=0, tiled=True)
    mixed = MIX_LOCAL * own_cols + (1.0 - MIX_LOCAL) * fresh
    weights_out = lax.dynamic_update_slice_in_dim(inner, mixed, offset, 1)
    anchor_out = lax.dynamic_update_slice_in_dim(anchor, new_anchor, offset, 1)
    momentum_out = lax.dynamic_update_slice_in_dim(momentum, new_moment, offset, 1)
    plan_out = jnp.reshape(plan, (1,))
    return (
        weights_out[None],
        first_out[None],
        second_out[None],
        anchor_out,
        momentum_out,
        plan_out,
    )


def solution(mesh):
    return jax.shard_map(
        body,
        mesh=mesh,
        in_specs=(
            P("rep", "fsdp", None),
            P("rep", "fsdp", None),
            P("rep", "fsdp", None),
            P("rep", "fsdp", None),
            P("rep", "fsdp", None),
            P(("fsdp", "rep"), None),
            P(("fsdp", "rep"), None),
            P(),
            P(),
        ),
        out_specs=(
            P("rep", "fsdp", None),
            P("rep", "fsdp", None),
            P("rep", "fsdp", None),
            P(("fsdp", "rep"), None),
            P(("fsdp", "rep"), None),
            P(),
        ),
        check_vma=False,
    )
```

profile of v0, /device:TPU:0, one launch (start us, length us, event | category | flops | bytes accessed | tf_op | source)
XLA Modules:
  0.0 361.9 jit_solution(17561571518181758148)
XLA Ops:
  7.2 0.0 all-gather.3.cloned.1.call-start
  7.2 3.3 slice.18
  10.5 0.0 all-gather.3.cloned.1.call-update
  10.5 0.0 all-gather.5.cloned.1.call-start
  10.6 0.1 slice_convert_fusion.1
  10.7 0.2 copy.17
  10.9 74.7 %all-gather.3.cloned.1.call-done = bf16[12288,512]{1,0:T(8,128)(2,1)} async-done(((bf16[1536,512]{1,0:T(8,128)(2,1)}), bf16[12288,512]{1,0:T(8,128)(2,1)}) %all-gather.3.cloned.1.call-update) | async-done | bytes 12582928 | tf_op jit(solution)/shard_map/all_gather | solution.py:66
  85.5 16.8 %copy.16 = bf16[512,12288]{1,0:T(8,128)(2,1)} copy(bf16[512,12288]{0,1:T(8,128)(2,1)} %bitcast.47) | data formatting | bytes 25165824 | tf_op jit(solution)/shard_map/dot_general | solution.py:64
  102.3 8.3 %multiply_reduce_fusion.2 = (f32[256,4]{0,1:T(4,128)S(1)}, f32[256,4,128]{0,2,1:T(8,128)S(1)}) fusion(bf16[4,128,12288]{2,1,0:T(8,128)(2,1)} %bitcast.48, bf16[1,256,12288]{2,1,0:T(8,128)(2,1)} %param.11), kind=kOutput, calls=%fused_computation.19 | convolution fusion | flops 3221486592 | bytes 19402752 | tf_op jit(solution)/shard_map/dot_general | solution.py:64
  110.6 0.1 multiply_reduce_fusion.1
  110.7 0.1 multiply_convert_fusion
  110.8 0.1 copy.18
  111.0 0.9 pad_maximum_fusion
  111.8 0.0 all-gather.5.cloned.1.call-update
  111.9 5.4 %copy.19 = bf16[32,8,8,1536]{3,2,1,0:T(8,128)(2,1)S(1)} copy(bf16[32,8,8,1536]{3,1,2,0:T(8,128)(2,1)} %bitcast.50) | data formatting | bytes 12582912
  117.3 4.8 %copy.15 = bf16[256,8,1536]{2,0,1:T(8,128)(2,1)} copy(bf16[256,8,1536]{2,1,0:T(8,128)(2,1)S(1)} %bitcast.46) | data formatting | bytes 12582912 | tf_op jit(solution)/shard_map/all_to_all | solution.py:34
  122.1 4.7 %all-to-all-start = ((bf16[256,8,1536]{2,0,1:T(8,128)(2,1)}), bf16[256,8,1536]{2,0,1:T(8,128)(2,1)}, u32[]{:S(2)}, u32[]{:S(2)}) async-start(bf16[256,8,1536]{2,0,1:T(8,128)(2,1)} %copy.15), calls=%async_computation | async-start | bytes 12582912 | tf_op jit(solution)/shard_map/all_to_all | solution.py:34
  126.8 0.2 reduce-scatter.2.cloned.1.call-start
  128.5 81.1 %all-to-all-done = bf16[256,8,1536]{2,0,1:T(8,128)(2,1)} async-done(((bf16[256,8,1536]{2,0,1:T(8,128)(2,1)}), bf16[256,8,1536]{2,0,1:T(8,128)(2,1)}, u32[]{:S(2)}, u32[]{:S(2)}) %all-to-all-start) | async-done | bytes 6291488 | tf_op jit(solution)/shard_map/all_to_all | solution.py:34
  209.6 64.2 %while.14 = (s32[]{:T(128)}, f32[1536,1024]{1,0:T(8,128)}, bf16[2048,1536]{1,0:T(8,128)(2,1)}, bf16[2048,1024]{1,0:T(8,128)(2,1)}, s32[]{:T(128)}, /*index=5*/s32[]{:T(128)}, s32[]{:T(128)}, s32[]{:T(128)}) while((s32[]{:T(128)}, f32[1536,1024]{1,0:T(8,128)}, bf16[2048,1536]{1,0:T(8,128)(2,1)}, bf16[2048,1024]{1,0:T(8,128)(2,1)}, ...), condition=%wide.region_3.0_spmd.clone, body=%wide.region_2.0_spmd.clone.sunk | while | flops 811597824 | bytes 70517960 | solution.py:86
  209.6 2.4 convolution_convert_fusion.2
  212.1 0.7 copy-done
  212.8 2.1 select_add_fusion.2
  215.0 2.7 copy-done.1
  217.7 2.4 convolution_convert_fusion.2
  220.1 0.7 copy-done
  220.8 2.1 select_add_fusion.2
  223.0 2.7 copy-done.1
  225.7 2.4 convolution_convert_fusion.2
  228.1 0.7 copy-done
  228.9 2.1 select_add_fusion.2
  231.0 2.7 copy-done.1
  233.7 2.4 convolution_convert_fusion.2
  236.2 0.7 copy-done
  236.9 2.1 select_add_fusion.2
  239.1 2.7 copy-done.1
  241.8 2.4 convolution_convert_fusion.2
  244.2 0.7 copy-done
  244.9 2.1 select_add_fusion.2
  247.1 2.7 copy-done.1
  249.8 2.4 convolution_convert_fusion.2
  252.2 0.7 copy-done
  253.0 2.1 select_add_fusion.2
  255.1 2.7 copy-done.1
  257.8 2.4 convolution_convert_fusion.2
  260.3 0.7 copy-done
  261.0 2.1 select_add_fusion.2
  263.2 2.7 copy-done.1
  265.8 2.4 convolution_convert_fusion.2
  268.3 0.7 copy-done
  269.0 2.1 select_add_fusion.2
  271.2 2.7 copy-done.1
  273.9 5.0 %multiply_reduce_fusion = f32[]{:T(128)} fusion(f32[1536,1024]{1,0:T(8,128)} %get-tuple-element.85), kind=kLoop, calls=%fused_computation.11 | loop fusion | flops 3145727 | bytes 6291460 | tf_op jit(solution)/shard_map/reduce_sum | solution.py:89
  278.9 12.4 %psum.7 = f32[]{:T(128)} all-reduce(f32[]{:T(128)} %multiply_reduce_fusion), channel_id=1, replica_groups=mesh['rep'=4,'fsdp'=8] {'fsdp'}, use_global_device_ids=true, to_apply=%region_5.0 | all-reduce | flops 1 | bytes 8 | tf_op jit(solution)/shard_map/psum | solution.py:89
  292.0 13.7 %fusion.7 = (f32[1,1536,1024]{2,1,0:T(8,128)}, f32[1536,1024]{1,0:T(8,128)S(1)}, f32[1,1536,1024]{2,1,0:T(8,128)}) fusion(f32[1536,1024]{1,0:T(8,128)} %get-tuple-element.85, f32[]{:T(128)S(6)} %min.11, f32[1,1536,1024]{2,1,0:T(8,128)} %param.15, f32[]{:T(128)} %bitcast.14, f32[]{:T(128)} %bitcast.12, f32[1,1536,1024]{2,1,0:T(8,128)} %param.14, f32[]{:T(128)} %bitcast.1, ...), kind=kLoop, calls=%fused_computation.14 | loop fusion | flops 25165824 | bytes 44040208 | tf_op jit(solution)/shard_map/broadcast_in_dim | solution.py:119
  305.8 2.7 copy-done.2
  308.4 1.0 constant_dynamic-slice_fusion
  309.4 0.0 reduce-scatter.2.cloned.1.call-update
  309.5 6.8 %copy.28 = f32[1,1536,1024]{2,1,0:T(8,128)} copy(f32[1,1536,1024]{2,1,0:T(8,128)} %bitcast.45) | data formatting | bytes 12582912
  316.2 16.8 %reduce-scatter.2.cloned.1.call-done = f32[384,128]{1,0:T(8,128)} async-done(((f32[1536,128]{1,0:T(8,128)}), f32[384,128]{1,0:T(8,128)}) %reduce-scatter.2.cloned.1.call-update) | async-done | bytes 196624 | tf_op jit(solution)/shard_map/reduce_scatter | solution.py:108
  333.1 1.0 constant_dynamic-update-slice_fusion
  334.1 0.0 copy-start.3
  334.1 18.0 %all_gather.11 = f32[1536,128]{1,0:T(8,128)S(1)} all-gather(f32[384,128]{1,0:T(8,128)S(1)} %get-tuple-element.110), channel_id=1, replica_groups=mesh['rep'=4,'fsdp'=8] {'rep'}, dimensions={0}, use_global_device_ids=true | all-gather | bytes 983040 | tf_op jit(solution)/shard_map/all_gather | solution.py:110
  352.1 2.1 bitcast_dynamic-update-slice_fusion
  (30 shorter events, 0.1 us)
Async XLA Ops:
  7.2 3.4 copy-start.7
  7.2 78.3 %all-gather.3.cloned.1.call-start = ((), (), s32[]{:S(2)}) async-start(), calls=%async_computation.2 | async-start | bytes 14155776 | tf_op jit(solution)/shard_map/all_gather | solution.py:66
  10.5 199.1 %all-gather.5.cloned.1.call-start = ((), (), s32[]{:S(2)}) async-start(), calls=%async_computation.3 | async-start | bytes 4718592 | tf_op jit(solution)/shard_map/all_gather | solution.py:73
  122.1 87.6 %all-to-all-start = ((bf16[256,8,1536]{2,0,1:T(8,128)(2,1)}), bf16[256,8,1536]{2,0,1:T(8,128)(2,1)}, u32[]{:S(2)}, u32[]{:S(2)}) async-start(bf16[256,8,1536]{2,0,1:T(8,128)(2,1)} %copy.15), calls=%async_computation | async-start | bytes 12582912 | tf_op jit(solution)/shard_map/all_to_all | solution.py:34
  126.8 206.2 %reduce-scatter.2.cloned.1.call-start = ((), (), s32[]{:S(2)}) async-start(), calls=%async_computation.4 | async-start | bytes 983040 | tf_op jit(solution)/shard_map/reduce_scatter | solution.py:108
  209.6 3.2 copy-start
  215.0 2.7 copy-start.1
  217.7 3.2 copy-start
  223.0 2.7 copy-start.1
  225.7 3.2 copy-start
  231.0 2.7 copy-start.1
  233.7 3.2 copy-start
  239.1 2.7 copy-start.1
  241.8 3.2 copy-start
  247.1 2.7 copy-start.1
  249.8 3.2 copy-start
  255.1 2.7 copy-start.1
  257.8 3.2 copy-start
  263.1 2.7 copy-start.1
  265.8 3.2 copy-start
  271.2 2.7 copy-start.1
  305.8 2.7 copy-start.2
  309.4 23.6 %copy-start.4 = (f32[384,1024]{1,0:T(8,128)S(1)}, f32[384,1024]{1,0:T(8,128)}, u32[]{:S(2)}) copy-start(f32[384,1024]{1,0:T(8,128)} %param.16) | copy-start | bytes 4718596
  309.4 23.6 %copy-start.6 = (f32[384,1024]{1,0:T(8,128)S(1)}, f32[384,1024]{1,0:T(8,128)}, u32[]{:S(2)}) copy-start(f32[384,1024]{1,0:T(8,128)} %param.17) | copy-start | bytes 4718596
  334.1 20.1 %copy-start.3 = (f32[384,1024]{1,0:T(8,128)}, f32[384,1024]{1,0:T(8,128)S(1)}, u32[]{:S(2)}) copy-start(f32[384,1024]{1,0:T(8,128)S(1)} %get-tuple-element.109) | copy-start | bytes 4718596
  334.1 20.1 %copy-start.5 = (f32[384,1024]{1,0:T(8,128)}, f32[384,1024]{1,0:T(8,128)S(1)}, u32[]{:S(2)}) copy-start(f32[384,1024]{1,0:T(8,128)S(1)} %get-tuple-element.114) | copy-start | bytes 4718596
Sparse Core Ops, SparseCore 0:
  10.6 74.8 all-gather.2
  112.0 48.2 all-gather.4
  309.6 23.4 reduce-scatter.1
where the time goes:
time: 363 us; the launch traced here: 362 us
  waiting for transfers between devices  173 us (48%)
  local copies, waits for them, and re-layouts  68.5 us (19%)
  other arithmetic  40.1 us (11%)
  blocking collectives  30.4 us (8%)
  matrix products  27.8 us (8%)
  between operations  17.2 us (5%)
  starting transfers between devices  5.05 us (1%)
    all_to_all x1, waiting for transfers between devices, token_columns(): lax.all_to_all(inputs, 'fsdp', split_axis=1, concat_axis=0, tiled=True)  81.1 us
    all_gather x1, waiting for transfers between devices, body(): lax.all_gather(key_weights, 'fsdp', axis=0, tiled=True)  74.7 us
    while x32, local copies, waits for them, and re-layouts  27.5 us
    dot_general x8, matrix products, one_block(): lax.dot_general(picked, shaped, (((0,), (0,)), ((), ())), preferred_eleme...  19.5 us
    all_gather x1, blocking collectives, body(): fresh = lax.all_gather(new_anchor, 'rep', axis=0, tiled=True)  18 us
    add x8, other arithmetic, one_block(): return carried + partial_sum.astype(jnp.float32)  17.1 us
    reduce_scatter x1, waiting for transfers between devices, body(): summed = lax.psum_scatter(own_cols, 'rep', scatter_dimension=0, tiled=True)  16.8 us
    dot_general x1, local copies, waits for them, and re-layouts, body(): jnp.dot(picked, lax.all_gather(key_weights, 'fsdp', axis=0, tiled=True),...  16.8 us
  transfers between devices with their start and end apart: 4, of which 3 were waited for; matrix products, arithmetic and copies ran while one was open for 5% of the time, Pallas kernels for 0%

commit v1 on v0

v1 whole, which is shorter than its diff:
```python
import jax
import jax.numpy as jnp
from jax import lax
from jax.sharding import PartitionSpec as P

HEAD = 128
WARMUP = 2000
STEPS_TOTAL = 100000
FRAG_COLS = 128


BETA_ONE = 0.9
BETA_TWO = 0.95
ADAM_EPS = 1e-08
DECAY = 0.1
PEAK_RATE = 0.0003
CLIP_NORM = 1.0
OUTER_MU = 0.9
OUTER_RATE = 0.7
MIX_LOCAL = 0.5


def key_backward(raw_keys, incoming):
    count = raw_keys.shape[0]
    heads = raw_keys.reshape(count, -1, HEAD)
    inverse = lax.rsqrt(jnp.mean(heads * heads, axis=2, keepdims=True) + 1e-06)
    normed = heads * inverse
    upper = incoming.astype(jnp.float32).reshape(heads.shape)
    back = inverse * (upper - normed * jnp.mean(upper * normed, axis=2, keepdims=True))
    return back.reshape(count, -1).astype(jnp.bfloat16)


def swap(block, axis, offset):
    count = lax.axis_size(axis)
    return lax.ppermute(block, axis, [(i, i ^ offset) for i in range(count)])


def gather_pairs(block, axis):
    count = lax.axis_size(axis)
    blocks = [block] + [swap(block, axis, k) for k in range(2, count, 2)]
    out = []
    for held in blocks:
        out += [held, swap(held, axis, 1)]
    return out


def body(
    tokens,
    cotangent,
    weights,
    first_moment,
    second_moment,
    anchor,
    momentum,
    due_fragment,
    step_count,
):
    inputs = tokens[0]
    incoming = cotangent[0]
    params = weights[0]
    kv_width = incoming.shape[1] // 2
    rows = params.shape[0]
    replicas = lax.axis_size("rep")
    shards = lax.axis_size("fsdp")
    me = lax.axis_index("fsdp")
    my_rep = lax.axis_index("rep")
    offset = due_fragment[0] * FRAG_COLS
    part = anchor.shape[0]

    old_cols = lax.dynamic_slice_in_dim(params, offset, FRAG_COLS, 1)
    anchor_cols = lax.dynamic_slice_in_dim(anchor, offset, FRAG_COLS, 1)
    moment_cols = lax.dynamic_slice_in_dim(momentum, offset, FRAG_COLS, 1)

    def rep_piece(cols, k):
        return lax.dynamic_slice_in_dim(cols, (my_rep ^ k) * part, part, 0)

    def rep_scatter(cols, wire):
        total = rep_piece(cols, 0)
        for k in range(1, replicas):
            total = total + swap(rep_piece(cols, k).astype(wire), "rep", k).astype(jnp.float32)
        return total

    def rep_gather(piece):
        pieces = [piece] + [swap(piece, "rep", k) for k in range(1, replicas)]
        out = jnp.zeros((part * replicas,) + piece.shape[1:], piece.dtype)
        for k in range(replicas):
            out = lax.dynamic_update_slice_in_dim(out, pieces[k], (my_rep ^ k) * part, 0)
        return out

    old_sum = rep_scatter(old_cols, jnp.float32)

    def token_piece(k):
        return lax.dynamic_slice_in_dim(inputs, (me ^ k) * rows, rows, 1)

    order = [k for k in range(2, shards) if k % 2 == 0] + [k for k in range(2, shards) if k % 2 == 1] + [1]
    key_weights = params[:, :kv_width].astype(jnp.bfloat16)
    columns = {0: token_piece(0)}
    for k in order:
        columns[k] = swap(token_piece(k), "fsdp", k)
    raw_keys = jnp.dot(columns[0], key_weights, preferred_element_type=jnp.float32)
    for k in order:
        partial_keys = jnp.dot(columns[k], key_weights, preferred_element_type=jnp.float32)
        raw_keys = raw_keys + swap(partial_keys.astype(jnp.bfloat16), "fsdp", k).astype(jnp.float32)
    key_back = key_backward(raw_keys, incoming[:, :kv_width])
    all_columns = jnp.concatenate([columns[k] for k in range(shards)], axis=0)
    values = jnp.concatenate(gather_pairs(incoming[:, kv_width:], "fsdp"), axis=0)
    keys = jnp.concatenate(gather_pairs(key_back, "fsdp"), axis=0)
    dims = (((0,), (0,)), ((), ()))
    grad_values = lax.dot_general(all_columns, values, dims, preferred_element_type=jnp.float32)
    grad_keys = lax.dot_general(all_columns, keys, dims, preferred_element_type=jnp.float32)
    own_square = jnp.sum(grad_values * grad_values) + jnp.sum(grad_keys * grad_keys)
    own_square = jnp.full((8, 128), own_square, jnp.float32)
    square = own_square
    for k in range(1, shards):
        square = square + swap(own_square, "fsdp", k)
    square = square[0, 0]
    gradient = jnp.concatenate([grad_keys, grad_values], axis=1)
    factor = jnp.minimum(1.0, CLIP_NORM / (jnp.sqrt(square) + 1e-06))
    steps_now = step_count[0].astype(jnp.float32)
    plan = jnp.minimum(1.0, steps_now / WARMUP) * (
        0.55 + 0.45 * jnp.cos(jnp.pi * steps_now / STEPS_TOTAL)
    )
    rate = PEAK_RATE * plan
    correct_one = 1.0 - jnp.power(BETA_ONE, steps_now)
    correct_two = 1.0 - jnp.power(BETA_TWO, steps_now)

    def adam(old, first, second, grad):
        clipped = grad * factor
        first_new = BETA_ONE * first + (1.0 - BETA_ONE) * clipped
        second_new = BETA_TWO * second + (1.0 - BETA_TWO) * clipped * clipped
        update = rate * (
            first_new / correct_one / (jnp.sqrt(second_new / correct_two) + ADAM_EPS) + DECAY * old
        )
        return update, first_new, second_new

    frag = [lax.dynamic_slice_in_dim(a, offset, FRAG_COLS, 1) for a in (params, first_moment[0], second_moment[0], gradient)]
    frag_update, _, _ = adam(*frag)
    own_cols = old_cols - frag_update
    update_sum = rep_scatter(frag_update, jnp.bfloat16)
    mean_inner = (old_sum - update_sum) / replicas
    pseudo = anchor_cols - mean_inner
    new_moment = OUTER_MU * moment_cols + pseudo
    new_anchor = anchor_cols - OUTER_RATE * (OUTER_MU * new_moment + pseudo)
    fresh = rep_gather(new_anchor)
    update, first_out, second_out = adam(params, first_moment[0], second_moment[0], gradient)
    inner = params - update
    mixed = MIX_LOCAL * own_cols + (1.0 - MIX_LOCAL) * fresh
    weights_out = lax.dynamic_update_slice_in_dim(inner, mixed, offset, 1)
    anchor_out = lax.dynamic_update_slice_in_dim(anchor, new_anchor, offset, 1)
    momentum_out = lax.dynamic_update_slice_in_dim(momentum, new_moment, offset, 1)
    plan_out = jnp.reshape(plan, (1,))
    return (
        weights_out[None],
        first_out[None],
        second_out[None],
        anchor_out,
        momentum_out,
        plan_out,
    )


def solution(mesh):
    return jax.shard_map(
        body,
        mesh=mesh,
        in_specs=(
            P("rep", "fsdp", None),
            P("rep", "fsdp", None),
            P("rep", "fsdp", None),
            P("rep", "fsdp", None),
            P("rep", "fsdp", None),
            P(("fsdp", "rep"), None),
            P(("fsdp", "rep"), None),
            P(),
            P(),
        ),
        out_specs=(
            P("rep", "fsdp", None),
            P("rep", "fsdp", None),
            P("rep", "fsdp", None),
            P(("fsdp", "rep"), None),
            P(("fsdp", "rep"), None),
            P(),
        ),
        check_vma=False,
    )
```

time: 363 us -> 267 us (0.74)
  waiting for transfers between devices: 173 us -> 83.8 us
  starting transfers between devices: 5.05 us -> 50.2 us
  blocking collectives: 30.4 us -> 0 us
  other arithmetic: 40.1 us -> 21.6 us
  between operations: 17.2 us -> 5.93 us
  local copies, waits for them, and re-layouts: 68.5 us -> 79.4 us
    ppermute x0 -> x44, waiting for transfers between devices: none -> 83.8 us  [swap(): return lax.ppermute(block, axis, [(i, i ^ offset) for i in range(count)])]
    all_to_all x1 -> x0, waiting for transfers between devices: 81.1 us -> none  [token_columns(): lax.all_to_all(inputs, 'fsdp', split_axis=1, concat_axis=0, tiled=True)]
    all_gather x2 -> x0, waiting for transfers between devices: 74.7 us -> none  [the longest x1 74.7 us: body(): lax.all_gather(key_weights, 'fsdp', axis=0, tiled=True)]
    ppermute x0 -> x44, starting transfers between devices: none -> 50.2 us  [swap(): return lax.ppermute(block, axis, [(i, i ^ offset) for i in range(count)])]
    unnamed x14 -> x61, local copies, waits for them, and re-layouts: 14.9 us -> 52.7 us
    while x32 -> x0, local copies, waits for them, and re-layouts: 27.5 us -> none
    dynamic_slice x1 -> x9, local copies, waits for them, and re-layouts: 0.99 us -> 19.6 us  [the longest x5 8.5 us: rep_piece(): return lax.dynamic_slice_in_dim(cols, (my_rep ^ k) * part, part, 0)]
    all_gather x1 -> x0, blocking collectives: 18 us -> none  [body(): fresh = lax.all_gather(new_anchor, 'rep', axis=0, tiled=True)]
  transfers between devices with their start and end apart: 4 -> 44, of which waited for: 3 -> 16; matrix products, arithmetic and copies ran while one was open for 5% -> 37% of each run, Pallas kernels for 0% -> 0%
where the time goes in v1:
time: 267 us; the launch traced here: 266 us
  waiting for transfers between devices  83.8 us (31%)
  local copies, waits for them, and re-layouts  79.4 us (30%)
  starting transfers between devices  50.2 us (19%)
  matrix products  24.6 us (9%)
  other arithmetic  21.6 us (8%)
  between operations  5.93 us (2%)
    ppermute x44, waiting for transfers between devices, swap(): return lax.ppermute(block, axis, [(i, i ^ offset) for i in range(count)])  83.8 us
    unnamed x61, local copies, waits for them, and re-layouts  52.7 us
    ppermute x44, starting transfers between devices, swap(): return lax.ppermute(block, axis, [(i, i ^ offset) for i in range(count)])  50.2 us
    sub x1, other arithmetic, body(): inner = params - update  12.2 us
    dot_general x7, matrix products, body(): jnp.dot(columns[k], key_weights, preferred_element_type=jnp.float32)  9.66 us
    dynamic_slice x5, local copies, waits for them, and re-layouts, rep_piece(): return lax.dynamic_slice_in_dim(cols, (my_rep ^ k) * part, part, 0)  8.5 us
    dot_general x1, matrix products, body(): lax.dot_general(all_columns, keys, dims, preferred_element_type=jnp.float32)  6.81 us
    dot_general x1, matrix products, body(): lax.dot_general(all_columns, values, dims, preferred_element_type=jnp.flo...  5.79 us
  transfers between devices with their start and end apart: 44, of which 16 were waited for; matrix products, arithmetic and copies ran while one was open for 37% of the time, Pallas kernels for 0%

profile of v1, /device:TPU:0, one launch (start us, length us, event | category | flops | bytes accessed | tf_op | source)
XLA Modules:
  0.0 265.6 jit_solution(14192969908162967693)
XLA Ops:
  0.6 2.8 %copy.73 = f32[384,1024]{1,0:T(8,128)} copy(f32[384,1024]{1,0:T(8,128)} %param.14) | data formatting | bytes 3145728
  4.6 5.0 %dynamic-slice_bitcast_fusion = (bf16[256,1536]{1,0:T(8,128)(2,1)}, bf16[256,1536]{1,0:T(8,128)(2,1)}, bf16[256,1536]{1,0:T(8,128)(2,1)}, bf16[256,1536]{1,0:T(8...) fusion(bf16[1,256,12288]{2,1,0:T(8,128)(2,1)} %param.9, ...), kind=kLoop, calls=%fused_computation.37 | loop fusion | bytes 11010076 | tf_op jit(solution)/shard_map/dynamic_slice | solution.py:93
  9.6 3.3 %collective-permute-start.6 = (bf16[256,1536]{1,0:T(8,128)(2,1)}, bf16[256,1536]{1,0:T(8,128)(2,1)}, u32[]{:S(2)}, u32[]{:S(2)}) collective-permute-start(bf16[256,1536]{1,0:T(8,128)(2,1)} %get-tuple-element.25), channel_id=1, source_target_pairs={{0,7},{1,6},{2,5},{3,4},{4,3},{5,2},{6,1},{7,0},{8,15},{9,14},{10,... | collective-permute-start | bytes 2359304 | tf_op jit(solution)/shard_map/ppermute | solution.py:35
  13.7 1.5 collective-permute-start.3
  16.4 2.2 convert_bitcast_fusion
  19.6 2.4 fusion.13
  21.9 2.1 constant_dynamic-slice_fusion.6
  24.0 1.2 bitcast_dynamic-update-slice_fusion.1
  25.2 6.0 %collective-permute-done.6 = bf16[256,1536]{1,0:T(8,128)(2,1)} collective-permute-done((bf16[256,1536]{1,0:T(8,128)(2,1)}, bf16[256,1536]{1,0:T(8,128)(2,1)}, u32[]{:S(2)}, u32[]{:S(2)}) %collective-permute-start.6) | collective-permute-done | bytes 786464 | tf_op jit(solution)/shard_map/ppermute | solution.py:35
  32.0 1.7 convolution_convert_fusion.1
  33.8 14.4 %collective-permute-done.4 = bf16[256,1536]{1,0:T(8,128)(2,1)} collective-permute-done((bf16[256,1536]{1,0:T(8,128)(2,1)}, bf16[256,1536]{1,0:T(8,128)(2,1)}, u32[]{:S(2)}, u32[]{:S(2)}) %collective-permute-start.4) | collective-permute-done | bytes 786464 | tf_op jit(solution)/shard_map/ppermute | solution.py:35
  48.1 2.4 collective-permute-start.5
  50.5 1.7 convolution_convert_fusion.2
  52.2 13.6 %collective-permute-done.3 = bf16[256,1536]{1,0:T(8,128)(2,1)} collective-permute-done((bf16[256,1536]{1,0:T(8,128)(2,1)}, bf16[256,1536]{1,0:T(8,128)(2,1)}, u32[]{:S(2)}, u32[]{:S(2)}) %collective-permute-start.3) | collective-permute-done | bytes 786464 | tf_op jit(solution)/shard_map/ppermute | solution.py:35
  65.8 1.2 collective-permute-start.12
  67.1 1.7 convolution_convert_fusion.5
  68.8 1.5 collective-permute-start.11
  70.3 1.7 convolution_convert_fusion.3
  72.7 1.7 convolution_convert_fusion.6
  75.8 6.9 %collective-permute-done.5 = bf16[256,1536]{1,0:T(8,128)(2,1)S(1)} collective-permute-done((bf16[256,1536]{1,0:T(8,128)(2,1)S(1)}, bf16[256,1536]{1,0:T(8,128)(2,1)S(1)}, u32[]{:S(2)}, u32[]{:S(2)}) %collective-permute-start.5) | collective-permute-done | bytes 786464 | tf_op jit(solution)/shard_map/ppermute | solution.py:35
  82.8 1.4 collective-permute-start.7
  84.8 1.2 constant_dynamic-update-slice_fusion.5
  86.0 1.2 constant_dynamic-update-slice_fusion.4
  88.2 4.9 %collective-permute-done.11 = bf16[256,512]{1,0:T(8,128)(2,1)S(1)} collective-permute-done((bf16[256,512]{1,0:T(8,128)(2,1)S(1)}, bf16[256,512]{1,0:T(8,128)(2,1)S(1)}, u32[]{:S(2)}, u32[]{:S(2)}) %collective-permute-start.11) | collective-permute-done | bytes 262176 | tf_op jit(solution)/shard_map/ppermute | solution.py:35
  93.0 3.2 %collective-permute-start.9 = (bf16[256,512]{1,0:T(8,128)(2,1)S(1)}, bf16[256,512]{1,0:T(8,128)(2,1)S(1)}, u32[]{:S(2)}, u32[]{:S(2)}) collective-permute-start(bf16[256,512]{1,0:T(8,128)(2,1)S(1)} %convolution_convert_fusion.4), channel_id=1, source_target_pairs={{0,6},{1,7},{2,4},{3,5},{4,2},{5,3},{6,0},{7,1},{8,14},{9,15},{10,... | collective-permute-start | bytes 786440 | tf_op jit(solution)/shard_map/ppermute | solution.py:35
  97.4 1.2 constant_dynamic-update-slice_fusion.2
  99.6 4.8 %collective-permute-done.9 = bf16[256,512]{1,0:T(8,128)(2,1)S(1)} collective-permute-done((bf16[256,512]{1,0:T(8,128)(2,1)S(1)}, bf16[256,512]{1,0:T(8,128)(2,1)S(1)}, u32[]{:S(2)}, u32[]{:S(2)}) %collective-permute-start.9) | collective-permute-done | bytes 262176 | tf_op jit(solution)/shard_map/ppermute | solution.py:35
  107.8 2.4 collective-permute-start.17
  110.1 1.5 collective-permute-start.15
  111.6 2.1 constant_dynamic-update-slice_fusion
  113.8 1.8 collective-permute-start.22
  115.7 1.3 collective-permute-done.17
  117.0 2.7 %collective-permute-start.26 = (bf16[256,512]{1,0:T(8,128)(2,1)S(1)}, bf16[256,512]{1,0:T(8,128)(2,1)S(1)}, u32[]{:S(2)}, u32[]{:S(2)}) collective-permute-start(bf16[256,512]{1,0:T(8,128)(2,1)S(1)} %get-tuple-element.36), channel_id=1, source_target_pairs={{0,6},{1,7},{2,4},{3,5},{4,2},{5,3},{6,0},{7,1},{8,14},{9,15},{10,... | collective-permute-start | bytes 786440 | tf_op jit(solution)/shard_map/ppermute | solution.py:35
  120.3 10.3 %collective-permute-done.22 = bf16[256,512]{1,0:T(8,128)(2,1)S(1)} collective-permute-done((bf16[256,512]{1,0:T(8,128)(2,1)S(1)}, bf16[256,512]{1,0:T(8,128)(2,1)S(1)}, u32[]{:S(2)}, u32[]{:S(2)}) %collective-permute-start.22) | collective-permute-done | bytes 262176 | tf_op jit(solution)/shard_map/ppermute | solution.py:35
  131.2 3.9 %collective-permute-done.26 = bf16[256,512]{1,0:T(8,128)(2,1)S(1)} collective-permute-done((bf16[256,512]{1,0:T(8,128)(2,1)S(1)}, bf16[256,512]{1,0:T(8,128)(2,1)S(1)}, u32[]{:S(2)}, u32[]{:S(2)}) %collective-permute-start.26) | collective-permute-done | bytes 262176 | tf_op jit(solution)/shard_map/ppermute | solution.py:35
  136.7 6.8 %multiply_reduce_fusion = (f32[]{:T(128)}, f32[1536,512]{0,1:T(8,128)S(1)}) fusion(bf16[2048,1536]{1,0:T(8,128)(2,1)} %constant_dynamic-update-slice_fusion, bf16[2048,512]{1,0:T(8,128)(2,1)S(1)} %constant_dynamic-update-slice_fusion.7), kind=kOutput, calls=%fused_computation.7 | convolution fusion | flops 3222798336 | bytes 11534340 | tf_op jit(solution)/shard_map/dot_general | solution.py:110
  143.6 5.8 %multiply_reduce_fusion.1 = (f32[]{:T(128)}, f32[1536,512]{0,1:T(8,128)}) fusion(bf16[2048,1536]{1,0:T(8,128)(2,1)S(1)} %bitcast.109, bf16[2048,512]{1,0:T(8,128)(2,1)S(1)} %constant_dynamic-update-slice_fusion.15), kind=kOutput, calls=%fused_computation.8 | convolution fusion | flops 3222798336 | bytes 11534340 | tf_op jit(solution)/shard_map/dot_general | solution.py:109
  150.7 2.8 %collective-permute-start.33 = (f32[8,128]{1,0:T(8,128)S(1)}, f32[8,128]{1,0:T(8,128)S(1)}, u32[]{:S(2)}, u32[]{:S(2)}) collective-permute-start(f32[8,128]{1,0:T(8,128)S(1)} %broadcast_in_dim.6), channel_id=1, source_target_pairs={{0,6},{1,7},{2,4},{3,5},{4,2},{5,3},{6,0},{7,1},{8,14},{9,15},{10,... | collective-permute-start | bytes 12296 | tf_op jit(solution)/shard_map/ppermute | solution.py:35
  153.5 2.5 constant_dynamic-slice_fusion.3
  156.0 1.5 collective-permute-start.31
  158.0 1.5 collective-permute-start.29
  159.8 1.7 constant_dynamic-slice_fusion.4
  161.6 6.6 %copy.18 = f32[1,1536,1024]{1,2,0:T(8,128)} copy(f32[1,1536,1024]{2,1,0:T(8,128)} %param.11) | data formatting | bytes 12582912 | tf_op args[2]
  168.9 1.7 copy.24
  170.7 1.7 copy.25
  172.4 1.8 copy.27
  175.0 2.3 copy.19
  178.5 6.6 %copy.15 = f32[1,1536,1024]{1,2,0:T(8,128)} copy(f32[1,1536,1024]{2,1,0:T(8,128)} %param.12) | data formatting | bytes 12582912 | tf_op args[3]
  185.0 6.6 %copy.16 = f32[1,1536,1024]{1,2,0:T(8,128)} copy(f32[1,1536,1024]{2,1,0:T(8,128)} %param.13) | data formatting | bytes 12582912 | tf_op args[4]
  191.6 2.8 %collective-permute-start.36 = (f32[384,128]{0,1:T(8,128)}, f32[384,128]{0,1:T(8,128)}, u32[]{:S(2)}, u32[]{:S(2)}) collective-permute-start(f32[384,128]{0,1:T(8,128)} %bitcast.107), channel_id=1, source_target_pairs={{0,16},{8,24},{16,0},{24,8},{1,17},{9,25},{17,1},{25,9},{2,18},{10... | collective-permute-start | bytes 589832 | tf_op jit(solution)/shard_map/ppermute | solution.py:35
  194.4 1.4 collective-permute-start.37
  198.1 2.5 fusion.10
  202.2 1.7 collective-permute-start.38
  203.9 2.5 collective-permute-start.40
  206.4 2.6 collective-permute-done.36
  209.0 12.2 %multiply_subtract_fusion = (f32[1,1536,1024]{1,2,0:T(8,128)}, f32[1,1536,1024]{1,2,0:T(8,128)}, f32[1,1536,1024]{1,2,0:T(8,128)}) fusion(f32[1,1536,1024]{1,2,0:T(8,128)} %copy.18, f32[]{:T(128)} %bitcast.15, f32[]{:T(128)} %bitcast.14, f32[]{:T(128)} %bitcast, f32[]{:T(128)} %bitcast.13, f32[1,1536,512]{1,2,0:T(8,128)} %bitcast.100, ...), kind=kLoop, calls=%fused_computation.5 | loop fusion | flops 26738688 | bytes 44040208 | tf_op jit(solution)/shard_map/sub | solution.py:146
  221.2 6.6 %copy.32 = f32[1,1536,1024]{2,1,0:T(8,128)} copy(f32[1,1536,1024]{1,2,0:T(8,128)} %get-tuple-element.17) | data formatting | bytes 12582912
  227.7 6.6 %copy.31 = f32[1,1536,1024]{2,1,0:T(8,128)} copy(f32[1,1536,1024]{1,2,0:T(8,128)} %get-tuple-element.18) | data formatting | bytes 12582912
  234.5 1.4 multiply_add_fusion.1
  236.1 2.9 %collective-permute-start.43 = (f32[384,128]{0,1:T(8,128)S(1)}, f32[384,128]{0,1:T(8,128)S(1)}, u32[]{:S(2)}, u32[]{:S(2)}) collective-permute-start(f32[384,128]{0,1:T(8,128)S(1)} %get-tuple-element.15), channel_id=1, source_target_pairs={{0,24},{8,16},{16,8},{24,0},{1,25},{9,17},{17,9},{25,1},{2,26},{10... | collective-permute-start | bytes 589832 | tf_op jit(solution)/shard_map/ppermute | solution.py:35
  239.1 2.0 collective-permute-start.42
  242.6 9.2 %collective-permute-done.41 = f32[384,128]{0,1:T(8,128)} collective-permute-done((f32[384,128]{0,1:T(8,128)S(1)}, f32[384,128]{0,1:T(8,128)}, u32[]{:S(2)}, u32[]{:S(2)}) %collective-permute-start.41) | collective-permute-done | bytes 196640 | tf_op jit(solution)/shard_map/ppermute | solution.py:35
  252.8 3.9 %collective-permute-done.42 = f32[384,128]{0,1:T(8,128)S(1)} collective-permute-done((f32[384,128]{0,1:T(8,128)S(1)}, f32[384,128]{0,1:T(8,128)S(1)}, u32[]{:S(2)}, u32[]{:S(2)}) %collective-permute-start.42) | collective-permute-done | bytes 196640 | tf_op jit(solution)/shard_map/ppermute | solution.py:35
  257.9 6.6 %copy.30 = f32[1,1536,1024]{2,1,0:T(8,128)} copy(f32[1,1536,1024]{1,2,0:T(8,128)} %bitcast_dynamic-update-slice_fusion) | data formatting | bytes 12582912
  (138 shorter events, 26.2 us)
Async XLA Ops:
  0.6 2.9 %copy-start.5 = (f32[384,1024]{1,0:T(8,128)S(1)}, f32[384,1024]{1,0:T(8,128)}, u32[]{:S(2)}) copy-start(f32[384,1024]{1,0:T(8,128)} %param.15) | copy-start | bytes 4718596
  3.5 12.9 %slice-start = ((s8[6291456]{0:T(1024)(128)(4,1)}), s8[2097152]{0:T(1024)(128)(4,1)S(1)}, s32[]{:S(2)}) async-start(s8[6291456]{0:T(1024)(128)(4,1)} %bitcast.97), calls=%async_computation | async-start | bytes 4194304
  4.6 11.8 %slice-start.1 = ((s8[6291456]{0:T(1024)(128)(4,1)}), s8[4194304]{0:T(1024)(128)(4,1)S(1)}, s32[]{:S(2)}) async-start(s8[6291456]{0:T(1024)(128)(4,1)} %bitcast.97), calls=%async_computation.1 | async-start | bytes 8388608
  9.6 21.6 %collective-permute-start.6 = (bf16[256,1536]{1,0:T(8,128)(2,1)}, bf16[256,1536]{1,0:T(8,128)(2,1)}, u32[]{:S(2)}, u32[]{:S(2)}) collective-permute-start(bf16[256,1536]{1,0:T(8,128)(2,1)} %get-tuple-element.25), channel_id=1, source_target_pairs={{0,7},{1,6},{2,5},{3,4},{4,3},{5,2},{6,1},{7,0},{8,15},{9,14},{10,... | collective-permute-start | bytes 2359304 | tf_op jit(solution)/shard_map/ppermute | solution.py:35
  12.9 35.2 %collective-permute-start.4 = (bf16[256,1536]{1,0:T(8,128)(2,1)}, bf16[256,1536]{1,0:T(8,128)(2,1)}, u32[]{:S(2)}, u32[]{:S(2)}) collective-permute-start(bf16[256,1536]{1,0:T(8,128)(2,1)} %get-tuple-element.26), channel_id=1, source_target_pairs={{0,5},{1,4},{2,7},{3,6},{4,1},{5,0},{6,3},{7,2},{8,13},{9,12},{10,... | collective-permute-start | bytes 2359304 | tf_op jit(solution)/shard_map/ppermute | solution.py:35
  13.7 52.1 %collective-permute-start.3 = (bf16[256,1536]{1,0:T(8,128)(2,1)}, bf16[256,1536]{1,0:T(8,128)(2,1)}, u32[]{:S(2)}, u32[]{:S(2)}) collective-permute-start(bf16[256,1536]{1,0:T(8,128)(2,1)} %get-tuple-element.27), channel_id=1, source_target_pairs={{0,4},{1,5},{2,6},{3,7},{4,0},{5,1},{6,2},{7,3},{8,12},{9,13},{10,... | collective-permute-start | bytes 2359304 | tf_op jit(solution)/shard_map/ppermute | solution.py:35
  15.2 53.5 %collective-permute-start.2 = (bf16[256,1536]{1,0:T(8,128)(2,1)}, bf16[256,1536]{1,0:T(8,128)(2,1)}, u32[]{:S(2)}, u32[]{:S(2)}) collective-permute-start(bf16[256,1536]{1,0:T(8,128)(2,1)} %get-tuple-element.28), channel_id=1, source_target_pairs={{0,3},{1,2},{2,1},{3,0},{4,7},{5,6},{6,5},{7,4},{8,11},{9,10},{10,... | collective-permute-start | bytes 2359304 | tf_op jit(solution)/shard_map/ppermute | solution.py:35
  15.2 3.4 %copy-start.6 = (bf16[1,256,1024]{2,1,0:T(8,128)(2,1)S(1)}, bf16[1,256,1024]{2,1,0:T(8,128)(2,1)}, u32[]{:S(2)}) copy-start(bf16[1,256,1024]{2,1,0:T(8,128)(2,1)} %param.10) | copy-start | bytes 1572868
  15.2 56.7 %collective-permute-start.1 = (bf16[256,1536]{1,0:T(8,128)(2,1)}, bf16[256,1536]{1,0:T(8,128)(2,1)}, u32[]{:S(2)}, u32[]{:S(2)}) collective-permute-start(bf16[256,1536]{1,0:T(8,128)(2,1)} %get-tuple-element.29), channel_id=1, source_target_pairs={{0,2},{1,3},{2,0},{3,1},{4,6},{5,7},{6,4},{7,5},{8,10},{9,11},{10,... | collective-permute-start | bytes 2359304 | tf_op jit(solution)/shard_map/ppermute | solution.py:35
  19.5 11.7 %copy-start.7 = (bf16[256,1536]{1,0:T(8,128)(2,1)S(1)}, bf16[256,1536]{1,0:T(8,128)(2,1)}, u32[]{:S(2)}) copy-start(bf16[256,1536]{1,0:T(8,128)(2,1)} %get-tuple-element.30) | copy-start | bytes 2359300
  19.5 12.5 %copy-start.4 = (bf16[1536,1024]{1,0:T(8,128)(2,1)S(1)}, bf16[1536,1024]{1,0:T(8,128)(2,1)}, u32[]{:S(2)}) copy-start(bf16[1536,1024]{1,0:T(8,128)(2,1)} %convert_bitcast_fusion) | copy-start | bytes 9437188
  31.2 43.2 %collective-permute-start = (bf16[256,1536]{1,0:T(8,128)(2,1)S(1)}, bf16[256,1536]{1,0:T(8,128)(2,1)S(1)}, u32[]{:S(2)}, u32[]{:S(2)}) collective-permute-start(bf16[256,1536]{1,0:T(8,128)(2,1)S(1)} %copy-done.7), channel_id=1, source_target_pairs={{0,1},{1,0},{2,3},{3,2},{4,5},{5,4},{6,7},{7,6},{8,9},{9,8},{10,11... | collective-permute-start | bytes 2359304 | tf_op jit(solution)/shard_map/ppermute | solution.py:35
  48.1 34.7 %collective-permute-start.5 = (bf16[256,1536]{1,0:T(8,128)(2,1)S(1)}, bf16[256,1536]{1,0:T(8,128)(2,1)S(1)}, u32[]{:S(2)}, u32[]{:S(2)}) collective-permute-start(bf16[256,1536]{1,0:T(8,128)(2,1)S(1)} %get-tuple-element.31), channel_id=1, source_target_pairs={{0,6},{1,7},{2,4},{3,5},{4,2},{5,3},{6,0},{7,1},{8,14},{9,15},{10,... | collective-permute-start | bytes 2359304 | tf_op jit(solution)/shard_map/ppermute | solution.py:35
  65.8 21.5 %collective-permute-start.12 = (bf16[256,512]{1,0:T(8,128)(2,1)S(1)}, bf16[256,512]{1,0:T(8,128)(2,1)S(1)}, u32[]{:S(2)}, u32[]{:S(2)}) collective-permute-start(bf16[256,512]{1,0:T(8,128)(2,1)S(1)} %convolution_convert_fusion.1), channel_id=1, source_target_pairs={{0,7},{1,6},{2,5},{3,4},{4,3},{5,2},{6,1},{7,0},{8,15},{9,14},{10,... | collective-permute-start | bytes 786440 | tf_op jit(solution)/shard_map/ppermute | solution.py:35
  68.8 24.2 %collective-permute-start.11 = (bf16[256,512]{1,0:T(8,128)(2,1)S(1)}, bf16[256,512]{1,0:T(8,128)(2,1)S(1)}, u32[]{:S(2)}, u32[]{:S(2)}) collective-permute-start(bf16[256,512]{1,0:T(8,128)(2,1)S(1)} %convolution_convert_fusion.2), channel_id=1, source_target_pairs={{0,5},{1,4},{2,7},{3,6},{4,1},{5,0},{6,3},{7,2},{8,13},{9,12},{10,... | collective-permute-start | bytes 786440 | tf_op jit(solution)/shard_map/ppermute | solution.py:35
  72.0 27.5 %collective-permute-start.8 = (bf16[256,512]{1,0:T(8,128)(2,1)S(1)}, bf16[256,512]{1,0:T(8,128)(2,1)S(1)}, u32[]{:S(2)}, u32[]{:S(2)}) collective-permute-start(bf16[256,512]{1,0:T(8,128)(2,1)S(1)} %convolution_convert_fusion.5), channel_id=1, source_target_pairs={{0,4},{1,5},{2,6},{3,7},{4,0},{5,1},{6,2},{7,3},{8,12},{9,13},{10,... | collective-permute-start | bytes 786440 | tf_op jit(solution)/shard_map/ppermute | solution.py:35
  74.4 25.1 %collective-permute-start.10 = (bf16[256,512]{1,0:T(8,128)(2,1)S(1)}, bf16[256,512]{1,0:T(8,128)(2,1)S(1)}, u32[]{:S(2)}, u32[]{:S(2)}) collective-permute-start(bf16[256,512]{1,0:T(8,128)(2,1)S(1)} %convolution_convert_fusion.3), channel_id=1, source_target_pairs={{0,3},{1,2},{2,1},{3,0},{4,7},{5,6},{6,5},{7,4},{8,11},{9,10},{10,... | collective-permute-start | bytes 786440 | tf_op jit(solution)/shard_map/ppermute | solution.py:35
  82.8 3.3 %copy-start.9 = (bf16[256,1536]{1,0:T(8,128)(2,1)}, bf16[256,1536]{1,0:T(8,128)(2,1)S(1)}, u32[]{:S(2)}) copy-start(bf16[256,1536]{1,0:T(8,128)(2,1)S(1)} %collective-permute-done.5) | copy-start | bytes 2359300
  82.8 16.8 %collective-permute-start.7 = (bf16[256,512]{1,0:T(8,128)(2,1)S(1)}, bf16[256,512]{1,0:T(8,128)(2,1)S(1)}, u32[]{:S(2)}, u32[]{:S(2)}) collective-permute-start(bf16[256,512]{1,0:T(8,128)(2,1)S(1)} %convolution_convert_fusion.6), channel_id=1, source_target_pairs={{0,2},{1,3},{2,0},{3,1},{4,6},{5,7},{6,4},{7,5},{8,10},{9,11},{10,... | collective-permute-start | bytes 786440 | tf_op jit(solution)/shard_map/ppermute | solution.py:35
  87.3 12.2 %collective-permute-start.13 = (bf16[256,512]{1,0:T(8,128)(2,1)S(1)}, bf16[256,512]{1,0:T(8,128)(2,1)S(1)}, u32[]{:S(2)}, u32[]{:S(2)}) collective-permute-start(bf16[256,512]{1,0:T(8,128)(2,1)S(1)} %convolution_convert_fusion), channel_id=1, source_target_pairs={{0,1},{1,0},{2,3},{3,2},{4,5},{5,4},{6,7},{7,6},{8,9},{9,8},{10,11... | collective-permute-start | bytes 786440 | tf_op jit(solution)/shard_map/ppermute | solution.py:35
  93.0 11.3 %collective-permute-start.9 = (bf16[256,512]{1,0:T(8,128)(2,1)S(1)}, bf16[256,512]{1,0:T(8,128)(2,1)S(1)}, u32[]{:S(2)}, u32[]{:S(2)}) collective-permute-start(bf16[256,512]{1,0:T(8,128)(2,1)S(1)} %convolution_convert_fusion.4), channel_id=1, source_target_pairs={{0,6},{1,7},{2,4},{3,5},{4,2},{5,3},{6,0},{7,1},{8,14},{9,15},{10,... | collective-permute-start | bytes 786440 | tf_op jit(solution)/shard_map/ppermute | solution.py:35
  98.6 5.8 %copy-start.11 = (bf16[2048,1536]{1,0:T(8,128)(2,1)}, bf16[2048,1536]{1,0:T(8,128)(2,1)S(1)}, u32[]{:S(2)}) copy-start(bf16[2048,1536]{1,0:T(8,128)(2,1)S(1)} %constant_dynamic-update-slice_fusion.2) | copy-start | bytes 18874372
  105.2 1.7 copy-start.10
  106.8 7.1 %collective-permute-start.14 = (bf16[256,512]{1,0:T(8,128)(2,1)S(1)}, bf16[256,512]{1,0:T(8,128)(2,1)S(1)}, u32[]{:S(2)}, u32[]{:S(2)}) collective-permute-start(bf16[256,512]{1,0:T(8,128)(2,1)S(1)} %get-tuple-element.20), channel_id=1, source_target_pairs={{0,1},{1,0},{2,3},{3,2},{4,5},{5,4},{6,7},{7,6},{8,9},{9,8},{10,11... | collective-permute-start | bytes 786440 | tf_op jit(solution)/shard_map/ppermute | solution.py:35
  107.8 9.2 %collective-permute-start.17 = (bf16[256,512]{1,0:T(8,128)(2,1)S(1)}, bf16[256,512]{1,0:T(8,128)(2,1)S(1)}, u32[]{:S(2)}, u32[]{:S(2)}) collective-permute-start(bf16[256,512]{1,0:T(8,128)(2,1)S(1)} %get-tuple-element.20), channel_id=1, source_target_pairs={{0,4},{1,5},{2,6},{3,7},{4,0},{5,1},{6,2},{7,3},{8,12},{9,13},{10,... | collective-permute-start | bytes 786440 | tf_op jit(solution)/shard_map/ppermute | solution.py:35
  110.1 9.6 %collective-permute-start.15 = (bf16[256,512]{1,0:T(8,128)(2,1)S(1)}, bf16[256,512]{1,0:T(8,128)(2,1)S(1)}, u32[]{:S(2)}, u32[]{:S(2)}) collective-permute-start(bf16[256,512]{1,0:T(8,128)(2,1)S(1)} %get-tuple-element.20), channel_id=1, source_target_pairs={{0,2},{1,3},{2,0},{3,1},{4,6},{5,7},{6,4},{7,5},{8,10},{9,11},{10,... | collective-permute-start | bytes 786440 | tf_op jit(solution)/shard_map/ppermute | solution.py:35
  111.6 8.6 %collective-permute-start.21 = (bf16[256,512]{1,0:T(8,128)(2,1)S(1)}, bf16[256,512]{1,0:T(8,128)(2,1)S(1)}, u32[]{:S(2)}, u32[]{:S(2)}) collective-permute-start(bf16[256,512]{1,0:T(8,128)(2,1)S(1)} %get-tuple-element.36), channel_id=1, source_target_pairs={{0,1},{1,0},{2,3},{3,2},{4,5},{5,4},{6,7},{7,6},{8,9},{9,8},{10,11... | collective-permute-start | bytes 786440 | tf_op jit(solution)/shard_map/ppermute | solution.py:35
  113.7 16.9 %collective-permute-start.19 = (bf16[256,512]{1,0:T(8,128)(2,1)S(1)}, bf16[256,512]{1,0:T(8,128)(2,1)S(1)}, u32[]{:S(2)}, u32[]{:S(2)}) collective-permute-start(bf16[256,512]{1,0:T(8,128)(2,1)S(1)} %get-tuple-element.20), channel_id=1, source_target_pairs={{0,6},{1,7},{2,4},{3,5},{4,2},{5,3},{6,0},{7,1},{8,14},{9,15},{10,... | collective-permute-start | bytes 786440 | tf_op jit(solution)/shard_map/ppermute | solution.py:35
  113.8 16.7 %collective-permute-start.22 = (bf16[256,512]{1,0:T(8,128)(2,1)S(1)}, bf16[256,512]{1,0:T(8,128)(2,1)S(1)}, u32[]{:S(2)}, u32[]{:S(2)}) collective-permute-start(bf16[256,512]{1,0:T(8,128)(2,1)S(1)} %get-tuple-element.36), channel_id=1, source_target_pairs={{0,2},{1,3},{2,0},{3,1},{4,6},{5,7},{6,4},{7,5},{8,10},{9,11},{10,... | collective-permute-start | bytes 786440 | tf_op jit(solution)/shard_map/ppermute | solution.py:35
  117.0 18.1 %collective-permute-start.26 = (bf16[256,512]{1,0:T(8,128)(2,1)S(1)}, bf16[256,512]{1,0:T(8,128)(2,1)S(1)}, u32[]{:S(2)}, u32[]{:S(2)}) collective-permute-start(bf16[256,512]{1,0:T(8,128)(2,1)S(1)} %get-tuple-element.36), channel_id=1, source_target_pairs={{0,6},{1,7},{2,4},{3,5},{4,2},{5,3},{6,0},{7,1},{8,14},{9,15},{10,... | collective-permute-start | bytes 786440 | tf_op jit(solution)/shard_map/ppermute | solution.py:35
  119.7 15.4 %collective-permute-start.24 = (bf16[256,512]{1,0:T(8,128)(2,1)S(1)}, bf16[256,512]{1,0:T(8,128)(2,1)S(1)}, u32[]{:S(2)}, u32[]{:S(2)}) collective-permute-start(bf16[256,512]{1,0:T(8,128)(2,1)S(1)} %get-tuple-element.36), channel_id=1, source_target_pairs={{0,4},{1,5},{2,6},{3,7},{4,0},{5,1},{6,2},{7,3},{8,12},{9,13},{10,... | collective-permute-start | bytes 786440 | tf_op jit(solution)/shard_map/ppermute | solution.py:35
  120.2 15.4 %collective-permute-start.16 = (bf16[256,512]{1,0:T(8,128)(2,1)S(1)}, bf16[256,512]{1,0:T(8,128)(2,1)S(1)}, u32[]{:S(2)}, u32[]{:S(2)}) collective-permute-start(bf16[256,512]{1,0:T(8,128)(2,1)S(1)} %collective-permute-done.15), channel_id=1, source_target_pairs={{0,1},{1,0},{2,3},{3,2},{4,5},{5,4},{6,7},{7,6},{8,9},{9,8},{10,11... | collective-permute-start | bytes 786440 | tf_op jit(solution)/shard_map/ppermute | solution.py:35
  130.6 5.2 %collective-permute-start.18 = (bf16[256,512]{1,0:T(8,128)(2,1)S(1)}, bf16[256,512]{1,0:T(8,128)(2,1)S(1)}, u32[]{:S(2)}, u32[]{:S(2)}) collective-permute-start(bf16[256,512]{1,0:T(8,128)(2,1)S(1)} %collective-permute-done.17), channel_id=1, source_target_pairs={{0,1},{1,0},{2,3},{3,2},{4,5},{5,4},{6,7},{7,6},{8,9},{9,8},{10,11... | collective-permute-start | bytes 786440 | tf_op jit(solution)/shard_map/ppermute | solution.py:35
  130.6 12.9 %collective-permute-start.23 = (bf16[256,512]{1,0:T(8,128)(2,1)S(1)}, bf16[256,512]{1,0:T(8,128)(2,1)S(1)}, u32[]{:S(2)}, u32[]{:S(2)}) collective-permute-start(bf16[256,512]{1,0:T(8,128)(2,1)S(1)} %collective-permute-done.22), channel_id=1, source_target_pairs={{0,1},{1,0},{2,3},{3,2},{4,5},{5,4},{6,7},{7,6},{8,9},{9,8},{10,11... | collective-permute-start | bytes 786440 | tf_op jit(solution)/shard_map/ppermute | solution.py:35
  135.1 1.5 collective-permute-start.20
  135.1 8.5 %collective-permute-start.27 = (bf16[256,512]{1,0:T(8,128)(2,1)S(1)}, bf16[256,512]{1,0:T(8,128)(2,1)S(1)}, u32[]{:S(2)}, u32[]{:S(2)}) collective-permute-start(bf16[256,512]{1,0:T(8,128)(2,1)S(1)} %collective-permute-done.26), channel_id=1, source_target_pairs={{0,1},{1,0},{2,3},{3,2},{4,5},{5,4},{6,7},{7,6},{8,9},{9,8},{10,11... | collective-permute-start | bytes 786440 | tf_op jit(solution)/shard_map/ppermute | solution.py:35
  135.6 7.9 %collective-permute-start.25 = (bf16[256,512]{1,0:T(8,128)(2,1)S(1)}, bf16[256,512]{1,0:T(8,128)(2,1)S(1)}, u32[]{:S(2)}, u32[]{:S(2)}) collective-permute-start(bf16[256,512]{1,0:T(8,128)(2,1)S(1)} %collective-permute-done.24), channel_id=1, source_target_pairs={{0,1},{1,0},{2,3},{3,2},{4,5},{5,4},{6,7},{7,6},{8,9},{9,8},{10,11... | collective-permute-start | bytes 786440 | tf_op jit(solution)/shard_map/ppermute | solution.py:35
  136.6 7.0 %slice-start.2 = ((s8[6291456]{0:T(1024)(128)(4,1)}), s8[4194304]{0:T(1024)(128)(4,1)S(1)}, s32[]{:S(2)}) async-start(s8[6291456]{0:T(1024)(128)(4,1)} %bitcast.108), calls=%async_computation.2 | async-start | bytes 8388608
  136.6 7.0 %slice-start.3 = ((s8[6291456]{0:T(1024)(128)(4,1)}), s8[2097152]{0:T(1024)(128)(4,1)S(1)}, s32[]{:S(2)}) async-start(s8[6291456]{0:T(1024)(128)(4,1)} %bitcast.108), calls=%async_computation.3 | async-start | bytes 4194304
  150.7 8.7 %collective-permute-start.33 = (f32[8,128]{1,0:T(8,128)S(1)}, f32[8,128]{1,0:T(8,128)S(1)}, u32[]{:S(2)}, u32[]{:S(2)}) collective-permute-start(f32[8,128]{1,0:T(8,128)S(1)} %broadcast_in_dim.6), channel_id=1, source_target_pairs={{0,6},{1,7},{2,4},{3,5},{4,2},{5,3},{6,0},{7,1},{8,14},{9,15},{10,... | collective-permute-start | bytes 12296 | tf_op jit(solution)/shard_map/ppermute | solution.py:35
  153.5 6.0 %collective-permute-start.32 = (f32[8,128]{1,0:T(8,128)S(1)}, f32[8,128]{1,0:T(8,128)S(1)}, u32[]{:S(2)}, u32[]{:S(2)}) collective-permute-start(f32[8,128]{1,0:T(8,128)S(1)} %broadcast_in_dim.6), channel_id=1, source_target_pairs={{0,5},{1,4},{2,7},{3,6},{4,1},{5,0},{6,3},{7,2},{8,13},{9,12},{10,... | collective-permute-start | bytes 12296 | tf_op jit(solution)/shard_map/ppermute | solution.py:35
  156.0 35.6 %collective-permute-start.31 = (f32[8,128]{1,0:T(8,128)S(1)}, f32[8,128]{1,0:T(8,128)S(1)}, u32[]{:S(2)}, u32[]{:S(2)}) collective-permute-start(f32[8,128]{1,0:T(8,128)S(1)} %broadcast_in_dim.6), channel_id=1, source_target_pairs={{0,4},{1,5},{2,6},{3,7},{4,0},{5,1},{6,2},{7,3},{8,12},{9,13},{10,... | collective-permute-start | bytes 12296 | tf_op jit(solution)/shard_map/ppermute | solution.py:35
  157.5 36.9 %collective-permute-start.30 = (f32[8,128]{1,0:T(8,128)S(1)}, f32[8,128]{1,0:T(8,128)}, u32[]{:S(2)}, u32[]{:S(2)}) collective-permute-start(f32[8,128]{1,0:T(8,128)S(1)} %broadcast_in_dim.6), channel_id=1, source_target_pairs={{0,3},{1,2},{2,1},{3,0},{4,7},{5,6},{6,5},{7,4},{8,11},{9,10},{10,... | collective-permute-start | bytes 12296 | tf_op jit(solution)/shard_map/ppermute | solution.py:35
  158.0 37.8 %collective-permute-start.29 = (f32[8,128]{1,0:T(8,128)S(1)}, f32[8,128]{1,0:T(8,128)}, u32[]{:S(2)}, u32[]{:S(2)}) collective-permute-start(f32[8,128]{1,0:T(8,128)S(1)} %broadcast_in_dim.6), channel_id=1, source_target_pairs={{0,2},{1,3},{2,0},{3,1},{4,6},{5,7},{6,4},{7,5},{8,10},{9,11},{10,... | collective-permute-start | bytes 12296 | tf_op jit(solution)/shard_map/ppermute | solution.py:35
  159.5 36.6 %collective-permute-start.34 = (f32[8,128]{1,0:T(8,128)S(1)}, f32[8,128]{1,0:T(8,128)}, u32[]{:S(2)}, u32[]{:S(2)}) collective-permute-start(f32[8,128]{1,0:T(8,128)S(1)} %broadcast_in_dim.6), channel_id=1, source_target_pairs={{0,7},{1,6},{2,5},{3,4},{4,3},{5,2},{6,1},{7,0},{8,15},{9,14},{10,... | collective-permute-start | bytes 12296 | tf_op jit(solution)/shard_map/ppermute | solution.py:35
  159.5 36.6 %collective-permute-start.28 = (f32[8,128]{1,0:T(8,128)S(1)}, f32[8,128]{1,0:T(8,128)}, u32[]{:S(2)}, u32[]{:S(2)}) collective-permute-start(f32[8,128]{1,0:T(8,128)S(1)} %broadcast_in_dim.6), channel_id=1, source_target_pairs={{0,1},{1,0},{2,3},{3,2},{4,5},{5,4},{6,7},{7,6},{8,9},{9,8},{10,11... | collective-permute-start | bytes 12296 | tf_op jit(solution)/shard_map/ppermute | solution.py:35
  191.6 17.4 %collective-permute-start.36 = (f32[384,128]{0,1:T(8,128)}, f32[384,128]{0,1:T(8,128)}, u32[]{:S(2)}, u32[]{:S(2)}) collective-permute-start(f32[384,128]{0,1:T(8,128)} %bitcast.107), channel_id=1, source_target_pairs={{0,16},{8,24},{16,0},{24,8},{1,17},{9,25},{17,1},{25,9},{2,18},{10... | collective-permute-start | bytes 589832 | tf_op jit(solution)/shard_map/ppermute | solution.py:35
  194.4 40.0 %collective-permute-start.37 = (f32[384,128]{0,1:T(8,128)}, f32[384,128]{0,1:T(8,128)}, u32[]{:S(2)}, u32[]{:S(2)}) collective-permute-start(f32[384,128]{0,1:T(8,128)} %bitcast.106), channel_id=1, source_target_pairs={{0,24},{8,16},{16,8},{24,0},{1,25},{9,17},{17,9},{25,1},{2,26},{10... | collective-permute-start | bytes 589832 | tf_op jit(solution)/shard_map/ppermute | solution.py:35
  195.7 38.7 %collective-permute-start.35 = (f32[384,128]{0,1:T(8,128)}, f32[384,128]{0,1:T(8,128)}, u32[]{:S(2)}, u32[]{:S(2)}) collective-permute-start(f32[384,128]{0,1:T(8,128)} %bitcast.105), channel_id=1, source_target_pairs={{0,8},{8,0},{16,24},{24,16},{1,9},{9,1},{17,25},{25,17},{2,10},{10... | collective-permute-start | bytes 589832 | tf_op jit(solution)/shard_map/ppermute | solution.py:35
  198.1 10.9 %copy-start = (f32[1,1536,1024]{1,2,0:T(8,128)S(1)}, f32[1,1536,1024]{1,2,0:T(8,128)}, u32[]{:S(2)}) copy-start(f32[1,1536,1024]{1,2,0:T(8,128)} %copy.15) | copy-start | bytes 18874372
  200.6 0.9 copy-start.2
  202.2 32.2 %collective-permute-start.38 = (bf16[384,128]{0,1:T(8,128)(2,1)}, bf16[384,128]{0,1:T(8,128)(2,1)}, u32[]{:S(2)}, u32[]{:S(2)}) collective-permute-start(bf16[384,128]{0,1:T(8,128)(2,1)} %get-tuple-element.32), channel_id=1, source_target_pairs={{0,8},{8,0},{16,24},{24,16},{1,9},{9,1},{17,25},{25,17},{2,10},{10... | collective-permute-start | bytes 294920 | tf_op jit(solution)/shard_map/ppermute | solution.py:35
  203.9 30.5 %collective-permute-start.40 = (bf16[384,128]{0,1:T(8,128)(2,1)}, bf16[384,128]{0,1:T(8,128)(2,1)}, u32[]{:S(2)}, u32[]{:S(2)}) collective-permute-start(bf16[384,128]{0,1:T(8,128)(2,1)} %get-tuple-element.33), channel_id=1, source_target_pairs={{0,24},{8,16},{16,8},{24,0},{1,25},{9,17},{17,9},{25,1},{2,26},{10... | collective-permute-start | bytes 294920 | tf_op jit(solution)/shard_map/ppermute | solution.py:35
  209.0 25.4 %collective-permute-start.39 = (bf16[384,128]{0,1:T(8,128)(2,1)}, bf16[384,128]{0,1:T(8,128)(2,1)}, u32[]{:S(2)}, u32[]{:S(2)}) collective-permute-start(bf16[384,128]{0,1:T(8,128)(2,1)} %get-tuple-element.34), channel_id=1, source_target_pairs={{0,16},{8,24},{16,0},{24,8},{1,17},{9,25},{17,1},{25,9},{2,18},{10... | collective-permute-start | bytes 294920 | tf_op jit(solution)/shard_map/ppermute | solution.py:35
  227.7 6.7 %copy-start.3 = (f32[1536,128]{0,1:T(8,128)S(1)}, f32[1536,128]{0,1:T(8,128)}, u32[]{:S(2)}) copy-start(f32[1536,128]{0,1:T(8,128)} %copy-done.2) | copy-start | bytes 2359300
  227.7 6.7 %copy-start.8 = (f32[1,384,128]{1,2,0:T(8,128)S(1)}, f32[1,384,128]{1,2,0:T(8,128)}, u32[]{:S(2)}) copy-start(f32[1,384,128]{1,2,0:T(8,128)} %copy.24) | copy-start | bytes 589828
  234.4 22.4 %copy-start.1 = (f32[1,1536,128]{1,2,0:T(8,128)S(1)}, f32[1,1536,128]{1,2,0:T(8,128)}, u32[]{:S(2)}) copy-start(f32[1,1536,128]{1,2,0:T(8,128)} %copy.19) | copy-start | bytes 2359300
  236.1 20.6 %collective-permute-start.43 = (f32[384,128]{0,1:T(8,128)S(1)}, f32[384,128]{0,1:T(8,128)S(1)}, u32[]{:S(2)}, u32[]{:S(2)}) collective-permute-start(f32[384,128]{0,1:T(8,128)S(1)} %get-tuple-element.15), channel_id=1, source_target_pairs={{0,24},{8,16},{16,8},{24,0},{1,25},{9,17},{17,9},{25,1},{2,26},{10... | collective-permute-start | bytes 589832 | tf_op jit(solution)/shard_map/ppermute | solution.py:35
  239.1 17.6 %collective-permute-start.42 = (f32[384,128]{0,1:T(8,128)S(1)}, f32[384,128]{0,1:T(8,128)S(1)}, u32[]{:S(2)}, u32[]{:S(2)}) collective-permute-start(f32[384,128]{0,1:T(8,128)S(1)} %get-tuple-element.15), channel_id=1, source_target_pairs={{0,16},{8,24},{16,0},{24,8},{1,17},{9,25},{17,1},{25,9},{2,18},{10... | collective-permute-start | bytes 589832 | tf_op jit(solution)/shard_map/ppermute | solution.py:35
  241.1 10.8 %collective-permute-start.41 = (f32[384,128]{0,1:T(8,128)S(1)}, f32[384,128]{0,1:T(8,128)}, u32[]{:S(2)}, u32[]{:S(2)}) collective-permute-start(f32[384,128]{0,1:T(8,128)S(1)} %get-tuple-element.15), channel_id=1, source_target_pairs={{0,8},{8,0},{16,24},{24,16},{1,9},{9,1},{17,25},{25,17},{2,10},{10... | collective-permute-start | bytes 589832 | tf_op jit(solution)/shard_map/ppermute | solution.py:35

commit v2 on v0

v2 whole, which is shorter than its diff:
```python
import functools

import jax
import jax.numpy as jnp
from jax import lax
from jax.experimental import pallas as pl
from jax.experimental.pallas import tpu as pltpu
from jax.sharding import Mesh, PartitionSpec as P

HEAD = 128
WARMUP = 2000
STEPS_TOTAL = 100000
FRAG_COLS = 128


BETA_ONE = 0.9
BETA_TWO = 0.95
ADAM_EPS = 1e-08
DECAY = 0.1
PEAK_RATE = 0.0003
CLIP_NORM = 1.0
OUTER_MU = 0.9
OUTER_RATE = 0.7
MIX_LOCAL = 0.5

MIB = 1 << 20
ANY = pl.BlockSpec(memory_space=pl.ANY)
BLOCKS = ("chip", "core")


def params_of(limit):
    return pltpu.CompilerParams(vmem_limit_bytes=limit * MIB)


def cost(flops, moved):
    return pl.CostEstimate(flops=int(flops), bytes_accessed=int(moved), transcendentals=0)


def pack_kernel(first, count, rows, tok_ref, out_ref, sems):
    def copy(s):
        return pltpu.make_async_copy(
            tok_ref.at[pl.ds(first, count), pl.ds(s * rows, rows)], out_ref.at[s], sems.at[s]
        )

    shards = out_ref.shape[0]
    for s in range(shards):
        copy(s).start()
    for s in range(shards):
        copy(s).wait()


def pack(tokens, first, count, rows):
    shards = tokens.shape[1] // rows
    return pl.pallas_call(
        functools.partial(pack_kernel, first, count, rows),
        out_shape=jax.ShapeDtypeStruct((shards, count, rows), tokens.dtype),
        in_specs=[ANY],
        out_specs=ANY,
        scratch_shapes=[pltpu.SemaphoreType.DMA((shards,))],
        cost_estimate=cost(0, 4 * shards * count * rows),
        name="pack",
    )(tokens)


def transpose_kernel(core_ref, x_ref, out_ref):
    out_ref[...] = x_ref[0, 0].T


def transpose_tokens(blocks, core):
    chips, cores, count, rows = blocks.shape
    return pl.pallas_call(
        transpose_kernel,
        out_shape=jax.ShapeDtypeStruct((rows, chips * cores * count), blocks.dtype),
        grid_spec=pltpu.PrefetchScalarGridSpec(
            num_scalar_prefetch=1,
            grid=(cores, chips),
            in_specs=[pl.BlockSpec((1, 1, count, rows), lambda o, c, core: (c, (core[0] + o) % 2, 0, 0))],
            out_specs=pl.BlockSpec((rows, count), lambda o, c, core: (0, o * chips + c)),
        ),
        compiler_params=params_of(16),
        cost_estimate=cost(0, 4 * blocks.size),
        name="transpose_tokens",
    )(core, blocks)


def key_kernel(part_ref, cot_ref, out_ref):
    raw = jnp.sum(part_ref[...].astype(jnp.float32), axis=0)
    for h in range(raw.shape[1] // HEAD):
        cols = slice(h * HEAD, (h + 1) * HEAD)
        head = raw[:, cols]
        inverse = lax.rsqrt(jnp.mean(head * head, axis=1, keepdims=True) + 1e-06)
        normed = head * inverse
        upper = cot_ref[:, cols].astype(jnp.float32)
        back = inverse * (upper - normed * jnp.mean(upper * normed, axis=1, keepdims=True))
        back = back.astype(out_ref.dtype)
        for c in range(out_ref.shape[0]):
            out_ref[c, :, cols] = back


def key_backward(parts, incoming):
    return pl.pallas_call(
        key_kernel,
        out_shape=jax.ShapeDtypeStruct(parts.shape, jnp.bfloat16),
        compiler_params=params_of(16),
        cost_estimate=cost(20 * parts.size, 4 * parts.size),
        name="key_backward",
    )(parts, incoming)


def grad_kernel(halves, has_base, last, *refs):
    refs = list(refs)
    terms = [(refs.pop(0), refs.pop(0), refs.pop(0)) for _ in range(halves)]
    base = refs.pop(0) if has_base else None
    square_in = refs.pop(0) if last and has_base else None
    out_ref = refs.pop(0)
    total = None
    for x_ref, same_ref, other_ref in terms:
        depth = same_ref.shape[0]
        for ref, at in ((same_ref, 0), (other_ref, depth)):
            term = jnp.dot(x_ref[:, at:at + depth], ref[...], preferred_element_type=jnp.float32)
            total = term if total is None else total + term
    if base is not None:
        total = total + base[...]
    out_ref[...] = total
    if last:
        sq_ref = refs.pop(0)

        @pl.when(pl.program_id(0) == 0)
        def _():
            sq_ref[...] = square_in[...] if square_in is not None else jnp.zeros_like(sq_ref)

        rows, width = total.shape
        squares = (total * total).reshape(rows // 8, 8, width).sum(axis=0)
        folded = squares[:, :HEAD]
        for h in range(1, width // HEAD):
            folded = folded + squares[:, h * HEAD:(h + 1) * HEAD]
        sq_ref[...] += folded


def gradient(terms, base=None, square=None, last=True):
    rows = terms[0][0].shape[0]
    width = terms[0][1].shape[1]
    step = 256 if rows % 256 == 0 else rows
    row_block = lambda cols: pl.BlockSpec((step, cols), lambda i: (i, 0))
    whole = lambda a: pl.BlockSpec(a.shape, lambda i: (0, 0))
    args, specs = [], []
    for x, same, other in terms:
        args += [x, same, other]
        specs += [row_block(x.shape[1]), whole(same), whole(other)]
    if base is not None:
        args.append(base)
        specs.append(row_block(width))
        if last:
            args.append(square)
            specs.append(whole(square))
    shapes = [jax.ShapeDtypeStruct((rows, width), jnp.float32)]
    outs = [row_block(width)]
    if last:
        shapes.append(jax.ShapeDtypeStruct((8, HEAD), jnp.float32))
        outs.append(pl.BlockSpec((8, HEAD), lambda i: (0, 0)))
    depth = sum(x.shape[1] for x, _, _ in terms)
    return pl.pallas_call(
        functools.partial(grad_kernel, len(terms), base is not None, last),
        out_shape=shapes,
        grid=(rows // step,),
        in_specs=specs,
        out_specs=outs,
        compiler_params=params_of(24),
        cost_estimate=cost(2 * rows * width * depth, 2 * rows * depth + 4 * rows * width),
        name="gradient",
    )(*args)


def adam(old, first, second, grad, scalars):
    factor, rate, inv_one, inv_two = (scalars[i] for i in range(4))
    clipped = grad * factor
    first_new = BETA_ONE * first + (1.0 - BETA_ONE) * clipped
    second_new = BETA_TWO * second + (1.0 - BETA_TWO) * clipped * clipped
    update = rate * (
        first_new * inv_one / (jnp.sqrt(second_new * inv_two) + ADAM_EPS) + DECAY * old
    )
    return update, first_new, second_new


def adam_kernel(sc_ref, w_ref, m_ref, v_ref, gk_ref, gv_ref, w_out, m_out, v_out):
    width = gk_ref.shape[1]
    for g_ref, cols in ((gk_ref, slice(0, width)), (gv_ref, slice(width, 2 * width))):
        old = w_ref[:, cols]
        update, first_new, second_new = adam(old, m_ref[:, cols], v_ref[:, cols], g_ref[...], sc_ref)
        w_out[:, cols] = old - update
        m_out[:, cols] = first_new
        v_out[:, cols] = second_new


def adam_all(scalars, w, m, v, gk, gv):
    rows, width = w.shape
    step = 128
    full = pl.BlockSpec((step, width), lambda i: (i, 0))
    half = pl.BlockSpec((step, width // 2), lambda i: (i, 0))
    return pl.pallas_call(
        adam_kernel,
        out_shape=[jax.ShapeDtypeStruct(w.shape, jnp.float32)] * 3,
        grid=(rows // step,),
        in_specs=[pl.BlockSpec(memory_space=pltpu.SMEM), full, full, full, half, half],
        out_specs=[full] * 3,
        compiler_params=params_of(16),
        cost_estimate=cost(20 * w.size, 28 * w.size),
        name="adam_all",
    )(scalars, w, m, v, gk, gv)


def frag_kernel(frag_ref, sc_ref, w_ref, m_ref, v_ref, gk_ref, gv_ref, out_ref):
    count = gk_ref.shape[1]
    grad = jnp.where(frag_ref[0] < frag_ref[1], gk_ref[...], gv_ref[...])
    update, _, _ = adam(w_ref[...], m_ref[...], v_ref[...], grad, sc_ref)
    del count
    out_ref[...] = update.astype(out_ref.dtype)


def adam_frag(frag, scalars, w, m, v, gk, gv):
    rows = w.shape[0]
    heads = gk.shape[1] // FRAG_COLS
    block = lambda at: pl.BlockSpec((rows, FRAG_COLS), at)
    due = block(lambda i, f: (0, f[0]))
    return pl.pallas_call(
        frag_kernel,
        out_shape=jax.ShapeDtypeStruct((rows, FRAG_COLS), jnp.bfloat16),
        grid_spec=pltpu.PrefetchScalarGridSpec(
            num_scalar_prefetch=1,
            grid=(1,),
            in_specs=[
                pl.BlockSpec(memory_space=pltpu.SMEM),
                due,
                due,
                due,
                block(lambda i, f: (0, jnp.minimum(f[0], heads - 1))),
                block(lambda i, f: (0, jnp.maximum(f[0] - heads, 0))),
            ],
            out_specs=block(lambda i, f: (0, 0)),
        ),
        compiler_params=params_of(16),
        cost_estimate=cost(20 * rows * FRAG_COLS, 22 * rows * FRAG_COLS),
        name="adam_frag",
    )(frag, scalars, w, m, v, gk, gv)


def columns_kernel(frag_ref, *refs):
    half = len(refs) // 2
    for src, dst in zip(refs[:half], refs[half:]):
        dst[...] = src[...]


def due_columns(frag, *arrays):
    specs = [pl.BlockSpec((a.shape[0], FRAG_COLS), lambda i, f: (0, f[0])) for a in arrays]
    outs = [pl.BlockSpec((a.shape[0], FRAG_COLS), lambda i, f: (0, 0)) for a in arrays]
    return pl.pallas_call(
        columns_kernel,
        out_shape=[jax.ShapeDtypeStruct((a.shape[0], FRAG_COLS), a.dtype) for a in arrays],
        grid_spec=pltpu.PrefetchScalarGridSpec(
            num_scalar_prefetch=1, grid=(1,), in_specs=specs, out_specs=outs
        ),
        compiler_params=params_of(16),
        cost_estimate=cost(0, sum(8 * a.shape[0] * FRAG_COLS for a in arrays)),
        name="due_columns",
    )(frag, *arrays)


def duplicate_kernel(*refs):
    half = (len(refs) - 1) // 2
    copies = [
        pltpu.make_async_copy(refs[i], refs[half + i], refs[-1].at[i]) for i in range(half)
    ]
    for copy in copies:
        copy.start()
    for copy in copies:
        copy.wait()


def duplicate(*arrays):
    return pl.pallas_call(
        duplicate_kernel,
        out_shape=[jax.ShapeDtypeStruct(a.shape, a.dtype) for a in arrays],
        in_specs=[ANY] * len(arrays),
        out_specs=[ANY] * len(arrays),
        scratch_shapes=[pltpu.SemaphoreType.DMA((len(arrays),))],
        cost_estimate=cost(0, sum(8 * a.size for a in arrays)),
        name="duplicate",
    )(*arrays)


def outer_kernel(
    share, frag_ref, w_ref, base_ref, sum_ref, a_ref, p_ref, m_ref, own_ref, w_out, a_out, m_out
):
    fresh = base_ref[...] - share * (1.0 + OUTER_MU) * OUTER_RATE * sum_ref[...].astype(jnp.float32)
    w_out[...] = MIX_LOCAL * w_ref[...] + (1.0 - MIX_LOCAL) * fresh
    pseudo = p_ref[...] + share * own_ref[...]
    new_moment = OUTER_MU * m_ref[...] + pseudo
    m_out[...] = new_moment
    a_out[...] = a_ref[...] - OUTER_RATE * (OUTER_MU * new_moment + pseudo)


def outer_step(frag, weights, base, update_sum, anchor, pseudo, momentum, own_sum, replicas):
    rows, part = weights.shape[0], anchor.shape[0]
    due = lambda count: pl.BlockSpec((count, FRAG_COLS), lambda i, f: (0, f[0]))
    plain = lambda count: pl.BlockSpec((count, FRAG_COLS), lambda i, f: (0, 0))
    return pl.pallas_call(
        functools.partial(outer_kernel, 1.0 / replicas),
        out_shape=[jax.ShapeDtypeStruct(a.shape, a.dtype) for a in (weights, anchor, momentum)],
        grid_spec=pltpu.PrefetchScalarGridSpec(
            num_scalar_prefetch=1,
            grid=(1,),
            in_specs=[due(rows), plain(rows), plain(rows), due(part), plain(part), due(part), plain(part)],
            out_specs=[due(rows), due(part), due(part)],
        ),
        input_output_aliases={1: 0, 4: 1, 6: 2},
        compiler_params=params_of(16),
        cost_estimate=cost(10 * rows * FRAG_COLS, 20 * rows * FRAG_COLS),
        name="outer_step",
    )(frag, weights, base, update_sum, anchor, pseudo, momentum, own_sum)


def exchange(blocks, axis):
    return lax.all_to_all(blocks, axis, split_axis=0, concat_axis=0, tiled=True)


def across(block):
    return lax.ppermute(block, "core", [(0, 1), (1, 0)])


def copies_of(block, count):
    return jnp.broadcast_to(block[None], (count,) + block.shape)


def body(
    tokens,
    cotangent,
    weights,
    first_moment,
    second_moment,
    anchor,
    momentum,
    due_fragment,
    step_count,
):
    inputs, incoming, params = tokens[0], cotangent[0], weights[0]
    tok_rows = inputs.shape[0]
    kv_width = incoming.shape[1] // 2
    rows = params.shape[0]
    part = anchor.shape[0]
    replicas = lax.axis_size("rep")
    chips = lax.axis_size("chip")
    core = lax.axis_index("core")
    core_one = jnp.reshape(core, (1,)).astype(jnp.int32)
    frag = jnp.stack([due_fragment[0], jnp.int32(kv_width // FRAG_COLS)])
    th = tok_rows // 2

    arrived = []
    for h in range(2):
        sent = pack(inputs, h * th, th, rows)
        arrived.append(exchange(sent, BLOCKS))

    key_weights = params[:, :kv_width].astype(jnp.bfloat16)
    flipped, keys = [], []
    for h in range(2):
        x = arrived[h]
        partial_keys = jnp.dot(
            x.reshape(-1, rows), key_weights, preferred_element_type=jnp.float32
        ).astype(jnp.bfloat16)
        partial_keys = partial_keys.reshape(chips, 2, th, kv_width)
        mine = lax.dynamic_index_in_dim(partial_keys, core, 1, keepdims=False)
        theirs = across(lax.dynamic_index_in_dim(partial_keys, 1 - core, 1, keepdims=False))
        summed = (mine.astype(jnp.float32) + theirs.astype(jnp.float32)).astype(jnp.bfloat16)
        parts = exchange(summed, "chip")
        back = key_backward(parts, incoming[h * th:(h + 1) * th, :kv_width])
        same = exchange(back, "chip")
        other = across(same)
        keys.append((same.reshape(-1, kv_width), other.reshape(-1, kv_width)))
        flipped.append(transpose_tokens(x.reshape(chips, 2, th, rows), core_one))

    values = incoming[:, kv_width:].reshape(2, th, kv_width)
    v_same = exchange(copies_of(values, chips), "chip")
    v_other = across(v_same)
    v_same = jnp.swapaxes(v_same, 0, 1).reshape(2, -1, kv_width)
    v_other = jnp.swapaxes(v_other, 0, 1).reshape(2, -1, kv_width)
    grad_values, square = gradient([(flipped[h], v_same[h], v_other[h]) for h in range(2)])
    grad_first = gradient([(flipped[0],) + keys[0]], last=False)[0]
    grad_keys, square = gradient([(flipped[1],) + keys[1]], grad_first, square)

    (old_cols,) = due_columns(frag, params)
    anchor_cols, moment_cols = due_columns(frag, anchor, momentum)
    old_sum = jnp.sum(exchange(old_cols.reshape(replicas, part, FRAG_COLS), "rep"), axis=0)
    pseudo_old = anchor_cols - old_sum / replicas
    base = anchor_cols - OUTER_RATE * (
        OUTER_MU * (OUTER_MU * moment_cols + pseudo_old) + pseudo_old
    )
    base = exchange(copies_of(base, replicas), "rep").reshape(rows, FRAG_COLS)
    anchor_copy, momentum_copy = duplicate(anchor, momentum)

    shards = 2 * chips
    square = jnp.sum(exchange(copies_of(square, shards), BLOCKS))
    factor = jnp.minimum(1.0, CLIP_NORM / (jnp.sqrt(square) + 1e-06))
    steps_now = step_count[0].astype(jnp.float32)
    plan = jnp.minimum(1.0, steps_now / WARMUP) * (
        0.55 + 0.45 * jnp.cos(jnp.pi * steps_now / STEPS_TOTAL)
    )
    rate = PEAK_RATE * plan
    inv_one = 1.0 / (1.0 - jnp.power(BETA_ONE, steps_now))
    inv_two = 1.0 / (1.0 - jnp.power(BETA_TWO, steps_now))
    scalars = jnp.stack([factor, rate, inv_one, inv_two])

    state = (params, first_moment[0], second_moment[0], grad_keys, grad_values)
    update = adam_frag(frag, scalars, *state)
    own_sum = jnp.sum(
        exchange(update.reshape(replicas, part, FRAG_COLS), "rep").astype(jnp.float32), axis=0
    )
    update_sum = exchange(copies_of(own_sum.astype(jnp.bfloat16), replicas), "rep")
    update_sum = update_sum.reshape(rows, FRAG_COLS)
    inner, first_out, second_out = adam_all(scalars, *state)
    weights_out, anchor_out, momentum_out = outer_step(
        frag, inner, base, update_sum, anchor_copy, pseudo_old, momentum_copy, own_sum, replicas
    )
    plan_out = jnp.reshape(plan, (1,))
    return (
        weights_out[None],
        first_out[None],
        second_out[None],
        anchor_out,
        momentum_out,
        plan_out,
    )


def solution(mesh):
    replicas, shards = mesh.shape["rep"], mesh.shape["fsdp"]
    fine = Mesh(mesh.devices.reshape(replicas, shards // 2, 2), ("rep",) + BLOCKS)
    tokens_spec = P("rep", BLOCKS, None)
    outer_spec = P(BLOCKS + ("rep",), None)
    return jax.shard_map(
        body,
        mesh=fine,
        in_specs=(tokens_spec,) * 5 + (outer_spec,) * 2 + (P(), P()),
        out_specs=(tokens_spec,) * 3 + (outer_spec,) * 2 + (P(),),
        check_vma=False,
    )
```

time: 363 us -> 529 us (1.46)
  Pallas kernels: 0 us -> 329 us
  waiting for transfers between devices: 173 us -> 77.5 us
  starting transfers between devices: 5.05 us -> 51.7 us
  blocking collectives: 30.4 us -> 0 us
  other arithmetic: 40.1 us -> 10.4 us
  local copies, waits for them, and re-layouts: 68.5 us -> 45.2 us
  matrix products: 27.8 us -> 8.31 us
  between operations: 17.2 us -> 4.42 us
    pallas_call x0 -> x15, Pallas kernels: none -> 329 us  [the longest x2 193 us: pack(): pl.pallas_call(functools.partial(pack_kernel, first, count, rows), out_sh...]
    all_gather x2 -> x0, waiting for transfers between devices: 74.7 us -> none  [the longest x1 74.7 us: body(): lax.all_gather(key_weights, 'fsdp', axis=0, tiled=True)]
    all_to_all x1 -> x12, starting transfers between devices: 4.74 us -> 51.2 us  [exchange(): return lax.all_to_all(blocks, axis, split_axis=0, concat_axis=0, tiled=True)]
    while x32 -> x0, local copies, waits for them, and re-layouts: 27.5 us -> none
    dot_general x9 -> x2, matrix products: 27.8 us -> 8.31 us  [body(): jnp.dot(x.reshape(-1, rows), key_weights, preferred_element_type=jnp.floa...]
    all_gather x1 -> x0, blocking collectives: 18 us -> none  [body(): fresh = lax.all_gather(new_anchor, 'rep', axis=0, tiled=True)]
    unnamed x14 -> x40, local copies, waits for them, and re-layouts: 14.9 us -> 32.8 us
    add x8 -> x0, other arithmetic: 17.1 us -> none  [one_block(): return carried + partial_sum.astype(jnp.float32)]
  transfers between devices with their start and end apart: 4 -> 17, of which waited for: 3 -> 10; matrix products, arithmetic and copies ran while one was open for 5% -> 5% of each run, Pallas kernels for 0% -> 43%
where the time goes in v2:
time: 529 us; the launch traced here: 527 us
  Pallas kernels  329 us (62%)
  waiting for transfers between devices  77.5 us (15%)
  starting transfers between devices  51.7 us (10%)
  local copies, waits for them, and re-layouts  45.2 us (9%)
  other arithmetic  10.4 us (2%)
  matrix products  8.31 us (2%)
    pallas_call x2, Pallas kernels, pack(): pl.pallas_call(functools.partial(pack_kernel, first, count, rows), out_sh...  193 us
    pallas_call x1, Pallas kernels, duplicate(): pl.pallas_call(duplicate_kernel, out_shape=[jax.ShapeDtypeStruct(a.shape,...  96.4 us
    all_to_all x12, waiting for transfers between devices, exchange(): return lax.all_to_all(blocks, axis, split_axis=0, concat_axis=0, tiled=True)  77.5 us
    all_to_all x12, starting transfers between devices, exchange(): return lax.all_to_all(blocks, axis, split_axis=0, concat_axis=0, tiled=True)  51.2 us
    unnamed x40, local copies, waits for them, and re-layouts  32.8 us
    pallas_call x3, Pallas kernels, gradient(): pl.pallas_call(functools.partial(grad_kernel, len(terms), base is not Non...  12.3 us
  transfers between devices with their start and end apart: 17, of which 10 were waited for; matrix products, arithmetic and copies ran while one was open for 5% of the time, Pallas kernels for 43%

profile of v2, /device:TPU:0, one launch (start us, length us, event | category | flops | bytes accessed | tf_op | source)
XLA Modules:
  0.0 526.6 jit_solution(10065268177965572339)
XLA Ops:
  0.6 96.5 %pack.3 = bf16[8,128,1536]{2,1,0:T(8,128)(2,1)} custom-call(bf16[256,12288]{1,0:T(8,128)(2,1)} %bitcast.64), custom_call_target="tpu_custom_call" | custom-call | bytes 6291456 | tf_op jit(solution)/shard_map/pack/pallas_call | solution.py:54
  97.1 5.2 all-to-all-start.3
  102.3 96.5 %pack.2 = bf16[8,128,1536]{2,1,0:T(8,128)(2,1)} custom-call(bf16[256,12288]{1,0:T(8,128)(2,1)} %bitcast.65), custom_call_target="tpu_custom_call" | custom-call | bytes 6291456 | tf_op jit(solution)/shard_map/pack/pallas_call | solution.py:54
  198.8 4.4 all-to-all-start
  203.2 1.0 slice.40
  204.2 3.7 convolution_convert_fusion
  207.9 1.0 copy-done.18
  208.9 0.8 dynamic-slice_bitcast_fusion
  210.2 30.9 %all-to-all-done = bf16[8,128,1536]{2,1,0:T(8,128)(2,1)} async-done(((bf16[8,128,1536]{2,1,0:T(8,128)(2,1)}), bf16[8,128,1536]{2,1,0:T(8,128)(2,1)}, u32[]{:S(2)}, u32[]{:S(2)}) %all-to-all-start) | async-done | bytes 3145760 | tf_op jit(solution)/shard_map/all_to_all | solution.py:323
  241.1 1.1 broadcast_in_dim.17
  242.2 4.3 all-to-all-start.6
  246.4 4.6 convolution_convert_fusion.1
  251.1 1.0 copy-done.19
  252.9 2.1 fusion
  255.0 4.3 all-to-all-done.6
  259.3 4.1 all-to-all-start.4
  263.5 2.1 fusion.1
  265.6 4.5 all-to-all-done.4.part_ref
  270.1 4.2 all-to-all-start.1
  274.4 1.0 fusion.4
  275.4 1.3 key_backward.3
  277.5 3.5 all-to-all-done.1.part_ref
  280.9 4.1 all-to-all-start.5
  285.1 1.3 key_backward.2
  287.2 4.5 all-to-all-done.5
  291.7 4.2 all-to-all-start.2
  296.6 2.2 fusion.3
  298.8 3.7 all-to-all-done.2
  302.6 1.3 fusion.2
  303.8 2.2 transpose_tokens.3.refs_0_
  306.0 5.5 %transpose_tokens.2.refs_3_.refs_0_ = bf16[1536,1024]{1,0:T(8,128)(2,1)S(1)} custom-call(s32[1]{0:T(128)} %bitcast.core_ref, bf16[4,2,128,1536]{3,2,1,0:T(8,128)(2,1)} %bitcast.2.x_ref), custom_call_target="tpu_custom_call" | custom-call | bytes 6291456 | tf_op jit(solution)/shard_map/transpose_tokens/pallas_call | solution.py:71
  311.6 4.5 gradient.4
  316.1 3.9 gradient.3.refs_3_
  320.0 4.0 gradient.5
  324.0 1.7 copy-done.7
  326.2 3.3 all-to-all-start.7
  329.7 2.8 copy-done
  333.1 0.9 copy-done.12
  334.3 4.9 all-to-all-start.8
  341.5 2.8 copy-done.1
  344.3 2.8 copy-done.3
  347.1 2.8 copy-done.5
  349.9 1.9 copy-done.8
  351.8 2.5 adam_frag.1
  354.3 5.4 %all-to-all-done.8 = f32[4,384,128]{2,1,0:T(8,128)} async-done(((f32[4,384,128]{2,1,0:T(8,128)}), f32[4,384,128]{2,1,0:T(8,128)}, u32[]{:S(2)}, u32[]{:S(2)}) %all-to-all-start.8) | async-done | bytes 786464 | tf_op jit(solution)/shard_map/all_to_all | solution.py:323
  359.7 4.1 all-to-all-start.10
  363.8 1.4 copy-done.10
  365.2 1.4 copy-done.11
  367.9 1.9 reduce_sum.28
  369.8 1.8 multiply_subtract_fusion.1
  371.5 3.6 all-to-all-done.10
  375.1 1.9 broadcast_in_dim.37
  376.9 4.2 all-to-all-start.9
  381.2 1.1 convert_reduce_fusion.own_ref
  382.9 16.6 %all-to-all-done.9 = f32[4,384,128]{2,1,0:T(8,128)} async-done(((f32[4,384,128]{2,1,0:T(8,128)}), f32[4,384,128]{2,1,0:T(8,128)}, u32[]{:S(2)}, u32[]{:S(2)}) %all-to-all-start.9) | async-done | bytes 786464 | tf_op jit(solution)/shard_map/all_to_all | solution.py:323
  399.5 1.7 broadcast_in_dim.38
  401.2 4.1 all-to-all-start.11
  405.3 96.4 %duplicate.1 = (f32[384,1024]{1,0:T(8,128)}, f32[384,1024]{1,0:T(8,128)}) custom-call(f32[384,1024]{1,0:T(8,128)} %refs_0_.3, f32[384,1024]{1,0:T(8,128)} %refs_1_.3), custom_call_target="tpu_custom_call" | custom-call | bytes 6291456 | tf_op jit(solution)/shard_map/duplicate/pallas_call | solution.py:280
  501.8 2.8 copy-done.2
  504.5 2.8 copy-done.4
  507.3 2.8 copy-done.6
  510.1 1.9 copy-done.9
  512.0 10.2 %adam_all.1 = (f32[1536,1024]{1,0:T(8,128)}, f32[1536,1024]{1,0:T(8,128)}, f32[1536,1024]{1,0:T(8,128)}) custom-call(f32[4]{0:T(128)S(1)} %pad_maximum_fusion.sc_ref, f32[1536,1024]{1,0:T(8,128)S(1)} %bitcast.51, f32[1536,1024]{1,0:T(8,128)S(1)} %bitcast.53, f32[1536,1024]{1,0:T(8,128)S(1)} %bitcast.55, f32[1536,512]{1,0:T(8,128)S(1)} %copy-done.9, ...), custom_call_target="tpu_custom_call" | custom-call | flops 31457280 | bytes 44040192 | tf_op jit(solution)/shard_map/adam_all/pallas_call | solution.py:200
  522.2 3.2 outer_step.1
  (46 shorter events, 7.4 us)
Async XLA Ops:
  97.1 101.7 %all-to-all-start.3 = ((bf16[8,128,1536]{2,1,0:T(8,128)(2,1)}), bf16[8,128,1536]{2,1,0:T(8,128)(2,1)S(1)}, u32[]{:S(2)}, u32[]{:S(2)}) async-start(bf16[8,128,1536]{2,1,0:T(8,128)(2,1)} %pack.3), calls=%async_computation.3 | async-start | bytes 6291456 | tf_op jit(solution)/shard_map/all_to_all | solution.py:323
  198.8 42.3 %all-to-all-start = ((bf16[8,128,1536]{2,1,0:T(8,128)(2,1)}), bf16[8,128,1536]{2,1,0:T(8,128)(2,1)}, u32[]{:S(2)}, u32[]{:S(2)}) async-start(bf16[8,128,1536]{2,1,0:T(8,128)(2,1)} %pack.2), calls=%async_computation | async-start | bytes 6291456 | tf_op jit(solution)/shard_map/all_to_all | solution.py:323
  207.9 1.0 copy-start.18
  209.7 43.2 %collective-permute-start.2 = (bf16[4,128,512]{2,1,0:T(8,128)(2,1)}, bf16[4,128,512]{2,1,0:T(8,128)(2,1)}, u32[]{:S(2)}, u32[]{:S(2)}) collective-permute-start(bf16[4,128,512]{2,1,0:T(8,128)(2,1)} %dynamic-slice_bitcast_fusion), channel_id=1, source_target_pairs={{0,1},{1,0},{2,3},{3,2},{4,5},{5,4},{6,7},{7,6},{8,9},{9,8},{10,11... | collective-permute-start | bytes 1572872 | tf_op jit(solution)/shard_map/ppermute | solution.py:327
  242.2 17.2 %all-to-all-start.6 = ((bf16[4,2,128,512]{3,2,1,0:T(8,128)(2,1)}), bf16[4,2,128,512]{3,2,1,0:T(8,128)(2,1)}, u32[]{:S(2)}, u32[]{:S(2)}) async-start(bf16[4,2,128,512]{3,2,1,0:T(8,128)(2,1)} %broadcast_in_dim.17), calls=%async_computation.6 | async-start | bytes 2097152 | tf_op jit(solution)/shard_map/all_to_all | solution.py:323
  251.1 1.0 copy-start.19
  252.9 10.6 %collective-permute-start = (bf16[4,128,512]{2,1,0:T(8,128)(2,1)}, bf16[4,128,512]{2,1,0:T(8,128)(2,1)}, u32[]{:S(2)}, u32[]{:S(2)}) collective-permute-start(bf16[4,128,512]{2,1,0:T(8,128)(2,1)} %dynamic-slice_bitcast_fusion.1), channel_id=1, source_target_pairs={{0,1},{1,0},{2,3},{3,2},{4,5},{5,4},{6,7},{7,6},{8,9},{9,8},{10,11... | collective-permute-start | bytes 1572872 | tf_op jit(solution)/shard_map/ppermute | solution.py:327
  259.3 10.8 %all-to-all-start.4 = ((bf16[4,128,512]{2,1,0:T(8,128)(2,1)}), bf16[4,128,512]{2,1,0:T(8,128)(2,1)}, u32[]{:S(2)}, u32[]{:S(2)}) async-start(bf16[4,128,512]{2,1,0:T(8,128)(2,1)} %fusion), calls=%async_computation.4 | async-start | bytes 1048576 | tf_op jit(solution)/shard_map/all_to_all | solution.py:323
  270.1 10.8 %all-to-all-start.1 = ((bf16[4,128,512]{2,1,0:T(8,128)(2,1)}), bf16[4,128,512]{2,1,0:T(8,128)(2,1)}, u32[]{:S(2)}, u32[]{:S(2)}) async-start(bf16[4,128,512]{2,1,0:T(8,128)(2,1)} %fusion.1), calls=%async_computation.1 | async-start | bytes 1048576 | tf_op jit(solution)/shard_map/all_to_all | solution.py:323
  274.3 28.3 %collective-permute-start.4 = (bf16[4,2,128,512]{3,2,1,0:T(8,128)(2,1)}, bf16[4,2,128,512]{3,2,1,0:T(8,128)(2,1)}, u32[]{:S(2)}, u32[]{:S(2)}) collective-permute-start(bf16[4,2,128,512]{3,2,1,0:T(8,128)(2,1)} %all-to-all-done.6), channel_id=1, source_target_pairs={{0,1},{1,0},{2,3},{3,2},{4,5},{5,4},{6,7},{7,6},{8,9},{9,8},{10,11... | collective-permute-start | bytes 3145736 | tf_op jit(solution)/shard_map/ppermute | solution.py:327
  276.7 0.8 copy-start.14
  280.9 10.8 %all-to-all-start.5 = ((bf16[4,128,512]{2,1,0:T(8,128)(2,1)}), bf16[4,128,512]{2,1,0:T(8,128)(2,1)}, u32[]{:S(2)}, u32[]{:S(2)}) async-start(bf16[4,128,512]{2,1,0:T(8,128)(2,1)} %copy-done.14), calls=%async_computation.5 | async-start | bytes 1048576 | tf_op jit(solution)/shard_map/all_to_all | solution.py:323
  286.4 0.8 copy-start.13
  291.7 10.8 %all-to-all-start.2 = ((bf16[4,128,512]{2,1,0:T(8,128)(2,1)}), bf16[4,128,512]{2,1,0:T(8,128)(2,1)}, u32[]{:S(2)}, u32[]{:S(2)}) async-start(bf16[4,128,512]{2,1,0:T(8,128)(2,1)} %copy-done.13), calls=%async_computation.2 | async-start | bytes 1048576 | tf_op jit(solution)/shard_map/all_to_all | solution.py:323
  298.8 17.3 %collective-permute-start.3 = (bf16[4,128,512]{2,1,0:T(8,128)(2,1)}, bf16[4,128,512]{2,1,0:T(8,128)(2,1)}, u32[]{:S(2)}, u32[]{:S(2)}) collective-permute-start(bf16[4,128,512]{2,1,0:T(8,128)(2,1)} %all-to-all-done.5), channel_id=1, source_target_pairs={{0,1},{1,0},{2,3},{3,2},{4,5},{5,4},{6,7},{7,6},{8,9},{9,8},{10,11... | collective-permute-start | bytes 1572872 | tf_op jit(solution)/shard_map/ppermute | solution.py:327
  302.6 17.4 %collective-permute-start.1 = (bf16[4,128,512]{2,1,0:T(8,128)(2,1)}, bf16[4,128,512]{2,1,0:T(8,128)(2,1)S(1)}, u32[]{:S(2)}, u32[]{:S(2)}) collective-permute-start(bf16[4,128,512]{2,1,0:T(8,128)(2,1)} %all-to-all-done.2), channel_id=1, source_target_pairs={{0,1},{1,0},{2,3},{3,2},{4,5},{5,4},{6,7},{7,6},{8,9},{9,8},{10,11... | collective-permute-start | bytes 1572872 | tf_op jit(solution)/shard_map/ppermute | solution.py:327
  306.0 5.6 %copy-start.15 = (bf16[1,4,128,512]{3,2,0,1:T(8,128)(2,1)S(1)}, bf16[1,4,128,512]{3,2,0,1:T(8,128)(2,1)}, u32[]{:S(2)}) copy-start(bf16[1,4,128,512]{3,2,0,1:T(8,128)(2,1)} %get-tuple-element.36) | copy-start | bytes 1572868
  306.0 5.6 %copy-start.16 = (bf16[1,4,128,512]{3,2,0,1:T(8,128)(2,1)S(1)}, bf16[1,4,128,512]{3,2,0,1:T(8,128)(2,1)}, u32[]{:S(2)}) copy-start(bf16[1,4,128,512]{3,2,0,1:T(8,128)(2,1)} %get-tuple-element.37) | copy-start | bytes 1572868
  323.9 1.7 copy-start.7
  326.2 8.1 %all-to-all-start.7 = ((f32[8,8,128]{2,1,0:T(8,128)}), f32[8,8,128]{2,1,0:T(8,128)S(1)}, u32[]{:S(2)}, u32[]{:S(2)}) async-start(f32[8,8,128]{2,1,0:T(8,128)} %broadcast_in_dim.36), calls=%async_computation.7 | async-start | bytes 65536 | tf_op jit(solution)/shard_map/all_to_all | solution.py:323
  329.7 2.8 copy-start
  333.1 0.9 copy-start.12
  334.3 25.3 %all-to-all-start.8 = ((f32[4,384,128]{2,1,0:T(8,128)}), f32[4,384,128]{2,1,0:T(8,128)}, u32[]{:S(2)}, u32[]{:S(2)}) async-start(f32[4,384,128]{2,1,0:T(8,128)} %bitcast.58), calls=%async_computation.8 | async-start | bytes 1572864 | tf_op jit(solution)/shard_map/all_to_all | solution.py:323
  341.5 2.8 copy-start.1
  344.3 2.8 copy-start.3
  347.1 2.8 copy-start.5
  349.9 1.9 copy-start.8
  359.7 15.4 %all-to-all-start.10 = ((bf16[4,384,128]{2,1,0:T(8,128)(2,1)}), bf16[4,384,128]{2,1,0:T(8,128)(2,1)}, u32[]{:S(2)}, u32[]{:S(2)}) async-start(bf16[4,384,128]{2,1,0:T(8,128)(2,1)} %bitcast.30), calls=%async_computation.10 | async-start | bytes 786432 | tf_op jit(solution)/shard_map/all_to_all | solution.py:323
  363.8 1.4 copy-start.10
  365.2 1.4 copy-start.11
  367.2 0.7 copy-start.17
  376.9 22.5 %all-to-all-start.9 = ((f32[4,384,128]{2,1,0:T(8,128)}), f32[4,384,128]{2,1,0:T(8,128)}, u32[]{:S(2)}, u32[]{:S(2)}) async-start(f32[4,384,128]{2,1,0:T(8,128)} %broadcast_in_dim.37), calls=%async_computation.9 | async-start | bytes 1572864 | tf_op jit(solution)/shard_map/all_to_all | solution.py:323
  401.2 121.0 %all-to-all-start.11 = ((bf16[4,384,128]{2,1,0:T(8,128)(2,1)}), bf16[4,384,128]{2,1,0:T(8,128)(2,1)}, u32[]{:S(2)}, u32[]{:S(2)}) async-start(bf16[4,384,128]{2,1,0:T(8,128)(2,1)} %broadcast_in_dim.38), calls=%async_computation.11 | async-start | bytes 786432 | tf_op jit(solution)/shard_map/all_to_all | solution.py:323
  501.8 2.8 copy-start.2
  504.5 2.8 copy-start.4
  507.3 2.8 copy-start.6
  510.1 1.9 copy-start.9

commit v3 on v2

v3 whole, which is shorter than its diff:
```python
import functools

import jax
import jax.numpy as jnp
from jax import lax
from jax.experimental import pallas as pl
from jax.experimental.pallas import tpu as pltpu
from jax.sharding import PartitionSpec as P

HEAD = 128
WARMUP = 2000
STEPS_TOTAL = 100000
FRAG_COLS = 128


BETA_ONE = 0.9
BETA_TWO = 0.95
ADAM_EPS = 1e-08
DECAY = 0.1
PEAK_RATE = 0.0003
CLIP_NORM = 1.0
OUTER_MU = 0.9
OUTER_RATE = 0.7
MIX_LOCAL = 0.5

MIB = 1 << 20


def in_hbm(*arrays):
    return [pltpu.with_memory_space_constraint(a, pltpu.HBM) for a in arrays]


def params_of(limit):
    return pltpu.CompilerParams(vmem_limit_bytes=limit * MIB)


def cost(flops, moved):
    return pl.CostEstimate(flops=int(flops), bytes_accessed=int(moved), transcendentals=0)


def copy_kernel(src_ref, out_ref):
    out_ref[...] = src_ref[...].reshape(out_ref.shape)


def pack(tokens, first, count, rows):
    shards = tokens.shape[1] // rows
    return pl.pallas_call(
        copy_kernel,
        out_shape=jax.ShapeDtypeStruct((shards, count, rows), tokens.dtype),
        grid=(shards,),
        in_specs=[pl.BlockSpec((count, rows), lambda s: (first // count, s))],
        out_specs=pl.BlockSpec((1, count, rows), lambda s: (s, 0, 0)),
        compiler_params=params_of(8),
        cost_estimate=cost(0, 4 * shards * count * rows),
        name="pack",
    )(*in_hbm(tokens))


def transpose_kernel(me_ref, x_ref, out_ref):
    out_ref[...] = x_ref[0].T


def transpose_tokens(blocks, me):
    shards, count, rows = blocks.shape
    return pl.pallas_call(
        transpose_kernel,
        out_shape=jax.ShapeDtypeStruct((rows, shards * count), blocks.dtype),
        grid_spec=pltpu.PrefetchScalarGridSpec(
            num_scalar_prefetch=1,
            grid=(shards,),
            in_specs=[pl.BlockSpec((1, count, rows), lambda j, me: (me[0] ^ j, 0, 0))],
            out_specs=pl.BlockSpec((rows, count), lambda j, me: (0, j)),
        ),
        compiler_params=params_of(8),
        cost_estimate=cost(0, 4 * blocks.size),
        name="transpose_tokens",
    )(me, blocks)


def partial_kernel(me_ref, x_ref, w_ref, out_ref):
    out_ref[0] = jnp.dot(x_ref[0], w_ref[...], preferred_element_type=jnp.float32).astype(out_ref.dtype)


def partial_keys(blocks, key_weights, me, parity):
    shards, count, rows = blocks.shape
    width = key_weights.shape[1]
    return pl.pallas_call(
        partial_kernel,
        out_shape=jax.ShapeDtypeStruct((shards // 2, count, width), jnp.bfloat16),
        grid_spec=pltpu.PrefetchScalarGridSpec(
            num_scalar_prefetch=1,
            grid=(shards // 2,),
            in_specs=[
                pl.BlockSpec((1, count, rows), lambda m, me: (me[0] ^ (2 * m + parity), 0, 0)),
                pl.BlockSpec((rows, width), lambda m, me: (0, 0)),
            ],
            out_specs=pl.BlockSpec((1, count, width), lambda m, me: (m, 0, 0)),
        ),
        compiler_params=params_of(8),
        cost_estimate=cost(shards * count * rows * width, shards * count * rows),
        name="partial_keys",
    )(me, blocks, key_weights)


def key_kernel(*refs):
    *part_refs, cot_ref, out_ref = refs
    raw = sum(ref[...].astype(jnp.float32) for ref in part_refs)
    for h in range(raw.shape[1] // HEAD):
        cols = slice(h * HEAD, (h + 1) * HEAD)
        head = raw[:, cols]
        inverse = lax.rsqrt(jnp.mean(head * head, axis=1, keepdims=True) + 1e-06)
        normed = head * inverse
        upper = cot_ref[:, cols].astype(jnp.float32)
        back = inverse * (upper - normed * jnp.mean(upper * normed, axis=1, keepdims=True))
        out_ref[:, cols] = back.astype(out_ref.dtype)


def key_backward(parts, incoming):
    shape = parts[0].shape
    return pl.pallas_call(
        key_kernel,
        out_shape=jax.ShapeDtypeStruct(shape, jnp.bfloat16),
        compiler_params=params_of(8),
        cost_estimate=cost(60 * shape[0] * shape[1], 12 * shape[0] * shape[1]),
        name="key_backward",
    )(*parts, incoming)


def grad_kernel(counts, has_base, last, *refs):
    refs = list(refs)
    terms = []
    for count in counts:
        terms.append((refs.pop(0), refs[:count]))
        del refs[:count]
    base = refs.pop(0) if has_base else None
    square_in = refs.pop(0) if last and has_base else None
    out_ref = refs.pop(0)
    sq_ref = refs.pop(0) if last else None
    joined = refs

    @pl.when(pl.program_id(0) == 0)
    def _():
        for (_, blocks), held in zip(terms, joined):
            depth = blocks[0].shape[0]
            for j, block in enumerate(blocks):
                held[j * depth:(j + 1) * depth, :] = block[...]
        if last:
            sq_ref[...] = square_in[...] if has_base else jnp.zeros_like(sq_ref)

    total = base[...] if has_base else None
    for (x_ref, _), held in zip(terms, joined):
        term = jnp.dot(x_ref[...], held[...], preferred_element_type=jnp.float32)
        total = term if total is None else total + term
    out_ref[...] = total
    if last:
        rows, width = total.shape
        squares = (total * total).reshape(rows // 8, 8, width).sum(axis=0)
        folded = squares[:, :HEAD]
        for h in range(1, width // HEAD):
            folded = folded + squares[:, h * HEAD:(h + 1) * HEAD]
        sq_ref[...] += folded


def gradient(terms, base=None, square=None, last=True):
    rows = terms[0][0].shape[0]
    width = terms[0][1][0].shape[1]
    step = 256
    row_block = lambda cols: pl.BlockSpec((step, cols), lambda i: (i, 0))
    whole = lambda a: pl.BlockSpec(a.shape, lambda i: (0, 0))
    args, specs = [], []
    for x, blocks in terms:
        args += [x, *blocks]
        specs += [row_block(x.shape[1])] + [whole(b) for b in blocks]
    if base is not None:
        args.append(base)
        specs.append(row_block(width))
        if last:
            args.append(square)
            specs.append(whole(square))
    if last:
        shapes = [pltpu.HBM((rows, width), jnp.float32), jax.ShapeDtypeStruct((8, HEAD), jnp.float32)]
        outs = [row_block(width), pl.BlockSpec((8, HEAD), lambda i: (0, 0))]
    else:
        shapes = [jax.ShapeDtypeStruct((rows, width), jnp.float32)]
        outs = [row_block(width)]
    depth = sum(x.shape[1] for x, _ in terms)
    return pl.pallas_call(
        functools.partial(grad_kernel, [len(b) for _, b in terms], base is not None, last),
        out_shape=shapes,
        grid=(rows // step,),
        in_specs=specs,
        out_specs=outs,
        scratch_shapes=[pltpu.VMEM((x.shape[1], width), jnp.bfloat16) for x, _ in terms],
        compiler_params=params_of(20),
        cost_estimate=cost(2 * rows * width * depth, 2 * rows * depth + 4 * rows * width),
        name="gradient",
    )(*args)


def adam(old, first, second, grad, scalars):
    factor, rate, inv_one, inv_two = (scalars[i] for i in range(4))
    clipped = grad * factor
    first_new = BETA_ONE * first + (1.0 - BETA_ONE) * clipped
    second_new = BETA_TWO * second + (1.0 - BETA_TWO) * clipped * clipped
    update = rate * (
        first_new * inv_one / (jnp.sqrt(second_new * inv_two) + ADAM_EPS) + DECAY * old
    )
    return update, first_new, second_new


def adam_kernel(sc_ref, w_ref, m_ref, v_ref, gk_ref, gv_ref, w_out, m_out, v_out):
    width = gk_ref.shape[1]
    for g_ref, cols in ((gk_ref, slice(0, width)), (gv_ref, slice(width, 2 * width))):
        old = w_ref[:, cols]
        update, first_new, second_new = adam(old, m_ref[:, cols], v_ref[:, cols], g_ref[...], sc_ref)
        w_out[:, cols] = old - update
        m_out[:, cols] = first_new
        v_out[:, cols] = second_new


def adam_all(scalars, *state):
    rows, width = state[0].shape
    step = 128
    full = pl.BlockSpec((step, width), lambda i: (i, 0))
    half = pl.BlockSpec((step, width // 2), lambda i: (i, 0))
    return pl.pallas_call(
        adam_kernel,
        out_shape=[pltpu.HBM((rows, width), jnp.float32)] * 3,
        grid=(rows // step,),
        in_specs=[pl.BlockSpec(memory_space=pltpu.SMEM), full, full, full, half, half],
        out_specs=[full] * 3,
        compiler_params=params_of(16),
        cost_estimate=cost(20 * rows * width, 28 * rows * width),
        name="adam_all",
    )(scalars, *in_hbm(*state))


def frag_kernel(place_ref, sc_ref, w_ref, m_ref, v_ref, gk_ref, gv_ref, out_ref):
    heads = place_ref[2]
    grad = jnp.where(place_ref[0] < heads, gk_ref[...], gv_ref[...])
    update, _, _ = adam(w_ref[...], m_ref[...], v_ref[...], grad, sc_ref)
    out_ref[0] = update.astype(out_ref.dtype)


def adam_frag(place, scalars, part, *state):
    rows = state[0].shape[0]
    block = lambda at: pl.BlockSpec((part, FRAG_COLS), at)
    due = block(lambda j, p: (p[1] ^ j, p[0]))
    return pl.pallas_call(
        frag_kernel,
        out_shape=jax.ShapeDtypeStruct((rows // part, part, FRAG_COLS), jnp.bfloat16),
        grid_spec=pltpu.PrefetchScalarGridSpec(
            num_scalar_prefetch=1,
            grid=(rows // part,),
            in_specs=[
                pl.BlockSpec(memory_space=pltpu.SMEM),
                due,
                due,
                due,
                block(lambda j, p: (p[1] ^ j, jnp.minimum(p[0], p[2] - 1))),
                block(lambda j, p: (p[1] ^ j, jnp.maximum(p[0] - p[2], 0))),
            ],
            out_specs=pl.BlockSpec((1, part, FRAG_COLS), lambda j, p: (j, 0, 0)),
        ),
        compiler_params=params_of(8),
        cost_estimate=cost(20 * rows * FRAG_COLS, 22 * rows * FRAG_COLS),
        name="adam_frag",
    )(place, scalars, *in_hbm(*state))


def pick_kernel(place_ref, src_ref, out_ref):
    out_ref[...] = src_ref[...].reshape(out_ref.shape)


def due_columns(place, array, part):
    blocks = array.shape[0] // part
    at = (lambda j, p: (p[1] ^ j, p[0])) if blocks > 1 else (lambda j, p: (0, p[0]))
    return pl.pallas_call(
        pick_kernel,
        out_shape=jax.ShapeDtypeStruct((blocks, part, FRAG_COLS), array.dtype),
        grid_spec=pltpu.PrefetchScalarGridSpec(
            num_scalar_prefetch=1,
            grid=(blocks,),
            in_specs=[pl.BlockSpec((part, FRAG_COLS), at)],
            out_specs=pl.BlockSpec((1, part, FRAG_COLS), lambda j, p: (j, 0, 0)),
        ),
        compiler_params=params_of(8),
        cost_estimate=cost(0, 8 * blocks * part * FRAG_COLS),
        name="due_columns",
    )(place, *in_hbm(array))


def duplicate(array):
    rows, width = array.shape
    step = rows // 4 if rows % 32 == 0 else rows
    block = pl.BlockSpec((step, width), lambda i: (i, 0))
    return pl.pallas_call(
        copy_kernel,
        out_shape=pltpu.HBM((rows, width), array.dtype),
        grid=(rows // step,),
        in_specs=[block],
        out_specs=block,
        compiler_params=params_of(8),
        cost_estimate=cost(0, 8 * array.size),
        name="duplicate",
    )(*in_hbm(array))


def outer_kernel(share, place_ref, w_ref, base_ref, sum_ref, a_ref, p_ref, m_ref, own_ref, w_out, a_out, m_out):
    fresh = base_ref[0] - share * (1.0 + OUTER_MU) * OUTER_RATE * sum_ref[0].astype(jnp.float32)
    w_out[...] = MIX_LOCAL * w_ref[...] + (1.0 - MIX_LOCAL) * fresh

    @pl.when(pl.program_id(0) == 0)
    def _():
        pseudo = p_ref[...] + share * own_ref[...]
        new_moment = OUTER_MU * m_ref[...] + pseudo
        m_out[...] = new_moment
        a_out[...] = a_ref[...] - OUTER_RATE * (OUTER_MU * new_moment + pseudo)


def outer_step(place, weights, base, update_sum, anchor, pseudo, momentum, own_sum, replicas):
    part = anchor.shape[0]
    mixed = pl.BlockSpec((part, FRAG_COLS), lambda j, p: (p[1] ^ j, p[0]))
    pieces = pl.BlockSpec((1, part, FRAG_COLS), lambda j, p: (j, 0, 0))
    due = pl.BlockSpec((part, FRAG_COLS), lambda j, p: (0, p[0]))
    plain = pl.BlockSpec((part, FRAG_COLS), lambda j, p: (0, 0))
    return pl.pallas_call(
        functools.partial(outer_kernel, 1.0 / replicas),
        out_shape=[pltpu.HBM(a.shape, a.dtype) for a in (weights, anchor, momentum)],
        grid_spec=pltpu.PrefetchScalarGridSpec(
            num_scalar_prefetch=1,
            grid=(replicas,),
            in_specs=[mixed, pieces, pieces, due, plain, due, plain],
            out_specs=[mixed, due, due],
        ),
        input_output_aliases={1: 0, 4: 1, 6: 2},
        compiler_params=params_of(8),
        cost_estimate=cost(10 * replicas * part * FRAG_COLS, 20 * replicas * part * FRAG_COLS),
        name="outer_step",
    )(
        place, *in_hbm(weights), base, update_sum, *in_hbm(anchor), pseudo, *in_hbm(momentum), own_sum
    )


def swap(block, axis, offset):
    count = lax.axis_size(axis)
    return lax.ppermute(block, axis, [(i, i ^ offset) for i in range(count)])


def gather_pairs(block):
    blocks = [block] + [swap(block, "fsdp", k) for k in range(2, lax.axis_size("fsdp"), 2)]
    out = []
    for held in blocks:
        out += [held, swap(held, "fsdp", 1)]
    return out


def after(value, *others):
    return lax.optimization_barrier((value,) + others)[0]


def body(
    tokens,
    cotangent,
    weights,
    first_moment,
    second_moment,
    anchor,
    momentum,
    due_fragment,
    step_count,
):
    inputs, incoming, params = tokens[0], cotangent[0], weights[0]
    tok_rows = inputs.shape[0]
    kv_width = incoming.shape[1] // 2
    rows = params.shape[0]
    part = anchor.shape[0]
    replicas = lax.axis_size("rep")
    shards = lax.axis_size("fsdp")
    me = jnp.reshape(lax.axis_index("fsdp"), (1,)).astype(jnp.int32)
    place = jnp.stack(
        [due_fragment[0], lax.axis_index("rep").astype(jnp.int32), jnp.int32(kv_width // FRAG_COLS)]
    )
    th = tok_rows // 2

    packed = [pack(inputs, h * th, th, rows) for h in range(2)]
    arrived = [lax.all_to_all(sent, "fsdp", 0, 0, tiled=True) for sent in packed]
    arrived[0] = after(arrived[0], packed[1])

    def rep_sum(pieces):
        total = pieces[0].astype(jnp.float32)
        for k in range(1, replicas):
            total = total + swap(pieces[k], "rep", k).astype(jnp.float32)
        return total

    def rep_pieces(piece):
        return jnp.stack([piece] + [swap(piece, "rep", k) for k in range(1, replicas)])

    old_sum = rep_sum(due_columns(place, params, part))
    anchor_cols = due_columns(place, anchor, part)[0]
    moment_cols = due_columns(place, momentum, part)[0]
    pseudo_old = anchor_cols - old_sum / replicas
    base = rep_pieces(
        anchor_cols - OUTER_RATE * (OUTER_MU * (OUTER_MU * moment_cols + pseudo_old) + pseudo_old)
    )
    anchor_copy, momentum_copy = duplicate(anchor), duplicate(momentum)
    arrived[1] = after(arrived[1], base, anchor_copy, momentum_copy)

    key_weights = params[:, :kv_width].astype(jnp.bfloat16)
    flipped, keys = [], []
    for h in range(2):
        x = arrived[h]
        theirs = swap(partial_keys(x, key_weights, me, 1), "fsdp", 1)
        mine = partial_keys(x, key_weights, me, 0)
        parts = []
        for m in range(shards // 2):
            both = mine[m].astype(jnp.float32) + theirs[m].astype(jnp.float32)
            both = both.astype(jnp.bfloat16)
            parts.append(swap(both, "fsdp", 2 * m) if m else both)
        keys.append(gather_pairs(key_backward(parts, incoming[h * th:(h + 1) * th, :kv_width])))
        flipped.append(transpose_tokens(x, me))

    values = gather_pairs(after(incoming[:, kv_width:], arrived[0]))
    terms = [(flipped[h], [v[h * th:(h + 1) * th] for v in values]) for h in range(2)]
    grad_values, square = gradient(terms)
    grad_first = gradient([(flipped[0], keys[0])], last=False)[0]
    grad_keys, square = gradient([(flipped[1], keys[1])], grad_first, square)

    k = 1
    while k < shards:
        square = square + swap(square, "fsdp", k)
        k *= 2
    square = jnp.sum(square)
    factor = jnp.minimum(1.0, CLIP_NORM / (jnp.sqrt(square) + 1e-06))
    steps_now = step_count[0].astype(jnp.float32)
    plan = jnp.minimum(1.0, steps_now / WARMUP) * (
        0.55 + 0.45 * jnp.cos(jnp.pi * steps_now / STEPS_TOTAL)
    )
    rate = PEAK_RATE * plan
    inv_one = 1.0 / (1.0 - jnp.power(BETA_ONE, steps_now))
    inv_two = 1.0 / (1.0 - jnp.power(BETA_TWO, steps_now))
    scalars = jnp.stack([factor, rate, inv_one, inv_two])

    state = (params, first_moment[0], second_moment[0], grad_keys, grad_values)
    own_sum = rep_sum(adam_frag(place, scalars, part, *state))
    update_sum = rep_pieces(own_sum.astype(jnp.bfloat16))
    inner, first_out, second_out = adam_all(scalars, *state)
    weights_out, anchor_out, momentum_out = outer_step(
        place, inner, base, update_sum, anchor_copy, pseudo_old, momentum_copy, own_sum, replicas
    )
    plan_out = jnp.reshape(plan, (1,))
    return (
        weights_out[None],
        first_out[None],
        second_out[None],
        anchor_out,
        momentum_out,
        plan_out,
    )


def solution(mesh):
    tokens_spec = P("rep", "fsdp", None)
    outer_spec = P(("fsdp", "rep"), None)
    return jax.shard_map(
        body,
        mesh=mesh,
        in_specs=(tokens_spec,) * 5 + (outer_spec,) * 2 + (P(), P()),
        out_specs=(tokens_spec,) * 3 + (outer_spec,) * 2 + (P(),),
        check_vma=False,
    )
```

time: 529 us -> 224 us (0.42)
  Pallas kernels: 329 us -> 78.7 us
  local copies, waits for them, and re-layouts: 45.2 us -> 14.2 us
  waiting for transfers between devices: 77.5 us -> 68.3 us
  matrix products: 8.31 us -> 0 us
  other arithmetic: 10.4 us -> 4.08 us
    pallas_call x14 -> x20, Pallas kernels: 326 us -> 74.4 us  [the longest x1 19.1 us: adam_all(): pl.pallas_call(adam_kernel, out_shape=[pltpu.HBM((rows, width), jnp.float...]
    all_to_all x12 -> x2, waiting for transfers between devices: 77.5 us -> 31.9 us  [body(): lax.all_to_all(sent, 'fsdp', 0, 0, tiled=True)]
    ppermute x5 -> x44, starting transfers between devices: 0.56 us -> 42.8 us  [swap(): return lax.ppermute(block, axis, [(i, i ^ offset) for i in range(count)])]
    all_to_all x12 -> x2, starting transfers between devices: 51.2 us -> 9.63 us  [body(): lax.all_to_all(sent, 'fsdp', 0, 0, tiled=True)]
    ppermute x5 -> x44, waiting for transfers between devices: 0.01 us -> 36.4 us  [swap(): return lax.ppermute(block, axis, [(i, i ^ offset) for i in range(count)])]
    unnamed x40 -> x26, local copies, waits for them, and re-layouts: 32.8 us -> 7.2 us
    dot_general x2 -> x0, matrix products: 8.31 us -> none  [body(): jnp.dot(x.reshape(-1, rows), key_weights, preferred_element_type=jnp.floa...]
  transfers between devices with their start and end apart: 17 -> 46, of which waited for: 10 -> 18; matrix products, arithmetic and copies ran while one was open for 5% -> 5% of each run, Pallas kernels for 43% -> 28%
where the time goes in v3:
time: 224 us; the launch traced here: 222 us
  Pallas kernels  78.7 us (35%)
  waiting for transfers between devices  68.3 us (30%)
  starting transfers between devices  52.5 us (23%)
  local copies, waits for them, and re-layouts  14.2 us (6%)
  between operations  4.49 us (2%)
  other arithmetic  4.08 us (2%)
    ppermute x44, starting transfers between devices, swap(): return lax.ppermute(block, axis, [(i, i ^ offset) for i in range(count)])  42.8 us
    ppermute x44, waiting for transfers between devices, swap(): return lax.ppermute(block, axis, [(i, i ^ offset) for i in range(count)])  36.4 us
    all_to_all x2, waiting for transfers between devices, body(): lax.all_to_all(sent, 'fsdp', 0, 0, tiled=True)  31.9 us
    pallas_call x1, Pallas kernels, adam_all(): pl.pallas_call(adam_kernel, out_shape=[pltpu.HBM((rows, width), jnp.float...  19.1 us
    pallas_call x3, Pallas kernels, gradient(): pl.pallas_call(functools.partial(grad_kernel, [len(b) for _, b in terms],...  12.4 us
    all_to_all x2, starting transfers between devices, body(): lax.all_to_all(sent, 'fsdp', 0, 0, tiled=True)  9.63 us
    pallas_call x4, Pallas kernels, partial_keys(): pl.pallas_call(partial_kernel, out_shape=jax.ShapeDtypeStruct((shards //...  9.57 us
    pallas_call x2, Pallas kernels, pack(): pl.pallas_call(copy_kernel, out_shape=jax.ShapeDtypeStruct((shards, count...  8.68 us
  transfers between devices with their start and end apart: 46, of which 18 were waited for; matrix products, arithmetic and copies ran while one was open for 5% of the time, Pallas kernels for 28%

profile of v3, /device:TPU:0, one launch (start us, length us, event | category | flops | bytes accessed | tf_op | source)
XLA Modules:
  0.0 222.2 jit_solution(17719254649008108309)
XLA Ops:
  0.6 4.3 %pack.2 = bf16[8,128,1536]{2,1,0:T(8,128)(2,1)S(1)} custom-call(bf16[256,12288]{1,0:T(8,128)(2,1)} %bitcast.84), custom_call_target="tpu_custom_call" | custom-call | bytes 6291456 | tf_op jit(solution)/shard_map/pack/pallas_call | solution.py:47
  5.0 1.7 copy-done.4
  6.6 5.2 %all-to-all-start = ((bf16[8,128,1536]{2,1,0:T(8,128)(2,1)}), bf16[8,128,1536]{2,1,0:T(8,128)(2,1)S(1)}, u32[]{:S(2)}, u32[]{:S(2)}) async-start(bf16[8,128,1536]{2,1,0:T(8,128)(2,1)} %copy-done.4), calls=%async_computation | async-start | bytes 6291456 | tf_op jit(solution)/shard_map/all_to_all | solution.py:387
  11.8 4.3 %pack.3 = bf16[8,128,1536]{2,1,0:T(8,128)(2,1)S(1)} custom-call(bf16[256,12288]{1,0:T(8,128)(2,1)} %bitcast.85), custom_call_target="tpu_custom_call" | custom-call | bytes 6291456 | tf_op jit(solution)/shard_map/pack/pallas_call | solution.py:47
  16.2 1.7 copy-done.3
  17.8 31.9 %all-to-all-done.x_ref = bf16[8,128,1536]{2,1,0:T(8,128)(2,1)S(1)} async-done(((bf16[8,128,1536]{2,1,0:T(8,128)(2,1)}), bf16[8,128,1536]{2,1,0:T(8,128)(2,1)S(1)}, u32[]{:S(2)}, u32[]{:S(2)}) %all-to-all-start) | async-done | bytes 3145760 | tf_op jit(solution)/shard_map/all_to_all | solution.py:387
  49.7 4.5 %all-to-all-start.1 = ((bf16[8,128,1536]{2,1,0:T(8,128)(2,1)}), bf16[8,128,1536]{2,1,0:T(8,128)(2,1)}, u32[]{:S(2)}, u32[]{:S(2)}) async-start(bf16[8,128,1536]{2,1,0:T(8,128)(2,1)} %copy-done.3), calls=%async_computation.1 | async-start | bytes 6291456 | tf_op jit(solution)/shard_map/all_to_all | solution.py:387
  54.9 2.6 %due_columns.5 = f32[4,384,128]{2,1,0:T(8,128)S(1)} custom-call(s32[3]{0:T(128)S(1)} %pad_add_fusion.place_ref, f32[1536,1024]{1,0:T(8,128)} %bitcast.80), custom_call_target="tpu_custom_call" | custom-call | bytes 1572864 | tf_op jit(solution)/shard_map/due_columns/pallas_call | solution.py:278
  59.2 1.6 collective-permute-start
  60.8 2.5 %collective-permute-start.2 = (f32[384,128]{1,0:T(8,128)}, f32[384,128]{1,0:T(8,128)}, u32[]{:S(2)}, u32[]{:S(2)}) collective-permute-start(f32[384,128]{1,0:T(8,128)} %get-tuple-element.45), channel_id=1, source_target_pairs={{0,24},{8,16},{16,8},{24,0},{1,25},{9,17},{17,9},{25,1},{2,26},{10... | collective-permute-start | bytes 589832 | tf_op jit(solution)/shard_map/ppermute | solution.py:347
  63.4 3.2 %slice.256.w_ref = bf16[1536,512]{1,0:T(8,128)(2,1)} slice(f32[1536,1024]{1,0:T(8,128)} %bitcast.81), slice={[0:1536], [0:512]} | slice | bytes 3145728 | tf_op jit(solution)/shard_map/slice | solution.py:409
  66.6 1.5 due_columns.3
  68.1 3.6 %duplicate.2.a_ref = f32[384,1024]{1,0:T(8,128)} custom-call(f32[384,1024]{1,0:T(8,128)} %src_ref.6), custom_call_target="tpu_custom_call" | custom-call | bytes 3145728 | tf_op jit(solution)/shard_map/duplicate/pallas_call | solution.py:297
  71.7 1.5 due_columns.4
  73.2 3.6 %duplicate.3.m_ref = f32[384,1024]{1,0:T(8,128)} custom-call(f32[384,1024]{1,0:T(8,128)} %src_ref.7), custom_call_target="tpu_custom_call" | custom-call | bytes 3145728 | tf_op jit(solution)/shard_map/duplicate/pallas_call | solution.py:297
  76.8 1.8 slice.200
  78.6 2.9 %collective-permute-done.1 = f32[384,128]{1,0:T(8,128)} collective-permute-done((f32[384,128]{1,0:T(8,128)}, f32[384,128]{1,0:T(8,128)}, u32[]{:S(2)}, u32[]{:S(2)}) %collective-permute-start.1) | collective-permute-done | bytes 196640 | tf_op jit(solution)/shard_map/ppermute | solution.py:347
  81.5 2.0 fusion.10
  83.5 2.6 %collective-permute-start.5 = (f32[384,128]{1,0:T(8,128)S(1)}, f32[384,128]{1,0:T(8,128)S(1)}, u32[]{:S(2)}, u32[]{:S(2)}) collective-permute-start(f32[384,128]{1,0:T(8,128)S(1)} %get-tuple-element.34), channel_id=1, source_target_pairs={{0,24},{8,16},{16,8},{24,0},{1,25},{9,17},{17,9},{25,1},{2,26},{10... | collective-permute-start | bytes 589832 | tf_op jit(solution)/shard_map/ppermute | solution.py:347
  86.1 1.7 collective-permute-start.3
  87.9 1.0 fusion.22
  88.9 4.4 %collective-permute-done.5 = f32[384,128]{1,0:T(8,128)S(1)} collective-permute-done((f32[384,128]{1,0:T(8,128)S(1)}, f32[384,128]{1,0:T(8,128)S(1)}, u32[]{:S(2)}, u32[]{:S(2)}) %collective-permute-start.5) | collective-permute-done | bytes 196640 | tf_op jit(solution)/shard_map/ppermute | solution.py:347
  93.2 8.2 %collective-permute-done.4 = f32[384,128]{1,0:T(8,128)S(1)} collective-permute-done((f32[384,128]{1,0:T(8,128)S(1)}, f32[384,128]{1,0:T(8,128)S(1)}, u32[]{:S(2)}, u32[]{:S(2)}) %collective-permute-start.4) | collective-permute-done | bytes 196640 | tf_op jit(solution)/shard_map/ppermute | solution.py:347
  101.5 0.9 pad_maximum_fusion.base_ref
  102.4 1.5 partial_keys.5
  104.7 1.5 partial_keys.4
  107.1 2.4 %collective-permute-start.33 = (bf16[256,512]{1,0:T(8,128)(2,1)}, bf16[256,512]{1,0:T(8,128)(2,1)S(1)}, u32[]{:S(2)}, u32[]{:S(2)}) collective-permute-start(bf16[256,512]{1,0:T(8,128)(2,1)} %slice.200), channel_id=1, source_target_pairs={{0,6},{1,7},{2,4},{3,5},{4,2},{5,3},{6,0},{7,1},{8,14},{9,15},{10,... | collective-permute-start | bytes 786440 | tf_op jit(solution)/shard_map/ppermute | solution.py:347
  110.5 1.4 copy-done.1
  112.0 3.3 %partial_keys.7 = bf16[4,128,512]{2,1,0:T(8,128)(2,1)S(1)} custom-call(s32[1]{0:T(128)} %bitcast.1.me_ref, bf16[8,128,1536]{2,1,0:T(8,128)(2,1)} %all-to-all-done.1.x_ref, bf16[1536,512]{1,0:T(8,128)(2,1)S(1)} %copy-done.1), custom_call_target="tpu_custom_call" | custom-call | flops 805306368 | bytes 1572864 | tf_op jit(solution)/shard_map/partial_keys/pallas_call | solution.py:87
  115.3 3.2 %partial_keys.6 = bf16[4,128,512]{2,1,0:T(8,128)(2,1)S(1)} custom-call(s32[1]{0:T(128)} %bitcast.1.me_ref, bf16[8,128,1536]{2,1,0:T(8,128)(2,1)} %all-to-all-done.1.x_ref, bf16[1536,512]{1,0:T(8,128)(2,1)S(1)} %copy-done.2), custom_call_target="tpu_custom_call" | custom-call | flops 805306368 | bytes 1572864 | tf_op jit(solution)/shard_map/partial_keys/pallas_call | solution.py:87
  118.5 2.1 transpose_tokens.2.refs_9_.refs_0_
  120.7 5.5 %transpose_tokens.3.refs_0_ = bf16[1536,1024]{1,0:T(8,128)(2,1)S(1)} custom-call(s32[1]{0:T(128)} %bitcast.1.me_ref, bf16[8,128,1536]{2,1,0:T(8,128)(2,1)} %all-to-all-done.1.x_ref), custom_call_target="tpu_custom_call" | custom-call | bytes 6291456 | tf_op jit(solution)/shard_map/transpose_tokens/pallas_call | solution.py:65
  128.4 2.4 %collective-permute-start.9 = (bf16[128,512]{1,0:T(8,128)(2,1)S(1)}, bf16[128,512]{1,0:T(8,128)(2,1)S(1)}, u32[]{:S(2)}, u32[]{:S(2)}) collective-permute-start(bf16[128,512]{1,0:T(8,128)(2,1)S(1)} %get-tuple-element.40), channel_id=1, source_target_pairs={{0,6},{1,7},{2,4},{3,5},{4,2},{5,3},{6,0},{7,1},{8,14},{9,15},{10,... | collective-permute-start | bytes 393224 | tf_op jit(solution)/shard_map/ppermute | solution.py:347
  132.2 2.4 %collective-permute-start.20 = (bf16[128,512]{1,0:T(8,128)(2,1)S(1)}, bf16[128,512]{1,0:T(8,128)(2,1)S(1)}, u32[]{:S(2)}, u32[]{:S(2)}) collective-permute-start(bf16[128,512]{1,0:T(8,128)(2,1)S(1)} %get-tuple-element.36), channel_id=1, source_target_pairs={{0,6},{1,7},{2,4},{3,5},{4,2},{5,3},{6,0},{7,1},{8,14},{9,15},{10,... | collective-permute-start | bytes 393224 | tf_op jit(solution)/shard_map/ppermute | solution.py:347
  135.3 1.9 collective-permute-start.19
  137.2 1.8 collective-permute-done.8.refs_2_
  139.0 1.0 collective-permute-start.18
  140.3 1.6 collective-permute-start.15
  141.9 0.9 collective-permute-start.13
  143.6 1.8 collective-permute-done.18.refs_1_
  145.6 1.6 collective-permute-start.26
  147.2 1.0 collective-permute-start.24
  148.2 1.0 collective-permute-start.22
  149.2 1.1 collective-permute-start.11
  150.3 2.6 %collective-permute-done.13.refs_5_ = bf16[128,512]{1,0:T(8,128)(2,1)S(1)} collective-permute-done((bf16[128,512]{1,0:T(8,128)(2,1)S(1)}, bf16[128,512]{1,0:T(8,128)(2,1)S(1)}, u32[]{:S(2)}, u32[]{:S(2)}) %collective-permute-start.13) | collective-permute-done | bytes 131104 | tf_op jit(solution)/shard_map/ppermute | solution.py:347
  153.5 1.4 collective-permute-done.24.refs_5_
  155.4 5.4 %gradient.4 = (f32[1536,512]{1,0:T(8,128)}, f32[8,128]{1,0:T(8,128)S(1)}) custom-call(bf16[1536,1024]{1,0:T(8,128)(2,1)S(1)} %transpose_tokens.3.refs_0_, bf16[128,512]{1,0:T(8,128)(2,1)S(1)} %get-tuple-element.67.refs_1_, bf16[128,512]{1,0:T(8,128)(2,1)S(1)} %get-tuple-element.65.refs_2_, bf16[128,512]{1,0:T(8,128)(2,1)S(1)} %get-tuple-element.63.refs_3_, ...), custom_call_target="tpu_custom_call" | custom-call | flops 3221225472 | bytes 9437184 | tf_op jit(solution)/shard_map/gradient/pallas_call | solution.py:187
  161.8 2.7 %gradient.3.refs_9_ = f32[1536,512]{1,0:T(8,128)S(1)} custom-call(bf16[1536,1024]{1,0:T(8,128)(2,1)S(1)} %transpose_tokens.3.refs_0_, bf16[128,512]{1,0:T(8,128)(2,1)S(1)} %key_backward.3.refs_1_, bf16[128,512]{1,0:T(8,128)(2,1)S(1)} %collective-permute-done.21.refs_2_, bf16[128,512]{1,0:T(8,128)(2,1)S(1)} %collective-permute-done.22.refs_3_, ...), custom_call_target="tpu_custom_call" | custom-call | flops 1610612736 | bytes 6291456 | tf_op jit(solution)/shard_map/gradient/pallas_call | solution.py:187
  164.6 4.3 %gradient.5 = (f32[1536,512]{1,0:T(8,128)}, f32[8,128]{1,0:T(8,128)S(1)}) custom-call(bf16[1536,1024]{1,0:T(8,128)(2,1)S(1)} %transpose_tokens.2.refs_9_.refs_0_, bf16[128,512]{1,0:T(8,128)(2,1)S(1)} %key_backward.2.refs_1_, bf16[128,512]{1,0:T(8,128)(2,1)S(1)} %collective-permute-done.10.refs_2_, bf16[128,512]{1,0:T(8,128)(2,1)S(1)} %collective-permute-done.11.refs_3_, ...), custom_call_target="tpu_custom_call" | custom-call | flops 1610612736 | bytes 6291456 | tf_op jit(solution)/shard_map/gradient/pallas_call | solution.py:187
  169.0 1.1 collective-permute-done.35
  170.1 1.4 collective-permute-start.36
  171.4 2.3 %collective-permute-done.36 = f32[8,128]{1,0:T(8,128)S(1)} collective-permute-done((f32[8,128]{1,0:T(8,128)S(1)}, f32[8,128]{1,0:T(8,128)S(1)}, u32[]{:S(2)}, u32[]{:S(2)}) %collective-permute-start.36) | collective-permute-done | bytes 4128 | tf_op jit(solution)/shard_map/ppermute | solution.py:347
  173.7 1.4 collective-permute-start.37
  176.0 1.3 collective-permute-done.37
  178.7 3.9 %adam_frag.1 = bf16[4,384,128]{2,1,0:T(8,128)(2,1)S(1)} custom-call(s32[3]{0:T(128)S(1)} %pad_add_fusion.place_ref, f32[4]{0:T(128)S(1)} %pad_maximum_fusion.2.sc_ref, f32[1536,1024]{1,0:T(8,128)} %bitcast.82, f32[1536,1024]{1,0:T(8,128)} %bitcast.86, f32[1536,1024]{1,0:T(8,128)} %bitcast.88, f32[1536,512]{1,0:T(8,128)} %get-tuple-element.24.gk_ref, ...), custom_call_target="tpu_custom_call" | custom-call | flops 3932160 | bytes 4325376 | tf_op jit(solution)/shard_map/adam_frag/pallas_call | solution.py:249
  182.7 2.0 collective-permute-start.40
  184.7 1.4 collective-permute-start.39
  186.2 1.6 collective-permute-done.38
  187.8 1.5 collective-permute-done.40
  189.3 3.7 %collective-permute-done.39 = bf16[384,128]{1,0:T(8,128)(2,1)S(1)} collective-permute-done((bf16[384,128]{1,0:T(8,128)(2,1)S(1)}, bf16[384,128]{1,0:T(8,128)(2,1)S(1)}, u32[]{:S(2)}, u32[]{:S(2)}) %collective-permute-start.39) | collective-permute-done | bytes 98336 | tf_op jit(solution)/shard_map/ppermute | solution.py:347
  193.1 2.1 collective-permute-start.43
  195.2 2.4 %collective-permute-start.41 = (bf16[384,128]{1,0:T(8,128)(2,1)S(1)}, bf16[384,128]{1,0:T(8,128)(2,1)S(1)}, u32[]{:S(2)}, u32[]{:S(2)}) collective-permute-start(bf16[384,128]{1,0:T(8,128)(2,1)S(1)} %get-tuple-element.32), channel_id=1, source_target_pairs={{0,8},{8,0},{16,24},{24,16},{1,9},{9,1},{17,25},{25,17},{2,10},{10... | collective-permute-start | bytes 294920 | tf_op jit(solution)/shard_map/ppermute | solution.py:347
  197.5 19.1 %adam_all.1 = (f32[1536,1024]{1,0:T(8,128)}, f32[1536,1024]{1,0:T(8,128)}, f32[1536,1024]{1,0:T(8,128)}) custom-call(f32[4]{0:T(128)S(1)} %pad_maximum_fusion.2.sc_ref, f32[1536,1024]{1,0:T(8,128)} %bitcast.83, f32[1536,1024]{1,0:T(8,128)} %bitcast.87, f32[1536,1024]{1,0:T(8,128)} %bitcast.89, f32[1536,512]{1,0:T(8,128)} %get-tuple-element.24.gk_ref, ...), custom_call_target="tpu_custom_call" | custom-call | flops 31457280 | bytes 44040192 | tf_op jit(solution)/shard_map/adam_all/pallas_call | solution.py:226
  216.8 4.3 %outer_step.1 = (f32[1536,1024]{1,0:T(8,128)}, f32[384,1024]{1,0:T(8,128)}, f32[384,1024]{1,0:T(8,128)}) custom-call(s32[3]{0:T(128)S(1)} %pad_add_fusion.place_ref, f32[1536,1024]{1,0:T(8,128)} %get-tuple-element.26.w_ref, f32[4,384,128]{2,1,0:T(8,128)S(1)} %copy-done.6, ...), custom_call_target="tpu_custom_call", output_to_operand_aliasing={{0}: (1, {}), {1}: (4, {}), {2}: (6, {})} | custom-call | flops 1966080 | bytes 3932160 | tf_op jit(solution)/shard_map/outer_step/pallas_call | solution.py:327
  (99 shorter events, 13.2 us)
Async XLA Ops:
  5.0 1.7 copy-start.4
  6.6 43.1 %all-to-all-start = ((bf16[8,128,1536]{2,1,0:T(8,128)(2,1)}), bf16[8,128,1536]{2,1,0:T(8,128)(2,1)S(1)}, u32[]{:S(2)}, u32[]{:S(2)}) async-start(bf16[8,128,1536]{2,1,0:T(8,128)(2,1)} %copy-done.4), calls=%async_computation | async-start | bytes 6291456 | tf_op jit(solution)/shard_map/all_to_all | solution.py:387
  16.2 1.7 copy-start.3
  49.7 57.4 %all-to-all-start.1 = ((bf16[8,128,1536]{2,1,0:T(8,128)(2,1)}), bf16[8,128,1536]{2,1,0:T(8,128)(2,1)}, u32[]{:S(2)}, u32[]{:S(2)}) async-start(bf16[8,128,1536]{2,1,0:T(8,128)(2,1)} %copy-done.3), calls=%async_computation.1 | async-start | bytes 6291456 | tf_op jit(solution)/shard_map/all_to_all | solution.py:387
  57.5 0.9 copy-start.5
  59.2 19.3 %collective-permute-start = (f32[384,128]{1,0:T(8,128)}, f32[384,128]{1,0:T(8,128)}, u32[]{:S(2)}, u32[]{:S(2)}) collective-permute-start(f32[384,128]{1,0:T(8,128)} %get-tuple-element.44), channel_id=1, source_target_pairs={{0,8},{8,0},{16,24},{24,16},{1,9},{9,1},{17,25},{25,17},{2,10},{10... | collective-permute-start | bytes 589832 | tf_op jit(solution)/shard_map/ppermute | solution.py:347
  60.8 17.7 %collective-permute-start.2 = (f32[384,128]{1,0:T(8,128)}, f32[384,128]{1,0:T(8,128)}, u32[]{:S(2)}, u32[]{:S(2)}) collective-permute-start(f32[384,128]{1,0:T(8,128)} %get-tuple-element.45), channel_id=1, source_target_pairs={{0,24},{8,16},{16,8},{24,0},{1,25},{9,17},{17,9},{25,1},{2,26},{10... | collective-permute-start | bytes 589832 | tf_op jit(solution)/shard_map/ppermute | solution.py:347
  63.3 18.2 %collective-permute-start.1 = (f32[384,128]{1,0:T(8,128)}, f32[384,128]{1,0:T(8,128)}, u32[]{:S(2)}, u32[]{:S(2)}) collective-permute-start(f32[384,128]{1,0:T(8,128)} %get-tuple-element.46), channel_id=1, source_target_pairs={{0,16},{8,24},{16,0},{24,8},{1,17},{9,25},{17,1},{25,9},{2,18},{10... | collective-permute-start | bytes 589832 | tf_op jit(solution)/shard_map/ppermute | solution.py:347
  76.8 25.6 %copy-start = (bf16[1536,512]{1,0:T(8,128)(2,1)S(1)}, bf16[1536,512]{1,0:T(8,128)(2,1)}, u32[]{:S(2)}) copy-start(bf16[1536,512]{1,0:T(8,128)(2,1)} %slice.256.w_ref) | copy-start | bytes 4718596
  83.5 9.7 %collective-permute-start.5 = (f32[384,128]{1,0:T(8,128)S(1)}, f32[384,128]{1,0:T(8,128)S(1)}, u32[]{:S(2)}, u32[]{:S(2)}) collective-permute-start(f32[384,128]{1,0:T(8,128)S(1)} %get-tuple-element.34), channel_id=1, source_target_pairs={{0,24},{8,16},{16,8},{24,0},{1,25},{9,17},{17,9},{25,1},{2,26},{10... | collective-permute-start | bytes 589832 | tf_op jit(solution)/shard_map/ppermute | solution.py:347
  86.1 15.3 %collective-permute-start.4 = (f32[384,128]{1,0:T(8,128)S(1)}, f32[384,128]{1,0:T(8,128)S(1)}, u32[]{:S(2)}, u32[]{:S(2)}) collective-permute-start(f32[384,128]{1,0:T(8,128)S(1)} %get-tuple-element.34), channel_id=1, source_target_pairs={{0,16},{8,24},{16,0},{24,8},{1,17},{9,25},{17,1},{25,9},{2,18},{10... | collective-permute-start | bytes 589832 | tf_op jit(solution)/shard_map/ppermute | solution.py:347
  86.1 15.3 %collective-permute-start.3 = (f32[384,128]{1,0:T(8,128)S(1)}, f32[384,128]{1,0:T(8,128)S(1)}, u32[]{:S(2)}, u32[]{:S(2)}) collective-permute-start(f32[384,128]{1,0:T(8,128)S(1)} %get-tuple-element.34), channel_id=1, source_target_pairs={{0,8},{8,0},{16,24},{24,16},{1,9},{9,1},{17,25},{25,17},{2,10},{10... | collective-permute-start | bytes 589832 | tf_op jit(solution)/shard_map/ppermute | solution.py:347
  103.9 0.8 copy-start.10
  106.3 0.8 copy-start.7
  107.1 19.7 %collective-permute-start.33 = (bf16[256,512]{1,0:T(8,128)(2,1)}, bf16[256,512]{1,0:T(8,128)(2,1)S(1)}, u32[]{:S(2)}, u32[]{:S(2)}) collective-permute-start(bf16[256,512]{1,0:T(8,128)(2,1)} %slice.200), channel_id=1, source_target_pairs={{0,6},{1,7},{2,4},{3,5},{4,2},{5,3},{6,0},{7,1},{8,14},{9,15},{10,... | collective-permute-start | bytes 786440 | tf_op jit(solution)/shard_map/ppermute | solution.py:347
  109.4 17.4 %collective-permute-start.31 = (bf16[256,512]{1,0:T(8,128)(2,1)}, bf16[256,512]{1,0:T(8,128)(2,1)S(1)}, u32[]{:S(2)}, u32[]{:S(2)}) collective-permute-start(bf16[256,512]{1,0:T(8,128)(2,1)} %slice.200), channel_id=1, source_target_pairs={{0,4},{1,5},{2,6},{3,7},{4,0},{5,1},{6,2},{7,3},{8,12},{9,13},{10,... | collective-permute-start | bytes 786440 | tf_op jit(solution)/shard_map/ppermute | solution.py:347
  109.9 17.4 %collective-permute-start.29 = (bf16[256,512]{1,0:T(8,128)(2,1)}, bf16[256,512]{1,0:T(8,128)(2,1)S(1)}, u32[]{:S(2)}, u32[]{:S(2)}) collective-permute-start(bf16[256,512]{1,0:T(8,128)(2,1)} %slice.200), channel_id=1, source_target_pairs={{0,2},{1,3},{2,0},{3,1},{4,6},{5,7},{6,4},{7,5},{8,10},{9,11},{10,... | collective-permute-start | bytes 786440 | tf_op jit(solution)/shard_map/ppermute | solution.py:347
  110.5 17.0 %collective-permute-start.28 = (bf16[256,512]{1,0:T(8,128)(2,1)}, bf16[256,512]{1,0:T(8,128)(2,1)S(1)}, u32[]{:S(2)}, u32[]{:S(2)}) collective-permute-start(bf16[256,512]{1,0:T(8,128)(2,1)} %slice.200), channel_id=1, source_target_pairs={{0,1},{1,0},{2,3},{3,2},{4,5},{5,4},{6,7},{7,6},{8,9},{9,8},{10,11... | collective-permute-start | bytes 786440 | tf_op jit(solution)/shard_map/ppermute | solution.py:347
  110.5 1.4 copy-start.1
  112.0 3.3 %copy-start.12 = (bf16[256,512]{1,0:T(8,128)(2,1)S(1)}, bf16[256,512]{1,0:T(8,128)(2,1)}, u32[]{:S(2)}) copy-start(bf16[256,512]{1,0:T(8,128)(2,1)} %slice.200) | copy-start | bytes 786436
  112.0 3.4 %copy-start.2 = (bf16[1536,512]{1,0:T(8,128)(2,1)S(1)}, bf16[1536,512]{1,0:T(8,128)(2,1)}, u32[]{:S(2)}) copy-start(bf16[1536,512]{1,0:T(8,128)(2,1)} %slice.256.w_ref) | copy-start | bytes 4718596
  120.6 5.5 %copy-start.11 = (bf16[4,128,512]{2,1,0:T(8,128)(2,1)S(1)}, bf16[4,128,512]{2,1,0:T(8,128)(2,1)}, u32[]{:S(2)}) copy-start(bf16[4,128,512]{2,1,0:T(8,128)(2,1)} %copy-done.10) | copy-start | bytes 1572868
  120.6 7.6 %copy-start.8 = (bf16[4,128,512]{2,1,0:T(8,128)(2,1)S(1)}, bf16[4,128,512]{2,1,0:T(8,128)(2,1)}, u32[]{:S(2)}) copy-start(bf16[4,128,512]{2,1,0:T(8,128)(2,1)} %copy-done.7) | copy-start | bytes 1572868
  126.1 2.1 collective-permute-start.6
  126.7 4.1 %collective-permute-start.17 = (bf16[4,128,512]{2,1,0:T(8,128)(2,1)S(1)}, bf16[4,128,512]{2,1,0:T(8,128)(2,1)S(1)}, u32[]{:S(2)}, u32[]{:S(2)}) collective-permute-start(bf16[4,128,512]{2,1,0:T(8,128)(2,1)S(1)} %partial_keys.7), channel_id=1, source_target_pairs={{0,1},{1,0},{2,3},{3,2},{4,5},{5,4},{6,7},{7,6},{8,9},{9,8},{10,11... | collective-permute-start | bytes 1572872 | tf_op jit(solution)/shard_map/ppermute | solution.py:347
  126.8 4.7 %collective-permute-start.34 = (bf16[256,512]{1,0:T(8,128)(2,1)S(1)}, bf16[256,512]{1,0:T(8,128)(2,1)S(1)}, u32[]{:S(2)}, u32[]{:S(2)}) collective-permute-start(bf16[256,512]{1,0:T(8,128)(2,1)S(1)} %collective-permute-done.33), channel_id=1, source_target_pairs={{0,1},{1,0},{2,3},{3,2},{4,5},{5,4},{6,7},{7,6},{8,9},{9,8},{10,11... | collective-permute-start | bytes 786440 | tf_op jit(solution)/shard_map/ppermute | solution.py:347
  127.4 4.9 %collective-permute-start.32 = (bf16[256,512]{1,0:T(8,128)(2,1)S(1)}, bf16[256,512]{1,0:T(8,128)(2,1)S(1)}, u32[]{:S(2)}, u32[]{:S(2)}) collective-permute-start(bf16[256,512]{1,0:T(8,128)(2,1)S(1)} %collective-permute-done.31), channel_id=1, source_target_pairs={{0,1},{1,0},{2,3},{3,2},{4,5},{5,4},{6,7},{7,6},{8,9},{9,8},{10,11... | collective-permute-start | bytes 786440 | tf_op jit(solution)/shard_map/ppermute | solution.py:347
  127.5 20.6 %collective-permute-start.30 = (bf16[256,512]{1,0:T(8,128)(2,1)S(1)}, bf16[256,512]{1,0:T(8,128)(2,1)S(1)}, u32[]{:S(2)}, u32[]{:S(2)}) collective-permute-start(bf16[256,512]{1,0:T(8,128)(2,1)S(1)} %collective-permute-done.29), channel_id=1, source_target_pairs={{0,1},{1,0},{2,3},{3,2},{4,5},{5,4},{6,7},{7,6},{8,9},{9,8},{10,11... | collective-permute-start | bytes 786440 | tf_op jit(solution)/shard_map/ppermute | solution.py:347
  128.4 6.9 %collective-permute-start.9 = (bf16[128,512]{1,0:T(8,128)(2,1)S(1)}, bf16[128,512]{1,0:T(8,128)(2,1)S(1)}, u32[]{:S(2)}, u32[]{:S(2)}) collective-permute-start(bf16[128,512]{1,0:T(8,128)(2,1)S(1)} %get-tuple-element.40), channel_id=1, source_target_pairs={{0,6},{1,7},{2,4},{3,5},{4,2},{5,3},{6,0},{7,1},{8,14},{9,15},{10,... | collective-permute-start | bytes 393224 | tf_op jit(solution)/shard_map/ppermute | solution.py:347
  130.8 8.2 %collective-permute-start.8 = (bf16[128,512]{1,0:T(8,128)(2,1)S(1)}, bf16[128,512]{1,0:T(8,128)(2,1)S(1)}, u32[]{:S(2)}, u32[]{:S(2)}) collective-permute-start(bf16[128,512]{1,0:T(8,128)(2,1)S(1)} %get-tuple-element.41), channel_id=1, source_target_pairs={{0,4},{1,5},{2,6},{3,7},{4,0},{5,1},{6,2},{7,3},{8,12},{9,13},{10,... | collective-permute-start | bytes 393224 | tf_op jit(solution)/shard_map/ppermute | solution.py:347
  131.5 8.5 %collective-permute-start.7 = (bf16[128,512]{1,0:T(8,128)(2,1)S(1)}, bf16[128,512]{1,0:T(8,128)(2,1)S(1)}, u32[]{:S(2)}, u32[]{:S(2)}) collective-permute-start(bf16[128,512]{1,0:T(8,128)(2,1)S(1)} %get-tuple-element.42), channel_id=1, source_target_pairs={{0,2},{1,3},{2,0},{3,1},{4,6},{5,7},{6,4},{7,5},{8,10},{9,11},{10,... | collective-permute-start | bytes 393224 | tf_op jit(solution)/shard_map/ppermute | solution.py:347
  132.2 9.7 %collective-permute-start.20 = (bf16[128,512]{1,0:T(8,128)(2,1)S(1)}, bf16[128,512]{1,0:T(8,128)(2,1)S(1)}, u32[]{:S(2)}, u32[]{:S(2)}) collective-permute-start(bf16[128,512]{1,0:T(8,128)(2,1)S(1)} %get-tuple-element.36), channel_id=1, source_target_pairs={{0,6},{1,7},{2,4},{3,5},{4,2},{5,3},{6,0},{7,1},{8,14},{9,15},{10,... | collective-permute-start | bytes 393224 | tf_op jit(solution)/shard_map/ppermute | solution.py:347
  135.3 8.3 %collective-permute-start.19 = (bf16[128,512]{1,0:T(8,128)(2,1)S(1)}, bf16[128,512]{1,0:T(8,128)(2,1)S(1)}, u32[]{:S(2)}, u32[]{:S(2)}) collective-permute-start(bf16[128,512]{1,0:T(8,128)(2,1)S(1)} %get-tuple-element.37), channel_id=1, source_target_pairs={{0,4},{1,5},{2,6},{3,7},{4,0},{5,1},{6,2},{7,3},{8,12},{9,13},{10,... | collective-permute-start | bytes 393224 | tf_op jit(solution)/shard_map/ppermute | solution.py:347
  139.0 6.4 %collective-permute-start.18 = (bf16[128,512]{1,0:T(8,128)(2,1)S(1)}, bf16[128,512]{1,0:T(8,128)(2,1)S(1)}, u32[]{:S(2)}, u32[]{:S(2)}) collective-permute-start(bf16[128,512]{1,0:T(8,128)(2,1)S(1)} %get-tuple-element.38), channel_id=1, source_target_pairs={{0,2},{1,3},{2,0},{3,1},{4,6},{5,7},{6,4},{7,5},{8,10},{9,11},{10,... | collective-permute-start | bytes 393224 | tf_op jit(solution)/shard_map/ppermute | solution.py:347
  140.3 8.9 %collective-permute-start.15 = (bf16[128,512]{1,0:T(8,128)(2,1)S(1)}, bf16[128,512]{1,0:T(8,128)(2,1)S(1)}, u32[]{:S(2)}, u32[]{:S(2)}) collective-permute-start(bf16[128,512]{1,0:T(8,128)(2,1)S(1)} %key_backward.2.refs_1_), channel_id=1, source_target_pairs={{0,6},{1,7},{2,4},{3,5},{4,2},{5,3},{6,0},{7,1},{8,14},{9,15},{10,... | collective-permute-start | bytes 393224 | tf_op jit(solution)/shard_map/ppermute | solution.py:347
  141.9 11.0 %collective-permute-start.13 = (bf16[128,512]{1,0:T(8,128)(2,1)S(1)}, bf16[128,512]{1,0:T(8,128)(2,1)S(1)}, u32[]{:S(2)}, u32[]{:S(2)}) collective-permute-start(bf16[128,512]{1,0:T(8,128)(2,1)S(1)} %key_backward.2.refs_1_), channel_id=1, source_target_pairs={{0,4},{1,5},{2,6},{3,7},{4,0},{5,1},{6,2},{7,3},{8,12},{9,13},{10,... | collective-permute-start | bytes 393224 | tf_op jit(solution)/shard_map/ppermute | solution.py:347
  145.6 7.4 %collective-permute-start.26 = (bf16[128,512]{1,0:T(8,128)(2,1)S(1)}, bf16[128,512]{1,0:T(8,128)(2,1)S(1)}, u32[]{:S(2)}, u32[]{:S(2)}) collective-permute-start(bf16[128,512]{1,0:T(8,128)(2,1)S(1)} %key_backward.3.refs_1_), channel_id=1, source_target_pairs={{0,6},{1,7},{2,4},{3,5},{4,2},{5,3},{6,0},{7,1},{8,14},{9,15},{10,... | collective-permute-start | bytes 393224 | tf_op jit(solution)/shard_map/ppermute | solution.py:347
  147.2 7.7 %collective-permute-start.24 = (bf16[128,512]{1,0:T(8,128)(2,1)S(1)}, bf16[128,512]{1,0:T(8,128)(2,1)S(1)}, u32[]{:S(2)}, u32[]{:S(2)}) collective-permute-start(bf16[128,512]{1,0:T(8,128)(2,1)S(1)} %key_backward.3.refs_1_), channel_id=1, source_target_pairs={{0,4},{1,5},{2,6},{3,7},{4,0},{5,1},{6,2},{7,3},{8,12},{9,13},{10,... | collective-permute-start | bytes 393224 | tf_op jit(solution)/shard_map/ppermute | solution.py:347
  148.2 6.7 %collective-permute-start.22 = (bf16[128,512]{1,0:T(8,128)(2,1)S(1)}, bf16[128,512]{1,0:T(8,128)(2,1)S(1)}, u32[]{:S(2)}, u32[]{:S(2)}) collective-permute-start(bf16[128,512]{1,0:T(8,128)(2,1)S(1)} %key_backward.3.refs_1_), channel_id=1, source_target_pairs={{0,2},{1,3},{2,0},{3,1},{4,6},{5,7},{6,4},{7,5},{8,10},{9,11},{10,... | collective-permute-start | bytes 393224 | tf_op jit(solution)/shard_map/ppermute | solution.py:347
  149.2 11.6 %collective-permute-start.11 = (bf16[128,512]{1,0:T(8,128)(2,1)S(1)}, bf16[128,512]{1,0:T(8,128)(2,1)S(1)}, u32[]{:S(2)}, u32[]{:S(2)}) collective-permute-start(bf16[128,512]{1,0:T(8,128)(2,1)S(1)} %key_backward.2.refs_1_), channel_id=1, source_target_pairs={{0,2},{1,3},{2,0},{3,1},{4,6},{5,7},{6,4},{7,5},{8,10},{9,11},{10,... | collective-permute-start | bytes 393224 | tf_op jit(solution)/shard_map/ppermute | solution.py:347
  152.9 7.9 %collective-permute-start.21 = (bf16[128,512]{1,0:T(8,128)(2,1)S(1)}, bf16[128,512]{1,0:T(8,128)(2,1)S(1)}, u32[]{:S(2)}, u32[]{:S(2)}) collective-permute-start(bf16[128,512]{1,0:T(8,128)(2,1)S(1)} %key_backward.3.refs_1_), channel_id=1, source_target_pairs={{0,1},{1,0},{2,3},{3,2},{4,5},{5,4},{6,7},{7,6},{8,9},{9,8},{10,11... | collective-permute-start | bytes 393224 | tf_op jit(solution)/shard_map/ppermute | solution.py:347
  153.0 8.3 %collective-permute-start.27 = (bf16[128,512]{1,0:T(8,128)(2,1)S(1)}, bf16[128,512]{1,0:T(8,128)(2,1)S(1)}, u32[]{:S(2)}, u32[]{:S(2)}) collective-permute-start(bf16[128,512]{1,0:T(8,128)(2,1)S(1)} %collective-permute-done.26.refs_7_), channel_id=1, source_target_pairs={{0,1},{1,0},{2,3},{3,2},{4,5},{5,4},{6,7},{7,6},{8,9},{9,8},{10,11... | collective-permute-start | bytes 393224 | tf_op jit(solution)/shard_map/ppermute | solution.py:347
  154.9 6.5 %collective-permute-start.25 = (bf16[128,512]{1,0:T(8,128)(2,1)S(1)}, bf16[128,512]{1,0:T(8,128)(2,1)S(1)}, u32[]{:S(2)}, u32[]{:S(2)}) collective-permute-start(bf16[128,512]{1,0:T(8,128)(2,1)S(1)} %collective-permute-done.24.refs_5_), channel_id=1, source_target_pairs={{0,1},{1,0},{2,3},{3,2},{4,5},{5,4},{6,7},{7,6},{8,9},{9,8},{10,11... | collective-permute-start | bytes 393224 | tf_op jit(solution)/shard_map/ppermute | solution.py:347
  154.9 7.0 %collective-permute-start.23 = (bf16[128,512]{1,0:T(8,128)(2,1)S(1)}, bf16[128,512]{1,0:T(8,128)(2,1)S(1)}, u32[]{:S(2)}, u32[]{:S(2)}) collective-permute-start(bf16[128,512]{1,0:T(8,128)(2,1)S(1)} %collective-permute-done.22.refs_3_), channel_id=1, source_target_pairs={{0,1},{1,0},{2,3},{3,2},{4,5},{5,4},{6,7},{7,6},{8,9},{9,8},{10,11... | collective-permute-start | bytes 393224 | tf_op jit(solution)/shard_map/ppermute | solution.py:347
  160.8 3.8 %collective-permute-start.10 = (bf16[128,512]{1,0:T(8,128)(2,1)S(1)}, bf16[128,512]{1,0:T(8,128)(2,1)S(1)}, u32[]{:S(2)}, u32[]{:S(2)}) collective-permute-start(bf16[128,512]{1,0:T(8,128)(2,1)S(1)} %key_backward.2.refs_1_), channel_id=1, source_target_pairs={{0,1},{1,0},{2,3},{3,2},{4,5},{5,4},{6,7},{7,6},{8,9},{9,8},{10,11... | collective-permute-start | bytes 393224 | tf_op jit(solution)/shard_map/ppermute | solution.py:347
  160.8 3.8 %collective-permute-start.16 = (bf16[128,512]{1,0:T(8,128)(2,1)S(1)}, bf16[128,512]{1,0:T(8,128)(2,1)S(1)}, u32[]{:S(2)}, u32[]{:S(2)}) collective-permute-start(bf16[128,512]{1,0:T(8,128)(2,1)S(1)} %collective-permute-done.15.refs_7_), channel_id=1, source_target_pairs={{0,1},{1,0},{2,3},{3,2},{4,5},{5,4},{6,7},{7,6},{8,9},{9,8},{10,11... | collective-permute-start | bytes 393224 | tf_op jit(solution)/shard_map/ppermute | solution.py:347
  161.3 3.3 %collective-permute-start.14 = (bf16[128,512]{1,0:T(8,128)(2,1)S(1)}, bf16[128,512]{1,0:T(8,128)(2,1)S(1)}, u32[]{:S(2)}, u32[]{:S(2)}) collective-permute-start(bf16[128,512]{1,0:T(8,128)(2,1)S(1)} %collective-permute-done.13.refs_5_), channel_id=1, source_target_pairs={{0,1},{1,0},{2,3},{3,2},{4,5},{5,4},{6,7},{7,6},{8,9},{9,8},{10,11... | collective-permute-start | bytes 393224 | tf_op jit(solution)/shard_map/ppermute | solution.py:347
  161.4 3.2 %collective-permute-start.12 = (bf16[128,512]{1,0:T(8,128)(2,1)S(1)}, bf16[128,512]{1,0:T(8,128)(2,1)S(1)}, u32[]{:S(2)}, u32[]{:S(2)}) collective-permute-start(bf16[128,512]{1,0:T(8,128)(2,1)S(1)} %collective-permute-done.11.refs_3_), channel_id=1, source_target_pairs={{0,1},{1,0},{2,3},{3,2},{4,5},{5,4},{6,7},{7,6},{8,9},{9,8},{10,11... | collective-permute-start | bytes 393224 | tf_op jit(solution)/shard_map/ppermute | solution.py:347
  168.9 1.2 collective-permute-start.35
  170.1 3.6 %collective-permute-start.36 = (f32[8,128]{1,0:T(8,128)S(1)}, f32[8,128]{1,0:T(8,128)S(1)}, u32[]{:S(2)}, u32[]{:S(2)}) collective-permute-start(f32[8,128]{1,0:T(8,128)S(1)} %add.81), channel_id=1, source_target_pairs={{0,2},{1,3},{2,0},{3,1},{4,6},{5,7},{6,4},{7,5},{8,10},{9,11},{10,... | collective-permute-start | bytes 12296 | tf_op jit(solution)/shard_map/ppermute | solution.py:347
  173.7 3.6 %collective-permute-start.37 = (f32[8,128]{1,0:T(8,128)S(1)}, f32[8,128]{1,0:T(8,128)S(1)}, u32[]{:S(2)}, u32[]{:S(2)}) collective-permute-start(f32[8,128]{1,0:T(8,128)S(1)} %add.82), channel_id=1, source_target_pairs={{0,4},{1,5},{2,6},{3,7},{4,0},{5,1},{6,2},{7,3},{8,12},{9,13},{10,... | collective-permute-start | bytes 12296 | tf_op jit(solution)/shard_map/ppermute | solution.py:347
  182.6 5.1 %collective-permute-start.38 = (bf16[384,128]{1,0:T(8,128)(2,1)S(1)}, bf16[384,128]{1,0:T(8,128)(2,1)S(1)}, u32[]{:S(2)}, u32[]{:S(2)}) collective-permute-start(bf16[384,128]{1,0:T(8,128)(2,1)S(1)} %get-tuple-element.49), channel_id=1, source_target_pairs={{0,8},{8,0},{16,24},{24,16},{1,9},{9,1},{17,25},{25,17},{2,10},{10... | collective-permute-start | bytes 294920 | tf_op jit(solution)/shard_map/ppermute | solution.py:347
  182.7 6.6 %collective-permute-start.40 = (bf16[384,128]{1,0:T(8,128)(2,1)S(1)}, bf16[384,128]{1,0:T(8,128)(2,1)S(1)}, u32[]{:S(2)}, u32[]{:S(2)}) collective-permute-start(bf16[384,128]{1,0:T(8,128)(2,1)S(1)} %get-tuple-element.50), channel_id=1, source_target_pairs={{0,24},{8,16},{16,8},{24,0},{1,25},{9,17},{17,9},{25,1},{2,26},{10... | collective-permute-start | bytes 294920 | tf_op jit(solution)/shard_map/ppermute | solution.py:347
  184.7 8.3 %collective-permute-start.39 = (bf16[384,128]{1,0:T(8,128)(2,1)S(1)}, bf16[384,128]{1,0:T(8,128)(2,1)S(1)}, u32[]{:S(2)}, u32[]{:S(2)}) collective-permute-start(bf16[384,128]{1,0:T(8,128)(2,1)S(1)} %get-tuple-element.51), channel_id=1, source_target_pairs={{0,16},{8,24},{16,0},{24,8},{1,17},{9,25},{17,1},{25,9},{2,18},{10... | collective-permute-start | bytes 294920 | tf_op jit(solution)/shard_map/ppermute | solution.py:347
  193.1 23.7 %copy-start.6 = (f32[4,384,128]{2,1,0:T(8,128)S(1)}, f32[4,384,128]{2,1,0:T(8,128)}, u32[]{:S(2)}) copy-start(f32[4,384,128]{2,1,0:T(8,128)} %pad_maximum_fusion.base_ref) | copy-start | bytes 2359300
  193.1 23.7 %copy-start.9 = (f32[384,128]{1,0:T(8,128)S(1)}, f32[384,128]{1,0:T(8,128)}, u32[]{:S(2)}) copy-start(f32[384,128]{1,0:T(8,128)} %get-tuple-element.35.p_ref) | copy-start | bytes 589828
  193.1 23.6 %collective-permute-start.43 = (bf16[384,128]{1,0:T(8,128)(2,1)S(1)}, bf16[384,128]{1,0:T(8,128)(2,1)S(1)}, u32[]{:S(2)}, u32[]{:S(2)}) collective-permute-start(bf16[384,128]{1,0:T(8,128)(2,1)S(1)} %get-tuple-element.32), channel_id=1, source_target_pairs={{0,24},{8,16},{16,8},{24,0},{1,25},{9,17},{17,9},{25,1},{2,26},{10... | collective-permute-start | bytes 294920 | tf_op jit(solution)/shard_map/ppermute | solution.py:347
  195.2 21.5 %collective-permute-start.42 = (bf16[384,128]{1,0:T(8,128)(2,1)S(1)}, bf16[384,128]{1,0:T(8,128)(2,1)S(1)}, u32[]{:S(2)}, u32[]{:S(2)}) collective-permute-start(bf16[384,128]{1,0:T(8,128)(2,1)S(1)} %get-tuple-element.32), channel_id=1, source_target_pairs={{0,16},{8,24},{16,0},{24,8},{1,17},{9,25},{17,1},{25,9},{2,18},{10... | collective-permute-start | bytes 294920 | tf_op jit(solution)/shard_map/ppermute | solution.py:347
  195.2 21.5 %collective-permute-start.41 = (bf16[384,128]{1,0:T(8,128)(2,1)S(1)}, bf16[384,128]{1,0:T(8,128)(2,1)S(1)}, u32[]{:S(2)}, u32[]{:S(2)}) collective-permute-start(bf16[384,128]{1,0:T(8,128)(2,1)S(1)} %get-tuple-element.32), channel_id=1, source_target_pairs={{0,8},{8,0},{16,24},{24,16},{1,9},{9,1},{17,25},{25,17},{2,10},{10... | collective-permute-start | bytes 294920 | tf_op jit(solution)/shard_map/ppermute | solution.py:347

commit v4 on v3

v4 whole, which is shorter than its diff:
```python
import functools

import jax
import jax.numpy as jnp
from jax import lax
from jax.experimental import pallas as pl
from jax.experimental.pallas import tpu as pltpu
from jax.sharding import PartitionSpec as P

HEAD = 128
WARMUP = 2000
STEPS_TOTAL = 100000
FRAG_COLS = 128


BETA_ONE = 0.9
BETA_TWO = 0.95
ADAM_EPS = 1e-08
DECAY = 0.1
PEAK_RATE = 0.0003
CLIP_NORM = 1.0
OUTER_MU = 0.9
OUTER_RATE = 0.7
MIX_LOCAL = 0.5

MIB = 1 << 20


def in_hbm(*arrays):
    return [pltpu.with_memory_space_constraint(a, pltpu.HBM) for a in arrays]


def params_of(limit):
    return pltpu.CompilerParams(vmem_limit_bytes=limit * MIB)


def cost(flops, moved):
    return pl.CostEstimate(flops=int(flops), bytes_accessed=int(moved), transcendentals=0)


def copy_kernel(src_ref, out_ref):
    out_ref[...] = src_ref[...].reshape(out_ref.shape)


def pack_kernel(me_ref, src_ref, out_ref):
    out_ref[...] = src_ref[...]


def pack(tokens, me, offset, half, count, rows):
    return pl.pallas_call(
        pack_kernel,
        out_shape=jax.ShapeDtypeStruct((count, rows), tokens.dtype),
        grid_spec=pltpu.PrefetchScalarGridSpec(
            num_scalar_prefetch=1,
            grid=(1,),
            in_specs=[pl.BlockSpec((count, rows), lambda i, me: (half, me[0] ^ offset))],
            out_specs=pl.BlockSpec((count, rows), lambda i, me: (0, 0)),
        ),
        compiler_params=params_of(4),
        cost_estimate=cost(0, 4 * count * rows),
        name="pack",
    )(me, *in_hbm(tokens))


def transpose_kernel(*refs):
    *x_refs, out_ref = refs
    count = x_refs[0].shape[0]
    for j, ref in enumerate(x_refs):
        out_ref[:, j * count:(j + 1) * count] = ref[...].T


def transpose_tokens(blocks):
    count, rows = blocks[0].shape
    step = 256
    return pl.pallas_call(
        transpose_kernel,
        out_shape=jax.ShapeDtypeStruct((rows, len(blocks) * count), blocks[0].dtype),
        grid=(rows // step,),
        in_specs=[pl.BlockSpec((count, step), lambda i: (0, i))] * len(blocks),
        out_specs=pl.BlockSpec((step, len(blocks) * count), lambda i: (i, 0)),
        compiler_params=params_of(8),
        cost_estimate=cost(0, 4 * len(blocks) * count * rows),
        name="transpose_tokens",
    )(*blocks)


def cast_kernel(src_ref, out_ref):
    out_ref[...] = src_ref[...].astype(out_ref.dtype)


def cast_left(array, width):
    rows = array.shape[0]
    block = pl.BlockSpec((256, width), lambda i: (i, 0))
    return pl.pallas_call(
        cast_kernel,
        out_shape=jax.ShapeDtypeStruct((rows, width), jnp.bfloat16),
        grid=(rows // 256,),
        in_specs=[block],
        out_specs=block,
        compiler_params=params_of(8),
        cost_estimate=cost(0, 6 * rows * width),
        name="cast_left",
    )(*in_hbm(array))


def partial_kernel(*refs):
    *x_refs, w_ref, out_ref = refs
    for m, ref in enumerate(x_refs):
        out_ref[m] = jnp.dot(ref[...], w_ref[...], preferred_element_type=jnp.float32).astype(out_ref.dtype)


def partial_keys(blocks, key_weights):
    count, rows = blocks[0].shape
    width = key_weights.shape[1]
    return pl.pallas_call(
        partial_kernel,
        out_shape=jax.ShapeDtypeStruct((len(blocks), count, width), jnp.bfloat16),
        compiler_params=params_of(12),
        cost_estimate=cost(2 * len(blocks) * count * rows * width, 2 * len(blocks) * count * rows),
        name="partial_keys",
    )(*blocks, key_weights)


def summed_kernel(*refs):
    half = (len(refs) - 2) // 2
    x_refs, (w_ref, add_ref), out_refs = refs[:half], refs[half:half + 2], refs[half + 2:]
    for m, ref in enumerate(x_refs):
        total = jnp.dot(ref[...], w_ref[...], preferred_element_type=jnp.float32)
        out_refs[m][...] = (total + add_ref[m].astype(jnp.float32)).astype(out_refs[m].dtype)


def summed_keys(blocks, key_weights, others):
    count, rows = blocks[0].shape
    width = key_weights.shape[1]
    return pl.pallas_call(
        summed_kernel,
        out_shape=[jax.ShapeDtypeStruct((count, width), jnp.bfloat16)] * len(blocks),
        compiler_params=params_of(12),
        cost_estimate=cost(2 * len(blocks) * count * rows * width, 2 * len(blocks) * count * rows),
        name="summed_keys",
    )(*blocks, key_weights, others)


def key_kernel(*refs):
    *part_refs, cot_ref, out_ref = refs
    raw = sum(ref[...].astype(jnp.float32) for ref in part_refs)
    for h in range(raw.shape[1] // HEAD):
        cols = slice(h * HEAD, (h + 1) * HEAD)
        head = raw[:, cols]
        inverse = lax.rsqrt(jnp.mean(head * head, axis=1, keepdims=True) + 1e-06)
        normed = head * inverse
        upper = cot_ref[:, cols].astype(jnp.float32)
        back = inverse * (upper - normed * jnp.mean(upper * normed, axis=1, keepdims=True))
        out_ref[:, cols] = back.astype(out_ref.dtype)


def key_backward(parts, incoming, half):
    block = pl.BlockSpec(parts[0].shape, lambda i: (0, 0))
    cot = pl.BlockSpec(parts[0].shape, lambda i: (half, 0))
    size = parts[0].size
    return pl.pallas_call(
        key_kernel,
        out_shape=jax.ShapeDtypeStruct(parts[0].shape, jnp.bfloat16),
        grid=(1,),
        in_specs=[block] * len(parts) + [cot],
        out_specs=block,
        compiler_params=params_of(8),
        cost_estimate=cost(60 * size, 12 * size),
        name="key_backward",
    )(*parts, incoming)


def grad_kernel(counts, has_base, last, *refs):
    refs = list(refs)
    place_ref = refs.pop(0)
    terms = []
    for count in counts:
        terms.append((refs.pop(0), refs[:count]))
        del refs[:count]
    base = refs.pop(0) if has_base else None
    square_in, due_in = (refs.pop(0), refs.pop(0)) if last and has_base else (None, None)
    out_ref = refs.pop(0)
    sq_ref, due_ref = (refs.pop(0), refs.pop(0)) if last else (None, None)
    joined = refs

    @pl.when(pl.program_id(0) == 0)
    def _():
        for (_, blocks), held in zip(terms, joined):
            depth = blocks[0].shape[0]
            for j, block in enumerate(blocks):
                held[j * depth:(j + 1) * depth, :] = block[...]
        if last:
            sq_ref[...] = square_in[...] if has_base else jnp.zeros_like(sq_ref)

    total = base[...] if has_base else None
    for (x_ref, _), held in zip(terms, joined):
        term = jnp.dot(x_ref[...], held[...], preferred_element_type=jnp.float32)
        total = term if total is None else total + term
    out_ref[...] = total
    if last:
        rows, width = total.shape
        squares = (total * total).reshape(rows // 8, 8, width).sum(axis=0)
        folded = squares[:, :HEAD]
        for h in range(1, width // HEAD):
            folded = folded + squares[:, h * HEAD:(h + 1) * HEAD]
        sq_ref[...] += folded
        heads = width // FRAG_COLS
        mine = place_ref[0] - (0 if has_base else heads)
        mine = jnp.minimum(jnp.maximum(mine, 0), heads - 1) * FRAG_COLS
        column = out_ref[:, pl.ds(pl.multiple_of(mine, FRAG_COLS), FRAG_COLS)]
        if has_base:
            column = jnp.where(place_ref[0] < heads, column, due_in[...])
        due_ref[...] = column


def gradient(place, terms, base=None, square=None, due=None, last=True):
    rows = terms[0][0].shape[0]
    width = terms[0][1][0].shape[1]
    step = 256
    row_block = lambda cols: pl.BlockSpec((step, cols), lambda i, p: (i, 0))
    fixed = pl.BlockSpec((8, HEAD), lambda i, p: (0, 0))
    args, specs, scratch = [], [], []
    for x, blocks, at in terms:
        args += [x, *blocks]
        depth = x.shape[1] // len(blocks)
        specs += [row_block(x.shape[1])]
        specs += [pl.BlockSpec((depth, width), lambda i, p, at=at: (at, 0))] * len(blocks)
        scratch.append(pltpu.VMEM((x.shape[1], width), jnp.bfloat16))
    if base is not None:
        args.append(base)
        specs.append(row_block(width))
        if last:
            args += [square, due]
            specs += [fixed, row_block(FRAG_COLS)]
    if last:
        shapes = [
            pltpu.HBM((rows, width), jnp.float32),
            jax.ShapeDtypeStruct((8, HEAD), jnp.float32),
            jax.ShapeDtypeStruct((rows, FRAG_COLS), jnp.float32),
        ]
        outs = [row_block(width), fixed, row_block(FRAG_COLS)]
    else:
        shapes = [jax.ShapeDtypeStruct((rows, width), jnp.float32)]
        outs = [row_block(width)]
    depth = sum(x.shape[1] for x, _, _ in terms)
    return pl.pallas_call(
        functools.partial(grad_kernel, [len(b) for _, b, _ in terms], base is not None, last),
        out_shape=shapes,
        grid_spec=pltpu.PrefetchScalarGridSpec(
            num_scalar_prefetch=1,
            grid=(rows // step,),
            in_specs=specs,
            out_specs=outs,
            scratch_shapes=scratch,
        ),
        compiler_params=params_of(20),
        cost_estimate=cost(2 * rows * width * depth, 2 * rows * depth + 4 * rows * width),
        name="gradient",
    )(place, *args)


def adam(old, first, second, grad, scalars):
    factor, rate, inv_one, inv_two = (scalars[i] for i in range(4))
    clipped = grad * factor
    first_new = BETA_ONE * first + (1.0 - BETA_ONE) * clipped
    second_new = BETA_TWO * second + (1.0 - BETA_TWO) * clipped * clipped
    update = rate * (
        first_new * inv_one / (jnp.sqrt(second_new * inv_two) + ADAM_EPS) + DECAY * old
    )
    return update, first_new, second_new


def adam_kernel(extra, sc_ref, w_ref, m_ref, v_ref, gk_ref, gv_ref, *refs):
    w_out, m_out, v_out, *done = refs[extra:]
    width = gk_ref.shape[1]
    for g_ref, cols in ((gk_ref, slice(0, width)), (gv_ref, slice(width, 2 * width))):
        old = w_ref[:, cols]
        update, first_new, second_new = adam(old, m_ref[:, cols], v_ref[:, cols], g_ref[...], sc_ref)
        w_out[:, cols] = old - update
        m_out[:, cols] = first_new
        v_out[:, cols] = second_new
    for ref in done:
        ref[...] = jnp.zeros_like(ref)


def adam_rows(scalars, state, first, last, into=()):
    rows, width = state[0].shape
    step = 256
    full = pl.BlockSpec((step, width), lambda i: (i + first, 0))
    half = pl.BlockSpec((step, width // 2), lambda i: (i + first, 0))
    shapes = [pltpu.HBM((rows, width), jnp.float32)] * 3
    outs = [full] * 3
    if not into:
        shapes.append(jax.ShapeDtypeStruct((8, HEAD), jnp.float32))
        outs.append(pl.BlockSpec((8, HEAD), lambda i: (0, 0)))
    count = (last - first) * step
    return pl.pallas_call(
        functools.partial(adam_kernel, len(into)),
        out_shape=shapes,
        grid=(last - first,),
        in_specs=[pl.BlockSpec(memory_space=pltpu.SMEM), full, full, full, half, half]
        + [pl.BlockSpec(memory_space=pl.ANY)] * len(into),
        out_specs=outs,
        input_output_aliases={6 + i: i for i in range(len(into))},
        compiler_params=params_of(24),
        cost_estimate=cost(20 * count * width, 28 * count * width),
        name="adam_rows",
    )(scalars, *in_hbm(*state), *in_hbm(*into))


def frag_kernel(place_ref, sc_ref, w_ref, m_ref, v_ref, g_ref, inner_ref, *out_refs):
    blocks, part, _ = w_ref.shape
    for j in range(blocks):
        at = pl.multiple_of((place_ref[1] ^ j) * part, 8)
        old = w_ref[j]
        update, _, _ = adam(old, m_ref[j], v_ref[j], g_ref[pl.ds(at, part), :], sc_ref)
        inner_ref[j] = old - update
        out_refs[j][...] = update.astype(out_refs[j].dtype)


def adam_frag(place, scalars, old, first, second, grad):
    blocks, part, width = old.shape
    smem = pl.BlockSpec(memory_space=pltpu.SMEM)
    vmem = pl.BlockSpec(memory_space=pltpu.VMEM)
    return pl.pallas_call(
        frag_kernel,
        out_shape=[jax.ShapeDtypeStruct(old.shape, jnp.float32)]
        + [jax.ShapeDtypeStruct((part, width), jnp.bfloat16)] * blocks,
        in_specs=[smem, smem] + [vmem] * 4,
        out_specs=[vmem] * (1 + blocks),
        compiler_params=params_of(12),
        cost_estimate=cost(20 * old.size, 22 * old.size),
        name="adam_frag",
    )(place, scalars, old, first, second, grad)


def pick_kernel(place_ref, *refs):
    half = len(refs) // 2
    for src_ref, out_ref in zip(refs[:half], refs[half:]):
        out_ref[...] = src_ref[...].reshape(out_ref.shape)


def due_columns(place, part, *arrays):
    blocks = arrays[0].shape[0] // part
    at = (lambda j, p: (p[1] ^ j, p[0])) if blocks > 1 else (lambda j, p: (0, p[0]))
    return pl.pallas_call(
        pick_kernel,
        out_shape=[jax.ShapeDtypeStruct((blocks, part, FRAG_COLS), a.dtype) for a in arrays],
        grid_spec=pltpu.PrefetchScalarGridSpec(
            num_scalar_prefetch=1,
            grid=(blocks,),
            in_specs=[pl.BlockSpec((part, FRAG_COLS), at)] * len(arrays),
            out_specs=[pl.BlockSpec((1, part, FRAG_COLS), lambda j, p: (j, 0, 0))] * len(arrays),
        ),
        compiler_params=params_of(8),
        cost_estimate=cost(0, 8 * blocks * part * FRAG_COLS * len(arrays)),
        name="due_columns",
    )(place, *in_hbm(*arrays))


def duplicate(array):
    rows, width = array.shape
    step = rows // 4 if rows % 32 == 0 else rows
    block = pl.BlockSpec((step, width), lambda i: (i, 0))
    return pl.pallas_call(
        copy_kernel,
        out_shape=pltpu.HBM((rows, width), array.dtype),
        grid=(rows // step,),
        in_specs=[block],
        out_specs=block,
        compiler_params=params_of(8),
        cost_estimate=cost(0, 8 * array.size),
        name="duplicate",
    )(*in_hbm(array))


def outer_kernel(replicas, place_ref, *refs):
    share = 1.0 / replicas
    base_refs, sum_refs = refs[3:3 + replicas], refs[3 + replicas:3 + 2 * replicas]
    inner_ref, a_ref, p_ref, m_ref, own_ref, w_out, a_out, m_out = refs[3 + 2 * replicas:]
    scale = share * (1.0 + OUTER_MU) * OUTER_RATE
    for j in range(replicas):

        @pl.when(pl.program_id(0) == j)
        def _():
            fresh = base_refs[j][...] - scale * sum_refs[j][...].astype(jnp.float32)
            w_out[...] = MIX_LOCAL * inner_ref[0] + (1.0 - MIX_LOCAL) * fresh

    @pl.when(pl.program_id(0) == 0)
    def _():
        pseudo = p_ref[...] + share * own_ref[...]
        new_moment = OUTER_MU * m_ref[...] + pseudo
        m_out[...] = new_moment
        a_out[...] = a_ref[...] - OUTER_RATE * (OUTER_MU * new_moment + pseudo)


def outer_step(place, outputs, base, sums, inner, anchor, pseudo, momentum, own_sum):
    replicas, part = inner.shape[0], inner.shape[1]
    mixed = pl.BlockSpec((part, FRAG_COLS), lambda j, p: (p[1] ^ j, p[0]))
    pieces = pl.BlockSpec((1, part, FRAG_COLS), lambda j, p: (j, 0, 0))
    due = pl.BlockSpec((part, FRAG_COLS), lambda j, p: (0, p[0]))
    plain = pl.BlockSpec((part, FRAG_COLS), lambda j, p: (0, 0))
    whole = pl.BlockSpec(memory_space=pl.ANY)
    return pl.pallas_call(
        functools.partial(outer_kernel, replicas),
        out_shape=[pltpu.HBM(a.shape, a.dtype) for a in outputs],
        grid_spec=pltpu.PrefetchScalarGridSpec(
            num_scalar_prefetch=1,
            grid=(replicas,),
            in_specs=[whole] * 3 + [plain] * (2 * replicas) + [pieces] + [plain] * 4,
            out_specs=[mixed, due, due],
        ),
        input_output_aliases={1: 0, 2: 1, 3: 2},
        compiler_params=params_of(12),
        cost_estimate=cost(10 * replicas * part * FRAG_COLS, 20 * replicas * part * FRAG_COLS),
        name="outer_step",
    )(place, *in_hbm(*outputs), *base, *sums, inner, anchor, pseudo, momentum, own_sum)


def swap(block, axis, offset):
    count = lax.axis_size(axis)
    return lax.ppermute(block, axis, [(i, i ^ offset) for i in range(count)])


def after(value, *others):
    return lax.optimization_barrier((value,) + others)[0]


class Line:
    def __init__(self, axis, window):
        self.axis, self.window, self.ended = axis, window, []

    def swap(self, block, offset):
        if len(self.ended) >= self.window:
            block = after(block, self.ended[-self.window])
        self.ended.append(swap(block, self.axis, offset))
        return self.ended[-1]


def body(
    tokens,
    cotangent,
    weights,
    first_moment,
    second_moment,
    anchor,
    momentum,
    due_fragment,
    step_count,
):
    inputs, incoming, params = tokens[0], cotangent[0], weights[0]
    tok_rows = inputs.shape[0]
    kv_width = incoming.shape[1] // 2
    rows = params.shape[0]
    part = anchor.shape[0]
    replicas = lax.axis_size("rep")
    shards = lax.axis_size("fsdp")
    me = jnp.reshape(lax.axis_index("fsdp"), (1,)).astype(jnp.int32)
    place = jnp.stack([due_fragment[0], lax.axis_index("rep").astype(jnp.int32)])
    th = tok_rows // 2
    chips = range(2, shards, 2)
    order = sorted(range(2, shards), key=lambda k: (-bin(k >> 1).count("1"), k & 1, k)) + [1]

    line = Line("fsdp", 3)
    blocks = [[None] * shards, [None] * shards]

    def send_tokens(half, offsets):
        for k in offsets:
            blocks[half][k] = line.swap(pack(inputs, me, k, half, th, rows), k)

    send_tokens(0, order)
    early = blocks[0][order[0]]

    rep_line = Line("rep", 1)
    place_early = after(place, early)
    old, old_first, old_second = due_columns(place_early, part, params, first_moment[0], second_moment[0])
    anchor_cols, moment_cols = (c[0] for c in due_columns(place_early, part, anchor, momentum))
    old_sum = old[0]
    for k in range(1, replicas):
        old_sum = old_sum + rep_line.swap(old[k], k)
    pseudo_old = anchor_cols - old_sum / replicas
    base = anchor_cols - OUTER_RATE * (OUTER_MU * (OUTER_MU * moment_cols + pseudo_old) + pseudo_old)
    base = [base] + [rep_line.swap(base, k) for k in range(1, replicas)]
    anchor_copy, momentum_copy = duplicate(anchor), duplicate(momentum)

    key_weights = cast_left(after(params, early), kv_width)

    def sum_keys(half):
        x = blocks[half]
        x[0] = pack(inputs, me, 0, half, th, rows)
        theirs = swap(partial_keys(x[1::2], key_weights), "fsdp", 1)
        return summed_keys(x[0::2], key_weights, theirs)

    def scatter_keys(half, parts):
        parts = [parts[0]] + [line.swap(parts[k // 2], k) for k in chips]
        return key_backward(parts, incoming, half)

    def gather(block):
        out = []
        for held in [block] + [line.swap(block, k) for k in chips]:
            out += [held, swap(held, "fsdp", 1)]
        return out

    cut = (len(order) + 1) // 2
    send_tokens(1, order[:cut])
    back = scatter_keys(0, sum_keys(0))
    send_tokens(1, order[cut:])
    keys = [gather(back)]
    flipped = [transpose_tokens(blocks[0])]
    values = gather(incoming[:, kv_width:])
    (grad_first,) = gradient(place, [(flipped[0], keys[0], 0)], last=False)
    blocks[1][1] = after(blocks[1][1], base[-1], anchor_copy, momentum_copy, grad_first, old_second)
    back = scatter_keys(1, sum_keys(1))
    keys.append(gather(back))
    flipped.append(transpose_tokens(blocks[1]))
    grad_values, square, due = gradient(place, [(flipped[h], values, h) for h in range(2)])
    grad_keys, square, due = gradient(place, [(flipped[1], keys[1], 0)], grad_first, square, due)

    square = square + swap(square, "fsdp", 1)
    square = sum([swap(square, "fsdp", k) for k in chips], square)
    square = jnp.sum(square)
    factor = jnp.minimum(1.0, CLIP_NORM / (jnp.sqrt(square) + 1e-06))
    steps_now = step_count[0].astype(jnp.float32)
    plan = jnp.minimum(1.0, steps_now / WARMUP) * (
        0.55 + 0.45 * jnp.cos(jnp.pi * steps_now / STEPS_TOTAL)
    )
    rate = PEAK_RATE * plan
    inv_one = 1.0 / (1.0 - jnp.power(BETA_ONE, steps_now))
    inv_two = 1.0 / (1.0 - jnp.power(BETA_TWO, steps_now))
    scalars = jnp.stack([factor, rate, inv_one, inv_two])

    state = (params, first_moment[0], second_moment[0], grad_keys, grad_values)
    inner, *update = adam_frag(place, scalars, old, old_first, old_second, due)
    steps = rows // 256
    *results, ticket = adam_rows(scalars, state, 0, steps // 2)
    own_sum = update[0].astype(jnp.float32)
    for k in range(1, replicas):
        own_sum = own_sum + swap(update[k], "rep", k).astype(jnp.float32)
    own_sum = after(own_sum, ticket)
    sums = [own_sum.astype(jnp.bfloat16)]
    sums += [swap(sums[0], "rep", k) for k in range(1, replicas)]
    results = adam_rows(scalars, state, steps // 2, steps, results)
    weights_out, anchor_out, momentum_out = outer_step(
        place,
        (results[0], anchor_copy, momentum_copy),
        base,
        sums,
        inner,
        anchor_cols,
        pseudo_old,
        moment_cols,
        own_sum,
    )
    plan_out = jnp.reshape(plan, (1,))
    return (
        weights_out[None],
        results[1][None],
        results[2][None],
        anchor_out,
        momentum_out,
        plan_out,
    )


def solution(mesh):
    tokens_spec = P("rep", "fsdp", None)
    outer_spec = P(("fsdp", "rep"), None)
    return jax.shard_map(
        body,
        mesh=mesh,
        in_specs=(tokens_spec,) * 5 + (outer_spec,) * 2 + (P(), P()),
        out_specs=(tokens_spec,) * 3 + (outer_spec,) * 2 + (P(),),
        check_vma=False,
    )
```

time: 224 us -> 219 us (0.978)
  local copies, waits for them, and re-layouts: 14.2 us -> 2.63 us
  starting transfers between devices: 52.5 us -> 61.4 us
  other arithmetic: 4.08 us -> 1.58 us
    ppermute x44 -> x59, waiting for transfers between devices: 36.4 us -> 68.4 us  [swap(): return lax.ppermute(block, axis, [(i, i ^ offset) for i in range(count)])]
    all_to_all x2 -> x0, waiting for transfers between devices: 31.9 us -> none  [body(): lax.all_to_all(sent, 'fsdp', 0, 0, tiled=True)]
    ppermute x44 -> x59, starting transfers between devices: 42.8 us -> 61.4 us  [swap(): return lax.ppermute(block, axis, [(i, i ^ offset) for i in range(count)])]
    all_to_all x2 -> x0, starting transfers between devices: 9.63 us -> none  [body(): lax.all_to_all(sent, 'fsdp', 0, 0, tiled=True)]
    slice x11 -> x1, local copies, waits for them, and re-layouts: 6.16 us -> 0.02 us  [body(): values = gather(incoming[:, kv_width:])]
    unnamed x26 -> x40, local copies, waits for them, and re-layouts: 7.2 us -> 2.57 us
    pallas_call x19 -> x34, Pallas kernels: 71.5 us -> 71.9 us  [the longest x2 19.7 us: adam_rows(): pl.pallas_call(functools.partial(adam_kernel, len(into)), out_shape=shape...]
  transfers between devices with their start and end apart: 46 -> 59, of which waited for: 18 -> 24; matrix products, arithmetic and copies ran while one was open for 5% -> 0% of each run, Pallas kernels for 28% -> 32%
where the time goes in v4:
time: 219 us; the launch traced here: 218 us
  Pallas kernels  79 us (36%)
  waiting for transfers between devices  68.4 us (31%)
  starting transfers between devices  61.4 us (28%)
  between operations  4.61 us (2%)
  local copies, waits for them, and re-layouts  2.63 us (1%)
    ppermute x59, waiting for transfers between devices, swap(): return lax.ppermute(block, axis, [(i, i ^ offset) for i in range(count)])  68.4 us
    ppermute x59, starting transfers between devices, swap(): return lax.ppermute(block, axis, [(i, i ^ offset) for i in range(count)])  61.4 us
    pallas_call x2, Pallas kernels, adam_rows(): pl.pallas_call(functools.partial(adam_kernel, len(into)), out_shape=shape...  19.7 us
    pallas_call x16, Pallas kernels, pack(): pl.pallas_call(pack_kernel, out_shape=jax.ShapeDtypeStruct((count, rows),...  18.6 us
    pallas_call x3, Pallas kernels, gradient(): pl.pallas_call(functools.partial(grad_kernel, [len(b) for _, b, _ in term...  14.1 us
    pallas_call x2, Pallas kernels, duplicate(): pl.pallas_call(copy_kernel, out_shape=pltpu.HBM((rows, width), array.dtyp...  7.12 us
    pallas_call x2, Pallas kernels, due_columns(): pl.pallas_call(pick_kernel, out_shape=[jax.ShapeDtypeStruct((blocks, part...  4.74 us
  transfers between devices with their start and end apart: 59, of which 24 were waited for; matrix products, arithmetic and copies ran while one was open for 0% of the time, Pallas kernels for 32%

profile of v4, /device:TPU:0, one launch (start us, length us, event | category | flops | bytes accessed | tf_op | source)
XLA Modules:
  0.0 217.6 jit_solution(1086776067518618096)
XLA Ops:
  1.7 4.0 %collective-permute-start.1 = (bf16[128,1536]{1,0:T(8,128)(2,1)S(1)}, bf16[128,1536]{1,0:T(8,128)(2,1)S(1)}, u32[]{:S(2)}, u32[]{:S(2)}) collective-permute-start(bf16[128,1536]{1,0:T(8,128)(2,1)S(1)} %pack.21), channel_id=1, source_target_pairs={{0,6},{1,7},{2,4},{3,5},{4,2},{5,3},{6,0},{7,1},{8,14},{9,15},{10,... | collective-permute-start | bytes 1179656 | tf_op jit(solution)/shard_map/ppermute | solution.py:422
  9.7 5.9 %collective-permute-done.1.refs_3_.refs_6_ = bf16[128,1536]{1,0:T(8,128)(2,1)S(1)} collective-permute-done((bf16[128,1536]{1,0:T(8,128)(2,1)S(1)}, bf16[128,1536]{1,0:T(8,128)(2,1)S(1)}, u32[]{:S(2)}, u32[]{:S(2)}) %collective-permute-start.1) | collective-permute-done | bytes 393248 | tf_op jit(solution)/shard_map/ppermute | solution.py:422
  15.6 2.0 collective-permute-start.2
  17.6 1.8 pack.25
  19.4 1.8 pack.23
  21.1 1.8 pack.22
  22.9 1.6 collective-permute-done.refs_1_.refs_2_
  24.6 6.3 %collective-permute-done.4.refs_3_.refs_7_ = bf16[128,1536]{1,0:T(8,128)(2,1)S(1)} collective-permute-done((bf16[128,1536]{1,0:T(8,128)(2,1)S(1)}, bf16[128,1536]{1,0:T(8,128)(2,1)S(1)}, u32[]{:S(2)}, u32[]{:S(2)}) %collective-permute-start.4) | collective-permute-done | bytes 393248 | tf_op jit(solution)/shard_map/ppermute | solution.py:422
  30.9 1.9 collective-permute-start.5
  36.9 3.5 %cast_left.1.refs_4_ = bf16[1536,512]{1,0:T(8,128)(2,1)S(1)} custom-call(f32[1536,1024]{1,0:T(8,128)} %bitcast.55), custom_call_target="tpu_custom_call" | custom-call | bytes 4718592 | tf_op jit(solution)/shard_map/cast_left/pallas_call | solution.py:94
  40.4 3.1 %due_columns.3 = (f32[4,384,128]{2,1,0:T(8,128)S(1)}, f32[4,384,128]{2,1,0:T(8,128)S(1)}, f32[4,384,128]{2,1,0:T(8,128)S(1)}) custom-call(s32[2]{0:T(128)S(1)} %pad_add_fusion.place_ref.refs_0_, f32[1536,1024]{1,0:T(8,128)} %bitcast.56, f32[1536,1024]{1,0:T(8,128)} %bitcast.59, f32[1536,1024]{1,0:T(8,128)} %bitcast.62), custom_call_target="tpu_custom_call" | custom-call | bytes 4718592 | tf_op jit(solution)/shard_map/due_columns/pallas_call | solution.py:346
  45.3 1.3 collective-permute-start.8
  48.0 1.6 collective-permute-start.12
  51.7 1.3 collective-permute-start.18
  54.6 3.7 %collective-permute-done.8.refs_6_.refs_3_ = bf16[128,1536]{1,0:T(8,128)(2,1)S(1)} collective-permute-done((bf16[128,1536]{1,0:T(8,128)(2,1)S(1)}, bf16[128,1536]{1,0:T(8,128)(2,1)S(1)}, u32[]{:S(2)}, u32[]{:S(2)}) %collective-permute-start.8) | collective-permute-done | bytes 393248 | tf_op jit(solution)/shard_map/ppermute | solution.py:422
  58.7 2.6 %collective-permute-start.13 = (f32[384,128]{1,0:T(8,128)S(1)}, f32[384,128]{1,0:T(8,128)S(1)}, u32[]{:S(2)}, u32[]{:S(2)}) collective-permute-start(f32[384,128]{1,0:T(8,128)S(1)} %get-tuple-element.87), channel_id=1, source_target_pairs={{0,16},{8,24},{16,0},{24,8},{1,17},{9,25},{17,1},{25,9},{2,18},{10... | collective-permute-start | bytes 589832 | tf_op jit(solution)/shard_map/ppermute | solution.py:422
  62.3 7.2 %collective-permute-done.13 = f32[384,128]{1,0:T(8,128)S(1)} collective-permute-done((f32[384,128]{1,0:T(8,128)S(1)}, f32[384,128]{1,0:T(8,128)S(1)}, u32[]{:S(2)}, u32[]{:S(2)}) %collective-permute-start.13) | collective-permute-done | bytes 196640 | tf_op jit(solution)/shard_map/ppermute | solution.py:422
  69.5 3.5 %collective-permute-start.14 = (f32[384,128]{1,0:T(8,128)S(1)}, f32[384,128]{1,0:T(8,128)S(1)}, u32[]{:S(2)}, u32[]{:S(2)}) collective-permute-start(f32[384,128]{1,0:T(8,128)S(1)} %get-tuple-element.88), channel_id=1, source_target_pairs={{0,24},{8,16},{16,8},{24,0},{1,25},{9,17},{17,9},{25,1},{2,26},{10... | collective-permute-start | bytes 589832 | tf_op jit(solution)/shard_map/ppermute | solution.py:422
  74.0 1.2 collective-permute-start.21
  76.0 1.6 collective-permute-start.10
  80.7 1.6 due_columns.2
  83.2 1.7 collective-permute-start.23
  85.7 1.0 collective-permute-start.15
  87.0 1.6 collective-permute-start.29
  88.5 5.8 %collective-permute-done.23.refs_3_.refs_1_ = bf16[128,1536]{1,0:T(8,128)(2,1)S(1)} collective-permute-done((bf16[128,1536]{1,0:T(8,128)(2,1)S(1)}, bf16[128,1536]{1,0:T(8,128)(2,1)S(1)}, u32[]{:S(2)}, u32[]{:S(2)}) %collective-permute-start.23) | collective-permute-done | bytes 393248 | tf_op jit(solution)/shard_map/ppermute | solution.py:422
  94.3 1.2 collective-permute-start.24
  95.5 3.4 %collective-permute-done.26.refs_5_.refs_2_ = bf16[128,1536]{1,0:T(8,128)(2,1)S(1)} collective-permute-done((bf16[128,1536]{1,0:T(8,128)(2,1)S(1)}, bf16[128,1536]{1,0:T(8,128)(2,1)S(1)}, u32[]{:S(2)}, u32[]{:S(2)}) %collective-permute-start.26) | collective-permute-done | bytes 393248 | tf_op jit(solution)/shard_map/ppermute | solution.py:422
  99.3 2.0 collective-permute-start.16
  101.8 2.8 %collective-permute-done.27.refs_6_ = bf16[128,512]{1,0:T(8,128)(2,1)S(1)} collective-permute-done((bf16[128,512]{1,0:T(8,128)(2,1)S(1)}, bf16[128,512]{1,0:T(8,128)(2,1)S(1)}, u32[]{:S(2)}, u32[]{:S(2)}) %collective-permute-start.27) | collective-permute-done | bytes 131104 | tf_op jit(solution)/shard_map/ppermute | solution.py:422
  104.6 6.6 %collective-permute-done.16.refs_5_ = f32[384,128]{1,0:T(8,128)S(1)} collective-permute-done((f32[384,128]{1,0:T(8,128)S(1)}, f32[384,128]{1,0:T(8,128)S(1)}, u32[]{:S(2)}, u32[]{:S(2)}) %collective-permute-start.16) | collective-permute-done | bytes 196640 | tf_op jit(solution)/shard_map/ppermute | solution.py:422
  111.2 2.9 %collective-permute-start.17 = (f32[384,128]{1,0:T(8,128)S(1)}, f32[384,128]{1,0:T(8,128)S(1)}, u32[]{:S(2)}, u32[]{:S(2)}) collective-permute-start(f32[384,128]{1,0:T(8,128)S(1)} %get-tuple-element.91.refs_3_), channel_id=1, source_target_pairs={{0,24},{8,16},{16,8},{24,0},{1,25},{9,17},{17,9},{25,1},{2,26},{10... | collective-permute-start | bytes 589832 | tf_op jit(solution)/shard_map/ppermute | solution.py:422
  114.2 3.6 %duplicate.2.refs_1_ = f32[384,1024]{1,0:T(8,128)} custom-call(f32[384,1024]{1,0:T(8,128)} %src_ref.2), custom_call_target="tpu_custom_call" | custom-call | bytes 3145728 | tf_op jit(solution)/shard_map/duplicate/pallas_call | solution.py:365
  117.7 3.6 %duplicate.3.refs_2_ = f32[384,1024]{1,0:T(8,128)} custom-call(f32[384,1024]{1,0:T(8,128)} %src_ref.3), custom_call_target="tpu_custom_call" | custom-call | bytes 3145728 | tf_op jit(solution)/shard_map/duplicate/pallas_call | solution.py:365
  121.3 1.6 transpose_tokens.2.refs_1_
  123.0 3.3 %gradient.3.refs_10_ = f32[1536,512]{1,0:T(8,128)S(1)} custom-call(s32[2]{0:T(128)S(1)} %pad_add_fusion.place_ref.refs_0_, bf16[1536,1024]{1,0:T(8,128)(2,1)S(1)} %transpose_tokens.2.refs_1_, bf16[128,512]{1,0:T(8,128)(2,1)S(1)} %key_backward.2.refs_2_, bf16[128,512]{1,0:T(8,128)(2,1)S(1)} %collective-permute-done.22.refs_3_, ...), custom_call_target="tpu_custom_call" | custom-call | flops 1610612736 | bytes 6291456 | tf_op jit(solution)/shard_map/gradient/pallas_call | solution.py:246
  127.4 1.6 collective-permute-start.36
  129.0 1.3 collective-permute-start.34
  133.0 4.5 %collective-permute-done.36.refs_8_.refs_17_ = bf16[256,512]{1,0:T(8,128)(2,1)S(1)} collective-permute-done((bf16[256,512]{1,0:T(8,128)(2,1)S(1)}, bf16[256,512]{1,0:T(8,128)(2,1)S(1)}, u32[]{:S(2)}, u32[]{:S(2)}) %collective-permute-start.36) | collective-permute-done | bytes 262176 | tf_op jit(solution)/shard_map/ppermute | solution.py:422
  137.5 1.6 collective-permute-start.37
  139.6 3.4 %collective-permute-done.34.refs_6_.refs_15_ = bf16[256,512]{1,0:T(8,128)(2,1)S(1)} collective-permute-done((bf16[256,512]{1,0:T(8,128)(2,1)S(1)}, bf16[256,512]{1,0:T(8,128)(2,1)S(1)}, u32[]{:S(2)}, u32[]{:S(2)}) %collective-permute-start.34) | collective-permute-done | bytes 262176 | tf_op jit(solution)/shard_map/ppermute | solution.py:422
  143.0 1.7 collective-permute-start.35
  145.5 2.9 %collective-permute-done.35.refs_2_ = bf16[128,512]{1,0:T(8,128)(2,1)S(1)} collective-permute-done((bf16[128,512]{1,0:T(8,128)(2,1)S(1)}, bf16[128,512]{1,0:T(8,128)(2,1)S(1)}, u32[]{:S(2)}, u32[]{:S(2)}) %collective-permute-start.35) | collective-permute-done | bytes 131104 | tf_op jit(solution)/shard_map/ppermute | solution.py:422
  148.4 1.4 collective-permute-done.33.refs_1_
  150.6 1.3 collective-permute-start.41
  151.9 1.7 collective-permute-start.43
  153.6 1.6 transpose_tokens.3.refs_10_.refs_1_
  156.1 1.1 collective-permute-done.41.refs_6_
  157.2 1.4 collective-permute-done.43.refs_8_
  158.6 6.0 %gradient.4 = (f32[1536,512]{1,0:T(8,128)}, f32[8,128]{1,0:T(8,128)S(1)}, f32[1536,128]{1,0:T(8,128)S(1)}) custom-call(s32[2]{0:T(128)S(1)} %pad_add_fusion.place_ref.refs_0_, bf16[1536,1024]{1,0:T(8,128)(2,1)S(1)} %transpose_tokens.2.refs_1_, bf16[256,512]{1,0:T(8,128)(2,1)S(1)} %slice.20.refs_2_.refs_11_, ...), custom_call_target="tpu_custom_call" | custom-call | flops 3221225472 | bytes 9437184 | tf_op jit(solution)/shard_map/gradient/pallas_call | solution.py:246
  164.6 4.9 %gradient.5 = (f32[1536,512]{1,0:T(8,128)}, f32[8,128]{1,0:T(8,128)S(1)}, f32[1536,128]{1,0:T(8,128)S(1)}) custom-call(s32[2]{0:T(128)S(1)} %pad_add_fusion.place_ref.refs_0_, bf16[1536,1024]{1,0:T(8,128)(2,1)S(1)} %transpose_tokens.3.refs_10_.refs_1_, bf16[128,512]{1,0:T(8,128)(2,1)S(1)} %key_backward.3.refs_2_, ...), custom_call_target="tpu_custom_call" | custom-call | flops 1610612736 | bytes 6291456 | tf_op jit(solution)/shard_map/gradient/pallas_call | solution.py:246
  170.8 2.1 collective-permute-start.52
  172.9 1.1 collective-permute-start.51
  175.3 1.2 collective-permute-done.51
  176.5 1.1 collective-permute-done.50
  179.0 1.2 adam_frag.1
  180.3 1.3 collective-permute-start.54
  181.5 3.1 %collective-permute-start.55 = (bf16[384,128]{1,0:T(8,128)(2,1)S(1)}, bf16[384,128]{1,0:T(8,128)(2,1)S(1)}, u32[]{:S(2)}, u32[]{:S(2)}) collective-permute-start(bf16[384,128]{1,0:T(8,128)(2,1)S(1)} %get-tuple-element.133), channel_id=1, source_target_pairs={{0,24},{8,16},{16,8},{24,0},{1,25},{9,17},{17,9},{25,1},{2,26},{10... | collective-permute-start | bytes 294920 | tf_op jit(solution)/shard_map/ppermute | solution.py:422
  184.6 1.4 collective-permute-done.53
  186.1 3.6 %collective-permute-done.54 = bf16[384,128]{1,0:T(8,128)(2,1)S(1)} collective-permute-done((bf16[384,128]{1,0:T(8,128)(2,1)S(1)}, bf16[384,128]{1,0:T(8,128)(2,1)S(1)}, u32[]{:S(2)}, u32[]{:S(2)}) %collective-permute-start.54) | collective-permute-done | bytes 98336 | tf_op jit(solution)/shard_map/ppermute | solution.py:422
  189.7 1.5 collective-permute-start.58
  191.3 2.6 %collective-permute-start.57 = (bf16[384,128]{1,0:T(8,128)(2,1)S(1)}, bf16[384,128]{1,0:T(8,128)(2,1)S(1)}, u32[]{:S(2)}, u32[]{:S(2)}) collective-permute-start(bf16[384,128]{1,0:T(8,128)(2,1)S(1)} %convert_element_type.24.refs_7_), channel_id=1, source_target_pairs={{0,16},{8,24},{16,0},{24,8},{1,17},{9,25},{17,1},{25,9},{2,18},{10... | collective-permute-start | bytes 294920 | tf_op jit(solution)/shard_map/ppermute | solution.py:422
  194.2 9.8 %adam_rows.2 = (f32[1536,1024]{1,0:T(8,128)}, f32[1536,1024]{1,0:T(8,128)}, f32[1536,1024]{1,0:T(8,128)}, f32[8,128]{1,0:T(8,128)}) custom-call(f32[4]{0:T(128)S(1)} %pad_maximum_fusion.sc_ref, f32[1536,1024]{1,0:T(8,128)} %bitcast.57, f32[1536,1024]{1,0:T(8,128)} %bitcast.60, f32[1536,1024]{1,0:T(8,128)} %bitcast.63, ...), custom_call_target="tpu_custom_call" | custom-call | flops 15728640 | bytes 22020096 | tf_op jit(solution)/shard_map/adam_rows/pallas_call | solution.py:297
  204.1 9.9 %adam_rows.3 = (f32[1536,1024]{1,0:T(8,128)}, f32[1536,1024]{1,0:T(8,128)}, f32[1536,1024]{1,0:T(8,128)}) custom-call(f32[4]{0:T(128)S(1)} %pad_maximum_fusion.sc_ref, f32[1536,1024]{1,0:T(8,128)} %bitcast.58, f32[1536,1024]{1,0:T(8,128)} %bitcast.61, f32[1536,1024]{1,0:T(8,128)} %bitcast.64, ...), custom_call_target="tpu_custom_call", output_to_operand_aliasing={{0}: (6, {}), {1}: (7, {}), {2}: (8, {})} | custom-call | flops 15728640 | bytes 22020096 | tf_op jit(solution)/shard_map/adam_rows/pallas_call | solution.py:297
  214.1 2.4 %outer_step.1 = (f32[1536,1024]{1,0:T(8,128)}, f32[384,1024]{1,0:T(8,128)}, f32[384,1024]{1,0:T(8,128)}) custom-call(s32[2]{0:T(128)S(1)} %pad_add_fusion.place_ref.refs_0_, f32[1536,1024]{1,0:T(8,128)} %get-tuple-element.127.refs_0_, f32[384,1024]{1,0:T(8,128)} %duplicate.2.refs_1_, ...), custom_call_target="tpu_custom_call", output_to_operand_aliasing={{0}: (1, {}), {1}: (2, {}), {2}: (3, {})} | custom-call | flops 1966080 | bytes 3932160 | tf_op jit(solution)/shard_map/outer_step/pallas_call | solution.py:404
  (139 shorter events, 34.1 us)
Async XLA Ops:
  1.7 13.9 %collective-permute-start.1 = (bf16[128,1536]{1,0:T(8,128)(2,1)S(1)}, bf16[128,1536]{1,0:T(8,128)(2,1)S(1)}, u32[]{:S(2)}, u32[]{:S(2)}) collective-permute-start(bf16[128,1536]{1,0:T(8,128)(2,1)S(1)} %pack.21), channel_id=1, source_target_pairs={{0,6},{1,7},{2,4},{3,5},{4,2},{5,3},{6,0},{7,1},{8,14},{9,15},{10,... | collective-permute-start | bytes 1179656 | tf_op jit(solution)/shard_map/ppermute | solution.py:422
  6.6 17.9 %collective-permute-start = (bf16[128,1536]{1,0:T(8,128)(2,1)S(1)}, bf16[128,1536]{1,0:T(8,128)(2,1)S(1)}, u32[]{:S(2)}, u32[]{:S(2)}) collective-permute-start(bf16[128,1536]{1,0:T(8,128)(2,1)S(1)} %pack.19), channel_id=1, source_target_pairs={{0,2},{1,3},{2,0},{3,1},{4,6},{5,7},{6,4},{7,5},{8,10},{9,11},{10,... | collective-permute-start | bytes 1179656 | tf_op jit(solution)/shard_map/ppermute | solution.py:422
  8.3 22.6 %collective-permute-start.4 = (bf16[128,1536]{1,0:T(8,128)(2,1)S(1)}, bf16[128,1536]{1,0:T(8,128)(2,1)S(1)}, u32[]{:S(2)}, u32[]{:S(2)}) collective-permute-start(bf16[128,1536]{1,0:T(8,128)(2,1)S(1)} %pack.24), channel_id=1, source_target_pairs={{0,7},{1,6},{2,5},{3,4},{4,3},{5,2},{6,1},{7,0},{8,15},{9,14},{10,... | collective-permute-start | bytes 1179656 | tf_op jit(solution)/shard_map/ppermute | solution.py:422
  15.6 17.9 %collective-permute-start.2 = (bf16[128,1536]{1,0:T(8,128)(2,1)S(1)}, bf16[128,1536]{1,0:T(8,128)(2,1)S(1)}, u32[]{:S(2)}, u32[]{:S(2)}) collective-permute-start(bf16[128,1536]{1,0:T(8,128)(2,1)S(1)} %pack.20), channel_id=1, source_target_pairs={{0,4},{1,5},{2,6},{3,7},{4,0},{5,1},{6,2},{7,3},{8,12},{9,13},{10,... | collective-permute-start | bytes 1179656 | tf_op jit(solution)/shard_map/ppermute | solution.py:422
  30.9 14.4 %collective-permute-start.5 = (bf16[128,1536]{1,0:T(8,128)(2,1)}, bf16[128,1536]{1,0:T(8,128)(2,1)S(1)}, u32[]{:S(2)}, u32[]{:S(2)}) collective-permute-start(bf16[128,1536]{1,0:T(8,128)(2,1)} %pack.23), channel_id=1, source_target_pairs={{0,3},{1,2},{2,1},{3,0},{4,7},{5,6},{6,5},{7,4},{8,11},{9,10},{10,... | collective-permute-start | bytes 1179656 | tf_op jit(solution)/shard_map/ppermute | solution.py:422
  32.8 13.9 %collective-permute-start.6 = (bf16[128,1536]{1,0:T(8,128)(2,1)}, bf16[128,1536]{1,0:T(8,128)(2,1)S(1)}, u32[]{:S(2)}, u32[]{:S(2)}) collective-permute-start(bf16[128,1536]{1,0:T(8,128)(2,1)} %pack.25), channel_id=1, source_target_pairs={{0,5},{1,4},{2,7},{3,6},{4,1},{5,0},{6,3},{7,2},{8,13},{9,12},{10,... | collective-permute-start | bytes 1179656 | tf_op jit(solution)/shard_map/ppermute | solution.py:422
  33.5 13.2 %collective-permute-start.3 = (bf16[128,1536]{1,0:T(8,128)(2,1)}, bf16[128,1536]{1,0:T(8,128)(2,1)S(1)}, u32[]{:S(2)}, u32[]{:S(2)}) collective-permute-start(bf16[128,1536]{1,0:T(8,128)(2,1)} %pack.22), channel_id=1, source_target_pairs={{0,1},{1,0},{2,3},{3,2},{4,5},{5,4},{6,7},{7,6},{8,9},{9,8},{10,11... | collective-permute-start | bytes 1179656 | tf_op jit(solution)/shard_map/ppermute | solution.py:422
  45.3 12.9 %collective-permute-start.8 = (bf16[128,1536]{1,0:T(8,128)(2,1)S(1)}, bf16[128,1536]{1,0:T(8,128)(2,1)S(1)}, u32[]{:S(2)}, u32[]{:S(2)}) collective-permute-start(bf16[128,1536]{1,0:T(8,128)(2,1)S(1)} %copy-done.13), channel_id=1, source_target_pairs={{0,6},{1,7},{2,4},{3,5},{4,2},{5,3},{6,0},{7,1},{8,14},{9,15},{10,... | collective-permute-start | bytes 1179656 | tf_op jit(solution)/shard_map/ppermute | solution.py:422
  47.7 25.3 %collective-permute-start.7 = (bf16[4,128,512]{2,1,0:T(8,128)(2,1)S(1)}, bf16[4,128,512]{2,1,0:T(8,128)(2,1)S(1)}, u32[]{:S(2)}, u32[]{:S(2)}) collective-permute-start(bf16[4,128,512]{2,1,0:T(8,128)(2,1)S(1)} %partial_keys.2), channel_id=1, source_target_pairs={{0,1},{1,0},{2,3},{3,2},{4,5},{5,4},{6,7},{7,6},{8,9},{9,8},{10,11... | collective-permute-start | bytes 1572872 | tf_op jit(solution)/shard_map/ppermute | solution.py:422
  48.0 10.6 %collective-permute-start.12 = (f32[384,128]{1,0:T(8,128)S(1)}, f32[384,128]{1,0:T(8,128)S(1)}, u32[]{:S(2)}, u32[]{:S(2)}) collective-permute-start(f32[384,128]{1,0:T(8,128)S(1)} %get-tuple-element.142), channel_id=1, source_target_pairs={{0,8},{8,0},{16,24},{24,16},{1,9},{9,1},{17,25},{25,17},{2,10},{10... | collective-permute-start | bytes 589832 | tf_op jit(solution)/shard_map/ppermute | solution.py:422
  51.7 22.3 %collective-permute-start.18 = (bf16[128,1536]{1,0:T(8,128)(2,1)S(1)}, bf16[128,1536]{1,0:T(8,128)(2,1)S(1)}, u32[]{:S(2)}, u32[]{:S(2)}) collective-permute-start(bf16[128,1536]{1,0:T(8,128)(2,1)S(1)} %pack.28), channel_id=1, source_target_pairs={{0,7},{1,6},{2,5},{3,4},{4,3},{5,2},{6,1},{7,0},{8,15},{9,14},{10,... | collective-permute-start | bytes 1179656 | tf_op jit(solution)/shard_map/ppermute | solution.py:422
  53.0 21.0 %collective-permute-start.20 = (bf16[128,1536]{1,0:T(8,128)(2,1)S(1)}, bf16[128,1536]{1,0:T(8,128)(2,1)S(1)}, u32[]{:S(2)}, u32[]{:S(2)}) collective-permute-start(bf16[128,1536]{1,0:T(8,128)(2,1)S(1)} %pack.29), channel_id=1, source_target_pairs={{0,2},{1,3},{2,0},{3,1},{4,6},{5,7},{6,4},{7,5},{8,10},{9,11},{10,... | collective-permute-start | bytes 1179656 | tf_op jit(solution)/shard_map/ppermute | solution.py:422
  58.2 17.7 %collective-permute-start.9 = (bf16[128,1536]{1,0:T(8,128)(2,1)S(1)}, bf16[128,1536]{1,0:T(8,128)(2,1)S(1)}, u32[]{:S(2)}, u32[]{:S(2)}) collective-permute-start(bf16[128,1536]{1,0:T(8,128)(2,1)S(1)} %pack.26), channel_id=1, source_target_pairs={{0,4},{1,5},{2,6},{3,7},{4,0},{5,1},{6,2},{7,3},{8,12},{9,13},{10,... | collective-permute-start | bytes 1179656 | tf_op jit(solution)/shard_map/ppermute | solution.py:422
  58.7 10.8 %collective-permute-start.13 = (f32[384,128]{1,0:T(8,128)S(1)}, f32[384,128]{1,0:T(8,128)S(1)}, u32[]{:S(2)}, u32[]{:S(2)}) collective-permute-start(f32[384,128]{1,0:T(8,128)S(1)} %get-tuple-element.87), channel_id=1, source_target_pairs={{0,16},{8,24},{16,0},{24,8},{1,17},{9,25},{17,1},{25,9},{2,18},{10... | collective-permute-start | bytes 589832 | tf_op jit(solution)/shard_map/ppermute | solution.py:422
  69.5 15.4 %collective-permute-start.14 = (f32[384,128]{1,0:T(8,128)S(1)}, f32[384,128]{1,0:T(8,128)S(1)}, u32[]{:S(2)}, u32[]{:S(2)}) collective-permute-start(f32[384,128]{1,0:T(8,128)S(1)} %get-tuple-element.88), channel_id=1, source_target_pairs={{0,24},{8,16},{16,8},{24,0},{1,25},{9,17},{17,9},{25,1},{2,26},{10... | collective-permute-start | bytes 589832 | tf_op jit(solution)/shard_map/ppermute | solution.py:422
  74.0 8.3 %collective-permute-start.21 = (bf16[128,512]{1,0:T(8,128)(2,1)S(1)}, bf16[128,512]{1,0:T(8,128)(2,1)S(1)}, u32[]{:S(2)}, u32[]{:S(2)}) collective-permute-start(bf16[128,512]{1,0:T(8,128)(2,1)S(1)} %get-tuple-element.98), channel_id=1, source_target_pairs={{0,4},{1,5},{2,6},{3,7},{4,0},{5,1},{6,2},{7,3},{8,12},{9,13},{10,... | collective-permute-start | bytes 393224 | tf_op jit(solution)/shard_map/ppermute | solution.py:422
  75.2 7.1 %collective-permute-start.19 = (bf16[128,512]{1,0:T(8,128)(2,1)S(1)}, bf16[128,512]{1,0:T(8,128)(2,1)S(1)}, u32[]{:S(2)}, u32[]{:S(2)}) collective-permute-start(bf16[128,512]{1,0:T(8,128)(2,1)S(1)} %get-tuple-element.95), channel_id=1, source_target_pairs={{0,2},{1,3},{2,0},{3,1},{4,6},{5,7},{6,4},{7,5},{8,10},{9,11},{10,... | collective-permute-start | bytes 393224 | tf_op jit(solution)/shard_map/ppermute | solution.py:422
  76.0 7.2 %collective-permute-start.10 = (bf16[128,512]{1,0:T(8,128)(2,1)S(1)}, bf16[128,512]{1,0:T(8,128)(2,1)S(1)}, u32[]{:S(2)}, u32[]{:S(2)}) collective-permute-start(bf16[128,512]{1,0:T(8,128)(2,1)S(1)} %get-tuple-element.81), channel_id=1, source_target_pairs={{0,6},{1,7},{2,4},{3,5},{4,2},{5,3},{6,0},{7,1},{8,14},{9,15},{10,... | collective-permute-start | bytes 393224 | tf_op jit(solution)/shard_map/ppermute | solution.py:422
  82.3 39.0 %copy-start.5 = (f32[1,384,128]{2,1,0:T(8,128)}, f32[1,384,128]{2,1,0:T(8,128)S(1)}, u32[]{:S(2)}) copy-start(f32[1,384,128]{2,1,0:T(8,128)S(1)} %get-tuple-element.84) | copy-start | bytes 589828
  82.3 39.0 %copy-start.7 = (f32[1,384,128]{2,1,0:T(8,128)}, f32[1,384,128]{2,1,0:T(8,128)S(1)}, u32[]{:S(2)}) copy-start(f32[1,384,128]{2,1,0:T(8,128)S(1)} %get-tuple-element.85) | copy-start | bytes 589828
  83.2 3.7 %collective-permute-start.11 = (bf16[128,1536]{1,0:T(8,128)(2,1)S(1)}, bf16[128,1536]{1,0:T(8,128)(2,1)S(1)}, u32[]{:S(2)}, u32[]{:S(2)}) collective-permute-start(bf16[128,1536]{1,0:T(8,128)(2,1)S(1)} %pack.17), channel_id=1, source_target_pairs={{0,1},{1,0},{2,3},{3,2},{4,5},{5,4},{6,7},{7,6},{8,9},{9,8},{10,11... | collective-permute-start | bytes 1179656 | tf_op jit(solution)/shard_map/ppermute | solution.py:422
  83.2 11.1 %collective-permute-start.23 = (bf16[128,1536]{1,0:T(8,128)(2,1)S(1)}, bf16[128,1536]{1,0:T(8,128)(2,1)S(1)}, u32[]{:S(2)}, u32[]{:S(2)}) collective-permute-start(bf16[128,1536]{1,0:T(8,128)(2,1)S(1)} %pack.30), channel_id=1, source_target_pairs={{0,3},{1,2},{2,1},{3,0},{4,7},{5,6},{6,5},{7,4},{8,11},{9,10},{10,... | collective-permute-start | bytes 1179656 | tf_op jit(solution)/shard_map/ppermute | solution.py:422
  84.9 14.0 %collective-permute-start.26 = (bf16[128,1536]{1,0:T(8,128)(2,1)S(1)}, bf16[128,1536]{1,0:T(8,128)(2,1)S(1)}, u32[]{:S(2)}, u32[]{:S(2)}) collective-permute-start(bf16[128,1536]{1,0:T(8,128)(2,1)S(1)} %pack.31), channel_id=1, source_target_pairs={{0,5},{1,4},{2,7},{3,6},{4,1},{5,0},{6,3},{7,2},{8,13},{9,12},{10,... | collective-permute-start | bytes 1179656 | tf_op jit(solution)/shard_map/ppermute | solution.py:422
  85.6 35.7 %copy-start.9 = (f32[384,128]{1,0:T(8,128)}, f32[384,128]{1,0:T(8,128)S(1)}, u32[]{:S(2)}) copy-start(f32[384,128]{1,0:T(8,128)S(1)} %get-tuple-element.91.refs_3_) | copy-start | bytes 589828
  85.7 13.6 %collective-permute-start.15 = (f32[384,128]{1,0:T(8,128)S(1)}, f32[384,128]{1,0:T(8,128)S(1)}, u32[]{:S(2)}, u32[]{:S(2)}) collective-permute-start(f32[384,128]{1,0:T(8,128)S(1)} %get-tuple-element.91.refs_3_), channel_id=1, source_target_pairs={{0,8},{8,0},{16,24},{24,16},{1,9},{9,1},{17,25},{25,17},{2,10},{10... | collective-permute-start | bytes 589832 | tf_op jit(solution)/shard_map/ppermute | solution.py:422
  87.0 14.3 %collective-permute-start.29 = (bf16[128,512]{1,0:T(8,128)(2,1)S(1)}, bf16[128,512]{1,0:T(8,128)(2,1)S(1)}, u32[]{:S(2)}, u32[]{:S(2)}) collective-permute-start(bf16[128,512]{1,0:T(8,128)(2,1)S(1)} %key_backward.2.refs_2_), channel_id=1, source_target_pairs={{0,6},{1,7},{2,4},{3,5},{4,2},{5,3},{6,0},{7,1},{8,14},{9,15},{10,... | collective-permute-start | bytes 393224 | tf_op jit(solution)/shard_map/ppermute | solution.py:422
  94.3 7.4 %collective-permute-start.24 = (bf16[128,512]{1,0:T(8,128)(2,1)S(1)}, bf16[128,512]{1,0:T(8,128)(2,1)S(1)}, u32[]{:S(2)}, u32[]{:S(2)}) collective-permute-start(bf16[128,512]{1,0:T(8,128)(2,1)S(1)} %key_backward.2.refs_2_), channel_id=1, source_target_pairs={{0,2},{1,3},{2,0},{3,1},{4,6},{5,7},{6,4},{7,5},{8,10},{9,11},{10,... | collective-permute-start | bytes 393224 | tf_op jit(solution)/shard_map/ppermute | solution.py:422
  98.9 5.7 %collective-permute-start.27 = (bf16[128,512]{1,0:T(8,128)(2,1)S(1)}, bf16[128,512]{1,0:T(8,128)(2,1)S(1)}, u32[]{:S(2)}, u32[]{:S(2)}) collective-permute-start(bf16[128,512]{1,0:T(8,128)(2,1)S(1)} %key_backward.2.refs_2_), channel_id=1, source_target_pairs={{0,4},{1,5},{2,6},{3,7},{4,0},{5,1},{6,2},{7,3},{8,12},{9,13},{10,... | collective-permute-start | bytes 393224 | tf_op jit(solution)/shard_map/ppermute | solution.py:422
  99.3 22.1 %copy-start.14 = (f32[384,128]{1,0:T(8,128)}, f32[384,128]{1,0:T(8,128)S(1)}, u32[]{:S(2)}) copy-start(f32[384,128]{1,0:T(8,128)S(1)} %collective-permute-done.15.refs_4_) | copy-start | bytes 589828
  99.3 12.0 %collective-permute-start.16 = (f32[384,128]{1,0:T(8,128)S(1)}, f32[384,128]{1,0:T(8,128)S(1)}, u32[]{:S(2)}, u32[]{:S(2)}) collective-permute-start(f32[384,128]{1,0:T(8,128)S(1)} %get-tuple-element.91.refs_3_), channel_id=1, source_target_pairs={{0,16},{8,24},{16,0},{24,8},{1,17},{9,25},{17,1},{25,9},{2,18},{10... | collective-permute-start | bytes 589832 | tf_op jit(solution)/shard_map/ppermute | solution.py:422
  101.2 21.7 %collective-permute-start.22 = (bf16[128,512]{1,0:T(8,128)(2,1)S(1)}, bf16[128,512]{1,0:T(8,128)(2,1)S(1)}, u32[]{:S(2)}, u32[]{:S(2)}) collective-permute-start(bf16[128,512]{1,0:T(8,128)(2,1)S(1)} %key_backward.2.refs_2_), channel_id=1, source_target_pairs={{0,1},{1,0},{2,3},{3,2},{4,5},{5,4},{6,7},{7,6},{8,9},{9,8},{10,11... | collective-permute-start | bytes 393224 | tf_op jit(solution)/shard_map/ppermute | solution.py:422
  101.2 21.7 %collective-permute-start.30 = (bf16[128,512]{1,0:T(8,128)(2,1)S(1)}, bf16[128,512]{1,0:T(8,128)(2,1)S(1)}, u32[]{:S(2)}, u32[]{:S(2)}) collective-permute-start(bf16[128,512]{1,0:T(8,128)(2,1)S(1)} %collective-permute-done.29.refs_8_), channel_id=1, source_target_pairs={{0,1},{1,0},{2,3},{3,2},{4,5},{5,4},{6,7},{7,6},{8,9},{9,8},{10,11... | collective-permute-start | bytes 393224 | tf_op jit(solution)/shard_map/ppermute | solution.py:422
  101.8 21.2 %collective-permute-start.25 = (bf16[128,512]{1,0:T(8,128)(2,1)S(1)}, bf16[128,512]{1,0:T(8,128)(2,1)S(1)}, u32[]{:S(2)}, u32[]{:S(2)}) collective-permute-start(bf16[128,512]{1,0:T(8,128)(2,1)S(1)} %collective-permute-done.24.refs_4_), channel_id=1, source_target_pairs={{0,1},{1,0},{2,3},{3,2},{4,5},{5,4},{6,7},{7,6},{8,9},{9,8},{10,11... | collective-permute-start | bytes 393224 | tf_op jit(solution)/shard_map/ppermute | solution.py:422
  104.6 18.3 %collective-permute-start.28 = (bf16[128,512]{1,0:T(8,128)(2,1)S(1)}, bf16[128,512]{1,0:T(8,128)(2,1)S(1)}, u32[]{:S(2)}, u32[]{:S(2)}) collective-permute-start(bf16[128,512]{1,0:T(8,128)(2,1)S(1)} %collective-permute-done.27.refs_6_), channel_id=1, source_target_pairs={{0,1},{1,0},{2,3},{3,2},{4,5},{5,4},{6,7},{7,6},{8,9},{9,8},{10,11... | collective-permute-start | bytes 393224 | tf_op jit(solution)/shard_map/ppermute | solution.py:422
  111.2 15.0 %collective-permute-start.17 = (f32[384,128]{1,0:T(8,128)S(1)}, f32[384,128]{1,0:T(8,128)S(1)}, u32[]{:S(2)}, u32[]{:S(2)}) collective-permute-start(f32[384,128]{1,0:T(8,128)S(1)} %get-tuple-element.91.refs_3_), channel_id=1, source_target_pairs={{0,24},{8,16},{16,8},{24,0},{1,25},{9,17},{17,9},{25,1},{2,26},{10... | collective-permute-start | bytes 589832 | tf_op jit(solution)/shard_map/ppermute | solution.py:422
  127.3 4.7 %collective-permute-start.31 = (bf16[4,128,512]{2,1,0:T(8,128)(2,1)S(1)}, bf16[4,128,512]{2,1,0:T(8,128)(2,1)S(1)}, u32[]{:S(2)}, u32[]{:S(2)}) collective-permute-start(bf16[4,128,512]{2,1,0:T(8,128)(2,1)S(1)} %partial_keys.3), channel_id=1, source_target_pairs={{0,1},{1,0},{2,3},{3,2},{4,5},{5,4},{6,7},{7,6},{8,9},{9,8},{10,11... | collective-permute-start | bytes 1572872 | tf_op jit(solution)/shard_map/ppermute | solution.py:422
  127.4 10.1 %collective-permute-start.36 = (bf16[256,512]{1,0:T(8,128)(2,1)S(1)}, bf16[256,512]{1,0:T(8,128)(2,1)S(1)}, u32[]{:S(2)}, u32[]{:S(2)}) collective-permute-start(bf16[256,512]{1,0:T(8,128)(2,1)S(1)} %slice.20.refs_2_.refs_11_), channel_id=1, source_target_pairs={{0,6},{1,7},{2,4},{3,5},{4,2},{5,3},{6,0},{7,1},{8,14},{9,15},{10,... | collective-permute-start | bytes 786440 | tf_op jit(solution)/shard_map/ppermute | solution.py:422
  129.0 14.0 %collective-permute-start.34 = (bf16[256,512]{1,0:T(8,128)(2,1)S(1)}, bf16[256,512]{1,0:T(8,128)(2,1)S(1)}, u32[]{:S(2)}, u32[]{:S(2)}) collective-permute-start(bf16[256,512]{1,0:T(8,128)(2,1)S(1)} %slice.20.refs_2_.refs_11_), channel_id=1, source_target_pairs={{0,4},{1,5},{2,6},{3,7},{4,0},{5,1},{6,2},{7,3},{8,12},{9,13},{10,... | collective-permute-start | bytes 786440 | tf_op jit(solution)/shard_map/ppermute | solution.py:422
  130.3 14.4 %collective-permute-start.32 = (bf16[256,512]{1,0:T(8,128)(2,1)S(1)}, bf16[256,512]{1,0:T(8,128)(2,1)S(1)}, u32[]{:S(2)}, u32[]{:S(2)}) collective-permute-start(bf16[256,512]{1,0:T(8,128)(2,1)S(1)} %slice.20.refs_2_.refs_11_), channel_id=1, source_target_pairs={{0,2},{1,3},{2,0},{3,1},{4,6},{5,7},{6,4},{7,5},{8,10},{9,11},{10,... | collective-permute-start | bytes 786440 | tf_op jit(solution)/shard_map/ppermute | solution.py:422
  137.5 8.0 %collective-permute-start.37 = (bf16[128,512]{1,0:T(8,128)(2,1)S(1)}, bf16[128,512]{1,0:T(8,128)(2,1)S(1)}, u32[]{:S(2)}, u32[]{:S(2)}) collective-permute-start(bf16[128,512]{1,0:T(8,128)(2,1)S(1)} %get-tuple-element.115), channel_id=1, source_target_pairs={{0,6},{1,7},{2,4},{3,5},{4,2},{5,3},{6,0},{7,1},{8,14},{9,15},{10,... | collective-permute-start | bytes 393224 | tf_op jit(solution)/shard_map/ppermute | solution.py:422
  139.1 11.5 %collective-permute-start.45 = (bf16[256,512]{1,0:T(8,128)(2,1)S(1)}, bf16[256,512]{1,0:T(8,128)(2,1)S(1)}, u32[]{:S(2)}, u32[]{:S(2)}) collective-permute-start(bf16[256,512]{1,0:T(8,128)(2,1)S(1)} %slice.20.refs_2_.refs_11_), channel_id=1, source_target_pairs={{0,1},{1,0},{2,3},{3,2},{4,5},{5,4},{6,7},{7,6},{8,9},{9,8},{10,11... | collective-permute-start | bytes 786440 | tf_op jit(solution)/shard_map/ppermute | solution.py:422
  139.1 12.8 %collective-permute-start.48 = (bf16[256,512]{1,0:T(8,128)(2,1)S(1)}, bf16[256,512]{1,0:T(8,128)(2,1)S(1)}, u32[]{:S(2)}, u32[]{:S(2)}) collective-permute-start(bf16[256,512]{1,0:T(8,128)(2,1)S(1)} %collective-permute-done.36.refs_8_.refs_17_), channel_id=1, source_target_pairs={{0,1},{1,0},{2,3},{3,2},{4,5},{5,4},{6,7},{7,6},{8,9},{9,8},{10,11... | collective-permute-start | bytes 786440 | tf_op jit(solution)/shard_map/ppermute | solution.py:422
  143.0 5.4 %collective-permute-start.35 = (bf16[128,512]{1,0:T(8,128)(2,1)S(1)}, bf16[128,512]{1,0:T(8,128)(2,1)S(1)}, u32[]{:S(2)}, u32[]{:S(2)}) collective-permute-start(bf16[128,512]{1,0:T(8,128)(2,1)S(1)} %get-tuple-element.112), channel_id=1, source_target_pairs={{0,4},{1,5},{2,6},{3,7},{4,0},{5,1},{6,2},{7,3},{8,12},{9,13},{10,... | collective-permute-start | bytes 393224 | tf_op jit(solution)/shard_map/ppermute | solution.py:422
  144.7 5.1 %collective-permute-start.33 = (bf16[128,512]{1,0:T(8,128)(2,1)S(1)}, bf16[128,512]{1,0:T(8,128)(2,1)S(1)}, u32[]{:S(2)}, u32[]{:S(2)}) collective-permute-start(bf16[128,512]{1,0:T(8,128)(2,1)S(1)} %get-tuple-element.109), channel_id=1, source_target_pairs={{0,2},{1,3},{2,0},{3,1},{4,6},{5,7},{6,4},{7,5},{8,10},{9,11},{10,... | collective-permute-start | bytes 393224 | tf_op jit(solution)/shard_map/ppermute | solution.py:422
  145.5 9.7 %collective-permute-start.46 = (bf16[256,512]{1,0:T(8,128)(2,1)S(1)}, bf16[256,512]{1,0:T(8,128)(2,1)S(1)}, u32[]{:S(2)}, u32[]{:S(2)}) collective-permute-start(bf16[256,512]{1,0:T(8,128)(2,1)S(1)} %collective-permute-done.32.refs_4_.refs_13_), channel_id=1, source_target_pairs={{0,1},{1,0},{2,3},{3,2},{4,5},{5,4},{6,7},{7,6},{8,9},{9,8},{10,11... | collective-permute-start | bytes 786440 | tf_op jit(solution)/shard_map/ppermute | solution.py:422
  148.4 10.2 %collective-permute-start.47 = (bf16[256,512]{1,0:T(8,128)(2,1)S(1)}, bf16[256,512]{1,0:T(8,128)(2,1)S(1)}, u32[]{:S(2)}, u32[]{:S(2)}) collective-permute-start(bf16[256,512]{1,0:T(8,128)(2,1)S(1)} %collective-permute-done.34.refs_6_.refs_15_), channel_id=1, source_target_pairs={{0,1},{1,0},{2,3},{3,2},{4,5},{5,4},{6,7},{7,6},{8,9},{9,8},{10,11... | collective-permute-start | bytes 786440 | tf_op jit(solution)/shard_map/ppermute | solution.py:422
  150.1 6.0 %collective-permute-start.39 = (bf16[128,512]{1,0:T(8,128)(2,1)S(1)}, bf16[128,512]{1,0:T(8,128)(2,1)S(1)}, u32[]{:S(2)}, u32[]{:S(2)}) collective-permute-start(bf16[128,512]{1,0:T(8,128)(2,1)S(1)} %key_backward.3.refs_2_), channel_id=1, source_target_pairs={{0,2},{1,3},{2,0},{3,1},{4,6},{5,7},{6,4},{7,5},{8,10},{9,11},{10,... | collective-permute-start | bytes 393224 | tf_op jit(solution)/shard_map/ppermute | solution.py:422
  150.6 6.6 %collective-permute-start.41 = (bf16[128,512]{1,0:T(8,128)(2,1)S(1)}, bf16[128,512]{1,0:T(8,128)(2,1)S(1)}, u32[]{:S(2)}, u32[]{:S(2)}) collective-permute-start(bf16[128,512]{1,0:T(8,128)(2,1)S(1)} %key_backward.3.refs_2_), channel_id=1, source_target_pairs={{0,4},{1,5},{2,6},{3,7},{4,0},{5,1},{6,2},{7,3},{8,12},{9,13},{10,... | collective-permute-start | bytes 393224 | tf_op jit(solution)/shard_map/ppermute | solution.py:422
  151.9 6.7 %collective-permute-start.43 = (bf16[128,512]{1,0:T(8,128)(2,1)S(1)}, bf16[128,512]{1,0:T(8,128)(2,1)S(1)}, u32[]{:S(2)}, u32[]{:S(2)}) collective-permute-start(bf16[128,512]{1,0:T(8,128)(2,1)S(1)} %key_backward.3.refs_2_), channel_id=1, source_target_pairs={{0,6},{1,7},{2,4},{3,5},{4,2},{5,3},{6,0},{7,1},{8,14},{9,15},{10,... | collective-permute-start | bytes 393224 | tf_op jit(solution)/shard_map/ppermute | solution.py:422
  155.2 9.3 %collective-permute-start.38 = (bf16[128,512]{1,0:T(8,128)(2,1)S(1)}, bf16[128,512]{1,0:T(8,128)(2,1)S(1)}, u32[]{:S(2)}, u32[]{:S(2)}) collective-permute-start(bf16[128,512]{1,0:T(8,128)(2,1)S(1)} %key_backward.3.refs_2_), channel_id=1, source_target_pairs={{0,1},{1,0},{2,3},{3,2},{4,5},{5,4},{6,7},{7,6},{8,9},{9,8},{10,11... | collective-permute-start | bytes 393224 | tf_op jit(solution)/shard_map/ppermute | solution.py:422
  156.1 8.5 %collective-permute-start.40 = (bf16[128,512]{1,0:T(8,128)(2,1)S(1)}, bf16[128,512]{1,0:T(8,128)(2,1)S(1)}, u32[]{:S(2)}, u32[]{:S(2)}) collective-permute-start(bf16[128,512]{1,0:T(8,128)(2,1)S(1)} %collective-permute-done.39.refs_4_), channel_id=1, source_target_pairs={{0,1},{1,0},{2,3},{3,2},{4,5},{5,4},{6,7},{7,6},{8,9},{9,8},{10,11... | collective-permute-start | bytes 393224 | tf_op jit(solution)/shard_map/ppermute | solution.py:422
  157.2 7.4 %collective-permute-start.42 = (bf16[128,512]{1,0:T(8,128)(2,1)S(1)}, bf16[128,512]{1,0:T(8,128)(2,1)S(1)}, u32[]{:S(2)}, u32[]{:S(2)}) collective-permute-start(bf16[128,512]{1,0:T(8,128)(2,1)S(1)} %collective-permute-done.41.refs_6_), channel_id=1, source_target_pairs={{0,1},{1,0},{2,3},{3,2},{4,5},{5,4},{6,7},{7,6},{8,9},{9,8},{10,11... | collective-permute-start | bytes 393224 | tf_op jit(solution)/shard_map/ppermute | solution.py:422
  158.6 6.0 %collective-permute-start.44 = (bf16[128,512]{1,0:T(8,128)(2,1)S(1)}, bf16[128,512]{1,0:T(8,128)(2,1)S(1)}, u32[]{:S(2)}, u32[]{:S(2)}) collective-permute-start(bf16[128,512]{1,0:T(8,128)(2,1)S(1)} %collective-permute-done.43.refs_8_), channel_id=1, source_target_pairs={{0,1},{1,0},{2,3},{3,2},{4,5},{5,4},{6,7},{7,6},{8,9},{9,8},{10,11... | collective-permute-start | bytes 393224 | tf_op jit(solution)/shard_map/ppermute | solution.py:422
  164.6 14.4 %copy-start.2 = (f32[4,384,128]{2,1,0:T(8,128)S(1)}, f32[4,384,128]{2,1,0:T(8,128)}, u32[]{:S(2)}) copy-start(f32[4,384,128]{2,1,0:T(8,128)} %copy-done.1) | copy-start | bytes 2359300
  169.5 1.3 collective-permute-start.49
  170.8 4.5 %collective-permute-start.52 = (f32[8,128]{1,0:T(8,128)S(1)}, f32[8,128]{1,0:T(8,128)S(1)}, u32[]{:S(2)}, u32[]{:S(2)}) collective-permute-start(f32[8,128]{1,0:T(8,128)S(1)} %add.44), channel_id=1, source_target_pairs={{0,6},{1,7},{2,4},{3,5},{4,2},{5,3},{6,0},{7,1},{8,14},{9,15},{10,... | collective-permute-start | bytes 12296 | tf_op jit(solution)/shard_map/ppermute | solution.py:422
  172.9 3.6 %collective-permute-start.51 = (f32[8,128]{1,0:T(8,128)S(1)}, f32[8,128]{1,0:T(8,128)S(1)}, u32[]{:S(2)}, u32[]{:S(2)}) collective-permute-start(f32[8,128]{1,0:T(8,128)S(1)} %add.44), channel_id=1, source_target_pairs={{0,4},{1,5},{2,6},{3,7},{4,0},{5,1},{6,2},{7,3},{8,12},{9,13},{10,... | collective-permute-start | bytes 12296 | tf_op jit(solution)/shard_map/ppermute | solution.py:422
  174.0 3.6 %collective-permute-start.50 = (f32[8,128]{1,0:T(8,128)S(1)}, f32[8,128]{1,0:T(8,128)S(1)}, u32[]{:S(2)}, u32[]{:S(2)}) collective-permute-start(f32[8,128]{1,0:T(8,128)S(1)} %add.44), channel_id=1, source_target_pairs={{0,2},{1,3},{2,0},{3,1},{4,6},{5,7},{6,4},{7,5},{8,10},{9,11},{10,... | collective-permute-start | bytes 12296 | tf_op jit(solution)/shard_map/ppermute | solution.py:422
  180.2 5.9 %collective-permute-start.53 = (bf16[384,128]{1,0:T(8,128)(2,1)S(1)}, bf16[384,128]{1,0:T(8,128)(2,1)S(1)}, u32[]{:S(2)}, u32[]{:S(2)}) collective-permute-start(bf16[384,128]{1,0:T(8,128)(2,1)S(1)} %get-tuple-element.131), channel_id=1, source_target_pairs={{0,8},{8,0},{16,24},{24,16},{1,9},{9,1},{17,25},{25,17},{2,10},{10... | collective-permute-start | bytes 294920 | tf_op jit(solution)/shard_map/ppermute | solution.py:422
  180.3 9.4 %collective-permute-start.54 = (bf16[384,128]{1,0:T(8,128)(2,1)S(1)}, bf16[384,128]{1,0:T(8,128)(2,1)S(1)}, u32[]{:S(2)}, u32[]{:S(2)}) collective-permute-start(bf16[384,128]{1,0:T(8,128)(2,1)S(1)} %get-tuple-element.132), channel_id=1, source_target_pairs={{0,16},{8,24},{16,0},{24,8},{1,17},{9,25},{17,1},{25,9},{2,18},{10... | collective-permute-start | bytes 294920 | tf_op jit(solution)/shard_map/ppermute | solution.py:422
  181.5 8.2 %collective-permute-start.55 = (bf16[384,128]{1,0:T(8,128)(2,1)S(1)}, bf16[384,128]{1,0:T(8,128)(2,1)S(1)}, u32[]{:S(2)}, u32[]{:S(2)}) collective-permute-start(bf16[384,128]{1,0:T(8,128)(2,1)S(1)} %get-tuple-element.133), channel_id=1, source_target_pairs={{0,24},{8,16},{16,8},{24,0},{1,25},{9,17},{17,9},{25,1},{2,26},{10... | collective-permute-start | bytes 294920 | tf_op jit(solution)/shard_map/ppermute | solution.py:422
  189.7 24.3 %collective-permute-start.58 = (bf16[384,128]{1,0:T(8,128)(2,1)S(1)}, bf16[384,128]{1,0:T(8,128)(2,1)S(1)}, u32[]{:S(2)}, u32[]{:S(2)}) collective-permute-start(bf16[384,128]{1,0:T(8,128)(2,1)S(1)} %convert_element_type.24.refs_7_), channel_id=1, source_target_pairs={{0,24},{8,16},{16,8},{24,0},{1,25},{9,17},{17,9},{25,1},{2,26},{10... | collective-permute-start | bytes 294920 | tf_op jit(solution)/shard_map/ppermute | solution.py:422
  191.3 22.7 %collective-permute-start.57 = (bf16[384,128]{1,0:T(8,128)(2,1)S(1)}, bf16[384,128]{1,0:T(8,128)(2,1)S(1)}, u32[]{:S(2)}, u32[]{:S(2)}) collective-permute-start(bf16[384,128]{1,0:T(8,128)(2,1)S(1)} %convert_element_type.24.refs_7_), channel_id=1, source_target_pairs={{0,16},{8,24},{16,0},{24,8},{1,17},{9,25},{17,1},{25,9},{2,18},{10... | collective-permute-start | bytes 294920 | tf_op jit(solution)/shard_map/ppermute | solution.py:422
  193.9 20.1 %collective-permute-start.56 = (bf16[384,128]{1,0:T(8,128)(2,1)S(1)}, bf16[384,128]{1,0:T(8,128)(2,1)S(1)}, u32[]{:S(2)}, u32[]{:S(2)}) collective-permute-start(bf16[384,128]{1,0:T(8,128)(2,1)S(1)} %convert_element_type.24.refs_7_), channel_id=1, source_target_pairs={{0,8},{8,0},{16,24},{24,16},{1,9},{9,1},{17,25},{25,17},{2,10},{10... | collective-permute-start | bytes 294920 | tf_op jit(solution)/shard_map/ppermute | solution.py:422
  (15 other events, 113.9 us)

commit v5 on v4

--- a/solution.py
+++ b/solution.py
@@ -46,14 +46,15 @@
     out_ref[...] = src_ref[...]
 
 
-def pack(tokens, me, offset, half, count, rows):
+def pack(tokens, me, offset, rows):
+    count = tokens.shape[0]
     return pl.pallas_call(
         pack_kernel,
         out_shape=jax.ShapeDtypeStruct((count, rows), tokens.dtype),
         grid_spec=pltpu.PrefetchScalarGridSpec(
             num_scalar_prefetch=1,
             grid=(1,),
-            in_specs=[pl.BlockSpec((count, rows), lambda i, me: (half, me[0] ^ offset))],
+            in_specs=[pl.BlockSpec((count, rows), lambda i, me: (0, me[0] ^ offset))],
             out_specs=pl.BlockSpec((count, rows), lambda i, me: (0, 0)),
         ),
         compiler_params=params_of(4),
@@ -103,42 +104,24 @@
     )(*in_hbm(array))
 
 
-def partial_kernel(*refs):
-    *x_refs, w_ref, out_ref = refs
-    for m, ref in enumerate(x_refs):
-        out_ref[m] = jnp.dot(ref[...], w_ref[...], preferred_element_type=jnp.float32).astype(out_ref.dtype)
-
-
-def partial_keys(blocks, key_weights):
-    count, rows = blocks[0].shape
+def partial_kernel(x_ref, w_ref, *refs):
+    *add_refs, out_ref = refs
+    total = jnp.dot(x_ref[...], w_ref[...], preferred_element_type=jnp.float32)
+    for ref in add_refs:
+        total = total + ref[...].astype(jnp.float32)
+    out_ref[...] = total.astype(out_ref.dtype)
+
+
+def partial_keys(block, key_weights, *others):
+    count, rows = block.shape
     width = key_weights.shape[1]
     return pl.pallas_call(
         partial_kernel,
-        out_shape=jax.ShapeDtypeStruct((len(blocks), count, width), jnp.bfloat16),
-        compiler_params=params_of(12),
-        cost_estimate=cost(2 * len(blocks) * count * rows * width, 2 * len(blocks) * count * rows),
+        out_shape=jax.ShapeDtypeStruct((count, width), jnp.bfloat16),
+        compiler_params=params_of(8),
+        cost_estimate=cost(2 * count * rows * width, 2 * count * rows),
         name="partial_keys",
-    )(*blocks, key_weights)
-
-
-def summed_kernel(*refs):
-    half = (len(refs) - 2) // 2
-    x_refs, (w_ref, add_ref), out_refs = refs[:half], refs[half:half + 2], refs[half + 2:]
-    for m, ref in enumerate(x_refs):
-        total = jnp.dot(ref[...], w_ref[...], preferred_element_type=jnp.float32)
-        out_refs[m][...] = (total + add_ref[m].astype(jnp.float32)).astype(out_refs[m].dtype)
-
-
-def summed_keys(blocks, key_weights, others):
-    count, rows = blocks[0].shape
-    width = key_weights.shape[1]
-    return pl.pallas_call(
-        summed_kernel,
-        out_shape=[jax.ShapeDtypeStruct((count, width), jnp.bfloat16)] * len(blocks),
-        compiler_params=params_of(12),
-        cost_estimate=cost(2 * len(blocks) * count * rows * width, 2 * len(blocks) * count * rows),
-        name="summed_keys",
-    )(*blocks, key_weights, others)
+    )(block, key_weights, *others)
 
 
 def key_kernel(*refs):
@@ -154,9 +137,9 @@
         out_ref[:, cols] = back.astype(out_ref.dtype)
 
 
-def key_backward(parts, incoming, half):
+def key_backward(parts, incoming):
     block = pl.BlockSpec(parts[0].shape, lambda i: (0, 0))
-    cot = pl.BlockSpec(parts[0].shape, lambda i: (half, 0))
+    cot = pl.BlockSpec(parts[0].shape, lambda i: (0, 0))
     size = parts[0].size
     return pl.pallas_call(
         key_kernel,
@@ -220,11 +203,10 @@
     row_block = lambda cols: pl.BlockSpec((step, cols), lambda i, p: (i, 0))
     fixed = pl.BlockSpec((8, HEAD), lambda i, p: (0, 0))
     args, specs, scratch = [], [], []
-    for x, blocks, at in terms:
+    for x, blocks in terms:
         args += [x, *blocks]
-        depth = x.shape[1] // len(blocks)
         specs += [row_block(x.shape[1])]
-        specs += [pl.BlockSpec((depth, width), lambda i, p, at=at: (at, 0))] * len(blocks)
+        specs += [pl.BlockSpec(b.shape, lambda i, p: (0, 0)) for b in blocks]
         scratch.append(pltpu.VMEM((x.shape[1], width), jnp.bfloat16))
     if base is not None:
         args.append(base)
@@ -242,9 +224,9 @@
     else:
         shapes = [jax.ShapeDtypeStruct((rows, width), jnp.float32)]
         outs = [row_block(width)]
-    depth = sum(x.shape[1] for x, _, _ in terms)
-    return pl.pallas_call(
-        functools.partial(grad_kernel, [len(b) for _, b, _ in terms], base is not None, last),
+    depth = sum(x.shape[1] for x, _ in terms)
+    return pl.pallas_call(
+        functools.partial(grad_kernel, [len(b) for _, b in terms], base is not None, last),
         out_shape=shapes,
         grid_spec=pltpu.PrefetchScalarGridSpec(
             num_scalar_prefetch=1,
@@ -259,8 +241,13 @@
     )(place, *args)
 
 
-def adam(old, first, second, grad, scalars):
-    factor, rate, inv_one, inv_two = (scalars[i] for i in range(4))
+def clip_factor(square_refs):
+    square = jnp.sum(sum(ref[...] for ref in square_refs), keepdims=True)
+    return jnp.minimum(1.0, CLIP_NORM / (jnp.sqrt(square) + 1e-06))
+
+
+def adam(old, first, second, grad, factor, scalars):
+    rate, inv_one, inv_two = (scalars[i] for i in range(3))
     clipped = grad * factor
     first_new = BETA_ONE * first + (1.0 - BETA_ONE) * clipped
     second_new = BETA_TWO * second + (1.0 - BETA_TWO) * clipped * clipped
@@ -270,12 +257,15 @@
     return update, first_new, second_new
 
 
-def adam_kernel(extra, sc_ref, w_ref, m_ref, v_ref, gk_ref, gv_ref, *refs):
-    w_out, m_out, v_out, *done = refs[extra:]
+def adam_kernel(squares, extra, sc_ref, w_ref, m_ref, v_ref, gk_ref, gv_ref, *refs):
+    factor = clip_factor(refs[:squares])
+    w_out, m_out, v_out, *done = refs[squares + extra:]
     width = gk_ref.shape[1]
     for g_ref, cols in ((gk_ref, slice(0, width)), (gv_ref, slice(width, 2 * width))):
         old = w_ref[:, cols]
-        update, first_new, second_new = adam(old, m_ref[:, cols], v_ref[:, cols], g_ref[...], sc_ref)
+        update, first_new, second_new = adam(
+            old, m_ref[:, cols], v_ref[:, cols], g_ref[...], factor, sc_ref
+        )
         w_out[:, cols] = old - update
         m_out[:, cols] = first_new
         v_out[:, cols] = second_new
@@ -283,7 +273,7 @@
         ref[...] = jnp.zeros_like(ref)
 
 
-def adam_rows(scalars, state, first, last, into=()):
+def adam_rows(scalars, squares, state, first, last, into=()):
     rows, width = state[0].shape
     step = 256
     full = pl.BlockSpec((step, width), lambda i: (i + first, 0))
@@ -295,43 +285,46 @@
         outs.append(pl.BlockSpec((8, HEAD), lambda i: (0, 0)))
     count = (last - first) * step
     return pl.pallas_call(
-        functools.partial(adam_kernel, len(into)),
+        functools.partial(adam_kernel, len(squares), len(into)),
         out_shape=shapes,
         grid=(last - first,),
         in_specs=[pl.BlockSpec(memory_space=pltpu.SMEM), full, full, full, half, half]
+        + [pl.BlockSpec((8, HEAD), lambda i: (0, 0))] * len(squares)
         + [pl.BlockSpec(memory_space=pl.ANY)] * len(into),
         out_specs=outs,
-        input_output_aliases={6 + i: i for i in range(len(into))},
+        input_output_aliases={6 + len(squares) + i: i for i in range(len(into))},
         compiler_params=params_of(24),
         cost_estimate=cost(20 * count * width, 28 * count * width),
         name="adam_rows",
-    )(scalars, *in_hbm(*state), *in_hbm(*into))
-
-
-def frag_kernel(place_ref, sc_ref, w_ref, m_ref, v_ref, g_ref, inner_ref, *out_refs):
+    )(scalars, *in_hbm(*state), *squares, *in_hbm(*into))
+
+
+def frag_kernel(squares, place_ref, sc_ref, w_ref, m_ref, v_ref, g_ref, *refs):
     blocks, part, _ = w_ref.shape
+    factor = clip_factor(refs[:squares])
+    inner_ref, *out_refs = refs[squares:]
     for j in range(blocks):
         at = pl.multiple_of((place_ref[1] ^ j) * part, 8)
         old = w_ref[j]
-        update, _, _ = adam(old, m_ref[j], v_ref[j], g_ref[pl.ds(at, part), :], sc_ref)
+        update, _, _ = adam(old, m_ref[j], v_ref[j], g_ref[pl.ds(at, part), :], factor, sc_ref)
         inner_ref[j] = old - update
         out_refs[j][...] = update.astype(out_refs[j].dtype)
 
 
-def adam_frag(place, scalars, old, first, second, grad):
+def adam_frag(place, scalars, squares, old, first, second, grad):
     blocks, part, width = old.shape
     smem = pl.BlockSpec(memory_space=pltpu.SMEM)
     vmem = pl.BlockSpec(memory_space=pltpu.VMEM)
     return pl.pallas_call(
-        frag_kernel,
+        functools.partial(frag_kernel, len(squares)),
         out_shape=[jax.ShapeDtypeStruct(old.shape, jnp.float32)]
         + [jax.ShapeDtypeStruct((part, width), jnp.bfloat16)] * blocks,
-        in_specs=[smem, smem] + [vmem] * 4,
+        in_specs=[smem, smem] + [vmem] * (4 + len(squares)),
         out_specs=[vmem] * (1 + blocks),
         compiler_params=params_of(12),
         cost_estimate=cost(20 * old.size, 22 * old.size),
         name="adam_frag",
-    )(place, scalars, old, first, second, grad)
+    )(place, scalars, old, first, second, grad, *squares)
 
 
 def pick_kernel(place_ref, *refs):
@@ -377,7 +370,7 @@
 def outer_kernel(replicas, place_ref, *refs):
     share = 1.0 / replicas
     base_refs, sum_refs = refs[3:3 + replicas], refs[3 + replicas:3 + 2 * replicas]
-    inner_ref, a_ref, p_ref, m_ref, own_ref, w_out, a_out, m_out = refs[3 + 2 * replicas:]
+    inner_ref, a_ref, p_ref, m_ref, own_ref, _, w_out, a_out, m_out = refs[3 + 2 * replicas:]
     scale = share * (1.0 + OUTER_MU) * OUTER_RATE
     for j in range(replicas):
 
@@ -394,7 +387,7 @@
         a_out[...] = a_ref[...] - OUTER_RATE * (OUTER_MU * new_moment + pseudo)
 
 
-def outer_step(place, outputs, base, sums, inner, anchor, pseudo, momentum, own_sum):
+def outer_step(place, outputs, base, sums, inner, anchor, pseudo, momentum, own_sum, ticket):
     replicas, part = inner.shape[0], inner.shape[1]
     mixed = pl.BlockSpec((part, FRAG_COLS), lambda j, p: (p[1] ^ j, p[0]))
     pieces = pl.BlockSpec((1, part, FRAG_COLS), lambda j, p: (j, 0, 0))
@@ -407,14 +400,14 @@
         grid_spec=pltpu.PrefetchScalarGridSpec(
             num_scalar_prefetch=1,
             grid=(replicas,),
-            in_specs=[whole] * 3 + [plain] * (2 * replicas) + [pieces] + [plain] * 4,
+            in_specs=[whole] * 3 + [plain] * (2 * replicas) + [pieces] + [plain] * 4 + [whole],
             out_specs=[mixed, due, due],
         ),
         input_output_aliases={1: 0, 2: 1, 3: 2},
         compiler_params=params_of(12),
         cost_estimate=cost(10 * replicas * part * FRAG_COLS, 20 * replicas * part * FRAG_COLS),
         name="outer_step",
-    )(place, *in_hbm(*outputs), *base, *sums, inner, anchor, pseudo, momentum, own_sum)
+    )(place, *in_hbm(*outputs), *base, *sums, inner, anchor, pseudo, momentum, own_sum, ticket)
 
 
 def swap(block, axis, offset):
@@ -424,6 +417,11 @@
 
 def after(value, *others):
     return lax.optimization_barrier((value,) + others)[0]
+
+
+def by_device(pieces, me):
+    count = pieces.shape[0]
+    return jnp.stack([lax.dynamic_index_in_dim(pieces, me ^ k, 0, keepdims=False) for k in range(count)])
 
 
 class Line:
@@ -449,77 +447,39 @@
     step_count,
 ):
     inputs, incoming, params = tokens[0], cotangent[0], weights[0]
-    tok_rows = inputs.shape[0]
     kv_width = incoming.shape[1] // 2
     rows = params.shape[0]
     part = anchor.shape[0]
     replicas = lax.axis_size("rep")
     shards = lax.axis_size("fsdp")
     me = jnp.reshape(lax.axis_index("fsdp"), (1,)).astype(jnp.int32)
-    place = jnp.stack([due_fragment[0], lax.axis_index("rep").astype(jnp.int32)])
-    th = tok_rows // 2
+    my_rep = lax.axis_index("rep").astype(jnp.int32)
+    place = jnp.stack([due_fragment[0], my_rep])
     chips = range(2, shards, 2)
-    order = sorted(range(2, shards), key=lambda k: (-bin(k >> 1).count("1"), k & 1, k)) + [1]
-
-    line = Line("fsdp", 3)
-    blocks = [[None] * shards, [None] * shards]
-
-    def send_tokens(half, offsets):
-        for k in offsets:
-            blocks[half][k] = line.swap(pack(inputs, me, k, half, th, rows), k)
-
-    send_tokens(0, order)
-    early = blocks[0][order[0]]
-
-    rep_line = Line("rep", 1)
+    far = sorted(chips, key=lambda k: (-bin(k).count("1"), k))
+
+    line = Line("fsdp", 4)
+    values = {0: incoming[:, kv_width:]}
+    for k in chips:
+        values[k] = line.swap(values[0], k)
+
+    groups = [[k] for k in far if bin(k).count("1") > 1]
+    groups += [[k for k in far if bin(k).count("1") == 1]]
+    blocks = {0: pack(inputs, me, 0, rows)}
+    for group in groups:
+        for odd in range(2):
+            for k in group:
+                blocks[k + odd] = line.swap(pack(inputs, me, k + odd, rows), k + odd)
+    early = blocks[far[0]]
+    blocks[1] = swap(pack(inputs, after(me, early), 1, rows), "fsdp", 1)
+    value_list = [values[k] for k in range(0, shards, 2)]
+    crossed = swap(after(jnp.stack(value_list), early), "fsdp", 1)
+    value_list = [v for m in range(shards // 2) for v in (value_list[m], crossed[m])]
+
+    def to_all(pieces):
+        return lax.all_to_all(pieces, "rep", 0, 0, tiled=True)
+
     place_early = after(place, early)
-    old, old_first, old_second = due_columns(place_early, part, params, first_moment[0], second_moment[0])
-    anchor_cols, moment_cols = (c[0] for c in due_columns(place_early, part, anchor, momentum))
-    old_sum = old[0]
-    for k in range(1, replicas):
-        old_sum = old_sum + rep_line.swap(old[k], k)
-    pseudo_old = anchor_cols - old_sum / replicas
-    base = anchor_cols - OUTER_RATE * (OUTER_MU * (OUTER_MU * moment_cols + pseudo_old) + pseudo_old)
-    base = [base] + [rep_line.swap(base, k) for k in range(1, replicas)]
-    anchor_copy, momentum_copy = duplicate(anchor), duplicate(momentum)
-
-    key_weights = cast_left(after(params, early), kv_width)
-
-    def sum_keys(half):
-        x = blocks[half]
-        x[0] = pack(inputs, me, 0, half, th, rows)
-        theirs = swap(partial_keys(x[1::2], key_weights), "fsdp", 1)
-        return summed_keys(x[0::2], key_weights, theirs)
-
-    def scatter_keys(half, parts):
-        parts = [parts[0]] + [line.swap(parts[k // 2], k) for k in chips]
-        return key_backward(parts, incoming, half)
-
-    def gather(block):
-        out = []
-        for held in [block] + [line.swap(block, k) for k in chips]:
-            out += [held, swap(held, "fsdp", 1)]
-        return out
-
-    cut = (len(order) + 1) // 2
-    send_tokens(1, order[:cut])
-    back = scatter_keys(0, sum_keys(0))
-    send_tokens(1, order[cut:])
-    keys = [gather(back)]
-    flipped = [transpose_tokens(blocks[0])]
-    values = gather(incoming[:, kv_width:])
-    (grad_first,) = gradient(place, [(flipped[0], keys[0], 0)], last=False)
-    blocks[1][1] = after(blocks[1][1], base[-1], anchor_copy, momentum_copy, grad_first, old_second)
-    back = scatter_keys(1, sum_keys(1))
-    keys.append(gather(back))
-    flipped.append(transpose_tokens(blocks[1]))
-    grad_values, square, due = gradient(place, [(flipped[h], values, h) for h in range(2)])
-    grad_keys, square, due = gradient(place, [(flipped[1], keys[1], 0)], grad_first, square, due)
-
-    square = square + swap(square, "fsdp", 1)
-    square = sum([swap(square, "fsdp", k) for k in chips], square)
-    square = jnp.sum(square)
-    factor = jnp.minimum(1.0, CLIP_NORM / (jnp.sqrt(square) + 1e-06))
     steps_now = step_count[0].astype(jnp.float32)
     plan = jnp.minimum(1.0, steps_now / WARMUP) * (
         0.55 + 0.45 * jnp.cos(jnp.pi * steps_now / STEPS_TOTAL)
@@ -527,19 +487,57 @@
     rate = PEAK_RATE * plan
     inv_one = 1.0 / (1.0 - jnp.power(BETA_ONE, steps_now))
     inv_two = 1.0 / (1.0 - jnp.power(BETA_TWO, steps_now))
-    scalars = jnp.stack([factor, rate, inv_one, inv_two])
+    scalars = jnp.stack([rate, inv_one, inv_two])
+    old, old_first, old_second = due_columns(place_early, part, params, first_moment[0], second_moment[0])
+    anchor_cols, moment_cols = (c[0] for c in due_columns(place_early, part, anchor, momentum))
+    old_sum = jnp.sum(to_all(by_device(old, my_rep)), axis=0)
+    pseudo_old = anchor_cols - old_sum / replicas
+    base = anchor_cols - OUTER_RATE * (OUTER_MU * (OUTER_MU * moment_cols + pseudo_old) + pseudo_old)
+    base = to_all(jnp.broadcast_to(base[None], (replicas,) + base.shape))
+    base = by_device(base, my_rep)
+    base = [base[j] for j in range(replicas)]
+    anchor_copy, momentum_copy = duplicate(anchor), duplicate(momentum)
+    key_weights = cast_left(after(params, early), kv_width)
+
+    last = far[-1]
+    blocks[last + 1] = after(
+        blocks[last + 1], base[-1], anchor_copy, momentum_copy, old_second, scalars, value_list[-1]
+    )
+    parts = []
+    for k in far + [0]:
+        theirs = swap(partial_keys(blocks[k + 1], key_weights), "fsdp", 1)
+        part_k = partial_keys(blocks[k], key_weights, theirs)
+        parts.append(line.swap(part_k, k) if k else part_k)
+    back = key_backward(parts, incoming)
+    keys = []
+    for held in [back] + [line.swap(back, k) for k in chips]:
+        keys += [held, swap(held, "fsdp", 1)]
+
+    cut = shards // 2
+    flipped = [
+        transpose_tokens([blocks[k] for k in range(cut)]),
+        transpose_tokens([blocks[k] for k in range(cut, shards)]),
+    ]
+    grad_values, square, due = gradient(
+        place, [(flipped[0], value_list[:cut]), (flipped[1], value_list[cut:])]
+    )
+    (grad_first,) = gradient(place, [(flipped[0], keys[:cut])], last=False)
+    grad_keys, square, due = gradient(place, [(flipped[1], keys[cut:])], grad_first, square, due)
+
+    square = square + swap(square, "fsdp", 1)
+    squares = [square] + [swap(square, "fsdp", k) for k in chips]
 
     state = (params, first_moment[0], second_moment[0], grad_keys, grad_values)
-    inner, *update = adam_frag(place, scalars, old, old_first, old_second, due)
+    inner, *update = adam_frag(place, scalars, squares, old, old_first, old_second, due)
     steps = rows // 256
-    *results, ticket = adam_rows(scalars, state, 0, steps // 2)
+    *results, ticket = adam_rows(scalars, squares, state, 0, steps // 2)
     own_sum = update[0].astype(jnp.float32)
     for k in range(1, replicas):
         own_sum = own_sum + swap(update[k], "rep", k).astype(jnp.float32)
-    own_sum = after(own_sum, ticket)
+    own_sum, ticket = lax.optimization_barrier((own_sum, ticket))
     sums = [own_sum.astype(jnp.bfloat16)]
     sums += [swap(sums[0], "rep", k) for k in range(1, replicas)]
-    results = adam_rows(scalars, state, steps // 2, steps, results)
+    results = adam_rows(scalars, squares, state, steps // 2, steps, results)
     weights_out, anchor_out, momentum_out = outer_step(
         place,
         (results[0], anchor_copy, momentum_copy),
@@ -550,6 +548,7 @@
         pseudo_old,
         moment_cols,
         own_sum,
+        ticket,
     )
     plan_out = jnp.reshape(plan, (1,))
     return (

time: 219 us -> 205 us (0.936)
  starting transfers between devices: 61.4 us -> 44.2 us
  waiting for transfers between devices: 68.4 us -> 56.2 us
  Pallas kernels: 79 us -> 86.1 us
  local copies, waits for them, and re-layouts: 2.63 us -> 8.03 us
  other arithmetic: 1.58 us -> 5.18 us
    ppermute x59 -> x35, starting transfers between devices: 61.4 us -> 34.3 us  [swap(): return lax.ppermute(block, axis, [(i, i ^ offset) for i in range(count)])]
    ppermute x59 -> x35, waiting for transfers between devices: 68.4 us -> 56.2 us  [swap(): return lax.ppermute(block, axis, [(i, i ^ offset) for i in range(count)])]
    all_to_all x0 -> x2, starting transfers between devices: none -> 9.87 us  [to_all(): return lax.all_to_all(pieces, 'rep', 0, 0, tiled=True)]
    pallas_call x10 -> x14, Pallas kernels: 39 us -> 46.1 us  [the longest x2 19.5 us: adam_rows(): pl.pallas_call(functools.partial(adam_kernel, len(squares), len(into)), o...]
    pallas_call x16 -> x8, Pallas kernels: 18.6 us -> 13.9 us  [pack(): pl.pallas_call(pack_kernel, out_shape=jax.ShapeDtypeStruct((count, rows),...]
    pallas_call x2, Pallas kernels: 3.19 us -> 7.8 us  [transpose_tokens(): pl.pallas_call(transpose_kernel, out_shape=jax.ShapeDtypeStruct((rows, le...]
    squeeze x1 -> x2, local copies, waits for them, and re-layouts: 0.04 us -> 3.46 us  [the longest x1 2.19 us: body(): crossed[m]]
  transfers between devices with their start and end apart: 59 -> 37, of which waited for: 24 -> 12; matrix products, arithmetic and copies ran while one was open for 0% -> 4% of each run, Pallas kernels for 32% -> 36%
where the time goes in v5:
time: 205 us; the launch traced here: 204 us
  Pallas kernels  86.1 us (42%)
  waiting for transfers between devices  56.2 us (27%)
  starting transfers between devices  44.2 us (22%)
  local copies, waits for them, and re-layouts  8.03 us (4%)
  other arithmetic  5.18 us (3%)
  between operations  3.87 us (2%)
    ppermute x35, waiting for transfers between devices, swap(): return lax.ppermute(block, axis, [(i, i ^ offset) for i in range(count)])  56.2 us
    ppermute x35, starting transfers between devices, swap(): return lax.ppermute(block, axis, [(i, i ^ offset) for i in range(count)])  34.3 us
    pallas_call x2, Pallas kernels, adam_rows(): pl.pallas_call(functools.partial(adam_kernel, len(squares), len(into)), o...  19.5 us
    pallas_call x3, Pallas kernels, gradient(): pl.pallas_call(functools.partial(grad_kernel, [len(b) for _, b in terms],...  14.3 us
    pallas_call x8, Pallas kernels, pack(): pl.pallas_call(pack_kernel, out_shape=jax.ShapeDtypeStruct((count, rows),...  13.9 us
    pallas_call x8, Pallas kernels, partial_keys(): pl.pallas_call(partial_kernel, out_shape=jax.ShapeDtypeStruct((count, wid...  10.7 us
    all_to_all x2, starting transfers between devices, to_all(): return lax.all_to_all(pieces, 'rep', 0, 0, tiled=True)  9.87 us
    pallas_call x2, Pallas kernels, transpose_tokens(): pl.pallas_call(transpose_kernel, out_shape=jax.ShapeDtypeStruct((rows, le...  7.8 us
  transfers between devices with their start and end apart: 37, of which 12 were waited for; matrix products, arithmetic and copies ran while one was open for 4% of the time, Pallas kernels for 36%

profile of v5, /device:TPU:0, one launch (start us, length us, event | category | flops | bytes accessed | tf_op | source)
XLA Modules:
  0.0 203.6 jit_solution(9819588358306273710)
XLA Ops:
  0.6 1.2 pack.11
  1.8 4.0 %collective-permute-start.5 = (bf16[256,1536]{1,0:T(8,128)(2,1)S(1)}, bf16[256,1536]{1,0:T(8,128)(2,1)S(1)}, u32[]{:S(2)}, u32[]{:S(2)}) collective-permute-start(bf16[256,1536]{1,0:T(8,128)(2,1)S(1)} %pack.11), channel_id=1, source_target_pairs={{0,6},{1,7},{2,4},{3,5},{4,2},{5,3},{6,0},{7,1},{8,14},{9,15},{10,... | collective-permute-start | bytes 2359304 | tf_op jit(solution)/shard_map/ppermute | solution.py:415
  6.5 16.8 %collective-permute-done.5.refs_2_.x_ref = bf16[256,1536]{1,0:T(8,128)(2,1)S(1)} collective-permute-done((bf16[256,1536]{1,0:T(8,128)(2,1)S(1)}, bf16[256,1536]{1,0:T(8,128)(2,1)S(1)}, u32[]{:S(2)}, u32[]{:S(2)}) %collective-permute-start.5) | collective-permute-done | bytes 786464 | tf_op jit(solution)/shard_map/ppermute | solution.py:415
  23.3 3.1 %due_columns.3 = (f32[4,384,128]{2,1,0:T(8,128)S(1)}, f32[4,384,128]{2,1,0:T(8,128)S(1)}, f32[4,384,128]{2,1,0:T(8,128)S(1)}) custom-call(s32[2]{0:T(128)S(1)} %pad_add_fusion.place_ref.refs_0_, f32[1536,1024]{1,0:T(8,128)} %bitcast.55, f32[1536,1024]{1,0:T(8,128)} %bitcast.59, f32[1536,1024]{1,0:T(8,128)} %bitcast.62), custom_call_target="tpu_custom_call" | custom-call | bytes 4718592 | tf_op jit(solution)/shard_map/due_columns/pallas_call | solution.py:339
  26.5 0.9 copy-done.7
  27.4 1.0 copy-done.9
  28.4 0.9 copy-done.3
  29.3 0.9 pad_maximum_fusion.1
  30.3 5.1 %all-to-all-start = ((f32[4,384,128]{2,1,0:T(8,128)}), f32[4,384,128]{2,1,0:T(8,128)}, u32[]{:S(2)}, u32[]{:S(2)}) async-start(f32[4,384,128]{2,1,0:T(8,128)} %pad_maximum_fusion.1), calls=%async_computation | async-start | bytes 1572864 | tf_op jit(solution)/shard_map/all_to_all | solution.py:480
  35.4 1.6 collective-permute-start.2
  36.9 1.5 collective-permute-start.6
  38.9 1.2 pack.13
  40.1 2.1 %pack.10 = bf16[256,1536]{1,0:T(8,128)(2,1)} custom-call(s32[1]{0:T(128)} %bitcast.4.me_ref, bf16[256,12288]{1,0:T(8,128)(2,1)} %bitcast.49), custom_call_target="tpu_custom_call" | custom-call | bytes 1572864 | tf_op jit(solution)/shard_map/pack/pallas_call | solution.py:51
  42.2 2.5 %collective-permute-done.2.refs_4_ = bf16[256,512]{1,0:T(8,128)(2,1)S(1)} collective-permute-done((bf16[256,512]{1,0:T(8,128)(2,1)S(1)}, bf16[256,512]{1,0:T(8,128)(2,1)S(1)}, u32[]{:S(2)}, u32[]{:S(2)}) %collective-permute-start.2) | collective-permute-done | bytes 262176 | tf_op jit(solution)/shard_map/ppermute | solution.py:415
  44.7 21.3 %collective-permute-done.6.refs_7_ = bf16[256,512]{1,0:T(8,128)(2,1)S(1)} collective-permute-done((bf16[256,512]{1,0:T(8,128)(2,1)S(1)}, bf16[256,512]{1,0:T(8,128)(2,1)S(1)}, u32[]{:S(2)}, u32[]{:S(2)}) %collective-permute-start.6) | collective-permute-done | bytes 262176 | tf_op jit(solution)/shard_map/ppermute | solution.py:415
  66.0 1.1 pad_maximum_fusion
  67.2 1.6 due_columns.2
  68.8 1.9 reduce_sum.9
  70.7 1.0 subtract_bitcast_fusion
  71.7 0.9 broadcast_in_dim.18
  72.6 4.8 %all-to-all-start.1 = ((f32[4,384,128]{2,1,0:T(8,128)}), f32[4,384,128]{2,1,0:T(8,128)}, u32[]{:S(2)}, u32[]{:S(2)}) async-start(f32[4,384,128]{2,1,0:T(8,128)} %broadcast_in_dim.18), calls=%async_computation.1 | async-start | bytes 1572864 | tf_op jit(solution)/shard_map/all_to_all | solution.py:480
  77.4 2.1 %pack.9 = bf16[256,1536]{1,0:T(8,128)(2,1)} custom-call(s32[1]{0:T(128)} %bitcast.4.me_ref, bf16[256,12288]{1,0:T(8,128)(2,1)} %bitcast.50), custom_call_target="tpu_custom_call" | custom-call | bytes 1572864 | tf_op jit(solution)/shard_map/pack/pallas_call | solution.py:51
  79.5 1.5 collective-permute-start.4
  81.0 2.1 %pack.12 = bf16[256,1536]{1,0:T(8,128)(2,1)} custom-call(s32[1]{0:T(128)} %bitcast.4.me_ref, bf16[256,12288]{1,0:T(8,128)(2,1)} %bitcast.51), custom_call_target="tpu_custom_call" | custom-call | bytes 1572864 | tf_op jit(solution)/shard_map/pack/pallas_call | solution.py:51
  83.1 2.1 %pack.8 = bf16[256,1536]{1,0:T(8,128)(2,1)} custom-call(s32[1]{0:T(128)} %bitcast.4.me_ref, bf16[256,12288]{1,0:T(8,128)(2,1)} %bitcast.52), custom_call_target="tpu_custom_call" | custom-call | bytes 1572864 | tf_op jit(solution)/shard_map/pack/pallas_call | solution.py:51
  86.7 1.5 collective-permute-start.9
  88.2 2.1 %pack.15 = bf16[256,1536]{1,0:T(8,128)(2,1)} custom-call(s32[1]{0:T(128)} %bitcast.4.me_ref, bf16[256,12288]{1,0:T(8,128)(2,1)} %bitcast.53), custom_call_target="tpu_custom_call" | custom-call | bytes 1572864 | tf_op jit(solution)/shard_map/pack/pallas_call | solution.py:51
  90.4 3.7 %duplicate.2.refs_1_ = f32[384,1024]{1,0:T(8,128)} custom-call(f32[384,1024]{1,0:T(8,128)} %src_ref.2), custom_call_target="tpu_custom_call" | custom-call | bytes 3145728 | tf_op jit(solution)/shard_map/duplicate/pallas_call | solution.py:358
  94.2 3.6 %duplicate.3.refs_2_ = f32[384,1024]{1,0:T(8,128)} custom-call(f32[384,1024]{1,0:T(8,128)} %src_ref.3), custom_call_target="tpu_custom_call" | custom-call | bytes 3145728 | tf_op jit(solution)/shard_map/duplicate/pallas_call | solution.py:358
  97.7 3.5 %cast_left.1.w_ref = bf16[1536,512]{1,0:T(8,128)(2,1)S(1)} custom-call(f32[1536,1024]{1,0:T(8,128)} %bitcast.56), custom_call_target="tpu_custom_call" | custom-call | bytes 4718592 | tf_op jit(solution)/shard_map/cast_left/pallas_call | solution.py:95
  101.2 1.3 partial_keys.8
  104.0 2.2 %slice_bitcast_fusion = (bf16[256,512]{1,0:T(8,128)(2,1)}, bf16[256,512]{1,0:T(8,128)(2,1)}, bf16[256,512]{1,0:T(8,128)(2,1)}, bf16[256,512]{1,0:T(8,128)(2,1)}) fusion(bf16[4,256,512]{2,1,0:T(8,128)(2,1)} %collective-permute-done.7), kind=kLoop, calls=%fused_computation.2 | loop fusion | bytes 2097152 | tf_op jit(solution)/shard_map/squeeze | solution.py:477
  106.2 1.3 dynamic-slice_bitcast_fusion
  107.8 1.7 partial_keys.12
  109.9 1.5 partial_keys.9
  111.4 1.4 collective-permute-start.10
  112.8 1.7 partial_keys.14
  114.6 1.7 partial_keys.11
  116.3 5.8 %collective-permute-done.1.refs_0_.x_ref = bf16[256,1536]{1,0:T(8,128)(2,1)} collective-permute-done((bf16[256,1536]{1,0:T(8,128)(2,1)}, bf16[256,1536]{1,0:T(8,128)(2,1)}, u32[]{:S(2)}, u32[]{:S(2)}) %collective-permute-start.1) | collective-permute-done | bytes 786464 | tf_op jit(solution)/shard_map/ppermute | solution.py:415
  122.1 2.1 %collective-permute-start.13 = (bf16[256,512]{1,0:T(8,128)(2,1)S(1)}, bf16[256,512]{1,0:T(8,128)(2,1)S(1)}, u32[]{:S(2)}, u32[]{:S(2)}) collective-permute-start(bf16[256,512]{1,0:T(8,128)(2,1)S(1)} %partial_keys.11), channel_id=1, source_target_pairs={{0,2},{1,3},{2,0},{3,1},{4,6},{5,7},{6,4},{7,5},{8,10},{9,11},{10,... | collective-permute-start | bytes 786440 | tf_op jit(solution)/shard_map/ppermute | solution.py:415
  124.2 1.7 partial_keys.13
  125.9 1.4 collective-permute-start.15
  127.3 1.2 pack.14.x_ref.refs_0_
  129.1 1.6 collective-permute-done.13.refs_1_
  130.7 3.2 %collective-permute-done.15.refs_2_ = bf16[256,512]{1,0:T(8,128)(2,1)S(1)} collective-permute-done((bf16[256,512]{1,0:T(8,128)(2,1)S(1)}, bf16[256,512]{1,0:T(8,128)(2,1)S(1)}, u32[]{:S(2)}, u32[]{:S(2)}) %collective-permute-start.15) | collective-permute-done | bytes 262176 | tf_op jit(solution)/shard_map/ppermute | solution.py:415
  134.5 1.5 collective-permute-start.18
  136.3 1.7 collective-permute-start.23
  138.1 3.8 %transpose_tokens.3.refs_1_ = bf16[1536,1024]{1,0:T(8,128)(2,1)S(1)} custom-call(bf16[256,1536]{1,0:T(8,128)(2,1)S(1)} %pack.14.x_ref.refs_0_, bf16[256,1536]{1,0:T(8,128)(2,1)} %collective-permute-done.16.x_ref.refs_1_, bf16[256,1536]{1,0:T(8,128)(2,1)} %collective-permute-done.9.x_ref.refs_2_, bf16[256,1536]{1,0:T(8,128)(2,1)S(1)} %copy-done.2), custom_call_target="tpu_custom_call" | custom-call | bytes 6291456 | tf_op jit(solution)/shard_map/transpose_tokens/pallas_call | solution.py:76
  142.0 4.0 %transpose_tokens.2.refs_6_.refs_1_ = bf16[1536,1024]{1,0:T(8,128)(2,1)S(1)} custom-call(bf16[256,1536]{1,0:T(8,128)(2,1)} %collective-permute-done.1.refs_0_.x_ref, bf16[256,1536]{1,0:T(8,128)(2,1)} %collective-permute-done.4.refs_1_.x_ref, bf16[256,1536]{1,0:T(8,128)(2,1)S(1)} %collective-permute-done.5.refs_2_.x_ref, ...), custom_call_target="tpu_custom_call" | custom-call | bytes 6291456 | tf_op jit(solution)/shard_map/transpose_tokens/pallas_call | solution.py:76
  146.0 1.2 collective-permute-done.18.refs_2_
  148.6 6.0 %gradient.4 = (f32[1536,512]{1,0:T(8,128)}, f32[8,128]{1,0:T(8,128)S(1)}, f32[1536,128]{1,0:T(8,128)S(1)}) custom-call(s32[2]{0:T(128)S(1)} %pad_add_fusion.place_ref.refs_0_, bf16[1536,1024]{1,0:T(8,128)(2,1)S(1)} %transpose_tokens.3.refs_1_, bf16[256,512]{1,0:T(8,128)(2,1)S(1)} %copy-done.12, bf16[256,512]{1,0:T(8,128)(2,1)S(1)} %copy-done.22, ...), custom_call_target="tpu_custom_call" | custom-call | flops 3221225472 | bytes 9437184 | tf_op jit(solution)/shard_map/gradient/pallas_call | solution.py:228
  154.6 3.3 %gradient.3.refs_6_ = f32[1536,512]{1,0:T(8,128)S(1)} custom-call(s32[2]{0:T(128)S(1)} %pad_add_fusion.place_ref.refs_0_, bf16[1536,1024]{1,0:T(8,128)(2,1)S(1)} %transpose_tokens.3.refs_1_, bf16[256,512]{1,0:T(8,128)(2,1)S(1)} %key_backward.1.refs_2_, bf16[256,512]{1,0:T(8,128)(2,1)S(1)} %collective-permute-done.22.refs_3_, ...), custom_call_target="tpu_custom_call" | custom-call | flops 1610612736 | bytes 6291456 | tf_op jit(solution)/shard_map/gradient/pallas_call | solution.py:228
  158.0 4.9 %gradient.5 = (f32[1536,512]{1,0:T(8,128)}, f32[8,128]{1,0:T(8,128)S(1)}, f32[1536,128]{1,0:T(8,128)S(1)}) custom-call(s32[2]{0:T(128)S(1)} %pad_add_fusion.place_ref.refs_0_, bf16[1536,1024]{1,0:T(8,128)(2,1)S(1)} %transpose_tokens.2.refs_6_.refs_1_, bf16[256,512]{1,0:T(8,128)(2,1)S(1)} %collective-permute-done.18.refs_2_, ...), custom_call_target="tpu_custom_call" | custom-call | flops 1610612736 | bytes 6291456 | tf_op jit(solution)/shard_map/gradient/pallas_call | solution.py:228
  163.4 0.8 collective-permute-done.25
  164.2 1.5 collective-permute-start.28
  166.3 1.4 collective-permute-start.26
  167.7 1.0 collective-permute-done.28.refs_3_
  169.9 1.5 adam_frag.1
  171.5 2.1 %collective-permute-start.29 = (bf16[384,128]{1,0:T(8,128)(2,1)S(1)}, bf16[384,128]{1,0:T(8,128)(2,1)S(1)}, u32[]{:S(2)}, u32[]{:S(2)}) collective-permute-start(bf16[384,128]{1,0:T(8,128)(2,1)S(1)} %get-tuple-element.82), channel_id=1, source_target_pairs={{0,8},{8,0},{16,24},{24,16},{1,9},{9,1},{17,25},{25,17},{2,10},{10... | collective-permute-start | bytes 294920 | tf_op jit(solution)/shard_map/ppermute | solution.py:415
  173.6 2.4 %collective-permute-start.30 = (bf16[384,128]{1,0:T(8,128)(2,1)S(1)}, bf16[384,128]{1,0:T(8,128)(2,1)S(1)}, u32[]{:S(2)}, u32[]{:S(2)}) collective-permute-start(bf16[384,128]{1,0:T(8,128)(2,1)S(1)} %get-tuple-element.83), channel_id=1, source_target_pairs={{0,16},{8,24},{16,0},{24,8},{1,17},{9,25},{17,1},{25,9},{2,18},{10... | collective-permute-start | bytes 294920 | tf_op jit(solution)/shard_map/ppermute | solution.py:415
  176.0 9.8 %adam_rows.2 = (f32[1536,1024]{1,0:T(8,128)}, f32[1536,1024]{1,0:T(8,128)}, f32[1536,1024]{1,0:T(8,128)}, f32[8,128]{1,0:T(8,128)S(1)}) custom-call(f32[3]{0:T(128)S(1)} %pad_maximum_fusion.2.sc_ref, f32[1536,1024]{1,0:T(8,128)} %bitcast.57, f32[1536,1024]{1,0:T(8,128)} %bitcast.60, f32[1536,1024]{1,0:T(8,128)} %bitcast.63, ...), custom_call_target="tpu_custom_call" | custom-call | flops 15728640 | bytes 22020096 | tf_op jit(solution)/shard_map/adam_rows/pallas_call | solution.py:287
  185.9 3.8 %collective-permute-start.34 = (bf16[384,128]{1,0:T(8,128)(2,1)S(1)}, bf16[384,128]{1,0:T(8,128)(2,1)S(1)}, u32[]{:S(2)}, u32[]{:S(2)}) collective-permute-start(bf16[384,128]{1,0:T(8,128)(2,1)S(1)} %convert_element_type.24.refs_7_), channel_id=1, source_target_pairs={{0,24},{8,16},{16,8},{24,0},{1,25},{9,17},{17,9},{25,1},{2,26},{10... | collective-permute-start | bytes 294920 | tf_op jit(solution)/shard_map/ppermute | solution.py:415
  190.4 9.8 %adam_rows.3 = (f32[1536,1024]{1,0:T(8,128)}, f32[1536,1024]{1,0:T(8,128)}, f32[1536,1024]{1,0:T(8,128)}) custom-call(f32[3]{0:T(128)S(1)} %pad_maximum_fusion.2.sc_ref, f32[1536,1024]{1,0:T(8,128)} %bitcast.58, f32[1536,1024]{1,0:T(8,128)} %bitcast.61, f32[1536,1024]{1,0:T(8,128)} %bitcast.64, ...), custom_call_target="tpu_custom_call", output_to_operand_aliasing={{0}: (10, {}), {1}: (11, {}), {2}: (12, {})} | custom-call | flops 15728640 | bytes 22020096 | tf_op jit(solution)/shard_map/adam_rows/pallas_call | solution.py:287
  200.2 2.4 %outer_step.1 = (f32[1536,1024]{1,0:T(8,128)}, f32[384,1024]{1,0:T(8,128)}, f32[384,1024]{1,0:T(8,128)}) custom-call(s32[2]{0:T(128)S(1)} %pad_add_fusion.place_ref.refs_0_, f32[1536,1024]{1,0:T(8,128)} %get-tuple-element.78.refs_0_, f32[384,1024]{1,0:T(8,128)} %duplicate.2.refs_1_, ...), custom_call_target="tpu_custom_call", output_to_operand_aliasing={{0}: (1, {}), {1}: (2, {}), {2}: (3, {})} | custom-call | flops 1966080 | bytes 3932160 | tf_op jit(solution)/shard_map/outer_step/pallas_call | solution.py:397
  (106 shorter events, 9.7 us)
Async XLA Ops:
  1.8 21.5 %collective-permute-start.5 = (bf16[256,1536]{1,0:T(8,128)(2,1)S(1)}, bf16[256,1536]{1,0:T(8,128)(2,1)S(1)}, u32[]{:S(2)}, u32[]{:S(2)}) collective-permute-start(bf16[256,1536]{1,0:T(8,128)(2,1)S(1)} %pack.11), channel_id=1, source_target_pairs={{0,6},{1,7},{2,4},{3,5},{4,2},{5,3},{6,0},{7,1},{8,14},{9,15},{10,... | collective-permute-start | bytes 2359304 | tf_op jit(solution)/shard_map/ppermute | solution.py:415
  26.5 0.9 copy-start.7
  27.4 1.0 copy-start.9
  28.3 7.0 %copy-start.5 = (bf16[1,256,1024]{2,1,0:T(8,128)(2,1)S(1)}, bf16[1,256,1024]{2,1,0:T(8,128)(2,1)}, u32[]{:S(2)}) copy-start(bf16[1,256,1024]{2,1,0:T(8,128)(2,1)} %param.10) | copy-start | bytes 1572868
  28.4 0.9 copy-start.3
  30.3 38.5 %all-to-all-start = ((f32[4,384,128]{2,1,0:T(8,128)}), f32[4,384,128]{2,1,0:T(8,128)}, u32[]{:S(2)}, u32[]{:S(2)}) async-start(f32[4,384,128]{2,1,0:T(8,128)} %pad_maximum_fusion.1), calls=%async_computation | async-start | bytes 1572864 | tf_op jit(solution)/shard_map/all_to_all | solution.py:480
  35.4 4.8 %copy-start.11 = (bf16[256,512]{1,0:T(8,128)(2,1)}, bf16[256,512]{1,0:T(8,128)(2,1)S(1)}, u32[]{:S(2)}) copy-start(bf16[256,512]{1,0:T(8,128)(2,1)S(1)} %get-tuple-element.107.refs_2_) | copy-start | bytes 786436
  35.4 9.3 %collective-permute-start.2 = (bf16[256,512]{1,0:T(8,128)(2,1)S(1)}, bf16[256,512]{1,0:T(8,128)(2,1)S(1)}, u32[]{:S(2)}, u32[]{:S(2)}) collective-permute-start(bf16[256,512]{1,0:T(8,128)(2,1)S(1)} %get-tuple-element.107.refs_2_), channel_id=1, source_target_pairs={{0,2},{1,3},{2,0},{3,1},{4,6},{5,7},{6,4},{7,5},{8,10},{9,11},{10,... | collective-permute-start | bytes 786440 | tf_op jit(solution)/shard_map/ppermute | solution.py:415
  36.9 29.1 %collective-permute-start.6 = (bf16[256,512]{1,0:T(8,128)(2,1)S(1)}, bf16[256,512]{1,0:T(8,128)(2,1)S(1)}, u32[]{:S(2)}, u32[]{:S(2)}) collective-permute-start(bf16[256,512]{1,0:T(8,128)(2,1)S(1)} %get-tuple-element.107.refs_2_), channel_id=1, source_target_pairs={{0,4},{1,5},{2,6},{3,7},{4,0},{5,1},{6,2},{7,3},{8,12},{9,13},{10,... | collective-permute-start | bytes 786440 | tf_op jit(solution)/shard_map/ppermute | solution.py:415
  38.4 27.6 %collective-permute-start = (bf16[256,512]{1,0:T(8,128)(2,1)S(1)}, bf16[256,512]{1,0:T(8,128)(2,1)S(1)}, u32[]{:S(2)}, u32[]{:S(2)}) collective-permute-start(bf16[256,512]{1,0:T(8,128)(2,1)S(1)} %get-tuple-element.107.refs_2_), channel_id=1, source_target_pairs={{0,6},{1,7},{2,4},{3,5},{4,2},{5,3},{6,0},{7,1},{8,14},{9,15},{10,... | collective-permute-start | bytes 786440 | tf_op jit(solution)/shard_map/ppermute | solution.py:415
  44.7 22.5 %copy-start.14 = (bf16[256,512]{1,0:T(8,128)(2,1)}, bf16[256,512]{1,0:T(8,128)(2,1)S(1)}, u32[]{:S(2)}) copy-start(bf16[256,512]{1,0:T(8,128)(2,1)S(1)} %collective-permute-done.2.refs_4_) | copy-start | bytes 786436
  44.7 34.8 %collective-permute-start.3 = (bf16[256,1536]{1,0:T(8,128)(2,1)}, bf16[256,1536]{1,0:T(8,128)(2,1)S(1)}, u32[]{:S(2)}, u32[]{:S(2)}) collective-permute-start(bf16[256,1536]{1,0:T(8,128)(2,1)} %pack.10), channel_id=1, source_target_pairs={{0,7},{1,6},{2,5},{3,4},{4,3},{5,2},{6,1},{7,0},{8,15},{9,14},{10,... | collective-permute-start | bytes 2359304 | tf_op jit(solution)/shard_map/ppermute | solution.py:415
  66.0 1.2 copy-start.16
  66.0 1.2 copy-start.18
  67.2 23.1 %collective-permute-start.11 = (bf16[256,1536]{1,0:T(8,128)(2,1)S(1)}, bf16[256,1536]{1,0:T(8,128)(2,1)S(1)}, u32[]{:S(2)}, u32[]{:S(2)}) collective-permute-start(bf16[256,1536]{1,0:T(8,128)(2,1)S(1)} %pack.13), channel_id=1, source_target_pairs={{0,3},{1,2},{2,1},{3,0},{4,7},{5,6},{6,5},{7,4},{8,11},{9,10},{10,... | collective-permute-start | bytes 2359304 | tf_op jit(solution)/shard_map/ppermute | solution.py:415
  67.2 36.6 %collective-permute-start.7 = (bf16[4,256,512]{2,1,0:T(8,128)(2,1)}, bf16[4,256,512]{2,1,0:T(8,128)(2,1)}, u32[]{:S(2)}, u32[]{:S(2)}) collective-permute-start(bf16[4,256,512]{2,1,0:T(8,128)(2,1)} %pad_maximum_fusion), channel_id=1, source_target_pairs={{0,1},{1,0},{2,3},{3,2},{4,5},{5,4},{6,7},{7,6},{8,9},{9,8},{10,11... | collective-permute-start | bytes 3145736 | tf_op jit(solution)/shard_map/ppermute | solution.py:415
  72.6 33.6 %all-to-all-start.1 = ((f32[4,384,128]{2,1,0:T(8,128)}), f32[4,384,128]{2,1,0:T(8,128)}, u32[]{:S(2)}, u32[]{:S(2)}) async-start(f32[4,384,128]{2,1,0:T(8,128)} %broadcast_in_dim.18), calls=%async_computation.1 | async-start | bytes 1572864 | tf_op jit(solution)/shard_map/all_to_all | solution.py:480
  79.5 28.0 %collective-permute-start.4 = (bf16[256,1536]{1,0:T(8,128)(2,1)}, bf16[256,1536]{1,0:T(8,128)(2,1)}, u32[]{:S(2)}, u32[]{:S(2)}) collective-permute-start(bf16[256,1536]{1,0:T(8,128)(2,1)} %pack.9), channel_id=1, source_target_pairs={{0,5},{1,4},{2,7},{3,6},{4,1},{5,0},{6,3},{7,2},{8,13},{9,12},{10,... | collective-permute-start | bytes 2359304 | tf_op jit(solution)/shard_map/ppermute | solution.py:415
  86.0 36.1 %collective-permute-start.1 = (bf16[256,1536]{1,0:T(8,128)(2,1)}, bf16[256,1536]{1,0:T(8,128)(2,1)}, u32[]{:S(2)}, u32[]{:S(2)}) collective-permute-start(bf16[256,1536]{1,0:T(8,128)(2,1)} %pack.8), channel_id=1, source_target_pairs={{0,4},{1,5},{2,6},{3,7},{4,0},{5,1},{6,2},{7,3},{8,12},{9,13},{10,... | collective-permute-start | bytes 2359304 | tf_op jit(solution)/shard_map/ppermute | solution.py:415
  86.7 24.7 %collective-permute-start.9 = (bf16[256,1536]{1,0:T(8,128)(2,1)}, bf16[256,1536]{1,0:T(8,128)(2,1)}, u32[]{:S(2)}, u32[]{:S(2)}) collective-permute-start(bf16[256,1536]{1,0:T(8,128)(2,1)} %pack.12), channel_id=1, source_target_pairs={{0,2},{1,3},{2,0},{3,1},{4,6},{5,7},{6,4},{7,5},{8,10},{9,11},{10,... | collective-permute-start | bytes 2359304 | tf_op jit(solution)/shard_map/ppermute | solution.py:415
  90.3 3.9 %copy-start = (bf16[256,1536]{1,0:T(8,128)(2,1)}, bf16[256,1536]{1,0:T(8,128)(2,1)S(1)}, u32[]{:S(2)}) copy-start(bf16[256,1536]{1,0:T(8,128)(2,1)S(1)} %collective-permute-done.11.x_ref.refs_3_) | copy-start | bytes 2359300
  90.3 22.5 %collective-permute-start.16 = (bf16[256,1536]{1,0:T(8,128)(2,1)}, bf16[256,1536]{1,0:T(8,128)(2,1)}, u32[]{:S(2)}, u32[]{:S(2)}) collective-permute-start(bf16[256,1536]{1,0:T(8,128)(2,1)} %pack.15), channel_id=1, source_target_pairs={{0,1},{1,0},{2,3},{3,2},{4,5},{5,4},{6,7},{7,6},{8,9},{9,8},{10,11... | collective-permute-start | bytes 2359304 | tf_op jit(solution)/shard_map/ppermute | solution.py:415
  101.2 1.3 copy-start.1
  103.0 0.7 copy-start.13
  103.8 5.8 %collective-permute-start.8 = (bf16[256,512]{1,0:T(8,128)(2,1)}, bf16[256,512]{1,0:T(8,128)(2,1)}, u32[]{:S(2)}, u32[]{:S(2)}) collective-permute-start(bf16[256,512]{1,0:T(8,128)(2,1)} %partial_keys.8), channel_id=1, source_target_pairs={{0,1},{1,0},{2,3},{3,2},{4,5},{5,4},{6,7},{7,6},{8,9},{9,8},{10,11... | collective-permute-start | bytes 786440 | tf_op jit(solution)/shard_map/ppermute | solution.py:415
  107.5 7.1 %collective-permute-start.12 = (bf16[256,512]{1,0:T(8,128)(2,1)}, bf16[256,512]{1,0:T(8,128)(2,1)S(1)}, u32[]{:S(2)}, u32[]{:S(2)}) collective-permute-start(bf16[256,512]{1,0:T(8,128)(2,1)} %copy-done.13), channel_id=1, source_target_pairs={{0,1},{1,0},{2,3},{3,2},{4,5},{5,4},{6,7},{7,6},{8,9},{9,8},{10,11... | collective-permute-start | bytes 786440 | tf_op jit(solution)/shard_map/ppermute | solution.py:415
  109.5 14.7 %collective-permute-start.14 = (bf16[256,512]{1,0:T(8,128)(2,1)S(1)}, bf16[256,512]{1,0:T(8,128)(2,1)S(1)}, u32[]{:S(2)}, u32[]{:S(2)}) collective-permute-start(bf16[256,512]{1,0:T(8,128)(2,1)S(1)} %partial_keys.12), channel_id=1, source_target_pairs={{0,1},{1,0},{2,3},{3,2},{4,5},{5,4},{6,7},{7,6},{8,9},{9,8},{10,11... | collective-permute-start | bytes 786440 | tf_op jit(solution)/shard_map/ppermute | solution.py:415
  111.4 17.7 %collective-permute-start.10 = (bf16[256,512]{1,0:T(8,128)(2,1)S(1)}, bf16[256,512]{1,0:T(8,128)(2,1)S(1)}, u32[]{:S(2)}, u32[]{:S(2)}) collective-permute-start(bf16[256,512]{1,0:T(8,128)(2,1)S(1)} %partial_keys.9), channel_id=1, source_target_pairs={{0,6},{1,7},{2,4},{3,5},{4,2},{5,3},{6,0},{7,1},{8,14},{9,15},{10,... | collective-permute-start | bytes 786440 | tf_op jit(solution)/shard_map/ppermute | solution.py:415
  114.5 14.0 %collective-permute-start.17 = (bf16[256,512]{1,0:T(8,128)(2,1)S(1)}, bf16[256,512]{1,0:T(8,128)(2,1)S(1)}, u32[]{:S(2)}, u32[]{:S(2)}) collective-permute-start(bf16[256,512]{1,0:T(8,128)(2,1)S(1)} %partial_keys.14), channel_id=1, source_target_pairs={{0,1},{1,0},{2,3},{3,2},{4,5},{5,4},{6,7},{7,6},{8,9},{9,8},{10,11... | collective-permute-start | bytes 786440 | tf_op jit(solution)/shard_map/ppermute | solution.py:415
  122.1 8.6 %collective-permute-start.13 = (bf16[256,512]{1,0:T(8,128)(2,1)S(1)}, bf16[256,512]{1,0:T(8,128)(2,1)S(1)}, u32[]{:S(2)}, u32[]{:S(2)}) collective-permute-start(bf16[256,512]{1,0:T(8,128)(2,1)S(1)} %partial_keys.11), channel_id=1, source_target_pairs={{0,2},{1,3},{2,0},{3,1},{4,6},{5,7},{6,4},{7,5},{8,10},{9,11},{10,... | collective-permute-start | bytes 786440 | tf_op jit(solution)/shard_map/ppermute | solution.py:415
  125.9 8.0 %collective-permute-start.15 = (bf16[256,512]{1,0:T(8,128)(2,1)S(1)}, bf16[256,512]{1,0:T(8,128)(2,1)S(1)}, u32[]{:S(2)}, u32[]{:S(2)}) collective-permute-start(bf16[256,512]{1,0:T(8,128)(2,1)S(1)} %partial_keys.13), channel_id=1, source_target_pairs={{0,4},{1,5},{2,6},{3,7},{4,0},{5,1},{6,2},{7,3},{8,12},{9,13},{10,... | collective-permute-start | bytes 786440 | tf_op jit(solution)/shard_map/ppermute | solution.py:415
  128.5 5.4 %copy-start.6 = (bf16[1,256,1024]{2,1,0:T(8,128)(2,1)S(1)}, bf16[1,256,1024]{2,1,0:T(8,128)(2,1)}, u32[]{:S(2)}) copy-start(bf16[1,256,1024]{2,1,0:T(8,128)(2,1)} %param.10) | copy-start | bytes 1572868
  128.5 9.5 %copy-start.2 = (bf16[256,1536]{1,0:T(8,128)(2,1)S(1)}, bf16[256,1536]{1,0:T(8,128)(2,1)}, u32[]{:S(2)}) copy-start(bf16[256,1536]{1,0:T(8,128)(2,1)} %copy-done) | copy-start | bytes 2359300
  134.5 12.8 %collective-permute-start.18 = (bf16[256,512]{1,0:T(8,128)(2,1)S(1)}, bf16[256,512]{1,0:T(8,128)(2,1)S(1)}, u32[]{:S(2)}, u32[]{:S(2)}) collective-permute-start(bf16[256,512]{1,0:T(8,128)(2,1)S(1)} %key_backward.1.refs_2_), channel_id=1, source_target_pairs={{0,4},{1,5},{2,6},{3,7},{4,0},{5,1},{6,2},{7,3},{8,12},{9,13},{10,... | collective-permute-start | bytes 786440 | tf_op jit(solution)/shard_map/ppermute | solution.py:415
  136.0 11.3 %collective-permute-start.20 = (bf16[256,512]{1,0:T(8,128)(2,1)S(1)}, bf16[256,512]{1,0:T(8,128)(2,1)S(1)}, u32[]{:S(2)}, u32[]{:S(2)}) collective-permute-start(bf16[256,512]{1,0:T(8,128)(2,1)S(1)} %key_backward.1.refs_2_), channel_id=1, source_target_pairs={{0,6},{1,7},{2,4},{3,5},{4,2},{5,3},{6,0},{7,1},{8,14},{9,15},{10,... | collective-permute-start | bytes 786440 | tf_op jit(solution)/shard_map/ppermute | solution.py:415
  136.3 12.2 %collective-permute-start.23 = (bf16[256,512]{1,0:T(8,128)(2,1)S(1)}, bf16[256,512]{1,0:T(8,128)(2,1)S(1)}, u32[]{:S(2)}, u32[]{:S(2)}) collective-permute-start(bf16[256,512]{1,0:T(8,128)(2,1)S(1)} %key_backward.1.refs_2_), channel_id=1, source_target_pairs={{0,2},{1,3},{2,0},{3,1},{4,6},{5,7},{6,4},{7,5},{8,10},{9,11},{10,... | collective-permute-start | bytes 786440 | tf_op jit(solution)/shard_map/ppermute | solution.py:415
  141.9 6.6 %copy-start.12 = (bf16[256,512]{1,0:T(8,128)(2,1)S(1)}, bf16[256,512]{1,0:T(8,128)(2,1)}, u32[]{:S(2)}) copy-start(bf16[256,512]{1,0:T(8,128)(2,1)} %copy-done.11) | copy-start | bytes 786436
  141.9 6.6 %copy-start.15 = (bf16[256,512]{1,0:T(8,128)(2,1)S(1)}, bf16[256,512]{1,0:T(8,128)(2,1)}, u32[]{:S(2)}) copy-start(bf16[256,512]{1,0:T(8,128)(2,1)} %copy-done.14) | copy-start | bytes 786436
  141.9 6.6 %copy-start.17 = (bf16[256,512]{1,0:T(8,128)(2,1)S(1)}, bf16[256,512]{1,0:T(8,128)(2,1)}, u32[]{:S(2)}) copy-start(bf16[256,512]{1,0:T(8,128)(2,1)} %copy-done.16) | copy-start | bytes 786436
  141.9 6.6 %copy-start.19 = (bf16[256,512]{1,0:T(8,128)(2,1)S(1)}, bf16[256,512]{1,0:T(8,128)(2,1)}, u32[]{:S(2)}) copy-start(bf16[256,512]{1,0:T(8,128)(2,1)} %copy-done.18) | copy-start | bytes 786436
  142.0 6.6 %copy-start.20 = (bf16[256,512]{1,0:T(8,128)(2,1)S(1)}, bf16[256,512]{1,0:T(8,128)(2,1)}, u32[]{:S(2)}) copy-start(bf16[256,512]{1,0:T(8,128)(2,1)} %get-tuple-element.94.refs_8_) | copy-start | bytes 786436
  142.0 6.6 %copy-start.21 = (bf16[256,512]{1,0:T(8,128)(2,1)S(1)}, bf16[256,512]{1,0:T(8,128)(2,1)}, u32[]{:S(2)}) copy-start(bf16[256,512]{1,0:T(8,128)(2,1)} %get-tuple-element.95.refs_5_) | copy-start | bytes 786436
  142.0 6.6 %copy-start.22 = (bf16[256,512]{1,0:T(8,128)(2,1)S(1)}, bf16[256,512]{1,0:T(8,128)(2,1)}, u32[]{:S(2)}) copy-start(bf16[256,512]{1,0:T(8,128)(2,1)} %get-tuple-element.96.refs_3_) | copy-start | bytes 786436
  142.0 6.6 %copy-start.23 = (bf16[256,512]{1,0:T(8,128)(2,1)S(1)}, bf16[256,512]{1,0:T(8,128)(2,1)}, u32[]{:S(2)}) copy-start(bf16[256,512]{1,0:T(8,128)(2,1)} %get-tuple-element.97.refs_10_) | copy-start | bytes 786436
  146.0 8.7 %collective-permute-start.22 = (bf16[256,512]{1,0:T(8,128)(2,1)S(1)}, bf16[256,512]{1,0:T(8,128)(2,1)S(1)}, u32[]{:S(2)}, u32[]{:S(2)}) collective-permute-start(bf16[256,512]{1,0:T(8,128)(2,1)S(1)} %key_backward.1.refs_2_), channel_id=1, source_target_pairs={{0,1},{1,0},{2,3},{3,2},{4,5},{5,4},{6,7},{7,6},{8,9},{9,8},{10,11... | collective-permute-start | bytes 786440 | tf_op jit(solution)/shard_map/ppermute | solution.py:415
  147.3 10.7 %collective-permute-start.19 = (bf16[256,512]{1,0:T(8,128)(2,1)S(1)}, bf16[256,512]{1,0:T(8,128)(2,1)S(1)}, u32[]{:S(2)}, u32[]{:S(2)}) collective-permute-start(bf16[256,512]{1,0:T(8,128)(2,1)S(1)} %collective-permute-done.18.refs_2_), channel_id=1, source_target_pairs={{0,1},{1,0},{2,3},{3,2},{4,5},{5,4},{6,7},{7,6},{8,9},{9,8},{10,11... | collective-permute-start | bytes 786440 | tf_op jit(solution)/shard_map/ppermute | solution.py:415
  147.3 10.7 %collective-permute-start.21 = (bf16[256,512]{1,0:T(8,128)(2,1)S(1)}, bf16[256,512]{1,0:T(8,128)(2,1)S(1)}, u32[]{:S(2)}, u32[]{:S(2)}) collective-permute-start(bf16[256,512]{1,0:T(8,128)(2,1)S(1)} %collective-permute-done.20.refs_4_), channel_id=1, source_target_pairs={{0,1},{1,0},{2,3},{3,2},{4,5},{5,4},{6,7},{7,6},{8,9},{9,8},{10,11... | collective-permute-start | bytes 786440 | tf_op jit(solution)/shard_map/ppermute | solution.py:415
  148.5 6.1 %collective-permute-start.24 = (bf16[256,512]{1,0:T(8,128)(2,1)S(1)}, bf16[256,512]{1,0:T(8,128)(2,1)S(1)}, u32[]{:S(2)}, u32[]{:S(2)}) collective-permute-start(bf16[256,512]{1,0:T(8,128)(2,1)S(1)} %collective-permute-done.23.refs_4_), channel_id=1, source_target_pairs={{0,1},{1,0},{2,3},{3,2},{4,5},{5,4},{6,7},{7,6},{8,9},{9,8},{10,11... | collective-permute-start | bytes 786440 | tf_op jit(solution)/shard_map/ppermute | solution.py:415
  158.0 11.9 %copy-start.4 = (f32[4,384,128]{2,1,0:T(8,128)S(1)}, f32[4,384,128]{2,1,0:T(8,128)}, u32[]{:S(2)}) copy-start(f32[4,384,128]{2,1,0:T(8,128)} %copy-done.3) | copy-start | bytes 2359300
  158.0 11.9 %copy-start.8 = (f32[4,384,128]{2,1,0:T(8,128)S(1)}, f32[4,384,128]{2,1,0:T(8,128)}, u32[]{:S(2)}) copy-start(f32[4,384,128]{2,1,0:T(8,128)} %copy-done.7) | copy-start | bytes 2359300
  158.0 11.9 %copy-start.10 = (f32[4,384,128]{2,1,0:T(8,128)S(1)}, f32[4,384,128]{2,1,0:T(8,128)}, u32[]{:S(2)}) copy-start(f32[4,384,128]{2,1,0:T(8,128)} %copy-done.9) | copy-start | bytes 2359300
  162.9 1.3 collective-permute-start.25
  164.2 4.5 %collective-permute-start.28 = (f32[8,128]{1,0:T(8,128)S(1)}, f32[8,128]{1,0:T(8,128)S(1)}, u32[]{:S(2)}, u32[]{:S(2)}) collective-permute-start(f32[8,128]{1,0:T(8,128)S(1)} %add.43.refs_0_), channel_id=1, source_target_pairs={{0,6},{1,7},{2,4},{3,5},{4,2},{5,3},{6,0},{7,1},{8,14},{9,15},{10,... | collective-permute-start | bytes 12296 | tf_op jit(solution)/shard_map/ppermute | solution.py:415
  165.7 3.6 %collective-permute-start.27 = (f32[8,128]{1,0:T(8,128)S(1)}, f32[8,128]{1,0:T(8,128)S(1)}, u32[]{:S(2)}, u32[]{:S(2)}) collective-permute-start(f32[8,128]{1,0:T(8,128)S(1)} %add.43.refs_0_), channel_id=1, source_target_pairs={{0,4},{1,5},{2,6},{3,7},{4,0},{5,1},{6,2},{7,3},{8,12},{9,13},{10,... | collective-permute-start | bytes 12296 | tf_op jit(solution)/shard_map/ppermute | solution.py:415
  166.3 3.6 %collective-permute-start.26 = (f32[8,128]{1,0:T(8,128)S(1)}, f32[8,128]{1,0:T(8,128)S(1)}, u32[]{:S(2)}, u32[]{:S(2)}) collective-permute-start(f32[8,128]{1,0:T(8,128)S(1)} %add.43.refs_0_), channel_id=1, source_target_pairs={{0,2},{1,3},{2,0},{3,1},{4,6},{5,7},{6,4},{7,5},{8,10},{9,11},{10,... | collective-permute-start | bytes 12296 | tf_op jit(solution)/shard_map/ppermute | solution.py:415
  171.5 14.3 %collective-permute-start.29 = (bf16[384,128]{1,0:T(8,128)(2,1)S(1)}, bf16[384,128]{1,0:T(8,128)(2,1)S(1)}, u32[]{:S(2)}, u32[]{:S(2)}) collective-permute-start(bf16[384,128]{1,0:T(8,128)(2,1)S(1)} %get-tuple-element.82), channel_id=1, source_target_pairs={{0,8},{8,0},{16,24},{24,16},{1,9},{9,1},{17,25},{25,17},{2,10},{10... | collective-permute-start | bytes 294920 | tf_op jit(solution)/shard_map/ppermute | solution.py:415
  173.6 12.2 %collective-permute-start.30 = (bf16[384,128]{1,0:T(8,128)(2,1)S(1)}, bf16[384,128]{1,0:T(8,128)(2,1)S(1)}, u32[]{:S(2)}, u32[]{:S(2)}) collective-permute-start(bf16[384,128]{1,0:T(8,128)(2,1)S(1)} %get-tuple-element.83), channel_id=1, source_target_pairs={{0,16},{8,24},{16,0},{24,8},{1,17},{9,25},{17,1},{25,9},{2,18},{10... | collective-permute-start | bytes 294920 | tf_op jit(solution)/shard_map/ppermute | solution.py:415
  175.9 9.9 %collective-permute-start.31 = (bf16[384,128]{1,0:T(8,128)(2,1)S(1)}, bf16[384,128]{1,0:T(8,128)(2,1)S(1)}, u32[]{:S(2)}, u32[]{:S(2)}) collective-permute-start(bf16[384,128]{1,0:T(8,128)(2,1)S(1)} %get-tuple-element.84), channel_id=1, source_target_pairs={{0,24},{8,16},{16,8},{24,0},{1,25},{9,17},{17,9},{25,1},{2,26},{10... | collective-permute-start | bytes 294920 | tf_op jit(solution)/shard_map/ppermute | solution.py:415
  176.0 14.3 %copy-start.24 = (f32[384,128]{1,0:T(8,128)S(1)}, f32[384,128]{1,0:T(8,128)}, u32[]{:S(2)}) copy-start(f32[384,128]{1,0:T(8,128)} %reduce_sum.9) | copy-start | bytes 589828
  185.9 14.2 %collective-permute-start.34 = (bf16[384,128]{1,0:T(8,128)(2,1)S(1)}, bf16[384,128]{1,0:T(8,128)(2,1)S(1)}, u32[]{:S(2)}, u32[]{:S(2)}) collective-permute-start(bf16[384,128]{1,0:T(8,128)(2,1)S(1)} %convert_element_type.24.refs_7_), channel_id=1, source_target_pairs={{0,24},{8,16},{16,8},{24,0},{1,25},{9,17},{17,9},{25,1},{2,26},{10... | collective-permute-start | bytes 294920 | tf_op jit(solution)/shard_map/ppermute | solution.py:415
  189.7 10.4 %collective-permute-start.33 = (bf16[384,128]{1,0:T(8,128)(2,1)S(1)}, bf16[384,128]{1,0:T(8,128)(2,1)S(1)}, u32[]{:S(2)}, u32[]{:S(2)}) collective-permute-start(bf16[384,128]{1,0:T(8,128)(2,1)S(1)} %convert_element_type.24.refs_7_), channel_id=1, source_target_pairs={{0,16},{8,24},{16,0},{24,8},{1,17},{9,25},{17,1},{25,9},{2,18},{10... | collective-permute-start | bytes 294920 | tf_op jit(solution)/shard_map/ppermute | solution.py:415
  189.7 10.4 %collective-permute-start.32 = (bf16[384,128]{1,0:T(8,128)(2,1)S(1)}, bf16[384,128]{1,0:T(8,128)(2,1)S(1)}, u32[]{:S(2)}, u32[]{:S(2)}) collective-permute-start(bf16[384,128]{1,0:T(8,128)(2,1)S(1)} %convert_element_type.24.refs_7_), channel_id=1, source_target_pairs={{0,8},{8,0},{16,24},{24,16},{1,9},{9,1},{17,25},{25,17},{2,10},{10... | collective-permute-start | bytes 294920 | tf_op jit(solution)/shard_map/ppermute | solution.py:415

commit v6 on v5

--- a/solution.py
+++ b/solution.py
@@ -153,7 +153,7 @@
     )(*parts, incoming)
 
 
-def grad_kernel(counts, has_base, last, *refs):
+def grad_kernel(counts, has_base, has_more, last, *refs):
     refs = list(refs)
     place_ref = refs.pop(0)
     terms = []
@@ -161,7 +161,7 @@
         terms.append((refs.pop(0), refs[:count]))
         del refs[:count]
     base = refs.pop(0) if has_base else None
-    square_in, due_in = (refs.pop(0), refs.pop(0)) if last and has_base else (None, None)
+    square_in, due_in = (refs.pop(0), refs.pop(0)) if has_more else (None, None)
     out_ref = refs.pop(0)
     sq_ref, due_ref = (refs.pop(0), refs.pop(0)) if last else (None, None)
     joined = refs
@@ -173,7 +173,7 @@
             for j, block in enumerate(blocks):
                 held[j * depth:(j + 1) * depth, :] = block[...]
         if last:
-            sq_ref[...] = square_in[...] if has_base else jnp.zeros_like(sq_ref)
+            sq_ref[...] = square_in[...] if has_more else jnp.zeros_like(sq_ref)
 
     total = base[...] if has_base else None
     for (x_ref, _), held in zip(terms, joined):
@@ -188,10 +188,10 @@
             folded = folded + squares[:, h * HEAD:(h + 1) * HEAD]
         sq_ref[...] += folded
         heads = width // FRAG_COLS
-        mine = place_ref[0] - (0 if has_base else heads)
+        mine = place_ref[0] - (0 if has_more else heads)
         mine = jnp.minimum(jnp.maximum(mine, 0), heads - 1) * FRAG_COLS
         column = out_ref[:, pl.ds(pl.multiple_of(mine, FRAG_COLS), FRAG_COLS)]
-        if has_base:
+        if has_more:
             column = jnp.where(place_ref[0] < heads, column, due_in[...])
         due_ref[...] = column
 
@@ -211,9 +211,9 @@
     if base is not None:
         args.append(base)
         specs.append(row_block(width))
-        if last:
-            args += [square, due]
-            specs += [fixed, row_block(FRAG_COLS)]
+    if square is not None:
+        args += [square, due]
+        specs += [fixed, row_block(FRAG_COLS)]
     if last:
         shapes = [
             pltpu.HBM((rows, width), jnp.float32),
@@ -226,7 +226,7 @@
         outs = [row_block(width)]
     depth = sum(x.shape[1] for x, _ in terms)
     return pl.pallas_call(
-        functools.partial(grad_kernel, [len(b) for _, b in terms], base is not None, last),
+        functools.partial(grad_kernel, [len(b) for _, b in terms], base is not None, square is not None, last),
         out_shape=shapes,
         grid_spec=pltpu.PrefetchScalarGridSpec(
             num_scalar_prefetch=1,
@@ -338,7 +338,7 @@
     at = (lambda j, p: (p[1] ^ j, p[0])) if blocks > 1 else (lambda j, p: (0, p[0]))
     return pl.pallas_call(
         pick_kernel,
-        out_shape=[jax.ShapeDtypeStruct((blocks, part, FRAG_COLS), a.dtype) for a in arrays],
+        out_shape=[pltpu.HBM((blocks, part, FRAG_COLS), a.dtype) for a in arrays],
         grid_spec=pltpu.PrefetchScalarGridSpec(
             num_scalar_prefetch=1,
             grid=(blocks,),
@@ -465,16 +465,17 @@
 
     groups = [[k] for k in far if bin(k).count("1") > 1]
     groups += [[k for k in far if bin(k).count("1") == 1]]
-    blocks = {0: pack(inputs, me, 0, rows)}
+    blocks, packed = {0: pack(inputs, me, 0, rows)}, {}
     for group in groups:
         for odd in range(2):
             for k in group:
-                blocks[k + odd] = line.swap(pack(inputs, me, k + odd, rows), k + odd)
-    early = blocks[far[0]]
+                packed[k + odd] = pack(inputs, me, k + odd, rows)
+                blocks[k + odd] = line.swap(packed[k + odd], k + odd)
+    early = packed[far[0] + 1]
     blocks[1] = swap(pack(inputs, after(me, early), 1, rows), "fsdp", 1)
-    value_list = [values[k] for k in range(0, shards, 2)]
-    crossed = swap(after(jnp.stack(value_list), early), "fsdp", 1)
-    value_list = [v for m in range(shards // 2) for v in (value_list[m], crossed[m])]
+    crossed = swap(jnp.stack([values[k] for k in range(0, shards, 2)]), "fsdp", 1)
+    for k in range(0, shards, 2):
+        values[k + 1] = crossed[k // 2]
 
     def to_all(pieces):
         return lax.all_to_all(pieces, "rep", 0, 0, tiled=True)
@@ -499,30 +500,36 @@
     anchor_copy, momentum_copy = duplicate(anchor), duplicate(momentum)
     key_weights = cast_left(after(params, early), kv_width)
 
+    spread = [0, 1] + [k + odd for k in far for odd in range(2)]
+    near, rest = spread[:shards // 2], spread[shards // 2:]
+    flipped = transpose_tokens([blocks[k] for k in near])
+    (values_first,) = gradient(place, [(flipped, [values[k] for k in near])], last=False)
+
     last = far[-1]
     blocks[last + 1] = after(
-        blocks[last + 1], base[-1], anchor_copy, momentum_copy, old_second, scalars, value_list[-1]
+        blocks[last + 1], base[-1], anchor_copy, momentum_copy, old_second, scalars, values_first
     )
     parts = []
     for k in far + [0]:
         theirs = swap(partial_keys(blocks[k + 1], key_weights), "fsdp", 1)
         part_k = partial_keys(blocks[k], key_weights, theirs)
         parts.append(line.swap(part_k, k) if k else part_k)
+    flipped_rest = transpose_tokens([blocks[k] for k in rest])
+    parts[-1] = after(parts[-1], flipped_rest)
     back = key_backward(parts, incoming)
-    keys = []
-    for held in [back] + [line.swap(back, k) for k in chips]:
-        keys += [held, swap(held, "fsdp", 1)]
-
-    cut = shards // 2
-    flipped = [
-        transpose_tokens([blocks[k] for k in range(cut)]),
-        transpose_tokens([blocks[k] for k in range(cut, shards)]),
-    ]
+    keys = {0: back}
+    for k in far:
+        keys[k] = line.swap(back, k)
+    for k in range(0, shards, 2):
+        keys[k + 1] = swap(keys[k], "fsdp", 1)
+
     grad_values, square, due = gradient(
-        place, [(flipped[0], value_list[:cut]), (flipped[1], value_list[cut:])]
-    )
-    (grad_first,) = gradient(place, [(flipped[0], keys[:cut])], last=False)
-    grad_keys, square, due = gradient(place, [(flipped[1], keys[cut:])], grad_first, square, due)
+        place, [(flipped_rest, [values[k] for k in rest])], values_first
+    )
+    (grad_first,) = gradient(place, [(flipped, [keys[k] for k in near])], last=False)
+    grad_keys, square, due = gradient(
+        place, [(flipped_rest, [keys[k] for k in rest])], grad_first, square, due
+    )
 
     square = square + swap(square, "fsdp", 1)
     squares = [square] + [swap(square, "fsdp", k) for k in chips]

time: 205 us -> 199 us (0.971)
  waiting for transfers between devices: 56.2 us -> 43.6 us
  Pallas kernels: 86.1 us -> 91 us
    ppermute x35, waiting for transfers between devices: 56.2 us -> 43.6 us  [swap(): return lax.ppermute(block, axis, [(i, i ^ offset) for i in range(count)])]
    pallas_call x2, Pallas kernels: 4.73 us -> 6.91 us  [due_columns(): pl.pallas_call(pick_kernel, out_shape=[pltpu.HBM((blocks, part, FRAG_COLS...]
    pallas_call x3 -> x4, Pallas kernels: 14.3 us -> 16.4 us  [gradient(): pl.pallas_call(functools.partial(grad_kernel, [len(b) for _, b in terms],...]
  transfers between devices with their start and end apart: 37 -> 37, of which waited for: 12 -> 13; matrix products, arithmetic and copies ran while one was open for 4% -> 4% of each run, Pallas kernels for 36% -> 38%
where the time goes in v6:
time: 199 us; the launch traced here: 197 us
  Pallas kernels  91 us (46%)
  starting transfers between devices  45.2 us (23%)
  waiting for transfers between devices  43.6 us (22%)
  local copies, waits for them, and re-layouts  8.28 us (4%)
  other arithmetic  5.33 us (3%)
  between operations  3.84 us (2%)
    ppermute x35, waiting for transfers between devices, swap(): return lax.ppermute(block, axis, [(i, i ^ offset) for i in range(count)])  43.6 us
    ppermute x35, starting transfers between devices, swap(): return lax.ppermute(block, axis, [(i, i ^ offset) for i in range(count)])  34 us
    pallas_call x2, Pallas kernels, adam_rows(): pl.pallas_call(functools.partial(adam_kernel, len(squares), len(into)), o...  19.6 us
    pallas_call x4, Pallas kernels, gradient(): pl.pallas_call(functools.partial(grad_kernel, [len(b) for _, b in terms],...  16.4 us
    pallas_call x8, Pallas kernels, pack(): pl.pallas_call(pack_kernel, out_shape=jax.ShapeDtypeStruct((count, rows),...  13 us
    pallas_call x8, Pallas kernels, partial_keys(): pl.pallas_call(partial_kernel, out_shape=jax.ShapeDtypeStruct((count, wid...  12 us
    all_to_all x2, starting transfers between devices, to_all(): return lax.all_to_all(pieces, 'rep', 0, 0, tiled=True)  11.1 us
    pallas_call x2, Pallas kernels, transpose_tokens(): pl.pallas_call(transpose_kernel, out_shape=jax.ShapeDtypeStruct((rows, le...  8.04 us
  transfers between devices with their start and end apart: 37, of which 13 were waited for; matrix products, arithmetic and copies ran while one was open for 4% of the time, Pallas kernels for 38%

profile of v6, /device:TPU:0, one launch (start us, length us, event | category | flops | bytes accessed | tf_op | source)
XLA Modules:
  0.0 197.3 jit_solution(184896776318244898)
XLA Ops:
  1.4 1.2 pack.13
  2.6 4.6 %due_columns.3 = (f32[4,384,128]{2,1,0:T(8,128)}, f32[4,384,128]{2,1,0:T(8,128)}, f32[4,384,128]{2,1,0:T(8,128)}) custom-call(s32[2]{0:T(128)S(1)} %pad_add_fusion.place_ref.refs_0_, f32[1536,1024]{1,0:T(8,128)} %bitcast.55, f32[1536,1024]{1,0:T(8,128)} %bitcast.59, f32[1536,1024]{1,0:T(8,128)} %bitcast.62), custom_call_target="tpu_custom_call" | custom-call | bytes 4718592 | tf_op jit(solution)/shard_map/due_columns/pallas_call | solution.py:339
  7.1 1.3 constant_dynamic-slice_fusion.3
  9.4 6.3 %all-to-all-start = ((f32[4,384,128]{2,1,0:T(8,128)}), f32[4,384,128]{2,1,0:T(8,128)}, u32[]{:S(2)}, u32[]{:S(2)}) async-start(f32[4,384,128]{2,1,0:T(8,128)} %pad_maximum_fusion.1), calls=%async_computation | async-start | bytes 1572864 | tf_op jit(solution)/shard_map/all_to_all | solution.py:481
  15.8 1.6 collective-permute-start.6
  17.3 1.5 collective-permute-start.4
  19.3 1.2 pack.10
  20.5 2.5 %collective-permute-start.2 = (bf16[256,1536]{1,0:T(8,128)(2,1)S(1)}, bf16[256,1536]{1,0:T(8,128)(2,1)S(1)}, u32[]{:S(2)}, u32[]{:S(2)}) collective-permute-start(bf16[256,1536]{1,0:T(8,128)(2,1)S(1)} %pack.10), channel_id=1, source_target_pairs={{0,6},{1,7},{2,4},{3,5},{4,2},{5,3},{6,0},{7,1},{8,14},{9,15},{10,... | collective-permute-start | bytes 2359304 | tf_op jit(solution)/shard_map/ppermute | solution.py:415
  23.0 2.0 %collective-permute-done.6.refs_2_ = bf16[256,512]{1,0:T(8,128)(2,1)S(1)} collective-permute-done((bf16[256,512]{1,0:T(8,128)(2,1)S(1)}, bf16[256,512]{1,0:T(8,128)(2,1)S(1)}, u32[]{:S(2)}, u32[]{:S(2)}) %collective-permute-start.6) | collective-permute-done | bytes 262176 | tf_op jit(solution)/shard_map/ppermute | solution.py:415
  25.1 6.7 %collective-permute-done.4.refs_4_ = bf16[256,512]{1,0:T(8,128)(2,1)S(1)} collective-permute-done((bf16[256,512]{1,0:T(8,128)(2,1)S(1)}, bf16[256,512]{1,0:T(8,128)(2,1)S(1)}, u32[]{:S(2)}, u32[]{:S(2)}) %collective-permute-start.4) | collective-permute-done | bytes 262176 | tf_op jit(solution)/shard_map/ppermute | solution.py:415
  31.8 16.8 %collective-permute-done.refs_4_ = bf16[256,512]{1,0:T(8,128)(2,1)S(1)} collective-permute-done((bf16[256,512]{1,0:T(8,128)(2,1)S(1)}, bf16[256,512]{1,0:T(8,128)(2,1)S(1)}, u32[]{:S(2)}, u32[]{:S(2)}) %collective-permute-start) | collective-permute-done | bytes 262176 | tf_op jit(solution)/shard_map/ppermute | solution.py:415
  48.5 1.1 pad_maximum_fusion
  49.6 1.5 collective-permute-start.7
  51.2 2.1 %pack.15 = bf16[256,1536]{1,0:T(8,128)(2,1)} custom-call(s32[1]{0:T(128)} %bitcast.4.me_ref, bf16[256,12288]{1,0:T(8,128)(2,1)} %bitcast.49), custom_call_target="tpu_custom_call" | custom-call | bytes 1572864 | tf_op jit(solution)/shard_map/pack/pallas_call | solution.py:51
  53.3 2.3 %due_columns.2 = (f32[1,384,128]{2,1,0:T(8,128)}, f32[1,384,128]{2,1,0:T(8,128)}) custom-call(s32[2]{0:T(128)S(1)} %pad_add_fusion.place_ref.refs_0_, f32[384,1024]{1,0:T(8,128)} %src_ref.2, f32[384,1024]{1,0:T(8,128)} %src_ref.3), custom_call_target="tpu_custom_call" | custom-call | bytes 786432 | tf_op jit(solution)/shard_map/due_columns/pallas_call | solution.py:339
  55.7 1.9 reduce_sum.9
  57.5 1.2 subtract_bitcast_fusion
  59.6 4.8 %all-to-all-start.1 = ((f32[4,384,128]{2,1,0:T(8,128)}), f32[4,384,128]{2,1,0:T(8,128)}, u32[]{:S(2)}, u32[]{:S(2)}) async-start(f32[4,384,128]{2,1,0:T(8,128)} %broadcast_in_dim.18), calls=%async_computation.1 | async-start | bytes 1572864 | tf_op jit(solution)/shard_map/all_to_all | solution.py:481
  64.4 1.2 pack.9
  66.1 2.1 %pack.12 = bf16[256,1536]{1,0:T(8,128)(2,1)} custom-call(s32[1]{0:T(128)} %bitcast.4.me_ref, bf16[256,12288]{1,0:T(8,128)(2,1)} %bitcast.51), custom_call_target="tpu_custom_call" | custom-call | bytes 1572864 | tf_op jit(solution)/shard_map/pack/pallas_call | solution.py:51
  68.1 1.6 collective-permute-done.7.refs_3_.x_ref
  69.7 1.2 collective-permute-start.8
  70.9 1.2 pack.14.refs_0_.x_ref
  72.1 2.1 %pack.11 = bf16[256,1536]{1,0:T(8,128)(2,1)} custom-call(s32[1]{0:T(128)} %bitcast.4.me_ref, bf16[256,12288]{1,0:T(8,128)(2,1)} %bitcast.53), custom_call_target="tpu_custom_call" | custom-call | bytes 1572864 | tf_op jit(solution)/shard_map/pack/pallas_call | solution.py:51
  74.2 2.1 %pack.8 = bf16[256,1536]{1,0:T(8,128)(2,1)} custom-call(s32[1]{0:T(128)} %bitcast.4.me_ref, bf16[256,12288]{1,0:T(8,128)(2,1)} %bitcast.54), custom_call_target="tpu_custom_call" | custom-call | bytes 1572864 | tf_op jit(solution)/shard_map/pack/pallas_call | solution.py:51
  76.3 3.6 %duplicate.2.refs_1_ = f32[384,1024]{1,0:T(8,128)} custom-call(f32[384,1024]{1,0:T(8,128)} %src_ref.2), custom_call_target="tpu_custom_call" | custom-call | bytes 3145728 | tf_op jit(solution)/shard_map/duplicate/pallas_call | solution.py:358
  79.9 3.6 %duplicate.3.refs_2_ = f32[384,1024]{1,0:T(8,128)} custom-call(f32[384,1024]{1,0:T(8,128)} %src_ref.3), custom_call_target="tpu_custom_call" | custom-call | bytes 3145728 | tf_op jit(solution)/shard_map/duplicate/pallas_call | solution.py:358
  84.3 3.5 %cast_left.1.w_ref = bf16[1536,512]{1,0:T(8,128)(2,1)S(1)} custom-call(f32[1536,1024]{1,0:T(8,128)} %bitcast.56), custom_call_target="tpu_custom_call" | custom-call | bytes 4718592 | tf_op jit(solution)/shard_map/cast_left/pallas_call | solution.py:95
  88.0 1.9 collective-permute-start.1
  89.9 1.5 collective-permute-start.5
  91.4 3.6 %transpose_tokens.2.refs_1_ = bf16[1536,1024]{1,0:T(8,128)(2,1)S(1)} custom-call(bf16[256,1536]{1,0:T(8,128)(2,1)S(1)} %pack.14.refs_0_.x_ref, bf16[256,1536]{1,0:T(8,128)(2,1)} %collective-permute-done.9.refs_1_.x_ref, bf16[256,1536]{1,0:T(8,128)(2,1)S(1)} %collective-permute-done.2.refs_2_.x_ref, bf16[256,1536]{1,0:T(8,128)(2,1)S(1)} %copy-done.7), custom_call_target="tpu_custom_call" | custom-call | bytes 6291456 | tf_op jit(solution)/shard_map/transpose_tokens/pallas_call | solution.py:76
  95.0 1.7 partial_keys.8
  96.8 2.0 %slice_bitcast_fusion = (bf16[256,512]{1,0:T(8,128)(2,1)}, bf16[256,512]{1,0:T(8,128)(2,1)}, bf16[256,512]{1,0:T(8,128)(2,1)S(1)}, bf16[256,512]{1,0:T(8,128)(2,1)S(1)}) fusion(bf16[4,256,512]{2,1,0:T(8,128)(2,1)} %collective-permute-done.10), kind=kLoop, calls=%fused_computation.2 | loop fusion | bytes 2097152 | tf_op jit(solution)/shard_map/squeeze | solution.py:478
  98.8 3.3 %gradient.4.refs_6_ = f32[1536,512]{1,0:T(8,128)S(1)} custom-call(s32[2]{0:T(128)S(1)} %pad_add_fusion.place_ref.refs_0_, bf16[1536,1024]{1,0:T(8,128)(2,1)S(1)} %transpose_tokens.2.refs_1_, bf16[256,512]{1,0:T(8,128)(2,1)S(1)} %get-tuple-element.107.refs_2_, bf16[256,512]{1,0:T(8,128)(2,1)S(1)} %get-tuple-element.97.refs_3_, ...), custom_call_target="tpu_custom_call" | custom-call | flops 1610612736 | bytes 6291456 | tf_op jit(solution)/shard_map/gradient/pallas_call | solution.py:228
  102.2 1.7 copy-done.2
  103.8 1.3 partial_keys.10
  106.5 1.3 dynamic-slice_bitcast_fusion
  107.8 1.7 partial_keys.12
  109.6 1.7 partial_keys.14
  111.9 1.5 partial_keys.9
  113.6 1.8 partial_keys.11
  115.3 2.0 collective-permute-start.14
  117.3 1.7 partial_keys.13
  119.0 1.6 collective-permute-start.16
  121.3 4.4 %transpose_tokens.3.refs_1_ = bf16[1536,1024]{1,0:T(8,128)(2,1)S(1)} custom-call(bf16[256,1536]{1,0:T(8,128)(2,1)} %collective-permute-done.1.refs_0_.x_ref, bf16[256,1536]{1,0:T(8,128)(2,1)S(1)} %copy-done.5, bf16[256,1536]{1,0:T(8,128)(2,1)} %collective-permute-done.5.refs_2_.x_ref, bf16[256,1536]{1,0:T(8,128)(2,1)} %collective-permute-done.8.refs_3_.x_ref), custom_call_target="tpu_custom_call" | custom-call | bytes 6291456 | tf_op jit(solution)/shard_map/transpose_tokens/pallas_call | solution.py:76
  125.7 1.6 collective-permute-done.14.refs_1_
  129.4 1.7 collective-permute-start.18
  131.0 1.3 collective-permute-start.20
  132.3 6.7 %collective-permute-done.23.refs_4_ = bf16[256,512]{1,0:T(8,128)(2,1)S(1)} collective-permute-done((bf16[256,512]{1,0:T(8,128)(2,1)S(1)}, bf16[256,512]{1,0:T(8,128)(2,1)S(1)}, u32[]{:S(2)}, u32[]{:S(2)}) %collective-permute-start.23) | collective-permute-done | bytes 262176 | tf_op jit(solution)/shard_map/ppermute | solution.py:415
  139.0 3.1 %collective-permute-done.18.refs_2_ = bf16[256,512]{1,0:T(8,128)(2,1)S(1)} collective-permute-done((bf16[256,512]{1,0:T(8,128)(2,1)S(1)}, bf16[256,512]{1,0:T(8,128)(2,1)S(1)}, u32[]{:S(2)}, u32[]{:S(2)}) %collective-permute-start.18) | collective-permute-done | bytes 262176 | tf_op jit(solution)/shard_map/ppermute | solution.py:415
  143.2 4.9 %gradient.6 = (f32[1536,512]{1,0:T(8,128)}, f32[8,128]{1,0:T(8,128)S(1)}, f32[1536,128]{1,0:T(8,128)S(1)}) custom-call(s32[2]{0:T(128)S(1)} %pad_add_fusion.place_ref.refs_0_, bf16[1536,1024]{1,0:T(8,128)(2,1)S(1)} %transpose_tokens.3.refs_1_, bf16[256,512]{1,0:T(8,128)(2,1)S(1)} %copy-done.13, bf16[256,512]{1,0:T(8,128)(2,1)S(1)} %copy-done.17, ...), custom_call_target="tpu_custom_call" | custom-call | flops 1610612736 | bytes 6291456 | tf_op jit(solution)/shard_map/gradient/pallas_call | solution.py:228
  148.1 3.3 %gradient.5.refs_6_ = f32[1536,512]{1,0:T(8,128)S(1)} custom-call(s32[2]{0:T(128)S(1)} %pad_add_fusion.place_ref.refs_0_, bf16[1536,1024]{1,0:T(8,128)(2,1)S(1)} %copy-done.1, bf16[256,512]{1,0:T(8,128)(2,1)S(1)} %key_backward.1.refs_2_, bf16[256,512]{1,0:T(8,128)(2,1)S(1)} %collective-permute-done.22.refs_3_, ...), custom_call_target="tpu_custom_call" | custom-call | flops 1610612736 | bytes 6291456 | tf_op jit(solution)/shard_map/gradient/pallas_call | solution.py:228
  151.4 4.9 %gradient.7 = (f32[1536,512]{1,0:T(8,128)}, f32[8,128]{1,0:T(8,128)S(1)}, f32[1536,128]{1,0:T(8,128)S(1)}) custom-call(s32[2]{0:T(128)S(1)} %pad_add_fusion.place_ref.refs_0_, bf16[1536,1024]{1,0:T(8,128)(2,1)S(1)} %transpose_tokens.3.refs_1_, bf16[256,512]{1,0:T(8,128)(2,1)S(1)} %collective-permute-done.18.refs_2_, ...), custom_call_target="tpu_custom_call" | custom-call | flops 1610612736 | bytes 6291456 | tf_op jit(solution)/shard_map/gradient/pallas_call | solution.py:228
  157.7 1.2 collective-permute-start.28
  158.9 1.1 collective-permute-start.27
  159.9 1.2 collective-permute-start.26
  162.5 1.1 collective-permute-done.26.refs_1_
  163.6 1.5 adam_frag.1
  166.0 2.8 %collective-permute-start.30 = (bf16[384,128]{1,0:T(8,128)(2,1)S(1)}, bf16[384,128]{1,0:T(8,128)(2,1)S(1)}, u32[]{:S(2)}, u32[]{:S(2)}) collective-permute-start(bf16[384,128]{1,0:T(8,128)(2,1)S(1)} %get-tuple-element.83), channel_id=1, source_target_pairs={{0,16},{8,24},{16,0},{24,8},{1,17},{9,25},{17,1},{25,9},{2,18},{10... | collective-permute-start | bytes 294920 | tf_op jit(solution)/shard_map/ppermute | solution.py:415
  169.6 9.8 %adam_rows.2 = (f32[1536,1024]{1,0:T(8,128)}, f32[1536,1024]{1,0:T(8,128)}, f32[1536,1024]{1,0:T(8,128)}, f32[8,128]{1,0:T(8,128)S(1)}) custom-call(f32[3]{0:T(128)S(1)} %pad_maximum_fusion.2.sc_ref, f32[1536,1024]{1,0:T(8,128)} %bitcast.57, f32[1536,1024]{1,0:T(8,128)} %bitcast.60, f32[1536,1024]{1,0:T(8,128)} %bitcast.63, ...), custom_call_target="tpu_custom_call" | custom-call | flops 15728640 | bytes 22020096 | tf_op jit(solution)/shard_map/adam_rows/pallas_call | solution.py:287
  179.5 3.2 %collective-permute-start.34 = (bf16[384,128]{1,0:T(8,128)(2,1)S(1)}, bf16[384,128]{1,0:T(8,128)(2,1)S(1)}, u32[]{:S(2)}, u32[]{:S(2)}) collective-permute-start(bf16[384,128]{1,0:T(8,128)(2,1)S(1)} %convert_element_type.24.refs_7_), channel_id=1, source_target_pairs={{0,24},{8,16},{16,8},{24,0},{1,25},{9,17},{17,9},{25,1},{2,26},{10... | collective-permute-start | bytes 294920 | tf_op jit(solution)/shard_map/ppermute | solution.py:415
  182.6 1.3 collective-permute-start.32
  184.0 9.8 %adam_rows.3 = (f32[1536,1024]{1,0:T(8,128)}, f32[1536,1024]{1,0:T(8,128)}, f32[1536,1024]{1,0:T(8,128)}) custom-call(f32[3]{0:T(128)S(1)} %pad_maximum_fusion.2.sc_ref, f32[1536,1024]{1,0:T(8,128)} %bitcast.58, f32[1536,1024]{1,0:T(8,128)} %bitcast.61, f32[1536,1024]{1,0:T(8,128)} %bitcast.64, ...), custom_call_target="tpu_custom_call", output_to_operand_aliasing={{0}: (10, {}), {1}: (11, {}), {2}: (12, {})} | custom-call | flops 15728640 | bytes 22020096 | tf_op jit(solution)/shard_map/adam_rows/pallas_call | solution.py:287
  193.8 2.4 %outer_step.1 = (f32[1536,1024]{1,0:T(8,128)}, f32[384,1024]{1,0:T(8,128)}, f32[384,1024]{1,0:T(8,128)}) custom-call(s32[2]{0:T(128)S(1)} %pad_add_fusion.place_ref.refs_0_, f32[1536,1024]{1,0:T(8,128)} %get-tuple-element.78.refs_0_, f32[384,1024]{1,0:T(8,128)} %duplicate.2.refs_1_, ...), custom_call_target="tpu_custom_call", output_to_operand_aliasing={{0}: (1, {}), {1}: (2, {}), {2}: (3, {})} | custom-call | flops 1966080 | bytes 3932160 | tf_op jit(solution)/shard_map/outer_step/pallas_call | solution.py:397
  (105 shorter events, 13.5 us)
Async XLA Ops:
  7.1 8.6 %copy-start.10 = (bf16[1,256,1024]{2,1,0:T(8,128)(2,1)S(1)}, bf16[1,256,1024]{2,1,0:T(8,128)(2,1)}, u32[]{:S(2)}) copy-start(bf16[1,256,1024]{2,1,0:T(8,128)(2,1)} %param.10) | copy-start | bytes 1572868
  9.4 46.2 %all-to-all-start = ((f32[4,384,128]{2,1,0:T(8,128)}), f32[4,384,128]{2,1,0:T(8,128)}, u32[]{:S(2)}, u32[]{:S(2)}) async-start(f32[4,384,128]{2,1,0:T(8,128)} %pad_maximum_fusion.1), calls=%async_computation | async-start | bytes 1572864 | tf_op jit(solution)/shard_map/all_to_all | solution.py:481
  15.8 9.3 %collective-permute-start.6 = (bf16[256,512]{1,0:T(8,128)(2,1)S(1)}, bf16[256,512]{1,0:T(8,128)(2,1)S(1)}, u32[]{:S(2)}, u32[]{:S(2)}) collective-permute-start(bf16[256,512]{1,0:T(8,128)(2,1)S(1)} %get-tuple-element.107.refs_2_), channel_id=1, source_target_pairs={{0,2},{1,3},{2,0},{3,1},{4,6},{5,7},{6,4},{7,5},{8,10},{9,11},{10,... | collective-permute-start | bytes 786440 | tf_op jit(solution)/shard_map/ppermute | solution.py:415
  17.3 14.4 %collective-permute-start.4 = (bf16[256,512]{1,0:T(8,128)(2,1)S(1)}, bf16[256,512]{1,0:T(8,128)(2,1)S(1)}, u32[]{:S(2)}, u32[]{:S(2)}) collective-permute-start(bf16[256,512]{1,0:T(8,128)(2,1)S(1)} %get-tuple-element.107.refs_2_), channel_id=1, source_target_pairs={{0,6},{1,7},{2,4},{3,5},{4,2},{5,3},{6,0},{7,1},{8,14},{9,15},{10,... | collective-permute-start | bytes 786440 | tf_op jit(solution)/shard_map/ppermute | solution.py:415
  18.8 29.7 %collective-permute-start = (bf16[256,512]{1,0:T(8,128)(2,1)S(1)}, bf16[256,512]{1,0:T(8,128)(2,1)S(1)}, u32[]{:S(2)}, u32[]{:S(2)}) collective-permute-start(bf16[256,512]{1,0:T(8,128)(2,1)S(1)} %get-tuple-element.107.refs_2_), channel_id=1, source_target_pairs={{0,4},{1,5},{2,6},{3,7},{4,0},{5,1},{6,2},{7,3},{8,12},{9,13},{10,... | collective-permute-start | bytes 786440 | tf_op jit(solution)/shard_map/ppermute | solution.py:415
  20.5 45.1 %collective-permute-start.2 = (bf16[256,1536]{1,0:T(8,128)(2,1)S(1)}, bf16[256,1536]{1,0:T(8,128)(2,1)S(1)}, u32[]{:S(2)}, u32[]{:S(2)}) collective-permute-start(bf16[256,1536]{1,0:T(8,128)(2,1)S(1)} %pack.10), channel_id=1, source_target_pairs={{0,6},{1,7},{2,4},{3,5},{4,2},{5,3},{6,0},{7,1},{8,14},{9,15},{10,... | collective-permute-start | bytes 2359304 | tf_op jit(solution)/shard_map/ppermute | solution.py:415
  25.1 28.1 %copy-start.12 = (bf16[256,512]{1,0:T(8,128)(2,1)}, bf16[256,512]{1,0:T(8,128)(2,1)S(1)}, u32[]{:S(2)}) copy-start(bf16[256,512]{1,0:T(8,128)(2,1)S(1)} %collective-permute-done.6.refs_2_) | copy-start | bytes 786436
  31.7 21.5 %copy-start.18 = (bf16[256,512]{1,0:T(8,128)(2,1)}, bf16[256,512]{1,0:T(8,128)(2,1)S(1)}, u32[]{:S(2)}) copy-start(bf16[256,512]{1,0:T(8,128)(2,1)S(1)} %collective-permute-done.4.refs_4_) | copy-start | bytes 786436
  48.5 4.7 %copy-start.14 = (bf16[256,512]{1,0:T(8,128)(2,1)}, bf16[256,512]{1,0:T(8,128)(2,1)S(1)}, u32[]{:S(2)}) copy-start(bf16[256,512]{1,0:T(8,128)(2,1)S(1)} %collective-permute-done.refs_4_) | copy-start | bytes 786436
  49.6 47.2 %collective-permute-start.10 = (bf16[4,256,512]{2,1,0:T(8,128)(2,1)}, bf16[4,256,512]{2,1,0:T(8,128)(2,1)}, u32[]{:S(2)}, u32[]{:S(2)}) collective-permute-start(bf16[4,256,512]{2,1,0:T(8,128)(2,1)} %pad_maximum_fusion), channel_id=1, source_target_pairs={{0,1},{1,0},{2,3},{3,2},{4,5},{5,4},{6,7},{7,6},{8,9},{9,8},{10,11... | collective-permute-start | bytes 3145736 | tf_op jit(solution)/shard_map/ppermute | solution.py:415
  49.6 20.1 %collective-permute-start.7 = (bf16[256,1536]{1,0:T(8,128)(2,1)S(1)}, bf16[256,1536]{1,0:T(8,128)(2,1)S(1)}, u32[]{:S(2)}, u32[]{:S(2)}) collective-permute-start(bf16[256,1536]{1,0:T(8,128)(2,1)S(1)} %pack.13), channel_id=1, source_target_pairs={{0,7},{1,6},{2,5},{3,4},{4,3},{5,2},{6,1},{7,0},{8,15},{9,14},{10,... | collective-permute-start | bytes 2359304 | tf_op jit(solution)/shard_map/ppermute | solution.py:415
  53.2 36.6 %collective-permute-start.9 = (bf16[256,1536]{1,0:T(8,128)(2,1)}, bf16[256,1536]{1,0:T(8,128)(2,1)}, u32[]{:S(2)}, u32[]{:S(2)}) collective-permute-start(bf16[256,1536]{1,0:T(8,128)(2,1)} %pack.15), channel_id=1, source_target_pairs={{0,1},{1,0},{2,3},{3,2},{4,5},{5,4},{6,7},{7,6},{8,9},{9,8},{10,11... | collective-permute-start | bytes 2359304 | tf_op jit(solution)/shard_map/ppermute | solution.py:415
  59.6 46.9 %all-to-all-start.1 = ((f32[4,384,128]{2,1,0:T(8,128)}), f32[4,384,128]{2,1,0:T(8,128)}, u32[]{:S(2)}, u32[]{:S(2)}) async-start(f32[4,384,128]{2,1,0:T(8,128)} %broadcast_in_dim.18), calls=%async_computation.1 | async-start | bytes 1572864 | tf_op jit(solution)/shard_map/all_to_all | solution.py:481
  65.6 38.2 %collective-permute-start.3 = (bf16[256,1536]{1,0:T(8,128)(2,1)S(1)}, bf16[256,1536]{1,0:T(8,128)(2,1)S(1)}, u32[]{:S(2)}, u32[]{:S(2)}) collective-permute-start(bf16[256,1536]{1,0:T(8,128)(2,1)S(1)} %pack.9), channel_id=1, source_target_pairs={{0,3},{1,2},{2,1},{3,0},{4,7},{5,6},{6,5},{7,4},{8,11},{9,10},{10,... | collective-permute-start | bytes 2359304 | tf_op jit(solution)/shard_map/ppermute | solution.py:415
  69.7 2.4 %copy-start.6 = (bf16[256,1536]{1,0:T(8,128)(2,1)}, bf16[256,1536]{1,0:T(8,128)(2,1)S(1)}, u32[]{:S(2)}) copy-start(bf16[256,1536]{1,0:T(8,128)(2,1)S(1)} %collective-permute-done.7.refs_3_.x_ref) | copy-start | bytes 2359300
  69.7 38.1 %collective-permute-start.8 = (bf16[256,1536]{1,0:T(8,128)(2,1)}, bf16[256,1536]{1,0:T(8,128)(2,1)}, u32[]{:S(2)}, u32[]{:S(2)}) collective-permute-start(bf16[256,1536]{1,0:T(8,128)(2,1)} %pack.12), channel_id=1, source_target_pairs={{0,5},{1,4},{2,7},{3,6},{4,1},{5,0},{6,3},{7,2},{8,13},{9,12},{10,... | collective-permute-start | bytes 2359304 | tf_op jit(solution)/shard_map/ppermute | solution.py:415
  84.3 7.1 %copy-start.7 = (bf16[256,1536]{1,0:T(8,128)(2,1)S(1)}, bf16[256,1536]{1,0:T(8,128)(2,1)}, u32[]{:S(2)}) copy-start(bf16[256,1536]{1,0:T(8,128)(2,1)} %copy-done.6) | copy-start | bytes 2359300
  88.0 25.5 %collective-permute-start.1 = (bf16[256,1536]{1,0:T(8,128)(2,1)}, bf16[256,1536]{1,0:T(8,128)(2,1)}, u32[]{:S(2)}, u32[]{:S(2)}) collective-permute-start(bf16[256,1536]{1,0:T(8,128)(2,1)} %pack.8), channel_id=1, source_target_pairs={{0,2},{1,3},{2,0},{3,1},{4,6},{5,7},{6,4},{7,5},{8,10},{9,11},{10,... | collective-permute-start | bytes 2359304 | tf_op jit(solution)/shard_map/ppermute | solution.py:415
  89.9 25.5 %collective-permute-start.5 = (bf16[256,1536]{1,0:T(8,128)(2,1)}, bf16[256,1536]{1,0:T(8,128)(2,1)}, u32[]{:S(2)}, u32[]{:S(2)}) collective-permute-start(bf16[256,1536]{1,0:T(8,128)(2,1)} %pack.11), channel_id=1, source_target_pairs={{0,4},{1,5},{2,6},{3,7},{4,0},{5,1},{6,2},{7,3},{8,12},{9,13},{10,... | collective-permute-start | bytes 2359304 | tf_op jit(solution)/shard_map/ppermute | solution.py:415
  95.0 7.1 %copy-start = (bf16[1536,1024]{1,0:T(8,128)(2,1)}, bf16[1536,1024]{1,0:T(8,128)(2,1)S(1)}, u32[]{:S(2)}) copy-start(bf16[1536,1024]{1,0:T(8,128)(2,1)S(1)} %transpose_tokens.2.refs_1_) | copy-start | bytes 9437188
  95.0 3.8 %copy-start.19 = (bf16[256,512]{1,0:T(8,128)(2,1)S(1)}, bf16[256,512]{1,0:T(8,128)(2,1)}, u32[]{:S(2)}) copy-start(bf16[256,512]{1,0:T(8,128)(2,1)} %copy-done.18) | copy-start | bytes 786436
  96.8 14.6 %collective-permute-start.11 = (bf16[256,512]{1,0:T(8,128)(2,1)}, bf16[256,512]{1,0:T(8,128)(2,1)}, u32[]{:S(2)}, u32[]{:S(2)}) collective-permute-start(bf16[256,512]{1,0:T(8,128)(2,1)} %partial_keys.8), channel_id=1, source_target_pairs={{0,1},{1,0},{2,3},{3,2},{4,5},{5,4},{6,7},{7,6},{8,9},{9,8},{10,11... | collective-permute-start | bytes 786440 | tf_op jit(solution)/shard_map/ppermute | solution.py:415
  102.1 1.7 copy-start.2
  105.1 0.9 copy-start.4
  106.0 7.5 %collective-permute-start.13 = (bf16[256,512]{1,0:T(8,128)(2,1)}, bf16[256,512]{1,0:T(8,128)(2,1)}, u32[]{:S(2)}, u32[]{:S(2)}) collective-permute-start(bf16[256,512]{1,0:T(8,128)(2,1)} %partial_keys.10), channel_id=1, source_target_pairs={{0,1},{1,0},{2,3},{3,2},{4,5},{5,4},{6,7},{7,6},{8,9},{9,8},{10,11... | collective-permute-start | bytes 786440 | tf_op jit(solution)/shard_map/ppermute | solution.py:415
  109.5 7.8 %collective-permute-start.15 = (bf16[256,512]{1,0:T(8,128)(2,1)S(1)}, bf16[256,512]{1,0:T(8,128)(2,1)S(1)}, u32[]{:S(2)}, u32[]{:S(2)}) collective-permute-start(bf16[256,512]{1,0:T(8,128)(2,1)S(1)} %partial_keys.12), channel_id=1, source_target_pairs={{0,1},{1,0},{2,3},{3,2},{4,5},{5,4},{6,7},{7,6},{8,9},{9,8},{10,11... | collective-permute-start | bytes 786440 | tf_op jit(solution)/shard_map/ppermute | solution.py:415
  111.3 9.3 %collective-permute-start.17 = (bf16[256,512]{1,0:T(8,128)(2,1)S(1)}, bf16[256,512]{1,0:T(8,128)(2,1)S(1)}, u32[]{:S(2)}, u32[]{:S(2)}) collective-permute-start(bf16[256,512]{1,0:T(8,128)(2,1)S(1)} %partial_keys.14), channel_id=1, source_target_pairs={{0,1},{1,0},{2,3},{3,2},{4,5},{5,4},{6,7},{7,6},{8,9},{9,8},{10,11... | collective-permute-start | bytes 786440 | tf_op jit(solution)/shard_map/ppermute | solution.py:415
  113.4 12.3 %collective-permute-start.12 = (bf16[256,512]{1,0:T(8,128)(2,1)S(1)}, bf16[256,512]{1,0:T(8,128)(2,1)S(1)}, u32[]{:S(2)}, u32[]{:S(2)}) collective-permute-start(bf16[256,512]{1,0:T(8,128)(2,1)S(1)} %partial_keys.9), channel_id=1, source_target_pairs={{0,6},{1,7},{2,4},{3,5},{4,2},{5,3},{6,0},{7,1},{8,14},{9,15},{10,... | collective-permute-start | bytes 786440 | tf_op jit(solution)/shard_map/ppermute | solution.py:415
  115.3 5.9 %copy-start.5 = (bf16[256,1536]{1,0:T(8,128)(2,1)S(1)}, bf16[256,1536]{1,0:T(8,128)(2,1)}, u32[]{:S(2)}) copy-start(bf16[256,1536]{1,0:T(8,128)(2,1)} %copy-done.4) | copy-start | bytes 2359300
  115.3 11.9 %collective-permute-start.14 = (bf16[256,512]{1,0:T(8,128)(2,1)S(1)}, bf16[256,512]{1,0:T(8,128)(2,1)S(1)}, u32[]{:S(2)}, u32[]{:S(2)}) collective-permute-start(bf16[256,512]{1,0:T(8,128)(2,1)S(1)} %partial_keys.11), channel_id=1, source_target_pairs={{0,2},{1,3},{2,0},{3,1},{4,6},{5,7},{6,4},{7,5},{8,10},{9,11},{10,... | collective-permute-start | bytes 786440 | tf_op jit(solution)/shard_map/ppermute | solution.py:415
  119.0 9.2 %collective-permute-start.16 = (bf16[256,512]{1,0:T(8,128)(2,1)S(1)}, bf16[256,512]{1,0:T(8,128)(2,1)S(1)}, u32[]{:S(2)}, u32[]{:S(2)}) collective-permute-start(bf16[256,512]{1,0:T(8,128)(2,1)S(1)} %partial_keys.13), channel_id=1, source_target_pairs={{0,4},{1,5},{2,6},{3,7},{4,0},{5,1},{6,2},{7,3},{8,12},{9,13},{10,... | collective-permute-start | bytes 786440 | tf_op jit(solution)/shard_map/ppermute | solution.py:415
  121.2 7.0 %copy-start.11 = (bf16[1,256,1024]{2,1,0:T(8,128)(2,1)S(1)}, bf16[1,256,1024]{2,1,0:T(8,128)(2,1)}, u32[]{:S(2)}) copy-start(bf16[1,256,1024]{2,1,0:T(8,128)(2,1)} %param.10) | copy-start | bytes 1572868
  121.2 21.9 %copy-start.3 = (f32[1536,512]{1,0:T(8,128)S(1)}, f32[1536,512]{1,0:T(8,128)}, u32[]{:S(2)}) copy-start(f32[1536,512]{1,0:T(8,128)} %copy-done.2) | copy-start | bytes 9437188
  121.2 21.9 %copy-start.13 = (bf16[256,512]{1,0:T(8,128)(2,1)S(1)}, bf16[256,512]{1,0:T(8,128)(2,1)}, u32[]{:S(2)}) copy-start(bf16[256,512]{1,0:T(8,128)(2,1)} %copy-done.12) | copy-start | bytes 786436
  121.2 21.9 %copy-start.15 = (bf16[256,512]{1,0:T(8,128)(2,1)S(1)}, bf16[256,512]{1,0:T(8,128)(2,1)}, u32[]{:S(2)}) copy-start(bf16[256,512]{1,0:T(8,128)(2,1)} %copy-done.14) | copy-start | bytes 786436
  121.2 21.9 %copy-start.16 = (bf16[256,512]{1,0:T(8,128)(2,1)S(1)}, bf16[256,512]{1,0:T(8,128)(2,1)}, u32[]{:S(2)}) copy-start(bf16[256,512]{1,0:T(8,128)(2,1)} %get-tuple-element.94.refs_5_) | copy-start | bytes 786436
  121.2 21.9 %copy-start.17 = (bf16[256,512]{1,0:T(8,128)(2,1)S(1)}, bf16[256,512]{1,0:T(8,128)(2,1)}, u32[]{:S(2)}) copy-start(bf16[256,512]{1,0:T(8,128)(2,1)} %get-tuple-element.95.refs_3_) | copy-start | bytes 786436
  128.8 10.2 %collective-permute-start.23 = (bf16[256,512]{1,0:T(8,128)(2,1)S(1)}, bf16[256,512]{1,0:T(8,128)(2,1)S(1)}, u32[]{:S(2)}, u32[]{:S(2)}) collective-permute-start(bf16[256,512]{1,0:T(8,128)(2,1)S(1)} %key_backward.1.refs_2_), channel_id=1, source_target_pairs={{0,6},{1,7},{2,4},{3,5},{4,2},{5,3},{6,0},{7,1},{8,14},{9,15},{10,... | collective-permute-start | bytes 786440 | tf_op jit(solution)/shard_map/ppermute | solution.py:415
  129.4 12.8 %collective-permute-start.18 = (bf16[256,512]{1,0:T(8,128)(2,1)S(1)}, bf16[256,512]{1,0:T(8,128)(2,1)S(1)}, u32[]{:S(2)}, u32[]{:S(2)}) collective-permute-start(bf16[256,512]{1,0:T(8,128)(2,1)S(1)} %key_backward.1.refs_2_), channel_id=1, source_target_pairs={{0,2},{1,3},{2,0},{3,1},{4,6},{5,7},{6,4},{7,5},{8,10},{9,11},{10,... | collective-permute-start | bytes 786440 | tf_op jit(solution)/shard_map/ppermute | solution.py:415
  131.0 12.1 %collective-permute-start.20 = (bf16[256,512]{1,0:T(8,128)(2,1)S(1)}, bf16[256,512]{1,0:T(8,128)(2,1)S(1)}, u32[]{:S(2)}, u32[]{:S(2)}) collective-permute-start(bf16[256,512]{1,0:T(8,128)(2,1)S(1)} %key_backward.1.refs_2_), channel_id=1, source_target_pairs={{0,4},{1,5},{2,6},{3,7},{4,0},{5,1},{6,2},{7,3},{8,12},{9,13},{10,... | collective-permute-start | bytes 786440 | tf_op jit(solution)/shard_map/ppermute | solution.py:415
  132.3 15.7 %collective-permute-start.22 = (bf16[256,512]{1,0:T(8,128)(2,1)S(1)}, bf16[256,512]{1,0:T(8,128)(2,1)S(1)}, u32[]{:S(2)}, u32[]{:S(2)}) collective-permute-start(bf16[256,512]{1,0:T(8,128)(2,1)S(1)} %key_backward.1.refs_2_), channel_id=1, source_target_pairs={{0,1},{1,0},{2,3},{3,2},{4,5},{5,4},{6,7},{7,6},{8,9},{9,8},{10,11... | collective-permute-start | bytes 786440 | tf_op jit(solution)/shard_map/ppermute | solution.py:415
  139.0 9.0 %collective-permute-start.24 = (bf16[256,512]{1,0:T(8,128)(2,1)S(1)}, bf16[256,512]{1,0:T(8,128)(2,1)S(1)}, u32[]{:S(2)}, u32[]{:S(2)}) collective-permute-start(bf16[256,512]{1,0:T(8,128)(2,1)S(1)} %collective-permute-done.23.refs_4_), channel_id=1, source_target_pairs={{0,1},{1,0},{2,3},{3,2},{4,5},{5,4},{6,7},{7,6},{8,9},{9,8},{10,11... | collective-permute-start | bytes 786440 | tf_op jit(solution)/shard_map/ppermute | solution.py:415
  142.1 9.3 %collective-permute-start.19 = (bf16[256,512]{1,0:T(8,128)(2,1)S(1)}, bf16[256,512]{1,0:T(8,128)(2,1)S(1)}, u32[]{:S(2)}, u32[]{:S(2)}) collective-permute-start(bf16[256,512]{1,0:T(8,128)(2,1)S(1)} %collective-permute-done.18.refs_2_), channel_id=1, source_target_pairs={{0,1},{1,0},{2,3},{3,2},{4,5},{5,4},{6,7},{7,6},{8,9},{9,8},{10,11... | collective-permute-start | bytes 786440 | tf_op jit(solution)/shard_map/ppermute | solution.py:415
  143.1 8.3 %collective-permute-start.21 = (bf16[256,512]{1,0:T(8,128)(2,1)S(1)}, bf16[256,512]{1,0:T(8,128)(2,1)S(1)}, u32[]{:S(2)}, u32[]{:S(2)}) collective-permute-start(bf16[256,512]{1,0:T(8,128)(2,1)S(1)} %collective-permute-done.20.refs_4_), channel_id=1, source_target_pairs={{0,1},{1,0},{2,3},{3,2},{4,5},{5,4},{6,7},{7,6},{8,9},{9,8},{10,11... | collective-permute-start | bytes 786440 | tf_op jit(solution)/shard_map/ppermute | solution.py:415
  143.2 4.9 %copy-start.1 = (bf16[1536,1024]{1,0:T(8,128)(2,1)S(1)}, bf16[1536,1024]{1,0:T(8,128)(2,1)}, u32[]{:S(2)}) copy-start(bf16[1536,1024]{1,0:T(8,128)(2,1)} %copy-done) | copy-start | bytes 9437188
  151.4 12.1 %copy-start.8 = (f32[4,384,128]{2,1,0:T(8,128)S(1)}, f32[4,384,128]{2,1,0:T(8,128)}, u32[]{:S(2)}) copy-start(f32[4,384,128]{2,1,0:T(8,128)} %get-tuple-element.58.w_ref) | copy-start | bytes 2359300
  151.4 12.1 %copy-start.20 = (f32[4,384,128]{2,1,0:T(8,128)S(1)}, f32[4,384,128]{2,1,0:T(8,128)}, u32[]{:S(2)}) copy-start(f32[4,384,128]{2,1,0:T(8,128)} %get-tuple-element.79.m_ref) | copy-start | bytes 2359300
  151.4 12.1 %copy-start.21 = (f32[4,384,128]{2,1,0:T(8,128)S(1)}, f32[4,384,128]{2,1,0:T(8,128)}, u32[]{:S(2)}) copy-start(f32[4,384,128]{2,1,0:T(8,128)} %get-tuple-element.59.v_ref) | copy-start | bytes 2359300
  156.4 1.3 collective-permute-start.25
  157.7 4.5 %collective-permute-start.28 = (f32[8,128]{1,0:T(8,128)S(1)}, f32[8,128]{1,0:T(8,128)S(1)}, u32[]{:S(2)}, u32[]{:S(2)}) collective-permute-start(f32[8,128]{1,0:T(8,128)S(1)} %add.44.refs_0_), channel_id=1, source_target_pairs={{0,6},{1,7},{2,4},{3,5},{4,2},{5,3},{6,0},{7,1},{8,14},{9,15},{10,... | collective-permute-start | bytes 12296 | tf_op jit(solution)/shard_map/ppermute | solution.py:415
  158.9 3.6 %collective-permute-start.27 = (f32[8,128]{1,0:T(8,128)S(1)}, f32[8,128]{1,0:T(8,128)S(1)}, u32[]{:S(2)}, u32[]{:S(2)}) collective-permute-start(f32[8,128]{1,0:T(8,128)S(1)} %add.44.refs_0_), channel_id=1, source_target_pairs={{0,4},{1,5},{2,6},{3,7},{4,0},{5,1},{6,2},{7,3},{8,12},{9,13},{10,... | collective-permute-start | bytes 12296 | tf_op jit(solution)/shard_map/ppermute | solution.py:415
  159.9 3.6 %collective-permute-start.26 = (f32[8,128]{1,0:T(8,128)S(1)}, f32[8,128]{1,0:T(8,128)S(1)}, u32[]{:S(2)}, u32[]{:S(2)}) collective-permute-start(f32[8,128]{1,0:T(8,128)S(1)} %add.44.refs_0_), channel_id=1, source_target_pairs={{0,2},{1,3},{2,0},{3,1},{4,6},{5,7},{6,4},{7,5},{8,10},{9,11},{10,... | collective-permute-start | bytes 12296 | tf_op jit(solution)/shard_map/ppermute | solution.py:415
  165.1 14.3 %collective-permute-start.29 = (bf16[384,128]{1,0:T(8,128)(2,1)S(1)}, bf16[384,128]{1,0:T(8,128)(2,1)S(1)}, u32[]{:S(2)}, u32[]{:S(2)}) collective-permute-start(bf16[384,128]{1,0:T(8,128)(2,1)S(1)} %get-tuple-element.82), channel_id=1, source_target_pairs={{0,8},{8,0},{16,24},{24,16},{1,9},{9,1},{17,25},{25,17},{2,10},{10... | collective-permute-start | bytes 294920 | tf_op jit(solution)/shard_map/ppermute | solution.py:415
  166.0 13.4 %collective-permute-start.30 = (bf16[384,128]{1,0:T(8,128)(2,1)S(1)}, bf16[384,128]{1,0:T(8,128)(2,1)S(1)}, u32[]{:S(2)}, u32[]{:S(2)}) collective-permute-start(bf16[384,128]{1,0:T(8,128)(2,1)S(1)} %get-tuple-element.83), channel_id=1, source_target_pairs={{0,16},{8,24},{16,0},{24,8},{1,17},{9,25},{17,1},{25,9},{2,18},{10... | collective-permute-start | bytes 294920 | tf_op jit(solution)/shard_map/ppermute | solution.py:415
  168.8 10.6 %collective-permute-start.31 = (bf16[384,128]{1,0:T(8,128)(2,1)S(1)}, bf16[384,128]{1,0:T(8,128)(2,1)S(1)}, u32[]{:S(2)}, u32[]{:S(2)}) collective-permute-start(bf16[384,128]{1,0:T(8,128)(2,1)S(1)} %get-tuple-element.84), channel_id=1, source_target_pairs={{0,24},{8,16},{16,8},{24,0},{1,25},{9,17},{17,9},{25,1},{2,26},{10... | collective-permute-start | bytes 294920 | tf_op jit(solution)/shard_map/ppermute | solution.py:415
  169.6 14.4 %copy-start.9 = (f32[1,384,128]{2,1,0:T(8,128)S(1)}, f32[1,384,128]{2,1,0:T(8,128)}, u32[]{:S(2)}) copy-start(f32[1,384,128]{2,1,0:T(8,128)} %get-tuple-element.56) | copy-start | bytes 589828
  169.6 14.4 %copy-start.23 = (f32[384,128]{1,0:T(8,128)S(1)}, f32[384,128]{1,0:T(8,128)}, u32[]{:S(2)}) copy-start(f32[384,128]{1,0:T(8,128)} %reduce_sum.9) | copy-start | bytes 589828
  179.5 14.3 %collective-permute-start.34 = (bf16[384,128]{1,0:T(8,128)(2,1)S(1)}, bf16[384,128]{1,0:T(8,128)(2,1)S(1)}, u32[]{:S(2)}, u32[]{:S(2)}) collective-permute-start(bf16[384,128]{1,0:T(8,128)(2,1)S(1)} %convert_element_type.24.refs_7_), channel_id=1, source_target_pairs={{0,24},{8,16},{16,8},{24,0},{1,25},{9,17},{17,9},{25,1},{2,26},{10... | collective-permute-start | bytes 294920 | tf_op jit(solution)/shard_map/ppermute | solution.py:415
  182.6 11.2 %collective-permute-start.33 = (bf16[384,128]{1,0:T(8,128)(2,1)S(1)}, bf16[384,128]{1,0:T(8,128)(2,1)S(1)}, u32[]{:S(2)}, u32[]{:S(2)}) collective-permute-start(bf16[384,128]{1,0:T(8,128)(2,1)S(1)} %convert_element_type.24.refs_7_), channel_id=1, source_target_pairs={{0,16},{8,24},{16,0},{24,8},{1,17},{9,25},{17,1},{25,9},{2,18},{10... | collective-permute-start | bytes 294920 | tf_op jit(solution)/shard_map/ppermute | solution.py:415
  182.6 11.2 %collective-permute-start.32 = (bf16[384,128]{1,0:T(8,128)(2,1)S(1)}, bf16[384,128]{1,0:T(8,128)(2,1)S(1)}, u32[]{:S(2)}, u32[]{:S(2)}) collective-permute-start(bf16[384,128]{1,0:T(8,128)(2,1)S(1)} %convert_element_type.24.refs_7_), channel_id=1, source_target_pairs={{0,8},{8,0},{16,24},{24,16},{1,9},{9,1},{17,25},{25,17},{2,10},{10... | collective-permute-start | bytes 294920 | tf_op jit(solution)/shard_map/ppermute | solution.py:415
  184.0 9.8 %copy-start.22 = (f32[1,384,128]{2,1,0:T(8,128)S(1)}, f32[1,384,128]{2,1,0:T(8,128)}, u32[]{:S(2)}) copy-start(f32[1,384,128]{2,1,0:T(8,128)} %get-tuple-element.57) | copy-start | bytes 589828

commit v7 on v6

--- a/solution.py
+++ b/solution.py
@@ -38,51 +38,64 @@
     return pl.CostEstimate(flops=int(flops), bytes_accessed=int(moved), transcendentals=0)
 
 
-def copy_kernel(src_ref, out_ref):
-    out_ref[...] = src_ref[...].reshape(out_ref.shape)
-
-
-def pack_kernel(me_ref, src_ref, out_ref):
-    out_ref[...] = src_ref[...]
-
-
-def pack(tokens, me, offset, rows):
-    count = tokens.shape[0]
-    return pl.pallas_call(
-        pack_kernel,
-        out_shape=jax.ShapeDtypeStruct((count, rows), tokens.dtype),
+def pack_kernel(first, src_ref, out_ref, held, in_sems, out_sems):
+    shards, count, rows = out_ref.shape
+
+    def fetch(s):
+        block = src_ref.at[pl.ds(first, count), pl.ds(s * rows, rows)]
+        return pltpu.make_async_copy(block, held.at[s], in_sems.at[s])
+
+    def store(s):
+        return pltpu.make_async_copy(held.at[s], out_ref.at[s], out_sems.at[s])
+
+    for s in range(shards):
+        fetch(s).start()
+    for s in range(shards):
+        fetch(s).wait()
+        store(s).start()
+    for s in range(shards):
+        store(s).wait()
+
+
+def pack(tokens, first, count, rows):
+    shards = tokens.shape[1] // rows
+    shape = (shards, count, rows)
+    return pl.pallas_call(
+        functools.partial(pack_kernel, first),
+        out_shape=pltpu.HBM(shape, tokens.dtype),
+        in_specs=[pl.BlockSpec(memory_space=pl.ANY)],
+        out_specs=pl.BlockSpec(memory_space=pl.ANY),
+        scratch_shapes=[
+            pltpu.VMEM(shape, tokens.dtype),
+            pltpu.SemaphoreType.DMA((shards,)),
+            pltpu.SemaphoreType.DMA((shards,)),
+        ],
+        compiler_params=params_of(12),
+        cost_estimate=cost(0, 4 * shards * count * rows),
+        name="pack",
+    )(*in_hbm(tokens))
+
+
+def transpose_kernel(me_ref, even_ref, odd_ref, out_ref):
+    out_ref[...] = jnp.concatenate([even_ref[0], odd_ref[0]], axis=0).T
+
+
+def transpose_tokens(blocks, me):
+    shards, count, rows = blocks.shape
+    block = lambda odd: pl.BlockSpec((1, count, rows), lambda m, me: (me[0] ^ (2 * m + odd), 0, 0))
+    return pl.pallas_call(
+        transpose_kernel,
+        out_shape=jax.ShapeDtypeStruct((rows, shards * count), blocks.dtype),
         grid_spec=pltpu.PrefetchScalarGridSpec(
             num_scalar_prefetch=1,
-            grid=(1,),
-            in_specs=[pl.BlockSpec((count, rows), lambda i, me: (0, me[0] ^ offset))],
-            out_specs=pl.BlockSpec((count, rows), lambda i, me: (0, 0)),
+            grid=(shards // 2,),
+            in_specs=[block(0), block(1)],
+            out_specs=pl.BlockSpec((rows, 2 * count), lambda m, me: (0, m)),
         ),
-        compiler_params=params_of(4),
-        cost_estimate=cost(0, 4 * count * rows),
-        name="pack",
-    )(me, *in_hbm(tokens))
-
-
-def transpose_kernel(*refs):
-    *x_refs, out_ref = refs
-    count = x_refs[0].shape[0]
-    for j, ref in enumerate(x_refs):
-        out_ref[:, j * count:(j + 1) * count] = ref[...].T
-
-
-def transpose_tokens(blocks):
-    count, rows = blocks[0].shape
-    step = 256
-    return pl.pallas_call(
-        transpose_kernel,
-        out_shape=jax.ShapeDtypeStruct((rows, len(blocks) * count), blocks[0].dtype),
-        grid=(rows // step,),
-        in_specs=[pl.BlockSpec((count, step), lambda i: (0, i))] * len(blocks),
-        out_specs=pl.BlockSpec((step, len(blocks) * count), lambda i: (i, 0)),
-        compiler_params=params_of(8),
-        cost_estimate=cost(0, 4 * len(blocks) * count * rows),
+        compiler_params=params_of(12),
+        cost_estimate=cost(0, 4 * blocks.size),
         name="transpose_tokens",
-    )(*blocks)
+    )(me, blocks, blocks)
 
 
 def cast_kernel(src_ref, out_ref):
@@ -104,61 +117,86 @@
     )(*in_hbm(array))
 
 
-def partial_kernel(x_ref, w_ref, *refs):
-    *add_refs, out_ref = refs
-    total = jnp.dot(x_ref[...], w_ref[...], preferred_element_type=jnp.float32)
-    for ref in add_refs:
-        total = total + ref[...].astype(jnp.float32)
-    out_ref[...] = total.astype(out_ref.dtype)
-
-
-def partial_keys(block, key_weights, *others):
-    count, rows = block.shape
+def partial_kernel(me_ref, x_ref, w_ref, out_ref):
+    product = jnp.dot(x_ref[0], w_ref[...], preferred_element_type=jnp.float32)
+    out_ref[0] = product.astype(out_ref.dtype)
+
+
+def summed_kernel(me_ref, x_ref, w_ref, add_ref, *out_refs):
+    total = jnp.dot(x_ref[0], w_ref[...], preferred_element_type=jnp.float32)
+    total = (total + add_ref[0].astype(jnp.float32)).astype(out_refs[0].dtype)
+    for m, ref in enumerate(out_refs):
+
+        @pl.when(pl.program_id(0) == m)
+        def _():
+            ref[...] = total
+
+
+def partial_keys(blocks, key_weights, me, odd, others=None):
+    shards, count, rows = blocks.shape
     width = key_weights.shape[1]
-    return pl.pallas_call(
-        partial_kernel,
-        out_shape=jax.ShapeDtypeStruct((count, width), jnp.bfloat16),
-        compiler_params=params_of(8),
-        cost_estimate=cost(2 * count * rows * width, 2 * count * rows),
+    chips = shards // 2
+    stacked = pl.BlockSpec((1, count, width), lambda m, me: (m, 0, 0))
+    specs = [
+        pl.BlockSpec((1, count, rows), lambda m, me: (me[0] ^ (2 * m + odd), 0, 0)),
+        pl.BlockSpec((rows, width), lambda m, me: (0, 0)),
+    ]
+    if others is None:
+        kernel, args = partial_kernel, ()
+        shapes, outs = jax.ShapeDtypeStruct((chips, count, width), jnp.bfloat16), stacked
+    else:
+        kernel, args = summed_kernel, (others,)
+        specs.append(stacked)
+        shapes = [jax.ShapeDtypeStruct((count, width), jnp.bfloat16)] * chips
+        outs = [pl.BlockSpec((count, width), lambda m, me: (0, 0))] * chips
+    return pl.pallas_call(
+        kernel,
+        out_shape=shapes,
+        grid_spec=pltpu.PrefetchScalarGridSpec(
+            num_scalar_prefetch=1, grid=(chips,), in_specs=specs, out_specs=outs
+        ),
+        compiler_params=params_of(12),
+        cost_estimate=cost(2 * chips * count * rows * width, 2 * chips * count * rows),
         name="partial_keys",
-    )(block, key_weights, *others)
-
-
-def key_kernel(*refs):
+    )(me, blocks, key_weights, *args)
+
+
+def key_kernel(first, *refs):
     *part_refs, cot_ref, out_ref = refs
+    count = out_ref.shape[0]
     raw = sum(ref[...].astype(jnp.float32) for ref in part_refs)
     for h in range(raw.shape[1] // HEAD):
         cols = slice(h * HEAD, (h + 1) * HEAD)
         head = raw[:, cols]
         inverse = lax.rsqrt(jnp.mean(head * head, axis=1, keepdims=True) + 1e-06)
         normed = head * inverse
-        upper = cot_ref[:, cols].astype(jnp.float32)
+        upper = cot_ref[first:first + count, cols].astype(jnp.float32)
         back = inverse * (upper - normed * jnp.mean(upper * normed, axis=1, keepdims=True))
         out_ref[:, cols] = back.astype(out_ref.dtype)
 
 
-def key_backward(parts, incoming):
-    block = pl.BlockSpec(parts[0].shape, lambda i: (0, 0))
-    cot = pl.BlockSpec(parts[0].shape, lambda i: (0, 0))
-    size = parts[0].size
-    return pl.pallas_call(
-        key_kernel,
-        out_shape=jax.ShapeDtypeStruct(parts[0].shape, jnp.bfloat16),
+def key_backward(parts, incoming, first):
+    count, width = parts[0].shape
+    block = pl.BlockSpec((count, width), lambda i: (0, 0))
+    cot = pl.BlockSpec((incoming.shape[0], width), lambda i: (0, 0))
+    return pl.pallas_call(
+        functools.partial(key_kernel, first),
+        out_shape=jax.ShapeDtypeStruct((count, width), jnp.bfloat16),
         grid=(1,),
         in_specs=[block] * len(parts) + [cot],
         out_specs=block,
         compiler_params=params_of(8),
-        cost_estimate=cost(60 * size, 12 * size),
+        cost_estimate=cost(60 * count * width, 12 * count * width),
         name="key_backward",
     )(*parts, incoming)
 
 
-def grad_kernel(counts, has_base, has_more, last, *refs):
+def grad_kernel(firsts, has_base, has_more, last, *refs):
     refs = list(refs)
     place_ref = refs.pop(0)
     terms = []
-    for count in counts:
-        terms.append((refs.pop(0), refs[:count]))
+    for count, first in firsts:
+        terms.append((refs.pop(0), refs[:count], first))
         del refs[:count]
     base = refs.pop(0) if has_base else None
     square_in, due_in = (refs.pop(0), refs.pop(0)) if has_more else (None, None)
@@ -168,15 +206,15 @@
 
     @pl.when(pl.program_id(0) == 0)
     def _():
-        for (_, blocks), held in zip(terms, joined):
-            depth = blocks[0].shape[0]
+        for (_, blocks, first), held in zip(terms, joined):
+            depth = held.shape[0] // len(blocks)
             for j, block in enumerate(blocks):
-                held[j * depth:(j + 1) * depth, :] = block[...]
+                held[j * depth:(j + 1) * depth, :] = block[first:first + depth, :]
         if last:
             sq_ref[...] = square_in[...] if has_more else jnp.zeros_like(sq_ref)
 
     total = base[...] if has_base else None
-    for (x_ref, _), held in zip(terms, joined):
+    for (x_ref, _, _), held in zip(terms, joined):
         term = jnp.dot(x_ref[...], held[...], preferred_element_type=jnp.float32)
         total = term if total is None else total + term
     out_ref[...] = total
@@ -203,7 +241,7 @@
     row_block = lambda cols: pl.BlockSpec((step, cols), lambda i, p: (i, 0))
     fixed = pl.BlockSpec((8, HEAD), lambda i, p: (0, 0))
     args, specs, scratch = [], [], []
-    for x, blocks in terms:
+    for x, blocks, _ in terms:
         args += [x, *blocks]
         specs += [row_block(x.shape[1])]
         specs += [pl.BlockSpec(b.shape, lambda i, p: (0, 0)) for b in blocks]
@@ -224,9 +262,9 @@
     else:
         shapes = [jax.ShapeDtypeStruct((rows, width), jnp.float32)]
         outs = [row_block(width)]
-    depth = sum(x.shape[1] for x, _ in terms)
-    return pl.pallas_call(
-        functools.partial(grad_kernel, [len(b) for _, b in terms], base is not None, square is not None, last),
+    depth = sum(x.shape[1] for x, _, _ in terms)
+    return pl.pallas_call(
+        functools.partial(grad_kernel, [(len(b), first) for _, b, first in terms], base is not None, square is not None, last),
         out_shape=shapes,
         grid_spec=pltpu.PrefetchScalarGridSpec(
             num_scalar_prefetch=1,
@@ -351,20 +389,46 @@
     )(place, *in_hbm(*arrays))
 
 
-def duplicate(array):
-    rows, width = array.shape
-    step = rows // 4 if rows % 32 == 0 else rows
-    block = pl.BlockSpec((step, width), lambda i: (i, 0))
-    return pl.pallas_call(
-        copy_kernel,
-        out_shape=pltpu.HBM((rows, width), array.dtype),
-        grid=(rows // step,),
-        in_specs=[block],
-        out_specs=block,
+def duplicate_kernel(*refs):
+    half = (len(refs) - 3) // 2
+    held, in_sems, out_sems = refs[2 * half:]
+    streams = held.shape[1]
+    step = held.shape[2]
+    places = [(a, i, pl.ds(i * step, step)) for a in range(half) for i in range(streams)]
+    fetches = [
+        pltpu.make_async_copy(refs[a].at[at], held.at[a, i], in_sems.at[a, i]) for a, i, at in places
+    ]
+    stores = [
+        pltpu.make_async_copy(held.at[a, i], refs[half + a].at[at], out_sems.at[a, i])
+        for a, i, at in places
+    ]
+    for copy in fetches:
+        copy.start()
+    for fetch, store in zip(fetches, stores):
+        fetch.wait()
+        store.start()
+    for copy in stores:
+        copy.wait()
+
+
+def duplicate(*arrays):
+    rows, width = arrays[0].shape
+    streams = 4
+    whole = pl.BlockSpec(memory_space=pl.ANY)
+    return pl.pallas_call(
+        duplicate_kernel,
+        out_shape=[pltpu.HBM(a.shape, a.dtype) for a in arrays],
+        in_specs=[whole] * len(arrays),
+        out_specs=[whole] * len(arrays),
+        scratch_shapes=[
+            pltpu.VMEM((len(arrays), streams, rows // streams, width), arrays[0].dtype),
+            pltpu.SemaphoreType.DMA((len(arrays), streams)),
+            pltpu.SemaphoreType.DMA((len(arrays), streams)),
+        ],
         compiler_params=params_of(8),
-        cost_estimate=cost(0, 8 * array.size),
+        cost_estimate=cost(0, sum(8 * a.size for a in arrays)),
         name="duplicate",
-    )(*in_hbm(array))
+    )(*in_hbm(*arrays))
 
 
 def outer_kernel(replicas, place_ref, *refs):
@@ -417,22 +481,6 @@
 
 def after(value, *others):
     return lax.optimization_barrier((value,) + others)[0]
-
-
-def by_device(pieces, me):
-    count = pieces.shape[0]
-    return jnp.stack([lax.dynamic_index_in_dim(pieces, me ^ k, 0, keepdims=False) for k in range(count)])
-
-
-class Line:
-    def __init__(self, axis, window):
-        self.axis, self.window, self.ended = axis, window, []
-
-    def swap(self, block, offset):
-        if len(self.ended) >= self.window:
-            block = after(block, self.ended[-self.window])
-        self.ended.append(swap(block, self.axis, offset))
-        return self.ended[-1]
 
 
 def body(
@@ -456,31 +504,18 @@
     my_rep = lax.axis_index("rep").astype(jnp.int32)
     place = jnp.stack([due_fragment[0], my_rep])
     chips = range(2, shards, 2)
-    far = sorted(chips, key=lambda k: (-bin(k).count("1"), k))
-
-    line = Line("fsdp", 4)
-    values = {0: incoming[:, kv_width:]}
-    for k in chips:
-        values[k] = line.swap(values[0], k)
-
-    groups = [[k] for k in far if bin(k).count("1") > 1]
-    groups += [[k for k in far if bin(k).count("1") == 1]]
-    blocks, packed = {0: pack(inputs, me, 0, rows)}, {}
-    for group in groups:
-        for odd in range(2):
-            for k in group:
-                packed[k + odd] = pack(inputs, me, k + odd, rows)
-                blocks[k + odd] = line.swap(packed[k + odd], k + odd)
-    early = packed[far[0] + 1]
-    blocks[1] = swap(pack(inputs, after(me, early), 1, rows), "fsdp", 1)
-    crossed = swap(jnp.stack([values[k] for k in range(0, shards, 2)]), "fsdp", 1)
-    for k in range(0, shards, 2):
-        values[k + 1] = crossed[k // 2]
-
-    def to_all(pieces):
-        return lax.all_to_all(pieces, "rep", 0, 0, tiled=True)
-
-    place_early = after(place, early)
+    count = inputs.shape[0]
+    cuts = [(0, count * 3 // 4), (count * 3 // 4, count // 4)]
+
+    def gather(block):
+        held = [block] + [swap(block, "fsdp", k) for k in chips]
+        return [b for h in held for b in (h, swap(h, "fsdp", 1))]
+
+    values = gather(incoming[:, kv_width:])
+
+    packed = [pack(inputs, first, size, rows) for first, size in cuts]
+    arrived = [lax.all_to_all(p, "fsdp", 0, 0, tiled=True) for p in packed]
+
     steps_now = step_count[0].astype(jnp.float32)
     plan = jnp.minimum(1.0, steps_now / WARMUP) * (
         0.55 + 0.45 * jnp.cos(jnp.pi * steps_now / STEPS_TOTAL)
@@ -489,47 +524,36 @@
     inv_one = 1.0 / (1.0 - jnp.power(BETA_ONE, steps_now))
     inv_two = 1.0 / (1.0 - jnp.power(BETA_TWO, steps_now))
     scalars = jnp.stack([rate, inv_one, inv_two])
+    place_early = after(place, *values[2::2])
     old, old_first, old_second = due_columns(place_early, part, params, first_moment[0], second_moment[0])
     anchor_cols, moment_cols = (c[0] for c in due_columns(place_early, part, anchor, momentum))
-    old_sum = jnp.sum(to_all(by_device(old, my_rep)), axis=0)
+    old_sum = sum([swap(old[k], "rep", k) for k in range(1, replicas)], old[0])
     pseudo_old = anchor_cols - old_sum / replicas
     base = anchor_cols - OUTER_RATE * (OUTER_MU * (OUTER_MU * moment_cols + pseudo_old) + pseudo_old)
-    base = to_all(jnp.broadcast_to(base[None], (replicas,) + base.shape))
-    base = by_device(base, my_rep)
-    base = [base[j] for j in range(replicas)]
-    anchor_copy, momentum_copy = duplicate(anchor), duplicate(momentum)
-    key_weights = cast_left(after(params, early), kv_width)
-
-    spread = [0, 1] + [k + odd for k in far for odd in range(2)]
-    near, rest = spread[:shards // 2], spread[shards // 2:]
-    flipped = transpose_tokens([blocks[k] for k in near])
-    (values_first,) = gradient(place, [(flipped, [values[k] for k in near])], last=False)
-
-    last = far[-1]
-    blocks[last + 1] = after(
-        blocks[last + 1], base[-1], anchor_copy, momentum_copy, old_second, scalars, values_first
+    base = [base] + [swap(base, "rep", k) for k in range(1, replicas)]
+    anchor_copy, momentum_copy = duplicate(anchor, momentum)
+    key_weights = cast_left(params, kv_width)
+
+    def sum_keys(x, first, *before):
+        theirs = swap(partial_keys(x, key_weights, me, 1), "fsdp", 1)
+        parts = list(partial_keys(x, key_weights, me, 0, theirs))
+        parts = [parts[0]] + [swap(parts[k // 2], "fsdp", k) for k in chips]
+        parts[0] = after(parts[0], *before)
+        return gather(key_backward(parts, incoming, first))
+
+    arrived[0] = after(
+        arrived[0], packed[1], *base, anchor_copy, momentum_copy, old_second, scalars, *values
     )
-    parts = []
-    for k in far + [0]:
-        theirs = swap(partial_keys(blocks[k + 1], key_weights), "fsdp", 1)
-        part_k = partial_keys(blocks[k], key_weights, theirs)
-        parts.append(line.swap(part_k, k) if k else part_k)
-    flipped_rest = transpose_tokens([blocks[k] for k in rest])
-    parts[-1] = after(parts[-1], flipped_rest)
-    back = key_backward(parts, incoming)
-    keys = {0: back}
-    for k in far:
-        keys[k] = line.swap(back, k)
-    for k in range(0, shards, 2):
-        keys[k + 1] = swap(keys[k], "fsdp", 1)
-
-    grad_values, square, due = gradient(
-        place, [(flipped_rest, [values[k] for k in rest])], values_first
-    )
-    (grad_first,) = gradient(place, [(flipped, [keys[k] for k in near])], last=False)
-    grad_keys, square, due = gradient(
-        place, [(flipped_rest, [keys[k] for k in rest])], grad_first, square, due
-    )
+    flipped = [transpose_tokens(arrived[0], me)]
+    keys = [sum_keys(arrived[0], cuts[0][0], flipped[0])]
+    (values_first,) = gradient(place, [(flipped[0], values, cuts[0][0])], last=False)
+    arrived[1] = after(arrived[1], *keys[0], values_first)
+    flipped.append(transpose_tokens(arrived[1], me))
+    keys.append(sum_keys(arrived[1], cuts[1][0], flipped[1]))
+
+    (keys_first,) = gradient(place, [(flipped[0], keys[0], 0)], last=False)
+    grad_values, square, due = gradient(place, [(flipped[1], values, cuts[1][0])], values_first)
+    grad_keys, square, due = gradient(place, [(flipped[1], keys[1], 0)], keys_first, square, due)
 
     square = square + swap(square, "fsdp", 1)
     squares = [square] + [swap(square, "fsdp", k) for k in chips]

time: 199 us -> 256 us (1.29)
  waiting for transfers between devices: 43.6 us -> 112 us
  Pallas kernels: 91 us -> 80.5 us
  starting transfers between devices: 45.2 us -> 51.4 us
  other arithmetic: 5.33 us -> 2.17 us
  local copies, waits for them, and re-layouts: 8.28 us -> 5.16 us
    ppermute x35 -> x45, waiting for transfers between devices: 43.6 us -> 112 us  [swap(): return lax.ppermute(block, axis, [(i, i ^ offset) for i in range(count)])]
    pallas_call x25 -> x15, Pallas kernels: 57.1 us -> 45.5 us  [the longest x4 18.3 us: gradient(): pl.pallas_call(functools.partial(grad_kernel, [(len(b), first) for _, b,...]
    ppermute x35 -> x45, starting transfers between devices: 34 us -> 42.4 us  [swap(): return lax.ppermute(block, axis, [(i, i ^ offset) for i in range(count)])]
  transfers between devices with their start and end apart: 37 -> 47, of which waited for: 13 -> 18; matrix products, arithmetic and copies ran while one was open for 4% -> 1% of each run, Pallas kernels for 38% -> 23%
where the time goes in v7:
time: 256 us; the launch traced here: 255 us
  waiting for transfers between devices  112 us (44%)
  Pallas kernels  80.5 us (31%)
  starting transfers between devices  51.4 us (20%)
  local copies, waits for them, and re-layouts  5.16 us (2%)
  between operations  3.92 us (2%)
    ppermute x45, waiting for transfers between devices, swap(): return lax.ppermute(block, axis, [(i, i ^ offset) for i in range(count)])  112 us
    ppermute x45, starting transfers between devices, swap(): return lax.ppermute(block, axis, [(i, i ^ offset) for i in range(count)])  42.4 us
    pallas_call x2, Pallas kernels, adam_rows(): pl.pallas_call(functools.partial(adam_kernel, len(squares), len(into)), o...  19.5 us
    pallas_call x4, Pallas kernels, gradient(): pl.pallas_call(functools.partial(grad_kernel, [(len(b), first) for _, b,...  18.3 us
    pallas_call x4, Pallas kernels, partial_keys(): pl.pallas_call(kernel, out_shape=shapes, grid_spec=pltpu.PrefetchScalarGr...  11.5 us
    all_to_all x2, starting transfers between devices, body(): arrived = [lax.all_to_all(p, 'fsdp', 0, 0, tiled=True) for p in packed]  9.09 us
    pallas_call x2, Pallas kernels, due_columns(): pl.pallas_call(pick_kernel, out_shape=[pltpu.HBM((blocks, part, FRAG_COLS...  6.83 us
    pallas_call x2, Pallas kernels, pack(): pl.pallas_call(functools.partial(pack_kernel, first), out_shape=pltpu.HBM...  6.45 us
  transfers between devices with their start and end apart: 47, of which 18 were waited for; matrix products, arithmetic and copies ran while one was open for 1% of the time, Pallas kernels for 23%

profile of v7, /device:TPU:0, one launch (start us, length us, event | category | flops | bytes accessed | tf_op | source)
XLA Modules:
  0.0 255.2 jit_solution(11151024690043252644)
XLA Ops:
  0.6 4.2 %pack.3 = bf16[8,192,1536]{2,1,0:T(8,128)(2,1)} custom-call(bf16[256,12288]{1,0:T(8,128)(2,1)} %bitcast.50), custom_call_target="tpu_custom_call" | custom-call | bytes 9437184 | tf_op jit(solution)/shard_map/pack/pallas_call | solution.py:63
  4.8 5.3 %all-to-all-start.1 = ((bf16[8,192,1536]{2,1,0:T(8,128)(2,1)}), bf16[8,192,1536]{2,1,0:T(8,128)(2,1)}, u32[]{:S(2)}, u32[]{:S(2)}) async-start(bf16[8,192,1536]{2,1,0:T(8,128)(2,1)} %pack.3), calls=%async_computation.1 | async-start | bytes 9437184 | tf_op jit(solution)/shard_map/all_to_all | solution.py:517
  10.2 3.4 %collective-permute-start.2 = (bf16[256,512]{1,0:T(8,128)(2,1)S(1)}, bf16[256,512]{1,0:T(8,128)(2,1)S(1)}, u32[]{:S(2)}, u32[]{:S(2)}) collective-permute-start(bf16[256,512]{1,0:T(8,128)(2,1)S(1)} %slice.20.refs_2_), channel_id=1, source_target_pairs={{0,6},{1,7},{2,4},{3,5},{4,2},{5,3},{6,0},{7,1},{8,14},{9,15},{10,... | collective-permute-start | bytes 786440 | tf_op jit(solution)/shard_map/ppermute | solution.py:479
  14.9 56.4 %collective-permute-done.2.refs_8_ = bf16[256,512]{1,0:T(8,128)(2,1)S(1)} collective-permute-done((bf16[256,512]{1,0:T(8,128)(2,1)S(1)}, bf16[256,512]{1,0:T(8,128)(2,1)S(1)}, u32[]{:S(2)}, u32[]{:S(2)}) %collective-permute-start.2) | collective-permute-done | bytes 262176 | tf_op jit(solution)/shard_map/ppermute | solution.py:479
  71.3 3.8 %collective-permute-done.1.refs_6_ = bf16[256,512]{1,0:T(8,128)(2,1)S(1)} collective-permute-done((bf16[256,512]{1,0:T(8,128)(2,1)S(1)}, bf16[256,512]{1,0:T(8,128)(2,1)S(1)}, u32[]{:S(2)}, u32[]{:S(2)}) %collective-permute-start.1) | collective-permute-done | bytes 262176 | tf_op jit(solution)/shard_map/ppermute | solution.py:479
  75.2 4.5 %due_columns.3 = (f32[4,384,128]{2,1,0:T(8,128)}, f32[4,384,128]{2,1,0:T(8,128)}, f32[4,384,128]{2,1,0:T(8,128)}) custom-call(s32[2]{0:T(128)S(1)} %pad_add_fusion.place_ref.refs_0_, f32[1536,1024]{1,0:T(8,128)} %bitcast.40, f32[1536,1024]{1,0:T(8,128)} %bitcast.44, f32[1536,1024]{1,0:T(8,128)} %bitcast.47), custom_call_target="tpu_custom_call" | custom-call | bytes 4718592 | tf_op jit(solution)/shard_map/due_columns/pallas_call | solution.py:377
  79.7 1.2 slice_bitcast_fusion.2
  80.9 2.4 collective-permute-start.3
  83.3 2.5 collective-permute-start.5
  85.9 2.3 due_columns.2
  88.2 0.5 collective-permute-start.12
  88.8 7.1 %collective-permute-done.5 = f32[384,128]{1,0:T(8,128)S(1)} collective-permute-done((f32[384,128]{1,0:T(8,128)S(1)}, f32[384,128]{1,0:T(8,128)S(1)}, u32[]{:S(2)}, u32[]{:S(2)}) %collective-permute-start.5) | collective-permute-done | bytes 196640 | tf_op jit(solution)/shard_map/ppermute | solution.py:479
  95.9 7.1 %collective-permute-done.4 = f32[384,128]{1,0:T(8,128)S(1)} collective-permute-done((f32[384,128]{1,0:T(8,128)S(1)}, f32[384,128]{1,0:T(8,128)S(1)}, u32[]{:S(2)}, u32[]{:S(2)}) %collective-permute-start.4) | collective-permute-done | bytes 196640 | tf_op jit(solution)/shard_map/ppermute | solution.py:479
  103.0 2.0 multiply_subtract_fusion
  104.9 2.6 %collective-permute-start.8 = (f32[384,128]{1,0:T(8,128)}, f32[384,128]{1,0:T(8,128)}, u32[]{:S(2)}, u32[]{:S(2)}) collective-permute-start(f32[384,128]{1,0:T(8,128)} %get-tuple-element.92.refs_3_), channel_id=1, source_target_pairs={{0,24},{8,16},{16,8},{24,0},{1,25},{9,17},{17,9},{25,1},{2,26},{10... | collective-permute-start | bytes 589832 | tf_op jit(solution)/shard_map/ppermute | solution.py:479
  107.6 1.7 collective-permute-start.6
  109.3 3.5 %cast_left.1.w_ref = bf16[1536,512]{1,0:T(8,128)(2,1)S(1)} custom-call(f32[1536,1024]{1,0:T(8,128)} %bitcast.41), custom_call_target="tpu_custom_call" | custom-call | bytes 4718592 | tf_op jit(solution)/shard_map/cast_left/pallas_call | solution.py:108
  112.8 2.3 pack.2
  115.1 2.8 %duplicate.1 = (f32[384,1024]{1,0:T(8,128)}, f32[384,1024]{1,0:T(8,128)}) custom-call(f32[384,1024]{1,0:T(8,128)} %refs_0_.3, f32[384,1024]{1,0:T(8,128)} %refs_1_.3), custom_call_target="tpu_custom_call" | custom-call | bytes 6291456 | tf_op jit(solution)/shard_map/duplicate/pallas_call | solution.py:418
  118.9 3.9 %collective-permute-done.7.refs_5_ = f32[384,128]{1,0:T(8,128)} collective-permute-done((f32[384,128]{1,0:T(8,128)}, f32[384,128]{1,0:T(8,128)}, u32[]{:S(2)}, u32[]{:S(2)}) %collective-permute-start.7) | collective-permute-done | bytes 196640 | tf_op jit(solution)/shard_map/ppermute | solution.py:479
  122.8 4.5 %partial_keys.4 = bf16[4,192,512]{2,1,0:T(8,128)(2,1)} custom-call(s32[1]{0:T(128)} %bitcast.4.me_ref, bf16[8,192,1536]{2,1,0:T(8,128)(2,1)} %all-to-all-done.1.x_ref.even_ref.odd_ref, bf16[1536,512]{1,0:T(8,128)(2,1)S(1)} %cast_left.1.w_ref), custom_call_target="tpu_custom_call" | custom-call | flops 1207959552 | bytes 2359296 | tf_op jit(solution)/shard_map/partial_keys/pallas_call | solution.py:152
  127.3 3.8 %all-to-all-start = ((bf16[8,64,1536]{2,1,0:T(8,128)(2,1)}), bf16[8,64,1536]{2,1,0:T(8,128)(2,1)S(1)}, u32[]{:S(2)}, u32[]{:S(2)}) async-start(bf16[8,64,1536]{2,1,0:T(8,128)(2,1)} %pack.2), calls=%async_computation | async-start | bytes 3145728 | tf_op jit(solution)/shard_map/all_to_all | solution.py:517
  131.1 3.8 %partial_keys.5 = (bf16[192,512]{1,0:T(8,128)(2,1)S(1)}, bf16[192,512]{1,0:T(8,128)(2,1)S(1)}, bf16[192,512]{1,0:T(8,128)(2,1)S(1)}, bf16[192,512]{1,0:T(8,128)(2,1)S(1)}) custom-call(s32[1]{0:T(128)} %bitcast.4.me_ref, bf16[8,192,1536]{2,1,0:T(8,128)(2,1)} %all-to-all-done.1.x_ref.even_ref.odd_ref, bf16[1536,512]{1,0:T(8,128)(2,1)S(1)} %cast_left.1.w_ref, ...), custom_call_target="tpu_custom_call" | custom-call | flops 1207959552 | bytes 2359296 | tf_op jit(solution)/shard_map/partial_keys/pallas_call | solution.py:152
  135.0 1.9 collective-permute-start.14
  136.8 1.4 collective-permute-start.15
  138.7 4.2 %transpose_tokens.2.refs_1_ = bf16[1536,1536]{1,0:T(8,128)(2,1)S(1)} custom-call(s32[1]{0:T(128)} %bitcast.4.me_ref, bf16[8,192,1536]{2,1,0:T(8,128)(2,1)} %all-to-all-done.1.x_ref.even_ref.odd_ref, bf16[8,192,1536]{2,1,0:T(8,128)(2,1)} %all-to-all-done.1.x_ref.even_ref.odd_ref), custom_call_target="tpu_custom_call" | custom-call | bytes 9437184 | tf_op jit(solution)/shard_map/transpose_tokens/pallas_call | solution.py:86
  142.9 12.9 %collective-permute-done.14.refs_1_ = bf16[192,512]{1,0:T(8,128)(2,1)S(1)} collective-permute-done((bf16[192,512]{1,0:T(8,128)(2,1)S(1)}, bf16[192,512]{1,0:T(8,128)(2,1)S(1)}, u32[]{:S(2)}, u32[]{:S(2)}) %collective-permute-start.14) | collective-permute-done | bytes 196640 | tf_op jit(solution)/shard_map/ppermute | solution.py:479
  155.8 4.6 %collective-permute-done.16.refs_3_ = bf16[192,512]{1,0:T(8,128)(2,1)S(1)} collective-permute-done((bf16[192,512]{1,0:T(8,128)(2,1)S(1)}, bf16[192,512]{1,0:T(8,128)(2,1)S(1)}, u32[]{:S(2)}, u32[]{:S(2)}) %collective-permute-start.16) | collective-permute-done | bytes 196640 | tf_op jit(solution)/shard_map/ppermute | solution.py:479
  160.4 1.1 key_backward.2.refs_2_
  161.9 1.5 collective-permute-start.20
  163.4 1.5 collective-permute-start.18
  164.9 5.5 %collective-permute-done.22.refs_8_ = bf16[192,512]{1,0:T(8,128)(2,1)} collective-permute-done((bf16[192,512]{1,0:T(8,128)(2,1)}, bf16[192,512]{1,0:T(8,128)(2,1)}, u32[]{:S(2)}, u32[]{:S(2)}) %collective-permute-start.22) | collective-permute-done | bytes 196640 | tf_op jit(solution)/shard_map/ppermute | solution.py:479
  170.5 2.4 collective-permute-done.20.refs_6_
  173.4 4.1 %gradient.4.refs_10_ = f32[1536,512]{1,0:T(8,128)S(1)} custom-call(s32[2]{0:T(128)S(1)} %pad_add_fusion.place_ref.refs_0_, bf16[1536,1536]{1,0:T(8,128)(2,1)S(1)} %transpose_tokens.2.refs_1_, bf16[256,512]{1,0:T(8,128)(2,1)S(1)} %slice.20.refs_2_, bf16[256,512]{1,0:T(8,128)(2,1)S(1)} %copy-done.17, bf16[256,512]{1,0:T(8,128)(2,1)S(1)} %copy-done.14, ...), custom_call_target="tpu_custom_call" | custom-call | flops 2415919104 | bytes 7864320 | tf_op jit(solution)/shard_map/gradient/pallas_call | solution.py:266
  177.6 2.2 copy-done
  179.7 1.7 copy-done.1
  181.5 1.6 partial_keys.6
  183.3 1.3 collective-permute-done.24.add_ref
  184.7 1.6 partial_keys.7
  186.3 1.0 collective-permute-start.25
  187.3 0.8 collective-permute-start.26
  188.1 1.7 collective-permute-start.27
  189.8 0.9 transpose_tokens.3.refs_1_
  190.8 1.5 collective-permute-done.26.refs_2_
  192.3 1.0 collective-permute-done.27.refs_3_
  193.6 1.8 collective-permute-start.33
  195.4 1.3 collective-permute-start.31
  197.1 5.7 %gradient.5.refs_10_ = f32[1536,512]{1,0:T(8,128)S(1)} custom-call(s32[2]{0:T(128)S(1)} %pad_add_fusion.place_ref.refs_0_, bf16[1536,1536]{1,0:T(8,128)(2,1)S(1)} %bitcast.34, bf16[192,512]{1,0:T(8,128)(2,1)} %key_backward.2.refs_2_, bf16[192,512]{1,0:T(8,128)(2,1)} %collective-permute-done.17.refs_3_, bf16[192,512]{1,0:T(8,128)(2,1)} %collective-permute-done.18.refs_4_, ...), custom_call_target="tpu_custom_call" | custom-call | flops 2415919104 | bytes 7864320 | tf_op jit(solution)/shard_map/gradient/pallas_call | solution.py:266
  203.9 4.3 %gradient.6 = (f32[1536,512]{1,0:T(8,128)}, f32[8,128]{1,0:T(8,128)S(1)}, f32[1536,128]{1,0:T(8,128)S(1)}) custom-call(s32[2]{0:T(128)S(1)} %pad_add_fusion.place_ref.refs_0_, bf16[1536,512]{1,0:T(8,128)(2,1)S(1)} %transpose_tokens.3.refs_1_, bf16[256,512]{1,0:T(8,128)(2,1)S(1)} %slice.20.refs_2_, bf16[256,512]{1,0:T(8,128)(2,1)S(1)} %copy-done.18, ...), custom_call_target="tpu_custom_call" | custom-call | flops 805306368 | bytes 4718592 | tf_op jit(solution)/shard_map/gradient/pallas_call | solution.py:266
  208.3 4.3 %gradient.7 = (f32[1536,512]{1,0:T(8,128)}, f32[8,128]{1,0:T(8,128)S(1)}, f32[1536,128]{1,0:T(8,128)S(1)}) custom-call(s32[2]{0:T(128)S(1)} %pad_add_fusion.place_ref.refs_0_, bf16[1536,512]{1,0:T(8,128)(2,1)S(1)} %transpose_tokens.3.refs_1_, bf16[64,512]{1,0:T(8,128)(2,1)S(1)} %key_backward.3.refs_2_, bf16[64,512]{1,0:T(8,128)(2,1)S(1)} %collective-permute-done.28.refs_3_, ...), custom_call_target="tpu_custom_call" | custom-call | flops 805306368 | bytes 4718592 | tf_op jit(solution)/shard_map/gradient/pallas_call | solution.py:266
  212.6 1.1 collective-permute-done.35
  213.7 1.7 collective-permute-start.38
  215.5 1.3 collective-permute-start.37
  217.2 1.0 collective-permute-done.38.refs_3_
  218.2 0.8 collective-permute-done.37.refs_2_
  219.1 1.3 collective-permute-done.36.refs_1_
  220.3 1.5 adam_frag.1
  222.0 2.7 %collective-permute-start.40 = (bf16[384,128]{1,0:T(8,128)(2,1)S(1)}, bf16[384,128]{1,0:T(8,128)(2,1)S(1)}, u32[]{:S(2)}, u32[]{:S(2)}) collective-permute-start(bf16[384,128]{1,0:T(8,128)(2,1)S(1)} %get-tuple-element.81), channel_id=1, source_target_pairs={{0,16},{8,24},{16,0},{24,8},{1,17},{9,25},{17,1},{25,9},{2,18},{10... | collective-permute-start | bytes 294920 | tf_op jit(solution)/shard_map/ppermute | solution.py:479
  224.6 1.7 collective-permute-start.41
  226.3 9.7 %adam_rows.2 = (f32[1536,1024]{1,0:T(8,128)}, f32[1536,1024]{1,0:T(8,128)}, f32[1536,1024]{1,0:T(8,128)}, f32[8,128]{1,0:T(8,128)S(1)}) custom-call(f32[3]{0:T(128)S(1)} %pad_maximum_fusion.sc_ref, f32[1536,1024]{1,0:T(8,128)} %bitcast.42, f32[1536,1024]{1,0:T(8,128)} %bitcast.45, f32[1536,1024]{1,0:T(8,128)} %bitcast.48, ...), custom_call_target="tpu_custom_call" | custom-call | flops 15728640 | bytes 22020096 | tf_op jit(solution)/shard_map/adam_rows/pallas_call | solution.py:325
  236.2 2.2 collective-permute-start.44
  238.4 2.3 collective-permute-start.42
  240.6 9.8 %adam_rows.3 = (f32[1536,1024]{1,0:T(8,128)}, f32[1536,1024]{1,0:T(8,128)}, f32[1536,1024]{1,0:T(8,128)}) custom-call(f32[3]{0:T(128)S(1)} %pad_maximum_fusion.sc_ref, f32[1536,1024]{1,0:T(8,128)} %bitcast.43, f32[1536,1024]{1,0:T(8,128)} %bitcast.46, f32[1536,1024]{1,0:T(8,128)} %bitcast.49, ...), custom_call_target="tpu_custom_call", output_to_operand_aliasing={{0}: (10, {}), {1}: (11, {}), {2}: (12, {})} | custom-call | flops 15728640 | bytes 22020096 | tf_op jit(solution)/shard_map/adam_rows/pallas_call | solution.py:325
  250.5 3.6 %outer_step.1 = (f32[1536,1024]{1,0:T(8,128)}, f32[384,1024]{1,0:T(8,128)}, f32[384,1024]{1,0:T(8,128)}) custom-call(s32[2]{0:T(128)S(1)} %pad_add_fusion.place_ref.refs_0_, f32[1536,1024]{1,0:T(8,128)} %get-tuple-element.76.refs_0_, f32[384,1024]{1,0:T(8,128)} %get-tuple-element.53.refs_1_, ...), custom_call_target="tpu_custom_call", output_to_operand_aliasing={{0}: (1, {}), {1}: (2, {}), {2}: (3, {})} | custom-call | flops 1966080 | bytes 3932160 | tf_op jit(solution)/shard_map/outer_step/pallas_call | solution.py:461
  (131 shorter events, 5.5 us)
Async XLA Ops:
  4.8 118.0 %all-to-all-start.1 = ((bf16[8,192,1536]{2,1,0:T(8,128)(2,1)}), bf16[8,192,1536]{2,1,0:T(8,128)(2,1)}, u32[]{:S(2)}, u32[]{:S(2)}) async-start(bf16[8,192,1536]{2,1,0:T(8,128)(2,1)} %pack.3), calls=%async_computation.1 | async-start | bytes 9437184 | tf_op jit(solution)/shard_map/all_to_all | solution.py:517
  10.2 61.2 %collective-permute-start.2 = (bf16[256,512]{1,0:T(8,128)(2,1)S(1)}, bf16[256,512]{1,0:T(8,128)(2,1)S(1)}, u32[]{:S(2)}, u32[]{:S(2)}) collective-permute-start(bf16[256,512]{1,0:T(8,128)(2,1)S(1)} %slice.20.refs_2_), channel_id=1, source_target_pairs={{0,6},{1,7},{2,4},{3,5},{4,2},{5,3},{6,0},{7,1},{8,14},{9,15},{10,... | collective-permute-start | bytes 786440 | tf_op jit(solution)/shard_map/ppermute | solution.py:479
  13.5 61.6 %collective-permute-start.1 = (bf16[256,512]{1,0:T(8,128)(2,1)S(1)}, bf16[256,512]{1,0:T(8,128)(2,1)S(1)}, u32[]{:S(2)}, u32[]{:S(2)}) collective-permute-start(bf16[256,512]{1,0:T(8,128)(2,1)S(1)} %slice.20.refs_2_), channel_id=1, source_target_pairs={{0,4},{1,5},{2,6},{3,7},{4,0},{5,1},{6,2},{7,3},{8,12},{9,13},{10,... | collective-permute-start | bytes 786440 | tf_op jit(solution)/shard_map/ppermute | solution.py:479
  14.0 61.2 %collective-permute-start = (bf16[256,512]{1,0:T(8,128)(2,1)S(1)}, bf16[256,512]{1,0:T(8,128)(2,1)S(1)}, u32[]{:S(2)}, u32[]{:S(2)}) collective-permute-start(bf16[256,512]{1,0:T(8,128)(2,1)S(1)} %slice.20.refs_2_), channel_id=1, source_target_pairs={{0,2},{1,3},{2,0},{3,1},{4,6},{5,7},{6,4},{7,5},{8,10},{9,11},{10,... | collective-permute-start | bytes 786440 | tf_op jit(solution)/shard_map/ppermute | solution.py:479
  71.3 16.9 %copy-start.7 = (bf16[256,512]{1,0:T(8,128)(2,1)}, bf16[256,512]{1,0:T(8,128)(2,1)S(1)}, u32[]{:S(2)}) copy-start(bf16[256,512]{1,0:T(8,128)(2,1)S(1)} %collective-permute-done.2.refs_8_) | copy-start | bytes 786436
  75.1 13.6 %copy-start.10 = (bf16[256,512]{1,0:T(8,128)(2,1)}, bf16[256,512]{1,0:T(8,128)(2,1)S(1)}, u32[]{:S(2)}) copy-start(bf16[256,512]{1,0:T(8,128)(2,1)S(1)} %collective-permute-done.1.refs_6_) | copy-start | bytes 786436
  75.2 20.7 %copy-start.13 = (bf16[256,512]{1,0:T(8,128)(2,1)}, bf16[256,512]{1,0:T(8,128)(2,1)S(1)}, u32[]{:S(2)}) copy-start(bf16[256,512]{1,0:T(8,128)(2,1)S(1)} %collective-permute-done.refs_4_) | copy-start | bytes 786436
  80.9 7.9 %collective-permute-start.3 = (f32[384,128]{1,0:T(8,128)S(1)}, f32[384,128]{1,0:T(8,128)S(1)}, u32[]{:S(2)}, u32[]{:S(2)}) collective-permute-start(f32[384,128]{1,0:T(8,128)S(1)} %get-tuple-element.94), channel_id=1, source_target_pairs={{0,8},{8,0},{16,24},{24,16},{1,9},{9,1},{17,25},{25,17},{2,10},{10... | collective-permute-start | bytes 589832 | tf_op jit(solution)/shard_map/ppermute | solution.py:479
  83.3 12.6 %collective-permute-start.5 = (f32[384,128]{1,0:T(8,128)S(1)}, f32[384,128]{1,0:T(8,128)S(1)}, u32[]{:S(2)}, u32[]{:S(2)}) collective-permute-start(f32[384,128]{1,0:T(8,128)S(1)} %get-tuple-element.95), channel_id=1, source_target_pairs={{0,24},{8,16},{16,8},{24,0},{1,25},{9,17},{17,9},{25,1},{2,26},{10... | collective-permute-start | bytes 589832 | tf_op jit(solution)/shard_map/ppermute | solution.py:479
  85.8 17.2 %collective-permute-start.4 = (f32[384,128]{1,0:T(8,128)S(1)}, f32[384,128]{1,0:T(8,128)S(1)}, u32[]{:S(2)}, u32[]{:S(2)}) collective-permute-start(f32[384,128]{1,0:T(8,128)S(1)} %get-tuple-element.96), channel_id=1, source_target_pairs={{0,16},{8,24},{16,0},{24,8},{1,17},{9,25},{17,1},{25,9},{2,18},{10... | collective-permute-start | bytes 589832 | tf_op jit(solution)/shard_map/ppermute | solution.py:479
  85.9 21.7 %collective-permute-start.9 = (bf16[256,512]{1,0:T(8,128)(2,1)S(1)}, bf16[256,512]{1,0:T(8,128)(2,1)S(1)}, u32[]{:S(2)}, u32[]{:S(2)}) collective-permute-start(bf16[256,512]{1,0:T(8,128)(2,1)S(1)} %slice.20.refs_2_), channel_id=1, source_target_pairs={{0,1},{1,0},{2,3},{3,2},{4,5},{5,4},{6,7},{7,6},{8,9},{9,8},{10,11... | collective-permute-start | bytes 786440 | tf_op jit(solution)/shard_map/ppermute | solution.py:479
  88.2 19.3 %collective-permute-start.12 = (bf16[256,512]{1,0:T(8,128)(2,1)S(1)}, bf16[256,512]{1,0:T(8,128)(2,1)S(1)}, u32[]{:S(2)}, u32[]{:S(2)}) collective-permute-start(bf16[256,512]{1,0:T(8,128)(2,1)S(1)} %collective-permute-done.2.refs_8_), channel_id=1, source_target_pairs={{0,1},{1,0},{2,3},{3,2},{4,5},{5,4},{6,7},{7,6},{8,9},{9,8},{10,11... | collective-permute-start | bytes 786440 | tf_op jit(solution)/shard_map/ppermute | solution.py:479
  88.8 30.1 %collective-permute-start.11 = (bf16[256,512]{1,0:T(8,128)(2,1)S(1)}, bf16[256,512]{1,0:T(8,128)(2,1)S(1)}, u32[]{:S(2)}, u32[]{:S(2)}) collective-permute-start(bf16[256,512]{1,0:T(8,128)(2,1)S(1)} %collective-permute-done.1.refs_6_), channel_id=1, source_target_pairs={{0,1},{1,0},{2,3},{3,2},{4,5},{5,4},{6,7},{7,6},{8,9},{9,8},{10,11... | collective-permute-start | bytes 786440 | tf_op jit(solution)/shard_map/ppermute | solution.py:479
  95.9 23.0 %collective-permute-start.10 = (bf16[256,512]{1,0:T(8,128)(2,1)S(1)}, bf16[256,512]{1,0:T(8,128)(2,1)S(1)}, u32[]{:S(2)}, u32[]{:S(2)}) collective-permute-start(bf16[256,512]{1,0:T(8,128)(2,1)S(1)} %collective-permute-done.refs_4_), channel_id=1, source_target_pairs={{0,1},{1,0},{2,3},{3,2},{4,5},{5,4},{6,7},{7,6},{8,9},{9,8},{10,11... | collective-permute-start | bytes 786440 | tf_op jit(solution)/shard_map/ppermute | solution.py:479
  104.9 14.0 %collective-permute-start.8 = (f32[384,128]{1,0:T(8,128)}, f32[384,128]{1,0:T(8,128)}, u32[]{:S(2)}, u32[]{:S(2)}) collective-permute-start(f32[384,128]{1,0:T(8,128)} %get-tuple-element.92.refs_3_), channel_id=1, source_target_pairs={{0,24},{8,16},{16,8},{24,0},{1,25},{9,17},{17,9},{25,1},{2,26},{10... | collective-permute-start | bytes 589832 | tf_op jit(solution)/shard_map/ppermute | solution.py:479
  107.6 15.2 %collective-permute-start.7 = (f32[384,128]{1,0:T(8,128)}, f32[384,128]{1,0:T(8,128)}, u32[]{:S(2)}, u32[]{:S(2)}) collective-permute-start(f32[384,128]{1,0:T(8,128)} %get-tuple-element.92.refs_3_), channel_id=1, source_target_pairs={{0,16},{8,24},{16,0},{24,8},{1,17},{9,25},{17,1},{25,9},{2,18},{10... | collective-permute-start | bytes 589832 | tf_op jit(solution)/shard_map/ppermute | solution.py:479
  107.6 15.2 %collective-permute-start.6 = (f32[384,128]{1,0:T(8,128)}, f32[384,128]{1,0:T(8,128)}, u32[]{:S(2)}, u32[]{:S(2)}) collective-permute-start(f32[384,128]{1,0:T(8,128)} %get-tuple-element.92.refs_3_), channel_id=1, source_target_pairs={{0,8},{8,0},{16,24},{24,16},{1,9},{9,1},{17,25},{25,17},{2,10},{10... | collective-permute-start | bytes 589832 | tf_op jit(solution)/shard_map/ppermute | solution.py:479
  127.3 3.8 %collective-permute-start.13 = (bf16[4,192,512]{2,1,0:T(8,128)(2,1)}, bf16[4,192,512]{2,1,0:T(8,128)(2,1)}, u32[]{:S(2)}, u32[]{:S(2)}) collective-permute-start(bf16[4,192,512]{2,1,0:T(8,128)(2,1)} %partial_keys.4), channel_id=1, source_target_pairs={{0,1},{1,0},{2,3},{3,2},{4,5},{5,4},{6,7},{7,6},{8,9},{9,8},{10,11... | collective-permute-start | bytes 2359304 | tf_op jit(solution)/shard_map/ppermute | solution.py:479
  127.3 54.1 %all-to-all-start = ((bf16[8,64,1536]{2,1,0:T(8,128)(2,1)}), bf16[8,64,1536]{2,1,0:T(8,128)(2,1)S(1)}, u32[]{:S(2)}, u32[]{:S(2)}) async-start(bf16[8,64,1536]{2,1,0:T(8,128)(2,1)} %pack.2), calls=%async_computation | async-start | bytes 3145728 | tf_op jit(solution)/shard_map/all_to_all | solution.py:517
  135.0 20.8 %collective-permute-start.14 = (bf16[192,512]{1,0:T(8,128)(2,1)S(1)}, bf16[192,512]{1,0:T(8,128)(2,1)S(1)}, u32[]{:S(2)}, u32[]{:S(2)}) collective-permute-start(bf16[192,512]{1,0:T(8,128)(2,1)S(1)} %get-tuple-element.59), channel_id=1, source_target_pairs={{0,2},{1,3},{2,0},{3,1},{4,6},{5,7},{6,4},{7,5},{8,10},{9,11},{10,... | collective-permute-start | bytes 589832 | tf_op jit(solution)/shard_map/ppermute | solution.py:479
  136.8 18.9 %collective-permute-start.15 = (bf16[192,512]{1,0:T(8,128)(2,1)S(1)}, bf16[192,512]{1,0:T(8,128)(2,1)S(1)}, u32[]{:S(2)}, u32[]{:S(2)}) collective-permute-start(bf16[192,512]{1,0:T(8,128)(2,1)S(1)} %get-tuple-element.60), channel_id=1, source_target_pairs={{0,4},{1,5},{2,6},{3,7},{4,0},{5,1},{6,2},{7,3},{8,12},{9,13},{10,... | collective-permute-start | bytes 589832 | tf_op jit(solution)/shard_map/ppermute | solution.py:479
  138.3 22.1 %copy-start.4 = (bf16[1,256,1024]{2,1,0:T(8,128)(2,1)S(1)}, bf16[1,256,1024]{2,1,0:T(8,128)(2,1)}, u32[]{:S(2)}) copy-start(bf16[1,256,1024]{2,1,0:T(8,128)(2,1)} %param.10) | copy-start | bytes 1572868
  138.3 35.1 %copy-start.8 = (bf16[256,512]{1,0:T(8,128)(2,1)S(1)}, bf16[256,512]{1,0:T(8,128)(2,1)}, u32[]{:S(2)}) copy-start(bf16[256,512]{1,0:T(8,128)(2,1)} %copy-done.7) | copy-start | bytes 786436
  138.3 35.1 %copy-start.11 = (bf16[256,512]{1,0:T(8,128)(2,1)S(1)}, bf16[256,512]{1,0:T(8,128)(2,1)}, u32[]{:S(2)}) copy-start(bf16[256,512]{1,0:T(8,128)(2,1)} %copy-done.10) | copy-start | bytes 786436
  138.3 35.1 %copy-start.14 = (bf16[256,512]{1,0:T(8,128)(2,1)S(1)}, bf16[256,512]{1,0:T(8,128)(2,1)}, u32[]{:S(2)}) copy-start(bf16[256,512]{1,0:T(8,128)(2,1)} %copy-done.13) | copy-start | bytes 786436
  138.3 35.1 %copy-start.17 = (bf16[256,512]{1,0:T(8,128)(2,1)S(1)}, bf16[256,512]{1,0:T(8,128)(2,1)}, u32[]{:S(2)}) copy-start(bf16[256,512]{1,0:T(8,128)(2,1)} %copy-done.16) | copy-start | bytes 786436
  138.3 35.1 %copy-start.20 = (bf16[256,512]{1,0:T(8,128)(2,1)S(1)}, bf16[256,512]{1,0:T(8,128)(2,1)}, u32[]{:S(2)}) copy-start(bf16[256,512]{1,0:T(8,128)(2,1)} %copy-done.19) | copy-start | bytes 786436
  138.3 35.1 %copy-start.23 = (bf16[256,512]{1,0:T(8,128)(2,1)S(1)}, bf16[256,512]{1,0:T(8,128)(2,1)}, u32[]{:S(2)}) copy-start(bf16[256,512]{1,0:T(8,128)(2,1)} %copy-done.22) | copy-start | bytes 786436
  138.3 35.1 %copy-start.26 = (bf16[256,512]{1,0:T(8,128)(2,1)S(1)}, bf16[256,512]{1,0:T(8,128)(2,1)}, u32[]{:S(2)}) copy-start(bf16[256,512]{1,0:T(8,128)(2,1)} %copy-done.25) | copy-start | bytes 786436
  138.3 22.0 %collective-permute-start.16 = (bf16[192,512]{1,0:T(8,128)(2,1)S(1)}, bf16[192,512]{1,0:T(8,128)(2,1)S(1)}, u32[]{:S(2)}, u32[]{:S(2)}) collective-permute-start(bf16[192,512]{1,0:T(8,128)(2,1)S(1)} %get-tuple-element.61), channel_id=1, source_target_pairs={{0,6},{1,7},{2,4},{3,5},{4,2},{5,3},{6,0},{7,1},{8,14},{9,15},{10,... | collective-permute-start | bytes 589832 | tf_op jit(solution)/shard_map/ppermute | solution.py:479
  161.4 9.0 %collective-permute-start.22 = (bf16[192,512]{1,0:T(8,128)(2,1)}, bf16[192,512]{1,0:T(8,128)(2,1)}, u32[]{:S(2)}, u32[]{:S(2)}) collective-permute-start(bf16[192,512]{1,0:T(8,128)(2,1)} %key_backward.2.refs_2_), channel_id=1, source_target_pairs={{0,6},{1,7},{2,4},{3,5},{4,2},{5,3},{6,0},{7,1},{8,14},{9,15},{10,... | collective-permute-start | bytes 589832 | tf_op jit(solution)/shard_map/ppermute | solution.py:479
  161.9 10.9 %collective-permute-start.20 = (bf16[192,512]{1,0:T(8,128)(2,1)}, bf16[192,512]{1,0:T(8,128)(2,1)}, u32[]{:S(2)}, u32[]{:S(2)}) collective-permute-start(bf16[192,512]{1,0:T(8,128)(2,1)} %key_backward.2.refs_2_), channel_id=1, source_target_pairs={{0,4},{1,5},{2,6},{3,7},{4,0},{5,1},{6,2},{7,3},{8,12},{9,13},{10,... | collective-permute-start | bytes 589832 | tf_op jit(solution)/shard_map/ppermute | solution.py:479
  163.4 9.7 %collective-permute-start.18 = (bf16[192,512]{1,0:T(8,128)(2,1)}, bf16[192,512]{1,0:T(8,128)(2,1)}, u32[]{:S(2)}, u32[]{:S(2)}) collective-permute-start(bf16[192,512]{1,0:T(8,128)(2,1)} %key_backward.2.refs_2_), channel_id=1, source_target_pairs={{0,2},{1,3},{2,0},{3,1},{4,6},{5,7},{6,4},{7,5},{8,10},{9,11},{10,... | collective-permute-start | bytes 589832 | tf_op jit(solution)/shard_map/ppermute | solution.py:479
  164.9 16.5 %collective-permute-start.17 = (bf16[192,512]{1,0:T(8,128)(2,1)}, bf16[192,512]{1,0:T(8,128)(2,1)}, u32[]{:S(2)}, u32[]{:S(2)}) collective-permute-start(bf16[192,512]{1,0:T(8,128)(2,1)} %key_backward.2.refs_2_), channel_id=1, source_target_pairs={{0,1},{1,0},{2,3},{3,2},{4,5},{5,4},{6,7},{7,6},{8,9},{9,8},{10,11... | collective-permute-start | bytes 589832 | tf_op jit(solution)/shard_map/ppermute | solution.py:479
  170.5 11.0 %collective-permute-start.23 = (bf16[192,512]{1,0:T(8,128)(2,1)}, bf16[192,512]{1,0:T(8,128)(2,1)}, u32[]{:S(2)}, u32[]{:S(2)}) collective-permute-start(bf16[192,512]{1,0:T(8,128)(2,1)} %collective-permute-done.22.refs_8_), channel_id=1, source_target_pairs={{0,1},{1,0},{2,3},{3,2},{4,5},{5,4},{6,7},{7,6},{8,9},{9,8},{10,11... | collective-permute-start | bytes 589832 | tf_op jit(solution)/shard_map/ppermute | solution.py:479
  172.9 8.6 %collective-permute-start.21 = (bf16[192,512]{1,0:T(8,128)(2,1)}, bf16[192,512]{1,0:T(8,128)(2,1)}, u32[]{:S(2)}, u32[]{:S(2)}) collective-permute-start(bf16[192,512]{1,0:T(8,128)(2,1)} %collective-permute-done.20.refs_6_), channel_id=1, source_target_pairs={{0,1},{1,0},{2,3},{3,2},{4,5},{5,4},{6,7},{7,6},{8,9},{9,8},{10,11... | collective-permute-start | bytes 589832 | tf_op jit(solution)/shard_map/ppermute | solution.py:479
  173.1 8.3 %collective-permute-start.19 = (bf16[192,512]{1,0:T(8,128)(2,1)}, bf16[192,512]{1,0:T(8,128)(2,1)}, u32[]{:S(2)}, u32[]{:S(2)}) collective-permute-start(bf16[192,512]{1,0:T(8,128)(2,1)} %collective-permute-done.18.refs_4_), channel_id=1, source_target_pairs={{0,1},{1,0},{2,3},{3,2},{4,5},{5,4},{6,7},{7,6},{8,9},{9,8},{10,11... | collective-permute-start | bytes 589832 | tf_op jit(solution)/shard_map/ppermute | solution.py:479
  181.4 15.7 %slice-start = ((s8[4718592]{0:T(1024)(128)(4,1)}), s8[4194304]{0:T(1024)(128)(4,1)S(1)}, s32[]{:S(2)}) async-start(s8[4718592]{0:T(1024)(128)(4,1)} %bitcast.33), calls=%async_computation.2 | async-start | bytes 8388608
  183.1 14.1 %slice-start.1 = ((s8[4718592]{0:T(1024)(128)(4,1)}), s8[524288]{0:T(1024)(128)(4,1)S(1)}, s32[]{:S(2)}) async-start(s8[4718592]{0:T(1024)(128)(4,1)} %bitcast.33), calls=%async_computation.3 | async-start | bytes 1048576
  183.1 1.6 collective-permute-start.24
  186.3 4.5 %collective-permute-start.25 = (bf16[64,512]{1,0:T(8,128)(2,1)S(1)}, bf16[64,512]{1,0:T(8,128)(2,1)S(1)}, u32[]{:S(2)}, u32[]{:S(2)}) collective-permute-start(bf16[64,512]{1,0:T(8,128)(2,1)S(1)} %get-tuple-element.65), channel_id=1, source_target_pairs={{0,2},{1,3},{2,0},{3,1},{4,6},{5,7},{6,4},{7,5},{8,10},{9,11},{10,... | collective-permute-start | bytes 196616 | tf_op jit(solution)/shard_map/ppermute | solution.py:479
  187.3 5.0 %collective-permute-start.26 = (bf16[64,512]{1,0:T(8,128)(2,1)S(1)}, bf16[64,512]{1,0:T(8,128)(2,1)S(1)}, u32[]{:S(2)}, u32[]{:S(2)}) collective-permute-start(bf16[64,512]{1,0:T(8,128)(2,1)S(1)} %get-tuple-element.66), channel_id=1, source_target_pairs={{0,4},{1,5},{2,6},{3,7},{4,0},{5,1},{6,2},{7,3},{8,12},{9,13},{10,... | collective-permute-start | bytes 196616 | tf_op jit(solution)/shard_map/ppermute | solution.py:479
  188.1 5.2 %collective-permute-start.27 = (bf16[64,512]{1,0:T(8,128)(2,1)S(1)}, bf16[64,512]{1,0:T(8,128)(2,1)S(1)}, u32[]{:S(2)}, u32[]{:S(2)}) collective-permute-start(bf16[64,512]{1,0:T(8,128)(2,1)S(1)} %get-tuple-element.67), channel_id=1, source_target_pairs={{0,6},{1,7},{2,4},{3,5},{4,2},{5,3},{6,0},{7,1},{8,14},{9,15},{10,... | collective-permute-start | bytes 196616 | tf_op jit(solution)/shard_map/ppermute | solution.py:479
  193.5 10.4 %copy-start.2 = (f32[1536,512]{1,0:T(8,128)S(1)}, f32[1536,512]{1,0:T(8,128)}, u32[]{:S(2)}) copy-start(f32[1536,512]{1,0:T(8,128)} %copy-done.1) | copy-start | bytes 9437188
  193.6 9.3 %collective-permute-start.33 = (bf16[64,512]{1,0:T(8,128)(2,1)S(1)}, bf16[64,512]{1,0:T(8,128)(2,1)S(1)}, u32[]{:S(2)}, u32[]{:S(2)}) collective-permute-start(bf16[64,512]{1,0:T(8,128)(2,1)S(1)} %key_backward.3.refs_2_), channel_id=1, source_target_pairs={{0,6},{1,7},{2,4},{3,5},{4,2},{5,3},{6,0},{7,1},{8,14},{9,15},{10,... | collective-permute-start | bytes 196616 | tf_op jit(solution)/shard_map/ppermute | solution.py:479
  195.4 8.0 %collective-permute-start.31 = (bf16[64,512]{1,0:T(8,128)(2,1)S(1)}, bf16[64,512]{1,0:T(8,128)(2,1)S(1)}, u32[]{:S(2)}, u32[]{:S(2)}) collective-permute-start(bf16[64,512]{1,0:T(8,128)(2,1)S(1)} %key_backward.3.refs_2_), channel_id=1, source_target_pairs={{0,4},{1,5},{2,6},{3,7},{4,0},{5,1},{6,2},{7,3},{8,12},{9,13},{10,... | collective-permute-start | bytes 196616 | tf_op jit(solution)/shard_map/ppermute | solution.py:479
  196.6 6.8 %collective-permute-start.29 = (bf16[64,512]{1,0:T(8,128)(2,1)S(1)}, bf16[64,512]{1,0:T(8,128)(2,1)S(1)}, u32[]{:S(2)}, u32[]{:S(2)}) collective-permute-start(bf16[64,512]{1,0:T(8,128)(2,1)S(1)} %key_backward.3.refs_2_), channel_id=1, source_target_pairs={{0,2},{1,3},{2,0},{3,1},{4,6},{5,7},{6,4},{7,5},{8,10},{9,11},{10,... | collective-permute-start | bytes 196616 | tf_op jit(solution)/shard_map/ppermute | solution.py:479
  202.8 5.4 %collective-permute-start.28 = (bf16[64,512]{1,0:T(8,128)(2,1)S(1)}, bf16[64,512]{1,0:T(8,128)(2,1)S(1)}, u32[]{:S(2)}, u32[]{:S(2)}) collective-permute-start(bf16[64,512]{1,0:T(8,128)(2,1)S(1)} %key_backward.3.refs_2_), channel_id=1, source_target_pairs={{0,1},{1,0},{2,3},{3,2},{4,5},{5,4},{6,7},{7,6},{8,9},{9,8},{10,11... | collective-permute-start | bytes 196616 | tf_op jit(solution)/shard_map/ppermute | solution.py:479
  202.9 5.3 %collective-permute-start.34 = (bf16[64,512]{1,0:T(8,128)(2,1)S(1)}, bf16[64,512]{1,0:T(8,128)(2,1)S(1)}, u32[]{:S(2)}, u32[]{:S(2)}) collective-permute-start(bf16[64,512]{1,0:T(8,128)(2,1)S(1)} %collective-permute-done.33.refs_8_), channel_id=1, source_target_pairs={{0,1},{1,0},{2,3},{3,2},{4,5},{5,4},{6,7},{7,6},{8,9},{9,8},{10,11... | collective-permute-start | bytes 196616 | tf_op jit(solution)/shard_map/ppermute | solution.py:479
  203.4 4.9 %collective-permute-start.32 = (bf16[64,512]{1,0:T(8,128)(2,1)S(1)}, bf16[64,512]{1,0:T(8,128)(2,1)S(1)}, u32[]{:S(2)}, u32[]{:S(2)}) collective-permute-start(bf16[64,512]{1,0:T(8,128)(2,1)S(1)} %collective-permute-done.31.refs_6_), channel_id=1, source_target_pairs={{0,1},{1,0},{2,3},{3,2},{4,5},{5,4},{6,7},{7,6},{8,9},{9,8},{10,11... | collective-permute-start | bytes 196616 | tf_op jit(solution)/shard_map/ppermute | solution.py:479
  203.5 4.8 %collective-permute-start.30 = (bf16[64,512]{1,0:T(8,128)(2,1)S(1)}, bf16[64,512]{1,0:T(8,128)(2,1)S(1)}, u32[]{:S(2)}, u32[]{:S(2)}) collective-permute-start(bf16[64,512]{1,0:T(8,128)(2,1)S(1)} %collective-permute-done.29.refs_4_), channel_id=1, source_target_pairs={{0,1},{1,0},{2,3},{3,2},{4,5},{5,4},{6,7},{7,6},{8,9},{9,8},{10,11... | collective-permute-start | bytes 196616 | tf_op jit(solution)/shard_map/ppermute | solution.py:479
  208.2 12.1 %copy-start.6 = (f32[4,384,128]{2,1,0:T(8,128)S(1)}, f32[4,384,128]{2,1,0:T(8,128)}, u32[]{:S(2)}) copy-start(f32[4,384,128]{2,1,0:T(8,128)} %get-tuple-element.52.w_ref) | copy-start | bytes 2359300
  208.2 12.1 %copy-start.28 = (f32[4,384,128]{2,1,0:T(8,128)S(1)}, f32[4,384,128]{2,1,0:T(8,128)}, u32[]{:S(2)}) copy-start(f32[4,384,128]{2,1,0:T(8,128)} %get-tuple-element.77.m_ref) | copy-start | bytes 2359300
  208.2 12.1 %copy-start.29 = (f32[4,384,128]{2,1,0:T(8,128)S(1)}, f32[4,384,128]{2,1,0:T(8,128)}, u32[]{:S(2)}) copy-start(f32[4,384,128]{2,1,0:T(8,128)} %get-tuple-element.55.v_ref) | copy-start | bytes 2359300
  212.5 1.2 collective-permute-start.35
  213.7 4.5 %collective-permute-start.38 = (f32[8,128]{1,0:T(8,128)S(1)}, f32[8,128]{1,0:T(8,128)S(1)}, u32[]{:S(2)}, u32[]{:S(2)}) collective-permute-start(f32[8,128]{1,0:T(8,128)S(1)} %add.32.refs_0_), channel_id=1, source_target_pairs={{0,6},{1,7},{2,4},{3,5},{4,2},{5,3},{6,0},{7,1},{8,14},{9,15},{10,... | collective-permute-start | bytes 12296 | tf_op jit(solution)/shard_map/ppermute | solution.py:479
  215.5 3.6 %collective-permute-start.37 = (f32[8,128]{1,0:T(8,128)S(1)}, f32[8,128]{1,0:T(8,128)S(1)}, u32[]{:S(2)}, u32[]{:S(2)}) collective-permute-start(f32[8,128]{1,0:T(8,128)S(1)} %add.32.refs_0_), channel_id=1, source_target_pairs={{0,4},{1,5},{2,6},{3,7},{4,0},{5,1},{6,2},{7,3},{8,12},{9,13},{10,... | collective-permute-start | bytes 12296 | tf_op jit(solution)/shard_map/ppermute | solution.py:479
  216.7 3.6 %collective-permute-start.36 = (f32[8,128]{1,0:T(8,128)S(1)}, f32[8,128]{1,0:T(8,128)S(1)}, u32[]{:S(2)}, u32[]{:S(2)}) collective-permute-start(f32[8,128]{1,0:T(8,128)S(1)} %add.32.refs_0_), channel_id=1, source_target_pairs={{0,2},{1,3},{2,0},{3,1},{4,6},{5,7},{6,4},{7,5},{8,10},{9,11},{10,... | collective-permute-start | bytes 12296 | tf_op jit(solution)/shard_map/ppermute | solution.py:479
  221.9 14.2 %collective-permute-start.39 = (bf16[384,128]{1,0:T(8,128)(2,1)S(1)}, bf16[384,128]{1,0:T(8,128)(2,1)S(1)}, u32[]{:S(2)}, u32[]{:S(2)}) collective-permute-start(bf16[384,128]{1,0:T(8,128)(2,1)S(1)} %get-tuple-element.80), channel_id=1, source_target_pairs={{0,8},{8,0},{16,24},{24,16},{1,9},{9,1},{17,25},{25,17},{2,10},{10... | collective-permute-start | bytes 294920 | tf_op jit(solution)/shard_map/ppermute | solution.py:479
  222.0 14.1 %collective-permute-start.40 = (bf16[384,128]{1,0:T(8,128)(2,1)S(1)}, bf16[384,128]{1,0:T(8,128)(2,1)S(1)}, u32[]{:S(2)}, u32[]{:S(2)}) collective-permute-start(bf16[384,128]{1,0:T(8,128)(2,1)S(1)} %get-tuple-element.81), channel_id=1, source_target_pairs={{0,16},{8,24},{16,0},{24,8},{1,17},{9,25},{17,1},{25,9},{2,18},{10... | collective-permute-start | bytes 294920 | tf_op jit(solution)/shard_map/ppermute | solution.py:479
  224.6 11.5 %collective-permute-start.41 = (bf16[384,128]{1,0:T(8,128)(2,1)S(1)}, bf16[384,128]{1,0:T(8,128)(2,1)S(1)}, u32[]{:S(2)}, u32[]{:S(2)}) collective-permute-start(bf16[384,128]{1,0:T(8,128)(2,1)S(1)} %get-tuple-element.82), channel_id=1, source_target_pairs={{0,24},{8,16},{16,8},{24,0},{1,25},{9,17},{17,9},{25,1},{2,26},{10... | collective-permute-start | bytes 294920 | tf_op jit(solution)/shard_map/ppermute | solution.py:479
  236.2 14.3 %collective-permute-start.44 = (bf16[384,128]{1,0:T(8,128)(2,1)S(1)}, bf16[384,128]{1,0:T(8,128)(2,1)S(1)}, u32[]{:S(2)}, u32[]{:S(2)}) collective-permute-start(bf16[384,128]{1,0:T(8,128)(2,1)S(1)} %convert_element_type.24.refs_7_), channel_id=1, source_target_pairs={{0,24},{8,16},{16,8},{24,0},{1,25},{9,17},{17,9},{25,1},{2,26},{10... | collective-permute-start | bytes 294920 | tf_op jit(solution)/shard_map/ppermute | solution.py:479
  238.4 12.1 %collective-permute-start.43 = (bf16[384,128]{1,0:T(8,128)(2,1)S(1)}, bf16[384,128]{1,0:T(8,128)(2,1)S(1)}, u32[]{:S(2)}, u32[]{:S(2)}) collective-permute-start(bf16[384,128]{1,0:T(8,128)(2,1)S(1)} %convert_element_type.24.refs_7_), channel_id=1, source_target_pairs={{0,16},{8,24},{16,0},{24,8},{1,17},{9,25},{17,1},{25,9},{2,18},{10... | collective-permute-start | bytes 294920 | tf_op jit(solution)/shard_map/ppermute | solution.py:479
  238.4 12.1 %collective-permute-start.42 = (bf16[384,128]{1,0:T(8,128)(2,1)S(1)}, bf16[384,128]{1,0:T(8,128)(2,1)S(1)}, u32[]{:S(2)}, u32[]{:S(2)}) collective-permute-start(bf16[384,128]{1,0:T(8,128)(2,1)S(1)} %convert_element_type.24.refs_7_), channel_id=1, source_target_pairs={{0,8},{8,0},{16,24},{24,16},{1,9},{9,1},{17,25},{25,17},{2,10},{10... | collective-permute-start | bytes 294920 | tf_op jit(solution)/shard_map/ppermute | solution.py:479
  (18 other events, 153.6 us)

commit v8 on v7

--- a/solution.py
+++ b/solution.py
@@ -38,64 +38,48 @@
     return pl.CostEstimate(flops=int(flops), bytes_accessed=int(moved), transcendentals=0)
 
 
-def pack_kernel(first, src_ref, out_ref, held, in_sems, out_sems):
-    shards, count, rows = out_ref.shape
-
-    def fetch(s):
-        block = src_ref.at[pl.ds(first, count), pl.ds(s * rows, rows)]
-        return pltpu.make_async_copy(block, held.at[s], in_sems.at[s])
-
-    def store(s):
-        return pltpu.make_async_copy(held.at[s], out_ref.at[s], out_sems.at[s])
-
-    for s in range(shards):
-        fetch(s).start()
-    for s in range(shards):
-        fetch(s).wait()
-        store(s).start()
-    for s in range(shards):
-        store(s).wait()
-
-
-def pack(tokens, first, count, rows):
-    shards = tokens.shape[1] // rows
-    shape = (shards, count, rows)
-    return pl.pallas_call(
-        functools.partial(pack_kernel, first),
-        out_shape=pltpu.HBM(shape, tokens.dtype),
-        in_specs=[pl.BlockSpec(memory_space=pl.ANY)],
-        out_specs=pl.BlockSpec(memory_space=pl.ANY),
+def pack_kernel(offsets, me_ref, src_ref, *refs):
+    half = len(offsets)
+    out_refs, (held, in_sems, out_sems) = refs[:half], refs[half:]
+    streams = in_sems.shape[1]
+    count, rows = out_refs[0].shape
+    step = count // streams
+    fetches, stores = [], []
+    for i, offset in enumerate(offsets):
+        column = pl.multiple_of((me_ref[0] ^ offset) * rows, HEAD)
+        for j in range(streams):
+            at = pl.ds(j * step, step)
+            block = src_ref.at[at, pl.ds(column, rows)]
+            fetches.append(pltpu.make_async_copy(block, held.at[i, at], in_sems.at[i, j]))
+            stores.append(pltpu.make_async_copy(held.at[i, at], out_refs[i].at[at], out_sems.at[i, j]))
+    for copy in fetches:
+        copy.start()
+    for fetch, store in zip(fetches, stores):
+        fetch.wait()
+        store.start()
+    for copy in stores:
+        copy.wait()
+
+
+def pack(tokens, me, rows, offsets):
+    count = tokens.shape[0]
+    streams = 4
+    whole = pl.BlockSpec(memory_space=pl.ANY)
+    outs = pl.pallas_call(
+        functools.partial(pack_kernel, offsets),
+        out_shape=[pltpu.HBM((count, rows), tokens.dtype)] * len(offsets),
+        in_specs=[pl.BlockSpec(memory_space=pltpu.SMEM), whole],
+        out_specs=[whole] * len(offsets),
         scratch_shapes=[
-            pltpu.VMEM(shape, tokens.dtype),
-            pltpu.SemaphoreType.DMA((shards,)),
-            pltpu.SemaphoreType.DMA((shards,)),
+            pltpu.VMEM((len(offsets), count, rows), tokens.dtype),
+            pltpu.SemaphoreType.DMA((len(offsets), streams)),
+            pltpu.SemaphoreType.DMA((len(offsets), streams)),
         ],
         compiler_params=params_of(12),
-        cost_estimate=cost(0, 4 * shards * count * rows),
+        cost_estimate=cost(0, 4 * len(offsets) * count * rows),
         name="pack",
-    )(*in_hbm(tokens))
-
-
-def transpose_kernel(me_ref, even_ref, odd_ref, out_ref):
-    out_ref[...] = jnp.concatenate([even_ref[0], odd_ref[0]], axis=0).T
-
-
-def transpose_tokens(blocks, me):
-    shards, count, rows = blocks.shape
-    block = lambda odd: pl.BlockSpec((1, count, rows), lambda m, me: (me[0] ^ (2 * m + odd), 0, 0))
-    return pl.pallas_call(
-        transpose_kernel,
-        out_shape=jax.ShapeDtypeStruct((rows, shards * count), blocks.dtype),
-        grid_spec=pltpu.PrefetchScalarGridSpec(
-            num_scalar_prefetch=1,
-            grid=(shards // 2,),
-            in_specs=[block(0), block(1)],
-            out_specs=pl.BlockSpec((rows, 2 * count), lambda m, me: (0, m)),
-        ),
-        compiler_params=params_of(12),
-        cost_estimate=cost(0, 4 * blocks.size),
-        name="transpose_tokens",
-    )(me, blocks, blocks)
+    )(me, *in_hbm(tokens))
+    return dict(zip(offsets, outs))
 
 
 def cast_kernel(src_ref, out_ref):
@@ -117,48 +101,41 @@
     )(*in_hbm(array))
 
 
-def partial_kernel(me_ref, x_ref, w_ref, out_ref):
-    product = jnp.dot(x_ref[0], w_ref[...], preferred_element_type=jnp.float32)
-    out_ref[0] = product.astype(out_ref.dtype)
-
-
-def summed_kernel(me_ref, x_ref, w_ref, add_ref, *out_refs):
-    total = jnp.dot(x_ref[0], w_ref[...], preferred_element_type=jnp.float32)
-    total = (total + add_ref[0].astype(jnp.float32)).astype(out_refs[0].dtype)
-    for m, ref in enumerate(out_refs):
-
-        @pl.when(pl.program_id(0) == m)
-        def _():
-            ref[...] = total
-
-
-def partial_keys(blocks, key_weights, me, odd, others=None):
-    shards, count, rows = blocks.shape
+def partial_kernel(pieces, *refs):
+    x_refs, w_ref, (*add_refs, out_ref, flip_ref) = refs[:pieces], refs[pieces], refs[pieces + 1:]
+    x = jnp.concatenate([ref[...] for ref in x_refs], axis=1)
+    total = jnp.dot(x, w_ref[...], preferred_element_type=jnp.float32)
+    for ref in add_refs:
+        total = total + ref[...].astype(jnp.float32)
+    out_ref[...] = total.astype(out_ref.dtype)
+    step = x_refs[0].shape[1]
+    for i, ref in enumerate(x_refs):
+        flip_ref[i * step:(i + 1) * step, :] = ref[...].T
+
+
+def partial_keys(block, key_weights, *others):
+    count, rows = block.shape
     width = key_weights.shape[1]
-    chips = shards // 2
-    stacked = pl.BlockSpec((1, count, width), lambda m, me: (m, 0, 0))
-    specs = [
-        pl.BlockSpec((1, count, rows), lambda m, me: (me[0] ^ (2 * m + odd), 0, 0)),
-        pl.BlockSpec((rows, width), lambda m, me: (0, 0)),
-    ]
-    if others is None:
-        kernel, args = partial_kernel, ()
-        shapes, outs = jax.ShapeDtypeStruct((chips, count, width), jnp.bfloat16), stacked
-    else:
-        kernel, args = summed_kernel, (others,)
-        specs.append(stacked)
-        shapes = [jax.ShapeDtypeStruct((count, width), jnp.bfloat16)] * chips
-        outs = [pl.BlockSpec((count, width), lambda m, me: (0, 0))] * chips
-    return pl.pallas_call(
-        kernel,
-        out_shape=shapes,
-        grid_spec=pltpu.PrefetchScalarGridSpec(
-            num_scalar_prefetch=1, grid=(chips,), in_specs=specs, out_specs=outs
-        ),
+    pieces = 4 if rows % (4 * HEAD) == 0 else 2
+    fixed = lambda a: pl.BlockSpec(a.shape, lambda i: (0, 0))
+    return pl.pallas_call(
+        functools.partial(partial_kernel, pieces),
+        out_shape=[
+            jax.ShapeDtypeStruct((count, width), jnp.bfloat16),
+            jax.ShapeDtypeStruct((rows, count), jnp.bfloat16),
+        ],
+        grid=(1,),
+        in_specs=[pl.BlockSpec((count, rows // pieces), lambda i, c=c: (0, c)) for c in range(pieces)]
+        + [fixed(key_weights)]
+        + [fixed(o) for o in others],
+        out_specs=[
+            pl.BlockSpec((count, width), lambda i: (0, 0)),
+            pl.BlockSpec((rows, count), lambda i: (0, 0)),
+        ],
         compiler_params=params_of(12),
-        cost_estimate=cost(2 * chips * count * rows * width, 2 * chips * count * rows),
+        cost_estimate=cost(2 * count * rows * width, 4 * count * rows),
         name="partial_keys",
-    )(me, blocks, key_weights, *args)
+    )(*[block] * pieces, key_weights, *others)
 
 
 def key_kernel(first, *refs):
@@ -191,34 +168,26 @@
     )(*parts, incoming)
 
 
-def grad_kernel(firsts, has_base, has_more, last, *refs):
+def grad_kernel(count, has_base, has_more, last, place_ref, *refs):
     refs = list(refs)
-    place_ref = refs.pop(0)
-    terms = []
-    for count, first in firsts:
-        terms.append((refs.pop(0), refs[:count], first))
-        del refs[:count]
+    x_refs, u_refs = refs[:count], refs[count:2 * count]
+    refs = refs[2 * count:]
     base = refs.pop(0) if has_base else None
     square_in, due_in = (refs.pop(0), refs.pop(0)) if has_more else (None, None)
     out_ref = refs.pop(0)
-    sq_ref, due_ref = (refs.pop(0), refs.pop(0)) if last else (None, None)
-    joined = refs
-
-    @pl.when(pl.program_id(0) == 0)
-    def _():
-        for (_, blocks, first), held in zip(terms, joined):
-            depth = held.shape[0] // len(blocks)
-            for j, block in enumerate(blocks):
-                held[j * depth:(j + 1) * depth, :] = block[first:first + depth, :]
-        if last:
-            sq_ref[...] = square_in[...] if has_more else jnp.zeros_like(sq_ref)
-
-    total = base[...] if has_base else None
-    for (x_ref, _, _), held in zip(terms, joined):
-        term = jnp.dot(x_ref[...], held[...], preferred_element_type=jnp.float32)
-        total = term if total is None else total + term
+    x = jnp.concatenate([ref[...] for ref in x_refs], axis=1)
+    u = jnp.concatenate([ref[...] for ref in u_refs], axis=0)
+    total = jnp.dot(x, u, preferred_element_type=jnp.float32)
+    if has_base:
+        total = total + base[...]
     out_ref[...] = total
     if last:
+        sq_ref, due_ref = refs
+
+        @pl.when(pl.program_id(0) == 0)
+        def _():
+            sq_ref[...] = square_in[...] if has_more else jnp.zeros_like(sq_ref)
+
         rows, width = total.shape
         squares = (total * total).reshape(rows // 8, 8, width).sum(axis=0)
         folded = squares[:, :HEAD]
@@ -234,18 +203,15 @@
         due_ref[...] = column
 
 
-def gradient(place, terms, base=None, square=None, due=None, last=True):
-    rows = terms[0][0].shape[0]
-    width = terms[0][1][0].shape[1]
+def gradient(place, flipped, upstream, base=None, square=None, due=None, last=True):
+    rows, depth = flipped[0].shape
+    width = upstream[0].shape[1]
     step = 256
     row_block = lambda cols: pl.BlockSpec((step, cols), lambda i, p: (i, 0))
     fixed = pl.BlockSpec((8, HEAD), lambda i, p: (0, 0))
-    args, specs, scratch = [], [], []
-    for x, blocks, _ in terms:
-        args += [x, *blocks]
-        specs += [row_block(x.shape[1])]
-        specs += [pl.BlockSpec(b.shape, lambda i, p: (0, 0)) for b in blocks]
-        scratch.append(pltpu.VMEM((x.shape[1], width), jnp.bfloat16))
+    args = [*flipped, *upstream]
+    specs = [row_block(depth)] * len(flipped)
+    specs += [pl.BlockSpec((depth, width), lambda i, p: (0, 0))] * len(upstream)
     if base is not None:
         args.append(base)
         specs.append(row_block(width))
@@ -262,16 +228,12 @@
     else:
         shapes = [jax.ShapeDtypeStruct((rows, width), jnp.float32)]
         outs = [row_block(width)]
-    depth = sum(x.shape[1] for x, _, _ in terms)
-    return pl.pallas_call(
-        functools.partial(grad_kernel, [(len(b), first) for _, b, first in terms], base is not None, square is not None, last),
+    depth *= len(flipped)
+    return pl.pallas_call(
+        functools.partial(grad_kernel, len(flipped), base is not None, square is not None, last),
         out_shape=shapes,
         grid_spec=pltpu.PrefetchScalarGridSpec(
-            num_scalar_prefetch=1,
-            grid=(rows // step,),
-            in_specs=specs,
-            out_specs=outs,
-            scratch_shapes=scratch,
+            num_scalar_prefetch=1, grid=(rows // step,), in_specs=specs, out_specs=outs
         ),
         compiler_params=params_of(20),
         cost_estimate=cost(2 * rows * width * depth, 2 * rows * depth + 4 * rows * width),
@@ -481,6 +443,11 @@
 
 def after(value, *others):
     return lax.optimization_barrier((value,) + others)[0]
+
+
+def by_device(pieces, me):
+    count = pieces.shape[0]
+    return jnp.stack([lax.dynamic_index_in_dim(pieces, me ^ k, 0, keepdims=False) for k in range(count)])
 
 
 def body(
@@ -504,17 +471,26 @@
     my_rep = lax.axis_index("rep").astype(jnp.int32)
     place = jnp.stack([due_fragment[0], my_rep])
     chips = range(2, shards, 2)
-    count = inputs.shape[0]
-    cuts = [(0, count * 3 // 4), (count * 3 // 4, count // 4)]
-
-    def gather(block):
-        held = [block] + [swap(block, "fsdp", k) for k in chips]
-        return [b for h in held for b in (h, swap(h, "fsdp", 1))]
-
-    values = gather(incoming[:, kv_width:])
-
-    packed = [pack(inputs, first, size, rows) for first, size in cuts]
-    arrived = [lax.all_to_all(p, "fsdp", 0, 0, tiled=True) for p in packed]
+    far = sorted(chips, key=lambda k: (-bin(k).count("1"), k))
+    order = [k for k in far[:-2] for k in (k, k + 1)]
+    order += far[-2:] + [k + 1 for k in far[-2:]]
+
+    packed = pack(inputs, me, rows, tuple(order[:1]))
+    packed |= pack(inputs, me, rows, tuple(order[1:4]))
+    packed |= pack(inputs, me, rows, tuple(order[4:]))
+    blocks = {k: swap(packed[k], "fsdp", k) for k in order}
+    early = packed[order[-1]]
+    packed |= pack(inputs, after(me, early), rows, (0, 1))
+    blocks[0], blocks[1] = packed[0], swap(packed[1], "fsdp", 1)
+
+    values = {0: incoming[:, kv_width:]}
+    for i, k in enumerate(far):
+        values[k] = swap(after(values[0], blocks[order[i]]), "fsdp", k)
+    for k in range(0, shards, 2):
+        values[k + 1] = swap(values[k], "fsdp", 1)
+
+    def to_all(pieces):
+        return lax.all_to_all(pieces, "rep", 0, 0, tiled=True)
 
     steps_now = step_count[0].astype(jnp.float32)
     plan = jnp.minimum(1.0, steps_now / WARMUP) * (
@@ -524,36 +500,40 @@
     inv_one = 1.0 / (1.0 - jnp.power(BETA_ONE, steps_now))
     inv_two = 1.0 / (1.0 - jnp.power(BETA_TWO, steps_now))
     scalars = jnp.stack([rate, inv_one, inv_two])
-    place_early = after(place, *values[2::2])
+    place_early = after(place, early)
     old, old_first, old_second = due_columns(place_early, part, params, first_moment[0], second_moment[0])
     anchor_cols, moment_cols = (c[0] for c in due_columns(place_early, part, anchor, momentum))
-    old_sum = sum([swap(old[k], "rep", k) for k in range(1, replicas)], old[0])
+    old_sum = jnp.sum(to_all(by_device(old, my_rep)), axis=0)
     pseudo_old = anchor_cols - old_sum / replicas
     base = anchor_cols - OUTER_RATE * (OUTER_MU * (OUTER_MU * moment_cols + pseudo_old) + pseudo_old)
-    base = [base] + [swap(base, "rep", k) for k in range(1, replicas)]
+    base = by_device(to_all(jnp.broadcast_to(base[None], (replicas,) + base.shape)), my_rep)
+    base = [base[j] for j in range(replicas)]
     anchor_copy, momentum_copy = duplicate(anchor, momentum)
-    key_weights = cast_left(params, kv_width)
-
-    def sum_keys(x, first, *before):
-        theirs = swap(partial_keys(x, key_weights, me, 1), "fsdp", 1)
-        parts = list(partial_keys(x, key_weights, me, 0, theirs))
-        parts = [parts[0]] + [swap(parts[k // 2], "fsdp", k) for k in chips]
-        parts[0] = after(parts[0], *before)
-        return gather(key_backward(parts, incoming, first))
-
-    arrived[0] = after(
-        arrived[0], packed[1], *base, anchor_copy, momentum_copy, old_second, scalars, *values
-    )
-    flipped = [transpose_tokens(arrived[0], me)]
-    keys = [sum_keys(arrived[0], cuts[0][0], flipped[0])]
-    (values_first,) = gradient(place, [(flipped[0], values, cuts[0][0])], last=False)
-    arrived[1] = after(arrived[1], *keys[0], values_first)
-    flipped.append(transpose_tokens(arrived[1], me))
-    keys.append(sum_keys(arrived[1], cuts[1][0], flipped[1]))
-
-    (keys_first,) = gradient(place, [(flipped[0], keys[0], 0)], last=False)
-    grad_values, square, due = gradient(place, [(flipped[1], values, cuts[1][0])], values_first)
-    grad_keys, square, due = gradient(place, [(flipped[1], keys[1], 0)], keys_first, square, due)
+    key_weights = cast_left(after(params, early), kv_width)
+
+    parts, flipped = [], {}
+    for k in far + [0]:
+        theirs, flipped[k + 1] = partial_keys(blocks[k + 1], key_weights)
+        part_k, flipped[k] = partial_keys(blocks[k], key_weights, swap(theirs, "fsdp", 1))
+        parts.append(swap(part_k, "fsdp", k) if k else part_k)
+    parts[-1] = after(
+        parts[-1], *base, anchor_copy, momentum_copy, old_first, old_second, scalars, *values.values()
+    )
+    keys = {0: key_backward(parts, incoming, 0)}
+    for k in far:
+        keys[k] = swap(keys[0], "fsdp", k)
+    for k in range(0, shards, 2):
+        keys[k + 1] = swap(keys[k], "fsdp", 1)
+
+    spread = [0, 1] + [k + odd for k in far for odd in range(2)]
+    near, rest = spread[:shards // 2], spread[shards // 2:]
+    pick = lambda table, which: [table[k] for k in which]
+    (values_first,) = gradient(place, pick(flipped, near), pick(values, near), last=False)
+    grad_values, square, due = gradient(place, pick(flipped, rest), pick(values, rest), values_first)
+    (keys_first,) = gradient(place, pick(flipped, near), pick(keys, near), last=False)
+    grad_keys, square, due = gradient(
+        place, pick(flipped, rest), pick(keys, rest), keys_first, square, due
+    )
 
     square = square + swap(square, "fsdp", 1)
     squares = [square] + [swap(square, "fsdp", k) for k in chips]

time: 256 us -> 200 us (0.78)
  waiting for transfers between devices: 112 us -> 54.5 us
  local copies, waits for them, and re-layouts: 5.16 us -> 17 us
  Pallas kernels: 80.5 us -> 73.7 us
  starting transfers between devices: 51.4 us -> 47 us
    ppermute x45 -> x38, waiting for transfers between devices: 112 us -> 54.5 us  [swap(): return lax.ppermute(block, axis, [(i, i ^ offset) for i in range(count)])]
    unnamed x70 -> x62, local copies, waits for them, and re-layouts: 3.99 us -> 12.2 us
    ppermute x45 -> x38, starting transfers between devices: 42.4 us -> 35.6 us  [swap(): return lax.ppermute(block, axis, [(i, i ^ offset) for i in range(count)])]
    pallas_call x12 -> x16, Pallas kernels: 41.4 us -> 35.5 us  [the longest x4 17.2 us: gradient(): pl.pallas_call(functools.partial(grad_kernel, len(flipped), base is not N...]
  transfers between devices with their start and end apart: 47 -> 40, of which waited for: 18 -> 11; matrix products, arithmetic and copies ran while one was open for 1% -> 3% of each run, Pallas kernels for 23% -> 28%
where the time goes in v8:
time: 200 us; the launch traced here: 199 us
  Pallas kernels  73.7 us (37%)
  waiting for transfers between devices  54.5 us (27%)
  starting transfers between devices  47 us (24%)
  local copies, waits for them, and re-layouts  17 us (8%)
  between operations  3.77 us (2%)
  other arithmetic  3.45 us (2%)
    ppermute x38, waiting for transfers between devices, swap(): return lax.ppermute(block, axis, [(i, i ^ offset) for i in range(count)])  54.5 us
    ppermute x38, starting transfers between devices, swap(): return lax.ppermute(block, axis, [(i, i ^ offset) for i in range(count)])  35.6 us
    pallas_call x2, Pallas kernels, adam_rows(): pl.pallas_call(functools.partial(adam_kernel, len(squares), len(into)), o...  19.6 us
    pallas_call x4, Pallas kernels, gradient(): pl.pallas_call(functools.partial(grad_kernel, len(flipped), base is not N...  17.2 us
    unnamed x62, local copies, waits for them, and re-layouts  12.2 us
    all_to_all x2, starting transfers between devices, to_all(): return lax.all_to_all(pieces, 'rep', 0, 0, tiled=True)  11.4 us
    pallas_call x8, Pallas kernels, partial_keys(): pl.pallas_call(functools.partial(partial_kernel, pieces), out_shape=[jax....  9.17 us
    pallas_call x4, Pallas kernels, pack(): pl.pallas_call(functools.partial(pack_kernel, offsets), out_shape=[pltpu....  9.15 us
  transfers between devices with their start and end apart: 40, of which 11 were waited for; matrix products, arithmetic and copies ran while one was open for 3% of the time, Pallas kernels for 28%

profile of v8, /device:TPU:0, one launch (start us, length us, event | category | flops | bytes accessed | tf_op | source)
XLA Modules:
  0.0 199.4 jit_solution(13177624438946794949)
XLA Ops:
  1.4 2.3 %pack.5 = (bf16[256,1536]{1,0:T(8,128)(2,1)}, bf16[256,1536]{1,0:T(8,128)(2,1)}) custom-call(s32[1]{0:T(128)} %bitcast.4.me_ref, bf16[256,12288]{1,0:T(8,128)(2,1)} %bitcast.31), custom_call_target="tpu_custom_call" | custom-call | bytes 3145728 | tf_op jit(solution)/shard_map/pack/pallas_call | solution.py:68
  3.7 4.5 %due_columns.3 = (f32[4,384,128]{2,1,0:T(8,128)}, f32[4,384,128]{2,1,0:T(8,128)}, f32[4,384,128]{2,1,0:T(8,128)}) custom-call(s32[2]{0:T(128)S(1)} %pad_add_fusion.place_ref, f32[1536,1024]{1,0:T(8,128)} %bitcast.35, f32[1536,1024]{1,0:T(8,128)} %bitcast.39, f32[1536,1024]{1,0:T(8,128)} %bitcast.42), custom_call_target="tpu_custom_call" | custom-call | bytes 4718592 | tf_op jit(solution)/shard_map/due_columns/pallas_call | solution.py:339
  8.2 1.3 constant_dynamic-slice_fusion.3
  9.5 0.9 pad_maximum_fusion
  10.4 6.3 %all-to-all-start = ((f32[4,384,128]{2,1,0:T(8,128)}), f32[4,384,128]{2,1,0:T(8,128)}, u32[]{:S(2)}, u32[]{:S(2)}) async-start(f32[4,384,128]{2,1,0:T(8,128)} %pad_maximum_fusion), calls=%async_computation | async-start | bytes 1572864 | tf_op jit(solution)/shard_map/all_to_all | solution.py:493
  16.7 2.0 pack.6
  18.7 2.5 %collective-permute-start.6 = (bf16[256,1536]{1,0:T(8,128)(2,1)}, bf16[256,1536]{1,0:T(8,128)(2,1)S(1)}, u32[]{:S(2)}, u32[]{:S(2)}) collective-permute-start(bf16[256,1536]{1,0:T(8,128)(2,1)} %pack.6), channel_id=1, source_target_pairs={{0,6},{1,7},{2,4},{3,5},{4,2},{5,3},{6,0},{7,1},{8,14},{9,15},{10,... | collective-permute-start | bytes 2359304 | tf_op jit(solution)/shard_map/ppermute | solution.py:441
  22.0 2.6 %pack.4 = (bf16[256,1536]{1,0:T(8,128)(2,1)}, bf16[256,1536]{1,0:T(8,128)(2,1)}, bf16[256,1536]{1,0:T(8,128)(2,1)}) custom-call(s32[1]{0:T(128)} %bitcast.4.me_ref, bf16[256,12288]{1,0:T(8,128)(2,1)} %bitcast.33), custom_call_target="tpu_custom_call" | custom-call | bytes 4718592 | tf_op jit(solution)/shard_map/pack/pallas_call | solution.py:68
  24.6 1.4 collective-permute-start.7
  26.0 2.3 %pack.7 = (bf16[256,1536]{1,0:T(8,128)(2,1)}, bf16[256,1536]{1,0:T(8,128)(2,1)}) custom-call(s32[1]{0:T(128)} %bitcast.4.me_ref, bf16[256,12288]{1,0:T(8,128)(2,1)} %bitcast.34), custom_call_target="tpu_custom_call" | custom-call | bytes 3145728 | tf_op jit(solution)/shard_map/pack/pallas_call | solution.py:68
  28.3 1.3 collective-permute-start.12
  29.6 10.8 %collective-permute-done.6.refs_0_.refs_1_.refs_2_.refs_3_ = bf16[256,1536]{1,0:T(8,128)(2,1)S(1)} collective-permute-done((bf16[256,1536]{1,0:T(8,128)(2,1)}, bf16[256,1536]{1,0:T(8,128)(2,1)S(1)}, u32[]{:S(2)}, u32[]{:S(2)}) %collective-permute-start.6) | collective-permute-done | bytes 786464 | tf_op jit(solution)/shard_map/ppermute | solution.py:441
  40.4 1.5 collective-permute-start
  41.9 2.3 %due_columns.2 = (f32[1,384,128]{2,1,0:T(8,128)}, f32[1,384,128]{2,1,0:T(8,128)}) custom-call(s32[2]{0:T(128)S(1)} %pad_add_fusion.place_ref, f32[384,1024]{1,0:T(8,128)} %refs_0_.3, f32[384,1024]{1,0:T(8,128)} %refs_1_.3), custom_call_target="tpu_custom_call" | custom-call | bytes 786432 | tf_op jit(solution)/shard_map/due_columns/pallas_call | solution.py:339
  44.2 1.2 reduce_sum.9
  45.4 11.7 %collective-permute-done.4.refs_0_.refs_1_.refs_2_.refs_3_ = bf16[256,1536]{1,0:T(8,128)(2,1)S(1)} collective-permute-done((bf16[256,1536]{1,0:T(8,128)(2,1)}, bf16[256,1536]{1,0:T(8,128)(2,1)S(1)}, u32[]{:S(2)}, u32[]{:S(2)}) %collective-permute-start.4) | collective-permute-done | bytes 786464 | tf_op jit(solution)/shard_map/ppermute | solution.py:441
  57.1 0.9 copy-done.1
  58.0 1.5 collective-permute-start.3
  59.5 1.1 subtract_bitcast_fusion
  60.6 1.0 broadcast_in_dim.18
  61.6 5.1 %all-to-all-start.1 = ((f32[4,384,128]{2,1,0:T(8,128)}), f32[4,384,128]{2,1,0:T(8,128)}, u32[]{:S(2)}, u32[]{:S(2)}) async-start(f32[4,384,128]{2,1,0:T(8,128)} %broadcast_in_dim.18), calls=%async_computation.1 | async-start | bytes 1572864 | tf_op jit(solution)/shard_map/all_to_all | solution.py:493
  66.7 1.0 slice.4.refs_4_
  67.8 3.5 %cast_left.1.refs_4_ = bf16[1536,512]{1,0:T(8,128)(2,1)S(1)} custom-call(f32[1536,1024]{1,0:T(8,128)} %bitcast.36), custom_call_target="tpu_custom_call" | custom-call | bytes 4718592 | tf_op jit(solution)/shard_map/cast_left/pallas_call | solution.py:92
  71.8 0.9 copy-done.8
  72.7 1.4 collective-permute-start.14
  74.2 1.8 partial_keys.8
  76.8 1.8 partial_keys.12
  78.7 0.9 copy-done.4
  80.1 11.0 %collective-permute-done.refs_0_.refs_1_.refs_2_.refs_3_ = bf16[256,1536]{1,0:T(8,128)(2,1)S(1)} collective-permute-done((bf16[256,1536]{1,0:T(8,128)(2,1)}, bf16[256,1536]{1,0:T(8,128)(2,1)S(1)}, u32[]{:S(2)}, u32[]{:S(2)}) %collective-permute-start) | collective-permute-done | bytes 786464 | tf_op jit(solution)/shard_map/ppermute | solution.py:441
  92.2 2.9 %collective-permute-done.14.refs_6_ = bf16[256,512]{1,0:T(8,128)(2,1)S(1)} collective-permute-done((bf16[256,512]{1,0:T(8,128)(2,1)S(1)}, bf16[256,512]{1,0:T(8,128)(2,1)S(1)}, u32[]{:S(2)}, u32[]{:S(2)}) %collective-permute-start.14) | collective-permute-done | bytes 262176 | tf_op jit(solution)/shard_map/ppermute | solution.py:441
  95.1 1.6 collective-permute-start.16
  96.7 1.5 collective-permute-start.15
  98.2 2.8 %duplicate.1 = (f32[384,1024]{1,0:T(8,128)}, f32[384,1024]{1,0:T(8,128)}) custom-call(f32[384,1024]{1,0:T(8,128)} %refs_0_.3, f32[384,1024]{1,0:T(8,128)} %refs_1_.3), custom_call_target="tpu_custom_call" | custom-call | bytes 6291456 | tf_op jit(solution)/shard_map/duplicate/pallas_call | solution.py:380
  101.9 1.3 partial_keys.9
  104.1 1.3 partial_keys.13
  105.4 1.3 partial_keys.11
  109.3 2.4 %collective-permute-start.9 = (bf16[256,512]{1,0:T(8,128)(2,1)}, bf16[256,512]{1,0:T(8,128)(2,1)}, u32[]{:S(2)}, u32[]{:S(2)}) collective-permute-start(bf16[256,512]{1,0:T(8,128)(2,1)} %get-tuple-element.79), channel_id=1, source_target_pairs={{0,6},{1,7},{2,4},{3,5},{4,2},{5,3},{6,0},{7,1},{8,14},{9,15},{10,... | collective-permute-start | bytes 786440 | tf_op jit(solution)/shard_map/ppermute | solution.py:441
  114.3 1.4 dynamic-slice_bitcast_fusion
  115.8 1.9 collective-permute-done.10.refs_1_
  117.7 5.5 %collective-permute-done.11.refs_2_ = bf16[256,512]{1,0:T(8,128)(2,1)} collective-permute-done((bf16[256,512]{1,0:T(8,128)(2,1)}, bf16[256,512]{1,0:T(8,128)(2,1)}, u32[]{:S(2)}, u32[]{:S(2)}) %collective-permute-start.11) | collective-permute-done | bytes 262176 | tf_op jit(solution)/shard_map/ppermute | solution.py:441
  123.2 1.0 copy-done.17
  124.2 0.9 copy-done.22
  125.2 1.6 key_backward.1.refs_4_
  126.8 1.5 collective-permute-start.26
  128.3 1.5 collective-permute-start.23
  130.4 6.7 %collective-permute-done.26.refs_6_ = bf16[256,512]{1,0:T(8,128)(2,1)S(1)} collective-permute-done((bf16[256,512]{1,0:T(8,128)(2,1)S(1)}, bf16[256,512]{1,0:T(8,128)(2,1)S(1)}, u32[]{:S(2)}, u32[]{:S(2)}) %collective-permute-start.26) | collective-permute-done | bytes 262176 | tf_op jit(solution)/shard_map/ppermute | solution.py:441
  137.1 0.9 copy-done.24
  138.0 0.9 copy-done.26
  139.0 0.9 copy-done.28
  139.9 3.2 %gradient.5.refs_8_ = f32[1536,512]{1,0:T(8,128)S(1)} custom-call(s32[2]{0:T(128)S(1)} %pad_add_fusion.place_ref, bf16[1536,256]{1,0:T(8,128)(2,1)S(1)} %get-tuple-element.99.refs_0_, bf16[1536,256]{1,0:T(8,128)(2,1)S(1)} %copy-done.7, bf16[1536,256]{1,0:T(8,128)(2,1)S(1)} %get-tuple-element.101.refs_2_, bf16[1536,256]{1,0:T(8,128)(2,1)S(1)} %copy-done.5, ...), custom_call_target="tpu_custom_call" | custom-call | flops 1610612736 | bytes 6291456 | tf_op jit(solution)/shard_map/gradient/pallas_call | solution.py:232
  143.8 6.0 %gradient.6 = (f32[1536,512]{1,0:T(8,128)}, f32[8,128]{1,0:T(8,128)S(1)}, f32[1536,128]{1,0:T(8,128)S(1)}) custom-call(s32[2]{0:T(128)S(1)} %pad_add_fusion.place_ref, bf16[1536,256]{1,0:T(8,128)(2,1)S(1)} %copy-done.13, bf16[1536,256]{1,0:T(8,128)(2,1)S(1)} %copy-done.11, bf16[1536,256]{1,0:T(8,128)(2,1)S(1)} %copy-done.15, ...), custom_call_target="tpu_custom_call" | custom-call | flops 1610612736 | bytes 6291456 | tf_op jit(solution)/shard_map/gradient/pallas_call | solution.py:232
  149.8 3.2 %gradient.4.refs_8_ = f32[1536,512]{1,0:T(8,128)S(1)} custom-call(s32[2]{0:T(128)S(1)} %pad_add_fusion.place_ref, bf16[1536,256]{1,0:T(8,128)(2,1)S(1)} %get-tuple-element.99.refs_0_, bf16[1536,256]{1,0:T(8,128)(2,1)S(1)} %copy-done.7, bf16[1536,256]{1,0:T(8,128)(2,1)S(1)} %get-tuple-element.101.refs_2_, bf16[1536,256]{1,0:T(8,128)(2,1)S(1)} %copy-done.5, ...), custom_call_target="tpu_custom_call" | custom-call | flops 1610612736 | bytes 6291456 | tf_op jit(solution)/shard_map/gradient/pallas_call | solution.py:232
  153.0 4.8 %gradient.7 = (f32[1536,512]{1,0:T(8,128)}, f32[8,128]{1,0:T(8,128)S(1)}, f32[1536,128]{1,0:T(8,128)S(1)}) custom-call(s32[2]{0:T(128)S(1)} %pad_add_fusion.place_ref, bf16[1536,256]{1,0:T(8,128)(2,1)S(1)} %copy-done.13, bf16[1536,256]{1,0:T(8,128)(2,1)S(1)} %copy-done.11, bf16[1536,256]{1,0:T(8,128)(2,1)S(1)} %copy-done.15, ...), custom_call_target="tpu_custom_call" | custom-call | flops 1610612736 | bytes 6291456 | tf_op jit(solution)/shard_map/gradient/pallas_call | solution.py:232
  159.1 1.4 collective-permute-start.31
  160.5 1.5 collective-permute-start.30
  162.6 1.0 collective-permute-done.31.refs_3_
  164.1 1.5 collective-permute-done.29.refs_1_
  165.7 1.6 adam_frag.1
  167.2 1.8 collective-permute-start.32
  169.0 2.4 %collective-permute-start.33 = (bf16[384,128]{1,0:T(8,128)(2,1)S(1)}, bf16[384,128]{1,0:T(8,128)(2,1)S(1)}, u32[]{:S(2)}, u32[]{:S(2)}) collective-permute-start(bf16[384,128]{1,0:T(8,128)(2,1)S(1)} %get-tuple-element.115), channel_id=1, source_target_pairs={{0,16},{8,24},{16,0},{24,8},{1,17},{9,25},{17,1},{25,9},{2,18},{10... | collective-permute-start | bytes 294920 | tf_op jit(solution)/shard_map/ppermute | solution.py:441
  171.7 9.8 %adam_rows.2 = (f32[1536,1024]{1,0:T(8,128)}, f32[1536,1024]{1,0:T(8,128)}, f32[1536,1024]{1,0:T(8,128)}, f32[8,128]{1,0:T(8,128)S(1)}) custom-call(f32[3]{0:T(128)S(1)} %pad_maximum_fusion.1.sc_ref, f32[1536,1024]{1,0:T(8,128)} %bitcast.37, f32[1536,1024]{1,0:T(8,128)} %bitcast.40, f32[1536,1024]{1,0:T(8,128)} %bitcast.43, ...), custom_call_target="tpu_custom_call" | custom-call | flops 15728640 | bytes 22020096 | tf_op jit(solution)/shard_map/adam_rows/pallas_call | solution.py:287
  181.6 3.6 %collective-permute-start.37 = (bf16[384,128]{1,0:T(8,128)(2,1)S(1)}, bf16[384,128]{1,0:T(8,128)(2,1)S(1)}, u32[]{:S(2)}, u32[]{:S(2)}) collective-permute-start(bf16[384,128]{1,0:T(8,128)(2,1)S(1)} %convert_element_type.24.refs_7_), channel_id=1, source_target_pairs={{0,24},{8,16},{16,8},{24,0},{1,25},{9,17},{17,9},{25,1},{2,26},{10... | collective-permute-start | bytes 294920 | tf_op jit(solution)/shard_map/ppermute | solution.py:441
  186.1 9.8 %adam_rows.3 = (f32[1536,1024]{1,0:T(8,128)}, f32[1536,1024]{1,0:T(8,128)}, f32[1536,1024]{1,0:T(8,128)}) custom-call(f32[3]{0:T(128)S(1)} %pad_maximum_fusion.1.sc_ref, f32[1536,1024]{1,0:T(8,128)} %bitcast.38, f32[1536,1024]{1,0:T(8,128)} %bitcast.41, f32[1536,1024]{1,0:T(8,128)} %bitcast.44, ...), custom_call_target="tpu_custom_call", output_to_operand_aliasing={{0}: (10, {}), {1}: (11, {}), {2}: (12, {})} | custom-call | flops 15728640 | bytes 22020096 | tf_op jit(solution)/shard_map/adam_rows/pallas_call | solution.py:287
  195.9 2.4 %outer_step.1 = (f32[1536,1024]{1,0:T(8,128)}, f32[384,1024]{1,0:T(8,128)}, f32[384,1024]{1,0:T(8,128)}) custom-call(s32[2]{0:T(128)S(1)} %pad_add_fusion.place_ref, f32[1536,1024]{1,0:T(8,128)} %get-tuple-element.111.refs_0_, f32[384,1024]{1,0:T(8,128)} %get-tuple-element.91.refs_1_, ...), custom_call_target="tpu_custom_call", output_to_operand_aliasing={{0}: (1, {}), {1}: (2, {}), {2}: (3, {})} | custom-call | flops 1966080 | bytes 3932160 | tf_op jit(solution)/shard_map/outer_step/pallas_call | solution.py:423
  (116 shorter events, 14.8 us)
Async XLA Ops:
  10.4 33.8 %all-to-all-start = ((f32[4,384,128]{2,1,0:T(8,128)}), f32[4,384,128]{2,1,0:T(8,128)}, u32[]{:S(2)}, u32[]{:S(2)}) async-start(f32[4,384,128]{2,1,0:T(8,128)} %pad_maximum_fusion), calls=%async_computation | async-start | bytes 1572864 | tf_op jit(solution)/shard_map/all_to_all | solution.py:493
  18.7 21.7 %collective-permute-start.6 = (bf16[256,1536]{1,0:T(8,128)(2,1)}, bf16[256,1536]{1,0:T(8,128)(2,1)S(1)}, u32[]{:S(2)}, u32[]{:S(2)}) collective-permute-start(bf16[256,1536]{1,0:T(8,128)(2,1)} %pack.6), channel_id=1, source_target_pairs={{0,6},{1,7},{2,4},{3,5},{4,2},{5,3},{6,0},{7,1},{8,14},{9,15},{10,... | collective-permute-start | bytes 2359304 | tf_op jit(solution)/shard_map/ppermute | solution.py:441
  21.2 35.9 %collective-permute-start.4 = (bf16[256,1536]{1,0:T(8,128)(2,1)}, bf16[256,1536]{1,0:T(8,128)(2,1)S(1)}, u32[]{:S(2)}, u32[]{:S(2)}) collective-permute-start(bf16[256,1536]{1,0:T(8,128)(2,1)} %get-tuple-element.67), channel_id=1, source_target_pairs={{0,5},{1,4},{2,7},{3,6},{4,1},{5,0},{6,3},{7,2},{8,13},{9,12},{10,... | collective-permute-start | bytes 2359304 | tf_op jit(solution)/shard_map/ppermute | solution.py:441
  21.2 51.5 %collective-permute-start.1 = (bf16[256,1536]{1,0:T(8,128)(2,1)}, bf16[256,1536]{1,0:T(8,128)(2,1)}, u32[]{:S(2)}, u32[]{:S(2)}) collective-permute-start(bf16[256,1536]{1,0:T(8,128)(2,1)} %get-tuple-element.69), channel_id=1, source_target_pairs={{0,3},{1,2},{2,1},{3,0},{4,7},{5,6},{6,5},{7,4},{8,11},{9,10},{10,... | collective-permute-start | bytes 2359304 | tf_op jit(solution)/shard_map/ppermute | solution.py:441
  24.6 52.2 %collective-permute-start.7 = (bf16[256,1536]{1,0:T(8,128)(2,1)}, bf16[256,1536]{1,0:T(8,128)(2,1)}, u32[]{:S(2)}, u32[]{:S(2)}) collective-permute-start(bf16[256,1536]{1,0:T(8,128)(2,1)} %get-tuple-element.77), channel_id=1, source_target_pairs={{0,7},{1,6},{2,5},{3,4},{4,3},{5,2},{6,1},{7,0},{8,15},{9,14},{10,... | collective-permute-start | bytes 2359304 | tf_op jit(solution)/shard_map/ppermute | solution.py:441
  28.3 51.3 %collective-permute-start.12 = (bf16[256,1536]{1,0:T(8,128)(2,1)}, bf16[256,1536]{1,0:T(8,128)(2,1)S(1)}, u32[]{:S(2)}, u32[]{:S(2)}) collective-permute-start(bf16[256,1536]{1,0:T(8,128)(2,1)} %get-tuple-element.84), channel_id=1, source_target_pairs={{0,1},{1,0},{2,3},{3,2},{4,5},{5,4},{6,7},{7,6},{8,9},{9,8},{10,11... | collective-permute-start | bytes 2359304 | tf_op jit(solution)/shard_map/ppermute | solution.py:441
  40.4 50.7 %collective-permute-start = (bf16[256,1536]{1,0:T(8,128)(2,1)}, bf16[256,1536]{1,0:T(8,128)(2,1)S(1)}, u32[]{:S(2)}, u32[]{:S(2)}) collective-permute-start(bf16[256,1536]{1,0:T(8,128)(2,1)} %get-tuple-element.66), channel_id=1, source_target_pairs={{0,2},{1,3},{2,0},{3,1},{4,6},{5,7},{6,4},{7,5},{8,10},{9,11},{10,... | collective-permute-start | bytes 2359304 | tf_op jit(solution)/shard_map/ppermute | solution.py:441
  45.4 21.3 %copy-start.29 = (f32[384,128]{1,0:T(8,128)}, f32[384,128]{1,0:T(8,128)S(1)}, u32[]{:S(2)}) copy-start(f32[384,128]{1,0:T(8,128)S(1)} %reduce_sum.9) | copy-start | bytes 589828
  58.0 33.6 %collective-permute-start.3 = (bf16[256,1536]{1,0:T(8,128)(2,1)}, bf16[256,1536]{1,0:T(8,128)(2,1)S(1)}, u32[]{:S(2)}, u32[]{:S(2)}) collective-permute-start(bf16[256,1536]{1,0:T(8,128)(2,1)} %get-tuple-element.73), channel_id=1, source_target_pairs={{0,4},{1,5},{2,6},{3,7},{4,0},{5,1},{6,2},{7,3},{8,12},{9,13},{10,... | collective-permute-start | bytes 2359304 | tf_op jit(solution)/shard_map/ppermute | solution.py:441
  61.6 52.7 %all-to-all-start.1 = ((f32[4,384,128]{2,1,0:T(8,128)}), f32[4,384,128]{2,1,0:T(8,128)}, u32[]{:S(2)}, u32[]{:S(2)}) async-start(f32[4,384,128]{2,1,0:T(8,128)} %broadcast_in_dim.18), calls=%async_computation.1 | async-start | bytes 1572864 | tf_op jit(solution)/shard_map/all_to_all | solution.py:493
  66.7 4.5 %copy-start.2 = (bf16[256,1536]{1,0:T(8,128)(2,1)S(1)}, bf16[256,1536]{1,0:T(8,128)(2,1)}, u32[]{:S(2)}) copy-start(bf16[256,1536]{1,0:T(8,128)(2,1)} %copy-done.1) | copy-start | bytes 2359300
  71.8 0.9 copy-start.8
  72.7 22.4 %collective-permute-start.14 = (bf16[256,512]{1,0:T(8,128)(2,1)S(1)}, bf16[256,512]{1,0:T(8,128)(2,1)S(1)}, u32[]{:S(2)}, u32[]{:S(2)}) collective-permute-start(bf16[256,512]{1,0:T(8,128)(2,1)S(1)} %slice.4.refs_4_), channel_id=1, source_target_pairs={{0,6},{1,7},{2,4},{3,5},{4,2},{5,3},{6,0},{7,1},{8,14},{9,15},{10,... | collective-permute-start | bytes 786440 | tf_op jit(solution)/shard_map/ppermute | solution.py:441
  76.8 18.3 %collective-permute-start.2 = (bf16[256,512]{1,0:T(8,128)(2,1)S(1)}, bf16[256,512]{1,0:T(8,128)(2,1)S(1)}, u32[]{:S(2)}, u32[]{:S(2)}) collective-permute-start(bf16[256,512]{1,0:T(8,128)(2,1)S(1)} %get-tuple-element.70), channel_id=1, source_target_pairs={{0,1},{1,0},{2,3},{3,2},{4,5},{5,4},{6,7},{7,6},{8,9},{9,8},{10,11... | collective-permute-start | bytes 786440 | tf_op jit(solution)/shard_map/ppermute | solution.py:441
  78.6 0.9 copy-start.4
  79.5 17.2 %collective-permute-start.5 = (bf16[256,512]{1,0:T(8,128)(2,1)S(1)}, bf16[256,512]{1,0:T(8,128)(2,1)S(1)}, u32[]{:S(2)}, u32[]{:S(2)}) collective-permute-start(bf16[256,512]{1,0:T(8,128)(2,1)S(1)} %get-tuple-element.74), channel_id=1, source_target_pairs={{0,1},{1,0},{2,3},{3,2},{4,5},{5,4},{6,7},{7,6},{8,9},{9,8},{10,11... | collective-permute-start | bytes 786440 | tf_op jit(solution)/shard_map/ppermute | solution.py:441
  91.0 7.2 %collective-permute-start.8 = (bf16[256,512]{1,0:T(8,128)(2,1)S(1)}, bf16[256,512]{1,0:T(8,128)(2,1)S(1)}, u32[]{:S(2)}, u32[]{:S(2)}) collective-permute-start(bf16[256,512]{1,0:T(8,128)(2,1)S(1)} %get-tuple-element.78), channel_id=1, source_target_pairs={{0,1},{1,0},{2,3},{3,2},{4,5},{5,4},{6,7},{7,6},{8,9},{9,8},{10,11... | collective-permute-start | bytes 786440 | tf_op jit(solution)/shard_map/ppermute | solution.py:441
  91.6 10.3 %copy-start.6 = (bf16[1536,256]{1,0:T(8,128)(2,1)}, bf16[1536,256]{1,0:T(8,128)(2,1)S(1)}, u32[]{:S(2)}) copy-start(bf16[1536,256]{1,0:T(8,128)(2,1)S(1)} %get-tuple-element.100.refs_1_) | copy-start | bytes 2359300
  91.6 15.9 %collective-permute-start.17 = (bf16[256,512]{1,0:T(8,128)(2,1)S(1)}, bf16[256,512]{1,0:T(8,128)(2,1)S(1)}, u32[]{:S(2)}, u32[]{:S(2)}) collective-permute-start(bf16[256,512]{1,0:T(8,128)(2,1)S(1)} %slice.4.refs_4_), channel_id=1, source_target_pairs={{0,1},{1,0},{2,3},{3,2},{4,5},{5,4},{6,7},{7,6},{8,9},{9,8},{10,11... | collective-permute-start | bytes 786440 | tf_op jit(solution)/shard_map/ppermute | solution.py:441
  95.1 10.3 %copy-start.23 = (bf16[256,512]{1,0:T(8,128)(2,1)}, bf16[256,512]{1,0:T(8,128)(2,1)S(1)}, u32[]{:S(2)}) copy-start(bf16[256,512]{1,0:T(8,128)(2,1)S(1)} %collective-permute-done.14.refs_6_) | copy-start | bytes 786436
  95.1 13.7 %collective-permute-start.13 = (bf16[256,512]{1,0:T(8,128)(2,1)S(1)}, bf16[256,512]{1,0:T(8,128)(2,1)S(1)}, u32[]{:S(2)}, u32[]{:S(2)}) collective-permute-start(bf16[256,512]{1,0:T(8,128)(2,1)S(1)} %get-tuple-element.85), channel_id=1, source_target_pairs={{0,1},{1,0},{2,3},{3,2},{4,5},{5,4},{6,7},{7,6},{8,9},{9,8},{10,11... | collective-permute-start | bytes 786440 | tf_op jit(solution)/shard_map/ppermute | solution.py:441
  95.1 14.2 %collective-permute-start.16 = (bf16[256,512]{1,0:T(8,128)(2,1)S(1)}, bf16[256,512]{1,0:T(8,128)(2,1)}, u32[]{:S(2)}, u32[]{:S(2)}) collective-permute-start(bf16[256,512]{1,0:T(8,128)(2,1)S(1)} %slice.4.refs_4_), channel_id=1, source_target_pairs={{0,4},{1,5},{2,6},{3,7},{4,0},{5,1},{6,2},{7,3},{8,12},{9,13},{10,... | collective-permute-start | bytes 786440 | tf_op jit(solution)/shard_map/ppermute | solution.py:441
  96.7 15.0 %collective-permute-start.15 = (bf16[256,512]{1,0:T(8,128)(2,1)S(1)}, bf16[256,512]{1,0:T(8,128)(2,1)}, u32[]{:S(2)}, u32[]{:S(2)}) collective-permute-start(bf16[256,512]{1,0:T(8,128)(2,1)S(1)} %slice.4.refs_4_), channel_id=1, source_target_pairs={{0,2},{1,3},{2,0},{3,1},{4,6},{5,7},{6,4},{7,5},{8,10},{9,11},{10,... | collective-permute-start | bytes 786440 | tf_op jit(solution)/shard_map/ppermute | solution.py:441
  98.2 13.5 %collective-permute-start.20 = (bf16[256,512]{1,0:T(8,128)(2,1)S(1)}, bf16[256,512]{1,0:T(8,128)(2,1)S(1)}, u32[]{:S(2)}, u32[]{:S(2)}) collective-permute-start(bf16[256,512]{1,0:T(8,128)(2,1)S(1)} %collective-permute-done.14.refs_6_), channel_id=1, source_target_pairs={{0,1},{1,0},{2,3},{3,2},{4,5},{5,4},{6,7},{7,6},{8,9},{9,8},{10,11... | collective-permute-start | bytes 786440 | tf_op jit(solution)/shard_map/ppermute | solution.py:441
  101.9 11.1 %copy-start = (bf16[256,1536]{1,0:T(8,128)(2,1)S(1)}, bf16[256,1536]{1,0:T(8,128)(2,1)}, u32[]{:S(2)}) copy-start(bf16[256,1536]{1,0:T(8,128)(2,1)} %get-tuple-element.83.refs_0_.refs_1_.refs_2_.refs_3_) | copy-start | bytes 2359300
  105.4 31.6 %copy-start.5 = (bf16[1536,256]{1,0:T(8,128)(2,1)S(1)}, bf16[1536,256]{1,0:T(8,128)(2,1)}, u32[]{:S(2)}) copy-start(bf16[1536,256]{1,0:T(8,128)(2,1)} %copy-done.4) | copy-start | bytes 2359300
  105.4 31.6 %copy-start.7 = (bf16[1536,256]{1,0:T(8,128)(2,1)S(1)}, bf16[1536,256]{1,0:T(8,128)(2,1)}, u32[]{:S(2)}) copy-start(bf16[1536,256]{1,0:T(8,128)(2,1)} %copy-done.6) | copy-start | bytes 2359300
  108.3 9.4 %collective-permute-start.10 = (bf16[256,512]{1,0:T(8,128)(2,1)}, bf16[256,512]{1,0:T(8,128)(2,1)}, u32[]{:S(2)}, u32[]{:S(2)}) collective-permute-start(bf16[256,512]{1,0:T(8,128)(2,1)} %get-tuple-element.80), channel_id=1, source_target_pairs={{0,2},{1,3},{2,0},{3,1},{4,6},{5,7},{6,4},{7,5},{8,10},{9,11},{10,... | collective-permute-start | bytes 786440 | tf_op jit(solution)/shard_map/ppermute | solution.py:441
  108.8 14.4 %collective-permute-start.11 = (bf16[256,512]{1,0:T(8,128)(2,1)}, bf16[256,512]{1,0:T(8,128)(2,1)}, u32[]{:S(2)}, u32[]{:S(2)}) collective-permute-start(bf16[256,512]{1,0:T(8,128)(2,1)} %get-tuple-element.81), channel_id=1, source_target_pairs={{0,4},{1,5},{2,6},{3,7},{4,0},{5,1},{6,2},{7,3},{8,12},{9,13},{10,... | collective-permute-start | bytes 786440 | tf_op jit(solution)/shard_map/ppermute | solution.py:441
  109.3 13.9 %collective-permute-start.9 = (bf16[256,512]{1,0:T(8,128)(2,1)}, bf16[256,512]{1,0:T(8,128)(2,1)}, u32[]{:S(2)}, u32[]{:S(2)}) collective-permute-start(bf16[256,512]{1,0:T(8,128)(2,1)} %get-tuple-element.79), channel_id=1, source_target_pairs={{0,6},{1,7},{2,4},{3,5},{4,2},{5,3},{6,0},{7,1},{8,14},{9,15},{10,... | collective-permute-start | bytes 786440 | tf_op jit(solution)/shard_map/ppermute | solution.py:441
  111.8 4.0 %collective-permute-start.19 = (bf16[256,512]{1,0:T(8,128)(2,1)}, bf16[256,512]{1,0:T(8,128)(2,1)}, u32[]{:S(2)}, u32[]{:S(2)}) collective-permute-start(bf16[256,512]{1,0:T(8,128)(2,1)} %collective-permute-done.16.refs_6_), channel_id=1, source_target_pairs={{0,1},{1,0},{2,3},{3,2},{4,5},{5,4},{6,7},{7,6},{8,9},{9,8},{10,11... | collective-permute-start | bytes 786440 | tf_op jit(solution)/shard_map/ppermute | solution.py:441
  112.5 3.3 %collective-permute-start.18 = (bf16[256,512]{1,0:T(8,128)(2,1)}, bf16[256,512]{1,0:T(8,128)(2,1)}, u32[]{:S(2)}, u32[]{:S(2)}) collective-permute-start(bf16[256,512]{1,0:T(8,128)(2,1)} %collective-permute-done.15.refs_4_), channel_id=1, source_target_pairs={{0,1},{1,0},{2,3},{3,2},{4,5},{5,4},{6,7},{7,6},{8,9},{9,8},{10,11... | collective-permute-start | bytes 786440 | tf_op jit(solution)/shard_map/ppermute | solution.py:441
  114.3 29.4 %copy-start.9 = (bf16[1536,256]{1,0:T(8,128)(2,1)S(1)}, bf16[1536,256]{1,0:T(8,128)(2,1)}, u32[]{:S(2)}) copy-start(bf16[1536,256]{1,0:T(8,128)(2,1)} %copy-done.8) | copy-start | bytes 2359300
  114.3 29.4 %copy-start.11 = (bf16[1536,256]{1,0:T(8,128)(2,1)S(1)}, bf16[1536,256]{1,0:T(8,128)(2,1)}, u32[]{:S(2)}) copy-start(bf16[1536,256]{1,0:T(8,128)(2,1)} %copy-done.10) | copy-start | bytes 2359300
  114.3 29.4 %copy-start.13 = (bf16[1536,256]{1,0:T(8,128)(2,1)S(1)}, bf16[1536,256]{1,0:T(8,128)(2,1)}, u32[]{:S(2)}) copy-start(bf16[1536,256]{1,0:T(8,128)(2,1)} %copy-done.12) | copy-start | bytes 2359300
  114.3 29.4 %copy-start.15 = (bf16[1536,256]{1,0:T(8,128)(2,1)S(1)}, bf16[1536,256]{1,0:T(8,128)(2,1)}, u32[]{:S(2)}) copy-start(bf16[1536,256]{1,0:T(8,128)(2,1)} %copy-done.14) | copy-start | bytes 2359300
  123.2 1.0 copy-start.17
  124.2 0.9 copy-start.22
  126.8 10.3 %collective-permute-start.26 = (bf16[256,512]{1,0:T(8,128)(2,1)S(1)}, bf16[256,512]{1,0:T(8,128)(2,1)S(1)}, u32[]{:S(2)}, u32[]{:S(2)}) collective-permute-start(bf16[256,512]{1,0:T(8,128)(2,1)S(1)} %key_backward.1.refs_4_), channel_id=1, source_target_pairs={{0,6},{1,7},{2,4},{3,5},{4,2},{5,3},{6,0},{7,1},{8,14},{9,15},{10,... | collective-permute-start | bytes 786440 | tf_op jit(solution)/shard_map/ppermute | solution.py:441
  128.3 14.8 %collective-permute-start.23 = (bf16[256,512]{1,0:T(8,128)(2,1)S(1)}, bf16[256,512]{1,0:T(8,128)(2,1)S(1)}, u32[]{:S(2)}, u32[]{:S(2)}) collective-permute-start(bf16[256,512]{1,0:T(8,128)(2,1)S(1)} %key_backward.1.refs_4_), channel_id=1, source_target_pairs={{0,4},{1,5},{2,6},{3,7},{4,0},{5,1},{6,2},{7,3},{8,12},{9,13},{10,... | collective-permute-start | bytes 786440 | tf_op jit(solution)/shard_map/ppermute | solution.py:441
  129.8 13.9 %collective-permute-start.21 = (bf16[256,512]{1,0:T(8,128)(2,1)S(1)}, bf16[256,512]{1,0:T(8,128)(2,1)S(1)}, u32[]{:S(2)}, u32[]{:S(2)}) collective-permute-start(bf16[256,512]{1,0:T(8,128)(2,1)S(1)} %key_backward.1.refs_4_), channel_id=1, source_target_pairs={{0,2},{1,3},{2,0},{3,1},{4,6},{5,7},{6,4},{7,5},{8,10},{9,11},{10,... | collective-permute-start | bytes 786440 | tf_op jit(solution)/shard_map/ppermute | solution.py:441
  130.4 19.4 %collective-permute-start.25 = (bf16[256,512]{1,0:T(8,128)(2,1)S(1)}, bf16[256,512]{1,0:T(8,128)(2,1)S(1)}, u32[]{:S(2)}, u32[]{:S(2)}) collective-permute-start(bf16[256,512]{1,0:T(8,128)(2,1)S(1)} %key_backward.1.refs_4_), channel_id=1, source_target_pairs={{0,1},{1,0},{2,3},{3,2},{4,5},{5,4},{6,7},{7,6},{8,9},{9,8},{10,11... | collective-permute-start | bytes 786440 | tf_op jit(solution)/shard_map/ppermute | solution.py:441
  137.0 12.7 %collective-permute-start.27 = (bf16[256,512]{1,0:T(8,128)(2,1)S(1)}, bf16[256,512]{1,0:T(8,128)(2,1)S(1)}, u32[]{:S(2)}, u32[]{:S(2)}) collective-permute-start(bf16[256,512]{1,0:T(8,128)(2,1)S(1)} %collective-permute-done.26.refs_6_), channel_id=1, source_target_pairs={{0,1},{1,0},{2,3},{3,2},{4,5},{5,4},{6,7},{7,6},{8,9},{9,8},{10,11... | collective-permute-start | bytes 786440 | tf_op jit(solution)/shard_map/ppermute | solution.py:441
  137.1 1.0 copy-start.24
  138.0 0.9 copy-start.26
  139.0 0.9 copy-start.28
  143.1 9.9 %collective-permute-start.24 = (bf16[256,512]{1,0:T(8,128)(2,1)S(1)}, bf16[256,512]{1,0:T(8,128)(2,1)S(1)}, u32[]{:S(2)}, u32[]{:S(2)}) collective-permute-start(bf16[256,512]{1,0:T(8,128)(2,1)S(1)} %collective-permute-done.23.refs_6_), channel_id=1, source_target_pairs={{0,1},{1,0},{2,3},{3,2},{4,5},{5,4},{6,7},{7,6},{8,9},{9,8},{10,11... | collective-permute-start | bytes 786440 | tf_op jit(solution)/shard_map/ppermute | solution.py:441
  143.7 9.3 %collective-permute-start.22 = (bf16[256,512]{1,0:T(8,128)(2,1)S(1)}, bf16[256,512]{1,0:T(8,128)(2,1)S(1)}, u32[]{:S(2)}, u32[]{:S(2)}) collective-permute-start(bf16[256,512]{1,0:T(8,128)(2,1)S(1)} %collective-permute-done.21.refs_4_), channel_id=1, source_target_pairs={{0,1},{1,0},{2,3},{3,2},{4,5},{5,4},{6,7},{7,6},{8,9},{9,8},{10,11... | collective-permute-start | bytes 786440 | tf_op jit(solution)/shard_map/ppermute | solution.py:441
  149.8 15.9 %copy-start.3 = (f32[4,384,128]{2,1,0:T(8,128)S(1)}, f32[4,384,128]{2,1,0:T(8,128)}, u32[]{:S(2)}) copy-start(f32[4,384,128]{2,1,0:T(8,128)} %get-tuple-element.90.w_ref) | copy-start | bytes 2359300
  149.8 15.9 %copy-start.18 = (f32[4,384,128]{2,1,0:T(8,128)S(1)}, f32[4,384,128]{2,1,0:T(8,128)}, u32[]{:S(2)}) copy-start(f32[4,384,128]{2,1,0:T(8,128)} %get-tuple-element.93.m_ref) | copy-start | bytes 2359300
  149.8 15.9 %copy-start.19 = (f32[4,384,128]{2,1,0:T(8,128)S(1)}, f32[4,384,128]{2,1,0:T(8,128)}, u32[]{:S(2)}) copy-start(f32[4,384,128]{2,1,0:T(8,128)} %get-tuple-element.94.v_ref) | copy-start | bytes 2359300
  157.9 1.2 collective-permute-start.28
  159.1 4.5 %collective-permute-start.31 = (f32[8,128]{1,0:T(8,128)S(1)}, f32[8,128]{1,0:T(8,128)S(1)}, u32[]{:S(2)}, u32[]{:S(2)}) collective-permute-start(f32[8,128]{1,0:T(8,128)S(1)} %add.44.refs_0_), channel_id=1, source_target_pairs={{0,6},{1,7},{2,4},{3,5},{4,2},{5,3},{6,0},{7,1},{8,14},{9,15},{10,... | collective-permute-start | bytes 12296 | tf_op jit(solution)/shard_map/ppermute | solution.py:441
  160.5 3.6 %collective-permute-start.30 = (f32[8,128]{1,0:T(8,128)S(1)}, f32[8,128]{1,0:T(8,128)S(1)}, u32[]{:S(2)}, u32[]{:S(2)}) collective-permute-start(f32[8,128]{1,0:T(8,128)S(1)} %add.44.refs_0_), channel_id=1, source_target_pairs={{0,4},{1,5},{2,6},{3,7},{4,0},{5,1},{6,2},{7,3},{8,12},{9,13},{10,... | collective-permute-start | bytes 12296 | tf_op jit(solution)/shard_map/ppermute | solution.py:441
  162.1 3.6 %collective-permute-start.29 = (f32[8,128]{1,0:T(8,128)S(1)}, f32[8,128]{1,0:T(8,128)S(1)}, u32[]{:S(2)}, u32[]{:S(2)}) collective-permute-start(f32[8,128]{1,0:T(8,128)S(1)} %add.44.refs_0_), channel_id=1, source_target_pairs={{0,2},{1,3},{2,0},{3,1},{4,6},{5,7},{6,4},{7,5},{8,10},{9,11},{10,... | collective-permute-start | bytes 12296 | tf_op jit(solution)/shard_map/ppermute | solution.py:441
  167.2 14.3 %collective-permute-start.32 = (bf16[384,128]{1,0:T(8,128)(2,1)S(1)}, bf16[384,128]{1,0:T(8,128)(2,1)S(1)}, u32[]{:S(2)}, u32[]{:S(2)}) collective-permute-start(bf16[384,128]{1,0:T(8,128)(2,1)S(1)} %get-tuple-element.114), channel_id=1, source_target_pairs={{0,8},{8,0},{16,24},{24,16},{1,9},{9,1},{17,25},{25,17},{2,10},{10... | collective-permute-start | bytes 294920 | tf_op jit(solution)/shard_map/ppermute | solution.py:441
  169.0 12.4 %collective-permute-start.33 = (bf16[384,128]{1,0:T(8,128)(2,1)S(1)}, bf16[384,128]{1,0:T(8,128)(2,1)S(1)}, u32[]{:S(2)}, u32[]{:S(2)}) collective-permute-start(bf16[384,128]{1,0:T(8,128)(2,1)S(1)} %get-tuple-element.115), channel_id=1, source_target_pairs={{0,16},{8,24},{16,0},{24,8},{1,17},{9,25},{17,1},{25,9},{2,18},{10... | collective-permute-start | bytes 294920 | tf_op jit(solution)/shard_map/ppermute | solution.py:441
  171.4 10.1 %collective-permute-start.34 = (bf16[384,128]{1,0:T(8,128)(2,1)S(1)}, bf16[384,128]{1,0:T(8,128)(2,1)S(1)}, u32[]{:S(2)}, u32[]{:S(2)}) collective-permute-start(bf16[384,128]{1,0:T(8,128)(2,1)S(1)} %get-tuple-element.116), channel_id=1, source_target_pairs={{0,24},{8,16},{16,8},{24,0},{1,25},{9,17},{17,9},{25,1},{2,26},{10... | collective-permute-start | bytes 294920 | tf_op jit(solution)/shard_map/ppermute | solution.py:441
  171.7 14.4 %copy-start.16 = (f32[1,384,128]{2,1,0:T(8,128)S(1)}, f32[1,384,128]{2,1,0:T(8,128)}, u32[]{:S(2)}) copy-start(f32[1,384,128]{2,1,0:T(8,128)} %get-tuple-element.88) | copy-start | bytes 589828
  171.7 14.4 %copy-start.30 = (f32[384,128]{1,0:T(8,128)S(1)}, f32[384,128]{1,0:T(8,128)}, u32[]{:S(2)}) copy-start(f32[384,128]{1,0:T(8,128)} %copy-done.29) | copy-start | bytes 589828
  181.6 14.3 %collective-permute-start.37 = (bf16[384,128]{1,0:T(8,128)(2,1)S(1)}, bf16[384,128]{1,0:T(8,128)(2,1)S(1)}, u32[]{:S(2)}, u32[]{:S(2)}) collective-permute-start(bf16[384,128]{1,0:T(8,128)(2,1)S(1)} %convert_element_type.24.refs_7_), channel_id=1, source_target_pairs={{0,24},{8,16},{16,8},{24,0},{1,25},{9,17},{17,9},{25,1},{2,26},{10... | collective-permute-start | bytes 294920 | tf_op jit(solution)/shard_map/ppermute | solution.py:441
  185.2 10.7 %collective-permute-start.36 = (bf16[384,128]{1,0:T(8,128)(2,1)S(1)}, bf16[384,128]{1,0:T(8,128)(2,1)S(1)}, u32[]{:S(2)}, u32[]{:S(2)}) collective-permute-start(bf16[384,128]{1,0:T(8,128)(2,1)S(1)} %convert_element_type.24.refs_7_), channel_id=1, source_target_pairs={{0,16},{8,24},{16,0},{24,8},{1,17},{9,25},{17,1},{25,9},{2,18},{10... | collective-permute-start | bytes 294920 | tf_op jit(solution)/shard_map/ppermute | solution.py:441
  185.2 10.7 %collective-permute-start.35 = (bf16[384,128]{1,0:T(8,128)(2,1)S(1)}, bf16[384,128]{1,0:T(8,128)(2,1)S(1)}, u32[]{:S(2)}, u32[]{:S(2)}) collective-permute-start(bf16[384,128]{1,0:T(8,128)(2,1)S(1)} %convert_element_type.24.refs_7_), channel_id=1, source_target_pairs={{0,8},{8,0},{16,24},{24,16},{1,9},{9,1},{17,25},{25,17},{2,10},{10... | collective-permute-start | bytes 294920 | tf_op jit(solution)/shard_map/ppermute | solution.py:441
  186.1 9.8 %copy-start.20 = (f32[1,384,128]{2,1,0:T(8,128)S(1)}, f32[1,384,128]{2,1,0:T(8,128)}, u32[]{:S(2)}) copy-start(f32[1,384,128]{2,1,0:T(8,128)} %get-tuple-element.89) | copy-start | bytes 589828
  (7 other events, 5.6 us)

commit v9 on v8

--- a/solution.py
+++ b/solution.py
@@ -445,9 +445,15 @@
     return lax.optimization_barrier((value,) + others)[0]
 
 
-def by_device(pieces, me):
-    count = pieces.shape[0]
-    return jnp.stack([lax.dynamic_index_in_dim(pieces, me ^ k, 0, keepdims=False) for k in range(count)])
+class Line:
+    def __init__(self, axis, window):
+        self.axis, self.window, self.ended = axis, window, []
+
+    def swap(self, block, offset):
+        if len(self.ended) >= self.window:
+            block = after(block, self.ended[-self.window])
+        self.ended.append(swap(block, self.axis, offset))
+        return self.ended[-1]
 
 
 def body(
@@ -475,22 +481,20 @@
     order = [k for k in far[:-2] for k in (k, k + 1)]
     order += far[-2:] + [k + 1 for k in far[-2:]]
 
-    packed = pack(inputs, me, rows, tuple(order[:1]))
-    packed |= pack(inputs, me, rows, tuple(order[1:4]))
-    packed |= pack(inputs, me, rows, tuple(order[4:]))
-    blocks = {k: swap(packed[k], "fsdp", k) for k in order}
-    early = packed[order[-1]]
+    line = Line("fsdp", 3)
+    packed = {}
+    for offsets in (order[:1], order[1:4], order[4:]):
+        packed |= pack(inputs, me, rows, tuple(offsets))
+    blocks = {k: line.swap(packed[k], k) for k in order}
+    early = blocks[order[0]]
     packed |= pack(inputs, after(me, early), rows, (0, 1))
     blocks[0], blocks[1] = packed[0], swap(packed[1], "fsdp", 1)
 
     values = {0: incoming[:, kv_width:]}
-    for i, k in enumerate(far):
-        values[k] = swap(after(values[0], blocks[order[i]]), "fsdp", k)
+    for k in reversed(far):
+        values[k] = line.swap(values[0], k)
     for k in range(0, shards, 2):
         values[k + 1] = swap(values[k], "fsdp", 1)
-
-    def to_all(pieces):
-        return lax.all_to_all(pieces, "rep", 0, 0, tiled=True)
 
     steps_now = step_count[0].astype(jnp.float32)
     plan = jnp.minimum(1.0, steps_now / WARMUP) * (
@@ -501,13 +505,13 @@
     inv_two = 1.0 / (1.0 - jnp.power(BETA_TWO, steps_now))
     scalars = jnp.stack([rate, inv_one, inv_two])
     place_early = after(place, early)
-    old, old_first, old_second = due_columns(place_early, part, params, first_moment[0], second_moment[0])
+    (old,) = due_columns(place_early, part, params)
+    old_first, old_second = due_columns(place_early, part, first_moment[0], second_moment[0])
     anchor_cols, moment_cols = (c[0] for c in due_columns(place_early, part, anchor, momentum))
-    old_sum = jnp.sum(to_all(by_device(old, my_rep)), axis=0)
+    old_sum = sum([swap(old[k], "rep", k) for k in range(1, replicas)], old[0])
     pseudo_old = anchor_cols - old_sum / replicas
     base = anchor_cols - OUTER_RATE * (OUTER_MU * (OUTER_MU * moment_cols + pseudo_old) + pseudo_old)
-    base = by_device(to_all(jnp.broadcast_to(base[None], (replicas,) + base.shape)), my_rep)
-    base = [base[j] for j in range(replicas)]
+    base = [base] + [swap(base, "rep", k) for k in range(1, replicas)]
     anchor_copy, momentum_copy = duplicate(anchor, momentum)
     key_weights = cast_left(after(params, early), kv_width)
 
@@ -516,8 +520,12 @@
         theirs, flipped[k + 1] = partial_keys(blocks[k + 1], key_weights)
         part_k, flipped[k] = partial_keys(blocks[k], key_weights, swap(theirs, "fsdp", 1))
         parts.append(swap(part_k, "fsdp", k) if k else part_k)
+    spread = [0, 1] + [k + odd for k in far for odd in range(2)]
+    near, rest = spread[:shards // 2], spread[shards // 2:]
+    pick = lambda table, which: [table[k] for k in which]
+    (values_first,) = gradient(place, pick(flipped, near), pick(values, near), last=False)
     parts[-1] = after(
-        parts[-1], *base, anchor_copy, momentum_copy, old_first, old_second, scalars, *values.values()
+        parts[-1], *base, anchor_copy, momentum_copy, old_first, old_second, scalars, values_first
     )
     keys = {0: key_backward(parts, incoming, 0)}
     for k in far:
@@ -525,10 +533,6 @@
     for k in range(0, shards, 2):
         keys[k + 1] = swap(keys[k], "fsdp", 1)
 
-    spread = [0, 1] + [k + odd for k in far for odd in range(2)]
-    near, rest = spread[:shards // 2], spread[shards // 2:]
-    pick = lambda table, which: [table[k] for k in which]
-    (values_first,) = gradient(place, pick(flipped, near), pick(values, near), last=False)
     grad_values, square, due = gradient(place, pick(flipped, rest), pick(values, rest), values_first)
     (keys_first,) = gradient(place, pick(flipped, near), pick(keys, near), last=False)
     grad_keys, square, due = gradient(

time: 200 us -> 199 us (level)
  waiting for transfers between devices: 54.5 us -> 73.8 us
  local copies, waits for them, and re-layouts: 17 us -> 0.97 us
  other arithmetic: 3.45 us -> 0.31 us
    ppermute x38 -> x44, waiting for transfers between devices: 54.5 us -> 73.8 us  [swap(): return lax.ppermute(block, axis, [(i, i ^ offset) for i in range(count)])]
    ppermute x38 -> x44, starting transfers between devices: 35.6 us -> 47.3 us  [swap(): return lax.ppermute(block, axis, [(i, i ^ offset) for i in range(count)])]
    all_to_all x2 -> x0, starting transfers between devices: 11.4 us -> none  [to_all(): return lax.all_to_all(pieces, 'rep', 0, 0, tiled=True)]
    unnamed x62 -> x20, local copies, waits for them, and re-layouts: 12.2 us -> 0.91 us
    pallas_call x2 -> x3, Pallas kernels: 6.83 us -> 10.3 us  [due_columns(): pl.pallas_call(pick_kernel, out_shape=[pltpu.HBM((blocks, part, FRAG_COLS...]
    pallas_call x8, Pallas kernels: 9.17 us -> 5.85 us  [partial_keys(): pl.pallas_call(functools.partial(partial_kernel, pieces), out_shape=[jax....]
  transfers between devices with their start and end apart: 40 -> 44, of which waited for: 11 -> 15; matrix products, arithmetic and copies ran while one was open for 3% -> 0% of each run, Pallas kernels for 28% -> 31%
where the time goes in v9:
time: 199 us
  waiting for transfers between devices  73.8 us (37%)
  Pallas kernels  72.5 us (36%)
  starting transfers between devices  47.3 us (24%)
  between operations  3.68 us (2%)
    ppermute x44, waiting for transfers between devices, swap(): return lax.ppermute(block, axis, [(i, i ^ offset) for i in range(count)])  73.8 us
    ppermute x44, starting transfers between devices, swap(): return lax.ppermute(block, axis, [(i, i ^ offset) for i in range(count)])  47.3 us
    pallas_call x2, Pallas kernels, adam_rows(): pl.pallas_call(functools.partial(adam_kernel, len(squares), len(into)), o...  19.5 us
    pallas_call x4, Pallas kernels, gradient(): pl.pallas_call(functools.partial(grad_kernel, len(flipped), base is not N...  17 us
    pallas_call x3, Pallas kernels, due_columns(): pl.pallas_call(pick_kernel, out_shape=[pltpu.HBM((blocks, part, FRAG_COLS...  10.3 us
    pallas_call x4, Pallas kernels, pack(): pl.pallas_call(functools.partial(pack_kernel, offsets), out_shape=[pltpu....  9.19 us
    pallas_call x8, Pallas kernels, partial_keys(): pl.pallas_call(functools.partial(partial_kernel, pieces), out_shape=[jax....  5.85 us
  transfers between devices with their start and end apart: 44, of which 15 were waited for; matrix products, arithmetic and copies ran while one was open for 0% of the time, Pallas kernels for 31%

profile of v9, /device:TPU:0, one launch (start us, length us, event | category | flops | bytes accessed | tf_op | source)
XLA Modules:
  0.0 198.7 jit_solution(12786666688944496595)
XLA Ops:
  0.6 2.0 pack.5
  2.6 4.0 %collective-permute-start.1 = (bf16[256,1536]{1,0:T(8,128)(2,1)}, bf16[256,1536]{1,0:T(8,128)(2,1)S(1)}, u32[]{:S(2)}, u32[]{:S(2)}) collective-permute-start(bf16[256,1536]{1,0:T(8,128)(2,1)} %pack.5), channel_id=1, source_target_pairs={{0,6},{1,7},{2,4},{3,5},{4,2},{5,3},{6,0},{7,1},{8,14},{9,15},{10,... | collective-permute-start | bytes 2359304 | tf_op jit(solution)/shard_map/ppermute | solution.py:441
  6.6 2.6 %pack.4 = (bf16[256,1536]{1,0:T(8,128)(2,1)}, bf16[256,1536]{1,0:T(8,128)(2,1)}, bf16[256,1536]{1,0:T(8,128)(2,1)}) custom-call(s32[1]{0:T(128)} %bitcast.4.me_ref, bf16[256,12288]{1,0:T(8,128)(2,1)} %bitcast.40), custom_call_target="tpu_custom_call" | custom-call | bytes 4718592 | tf_op jit(solution)/shard_map/pack/pallas_call | solution.py:68
  9.2 0.6 collective-permute-start
  10.1 2.3 %pack.6 = (bf16[256,1536]{1,0:T(8,128)(2,1)}, bf16[256,1536]{1,0:T(8,128)(2,1)}) custom-call(s32[1]{0:T(128)} %bitcast.4.me_ref, bf16[256,12288]{1,0:T(8,128)(2,1)} %bitcast.41), custom_call_target="tpu_custom_call" | custom-call | bytes 3145728 | tf_op jit(solution)/shard_map/pack/pallas_call | solution.py:68
  12.4 12.7 %collective-permute-done.1.refs_0_.refs_1_.refs_2_.refs_3_ = bf16[256,1536]{1,0:T(8,128)(2,1)S(1)} collective-permute-done((bf16[256,1536]{1,0:T(8,128)(2,1)}, bf16[256,1536]{1,0:T(8,128)(2,1)S(1)}, u32[]{:S(2)}, u32[]{:S(2)}) %collective-permute-start.1) | collective-permute-done | bytes 786464 | tf_op jit(solution)/shard_map/ppermute | solution.py:441
  25.2 2.3 %pack.7 = (bf16[256,1536]{1,0:T(8,128)(2,1)}, bf16[256,1536]{1,0:T(8,128)(2,1)}) custom-call(s32[1]{0:T(128)} %bitcast.4.me_ref, bf16[256,12288]{1,0:T(8,128)(2,1)} %bitcast.42), custom_call_target="tpu_custom_call" | custom-call | bytes 3145728 | tf_op jit(solution)/shard_map/pack/pallas_call | solution.py:68
  27.5 15.0 %collective-permute-done.refs_0_.refs_1_.refs_2_.refs_3_ = bf16[256,1536]{1,0:T(8,128)(2,1)S(1)} collective-permute-done((bf16[256,1536]{1,0:T(8,128)(2,1)}, bf16[256,1536]{1,0:T(8,128)(2,1)S(1)}, u32[]{:S(2)}, u32[]{:S(2)}) %collective-permute-start) | collective-permute-done | bytes 786464 | tf_op jit(solution)/shard_map/ppermute | solution.py:441
  42.6 14.9 %collective-permute-done.2.refs_0_.refs_1_.refs_2_.refs_3_ = bf16[256,1536]{1,0:T(8,128)(2,1)S(1)} collective-permute-done((bf16[256,1536]{1,0:T(8,128)(2,1)}, bf16[256,1536]{1,0:T(8,128)(2,1)S(1)}, u32[]{:S(2)}, u32[]{:S(2)}) %collective-permute-start.2) | collective-permute-done | bytes 786464 | tf_op jit(solution)/shard_map/ppermute | solution.py:441
  57.4 0.9 copy-done.1
  58.3 1.8 collective-permute-start.3
  60.9 1.6 collective-permute-start.5
  62.5 3.8 %due_columns.4.w_ref = f32[4,384,128]{2,1,0:T(8,128)} custom-call(s32[2]{0:T(128)S(1)} %pad_add_fusion.place_ref, f32[1536,1024]{1,0:T(8,128)} %bitcast.43), custom_call_target="tpu_custom_call" | custom-call | bytes 1572864 | tf_op jit(solution)/shard_map/due_columns/pallas_call | solution.py:339
  66.4 3.5 %cast_left.1.refs_4_ = bf16[1536,512]{1,0:T(8,128)(2,1)S(1)} custom-call(f32[1536,1024]{1,0:T(8,128)} %bitcast.44), custom_call_target="tpu_custom_call" | custom-call | bytes 4718592 | tf_op jit(solution)/shard_map/cast_left/pallas_call | solution.py:92
  69.9 0.6 partial_keys.12
  70.8 1.6 collective-permute-start.14
  72.5 2.5 %collective-permute-done.6.refs_0_.refs_1_.refs_2_.refs_3_ = bf16[256,1536]{1,0:T(8,128)(2,1)S(1)} collective-permute-done((bf16[256,1536]{1,0:T(8,128)(2,1)}, bf16[256,1536]{1,0:T(8,128)(2,1)S(1)}, u32[]{:S(2)}, u32[]{:S(2)}) %collective-permute-start.6) | collective-permute-done | bytes 786464 | tf_op jit(solution)/shard_map/ppermute | solution.py:441
  75.0 3.8 %collective-permute-start.16 = (f32[384,128]{1,0:T(8,128)S(1)}, f32[384,128]{1,0:T(8,128)S(1)}, u32[]{:S(2)}, u32[]{:S(2)}) collective-permute-start(f32[384,128]{1,0:T(8,128)S(1)} %get-tuple-element.133), channel_id=1, source_target_pairs={{0,24},{8,16},{16,8},{24,0},{1,25},{9,17},{17,9},{25,1},{2,26},{10... | collective-permute-start | bytes 589832 | tf_op jit(solution)/shard_map/ppermute | solution.py:441
  78.8 1.6 collective-permute-start.15
  80.3 2.3 %due_columns.3 = (f32[1,384,128]{2,1,0:T(8,128)}, f32[1,384,128]{2,1,0:T(8,128)}) custom-call(s32[2]{0:T(128)S(1)} %pad_add_fusion.place_ref, f32[384,1024]{1,0:T(8,128)} %refs_0_.3, f32[384,1024]{1,0:T(8,128)} %refs_1_.3), custom_call_target="tpu_custom_call" | custom-call | bytes 786432 | tf_op jit(solution)/shard_map/due_columns/pallas_call | solution.py:339
  82.7 0.6 partial_keys.10
  83.2 0.6 partial_keys.14
  83.8 1.8 partial_keys.8
  85.6 0.6 collective-permute-start.13
  86.2 2.1 %collective-permute-start.21 = (bf16[256,512]{1,0:T(8,128)(2,1)S(1)}, bf16[256,512]{1,0:T(8,128)(2,1)S(1)}, u32[]{:S(2)}, u32[]{:S(2)}) collective-permute-start(bf16[256,512]{1,0:T(8,128)(2,1)S(1)} %slice.24.refs_4_), channel_id=1, source_target_pairs={{0,6},{1,7},{2,4},{3,5},{4,2},{5,3},{6,0},{7,1},{8,14},{9,15},{10,... | collective-permute-start | bytes 786440 | tf_op jit(solution)/shard_map/ppermute | solution.py:441
  88.3 7.3 %collective-permute-done.15 = f32[384,128]{1,0:T(8,128)S(1)} collective-permute-done((f32[384,128]{1,0:T(8,128)S(1)}, f32[384,128]{1,0:T(8,128)S(1)}, u32[]{:S(2)}, u32[]{:S(2)}) %collective-permute-start.15) | collective-permute-done | bytes 196640 | tf_op jit(solution)/shard_map/ppermute | solution.py:441
  96.3 1.0 collective-permute-done.5.refs_0_.refs_1_.refs_2_.refs_3_
  97.3 3.8 %collective-permute-start.19 = (f32[384,128]{1,0:T(8,128)S(1)}, f32[384,128]{1,0:T(8,128)S(1)}, u32[]{:S(2)}, u32[]{:S(2)}) collective-permute-start(f32[384,128]{1,0:T(8,128)S(1)} %get-tuple-element.130.refs_3_), channel_id=1, source_target_pairs={{0,24},{8,16},{16,8},{24,0},{1,25},{9,17},{17,9},{25,1},{2,26},{10... | collective-permute-start | bytes 589832 | tf_op jit(solution)/shard_map/ppermute | solution.py:441
  101.7 2.8 %duplicate.1 = (f32[384,1024]{1,0:T(8,128)}, f32[384,1024]{1,0:T(8,128)}) custom-call(f32[384,1024]{1,0:T(8,128)} %refs_0_.3, f32[384,1024]{1,0:T(8,128)} %refs_1_.3), custom_call_target="tpu_custom_call" | custom-call | bytes 6291456 | tf_op jit(solution)/shard_map/duplicate/pallas_call | solution.py:380
  105.4 0.6 partial_keys.13
  106.0 0.6 partial_keys.9
  106.6 0.6 partial_keys.11
  107.2 2.8 %collective-permute-start.9 = (bf16[256,512]{1,0:T(8,128)(2,1)S(1)}, bf16[256,512]{1,0:T(8,128)(2,1)S(1)}, u32[]{:S(2)}, u32[]{:S(2)}) collective-permute-start(bf16[256,512]{1,0:T(8,128)(2,1)S(1)} %get-tuple-element.84), channel_id=1, source_target_pairs={{0,6},{1,7},{2,4},{3,5},{4,2},{5,3},{6,0},{7,1},{8,14},{9,15},{10,... | collective-permute-start | bytes 786440 | tf_op jit(solution)/shard_map/ppermute | solution.py:441
  110.0 4.9 %collective-permute-done.18.refs_5_ = f32[384,128]{1,0:T(8,128)S(1)} collective-permute-done((f32[384,128]{1,0:T(8,128)S(1)}, f32[384,128]{1,0:T(8,128)S(1)}, u32[]{:S(2)}, u32[]{:S(2)}) %collective-permute-start.18) | collective-permute-done | bytes 196640 | tf_op jit(solution)/shard_map/ppermute | solution.py:441
  114.9 1.6 collective-permute-start.32
  116.5 1.5 collective-permute-start.10
  118.5 4.2 %due_columns.5 = (f32[4,384,128]{2,1,0:T(8,128)}, f32[4,384,128]{2,1,0:T(8,128)}) custom-call(s32[2]{0:T(128)S(1)} %pad_add_fusion.place_ref, f32[1536,1024]{1,0:T(8,128)} %bitcast.47, f32[1536,1024]{1,0:T(8,128)} %bitcast.50), custom_call_target="tpu_custom_call" | custom-call | bytes 3145728 | tf_op jit(solution)/shard_map/due_columns/pallas_call | solution.py:339
  122.7 0.6 partial_keys.15
  123.3 0.6 collective-permute-start.30
  123.9 4.1 %gradient.4.refs_8_ = f32[1536,512]{1,0:T(8,128)S(1)} custom-call(s32[2]{0:T(128)S(1)} %pad_add_fusion.place_ref, bf16[1536,256]{1,0:T(8,128)(2,1)S(1)} %get-tuple-element.99.refs_0_, bf16[1536,256]{1,0:T(8,128)(2,1)S(1)} %get-tuple-element.100.refs_1_, bf16[1536,256]{1,0:T(8,128)(2,1)S(1)} %get-tuple-element.101.refs_2_, ...), custom_call_target="tpu_custom_call" | custom-call | flops 1610612736 | bytes 6291456 | tf_op jit(solution)/shard_map/gradient/pallas_call | solution.py:232
  128.1 0.6 collective-permute-done.11.refs_2_
  129.3 2.6 %collective-permute-start.28 = (bf16[256,512]{1,0:T(8,128)(2,1)S(1)}, bf16[256,512]{1,0:T(8,128)(2,1)S(1)}, u32[]{:S(2)}, u32[]{:S(2)}) collective-permute-start(bf16[256,512]{1,0:T(8,128)(2,1)S(1)} %key_backward.1.refs_4_), channel_id=1, source_target_pairs={{0,6},{1,7},{2,4},{3,5},{4,2},{5,3},{6,0},{7,1},{8,14},{9,15},{10,... | collective-permute-start | bytes 786440 | tf_op jit(solution)/shard_map/ppermute | solution.py:441
  132.3 0.5 collective-permute-start.23
  133.4 6.1 %collective-permute-done.28.refs_6_ = bf16[256,512]{1,0:T(8,128)(2,1)S(1)} collective-permute-done((bf16[256,512]{1,0:T(8,128)(2,1)S(1)}, bf16[256,512]{1,0:T(8,128)(2,1)S(1)}, u32[]{:S(2)}, u32[]{:S(2)}) %collective-permute-start.28) | collective-permute-done | bytes 262176 | tf_op jit(solution)/shard_map/ppermute | solution.py:441
  139.5 4.5 %collective-permute-done.25.refs_6_ = bf16[256,512]{1,0:T(8,128)(2,1)S(1)} collective-permute-done((bf16[256,512]{1,0:T(8,128)(2,1)S(1)}, bf16[256,512]{1,0:T(8,128)(2,1)S(1)}, u32[]{:S(2)}, u32[]{:S(2)}) %collective-permute-start.25) | collective-permute-done | bytes 262176 | tf_op jit(solution)/shard_map/ppermute | solution.py:441
  144.5 4.8 %gradient.6 = (f32[1536,512]{1,0:T(8,128)}, f32[8,128]{1,0:T(8,128)S(1)}, f32[1536,128]{1,0:T(8,128)S(1)}) custom-call(s32[2]{0:T(128)S(1)} %pad_add_fusion.place_ref, bf16[1536,256]{1,0:T(8,128)(2,1)S(1)} %get-tuple-element.74.refs_0_, bf16[1536,256]{1,0:T(8,128)(2,1)S(1)} %get-tuple-element.75.refs_1_, bf16[1536,256]{1,0:T(8,128)(2,1)S(1)} %get-tuple-element.81.refs_2_, ...), custom_call_target="tpu_custom_call" | custom-call | flops 1610612736 | bytes 6291456 | tf_op jit(solution)/shard_map/gradient/pallas_call | solution.py:232
  149.3 3.2 %gradient.5.refs_8_ = f32[1536,512]{1,0:T(8,128)S(1)} custom-call(s32[2]{0:T(128)S(1)} %pad_add_fusion.place_ref, bf16[1536,256]{1,0:T(8,128)(2,1)S(1)} %get-tuple-element.99.refs_0_, bf16[1536,256]{1,0:T(8,128)(2,1)S(1)} %get-tuple-element.100.refs_1_, bf16[1536,256]{1,0:T(8,128)(2,1)S(1)} %get-tuple-element.101.refs_2_, ...), custom_call_target="tpu_custom_call" | custom-call | flops 1610612736 | bytes 6291456 | tf_op jit(solution)/shard_map/gradient/pallas_call | solution.py:232
  152.5 4.8 %gradient.7 = (f32[1536,512]{1,0:T(8,128)}, f32[8,128]{1,0:T(8,128)S(1)}, f32[1536,128]{1,0:T(8,128)S(1)}) custom-call(s32[2]{0:T(128)S(1)} %pad_add_fusion.place_ref, bf16[1536,256]{1,0:T(8,128)(2,1)S(1)} %get-tuple-element.74.refs_0_, bf16[1536,256]{1,0:T(8,128)(2,1)S(1)} %get-tuple-element.75.refs_1_, bf16[1536,256]{1,0:T(8,128)(2,1)S(1)} %get-tuple-element.81.refs_2_, ...), custom_call_target="tpu_custom_call" | custom-call | flops 1610612736 | bytes 6291456 | tf_op jit(solution)/shard_map/gradient/pallas_call | solution.py:232
  157.6 1.0 collective-permute-done.34
  158.5 1.7 collective-permute-start.37
  160.3 1.2 collective-permute-start.36
  161.5 0.5 collective-permute-start.35
  162.0 1.0 collective-permute-done.37.refs_3_
  163.0 0.8 collective-permute-done.36.refs_2_
  163.9 1.2 collective-permute-done.35.refs_1_
  165.1 1.6 adam_frag.1
  166.7 1.3 collective-permute-start.38
  168.0 2.4 %collective-permute-start.39 = (bf16[384,128]{1,0:T(8,128)(2,1)S(1)}, bf16[384,128]{1,0:T(8,128)(2,1)S(1)}, u32[]{:S(2)}, u32[]{:S(2)}) collective-permute-start(bf16[384,128]{1,0:T(8,128)(2,1)S(1)} %get-tuple-element.119), channel_id=1, source_target_pairs={{0,16},{8,24},{16,0},{24,8},{1,17},{9,25},{17,1},{25,9},{2,18},{10... | collective-permute-start | bytes 294920 | tf_op jit(solution)/shard_map/ppermute | solution.py:441
  170.3 0.8 collective-permute-start.40
  171.1 9.7 %adam_rows.2 = (f32[1536,1024]{1,0:T(8,128)}, f32[1536,1024]{1,0:T(8,128)}, f32[1536,1024]{1,0:T(8,128)}, f32[8,128]{1,0:T(8,128)S(1)}) custom-call(f32[3]{0:T(128)S(1)} %pad_maximum_fusion.sc_ref, f32[1536,1024]{1,0:T(8,128)} %bitcast.45, f32[1536,1024]{1,0:T(8,128)} %bitcast.48, f32[1536,1024]{1,0:T(8,128)} %bitcast.51, ...), custom_call_target="tpu_custom_call" | custom-call | flops 15728640 | bytes 22020096 | tf_op jit(solution)/shard_map/adam_rows/pallas_call | solution.py:287
  181.0 3.1 %collective-permute-start.43 = (bf16[384,128]{1,0:T(8,128)(2,1)S(1)}, bf16[384,128]{1,0:T(8,128)(2,1)S(1)}, u32[]{:S(2)}, u32[]{:S(2)}) collective-permute-start(bf16[384,128]{1,0:T(8,128)(2,1)S(1)} %convert_element_type.24.refs_7_), channel_id=1, source_target_pairs={{0,24},{8,16},{16,8},{24,0},{1,25},{9,17},{17,9},{25,1},{2,26},{10... | collective-permute-start | bytes 294920 | tf_op jit(solution)/shard_map/ppermute | solution.py:441
  184.1 1.3 collective-permute-start.41
  185.4 9.7 %adam_rows.3 = (f32[1536,1024]{1,0:T(8,128)}, f32[1536,1024]{1,0:T(8,128)}, f32[1536,1024]{1,0:T(8,128)}) custom-call(f32[3]{0:T(128)S(1)} %pad_maximum_fusion.sc_ref, f32[1536,1024]{1,0:T(8,128)} %bitcast.46, f32[1536,1024]{1,0:T(8,128)} %bitcast.49, f32[1536,1024]{1,0:T(8,128)} %bitcast.52, ...), custom_call_target="tpu_custom_call", output_to_operand_aliasing={{0}: (10, {}), {1}: (11, {}), {2}: (12, {})} | custom-call | flops 15728640 | bytes 22020096 | tf_op jit(solution)/shard_map/adam_rows/pallas_call | solution.py:287
  195.2 2.4 %outer_step.1 = (f32[1536,1024]{1,0:T(8,128)}, f32[384,1024]{1,0:T(8,128)}, f32[384,1024]{1,0:T(8,128)}) custom-call(s32[2]{0:T(128)S(1)} %pad_add_fusion.place_ref, f32[1536,1024]{1,0:T(8,128)} %get-tuple-element.115.refs_0_, f32[384,1024]{1,0:T(8,128)} %get-tuple-element.95.refs_1_, ...), custom_call_target="tpu_custom_call", output_to_operand_aliasing={{0}: (1, {}), {1}: (2, {}), {2}: (3, {})} | custom-call | flops 1966080 | bytes 3932160 | tf_op jit(solution)/shard_map/outer_step/pallas_call | solution.py:423
  (78 shorter events, 5.0 us)
Async XLA Ops:
  2.6 22.5 %collective-permute-start.1 = (bf16[256,1536]{1,0:T(8,128)(2,1)}, bf16[256,1536]{1,0:T(8,128)(2,1)S(1)}, u32[]{:S(2)}, u32[]{:S(2)}) collective-permute-start(bf16[256,1536]{1,0:T(8,128)(2,1)} %pack.5), channel_id=1, source_target_pairs={{0,6},{1,7},{2,4},{3,5},{4,2},{5,3},{6,0},{7,1},{8,14},{9,15},{10,... | collective-permute-start | bytes 2359304 | tf_op jit(solution)/shard_map/ppermute | solution.py:441
  9.2 33.4 %collective-permute-start = (bf16[256,1536]{1,0:T(8,128)(2,1)}, bf16[256,1536]{1,0:T(8,128)(2,1)S(1)}, u32[]{:S(2)}, u32[]{:S(2)}) collective-permute-start(bf16[256,1536]{1,0:T(8,128)(2,1)} %get-tuple-element.68), channel_id=1, source_target_pairs={{0,2},{1,3},{2,0},{3,1},{4,6},{5,7},{6,4},{7,5},{8,10},{9,11},{10,... | collective-permute-start | bytes 2359304 | tf_op jit(solution)/shard_map/ppermute | solution.py:441
  9.8 50.3 %copy-start.4 = (bf16[1,256,1024]{2,1,0:T(8,128)(2,1)S(1)}, bf16[1,256,1024]{2,1,0:T(8,128)(2,1)}, u32[]{:S(2)}) copy-start(bf16[1,256,1024]{2,1,0:T(8,128)(2,1)} %param.10) | copy-start | bytes 1572868
  9.8 47.6 %collective-permute-start.2 = (bf16[256,1536]{1,0:T(8,128)(2,1)}, bf16[256,1536]{1,0:T(8,128)(2,1)S(1)}, u32[]{:S(2)}, u32[]{:S(2)}) collective-permute-start(bf16[256,1536]{1,0:T(8,128)(2,1)} %get-tuple-element.71), channel_id=1, source_target_pairs={{0,7},{1,6},{2,5},{3,4},{4,3},{5,2},{6,1},{7,0},{8,15},{9,14},{10,... | collective-permute-start | bytes 2359304 | tf_op jit(solution)/shard_map/ppermute | solution.py:441
  27.5 43.4 %collective-permute-start.12 = (bf16[256,1536]{1,0:T(8,128)(2,1)}, bf16[256,1536]{1,0:T(8,128)(2,1)S(1)}, u32[]{:S(2)}, u32[]{:S(2)}) collective-permute-start(bf16[256,1536]{1,0:T(8,128)(2,1)} %get-tuple-element.89), channel_id=1, source_target_pairs={{0,1},{1,0},{2,3},{3,2},{4,5},{5,4},{6,7},{7,6},{8,9},{9,8},{10,11... | collective-permute-start | bytes 2359304 | tf_op jit(solution)/shard_map/ppermute | solution.py:441
  42.6 32.4 %collective-permute-start.6 = (bf16[256,1536]{1,0:T(8,128)(2,1)}, bf16[256,1536]{1,0:T(8,128)(2,1)S(1)}, u32[]{:S(2)}, u32[]{:S(2)}) collective-permute-start(bf16[256,1536]{1,0:T(8,128)(2,1)} %get-tuple-element.79), channel_id=1, source_target_pairs={{0,5},{1,4},{2,7},{3,6},{4,1},{5,0},{6,3},{7,2},{8,13},{9,12},{10,... | collective-permute-start | bytes 2359304 | tf_op jit(solution)/shard_map/ppermute | solution.py:441
  57.4 0.9 copy-start.1
  58.3 20.5 %collective-permute-start.3 = (bf16[256,1536]{1,0:T(8,128)(2,1)}, bf16[256,1536]{1,0:T(8,128)(2,1)}, u32[]{:S(2)}, u32[]{:S(2)}) collective-permute-start(bf16[256,1536]{1,0:T(8,128)(2,1)} %get-tuple-element.72), channel_id=1, source_target_pairs={{0,3},{1,2},{2,1},{3,0},{4,7},{5,6},{6,5},{7,4},{8,11},{9,10},{10,... | collective-permute-start | bytes 2359304 | tf_op jit(solution)/shard_map/ppermute | solution.py:441
  60.1 10.3 %collective-permute-start.20 = (bf16[256,512]{1,0:T(8,128)(2,1)S(1)}, bf16[256,512]{1,0:T(8,128)(2,1)}, u32[]{:S(2)}, u32[]{:S(2)}) collective-permute-start(bf16[256,512]{1,0:T(8,128)(2,1)S(1)} %slice.24.refs_4_), channel_id=1, source_target_pairs={{0,1},{1,0},{2,3},{3,2},{4,5},{5,4},{6,7},{7,6},{8,9},{9,8},{10,11... | collective-permute-start | bytes 786440 | tf_op jit(solution)/shard_map/ppermute | solution.py:441
  60.9 36.4 %collective-permute-start.5 = (bf16[256,1536]{1,0:T(8,128)(2,1)}, bf16[256,1536]{1,0:T(8,128)(2,1)S(1)}, u32[]{:S(2)}, u32[]{:S(2)}) collective-permute-start(bf16[256,1536]{1,0:T(8,128)(2,1)} %get-tuple-element.77), channel_id=1, source_target_pairs={{0,4},{1,5},{2,6},{3,7},{4,0},{5,1},{6,2},{7,3},{8,12},{9,13},{10,... | collective-permute-start | bytes 2359304 | tf_op jit(solution)/shard_map/ppermute | solution.py:441
  62.5 7.4 %copy-start.2 = (bf16[256,1536]{1,0:T(8,128)(2,1)S(1)}, bf16[256,1536]{1,0:T(8,128)(2,1)}, u32[]{:S(2)}) copy-start(bf16[256,1536]{1,0:T(8,128)(2,1)} %copy-done.1) | copy-start | bytes 2359300
  66.3 4.4 %copy-start.3 = (f32[4,384,128]{2,1,0:T(8,128)S(1)}, f32[4,384,128]{2,1,0:T(8,128)}, u32[]{:S(2)}) copy-start(f32[4,384,128]{2,1,0:T(8,128)} %due_columns.4.w_ref) | copy-start | bytes 2359300
  70.5 25.2 %collective-permute-start.8 = (bf16[256,512]{1,0:T(8,128)(2,1)S(1)}, bf16[256,512]{1,0:T(8,128)(2,1)S(1)}, u32[]{:S(2)}, u32[]{:S(2)}) collective-permute-start(bf16[256,512]{1,0:T(8,128)(2,1)S(1)} %get-tuple-element.83), channel_id=1, source_target_pairs={{0,1},{1,0},{2,3},{3,2},{4,5},{5,4},{6,7},{7,6},{8,9},{9,8},{10,11... | collective-permute-start | bytes 786440 | tf_op jit(solution)/shard_map/ppermute | solution.py:441
  70.8 14.8 %collective-permute-start.14 = (f32[384,128]{1,0:T(8,128)S(1)}, f32[384,128]{1,0:T(8,128)S(1)}, u32[]{:S(2)}, u32[]{:S(2)}) collective-permute-start(f32[384,128]{1,0:T(8,128)S(1)} %get-tuple-element.132), channel_id=1, source_target_pairs={{0,8},{8,0},{16,24},{24,16},{1,9},{9,1},{17,25},{25,17},{2,10},{10... | collective-permute-start | bytes 589832 | tf_op jit(solution)/shard_map/ppermute | solution.py:441
  75.0 11.2 %collective-permute-start.16 = (f32[384,128]{1,0:T(8,128)S(1)}, f32[384,128]{1,0:T(8,128)S(1)}, u32[]{:S(2)}, u32[]{:S(2)}) collective-permute-start(f32[384,128]{1,0:T(8,128)S(1)} %get-tuple-element.133), channel_id=1, source_target_pairs={{0,24},{8,16},{16,8},{24,0},{1,25},{9,17},{17,9},{25,1},{2,26},{10... | collective-permute-start | bytes 589832 | tf_op jit(solution)/shard_map/ppermute | solution.py:441
  78.8 16.9 %collective-permute-start.15 = (f32[384,128]{1,0:T(8,128)S(1)}, f32[384,128]{1,0:T(8,128)S(1)}, u32[]{:S(2)}, u32[]{:S(2)}) collective-permute-start(f32[384,128]{1,0:T(8,128)S(1)} %get-tuple-element.134), channel_id=1, source_target_pairs={{0,16},{8,24},{16,0},{24,8},{1,17},{9,25},{17,1},{25,9},{2,18},{10... | collective-permute-start | bytes 589832 | tf_op jit(solution)/shard_map/ppermute | solution.py:441
  82.6 13.5 %copy-start.8 = (f32[1,384,128]{2,1,0:T(8,128)S(1)}, f32[1,384,128]{2,1,0:T(8,128)}, u32[]{:S(2)}) copy-start(f32[1,384,128]{2,1,0:T(8,128)} %get-tuple-element.93) | copy-start | bytes 589828
  82.6 13.5 %copy-start.9 = (f32[1,384,128]{2,1,0:T(8,128)S(1)}, f32[1,384,128]{2,1,0:T(8,128)}, u32[]{:S(2)}) copy-start(f32[1,384,128]{2,1,0:T(8,128)} %get-tuple-element.94) | copy-start | bytes 589828
  85.6 32.4 %collective-permute-start.13 = (bf16[256,512]{1,0:T(8,128)(2,1)S(1)}, bf16[256,512]{1,0:T(8,128)(2,1)S(1)}, u32[]{:S(2)}, u32[]{:S(2)}) collective-permute-start(bf16[256,512]{1,0:T(8,128)(2,1)S(1)} %get-tuple-element.90), channel_id=1, source_target_pairs={{0,1},{1,0},{2,3},{3,2},{4,5},{5,4},{6,7},{7,6},{8,9},{9,8},{10,11... | collective-permute-start | bytes 786440 | tf_op jit(solution)/shard_map/ppermute | solution.py:441
  86.2 14.8 %collective-permute-start.21 = (bf16[256,512]{1,0:T(8,128)(2,1)S(1)}, bf16[256,512]{1,0:T(8,128)(2,1)S(1)}, u32[]{:S(2)}, u32[]{:S(2)}) collective-permute-start(bf16[256,512]{1,0:T(8,128)(2,1)S(1)} %slice.24.refs_4_), channel_id=1, source_target_pairs={{0,6},{1,7},{2,4},{3,5},{4,2},{5,3},{6,0},{7,1},{8,14},{9,15},{10,... | collective-permute-start | bytes 786440 | tf_op jit(solution)/shard_map/ppermute | solution.py:441
  95.7 5.8 %collective-permute-start.4 = (bf16[256,512]{1,0:T(8,128)(2,1)S(1)}, bf16[256,512]{1,0:T(8,128)(2,1)S(1)}, u32[]{:S(2)}, u32[]{:S(2)}) collective-permute-start(bf16[256,512]{1,0:T(8,128)(2,1)S(1)} %get-tuple-element.73), channel_id=1, source_target_pairs={{0,1},{1,0},{2,3},{3,2},{4,5},{5,4},{6,7},{7,6},{8,9},{9,8},{10,11... | collective-permute-start | bytes 786440 | tf_op jit(solution)/shard_map/ppermute | solution.py:441
  95.7 9.7 %collective-permute-start.7 = (bf16[256,512]{1,0:T(8,128)(2,1)S(1)}, bf16[256,512]{1,0:T(8,128)(2,1)S(1)}, u32[]{:S(2)}, u32[]{:S(2)}) collective-permute-start(bf16[256,512]{1,0:T(8,128)(2,1)S(1)} %get-tuple-element.80), channel_id=1, source_target_pairs={{0,1},{1,0},{2,3},{3,2},{4,5},{5,4},{6,7},{7,6},{8,9},{9,8},{10,11... | collective-permute-start | bytes 786440 | tf_op jit(solution)/shard_map/ppermute | solution.py:441
  97.3 9.9 %collective-permute-start.19 = (f32[384,128]{1,0:T(8,128)S(1)}, f32[384,128]{1,0:T(8,128)S(1)}, u32[]{:S(2)}, u32[]{:S(2)}) collective-permute-start(f32[384,128]{1,0:T(8,128)S(1)} %get-tuple-element.130.refs_3_), channel_id=1, source_target_pairs={{0,24},{8,16},{16,8},{24,0},{1,25},{9,17},{17,9},{25,1},{2,26},{10... | collective-permute-start | bytes 589832 | tf_op jit(solution)/shard_map/ppermute | solution.py:441
  101.1 13.9 %collective-permute-start.18 = (f32[384,128]{1,0:T(8,128)S(1)}, f32[384,128]{1,0:T(8,128)S(1)}, u32[]{:S(2)}, u32[]{:S(2)}) collective-permute-start(f32[384,128]{1,0:T(8,128)S(1)} %get-tuple-element.130.refs_3_), channel_id=1, source_target_pairs={{0,16},{8,24},{16,0},{24,8},{1,17},{9,25},{17,1},{25,9},{2,18},{10... | collective-permute-start | bytes 589832 | tf_op jit(solution)/shard_map/ppermute | solution.py:441
  101.4 15.1 %collective-permute-start.17 = (f32[384,128]{1,0:T(8,128)S(1)}, f32[384,128]{1,0:T(8,128)S(1)}, u32[]{:S(2)}, u32[]{:S(2)}) collective-permute-start(f32[384,128]{1,0:T(8,128)S(1)} %get-tuple-element.130.refs_3_), channel_id=1, source_target_pairs={{0,8},{8,0},{16,24},{24,16},{1,9},{9,1},{17,25},{25,17},{2,10},{10... | collective-permute-start | bytes 589832 | tf_op jit(solution)/shard_map/ppermute | solution.py:441
  105.3 17.9 %collective-permute-start.22 = (bf16[256,512]{1,0:T(8,128)(2,1)S(1)}, bf16[256,512]{1,0:T(8,128)(2,1)S(1)}, u32[]{:S(2)}, u32[]{:S(2)}) collective-permute-start(bf16[256,512]{1,0:T(8,128)(2,1)S(1)} %collective-permute-done.21.refs_6_), channel_id=1, source_target_pairs={{0,1},{1,0},{2,3},{3,2},{4,5},{5,4},{6,7},{7,6},{8,9},{9,8},{10,11... | collective-permute-start | bytes 786440 | tf_op jit(solution)/shard_map/ppermute | solution.py:441
  107.2 20.9 %collective-permute-start.9 = (bf16[256,512]{1,0:T(8,128)(2,1)S(1)}, bf16[256,512]{1,0:T(8,128)(2,1)S(1)}, u32[]{:S(2)}, u32[]{:S(2)}) collective-permute-start(bf16[256,512]{1,0:T(8,128)(2,1)S(1)} %get-tuple-element.84), channel_id=1, source_target_pairs={{0,6},{1,7},{2,4},{3,5},{4,2},{5,3},{6,0},{7,1},{8,14},{9,15},{10,... | collective-permute-start | bytes 786440 | tf_op jit(solution)/shard_map/ppermute | solution.py:441
  114.9 13.1 %collective-permute-start.32 = (bf16[256,512]{1,0:T(8,128)(2,1)S(1)}, bf16[256,512]{1,0:T(8,128)(2,1)S(1)}, u32[]{:S(2)}, u32[]{:S(2)}) collective-permute-start(bf16[256,512]{1,0:T(8,128)(2,1)S(1)} %slice.24.refs_4_), channel_id=1, source_target_pairs={{0,4},{1,5},{2,6},{3,7},{4,0},{5,1},{6,2},{7,3},{8,12},{9,13},{10,... | collective-permute-start | bytes 786440 | tf_op jit(solution)/shard_map/ppermute | solution.py:441
  116.5 11.6 %collective-permute-start.10 = (bf16[256,512]{1,0:T(8,128)(2,1)S(1)}, bf16[256,512]{1,0:T(8,128)(2,1)S(1)}, u32[]{:S(2)}, u32[]{:S(2)}) collective-permute-start(bf16[256,512]{1,0:T(8,128)(2,1)S(1)} %get-tuple-element.85), channel_id=1, source_target_pairs={{0,2},{1,3},{2,0},{3,1},{4,6},{5,7},{6,4},{7,5},{8,10},{9,11},{10,... | collective-permute-start | bytes 786440 | tf_op jit(solution)/shard_map/ppermute | solution.py:441
  118.0 10.7 %collective-permute-start.11 = (bf16[256,512]{1,0:T(8,128)(2,1)S(1)}, bf16[256,512]{1,0:T(8,128)(2,1)S(1)}, u32[]{:S(2)}, u32[]{:S(2)}) collective-permute-start(bf16[256,512]{1,0:T(8,128)(2,1)S(1)} %get-tuple-element.86), channel_id=1, source_target_pairs={{0,4},{1,5},{2,6},{3,7},{4,0},{5,1},{6,2},{7,3},{8,12},{9,13},{10,... | collective-permute-start | bytes 786440 | tf_op jit(solution)/shard_map/ppermute | solution.py:441
  118.5 4.2 %copy-start = (bf16[256,1536]{1,0:T(8,128)(2,1)S(1)}, bf16[256,1536]{1,0:T(8,128)(2,1)}, u32[]{:S(2)}) copy-start(bf16[256,1536]{1,0:T(8,128)(2,1)} %get-tuple-element.88.refs_0_.refs_1_.refs_2_.refs_3_) | copy-start | bytes 2359300
  122.7 6.1 %copy-start.5 = (bf16[1,256,1024]{2,1,0:T(8,128)(2,1)S(1)}, bf16[1,256,1024]{2,1,0:T(8,128)(2,1)}, u32[]{:S(2)}) copy-start(bf16[1,256,1024]{2,1,0:T(8,128)(2,1)} %param.10) | copy-start | bytes 1572868
  123.3 9.6 %collective-permute-start.30 = (bf16[256,512]{1,0:T(8,128)(2,1)S(1)}, bf16[256,512]{1,0:T(8,128)(2,1)S(1)}, u32[]{:S(2)}, u32[]{:S(2)}) collective-permute-start(bf16[256,512]{1,0:T(8,128)(2,1)S(1)} %slice.24.refs_4_), channel_id=1, source_target_pairs={{0,2},{1,3},{2,0},{3,1},{4,6},{5,7},{6,4},{7,5},{8,10},{9,11},{10,... | collective-permute-start | bytes 786440 | tf_op jit(solution)/shard_map/ppermute | solution.py:441
  128.0 4.8 %collective-permute-start.33 = (bf16[256,512]{1,0:T(8,128)(2,1)S(1)}, bf16[256,512]{1,0:T(8,128)(2,1)S(1)}, u32[]{:S(2)}, u32[]{:S(2)}) collective-permute-start(bf16[256,512]{1,0:T(8,128)(2,1)S(1)} %collective-permute-done.32.refs_6_), channel_id=1, source_target_pairs={{0,1},{1,0},{2,3},{3,2},{4,5},{5,4},{6,7},{7,6},{8,9},{9,8},{10,11... | collective-permute-start | bytes 786440 | tf_op jit(solution)/shard_map/ppermute | solution.py:441
  129.3 10.2 %collective-permute-start.28 = (bf16[256,512]{1,0:T(8,128)(2,1)S(1)}, bf16[256,512]{1,0:T(8,128)(2,1)S(1)}, u32[]{:S(2)}, u32[]{:S(2)}) collective-permute-start(bf16[256,512]{1,0:T(8,128)(2,1)S(1)} %key_backward.1.refs_4_), channel_id=1, source_target_pairs={{0,6},{1,7},{2,4},{3,5},{4,2},{5,3},{6,0},{7,1},{8,14},{9,15},{10,... | collective-permute-start | bytes 786440 | tf_op jit(solution)/shard_map/ppermute | solution.py:441
  131.9 12.1 %collective-permute-start.25 = (bf16[256,512]{1,0:T(8,128)(2,1)S(1)}, bf16[256,512]{1,0:T(8,128)(2,1)S(1)}, u32[]{:S(2)}, u32[]{:S(2)}) collective-permute-start(bf16[256,512]{1,0:T(8,128)(2,1)S(1)} %key_backward.1.refs_4_), channel_id=1, source_target_pairs={{0,4},{1,5},{2,6},{3,7},{4,0},{5,1},{6,2},{7,3},{8,12},{9,13},{10,... | collective-permute-start | bytes 786440 | tf_op jit(solution)/shard_map/ppermute | solution.py:441
  132.3 11.8 %collective-permute-start.23 = (bf16[256,512]{1,0:T(8,128)(2,1)S(1)}, bf16[256,512]{1,0:T(8,128)(2,1)S(1)}, u32[]{:S(2)}, u32[]{:S(2)}) collective-permute-start(bf16[256,512]{1,0:T(8,128)(2,1)S(1)} %key_backward.1.refs_4_), channel_id=1, source_target_pairs={{0,2},{1,3},{2,0},{3,1},{4,6},{5,7},{6,4},{7,5},{8,10},{9,11},{10,... | collective-permute-start | bytes 786440 | tf_op jit(solution)/shard_map/ppermute | solution.py:441
  132.9 11.6 %collective-permute-start.31 = (bf16[256,512]{1,0:T(8,128)(2,1)S(1)}, bf16[256,512]{1,0:T(8,128)(2,1)S(1)}, u32[]{:S(2)}, u32[]{:S(2)}) collective-permute-start(bf16[256,512]{1,0:T(8,128)(2,1)S(1)} %collective-permute-done.30.refs_4_), channel_id=1, source_target_pairs={{0,1},{1,0},{2,3},{3,2},{4,5},{5,4},{6,7},{7,6},{8,9},{9,8},{10,11... | collective-permute-start | bytes 786440 | tf_op jit(solution)/shard_map/ppermute | solution.py:441
  132.9 16.4 %collective-permute-start.27 = (bf16[256,512]{1,0:T(8,128)(2,1)S(1)}, bf16[256,512]{1,0:T(8,128)(2,1)S(1)}, u32[]{:S(2)}, u32[]{:S(2)}) collective-permute-start(bf16[256,512]{1,0:T(8,128)(2,1)S(1)} %key_backward.1.refs_4_), channel_id=1, source_target_pairs={{0,1},{1,0},{2,3},{3,2},{4,5},{5,4},{6,7},{7,6},{8,9},{9,8},{10,11... | collective-permute-start | bytes 786440 | tf_op jit(solution)/shard_map/ppermute | solution.py:441
  139.5 9.8 %collective-permute-start.29 = (bf16[256,512]{1,0:T(8,128)(2,1)S(1)}, bf16[256,512]{1,0:T(8,128)(2,1)S(1)}, u32[]{:S(2)}, u32[]{:S(2)}) collective-permute-start(bf16[256,512]{1,0:T(8,128)(2,1)S(1)} %collective-permute-done.28.refs_6_), channel_id=1, source_target_pairs={{0,1},{1,0},{2,3},{3,2},{4,5},{5,4},{6,7},{7,6},{8,9},{9,8},{10,11... | collective-permute-start | bytes 786440 | tf_op jit(solution)/shard_map/ppermute | solution.py:441
  144.0 8.5 %collective-permute-start.26 = (bf16[256,512]{1,0:T(8,128)(2,1)S(1)}, bf16[256,512]{1,0:T(8,128)(2,1)S(1)}, u32[]{:S(2)}, u32[]{:S(2)}) collective-permute-start(bf16[256,512]{1,0:T(8,128)(2,1)S(1)} %collective-permute-done.25.refs_6_), channel_id=1, source_target_pairs={{0,1},{1,0},{2,3},{3,2},{4,5},{5,4},{6,7},{7,6},{8,9},{9,8},{10,11... | collective-permute-start | bytes 786440 | tf_op jit(solution)/shard_map/ppermute | solution.py:441
  144.2 8.3 %collective-permute-start.24 = (bf16[256,512]{1,0:T(8,128)(2,1)S(1)}, bf16[256,512]{1,0:T(8,128)(2,1)S(1)}, u32[]{:S(2)}, u32[]{:S(2)}) collective-permute-start(bf16[256,512]{1,0:T(8,128)(2,1)S(1)} %collective-permute-done.23.refs_4_), channel_id=1, source_target_pairs={{0,1},{1,0},{2,3},{3,2},{4,5},{5,4},{6,7},{7,6},{8,9},{9,8},{10,11... | collective-permute-start | bytes 786440 | tf_op jit(solution)/shard_map/ppermute | solution.py:441
  149.3 15.8 %copy-start.6 = (f32[4,384,128]{2,1,0:T(8,128)S(1)}, f32[4,384,128]{2,1,0:T(8,128)}, u32[]{:S(2)}) copy-start(f32[4,384,128]{2,1,0:T(8,128)} %get-tuple-element.97.m_ref) | copy-start | bytes 2359300
  149.3 15.8 %copy-start.7 = (f32[4,384,128]{2,1,0:T(8,128)S(1)}, f32[4,384,128]{2,1,0:T(8,128)}, u32[]{:S(2)}) copy-start(f32[4,384,128]{2,1,0:T(8,128)} %get-tuple-element.98.v_ref) | copy-start | bytes 2359300
  157.4 1.2 collective-permute-start.34
  158.5 4.5 %collective-permute-start.37 = (f32[8,128]{1,0:T(8,128)S(1)}, f32[8,128]{1,0:T(8,128)S(1)}, u32[]{:S(2)}, u32[]{:S(2)}) collective-permute-start(f32[8,128]{1,0:T(8,128)S(1)} %add.32.refs_0_), channel_id=1, source_target_pairs={{0,6},{1,7},{2,4},{3,5},{4,2},{5,3},{6,0},{7,1},{8,14},{9,15},{10,... | collective-permute-start | bytes 12296 | tf_op jit(solution)/shard_map/ppermute | solution.py:441
  160.3 3.6 %collective-permute-start.36 = (f32[8,128]{1,0:T(8,128)S(1)}, f32[8,128]{1,0:T(8,128)S(1)}, u32[]{:S(2)}, u32[]{:S(2)}) collective-permute-start(f32[8,128]{1,0:T(8,128)S(1)} %add.32.refs_0_), channel_id=1, source_target_pairs={{0,4},{1,5},{2,6},{3,7},{4,0},{5,1},{6,2},{7,3},{8,12},{9,13},{10,... | collective-permute-start | bytes 12296 | tf_op jit(solution)/shard_map/ppermute | solution.py:441
  161.5 3.6 %collective-permute-start.35 = (f32[8,128]{1,0:T(8,128)S(1)}, f32[8,128]{1,0:T(8,128)S(1)}, u32[]{:S(2)}, u32[]{:S(2)}) collective-permute-start(f32[8,128]{1,0:T(8,128)S(1)} %add.32.refs_0_), channel_id=1, source_target_pairs={{0,2},{1,3},{2,0},{3,1},{4,6},{5,7},{6,4},{7,5},{8,10},{9,11},{10,... | collective-permute-start | bytes 12296 | tf_op jit(solution)/shard_map/ppermute | solution.py:441
  166.7 14.2 %collective-permute-start.38 = (bf16[384,128]{1,0:T(8,128)(2,1)S(1)}, bf16[384,128]{1,0:T(8,128)(2,1)S(1)}, u32[]{:S(2)}, u32[]{:S(2)}) collective-permute-start(bf16[384,128]{1,0:T(8,128)(2,1)S(1)} %get-tuple-element.118), channel_id=1, source_target_pairs={{0,8},{8,0},{16,24},{24,16},{1,9},{9,1},{17,25},{25,17},{2,10},{10... | collective-permute-start | bytes 294920 | tf_op jit(solution)/shard_map/ppermute | solution.py:441
  168.0 12.9 %collective-permute-start.39 = (bf16[384,128]{1,0:T(8,128)(2,1)S(1)}, bf16[384,128]{1,0:T(8,128)(2,1)S(1)}, u32[]{:S(2)}, u32[]{:S(2)}) collective-permute-start(bf16[384,128]{1,0:T(8,128)(2,1)S(1)} %get-tuple-element.119), channel_id=1, source_target_pairs={{0,16},{8,24},{16,0},{24,8},{1,17},{9,25},{17,1},{25,9},{2,18},{10... | collective-permute-start | bytes 294920 | tf_op jit(solution)/shard_map/ppermute | solution.py:441
  170.3 10.5 %collective-permute-start.40 = (bf16[384,128]{1,0:T(8,128)(2,1)S(1)}, bf16[384,128]{1,0:T(8,128)(2,1)S(1)}, u32[]{:S(2)}, u32[]{:S(2)}) collective-permute-start(bf16[384,128]{1,0:T(8,128)(2,1)S(1)} %get-tuple-element.120), channel_id=1, source_target_pairs={{0,24},{8,16},{16,8},{24,0},{1,25},{9,17},{17,9},{25,1},{2,26},{10... | collective-permute-start | bytes 294920 | tf_op jit(solution)/shard_map/ppermute | solution.py:441
  181.0 14.2 %collective-permute-start.43 = (bf16[384,128]{1,0:T(8,128)(2,1)S(1)}, bf16[384,128]{1,0:T(8,128)(2,1)S(1)}, u32[]{:S(2)}, u32[]{:S(2)}) collective-permute-start(bf16[384,128]{1,0:T(8,128)(2,1)S(1)} %convert_element_type.24.refs_7_), channel_id=1, source_target_pairs={{0,24},{8,16},{16,8},{24,0},{1,25},{9,17},{17,9},{25,1},{2,26},{10... | collective-permute-start | bytes 294920 | tf_op jit(solution)/shard_map/ppermute | solution.py:441
  184.1 11.1 %collective-permute-start.42 = (bf16[384,128]{1,0:T(8,128)(2,1)S(1)}, bf16[384,128]{1,0:T(8,128)(2,1)S(1)}, u32[]{:S(2)}, u32[]{:S(2)}) collective-permute-start(bf16[384,128]{1,0:T(8,128)(2,1)S(1)} %convert_element_type.24.refs_7_), channel_id=1, source_target_pairs={{0,16},{8,24},{16,0},{24,8},{1,17},{9,25},{17,1},{25,9},{2,18},{10... | collective-permute-start | bytes 294920 | tf_op jit(solution)/shard_map/ppermute | solution.py:441
  184.1 11.1 %collective-permute-start.41 = (bf16[384,128]{1,0:T(8,128)(2,1)S(1)}, bf16[384,128]{1,0:T(8,128)(2,1)S(1)}, u32[]{:S(2)}, u32[]{:S(2)}) collective-permute-start(bf16[384,128]{1,0:T(8,128)(2,1)S(1)} %convert_element_type.24.refs_7_), channel_id=1, source_target_pairs={{0,8},{8,0},{16,24},{24,16},{1,9},{9,1},{17,25},{25,17},{2,10},{10... | collective-permute-start | bytes 294920 | tf_op jit(solution)/shard_map/ppermute | solution.py:441

commit v10 on v9

--- a/solution.py
+++ b/solution.py
@@ -327,28 +327,33 @@
     )(place, scalars, old, first, second, grad, *squares)
 
 
-def pick_kernel(place_ref, *refs):
-    half = len(refs) // 2
-    for src_ref, out_ref in zip(refs[:half], refs[half:]):
-        out_ref[...] = src_ref[...].reshape(out_ref.shape)
+def pick_kernel(blocks, place_ref, *refs):
+    outs = refs[len(refs) // (blocks + 1) * blocks:]
+    for i, out_ref in enumerate(outs):
+        for j in range(blocks):
+            out_ref[j] = refs[i * blocks + j][...]
 
 
 def due_columns(place, part, *arrays):
     blocks = arrays[0].shape[0] // part
-    at = (lambda j, p: (p[1] ^ j, p[0])) if blocks > 1 else (lambda j, p: (0, p[0]))
-    return pl.pallas_call(
-        pick_kernel,
-        out_shape=[pltpu.HBM((blocks, part, FRAG_COLS), a.dtype) for a in arrays],
+    specs = []
+    for j in range(blocks):
+        at = (lambda i, p, j=j: (p[1] ^ j, p[0])) if blocks > 1 else (lambda i, p: (0, p[0]))
+        specs.append(pl.BlockSpec((part, FRAG_COLS), at))
+    shape = (blocks, part, FRAG_COLS)
+    return pl.pallas_call(
+        functools.partial(pick_kernel, blocks),
+        out_shape=[jax.ShapeDtypeStruct(shape, a.dtype) for a in arrays],
         grid_spec=pltpu.PrefetchScalarGridSpec(
             num_scalar_prefetch=1,
-            grid=(blocks,),
-            in_specs=[pl.BlockSpec((part, FRAG_COLS), at)] * len(arrays),
-            out_specs=[pl.BlockSpec((1, part, FRAG_COLS), lambda j, p: (j, 0, 0))] * len(arrays),
+            grid=(1,),
+            in_specs=specs * len(arrays),
+            out_specs=[pl.BlockSpec(shape, lambda i, p: (0, 0, 0))] * len(arrays),
         ),
-        compiler_params=params_of(8),
+        compiler_params=params_of(12),
         cost_estimate=cost(0, 8 * blocks * part * FRAG_COLS * len(arrays)),
         name="due_columns",
-    )(place, *in_hbm(*arrays))
+    )(place, *[a for array in in_hbm(*arrays) for a in [array] * blocks])
 
 
 def duplicate_kernel(*refs):
@@ -443,17 +448,6 @@
 
 def after(value, *others):
     return lax.optimization_barrier((value,) + others)[0]
-
-
-class Line:
-    def __init__(self, axis, window):
-        self.axis, self.window, self.ended = axis, window, []
-
-    def swap(self, block, offset):
-        if len(self.ended) >= self.window:
-            block = after(block, self.ended[-self.window])
-        self.ended.append(swap(block, self.axis, offset))
-        return self.ended[-1]
 
 
 def body(
@@ -481,18 +475,18 @@
     order = [k for k in far[:-2] for k in (k, k + 1)]
     order += far[-2:] + [k + 1 for k in far[-2:]]
 
-    line = Line("fsdp", 3)
+    (old,) = due_columns(place, part, params)
+    old_sums = [old[0]] + [swap(old[k], "rep", k) for k in range(1, replicas)]
+
     packed = {}
-    for offsets in (order[:1], order[1:4], order[4:]):
+    for offsets in (order[:1], order[1:4], order[4:], (0, 1)):
         packed |= pack(inputs, me, rows, tuple(offsets))
-    blocks = {k: line.swap(packed[k], k) for k in order}
-    early = blocks[order[0]]
-    packed |= pack(inputs, after(me, early), rows, (0, 1))
+    blocks = {k: swap(packed[k], "fsdp", k) for k in order}
     blocks[0], blocks[1] = packed[0], swap(packed[1], "fsdp", 1)
 
     values = {0: incoming[:, kv_width:]}
-    for k in reversed(far):
-        values[k] = line.swap(values[0], k)
+    for i, k in enumerate(far):
+        values[k] = swap(after(values[0], blocks[order[i]]), "fsdp", k)
     for k in range(0, shards, 2):
         values[k + 1] = swap(values[k], "fsdp", 1)
 
@@ -504,36 +498,38 @@
     inv_one = 1.0 / (1.0 - jnp.power(BETA_ONE, steps_now))
     inv_two = 1.0 / (1.0 - jnp.power(BETA_TWO, steps_now))
     scalars = jnp.stack([rate, inv_one, inv_two])
-    place_early = after(place, early)
-    (old,) = due_columns(place_early, part, params)
-    old_first, old_second = due_columns(place_early, part, first_moment[0], second_moment[0])
-    anchor_cols, moment_cols = (c[0] for c in due_columns(place_early, part, anchor, momentum))
-    old_sum = sum([swap(old[k], "rep", k) for k in range(1, replicas)], old[0])
-    pseudo_old = anchor_cols - old_sum / replicas
+    old_first, old_second = due_columns(place, part, first_moment[0], second_moment[0])
+    anchor_cols, moment_cols = (c[0] for c in due_columns(place, part, anchor, momentum))
+    pseudo_old = anchor_cols - sum(old_sums[1:], old_sums[0]) / replicas
     base = anchor_cols - OUTER_RATE * (OUTER_MU * (OUTER_MU * moment_cols + pseudo_old) + pseudo_old)
     base = [base] + [swap(base, "rep", k) for k in range(1, replicas)]
     anchor_copy, momentum_copy = duplicate(anchor, momentum)
-    key_weights = cast_left(after(params, early), kv_width)
-
+    key_weights = cast_left(params, kv_width)
+
+    last = far[-1]
+    blocks[last + 1] = after(blocks[last + 1], *base, anchor_copy, momentum_copy, scalars)
     parts, flipped = [], {}
     for k in far + [0]:
         theirs, flipped[k + 1] = partial_keys(blocks[k + 1], key_weights)
-        part_k, flipped[k] = partial_keys(blocks[k], key_weights, swap(theirs, "fsdp", 1))
+        theirs = swap(theirs, "fsdp", 1)
+        if k == last:
+            theirs = after(theirs, *parts[:1])
+        part_k, flipped[k] = partial_keys(blocks[k], key_weights, theirs)
         parts.append(swap(part_k, "fsdp", k) if k else part_k)
     spread = [0, 1] + [k + odd for k in far for odd in range(2)]
     near, rest = spread[:shards // 2], spread[shards // 2:]
     pick = lambda table, which: [table[k] for k in which]
     (values_first,) = gradient(place, pick(flipped, near), pick(values, near), last=False)
-    parts[-1] = after(
-        parts[-1], *base, anchor_copy, momentum_copy, old_first, old_second, scalars, values_first
-    )
+    parts[-1] = after(parts[-1], values_first)
     keys = {0: key_backward(parts, incoming, 0)}
     for k in far:
         keys[k] = swap(keys[0], "fsdp", k)
     for k in range(0, shards, 2):
         keys[k + 1] = swap(keys[k], "fsdp", 1)
 
-    grad_values, square, due = gradient(place, pick(flipped, rest), pick(values, rest), values_first)
+    grad_values, square, due = gradient(
+        after(place, old_first, old_second), pick(flipped, rest), pick(values, rest), values_first
+    )
     (keys_first,) = gradient(place, pick(flipped, near), pick(keys, near), last=False)
     grad_keys, square, due = gradient(
         place, pick(flipped, rest), pick(keys, rest), keys_first, square, due

time: 199 us -> 174 us (0.87)
  waiting for transfers between devices: 73.8 us -> 57.5 us
  Pallas kernels: 72.5 us -> 65.7 us
    ppermute x44, waiting for transfers between devices: 73.8 us -> 57.5 us  [swap(): return lax.ppermute(block, axis, [(i, i ^ offset) for i in range(count)])]
    pallas_call x3, Pallas kernels: 10.3 us -> 5.54 us  [due_columns(): pl.pallas_call(functools.partial(pick_kernel, blocks), out_shape=[jax.Sha...]
  transfers between devices with their start and end apart: 44 -> 44, of which waited for: 15 -> 18; matrix products, arithmetic and copies ran while one was open for 0% -> 0% of each run, Pallas kernels for 31% -> 32%
where the time goes in v10:
time: 174 us
  Pallas kernels  65.7 us (38%)
  waiting for transfers between devices  57.5 us (33%)
  starting transfers between devices  46.5 us (27%)
  between operations  3.67 us (2%)
    ppermute x44, waiting for transfers between devices, swap(): return lax.ppermute(block, axis, [(i, i ^ offset) for i in range(count)])  57.5 us
    ppermute x44, starting transfers between devices, swap(): return lax.ppermute(block, axis, [(i, i ^ offset) for i in range(count)])  46.5 us
    pallas_call x2, Pallas kernels, adam_rows(): pl.pallas_call(functools.partial(adam_kernel, len(squares), len(into)), o...  19.5 us
    pallas_call x4, Pallas kernels, gradient(): pl.pallas_call(functools.partial(grad_kernel, len(flipped), base is not N...  16 us
    pallas_call x4, Pallas kernels, pack(): pl.pallas_call(functools.partial(pack_kernel, offsets), out_shape=[pltpu....  9.19 us
    pallas_call x3, Pallas kernels, due_columns(): pl.pallas_call(functools.partial(pick_kernel, blocks), out_shape=[jax.Sha...  5.54 us
    pallas_call x8, Pallas kernels, partial_keys(): pl.pallas_call(functools.partial(partial_kernel, pieces), out_shape=[jax....  4.83 us
  transfers between devices with their start and end apart: 44, of which 18 were waited for; matrix products, arithmetic and copies ran while one was open for 0% of the time, Pallas kernels for 32%

profile of v10, /device:TPU:0, one launch (start us, length us, event | category | flops | bytes accessed | tf_op | source)
XLA Modules:
  0.0 173.8 jit_solution(4645699969177421146)
XLA Ops:
  1.4 1.8 %due_columns.4.w_ref = f32[4,384,128]{2,1,0:T(8,128)S(1)} custom-call(s32[2]{0:T(128)S(1)} %pad_add_fusion.place_ref, f32[1536,1024]{1,0:T(8,128)} %bitcast.39, f32[1536,1024]{1,0:T(8,128)} %bitcast.40, f32[1536,1024]{1,0:T(8,128)} %bitcast.41, f32[1536,1024]{1,0:T(8,128)} %bitcast.42), custom_call_target="tpu_custom_call" | custom-call | bytes 1572864 | tf_op jit(solution)/shard_map/due_columns/pallas_call | solution.py:344
  3.2 3.1 %collective-permute-start.5 = (f32[384,128]{1,0:T(8,128)S(1)}, f32[384,128]{1,0:T(8,128)S(1)}, u32[]{:S(2)}, u32[]{:S(2)}) collective-permute-start(f32[384,128]{1,0:T(8,128)S(1)} %get-tuple-element.126), channel_id=1, source_target_pairs={{0,8},{8,0},{16,24},{24,16},{1,9},{9,1},{17,25},{25,17},{2,10},{10... | collective-permute-start | bytes 589832 | tf_op jit(solution)/shard_map/ppermute | solution.py:446
  6.3 2.5 %collective-permute-start.7 = (f32[384,128]{1,0:T(8,128)S(1)}, f32[384,128]{1,0:T(8,128)S(1)}, u32[]{:S(2)}, u32[]{:S(2)}) collective-permute-start(f32[384,128]{1,0:T(8,128)S(1)} %get-tuple-element.127), channel_id=1, source_target_pairs={{0,24},{8,16},{16,8},{24,0},{1,25},{9,17},{17,9},{25,1},{2,26},{10... | collective-permute-start | bytes 589832 | tf_op jit(solution)/shard_map/ppermute | solution.py:446
  8.9 2.0 %pack.6 = bf16[256,1536]{1,0:T(8,128)(2,1)} custom-call(s32[1]{0:T(128)} %bitcast.4.me_ref, bf16[256,12288]{1,0:T(8,128)(2,1)} %bitcast.58), custom_call_target="tpu_custom_call" | custom-call | bytes 1572864 | tf_op jit(solution)/shard_map/pack/pallas_call | solution.py:68
  10.9 2.5 %collective-permute-start.12 = (bf16[256,1536]{1,0:T(8,128)(2,1)}, bf16[256,1536]{1,0:T(8,128)(2,1)S(1)}, u32[]{:S(2)}, u32[]{:S(2)}) collective-permute-start(bf16[256,1536]{1,0:T(8,128)(2,1)} %pack.6), channel_id=1, source_target_pairs={{0,6},{1,7},{2,4},{3,5},{4,2},{5,3},{6,0},{7,1},{8,14},{9,15},{10,... | collective-permute-start | bytes 2359304 | tf_op jit(solution)/shard_map/ppermute | solution.py:446
  13.4 2.6 %pack.4 = (bf16[256,1536]{1,0:T(8,128)(2,1)}, bf16[256,1536]{1,0:T(8,128)(2,1)}, bf16[256,1536]{1,0:T(8,128)(2,1)}) custom-call(s32[1]{0:T(128)} %bitcast.4.me_ref, bf16[256,12288]{1,0:T(8,128)(2,1)} %bitcast.59), custom_call_target="tpu_custom_call" | custom-call | bytes 4718592 | tf_op jit(solution)/shard_map/pack/pallas_call | solution.py:68
  16.1 1.6 due_columns.3
  17.7 1.2 collective-permute-done.7
  18.9 7.3 %collective-permute-done.6 = f32[384,128]{1,0:T(8,128)S(1)} collective-permute-done((f32[384,128]{1,0:T(8,128)S(1)}, f32[384,128]{1,0:T(8,128)S(1)}, u32[]{:S(2)}, u32[]{:S(2)}) %collective-permute-start.6) | collective-permute-done | bytes 196640 | tf_op jit(solution)/shard_map/ppermute | solution.py:446
  26.3 3.1 %collective-permute-start.10 = (f32[384,128]{1,0:T(8,128)S(1)}, f32[384,128]{1,0:T(8,128)S(1)}, u32[]{:S(2)}, u32[]{:S(2)}) collective-permute-start(f32[384,128]{1,0:T(8,128)S(1)} %get-tuple-element.124.refs_3_), channel_id=1, source_target_pairs={{0,24},{8,16},{16,8},{24,0},{1,25},{9,17},{17,9},{25,1},{2,26},{10... | collective-permute-start | bytes 589832 | tf_op jit(solution)/shard_map/ppermute | solution.py:446
  29.4 2.3 %pack.5 = (bf16[256,1536]{1,0:T(8,128)(2,1)}, bf16[256,1536]{1,0:T(8,128)(2,1)}) custom-call(s32[1]{0:T(128)} %bitcast.4.me_ref, bf16[256,12288]{1,0:T(8,128)(2,1)} %bitcast.60), custom_call_target="tpu_custom_call" | custom-call | bytes 3145728 | tf_op jit(solution)/shard_map/pack/pallas_call | solution.py:68
  31.8 4.3 %collective-permute-done.10.refs_6_ = f32[384,128]{1,0:T(8,128)S(1)} collective-permute-done((f32[384,128]{1,0:T(8,128)S(1)}, f32[384,128]{1,0:T(8,128)S(1)}, u32[]{:S(2)}, u32[]{:S(2)}) %collective-permute-start.10) | collective-permute-done | bytes 196640 | tf_op jit(solution)/shard_map/ppermute | solution.py:446
  36.1 6.5 %collective-permute-start.8 = (f32[384,128]{1,0:T(8,128)S(1)}, f32[384,128]{1,0:T(8,128)S(1)}, u32[]{:S(2)}, u32[]{:S(2)}) collective-permute-start(f32[384,128]{1,0:T(8,128)S(1)} %get-tuple-element.124.refs_3_), channel_id=1, source_target_pairs={{0,8},{8,0},{16,24},{24,16},{1,9},{9,1},{17,25},{25,17},{2,10},{10... | collective-permute-start | bytes 589832 | tf_op jit(solution)/shard_map/ppermute | solution.py:446
  42.5 1.8 %collective-permute-done.9.refs_5_ = f32[384,128]{1,0:T(8,128)S(1)} collective-permute-done((f32[384,128]{1,0:T(8,128)S(1)}, f32[384,128]{1,0:T(8,128)S(1)}, u32[]{:S(2)}, u32[]{:S(2)}) %collective-permute-start.9) | collective-permute-done | bytes 196640 | tf_op jit(solution)/shard_map/ppermute | solution.py:446
  44.3 2.3 %pack.7 = (bf16[256,1536]{1,0:T(8,128)(2,1)}, bf16[256,1536]{1,0:T(8,128)(2,1)}) custom-call(s32[1]{0:T(128)} %bitcast.4.me_ref, bf16[256,12288]{1,0:T(8,128)(2,1)} %bitcast.61), custom_call_target="tpu_custom_call" | custom-call | bytes 3145728 | tf_op jit(solution)/shard_map/pack/pallas_call | solution.py:68
  46.7 1.7 collective-permute-start.18
  48.3 0.5 collective-permute-start
  48.9 1.6 collective-permute-start.3
  50.5 3.5 %cast_left.1.refs_4_ = bf16[1536,512]{1,0:T(8,128)(2,1)S(1)} custom-call(f32[1536,1024]{1,0:T(8,128)} %bitcast.43), custom_call_target="tpu_custom_call" | custom-call | bytes 4718592 | tf_op jit(solution)/shard_map/cast_left/pallas_call | solution.py:92
  53.9 0.6 partial_keys.11
  54.6 9.9 %collective-permute-done.4.refs_0_.refs_1_.refs_2_.refs_3_ = bf16[256,1536]{1,0:T(8,128)(2,1)S(1)} collective-permute-done((bf16[256,1536]{1,0:T(8,128)(2,1)}, bf16[256,1536]{1,0:T(8,128)(2,1)S(1)}, u32[]{:S(2)}, u32[]{:S(2)}) %collective-permute-start.4) | collective-permute-done | bytes 786464 | tf_op jit(solution)/shard_map/ppermute | solution.py:446
  64.6 2.8 %duplicate.1 = (f32[384,1024]{1,0:T(8,128)}, f32[384,1024]{1,0:T(8,128)}) custom-call(f32[384,1024]{1,0:T(8,128)} %refs_0_.3, f32[384,1024]{1,0:T(8,128)} %refs_1_.3), custom_call_target="tpu_custom_call" | custom-call | bytes 6291456 | tf_op jit(solution)/shard_map/duplicate/pallas_call | solution.py:385
  68.4 2.4 %collective-permute-start.21 = (bf16[256,512]{1,0:T(8,128)(2,1)S(1)}, bf16[256,512]{1,0:T(8,128)(2,1)S(1)}, u32[]{:S(2)}, u32[]{:S(2)}) collective-permute-start(bf16[256,512]{1,0:T(8,128)(2,1)S(1)} %slice.24.refs_4_), channel_id=1, source_target_pairs={{0,6},{1,7},{2,4},{3,5},{4,2},{5,3},{6,0},{7,1},{8,14},{9,15},{10,... | collective-permute-start | bytes 786440 | tf_op jit(solution)/shard_map/ppermute | solution.py:446
  70.8 0.6 partial_keys.10
  71.5 0.6 partial_keys.8
  72.4 0.6 partial_keys.12
  73.4 8.2 %collective-permute-done.refs_0_.refs_1_.refs_2_.refs_3_ = bf16[256,1536]{1,0:T(8,128)(2,1)S(1)} collective-permute-done((bf16[256,1536]{1,0:T(8,128)(2,1)S(1)}, bf16[256,1536]{1,0:T(8,128)(2,1)S(1)}, u32[]{:S(2)}, u32[]{:S(2)}) %collective-permute-start) | collective-permute-done | bytes 786464 | tf_op jit(solution)/shard_map/ppermute | solution.py:446
  82.0 0.6 partial_keys.14
  82.6 5.3 %collective-permute-done.21.refs_6_ = bf16[256,512]{1,0:T(8,128)(2,1)S(1)} collective-permute-done((bf16[256,512]{1,0:T(8,128)(2,1)S(1)}, bf16[256,512]{1,0:T(8,128)(2,1)S(1)}, u32[]{:S(2)}, u32[]{:S(2)}) %collective-permute-start.21) | collective-permute-done | bytes 262176 | tf_op jit(solution)/shard_map/ppermute | solution.py:446
  88.4 0.8 collective-permute-start.32
  89.2 4.4 %collective-permute-done.15.refs_0_ = bf16[256,512]{1,0:T(8,128)(2,1)S(1)} collective-permute-done((bf16[256,512]{1,0:T(8,128)(2,1)S(1)}, bf16[256,512]{1,0:T(8,128)(2,1)S(1)}, u32[]{:S(2)}, u32[]{:S(2)}) %collective-permute-start.15) | collective-permute-done | bytes 262176 | tf_op jit(solution)/shard_map/ppermute | solution.py:446
  93.5 0.6 partial_keys.9
  94.2 0.6 collective-permute-start.16
  94.7 0.6 partial_keys.13
  95.3 1.8 %collective-permute-start.17 = (bf16[256,512]{1,0:T(8,128)(2,1)S(1)}, bf16[256,512]{1,0:T(8,128)(2,1)S(1)}, u32[]{:S(2)}, u32[]{:S(2)}) collective-permute-start(bf16[256,512]{1,0:T(8,128)(2,1)S(1)} %get-tuple-element.85), channel_id=1, source_target_pairs={{0,4},{1,5},{2,6},{3,7},{4,0},{5,1},{6,2},{7,3},{8,12},{9,13},{10,... | collective-permute-start | bytes 786440 | tf_op jit(solution)/shard_map/ppermute | solution.py:446
  97.1 0.6 partial_keys.15
  97.7 0.6 collective-permute-start.30
  98.3 0.8 collective-permute-done.32.refs_6_
  99.1 3.2 %gradient.4.refs_8_ = f32[1536,512]{1,0:T(8,128)S(1)} custom-call(s32[2]{0:T(128)S(1)} %pad_add_fusion.place_ref, bf16[1536,256]{1,0:T(8,128)(2,1)S(1)} %get-tuple-element.90.refs_0_, bf16[1536,256]{1,0:T(8,128)(2,1)S(1)} %get-tuple-element.91.refs_1_, bf16[1536,256]{1,0:T(8,128)(2,1)S(1)} %get-tuple-element.92.refs_2_, ...), custom_call_target="tpu_custom_call" | custom-call | flops 1610612736 | bytes 6291456 | tf_op jit(solution)/shard_map/gradient/pallas_call | solution.py:232
  102.3 1.0 collective-permute-done.16.refs_1_
  103.3 1.3 collective-permute-done.17.refs_2_
  104.7 0.5 key_backward.1.refs_4_
  105.2 1.7 collective-permute-start.28
  107.4 1.3 collective-permute-start.23
  109.5 5.9 %collective-permute-done.28.refs_6_ = bf16[256,512]{1,0:T(8,128)(2,1)S(1)} collective-permute-done((bf16[256,512]{1,0:T(8,128)(2,1)S(1)}, bf16[256,512]{1,0:T(8,128)(2,1)S(1)}, u32[]{:S(2)}, u32[]{:S(2)}) %collective-permute-start.28) | collective-permute-done | bytes 262176 | tf_op jit(solution)/shard_map/ppermute | solution.py:446
  115.4 2.1 %due_columns.5 = (f32[4,384,128]{2,1,0:T(8,128)S(1)}, f32[4,384,128]{2,1,0:T(8,128)S(1)}) custom-call(s32[2]{0:T(128)S(1)} %pad_add_fusion.place_ref, f32[1536,1024]{1,0:T(8,128)} %bitcast.46, f32[1536,1024]{1,0:T(8,128)} %bitcast.47, f32[1536,1024]{1,0:T(8,128)} %bitcast.48, f32[1536,1024]{1,0:T(8,128)} %bitcast.49, f32[1536,1024]{1,0:T(8,128)} %bitcast.52, ...), custom_call_target="tpu_custom_call" | custom-call | bytes 3145728 | tf_op jit(solution)/shard_map/due_columns/pallas_call | solution.py:344
  117.5 2.5 %collective-permute-done.25.refs_6_ = bf16[256,512]{1,0:T(8,128)(2,1)S(1)} collective-permute-done((bf16[256,512]{1,0:T(8,128)(2,1)S(1)}, bf16[256,512]{1,0:T(8,128)(2,1)S(1)}, u32[]{:S(2)}, u32[]{:S(2)}) %collective-permute-start.25) | collective-permute-done | bytes 262176 | tf_op jit(solution)/shard_map/ppermute | solution.py:446
  120.6 4.8 %gradient.6 = (f32[1536,512]{1,0:T(8,128)}, f32[8,128]{1,0:T(8,128)S(1)}, f32[1536,128]{1,0:T(8,128)S(1)}) custom-call(s32[2]{0:T(128)S(1)} %pad_add_fusion.place_ref, bf16[1536,256]{1,0:T(8,128)(2,1)S(1)} %get-tuple-element.68.refs_0_, bf16[1536,256]{1,0:T(8,128)(2,1)S(1)} %get-tuple-element.69.refs_1_, bf16[1536,256]{1,0:T(8,128)(2,1)S(1)} %get-tuple-element.82.refs_2_, ...), custom_call_target="tpu_custom_call" | custom-call | flops 1610612736 | bytes 6291456 | tf_op jit(solution)/shard_map/gradient/pallas_call | solution.py:232
  125.4 3.2 %gradient.5.refs_8_ = f32[1536,512]{1,0:T(8,128)S(1)} custom-call(s32[2]{0:T(128)S(1)} %pad_add_fusion.place_ref, bf16[1536,256]{1,0:T(8,128)(2,1)S(1)} %get-tuple-element.90.refs_0_, bf16[1536,256]{1,0:T(8,128)(2,1)S(1)} %get-tuple-element.91.refs_1_, bf16[1536,256]{1,0:T(8,128)(2,1)S(1)} %get-tuple-element.92.refs_2_, ...), custom_call_target="tpu_custom_call" | custom-call | flops 1610612736 | bytes 6291456 | tf_op jit(solution)/shard_map/gradient/pallas_call | solution.py:232
  128.6 4.8 %gradient.7 = (f32[1536,512]{1,0:T(8,128)}, f32[8,128]{1,0:T(8,128)S(1)}, f32[1536,128]{1,0:T(8,128)S(1)}) custom-call(s32[2]{0:T(128)S(1)} %pad_add_fusion.place_ref, bf16[1536,256]{1,0:T(8,128)(2,1)S(1)} %get-tuple-element.68.refs_0_, bf16[1536,256]{1,0:T(8,128)(2,1)S(1)} %get-tuple-element.69.refs_1_, bf16[1536,256]{1,0:T(8,128)(2,1)S(1)} %get-tuple-element.82.refs_2_, ...), custom_call_target="tpu_custom_call" | custom-call | flops 1610612736 | bytes 6291456 | tf_op jit(solution)/shard_map/gradient/pallas_call | solution.py:232
  133.4 1.2 collective-permute-done.34
  134.6 1.6 collective-permute-start.37
  136.6 1.5 collective-permute-start.35
  138.0 1.0 collective-permute-done.37.refs_3_
  139.1 0.7 collective-permute-done.36.refs_2_
  140.2 1.5 adam_frag.1
  141.7 1.5 collective-permute-start.38
  143.2 1.8 %collective-permute-start.39 = (bf16[384,128]{1,0:T(8,128)(2,1)S(1)}, bf16[384,128]{1,0:T(8,128)(2,1)S(1)}, u32[]{:S(2)}, u32[]{:S(2)}) collective-permute-start(bf16[384,128]{1,0:T(8,128)(2,1)S(1)} %get-tuple-element.113), channel_id=1, source_target_pairs={{0,16},{8,24},{16,0},{24,8},{1,17},{9,25},{17,1},{25,9},{2,18},{10... | collective-permute-start | bytes 294920 | tf_op jit(solution)/shard_map/ppermute | solution.py:446
  145.0 1.2 collective-permute-start.40
  146.2 9.7 %adam_rows.2 = (f32[1536,1024]{1,0:T(8,128)}, f32[1536,1024]{1,0:T(8,128)}, f32[1536,1024]{1,0:T(8,128)}, f32[8,128]{1,0:T(8,128)S(1)}) custom-call(f32[3]{0:T(128)S(1)} %pad_maximum_fusion.sc_ref, f32[1536,1024]{1,0:T(8,128)} %bitcast.44, f32[1536,1024]{1,0:T(8,128)} %bitcast.50, f32[1536,1024]{1,0:T(8,128)} %bitcast.56, ...), custom_call_target="tpu_custom_call" | custom-call | flops 15728640 | bytes 22020096 | tf_op jit(solution)/shard_map/adam_rows/pallas_call | solution.py:287
  156.0 2.7 %collective-permute-start.43 = (bf16[384,128]{1,0:T(8,128)(2,1)S(1)}, bf16[384,128]{1,0:T(8,128)(2,1)S(1)}, u32[]{:S(2)}, u32[]{:S(2)}) collective-permute-start(bf16[384,128]{1,0:T(8,128)(2,1)S(1)} %convert_element_type.24.refs_7_), channel_id=1, source_target_pairs={{0,24},{8,16},{16,8},{24,0},{1,25},{9,17},{17,9},{25,1},{2,26},{10... | collective-permute-start | bytes 294920 | tf_op jit(solution)/shard_map/ppermute | solution.py:446
  158.7 1.8 %collective-permute-start.41 = (bf16[384,128]{1,0:T(8,128)(2,1)S(1)}, bf16[384,128]{1,0:T(8,128)(2,1)S(1)}, u32[]{:S(2)}, u32[]{:S(2)}) collective-permute-start(bf16[384,128]{1,0:T(8,128)(2,1)S(1)} %convert_element_type.24.refs_7_), channel_id=1, source_target_pairs={{0,8},{8,0},{16,24},{24,16},{1,9},{9,1},{17,25},{25,17},{2,10},{10... | collective-permute-start | bytes 294920 | tf_op jit(solution)/shard_map/ppermute | solution.py:446
  160.5 9.7 %adam_rows.3 = (f32[1536,1024]{1,0:T(8,128)}, f32[1536,1024]{1,0:T(8,128)}, f32[1536,1024]{1,0:T(8,128)}) custom-call(f32[3]{0:T(128)S(1)} %pad_maximum_fusion.sc_ref, f32[1536,1024]{1,0:T(8,128)} %bitcast.45, f32[1536,1024]{1,0:T(8,128)} %bitcast.51, f32[1536,1024]{1,0:T(8,128)} %bitcast.57, ...), custom_call_target="tpu_custom_call", output_to_operand_aliasing={{0}: (10, {}), {1}: (11, {}), {2}: (12, {})} | custom-call | flops 15728640 | bytes 22020096 | tf_op jit(solution)/shard_map/adam_rows/pallas_call | solution.py:287
  170.3 2.4 %outer_step.1 = (f32[1536,1024]{1,0:T(8,128)}, f32[384,1024]{1,0:T(8,128)}, f32[384,1024]{1,0:T(8,128)}) custom-call(s32[2]{0:T(128)S(1)} %pad_add_fusion.place_ref, f32[1536,1024]{1,0:T(8,128)} %get-tuple-element.109.refs_0_, f32[384,1024]{1,0:T(8,128)} %get-tuple-element.74.refs_1_, ...), custom_call_target="tpu_custom_call", output_to_operand_aliasing={{0}: (1, {}), {1}: (2, {}), {2}: (3, {})} | custom-call | flops 1966080 | bytes 3932160 | tf_op jit(solution)/shard_map/outer_step/pallas_call | solution.py:428
  (66 shorter events, 4.9 us)
Async XLA Ops:
  3.2 14.5 %collective-permute-start.5 = (f32[384,128]{1,0:T(8,128)S(1)}, f32[384,128]{1,0:T(8,128)S(1)}, u32[]{:S(2)}, u32[]{:S(2)}) collective-permute-start(f32[384,128]{1,0:T(8,128)S(1)} %get-tuple-element.126), channel_id=1, source_target_pairs={{0,8},{8,0},{16,24},{24,16},{1,9},{9,1},{17,25},{25,17},{2,10},{10... | collective-permute-start | bytes 589832 | tf_op jit(solution)/shard_map/ppermute | solution.py:446
  6.3 12.6 %collective-permute-start.7 = (f32[384,128]{1,0:T(8,128)S(1)}, f32[384,128]{1,0:T(8,128)S(1)}, u32[]{:S(2)}, u32[]{:S(2)}) collective-permute-start(f32[384,128]{1,0:T(8,128)S(1)} %get-tuple-element.127), channel_id=1, source_target_pairs={{0,24},{8,16},{16,8},{24,0},{1,25},{9,17},{17,9},{25,1},{2,26},{10... | collective-permute-start | bytes 589832 | tf_op jit(solution)/shard_map/ppermute | solution.py:446
  8.8 17.4 %collective-permute-start.6 = (f32[384,128]{1,0:T(8,128)S(1)}, f32[384,128]{1,0:T(8,128)S(1)}, u32[]{:S(2)}, u32[]{:S(2)}) collective-permute-start(f32[384,128]{1,0:T(8,128)S(1)} %get-tuple-element.128), channel_id=1, source_target_pairs={{0,16},{8,24},{16,0},{24,8},{1,17},{9,25},{17,1},{25,9},{2,18},{10... | collective-permute-start | bytes 589832 | tf_op jit(solution)/shard_map/ppermute | solution.py:446
  10.9 37.5 %collective-permute-start.12 = (bf16[256,1536]{1,0:T(8,128)(2,1)}, bf16[256,1536]{1,0:T(8,128)(2,1)S(1)}, u32[]{:S(2)}, u32[]{:S(2)}) collective-permute-start(bf16[256,1536]{1,0:T(8,128)(2,1)} %pack.6), channel_id=1, source_target_pairs={{0,6},{1,7},{2,4},{3,5},{4,2},{5,3},{6,0},{7,1},{8,14},{9,15},{10,... | collective-permute-start | bytes 2359304 | tf_op jit(solution)/shard_map/ppermute | solution.py:446
  16.0 32.9 %collective-permute-start.13 = (bf16[256,1536]{1,0:T(8,128)(2,1)}, bf16[256,1536]{1,0:T(8,128)(2,1)S(1)}, u32[]{:S(2)}, u32[]{:S(2)}) collective-permute-start(bf16[256,1536]{1,0:T(8,128)(2,1)} %get-tuple-element.78), channel_id=1, source_target_pairs={{0,7},{1,6},{2,5},{3,4},{4,3},{5,2},{6,1},{7,0},{8,15},{9,14},{10,... | collective-permute-start | bytes 2359304 | tf_op jit(solution)/shard_map/ppermute | solution.py:446
  26.3 22.1 %copy-start.3 = (bf16[256,1536]{1,0:T(8,128)(2,1)S(1)}, bf16[256,1536]{1,0:T(8,128)(2,1)}, u32[]{:S(2)}) copy-start(bf16[256,1536]{1,0:T(8,128)(2,1)} %get-tuple-element.65) | copy-start | bytes 2359300
  26.3 22.6 %copy-start.2 = (bf16[256,1536]{1,0:T(8,128)(2,1)S(1)}, bf16[256,1536]{1,0:T(8,128)(2,1)}, u32[]{:S(2)}) copy-start(bf16[256,1536]{1,0:T(8,128)(2,1)} %get-tuple-element.70) | copy-start | bytes 2359300
  26.3 9.8 %collective-permute-start.10 = (f32[384,128]{1,0:T(8,128)S(1)}, f32[384,128]{1,0:T(8,128)S(1)}, u32[]{:S(2)}, u32[]{:S(2)}) collective-permute-start(f32[384,128]{1,0:T(8,128)S(1)} %get-tuple-element.124.refs_3_), channel_id=1, source_target_pairs={{0,24},{8,16},{16,8},{24,0},{1,25},{9,17},{17,9},{25,1},{2,26},{10... | collective-permute-start | bytes 589832 | tf_op jit(solution)/shard_map/ppermute | solution.py:446
  29.4 15.0 %collective-permute-start.9 = (f32[384,128]{1,0:T(8,128)S(1)}, f32[384,128]{1,0:T(8,128)S(1)}, u32[]{:S(2)}, u32[]{:S(2)}) collective-permute-start(f32[384,128]{1,0:T(8,128)S(1)} %get-tuple-element.124.refs_3_), channel_id=1, source_target_pairs={{0,16},{8,24},{16,0},{24,8},{1,17},{9,25},{17,1},{25,9},{2,18},{10... | collective-permute-start | bytes 589832 | tf_op jit(solution)/shard_map/ppermute | solution.py:446
  31.7 32.8 %collective-permute-start.4 = (bf16[256,1536]{1,0:T(8,128)(2,1)}, bf16[256,1536]{1,0:T(8,128)(2,1)S(1)}, u32[]{:S(2)}, u32[]{:S(2)}) collective-permute-start(bf16[256,1536]{1,0:T(8,128)(2,1)} %get-tuple-element.71), channel_id=1, source_target_pairs={{0,5},{1,4},{2,7},{3,6},{4,1},{5,0},{6,3},{7,2},{8,13},{9,12},{10,... | collective-permute-start | bytes 2359304 | tf_op jit(solution)/shard_map/ppermute | solution.py:446
  36.1 10.6 %collective-permute-start.8 = (f32[384,128]{1,0:T(8,128)S(1)}, f32[384,128]{1,0:T(8,128)S(1)}, u32[]{:S(2)}, u32[]{:S(2)}) collective-permute-start(f32[384,128]{1,0:T(8,128)S(1)} %get-tuple-element.124.refs_3_), channel_id=1, source_target_pairs={{0,8},{8,0},{16,24},{24,16},{1,9},{9,1},{17,25},{25,17},{2,10},{10... | collective-permute-start | bytes 589832 | tf_op jit(solution)/shard_map/ppermute | solution.py:446
  44.3 24.1 %collective-permute-start.1 = (bf16[256,1536]{1,0:T(8,128)(2,1)}, bf16[256,1536]{1,0:T(8,128)(2,1)S(1)}, u32[]{:S(2)}, u32[]{:S(2)}) collective-permute-start(bf16[256,1536]{1,0:T(8,128)(2,1)} %get-tuple-element.66), channel_id=1, source_target_pairs={{0,3},{1,2},{2,1},{3,0},{4,7},{5,6},{6,5},{7,4},{8,11},{9,10},{10,... | collective-permute-start | bytes 2359304 | tf_op jit(solution)/shard_map/ppermute | solution.py:446
  46.7 26.3 %collective-permute-start.18 = (bf16[256,1536]{1,0:T(8,128)(2,1)}, bf16[256,1536]{1,0:T(8,128)(2,1)S(1)}, u32[]{:S(2)}, u32[]{:S(2)}) collective-permute-start(bf16[256,1536]{1,0:T(8,128)(2,1)} %get-tuple-element.87), channel_id=1, source_target_pairs={{0,1},{1,0},{2,3},{3,2},{4,5},{5,4},{6,7},{7,6},{8,9},{9,8},{10,11... | collective-permute-start | bytes 2359304 | tf_op jit(solution)/shard_map/ppermute | solution.py:446
  48.3 33.2 %collective-permute-start = (bf16[256,1536]{1,0:T(8,128)(2,1)S(1)}, bf16[256,1536]{1,0:T(8,128)(2,1)S(1)}, u32[]{:S(2)}, u32[]{:S(2)}) collective-permute-start(bf16[256,1536]{1,0:T(8,128)(2,1)S(1)} %copy-done.3), channel_id=1, source_target_pairs={{0,2},{1,3},{2,0},{3,1},{4,6},{5,7},{6,4},{7,5},{8,10},{9,11},{10,... | collective-permute-start | bytes 2359304 | tf_op jit(solution)/shard_map/ppermute | solution.py:446
  48.9 19.4 %copy-start.1 = (bf16[1,256,1024]{2,1,0:T(8,128)(2,1)S(1)}, bf16[1,256,1024]{2,1,0:T(8,128)(2,1)}, u32[]{:S(2)}) copy-start(bf16[1,256,1024]{2,1,0:T(8,128)(2,1)} %param.10) | copy-start | bytes 1572868
  48.9 45.3 %collective-permute-start.3 = (bf16[256,1536]{1,0:T(8,128)(2,1)S(1)}, bf16[256,1536]{1,0:T(8,128)(2,1)S(1)}, u32[]{:S(2)}, u32[]{:S(2)}) collective-permute-start(bf16[256,1536]{1,0:T(8,128)(2,1)S(1)} %copy-done.2), channel_id=1, source_target_pairs={{0,4},{1,5},{2,6},{3,7},{4,0},{5,1},{6,2},{7,3},{8,12},{9,13},{10,... | collective-permute-start | bytes 2359304 | tf_op jit(solution)/shard_map/ppermute | solution.py:446
  64.5 7.6 %collective-permute-start.14 = (bf16[256,512]{1,0:T(8,128)(2,1)S(1)}, bf16[256,512]{1,0:T(8,128)(2,1)S(1)}, u32[]{:S(2)}, u32[]{:S(2)}) collective-permute-start(bf16[256,512]{1,0:T(8,128)(2,1)S(1)} %get-tuple-element.79), channel_id=1, source_target_pairs={{0,1},{1,0},{2,3},{3,2},{4,5},{5,4},{6,7},{7,6},{8,9},{9,8},{10,11... | collective-permute-start | bytes 786440 | tf_op jit(solution)/shard_map/ppermute | solution.py:446
  68.4 19.4 %collective-permute-start.21 = (bf16[256,512]{1,0:T(8,128)(2,1)S(1)}, bf16[256,512]{1,0:T(8,128)(2,1)S(1)}, u32[]{:S(2)}, u32[]{:S(2)}) collective-permute-start(bf16[256,512]{1,0:T(8,128)(2,1)S(1)} %slice.24.refs_4_), channel_id=1, source_target_pairs={{0,6},{1,7},{2,4},{3,5},{4,2},{5,3},{6,0},{7,1},{8,14},{9,15},{10,... | collective-permute-start | bytes 786440 | tf_op jit(solution)/shard_map/ppermute | solution.py:446
  72.1 15.8 %collective-permute-start.2 = (bf16[256,512]{1,0:T(8,128)(2,1)S(1)}, bf16[256,512]{1,0:T(8,128)(2,1)S(1)}, u32[]{:S(2)}, u32[]{:S(2)}) collective-permute-start(bf16[256,512]{1,0:T(8,128)(2,1)S(1)} %get-tuple-element.67), channel_id=1, source_target_pairs={{0,1},{1,0},{2,3},{3,2},{4,5},{5,4},{6,7},{7,6},{8,9},{9,8},{10,11... | collective-permute-start | bytes 786440 | tf_op jit(solution)/shard_map/ppermute | solution.py:446
  73.0 15.4 %collective-permute-start.11 = (bf16[256,512]{1,0:T(8,128)(2,1)S(1)}, bf16[256,512]{1,0:T(8,128)(2,1)S(1)}, u32[]{:S(2)}, u32[]{:S(2)}) collective-permute-start(bf16[256,512]{1,0:T(8,128)(2,1)S(1)} %get-tuple-element.77), channel_id=1, source_target_pairs={{0,1},{1,0},{2,3},{3,2},{4,5},{5,4},{6,7},{7,6},{8,9},{9,8},{10,11... | collective-permute-start | bytes 786440 | tf_op jit(solution)/shard_map/ppermute | solution.py:446
  81.6 15.5 %copy-start = (bf16[256,1536]{1,0:T(8,128)(2,1)S(1)}, bf16[256,1536]{1,0:T(8,128)(2,1)}, u32[]{:S(2)}) copy-start(bf16[256,1536]{1,0:T(8,128)(2,1)} %get-tuple-element.86.refs_0_.refs_1_.refs_2_.refs_3_) | copy-start | bytes 2359300
  81.6 12.0 %collective-permute-start.15 = (bf16[256,512]{1,0:T(8,128)(2,1)S(1)}, bf16[256,512]{1,0:T(8,128)(2,1)S(1)}, u32[]{:S(2)}, u32[]{:S(2)}) collective-permute-start(bf16[256,512]{1,0:T(8,128)(2,1)S(1)} %get-tuple-element.80), channel_id=1, source_target_pairs={{0,6},{1,7},{2,4},{3,5},{4,2},{5,3},{6,0},{7,1},{8,14},{9,15},{10,... | collective-permute-start | bytes 786440 | tf_op jit(solution)/shard_map/ppermute | solution.py:446
  87.9 7.5 %collective-permute-start.19 = (bf16[256,512]{1,0:T(8,128)(2,1)S(1)}, bf16[256,512]{1,0:T(8,128)(2,1)S(1)}, u32[]{:S(2)}, u32[]{:S(2)}) collective-permute-start(bf16[256,512]{1,0:T(8,128)(2,1)S(1)} %get-tuple-element.88), channel_id=1, source_target_pairs={{0,1},{1,0},{2,3},{3,2},{4,5},{5,4},{6,7},{7,6},{8,9},{9,8},{10,11... | collective-permute-start | bytes 786440 | tf_op jit(solution)/shard_map/ppermute | solution.py:446
  87.9 9.8 %collective-permute-start.20 = (bf16[256,512]{1,0:T(8,128)(2,1)S(1)}, bf16[256,512]{1,0:T(8,128)(2,1)S(1)}, u32[]{:S(2)}, u32[]{:S(2)}) collective-permute-start(bf16[256,512]{1,0:T(8,128)(2,1)S(1)} %slice.24.refs_4_), channel_id=1, source_target_pairs={{0,1},{1,0},{2,3},{3,2},{4,5},{5,4},{6,7},{7,6},{8,9},{9,8},{10,11... | collective-permute-start | bytes 786440 | tf_op jit(solution)/shard_map/ppermute | solution.py:446
  88.4 10.8 %collective-permute-start.32 = (bf16[256,512]{1,0:T(8,128)(2,1)S(1)}, bf16[256,512]{1,0:T(8,128)(2,1)S(1)}, u32[]{:S(2)}, u32[]{:S(2)}) collective-permute-start(bf16[256,512]{1,0:T(8,128)(2,1)S(1)} %slice.24.refs_4_), channel_id=1, source_target_pairs={{0,4},{1,5},{2,6},{3,7},{4,0},{5,1},{6,2},{7,3},{8,12},{9,13},{10,... | collective-permute-start | bytes 786440 | tf_op jit(solution)/shard_map/ppermute | solution.py:446
  93.5 5.6 %collective-permute-start.22 = (bf16[256,512]{1,0:T(8,128)(2,1)S(1)}, bf16[256,512]{1,0:T(8,128)(2,1)S(1)}, u32[]{:S(2)}, u32[]{:S(2)}) collective-permute-start(bf16[256,512]{1,0:T(8,128)(2,1)S(1)} %collective-permute-done.21.refs_6_), channel_id=1, source_target_pairs={{0,1},{1,0},{2,3},{3,2},{4,5},{5,4},{6,7},{7,6},{8,9},{9,8},{10,11... | collective-permute-start | bytes 786440 | tf_op jit(solution)/shard_map/ppermute | solution.py:446
  94.2 9.2 %collective-permute-start.16 = (bf16[256,512]{1,0:T(8,128)(2,1)S(1)}, bf16[256,512]{1,0:T(8,128)(2,1)S(1)}, u32[]{:S(2)}, u32[]{:S(2)}) collective-permute-start(bf16[256,512]{1,0:T(8,128)(2,1)S(1)} %get-tuple-element.84), channel_id=1, source_target_pairs={{0,2},{1,3},{2,0},{3,1},{4,6},{5,7},{6,4},{7,5},{8,10},{9,11},{10,... | collective-permute-start | bytes 786440 | tf_op jit(solution)/shard_map/ppermute | solution.py:446
  95.3 9.3 %collective-permute-start.17 = (bf16[256,512]{1,0:T(8,128)(2,1)S(1)}, bf16[256,512]{1,0:T(8,128)(2,1)S(1)}, u32[]{:S(2)}, u32[]{:S(2)}) collective-permute-start(bf16[256,512]{1,0:T(8,128)(2,1)S(1)} %get-tuple-element.85), channel_id=1, source_target_pairs={{0,4},{1,5},{2,6},{3,7},{4,0},{5,1},{6,2},{7,3},{8,12},{9,13},{10,... | collective-permute-start | bytes 786440 | tf_op jit(solution)/shard_map/ppermute | solution.py:446
  97.7 11.2 %collective-permute-start.30 = (bf16[256,512]{1,0:T(8,128)(2,1)S(1)}, bf16[256,512]{1,0:T(8,128)(2,1)S(1)}, u32[]{:S(2)}, u32[]{:S(2)}) collective-permute-start(bf16[256,512]{1,0:T(8,128)(2,1)S(1)} %slice.24.refs_4_), channel_id=1, source_target_pairs={{0,2},{1,3},{2,0},{3,1},{4,6},{5,7},{6,4},{7,5},{8,10},{9,11},{10,... | collective-permute-start | bytes 786440 | tf_op jit(solution)/shard_map/ppermute | solution.py:446
  99.1 9.8 %collective-permute-start.33 = (bf16[256,512]{1,0:T(8,128)(2,1)S(1)}, bf16[256,512]{1,0:T(8,128)(2,1)S(1)}, u32[]{:S(2)}, u32[]{:S(2)}) collective-permute-start(bf16[256,512]{1,0:T(8,128)(2,1)S(1)} %collective-permute-done.32.refs_6_), channel_id=1, source_target_pairs={{0,1},{1,0},{2,3},{3,2},{4,5},{5,4},{6,7},{7,6},{8,9},{9,8},{10,11... | collective-permute-start | bytes 786440 | tf_op jit(solution)/shard_map/ppermute | solution.py:446
  105.2 10.2 %collective-permute-start.28 = (bf16[256,512]{1,0:T(8,128)(2,1)S(1)}, bf16[256,512]{1,0:T(8,128)(2,1)S(1)}, u32[]{:S(2)}, u32[]{:S(2)}) collective-permute-start(bf16[256,512]{1,0:T(8,128)(2,1)S(1)} %key_backward.1.refs_4_), channel_id=1, source_target_pairs={{0,6},{1,7},{2,4},{3,5},{4,2},{5,3},{6,0},{7,1},{8,14},{9,15},{10,... | collective-permute-start | bytes 786440 | tf_op jit(solution)/shard_map/ppermute | solution.py:446
  106.9 13.1 %collective-permute-start.25 = (bf16[256,512]{1,0:T(8,128)(2,1)S(1)}, bf16[256,512]{1,0:T(8,128)(2,1)S(1)}, u32[]{:S(2)}, u32[]{:S(2)}) collective-permute-start(bf16[256,512]{1,0:T(8,128)(2,1)S(1)} %key_backward.1.refs_4_), channel_id=1, source_target_pairs={{0,4},{1,5},{2,6},{3,7},{4,0},{5,1},{6,2},{7,3},{8,12},{9,13},{10,... | collective-permute-start | bytes 786440 | tf_op jit(solution)/shard_map/ppermute | solution.py:446
  107.4 12.6 %collective-permute-start.23 = (bf16[256,512]{1,0:T(8,128)(2,1)S(1)}, bf16[256,512]{1,0:T(8,128)(2,1)S(1)}, u32[]{:S(2)}, u32[]{:S(2)}) collective-permute-start(bf16[256,512]{1,0:T(8,128)(2,1)S(1)} %key_backward.1.refs_4_), channel_id=1, source_target_pairs={{0,2},{1,3},{2,0},{3,1},{4,6},{5,7},{6,4},{7,5},{8,10},{9,11},{10,... | collective-permute-start | bytes 786440 | tf_op jit(solution)/shard_map/ppermute | solution.py:446
  108.9 11.6 %collective-permute-start.31 = (bf16[256,512]{1,0:T(8,128)(2,1)S(1)}, bf16[256,512]{1,0:T(8,128)(2,1)S(1)}, u32[]{:S(2)}, u32[]{:S(2)}) collective-permute-start(bf16[256,512]{1,0:T(8,128)(2,1)S(1)} %collective-permute-done.30.refs_4_), channel_id=1, source_target_pairs={{0,1},{1,0},{2,3},{3,2},{4,5},{5,4},{6,7},{7,6},{8,9},{9,8},{10,11... | collective-permute-start | bytes 786440 | tf_op jit(solution)/shard_map/ppermute | solution.py:446
  108.9 16.4 %collective-permute-start.27 = (bf16[256,512]{1,0:T(8,128)(2,1)S(1)}, bf16[256,512]{1,0:T(8,128)(2,1)S(1)}, u32[]{:S(2)}, u32[]{:S(2)}) collective-permute-start(bf16[256,512]{1,0:T(8,128)(2,1)S(1)} %key_backward.1.refs_4_), channel_id=1, source_target_pairs={{0,1},{1,0},{2,3},{3,2},{4,5},{5,4},{6,7},{7,6},{8,9},{9,8},{10,11... | collective-permute-start | bytes 786440 | tf_op jit(solution)/shard_map/ppermute | solution.py:446
  115.4 10.0 %collective-permute-start.29 = (bf16[256,512]{1,0:T(8,128)(2,1)S(1)}, bf16[256,512]{1,0:T(8,128)(2,1)S(1)}, u32[]{:S(2)}, u32[]{:S(2)}) collective-permute-start(bf16[256,512]{1,0:T(8,128)(2,1)S(1)} %collective-permute-done.28.refs_6_), channel_id=1, source_target_pairs={{0,1},{1,0},{2,3},{3,2},{4,5},{5,4},{6,7},{7,6},{8,9},{9,8},{10,11... | collective-permute-start | bytes 786440 | tf_op jit(solution)/shard_map/ppermute | solution.py:446
  120.0 8.5 %collective-permute-start.26 = (bf16[256,512]{1,0:T(8,128)(2,1)S(1)}, bf16[256,512]{1,0:T(8,128)(2,1)S(1)}, u32[]{:S(2)}, u32[]{:S(2)}) collective-permute-start(bf16[256,512]{1,0:T(8,128)(2,1)S(1)} %collective-permute-done.25.refs_6_), channel_id=1, source_target_pairs={{0,1},{1,0},{2,3},{3,2},{4,5},{5,4},{6,7},{7,6},{8,9},{9,8},{10,11... | collective-permute-start | bytes 786440 | tf_op jit(solution)/shard_map/ppermute | solution.py:446
  120.1 8.5 %collective-permute-start.24 = (bf16[256,512]{1,0:T(8,128)(2,1)S(1)}, bf16[256,512]{1,0:T(8,128)(2,1)S(1)}, u32[]{:S(2)}, u32[]{:S(2)}) collective-permute-start(bf16[256,512]{1,0:T(8,128)(2,1)S(1)} %collective-permute-done.23.refs_4_), channel_id=1, source_target_pairs={{0,1},{1,0},{2,3},{3,2},{4,5},{5,4},{6,7},{7,6},{8,9},{9,8},{10,11... | collective-permute-start | bytes 786440 | tf_op jit(solution)/shard_map/ppermute | solution.py:446
  133.4 1.2 collective-permute-start.34
  134.6 4.5 %collective-permute-start.37 = (f32[8,128]{1,0:T(8,128)S(1)}, f32[8,128]{1,0:T(8,128)S(1)}, u32[]{:S(2)}, u32[]{:S(2)}) collective-permute-start(f32[8,128]{1,0:T(8,128)S(1)} %add.32.refs_0_), channel_id=1, source_target_pairs={{0,6},{1,7},{2,4},{3,5},{4,2},{5,3},{6,0},{7,1},{8,14},{9,15},{10,... | collective-permute-start | bytes 12296 | tf_op jit(solution)/shard_map/ppermute | solution.py:446
  136.2 3.6 %collective-permute-start.36 = (f32[8,128]{1,0:T(8,128)S(1)}, f32[8,128]{1,0:T(8,128)S(1)}, u32[]{:S(2)}, u32[]{:S(2)}) collective-permute-start(f32[8,128]{1,0:T(8,128)S(1)} %add.32.refs_0_), channel_id=1, source_target_pairs={{0,4},{1,5},{2,6},{3,7},{4,0},{5,1},{6,2},{7,3},{8,12},{9,13},{10,... | collective-permute-start | bytes 12296 | tf_op jit(solution)/shard_map/ppermute | solution.py:446
  136.6 3.6 %collective-permute-start.35 = (f32[8,128]{1,0:T(8,128)S(1)}, f32[8,128]{1,0:T(8,128)S(1)}, u32[]{:S(2)}, u32[]{:S(2)}) collective-permute-start(f32[8,128]{1,0:T(8,128)S(1)} %add.32.refs_0_), channel_id=1, source_target_pairs={{0,2},{1,3},{2,0},{3,1},{4,6},{5,7},{6,4},{7,5},{8,10},{9,11},{10,... | collective-permute-start | bytes 12296 | tf_op jit(solution)/shard_map/ppermute | solution.py:446
  141.7 14.2 %collective-permute-start.38 = (bf16[384,128]{1,0:T(8,128)(2,1)S(1)}, bf16[384,128]{1,0:T(8,128)(2,1)S(1)}, u32[]{:S(2)}, u32[]{:S(2)}) collective-permute-start(bf16[384,128]{1,0:T(8,128)(2,1)S(1)} %get-tuple-element.112), channel_id=1, source_target_pairs={{0,8},{8,0},{16,24},{24,16},{1,9},{9,1},{17,25},{25,17},{2,10},{10... | collective-permute-start | bytes 294920 | tf_op jit(solution)/shard_map/ppermute | solution.py:446
  143.2 12.7 %collective-permute-start.39 = (bf16[384,128]{1,0:T(8,128)(2,1)S(1)}, bf16[384,128]{1,0:T(8,128)(2,1)S(1)}, u32[]{:S(2)}, u32[]{:S(2)}) collective-permute-start(bf16[384,128]{1,0:T(8,128)(2,1)S(1)} %get-tuple-element.113), channel_id=1, source_target_pairs={{0,16},{8,24},{16,0},{24,8},{1,17},{9,25},{17,1},{25,9},{2,18},{10... | collective-permute-start | bytes 294920 | tf_op jit(solution)/shard_map/ppermute | solution.py:446
  145.0 11.0 %collective-permute-start.40 = (bf16[384,128]{1,0:T(8,128)(2,1)S(1)}, bf16[384,128]{1,0:T(8,128)(2,1)S(1)}, u32[]{:S(2)}, u32[]{:S(2)}) collective-permute-start(bf16[384,128]{1,0:T(8,128)(2,1)S(1)} %get-tuple-element.114), channel_id=1, source_target_pairs={{0,24},{8,16},{16,8},{24,0},{1,25},{9,17},{17,9},{25,1},{2,26},{10... | collective-permute-start | bytes 294920 | tf_op jit(solution)/shard_map/ppermute | solution.py:446
  156.0 14.2 %collective-permute-start.43 = (bf16[384,128]{1,0:T(8,128)(2,1)S(1)}, bf16[384,128]{1,0:T(8,128)(2,1)S(1)}, u32[]{:S(2)}, u32[]{:S(2)}) collective-permute-start(bf16[384,128]{1,0:T(8,128)(2,1)S(1)} %convert_element_type.24.refs_7_), channel_id=1, source_target_pairs={{0,24},{8,16},{16,8},{24,0},{1,25},{9,17},{17,9},{25,1},{2,26},{10... | collective-permute-start | bytes 294920 | tf_op jit(solution)/shard_map/ppermute | solution.py:446
  158.7 11.5 %collective-permute-start.42 = (bf16[384,128]{1,0:T(8,128)(2,1)S(1)}, bf16[384,128]{1,0:T(8,128)(2,1)S(1)}, u32[]{:S(2)}, u32[]{:S(2)}) collective-permute-start(bf16[384,128]{1,0:T(8,128)(2,1)S(1)} %convert_element_type.24.refs_7_), channel_id=1, source_target_pairs={{0,16},{8,24},{16,0},{24,8},{1,17},{9,25},{17,1},{25,9},{2,18},{10... | collective-permute-start | bytes 294920 | tf_op jit(solution)/shard_map/ppermute | solution.py:446
  158.7 11.5 %collective-permute-start.41 = (bf16[384,128]{1,0:T(8,128)(2,1)S(1)}, bf16[384,128]{1,0:T(8,128)(2,1)S(1)}, u32[]{:S(2)}, u32[]{:S(2)}) collective-permute-start(bf16[384,128]{1,0:T(8,128)(2,1)S(1)} %convert_element_type.24.refs_7_), channel_id=1, source_target_pairs={{0,8},{8,0},{16,24},{24,16},{1,9},{9,1},{17,25},{25,17},{2,10},{10... | collective-permute-start | bytes 294920 | tf_op jit(solution)/shard_map/ppermute | solution.py:446

commit v11 on v10

--- a/solution.py
+++ b/solution.py
@@ -507,13 +507,13 @@
     key_weights = cast_left(params, kv_width)
 
     last = far[-1]
-    blocks[last + 1] = after(blocks[last + 1], *base, anchor_copy, momentum_copy, scalars)
+    blocks[last + 1] = after(blocks[last + 1], anchor_copy, momentum_copy, scalars, old_first, old_second)
     parts, flipped = [], {}
     for k in far + [0]:
         theirs, flipped[k + 1] = partial_keys(blocks[k + 1], key_weights)
         theirs = swap(theirs, "fsdp", 1)
         if k == last:
-            theirs = after(theirs, *parts[:1])
+            theirs = after(theirs, *parts[:1], *base)
         part_k, flipped[k] = partial_keys(blocks[k], key_weights, theirs)
         parts.append(swap(part_k, "fsdp", k) if k else part_k)
     spread = [0, 1] + [k + odd for k in far for odd in range(2)]
@@ -524,13 +524,16 @@
     keys = {0: key_backward(parts, incoming, 0)}
     for k in far:
         keys[k] = swap(keys[0], "fsdp", k)
-    for k in range(0, shards, 2):
-        keys[k + 1] = swap(keys[k], "fsdp", 1)
+    keys[1] = swap(keys[0], "fsdp", 1)
 
     grad_values, square, due = gradient(
-        after(place, old_first, old_second), pick(flipped, rest), pick(values, rest), values_first
-    )
+        place, pick(flipped, rest), pick(values, rest), values_first
+    )
+    for k in near[2::2]:
+        keys[k + 1] = swap(after(keys[k], square), "fsdp", 1)
     (keys_first,) = gradient(place, pick(flipped, near), pick(keys, near), last=False)
+    for k in rest[::2]:
+        keys[k + 1] = swap(after(keys[k], keys_first), "fsdp", 1)
     grad_keys, square, due = gradient(
         place, pick(flipped, rest), pick(keys, rest), keys_first, square, due
     )

time: 174 us -> 172 us (0.989)
  waiting for transfers between devices: 57.5 us -> 51.4 us
  starting transfers between devices: 46.5 us -> 50.1 us
    ppermute x44, waiting for transfers between devices: 57.5 us -> 51.4 us  [swap(): return lax.ppermute(block, axis, [(i, i ^ offset) for i in range(count)])]
    ppermute x44, starting transfers between devices: 46.5 us -> 50.1 us  [swap(): return lax.ppermute(block, axis, [(i, i ^ offset) for i in range(count)])]
  transfers between devices with their start and end apart: 44 -> 44, of which waited for: 18 -> 21; matrix products, arithmetic and copies ran while one was open for 0% -> 0% of each run, Pallas kernels for 32% -> 32%
where the time goes in v11:
time: 172 us; the launch traced here: 171 us
  Pallas kernels  65.7 us (38%)
  waiting for transfers between devices  51.4 us (30%)
  starting transfers between devices  50.1 us (29%)
  between operations  3.64 us (2%)
    ppermute x44, waiting for transfers between devices, swap(): return lax.ppermute(block, axis, [(i, i ^ offset) for i in range(count)])  51.4 us
    ppermute x44, starting transfers between devices, swap(): return lax.ppermute(block, axis, [(i, i ^ offset) for i in range(count)])  50.1 us
    pallas_call x2, Pallas kernels, adam_rows(): pl.pallas_call(functools.partial(adam_kernel, len(squares), len(into)), o...  19.5 us
    pallas_call x4, Pallas kernels, gradient(): pl.pallas_call(functools.partial(grad_kernel, len(flipped), base is not N...  16 us
    pallas_call x4, Pallas kernels, pack(): pl.pallas_call(functools.partial(pack_kernel, offsets), out_shape=[pltpu....  9.19 us
    pallas_call x3, Pallas kernels, due_columns(): pl.pallas_call(functools.partial(pick_kernel, blocks), out_shape=[jax.Sha...  5.55 us
    pallas_call x8, Pallas kernels, partial_keys(): pl.pallas_call(functools.partial(partial_kernel, pieces), out_shape=[jax....  4.82 us
    pallas_call x1, Pallas kernels, cast_left(): pl.pallas_call(cast_kernel, out_shape=jax.ShapeDtypeStruct((rows, width),...  3.46 us
  transfers between devices with their start and end apart: 44, of which 21 were waited for; matrix products, arithmetic and copies ran while one was open for 0% of the time, Pallas kernels for 32%

profile of v11, /device:TPU:0, one launch (start us, length us, event | category | flops | bytes accessed | tf_op | source)
XLA Modules:
  0.0 171.3 jit_solution(9065938691971583957)
XLA Ops:
  1.4 1.8 %due_columns.5.w_ref = f32[4,384,128]{2,1,0:T(8,128)S(1)} custom-call(s32[2]{0:T(128)S(1)} %pad_add_fusion.place_ref, f32[1536,1024]{1,0:T(8,128)} %bitcast.39, f32[1536,1024]{1,0:T(8,128)} %bitcast.40, f32[1536,1024]{1,0:T(8,128)} %bitcast.41, f32[1536,1024]{1,0:T(8,128)} %bitcast.42), custom_call_target="tpu_custom_call" | custom-call | bytes 1572864 | tf_op jit(solution)/shard_map/due_columns/pallas_call | solution.py:344
  3.2 3.1 %collective-permute-start.10 = (f32[384,128]{1,0:T(8,128)S(1)}, f32[384,128]{1,0:T(8,128)S(1)}, u32[]{:S(2)}, u32[]{:S(2)}) collective-permute-start(f32[384,128]{1,0:T(8,128)S(1)} %get-tuple-element.130), channel_id=1, source_target_pairs={{0,8},{8,0},{16,24},{24,16},{1,9},{9,1},{17,25},{25,17},{2,10},{10... | collective-permute-start | bytes 589832 | tf_op jit(solution)/shard_map/ppermute | solution.py:446
  6.3 2.5 %collective-permute-start.12 = (f32[384,128]{1,0:T(8,128)S(1)}, f32[384,128]{1,0:T(8,128)S(1)}, u32[]{:S(2)}, u32[]{:S(2)}) collective-permute-start(f32[384,128]{1,0:T(8,128)S(1)} %get-tuple-element.131), channel_id=1, source_target_pairs={{0,24},{8,16},{16,8},{24,0},{1,25},{9,17},{17,9},{25,1},{2,26},{10... | collective-permute-start | bytes 589832 | tf_op jit(solution)/shard_map/ppermute | solution.py:446
  8.9 2.0 %pack.6 = bf16[256,1536]{1,0:T(8,128)(2,1)} custom-call(s32[1]{0:T(128)} %bitcast.4.me_ref, bf16[256,12288]{1,0:T(8,128)(2,1)} %bitcast.58), custom_call_target="tpu_custom_call" | custom-call | bytes 1572864 | tf_op jit(solution)/shard_map/pack/pallas_call | solution.py:68
  10.9 2.5 %collective-permute-start.6 = (bf16[256,1536]{1,0:T(8,128)(2,1)}, bf16[256,1536]{1,0:T(8,128)(2,1)S(1)}, u32[]{:S(2)}, u32[]{:S(2)}) collective-permute-start(bf16[256,1536]{1,0:T(8,128)(2,1)} %pack.6), channel_id=1, source_target_pairs={{0,6},{1,7},{2,4},{3,5},{4,2},{5,3},{6,0},{7,1},{8,14},{9,15},{10,... | collective-permute-start | bytes 2359304 | tf_op jit(solution)/shard_map/ppermute | solution.py:446
  13.4 2.6 %pack.4 = (bf16[256,1536]{1,0:T(8,128)(2,1)}, bf16[256,1536]{1,0:T(8,128)(2,1)}, bf16[256,1536]{1,0:T(8,128)(2,1)}) custom-call(s32[1]{0:T(128)} %bitcast.4.me_ref, bf16[256,12288]{1,0:T(8,128)(2,1)} %bitcast.59), custom_call_target="tpu_custom_call" | custom-call | bytes 4718592 | tf_op jit(solution)/shard_map/pack/pallas_call | solution.py:68
  16.1 1.6 due_columns.4
  17.7 1.2 collective-permute-done.12
  18.9 7.3 %collective-permute-done.11 = f32[384,128]{1,0:T(8,128)S(1)} collective-permute-done((f32[384,128]{1,0:T(8,128)S(1)}, f32[384,128]{1,0:T(8,128)S(1)}, u32[]{:S(2)}, u32[]{:S(2)}) %collective-permute-start.11) | collective-permute-done | bytes 196640 | tf_op jit(solution)/shard_map/ppermute | solution.py:446
  26.3 3.1 %collective-permute-start.15 = (f32[384,128]{1,0:T(8,128)S(1)}, f32[384,128]{1,0:T(8,128)S(1)}, u32[]{:S(2)}, u32[]{:S(2)}) collective-permute-start(f32[384,128]{1,0:T(8,128)S(1)} %get-tuple-element.128.refs_3_), channel_id=1, source_target_pairs={{0,24},{8,16},{16,8},{24,0},{1,25},{9,17},{17,9},{25,1},{2,26},{10... | collective-permute-start | bytes 589832 | tf_op jit(solution)/shard_map/ppermute | solution.py:446
  29.4 2.3 %pack.5 = (bf16[256,1536]{1,0:T(8,128)(2,1)}, bf16[256,1536]{1,0:T(8,128)(2,1)}) custom-call(s32[1]{0:T(128)} %bitcast.4.me_ref, bf16[256,12288]{1,0:T(8,128)(2,1)} %bitcast.60), custom_call_target="tpu_custom_call" | custom-call | bytes 3145728 | tf_op jit(solution)/shard_map/pack/pallas_call | solution.py:68
  31.8 2.7 %collective-permute-start.4 = (bf16[256,1536]{1,0:T(8,128)(2,1)}, bf16[256,1536]{1,0:T(8,128)(2,1)S(1)}, u32[]{:S(2)}, u32[]{:S(2)}) collective-permute-start(bf16[256,1536]{1,0:T(8,128)(2,1)} %get-tuple-element.73), channel_id=1, source_target_pairs={{0,5},{1,4},{2,7},{3,6},{4,1},{5,0},{6,3},{7,2},{8,13},{9,12},{10,... | collective-permute-start | bytes 2359304 | tf_op jit(solution)/shard_map/ppermute | solution.py:446
  34.5 3.7 %collective-permute-start.14 = (f32[384,128]{1,0:T(8,128)S(1)}, f32[384,128]{1,0:T(8,128)S(1)}, u32[]{:S(2)}, u32[]{:S(2)}) collective-permute-start(f32[384,128]{1,0:T(8,128)S(1)} %get-tuple-element.128.refs_3_), channel_id=1, source_target_pairs={{0,16},{8,24},{16,0},{24,8},{1,17},{9,25},{17,1},{25,9},{2,18},{10... | collective-permute-start | bytes 589832 | tf_op jit(solution)/shard_map/ppermute | solution.py:446
  38.2 2.3 %pack.7 = (bf16[256,1536]{1,0:T(8,128)(2,1)}, bf16[256,1536]{1,0:T(8,128)(2,1)}) custom-call(s32[1]{0:T(128)} %bitcast.4.me_ref, bf16[256,12288]{1,0:T(8,128)(2,1)} %bitcast.61), custom_call_target="tpu_custom_call" | custom-call | bytes 3145728 | tf_op jit(solution)/shard_map/pack/pallas_call | solution.py:68
  40.5 1.7 %collective-permute-done.14.refs_5_ = f32[384,128]{1,0:T(8,128)S(1)} collective-permute-done((f32[384,128]{1,0:T(8,128)S(1)}, f32[384,128]{1,0:T(8,128)S(1)}, u32[]{:S(2)}, u32[]{:S(2)}) %collective-permute-start.14) | collective-permute-done | bytes 196640 | tf_op jit(solution)/shard_map/ppermute | solution.py:446
  42.2 1.6 collective-permute-start
  43.8 4.8 %collective-permute-done.7.refs_0_.refs_1_.refs_2_.refs_3_ = bf16[256,1536]{1,0:T(8,128)(2,1)S(1)} collective-permute-done((bf16[256,1536]{1,0:T(8,128)(2,1)}, bf16[256,1536]{1,0:T(8,128)(2,1)S(1)}, u32[]{:S(2)}, u32[]{:S(2)}) %collective-permute-start.7) | collective-permute-done | bytes 786464 | tf_op jit(solution)/shard_map/ppermute | solution.py:446
  49.1 3.5 %cast_left.1.refs_4_ = bf16[1536,512]{1,0:T(8,128)(2,1)S(1)} custom-call(f32[1536,1024]{1,0:T(8,128)} %bitcast.43), custom_call_target="tpu_custom_call" | custom-call | bytes 4718592 | tf_op jit(solution)/shard_map/cast_left/pallas_call | solution.py:92
  53.2 12.3 %collective-permute-done.1.refs_0_.refs_1_.refs_2_.refs_3_ = bf16[256,1536]{1,0:T(8,128)(2,1)S(1)} collective-permute-done((bf16[256,1536]{1,0:T(8,128)(2,1)}, bf16[256,1536]{1,0:T(8,128)(2,1)S(1)}, u32[]{:S(2)}, u32[]{:S(2)}) %collective-permute-start.1) | collective-permute-done | bytes 786464 | tf_op jit(solution)/shard_map/ppermute | solution.py:446
  65.5 1.0 collective-permute-start.8
  66.5 2.8 %duplicate.1 = (f32[384,1024]{1,0:T(8,128)}, f32[384,1024]{1,0:T(8,128)}) custom-call(f32[384,1024]{1,0:T(8,128)} %refs_0_.3, f32[384,1024]{1,0:T(8,128)} %refs_1_.3), custom_call_target="tpu_custom_call" | custom-call | bytes 6291456 | tf_op jit(solution)/shard_map/duplicate/pallas_call | solution.py:385
  70.2 2.1 %due_columns.3 = (f32[4,384,128]{2,1,0:T(8,128)S(1)}, f32[4,384,128]{2,1,0:T(8,128)S(1)}) custom-call(s32[2]{0:T(128)S(1)} %pad_add_fusion.place_ref, f32[1536,1024]{1,0:T(8,128)} %bitcast.46, f32[1536,1024]{1,0:T(8,128)} %bitcast.47, f32[1536,1024]{1,0:T(8,128)} %bitcast.48, f32[1536,1024]{1,0:T(8,128)} %bitcast.49, f32[1536,1024]{1,0:T(8,128)} %bitcast.52, ...), custom_call_target="tpu_custom_call" | custom-call | bytes 3145728 | tf_op jit(solution)/shard_map/due_columns/pallas_call | solution.py:344
  72.3 1.9 %collective-permute-start.13 = (f32[384,128]{1,0:T(8,128)S(1)}, f32[384,128]{1,0:T(8,128)S(1)}, u32[]{:S(2)}, u32[]{:S(2)}) collective-permute-start(f32[384,128]{1,0:T(8,128)S(1)} %get-tuple-element.128.refs_3_), channel_id=1, source_target_pairs={{0,8},{8,0},{16,24},{24,16},{1,9},{9,1},{17,25},{25,17},{2,10},{10... | collective-permute-start | bytes 589832 | tf_op jit(solution)/shard_map/ppermute | solution.py:446
  74.3 1.4 collective-permute-start.21
  76.9 0.6 partial_keys.12
  77.5 1.7 %collective-permute-done.13.refs_4_ = f32[384,128]{1,0:T(8,128)S(1)} collective-permute-done((f32[384,128]{1,0:T(8,128)S(1)}, f32[384,128]{1,0:T(8,128)S(1)}, u32[]{:S(2)}, u32[]{:S(2)}) %collective-permute-start.13) | collective-permute-done | bytes 196640 | tf_op jit(solution)/shard_map/ppermute | solution.py:446
  79.8 3.4 %collective-permute-done.refs_0_.refs_1_.refs_2_.refs_3_ = bf16[256,1536]{1,0:T(8,128)(2,1)S(1)} collective-permute-done((bf16[256,1536]{1,0:T(8,128)(2,1)S(1)}, bf16[256,1536]{1,0:T(8,128)(2,1)S(1)}, u32[]{:S(2)}, u32[]{:S(2)}) %collective-permute-start) | collective-permute-done | bytes 786464 | tf_op jit(solution)/shard_map/ppermute | solution.py:446
  83.2 1.4 collective-permute-start.9
  85.3 3.4 %collective-permute-done.21.refs_6_ = bf16[256,512]{1,0:T(8,128)(2,1)S(1)} collective-permute-done((bf16[256,512]{1,0:T(8,128)(2,1)S(1)}, bf16[256,512]{1,0:T(8,128)(2,1)S(1)}, u32[]{:S(2)}, u32[]{:S(2)}) %collective-permute-start.21) | collective-permute-done | bytes 262176 | tf_op jit(solution)/shard_map/ppermute | solution.py:446
  88.8 1.5 collective-permute-start.28
  90.3 1.5 collective-permute-start.26
  91.8 0.9 collective-permute-done.9.refs_0_
  92.7 0.6 partial_keys.9
  93.3 0.6 partial_keys.13
  93.9 1.6 collective-permute-start.16
  95.5 1.5 collective-permute-start.17
  98.3 1.1 collective-permute-done.26.refs_4_
  99.4 3.2 %gradient.4.refs_8_ = f32[1536,512]{1,0:T(8,128)S(1)} custom-call(s32[2]{0:T(128)S(1)} %pad_add_fusion.place_ref, bf16[1536,256]{1,0:T(8,128)(2,1)S(1)} %get-tuple-element.94.refs_0_, bf16[1536,256]{1,0:T(8,128)(2,1)S(1)} %get-tuple-element.95.refs_1_, bf16[1536,256]{1,0:T(8,128)(2,1)S(1)} %get-tuple-element.96.refs_2_, ...), custom_call_target="tpu_custom_call" | custom-call | flops 1610612736 | bytes 6291456 | tf_op jit(solution)/shard_map/gradient/pallas_call | solution.py:232
  102.6 1.7 %collective-permute-done.16.refs_1_ = bf16[256,512]{1,0:T(8,128)(2,1)S(1)} collective-permute-done((bf16[256,512]{1,0:T(8,128)(2,1)S(1)}, bf16[256,512]{1,0:T(8,128)(2,1)S(1)}, u32[]{:S(2)}, u32[]{:S(2)}) %collective-permute-start.16) | collective-permute-done | bytes 262176 | tf_op jit(solution)/shard_map/ppermute | solution.py:446
  104.9 2.0 %collective-permute-start.25 = (bf16[256,512]{1,0:T(8,128)(2,1)S(1)}, bf16[256,512]{1,0:T(8,128)(2,1)S(1)}, u32[]{:S(2)}, u32[]{:S(2)}) collective-permute-start(bf16[256,512]{1,0:T(8,128)(2,1)S(1)} %key_backward.1.refs_4_), channel_id=1, source_target_pairs={{0,6},{1,7},{2,4},{3,5},{4,2},{5,3},{6,0},{7,1},{8,14},{9,15},{10,... | collective-permute-start | bytes 786440 | tf_op jit(solution)/shard_map/ppermute | solution.py:446
  106.9 4.8 %gradient.5 = (f32[1536,512]{1,0:T(8,128)}, f32[8,128]{1,0:T(8,128)S(1)}, f32[1536,128]{1,0:T(8,128)S(1)}) custom-call(s32[2]{0:T(128)S(1)} %pad_add_fusion.place_ref, bf16[1536,256]{1,0:T(8,128)(2,1)S(1)} %get-tuple-element.70.refs_0_, bf16[1536,256]{1,0:T(8,128)(2,1)S(1)} %get-tuple-element.71.refs_1_, bf16[1536,256]{1,0:T(8,128)(2,1)S(1)} %get-tuple-element.86.refs_2_, ...), custom_call_target="tpu_custom_call" | custom-call | flops 1610612736 | bytes 6291456 | tf_op jit(solution)/shard_map/gradient/pallas_call | solution.py:232
  111.7 1.8 %collective-permute-done.25.refs_6_ = bf16[256,512]{1,0:T(8,128)(2,1)S(1)} collective-permute-done((bf16[256,512]{1,0:T(8,128)(2,1)S(1)}, bf16[256,512]{1,0:T(8,128)(2,1)S(1)}, u32[]{:S(2)}, u32[]{:S(2)}) %collective-permute-start.25) | collective-permute-done | bytes 262176 | tf_op jit(solution)/shard_map/ppermute | solution.py:446
  113.5 1.1 collective-permute-start.32
  114.6 2.1 %collective-permute-start.23 = (bf16[256,512]{1,0:T(8,128)(2,1)S(1)}, bf16[256,512]{1,0:T(8,128)(2,1)S(1)}, u32[]{:S(2)}, u32[]{:S(2)}) collective-permute-start(bf16[256,512]{1,0:T(8,128)(2,1)S(1)} %key_backward.1.refs_4_), channel_id=1, source_target_pairs={{0,2},{1,3},{2,0},{3,1},{4,6},{5,7},{6,4},{7,5},{8,10},{9,11},{10,... | collective-permute-start | bytes 786440 | tf_op jit(solution)/shard_map/ppermute | solution.py:446
  116.7 3.2 %gradient.6.refs_8_ = f32[1536,512]{1,0:T(8,128)S(1)} custom-call(s32[2]{0:T(128)S(1)} %pad_add_fusion.place_ref, bf16[1536,256]{1,0:T(8,128)(2,1)S(1)} %get-tuple-element.94.refs_0_, bf16[1536,256]{1,0:T(8,128)(2,1)S(1)} %get-tuple-element.95.refs_1_, bf16[1536,256]{1,0:T(8,128)(2,1)S(1)} %get-tuple-element.96.refs_2_, ...), custom_call_target="tpu_custom_call" | custom-call | flops 1610612736 | bytes 6291456 | tf_op jit(solution)/shard_map/gradient/pallas_call | solution.py:232
  119.8 2.4 %collective-permute-done.32.refs_6_ = bf16[256,512]{1,0:T(8,128)(2,1)S(1)} collective-permute-done((bf16[256,512]{1,0:T(8,128)(2,1)S(1)}, bf16[256,512]{1,0:T(8,128)(2,1)S(1)}, u32[]{:S(2)}, u32[]{:S(2)}) %collective-permute-start.32) | collective-permute-done | bytes 262176 | tf_op jit(solution)/shard_map/ppermute | solution.py:446
  122.2 1.1 collective-permute-done.23.refs_4_
  123.7 1.2 collective-permute-done.31.refs_5_
  124.9 4.8 %gradient.7 = (f32[1536,512]{1,0:T(8,128)}, f32[8,128]{1,0:T(8,128)S(1)}, f32[1536,128]{1,0:T(8,128)S(1)}) custom-call(s32[2]{0:T(128)S(1)} %pad_add_fusion.place_ref, bf16[1536,256]{1,0:T(8,128)(2,1)S(1)} %get-tuple-element.70.refs_0_, bf16[1536,256]{1,0:T(8,128)(2,1)S(1)} %get-tuple-element.71.refs_1_, bf16[1536,256]{1,0:T(8,128)(2,1)S(1)} %get-tuple-element.86.refs_2_, ...), custom_call_target="tpu_custom_call" | custom-call | flops 1610612736 | bytes 6291456 | tf_op jit(solution)/shard_map/gradient/pallas_call | solution.py:232
  129.8 1.0 collective-permute-done.34
  130.9 1.8 %collective-permute-start.37 = (f32[8,128]{1,0:T(8,128)S(1)}, f32[8,128]{1,0:T(8,128)S(1)}, u32[]{:S(2)}, u32[]{:S(2)}) collective-permute-start(f32[8,128]{1,0:T(8,128)S(1)} %add.32.refs_0_), channel_id=1, source_target_pairs={{0,6},{1,7},{2,4},{3,5},{4,2},{5,3},{6,0},{7,1},{8,14},{9,15},{10,... | collective-permute-start | bytes 12296 | tf_op jit(solution)/shard_map/ppermute | solution.py:446
  132.7 1.4 collective-permute-start.36
  134.4 1.0 collective-permute-done.37.refs_3_
  135.4 0.9 collective-permute-done.36.refs_2_
  136.3 1.4 collective-permute-done.35.refs_1_
  137.7 1.5 adam_frag.1
  139.2 1.6 collective-permute-start.38
  140.8 1.7 collective-permute-start.39
  142.5 1.2 collective-permute-start.40
  143.7 9.7 %adam_rows.2 = (f32[1536,1024]{1,0:T(8,128)}, f32[1536,1024]{1,0:T(8,128)}, f32[1536,1024]{1,0:T(8,128)}, f32[8,128]{1,0:T(8,128)S(1)}) custom-call(f32[3]{0:T(128)S(1)} %pad_maximum_fusion.sc_ref, f32[1536,1024]{1,0:T(8,128)} %bitcast.44, f32[1536,1024]{1,0:T(8,128)} %bitcast.50, f32[1536,1024]{1,0:T(8,128)} %bitcast.56, ...), custom_call_target="tpu_custom_call" | custom-call | flops 15728640 | bytes 22020096 | tf_op jit(solution)/shard_map/adam_rows/pallas_call | solution.py:287
  153.5 2.7 %collective-permute-start.43 = (bf16[384,128]{1,0:T(8,128)(2,1)S(1)}, bf16[384,128]{1,0:T(8,128)(2,1)S(1)}, u32[]{:S(2)}, u32[]{:S(2)}) collective-permute-start(bf16[384,128]{1,0:T(8,128)(2,1)S(1)} %convert_element_type.24.refs_7_), channel_id=1, source_target_pairs={{0,24},{8,16},{16,8},{24,0},{1,25},{9,17},{17,9},{25,1},{2,26},{10... | collective-permute-start | bytes 294920 | tf_op jit(solution)/shard_map/ppermute | solution.py:446
  156.3 1.7 %collective-permute-start.41 = (bf16[384,128]{1,0:T(8,128)(2,1)S(1)}, bf16[384,128]{1,0:T(8,128)(2,1)S(1)}, u32[]{:S(2)}, u32[]{:S(2)}) collective-permute-start(bf16[384,128]{1,0:T(8,128)(2,1)S(1)} %convert_element_type.24.refs_7_), channel_id=1, source_target_pairs={{0,8},{8,0},{16,24},{24,16},{1,9},{9,1},{17,25},{25,17},{2,10},{10... | collective-permute-start | bytes 294920 | tf_op jit(solution)/shard_map/ppermute | solution.py:446
  158.0 9.7 %adam_rows.3 = (f32[1536,1024]{1,0:T(8,128)}, f32[1536,1024]{1,0:T(8,128)}, f32[1536,1024]{1,0:T(8,128)}) custom-call(f32[3]{0:T(128)S(1)} %pad_maximum_fusion.sc_ref, f32[1536,1024]{1,0:T(8,128)} %bitcast.45, f32[1536,1024]{1,0:T(8,128)} %bitcast.51, f32[1536,1024]{1,0:T(8,128)} %bitcast.57, ...), custom_call_target="tpu_custom_call", output_to_operand_aliasing={{0}: (10, {}), {1}: (11, {}), {2}: (12, {})} | custom-call | flops 15728640 | bytes 22020096 | tf_op jit(solution)/shard_map/adam_rows/pallas_call | solution.py:287
  167.8 2.4 %outer_step.1 = (f32[1536,1024]{1,0:T(8,128)}, f32[384,1024]{1,0:T(8,128)}, f32[384,1024]{1,0:T(8,128)}) custom-call(s32[2]{0:T(128)S(1)} %pad_add_fusion.place_ref, f32[1536,1024]{1,0:T(8,128)} %get-tuple-element.113.refs_0_, f32[384,1024]{1,0:T(8,128)} %get-tuple-element.74.refs_1_, ...), custom_call_target="tpu_custom_call", output_to_operand_aliasing={{0}: (1, {}), {1}: (2, {}), {2}: (3, {})} | custom-call | flops 1966080 | bytes 3932160 | tf_op jit(solution)/shard_map/outer_step/pallas_call | solution.py:428
  (66 shorter events, 6.8 us)
Async XLA Ops:
  3.2 14.5 %collective-permute-start.10 = (f32[384,128]{1,0:T(8,128)S(1)}, f32[384,128]{1,0:T(8,128)S(1)}, u32[]{:S(2)}, u32[]{:S(2)}) collective-permute-start(f32[384,128]{1,0:T(8,128)S(1)} %get-tuple-element.130), channel_id=1, source_target_pairs={{0,8},{8,0},{16,24},{24,16},{1,9},{9,1},{17,25},{25,17},{2,10},{10... | collective-permute-start | bytes 589832 | tf_op jit(solution)/shard_map/ppermute | solution.py:446
  6.3 12.6 %collective-permute-start.12 = (f32[384,128]{1,0:T(8,128)S(1)}, f32[384,128]{1,0:T(8,128)S(1)}, u32[]{:S(2)}, u32[]{:S(2)}) collective-permute-start(f32[384,128]{1,0:T(8,128)S(1)} %get-tuple-element.131), channel_id=1, source_target_pairs={{0,24},{8,16},{16,8},{24,0},{1,25},{9,17},{17,9},{25,1},{2,26},{10... | collective-permute-start | bytes 589832 | tf_op jit(solution)/shard_map/ppermute | solution.py:446
  8.8 17.4 %collective-permute-start.11 = (f32[384,128]{1,0:T(8,128)S(1)}, f32[384,128]{1,0:T(8,128)S(1)}, u32[]{:S(2)}, u32[]{:S(2)}) collective-permute-start(f32[384,128]{1,0:T(8,128)S(1)} %get-tuple-element.132), channel_id=1, source_target_pairs={{0,16},{8,24},{16,0},{24,8},{1,17},{9,25},{17,1},{25,9},{2,18},{10... | collective-permute-start | bytes 589832 | tf_op jit(solution)/shard_map/ppermute | solution.py:446
  10.9 31.3 %collective-permute-start.6 = (bf16[256,1536]{1,0:T(8,128)(2,1)}, bf16[256,1536]{1,0:T(8,128)(2,1)S(1)}, u32[]{:S(2)}, u32[]{:S(2)}) collective-permute-start(bf16[256,1536]{1,0:T(8,128)(2,1)} %pack.6), channel_id=1, source_target_pairs={{0,6},{1,7},{2,4},{3,5},{4,2},{5,3},{6,0},{7,1},{8,14},{9,15},{10,... | collective-permute-start | bytes 2359304 | tf_op jit(solution)/shard_map/ppermute | solution.py:446
  16.0 32.6 %collective-permute-start.7 = (bf16[256,1536]{1,0:T(8,128)(2,1)}, bf16[256,1536]{1,0:T(8,128)(2,1)S(1)}, u32[]{:S(2)}, u32[]{:S(2)}) collective-permute-start(bf16[256,1536]{1,0:T(8,128)(2,1)} %get-tuple-element.80), channel_id=1, source_target_pairs={{0,7},{1,6},{2,5},{3,4},{4,3},{5,2},{6,1},{7,0},{8,15},{9,14},{10,... | collective-permute-start | bytes 2359304 | tf_op jit(solution)/shard_map/ppermute | solution.py:446
  26.2 16.0 %copy-start.3 = (bf16[256,1536]{1,0:T(8,128)(2,1)S(1)}, bf16[256,1536]{1,0:T(8,128)(2,1)}, u32[]{:S(2)}) copy-start(bf16[256,1536]{1,0:T(8,128)(2,1)} %get-tuple-element.67) | copy-start | bytes 2359300
  26.3 22.3 %copy-start.2 = (bf16[256,1536]{1,0:T(8,128)(2,1)S(1)}, bf16[256,1536]{1,0:T(8,128)(2,1)}, u32[]{:S(2)}) copy-start(bf16[256,1536]{1,0:T(8,128)(2,1)} %get-tuple-element.72) | copy-start | bytes 2359300
  26.3 8.2 %collective-permute-start.15 = (f32[384,128]{1,0:T(8,128)S(1)}, f32[384,128]{1,0:T(8,128)S(1)}, u32[]{:S(2)}, u32[]{:S(2)}) collective-permute-start(f32[384,128]{1,0:T(8,128)S(1)} %get-tuple-element.128.refs_3_), channel_id=1, source_target_pairs={{0,24},{8,16},{16,8},{24,0},{1,25},{9,17},{17,9},{25,1},{2,26},{10... | collective-permute-start | bytes 589832 | tf_op jit(solution)/shard_map/ppermute | solution.py:446
  31.7 33.8 %collective-permute-start.1 = (bf16[256,1536]{1,0:T(8,128)(2,1)}, bf16[256,1536]{1,0:T(8,128)(2,1)S(1)}, u32[]{:S(2)}, u32[]{:S(2)}) collective-permute-start(bf16[256,1536]{1,0:T(8,128)(2,1)} %get-tuple-element.68), channel_id=1, source_target_pairs={{0,3},{1,2},{2,1},{3,0},{4,7},{5,6},{6,5},{7,4},{8,11},{9,10},{10,... | collective-permute-start | bytes 2359304 | tf_op jit(solution)/shard_map/ppermute | solution.py:446
  31.8 40.6 %collective-permute-start.4 = (bf16[256,1536]{1,0:T(8,128)(2,1)}, bf16[256,1536]{1,0:T(8,128)(2,1)S(1)}, u32[]{:S(2)}, u32[]{:S(2)}) collective-permute-start(bf16[256,1536]{1,0:T(8,128)(2,1)} %get-tuple-element.73), channel_id=1, source_target_pairs={{0,5},{1,4},{2,7},{3,6},{4,1},{5,0},{6,3},{7,2},{8,13},{9,12},{10,... | collective-permute-start | bytes 2359304 | tf_op jit(solution)/shard_map/ppermute | solution.py:446
  34.5 7.7 %collective-permute-start.14 = (f32[384,128]{1,0:T(8,128)S(1)}, f32[384,128]{1,0:T(8,128)S(1)}, u32[]{:S(2)}, u32[]{:S(2)}) collective-permute-start(f32[384,128]{1,0:T(8,128)S(1)} %get-tuple-element.128.refs_3_), channel_id=1, source_target_pairs={{0,16},{8,24},{16,0},{24,8},{1,17},{9,25},{17,1},{25,9},{2,18},{10... | collective-permute-start | bytes 589832 | tf_op jit(solution)/shard_map/ppermute | solution.py:446
  42.2 37.1 %collective-permute-start.18 = (bf16[256,1536]{1,0:T(8,128)(2,1)}, bf16[256,1536]{1,0:T(8,128)(2,1)S(1)}, u32[]{:S(2)}, u32[]{:S(2)}) collective-permute-start(bf16[256,1536]{1,0:T(8,128)(2,1)} %get-tuple-element.91), channel_id=1, source_target_pairs={{0,1},{1,0},{2,3},{3,2},{4,5},{5,4},{6,7},{7,6},{8,9},{9,8},{10,11... | collective-permute-start | bytes 2359304 | tf_op jit(solution)/shard_map/ppermute | solution.py:446
  42.2 41.0 %collective-permute-start = (bf16[256,1536]{1,0:T(8,128)(2,1)S(1)}, bf16[256,1536]{1,0:T(8,128)(2,1)S(1)}, u32[]{:S(2)}, u32[]{:S(2)}) collective-permute-start(bf16[256,1536]{1,0:T(8,128)(2,1)S(1)} %copy-done.3), channel_id=1, source_target_pairs={{0,2},{1,3},{2,0},{3,1},{4,6},{5,7},{6,4},{7,5},{8,10},{9,11},{10,... | collective-permute-start | bytes 2359304 | tf_op jit(solution)/shard_map/ppermute | solution.py:446
  48.6 21.5 %copy-start.1 = (bf16[1,256,1024]{2,1,0:T(8,128)(2,1)S(1)}, bf16[1,256,1024]{2,1,0:T(8,128)(2,1)}, u32[]{:S(2)}) copy-start(bf16[1,256,1024]{2,1,0:T(8,128)(2,1)} %param.10) | copy-start | bytes 1572868
  48.6 36.6 %collective-permute-start.3 = (bf16[256,1536]{1,0:T(8,128)(2,1)S(1)}, bf16[256,1536]{1,0:T(8,128)(2,1)S(1)}, u32[]{:S(2)}, u32[]{:S(2)}) collective-permute-start(bf16[256,1536]{1,0:T(8,128)(2,1)S(1)} %copy-done.2), channel_id=1, source_target_pairs={{0,4},{1,5},{2,6},{3,7},{4,0},{5,1},{6,2},{7,3},{8,12},{9,13},{10,... | collective-permute-start | bytes 2359304 | tf_op jit(solution)/shard_map/ppermute | solution.py:446
  65.5 8.8 %collective-permute-start.8 = (bf16[256,512]{1,0:T(8,128)(2,1)S(1)}, bf16[256,512]{1,0:T(8,128)(2,1)S(1)}, u32[]{:S(2)}, u32[]{:S(2)}) collective-permute-start(bf16[256,512]{1,0:T(8,128)(2,1)S(1)} %get-tuple-element.81), channel_id=1, source_target_pairs={{0,1},{1,0},{2,3},{3,2},{4,5},{5,4},{6,7},{7,6},{8,9},{9,8},{10,11... | collective-permute-start | bytes 786440 | tf_op jit(solution)/shard_map/ppermute | solution.py:446
  72.3 6.9 %collective-permute-start.13 = (f32[384,128]{1,0:T(8,128)S(1)}, f32[384,128]{1,0:T(8,128)S(1)}, u32[]{:S(2)}, u32[]{:S(2)}) collective-permute-start(f32[384,128]{1,0:T(8,128)S(1)} %get-tuple-element.128.refs_3_), channel_id=1, source_target_pairs={{0,8},{8,0},{16,24},{24,16},{1,9},{9,1},{17,25},{25,17},{2,10},{10... | collective-permute-start | bytes 589832 | tf_op jit(solution)/shard_map/ppermute | solution.py:446
  74.3 14.5 %collective-permute-start.21 = (bf16[256,512]{1,0:T(8,128)(2,1)S(1)}, bf16[256,512]{1,0:T(8,128)(2,1)S(1)}, u32[]{:S(2)}, u32[]{:S(2)}) collective-permute-start(bf16[256,512]{1,0:T(8,128)(2,1)S(1)} %slice.24.refs_4_), channel_id=1, source_target_pairs={{0,6},{1,7},{2,4},{3,5},{4,2},{5,3},{6,0},{7,1},{8,14},{9,15},{10,... | collective-permute-start | bytes 786440 | tf_op jit(solution)/shard_map/ppermute | solution.py:446
  79.3 9.5 %collective-permute-start.2 = (bf16[256,512]{1,0:T(8,128)(2,1)S(1)}, bf16[256,512]{1,0:T(8,128)(2,1)S(1)}, u32[]{:S(2)}, u32[]{:S(2)}) collective-permute-start(bf16[256,512]{1,0:T(8,128)(2,1)S(1)} %get-tuple-element.69), channel_id=1, source_target_pairs={{0,1},{1,0},{2,3},{3,2},{4,5},{5,4},{6,7},{7,6},{8,9},{9,8},{10,11... | collective-permute-start | bytes 786440 | tf_op jit(solution)/shard_map/ppermute | solution.py:446
  79.3 11.0 %collective-permute-start.5 = (bf16[256,512]{1,0:T(8,128)(2,1)S(1)}, bf16[256,512]{1,0:T(8,128)(2,1)S(1)}, u32[]{:S(2)}, u32[]{:S(2)}) collective-permute-start(bf16[256,512]{1,0:T(8,128)(2,1)S(1)} %get-tuple-element.79), channel_id=1, source_target_pairs={{0,1},{1,0},{2,3},{3,2},{4,5},{5,4},{6,7},{7,6},{8,9},{9,8},{10,11... | collective-permute-start | bytes 786440 | tf_op jit(solution)/shard_map/ppermute | solution.py:446
  83.2 13.8 %copy-start = (bf16[256,1536]{1,0:T(8,128)(2,1)S(1)}, bf16[256,1536]{1,0:T(8,128)(2,1)}, u32[]{:S(2)}) copy-start(bf16[256,1536]{1,0:T(8,128)(2,1)} %get-tuple-element.90.refs_0_.refs_1_.refs_2_.refs_3_) | copy-start | bytes 2359300
  83.2 9.5 %collective-permute-start.9 = (bf16[256,512]{1,0:T(8,128)(2,1)S(1)}, bf16[256,512]{1,0:T(8,128)(2,1)S(1)}, u32[]{:S(2)}, u32[]{:S(2)}) collective-permute-start(bf16[256,512]{1,0:T(8,128)(2,1)S(1)} %get-tuple-element.82), channel_id=1, source_target_pairs={{0,6},{1,7},{2,4},{3,5},{4,2},{5,3},{6,0},{7,1},{8,14},{9,15},{10,... | collective-permute-start | bytes 786440 | tf_op jit(solution)/shard_map/ppermute | solution.py:446
  85.2 8.7 %collective-permute-start.20 = (bf16[256,512]{1,0:T(8,128)(2,1)S(1)}, bf16[256,512]{1,0:T(8,128)(2,1)S(1)}, u32[]{:S(2)}, u32[]{:S(2)}) collective-permute-start(bf16[256,512]{1,0:T(8,128)(2,1)S(1)} %slice.24.refs_4_), channel_id=1, source_target_pairs={{0,1},{1,0},{2,3},{3,2},{4,5},{5,4},{6,7},{7,6},{8,9},{9,8},{10,11... | collective-permute-start | bytes 786440 | tf_op jit(solution)/shard_map/ppermute | solution.py:446
  88.8 6.7 %collective-permute-start.19 = (bf16[256,512]{1,0:T(8,128)(2,1)S(1)}, bf16[256,512]{1,0:T(8,128)(2,1)S(1)}, u32[]{:S(2)}, u32[]{:S(2)}) collective-permute-start(bf16[256,512]{1,0:T(8,128)(2,1)S(1)} %get-tuple-element.92), channel_id=1, source_target_pairs={{0,1},{1,0},{2,3},{3,2},{4,5},{5,4},{6,7},{7,6},{8,9},{9,8},{10,11... | collective-permute-start | bytes 786440 | tf_op jit(solution)/shard_map/ppermute | solution.py:446
  88.8 9.5 %collective-permute-start.28 = (bf16[256,512]{1,0:T(8,128)(2,1)S(1)}, bf16[256,512]{1,0:T(8,128)(2,1)S(1)}, u32[]{:S(2)}, u32[]{:S(2)}) collective-permute-start(bf16[256,512]{1,0:T(8,128)(2,1)S(1)} %slice.24.refs_4_), channel_id=1, source_target_pairs={{0,4},{1,5},{2,6},{3,7},{4,0},{5,1},{6,2},{7,3},{8,12},{9,13},{10,... | collective-permute-start | bytes 786440 | tf_op jit(solution)/shard_map/ppermute | solution.py:446
  90.3 9.1 %collective-permute-start.26 = (bf16[256,512]{1,0:T(8,128)(2,1)S(1)}, bf16[256,512]{1,0:T(8,128)(2,1)S(1)}, u32[]{:S(2)}, u32[]{:S(2)}) collective-permute-start(bf16[256,512]{1,0:T(8,128)(2,1)S(1)} %slice.24.refs_4_), channel_id=1, source_target_pairs={{0,2},{1,3},{2,0},{3,1},{4,6},{5,7},{6,4},{7,5},{8,10},{9,11},{10,... | collective-permute-start | bytes 786440 | tf_op jit(solution)/shard_map/ppermute | solution.py:446
  92.7 6.7 %collective-permute-start.22 = (bf16[256,512]{1,0:T(8,128)(2,1)S(1)}, bf16[256,512]{1,0:T(8,128)(2,1)S(1)}, u32[]{:S(2)}, u32[]{:S(2)}) collective-permute-start(bf16[256,512]{1,0:T(8,128)(2,1)S(1)} %collective-permute-done.21.refs_6_), channel_id=1, source_target_pairs={{0,1},{1,0},{2,3},{3,2},{4,5},{5,4},{6,7},{7,6},{8,9},{9,8},{10,11... | collective-permute-start | bytes 786440 | tf_op jit(solution)/shard_map/ppermute | solution.py:446
  93.9 10.4 %collective-permute-start.16 = (bf16[256,512]{1,0:T(8,128)(2,1)S(1)}, bf16[256,512]{1,0:T(8,128)(2,1)S(1)}, u32[]{:S(2)}, u32[]{:S(2)}) collective-permute-start(bf16[256,512]{1,0:T(8,128)(2,1)S(1)} %get-tuple-element.88), channel_id=1, source_target_pairs={{0,2},{1,3},{2,0},{3,1},{4,6},{5,7},{6,4},{7,5},{8,10},{9,11},{10,... | collective-permute-start | bytes 786440 | tf_op jit(solution)/shard_map/ppermute | solution.py:446
  95.5 8.9 %collective-permute-start.17 = (bf16[256,512]{1,0:T(8,128)(2,1)S(1)}, bf16[256,512]{1,0:T(8,128)(2,1)S(1)}, u32[]{:S(2)}, u32[]{:S(2)}) collective-permute-start(bf16[256,512]{1,0:T(8,128)(2,1)S(1)} %get-tuple-element.89), channel_id=1, source_target_pairs={{0,4},{1,5},{2,6},{3,7},{4,0},{5,1},{6,2},{7,3},{8,12},{9,13},{10,... | collective-permute-start | bytes 786440 | tf_op jit(solution)/shard_map/ppermute | solution.py:446
  98.2 8.7 %collective-permute-start.29 = (bf16[256,512]{1,0:T(8,128)(2,1)S(1)}, bf16[256,512]{1,0:T(8,128)(2,1)S(1)}, u32[]{:S(2)}, u32[]{:S(2)}) collective-permute-start(bf16[256,512]{1,0:T(8,128)(2,1)S(1)} %collective-permute-done.28.refs_6_), channel_id=1, source_target_pairs={{0,1},{1,0},{2,3},{3,2},{4,5},{5,4},{6,7},{7,6},{8,9},{9,8},{10,11... | collective-permute-start | bytes 786440 | tf_op jit(solution)/shard_map/ppermute | solution.py:446
  99.4 7.5 %collective-permute-start.27 = (bf16[256,512]{1,0:T(8,128)(2,1)S(1)}, bf16[256,512]{1,0:T(8,128)(2,1)S(1)}, u32[]{:S(2)}, u32[]{:S(2)}) collective-permute-start(bf16[256,512]{1,0:T(8,128)(2,1)S(1)} %collective-permute-done.26.refs_4_), channel_id=1, source_target_pairs={{0,1},{1,0},{2,3},{3,2},{4,5},{5,4},{6,7},{7,6},{8,9},{9,8},{10,11... | collective-permute-start | bytes 786440 | tf_op jit(solution)/shard_map/ppermute | solution.py:446
  104.9 8.6 %collective-permute-start.25 = (bf16[256,512]{1,0:T(8,128)(2,1)S(1)}, bf16[256,512]{1,0:T(8,128)(2,1)S(1)}, u32[]{:S(2)}, u32[]{:S(2)}) collective-permute-start(bf16[256,512]{1,0:T(8,128)(2,1)S(1)} %key_backward.1.refs_4_), channel_id=1, source_target_pairs={{0,6},{1,7},{2,4},{3,5},{4,2},{5,3},{6,0},{7,1},{8,14},{9,15},{10,... | collective-permute-start | bytes 786440 | tf_op jit(solution)/shard_map/ppermute | solution.py:446
  111.7 5.0 %collective-permute-start.24 = (bf16[256,512]{1,0:T(8,128)(2,1)S(1)}, bf16[256,512]{1,0:T(8,128)(2,1)S(1)}, u32[]{:S(2)}, u32[]{:S(2)}) collective-permute-start(bf16[256,512]{1,0:T(8,128)(2,1)S(1)} %key_backward.1.refs_4_), channel_id=1, source_target_pairs={{0,1},{1,0},{2,3},{3,2},{4,5},{5,4},{6,7},{7,6},{8,9},{9,8},{10,11... | collective-permute-start | bytes 786440 | tf_op jit(solution)/shard_map/ppermute | solution.py:446
  113.5 3.2 %collective-permute-start.30 = (bf16[256,512]{1,0:T(8,128)(2,1)S(1)}, bf16[256,512]{1,0:T(8,128)(2,1)S(1)}, u32[]{:S(2)}, u32[]{:S(2)}) collective-permute-start(bf16[256,512]{1,0:T(8,128)(2,1)S(1)} %collective-permute-done.25.refs_6_), channel_id=1, source_target_pairs={{0,1},{1,0},{2,3},{3,2},{4,5},{5,4},{6,7},{7,6},{8,9},{9,8},{10,11... | collective-permute-start | bytes 786440 | tf_op jit(solution)/shard_map/ppermute | solution.py:446
  113.5 8.7 %collective-permute-start.32 = (bf16[256,512]{1,0:T(8,128)(2,1)S(1)}, bf16[256,512]{1,0:T(8,128)(2,1)S(1)}, u32[]{:S(2)}, u32[]{:S(2)}) collective-permute-start(bf16[256,512]{1,0:T(8,128)(2,1)S(1)} %key_backward.1.refs_4_), channel_id=1, source_target_pairs={{0,4},{1,5},{2,6},{3,7},{4,0},{5,1},{6,2},{7,3},{8,12},{9,13},{10,... | collective-permute-start | bytes 786440 | tf_op jit(solution)/shard_map/ppermute | solution.py:446
  114.6 8.8 %collective-permute-start.23 = (bf16[256,512]{1,0:T(8,128)(2,1)S(1)}, bf16[256,512]{1,0:T(8,128)(2,1)S(1)}, u32[]{:S(2)}, u32[]{:S(2)}) collective-permute-start(bf16[256,512]{1,0:T(8,128)(2,1)S(1)} %key_backward.1.refs_4_), channel_id=1, source_target_pairs={{0,2},{1,3},{2,0},{3,1},{4,6},{5,7},{6,4},{7,5},{8,10},{9,11},{10,... | collective-permute-start | bytes 786440 | tf_op jit(solution)/shard_map/ppermute | solution.py:446
  122.2 1.5 collective-permute-start.33
  123.4 1.5 collective-permute-start.31
  129.7 1.2 collective-permute-start.34
  130.9 4.5 %collective-permute-start.37 = (f32[8,128]{1,0:T(8,128)S(1)}, f32[8,128]{1,0:T(8,128)S(1)}, u32[]{:S(2)}, u32[]{:S(2)}) collective-permute-start(f32[8,128]{1,0:T(8,128)S(1)} %add.32.refs_0_), channel_id=1, source_target_pairs={{0,6},{1,7},{2,4},{3,5},{4,2},{5,3},{6,0},{7,1},{8,14},{9,15},{10,... | collective-permute-start | bytes 12296 | tf_op jit(solution)/shard_map/ppermute | solution.py:446
  132.7 3.6 %collective-permute-start.36 = (f32[8,128]{1,0:T(8,128)S(1)}, f32[8,128]{1,0:T(8,128)S(1)}, u32[]{:S(2)}, u32[]{:S(2)}) collective-permute-start(f32[8,128]{1,0:T(8,128)S(1)} %add.32.refs_0_), channel_id=1, source_target_pairs={{0,4},{1,5},{2,6},{3,7},{4,0},{5,1},{6,2},{7,3},{8,12},{9,13},{10,... | collective-permute-start | bytes 12296 | tf_op jit(solution)/shard_map/ppermute | solution.py:446
  134.1 3.6 %collective-permute-start.35 = (f32[8,128]{1,0:T(8,128)S(1)}, f32[8,128]{1,0:T(8,128)S(1)}, u32[]{:S(2)}, u32[]{:S(2)}) collective-permute-start(f32[8,128]{1,0:T(8,128)S(1)} %add.32.refs_0_), channel_id=1, source_target_pairs={{0,2},{1,3},{2,0},{3,1},{4,6},{5,7},{6,4},{7,5},{8,10},{9,11},{10,... | collective-permute-start | bytes 12296 | tf_op jit(solution)/shard_map/ppermute | solution.py:446
  139.2 14.2 %collective-permute-start.38 = (bf16[384,128]{1,0:T(8,128)(2,1)S(1)}, bf16[384,128]{1,0:T(8,128)(2,1)S(1)}, u32[]{:S(2)}, u32[]{:S(2)}) collective-permute-start(bf16[384,128]{1,0:T(8,128)(2,1)S(1)} %get-tuple-element.116), channel_id=1, source_target_pairs={{0,8},{8,0},{16,24},{24,16},{1,9},{9,1},{17,25},{25,17},{2,10},{10... | collective-permute-start | bytes 294920 | tf_op jit(solution)/shard_map/ppermute | solution.py:446
  140.8 12.6 %collective-permute-start.39 = (bf16[384,128]{1,0:T(8,128)(2,1)S(1)}, bf16[384,128]{1,0:T(8,128)(2,1)S(1)}, u32[]{:S(2)}, u32[]{:S(2)}) collective-permute-start(bf16[384,128]{1,0:T(8,128)(2,1)S(1)} %get-tuple-element.117), channel_id=1, source_target_pairs={{0,16},{8,24},{16,0},{24,8},{1,17},{9,25},{17,1},{25,9},{2,18},{10... | collective-permute-start | bytes 294920 | tf_op jit(solution)/shard_map/ppermute | solution.py:446
  142.5 10.9 %collective-permute-start.40 = (bf16[384,128]{1,0:T(8,128)(2,1)S(1)}, bf16[384,128]{1,0:T(8,128)(2,1)S(1)}, u32[]{:S(2)}, u32[]{:S(2)}) collective-permute-start(bf16[384,128]{1,0:T(8,128)(2,1)S(1)} %get-tuple-element.118), channel_id=1, source_target_pairs={{0,24},{8,16},{16,8},{24,0},{1,25},{9,17},{17,9},{25,1},{2,26},{10... | collective-permute-start | bytes 294920 | tf_op jit(solution)/shard_map/ppermute | solution.py:446
  153.5 14.2 %collective-permute-start.43 = (bf16[384,128]{1,0:T(8,128)(2,1)S(1)}, bf16[384,128]{1,0:T(8,128)(2,1)S(1)}, u32[]{:S(2)}, u32[]{:S(2)}) collective-permute-start(bf16[384,128]{1,0:T(8,128)(2,1)S(1)} %convert_element_type.24.refs_7_), channel_id=1, source_target_pairs={{0,24},{8,16},{16,8},{24,0},{1,25},{9,17},{17,9},{25,1},{2,26},{10... | collective-permute-start | bytes 294920 | tf_op jit(solution)/shard_map/ppermute | solution.py:446
  156.3 11.5 %collective-permute-start.42 = (bf16[384,128]{1,0:T(8,128)(2,1)S(1)}, bf16[384,128]{1,0:T(8,128)(2,1)S(1)}, u32[]{:S(2)}, u32[]{:S(2)}) collective-permute-start(bf16[384,128]{1,0:T(8,128)(2,1)S(1)} %convert_element_type.24.refs_7_), channel_id=1, source_target_pairs={{0,16},{8,24},{16,0},{24,8},{1,17},{9,25},{17,1},{25,9},{2,18},{10... | collective-permute-start | bytes 294920 | tf_op jit(solution)/shard_map/ppermute | solution.py:446
  156.3 11.5 %collective-permute-start.41 = (bf16[384,128]{1,0:T(8,128)(2,1)S(1)}, bf16[384,128]{1,0:T(8,128)(2,1)S(1)}, u32[]{:S(2)}, u32[]{:S(2)}) collective-permute-start(bf16[384,128]{1,0:T(8,128)(2,1)S(1)} %convert_element_type.24.refs_7_), channel_id=1, source_target_pairs={{0,8},{8,0},{16,24},{24,16},{1,9},{9,1},{17,25},{25,17},{2,10},{10... | collective-permute-start | bytes 294920 | tf_op jit(solution)/shard_map/ppermute | solution.py:446

commit v12 on v11

--- a/solution.py
+++ b/solution.py
@@ -296,7 +296,7 @@
         compiler_params=params_of(24),
         cost_estimate=cost(20 * count * width, 28 * count * width),
         name="adam_rows",
-    )(scalars, *in_hbm(*state), *squares, *in_hbm(*into))
+    )(scalars, *state[:3], *in_hbm(*state[3:]), *squares, *in_hbm(*into))
 
 
 def frag_kernel(squares, place_ref, sc_ref, w_ref, m_ref, v_ref, g_ref, *refs):
@@ -533,7 +533,7 @@
         keys[k + 1] = swap(after(keys[k], square), "fsdp", 1)
     (keys_first,) = gradient(place, pick(flipped, near), pick(keys, near), last=False)
     for k in rest[::2]:
-        keys[k + 1] = swap(after(keys[k], keys_first), "fsdp", 1)
+        keys[k + 1] = swap(after(keys[k], square), "fsdp", 1)
     grad_keys, square, due = gradient(
         place, pick(flipped, rest), pick(keys, rest), keys_first, square, due
     )

time: 172 us -> 165 us (0.959)
  Pallas kernels: 65.7 us -> 60.7 us
    pallas_call x2, Pallas kernels: 19.5 us -> 14.6 us  [adam_rows(): pl.pallas_call(functools.partial(adam_kernel, len(squares), len(into)), o...]
  transfers between devices with their start and end apart: 44 -> 44, of which waited for: 21 -> 18; matrix products, arithmetic and copies ran while one was open for 0% -> 0% of each run, Pallas kernels for 32% -> 31%
where the time goes in v12:
time: 165 us; the launch traced here: 164 us
  Pallas kernels  60.7 us (37%)
  waiting for transfers between devices  50.4 us (31%)
  starting transfers between devices  48.9 us (30%)
  between operations  3.73 us (2%)
    ppermute x44, waiting for transfers between devices, swap(): return lax.ppermute(block, axis, [(i, i ^ offset) for i in range(count)])  50.4 us
    ppermute x44, starting transfers between devices, swap(): return lax.ppermute(block, axis, [(i, i ^ offset) for i in range(count)])  48.9 us
    pallas_call x4, Pallas kernels, gradient(): pl.pallas_call(functools.partial(grad_kernel, len(flipped), base is not N...  16 us
    pallas_call x2, Pallas kernels, adam_rows(): pl.pallas_call(functools.partial(adam_kernel, len(squares), len(into)), o...  14.6 us
    pallas_call x4, Pallas kernels, pack(): pl.pallas_call(functools.partial(pack_kernel, offsets), out_shape=[pltpu....  9.19 us
    pallas_call x3, Pallas kernels, due_columns(): pl.pallas_call(functools.partial(pick_kernel, blocks), out_shape=[jax.Sha...  5.55 us
    pallas_call x8, Pallas kernels, partial_keys(): pl.pallas_call(functools.partial(partial_kernel, pieces), out_shape=[jax....  4.66 us
    pallas_call x1, Pallas kernels, cast_left(): pl.pallas_call(cast_kernel, out_shape=jax.ShapeDtypeStruct((rows, width),...  3.46 us
  transfers between devices with their start and end apart: 44, of which 18 were waited for; matrix products, arithmetic and copies ran while one was open for 0% of the time, Pallas kernels for 31%

profile of v12, /device:TPU:0, one launch (start us, length us, event | category | flops | bytes accessed | tf_op | source)
XLA Modules:
  0.0 164.0 jit_solution(15513803091876628051)
XLA Ops:
  1.4 1.8 %due_columns.5.w_ref = f32[4,384,128]{2,1,0:T(8,128)S(1)} custom-call(s32[2]{0:T(128)S(1)} %pad_add_fusion.place_ref, f32[1536,1024]{1,0:T(8,128)} %bitcast.35, f32[1536,1024]{1,0:T(8,128)} %bitcast.36, f32[1536,1024]{1,0:T(8,128)} %bitcast.37, f32[1536,1024]{1,0:T(8,128)} %bitcast.38), custom_call_target="tpu_custom_call" | custom-call | bytes 1572864 | tf_op jit(solution)/shard_map/due_columns/pallas_call | solution.py:344
  3.2 3.1 %collective-permute-start.10 = (f32[384,128]{1,0:T(8,128)S(1)}, f32[384,128]{1,0:T(8,128)S(1)}, u32[]{:S(2)}, u32[]{:S(2)}) collective-permute-start(f32[384,128]{1,0:T(8,128)S(1)} %get-tuple-element.130), channel_id=1, source_target_pairs={{0,8},{8,0},{16,24},{24,16},{1,9},{9,1},{17,25},{25,17},{2,10},{10... | collective-permute-start | bytes 589832 | tf_op jit(solution)/shard_map/ppermute | solution.py:446
  6.3 2.5 %collective-permute-start.12 = (f32[384,128]{1,0:T(8,128)S(1)}, f32[384,128]{1,0:T(8,128)S(1)}, u32[]{:S(2)}, u32[]{:S(2)}) collective-permute-start(f32[384,128]{1,0:T(8,128)S(1)} %get-tuple-element.131), channel_id=1, source_target_pairs={{0,24},{8,16},{16,8},{24,0},{1,25},{9,17},{17,9},{25,1},{2,26},{10... | collective-permute-start | bytes 589832 | tf_op jit(solution)/shard_map/ppermute | solution.py:446
  8.9 2.0 %pack.6 = bf16[256,1536]{1,0:T(8,128)(2,1)} custom-call(s32[1]{0:T(128)} %bitcast.4.me_ref, bf16[256,12288]{1,0:T(8,128)(2,1)} %bitcast.64), custom_call_target="tpu_custom_call" | custom-call | bytes 1572864 | tf_op jit(solution)/shard_map/pack/pallas_call | solution.py:68
  10.9 2.5 %collective-permute-start.6 = (bf16[256,1536]{1,0:T(8,128)(2,1)}, bf16[256,1536]{1,0:T(8,128)(2,1)S(1)}, u32[]{:S(2)}, u32[]{:S(2)}) collective-permute-start(bf16[256,1536]{1,0:T(8,128)(2,1)} %pack.6), channel_id=1, source_target_pairs={{0,6},{1,7},{2,4},{3,5},{4,2},{5,3},{6,0},{7,1},{8,14},{9,15},{10,... | collective-permute-start | bytes 2359304 | tf_op jit(solution)/shard_map/ppermute | solution.py:446
  13.4 2.6 %pack.4 = (bf16[256,1536]{1,0:T(8,128)(2,1)}, bf16[256,1536]{1,0:T(8,128)(2,1)}, bf16[256,1536]{1,0:T(8,128)(2,1)}) custom-call(s32[1]{0:T(128)} %bitcast.4.me_ref, bf16[256,12288]{1,0:T(8,128)(2,1)} %bitcast.65), custom_call_target="tpu_custom_call" | custom-call | bytes 4718592 | tf_op jit(solution)/shard_map/pack/pallas_call | solution.py:68
  16.1 1.6 due_columns.4
  17.7 1.2 collective-permute-done.12
  18.9 7.3 %collective-permute-done.11 = f32[384,128]{1,0:T(8,128)S(1)} collective-permute-done((f32[384,128]{1,0:T(8,128)S(1)}, f32[384,128]{1,0:T(8,128)S(1)}, u32[]{:S(2)}, u32[]{:S(2)}) %collective-permute-start.11) | collective-permute-done | bytes 196640 | tf_op jit(solution)/shard_map/ppermute | solution.py:446
  26.3 3.1 %collective-permute-start.15 = (f32[384,128]{1,0:T(8,128)S(1)}, f32[384,128]{1,0:T(8,128)S(1)}, u32[]{:S(2)}, u32[]{:S(2)}) collective-permute-start(f32[384,128]{1,0:T(8,128)S(1)} %get-tuple-element.128.refs_3_), channel_id=1, source_target_pairs={{0,24},{8,16},{16,8},{24,0},{1,25},{9,17},{17,9},{25,1},{2,26},{10... | collective-permute-start | bytes 589832 | tf_op jit(solution)/shard_map/ppermute | solution.py:446
  29.4 2.3 %pack.5 = (bf16[256,1536]{1,0:T(8,128)(2,1)}, bf16[256,1536]{1,0:T(8,128)(2,1)}) custom-call(s32[1]{0:T(128)} %bitcast.4.me_ref, bf16[256,12288]{1,0:T(8,128)(2,1)} %bitcast.66), custom_call_target="tpu_custom_call" | custom-call | bytes 3145728 | tf_op jit(solution)/shard_map/pack/pallas_call | solution.py:68
  31.8 2.7 %collective-permute-start.4 = (bf16[256,1536]{1,0:T(8,128)(2,1)}, bf16[256,1536]{1,0:T(8,128)(2,1)S(1)}, u32[]{:S(2)}, u32[]{:S(2)}) collective-permute-start(bf16[256,1536]{1,0:T(8,128)(2,1)} %get-tuple-element.73), channel_id=1, source_target_pairs={{0,5},{1,4},{2,7},{3,6},{4,1},{5,0},{6,3},{7,2},{8,13},{9,12},{10,... | collective-permute-start | bytes 2359304 | tf_op jit(solution)/shard_map/ppermute | solution.py:446
  34.5 3.7 %collective-permute-start.14 = (f32[384,128]{1,0:T(8,128)S(1)}, f32[384,128]{1,0:T(8,128)S(1)}, u32[]{:S(2)}, u32[]{:S(2)}) collective-permute-start(f32[384,128]{1,0:T(8,128)S(1)} %get-tuple-element.128.refs_3_), channel_id=1, source_target_pairs={{0,16},{8,24},{16,0},{24,8},{1,17},{9,25},{17,1},{25,9},{2,18},{10... | collective-permute-start | bytes 589832 | tf_op jit(solution)/shard_map/ppermute | solution.py:446
  38.2 2.3 %pack.7 = (bf16[256,1536]{1,0:T(8,128)(2,1)}, bf16[256,1536]{1,0:T(8,128)(2,1)}) custom-call(s32[1]{0:T(128)} %bitcast.4.me_ref, bf16[256,12288]{1,0:T(8,128)(2,1)} %bitcast.67), custom_call_target="tpu_custom_call" | custom-call | bytes 3145728 | tf_op jit(solution)/shard_map/pack/pallas_call | solution.py:68
  40.5 1.7 %collective-permute-done.14.refs_5_ = f32[384,128]{1,0:T(8,128)S(1)} collective-permute-done((f32[384,128]{1,0:T(8,128)S(1)}, f32[384,128]{1,0:T(8,128)S(1)}, u32[]{:S(2)}, u32[]{:S(2)}) %collective-permute-start.14) | collective-permute-done | bytes 196640 | tf_op jit(solution)/shard_map/ppermute | solution.py:446
  42.2 1.6 collective-permute-start
  43.8 4.8 %collective-permute-done.7.refs_0_.refs_1_.refs_2_.refs_3_ = bf16[256,1536]{1,0:T(8,128)(2,1)S(1)} collective-permute-done((bf16[256,1536]{1,0:T(8,128)(2,1)}, bf16[256,1536]{1,0:T(8,128)(2,1)S(1)}, u32[]{:S(2)}, u32[]{:S(2)}) %collective-permute-start.7) | collective-permute-done | bytes 786464 | tf_op jit(solution)/shard_map/ppermute | solution.py:446
  49.1 3.5 %cast_left.1.refs_4_ = bf16[1536,512]{1,0:T(8,128)(2,1)S(1)} custom-call(f32[1536,1024]{1,0:T(8,128)} %bitcast.39), custom_call_target="tpu_custom_call" | custom-call | bytes 4718592 | tf_op jit(solution)/shard_map/cast_left/pallas_call | solution.py:92
  52.6 0.6 partial_keys.11
  53.2 12.3 %collective-permute-done.1.refs_0_.refs_1_.refs_2_.refs_3_ = bf16[256,1536]{1,0:T(8,128)(2,1)S(1)} collective-permute-done((bf16[256,1536]{1,0:T(8,128)(2,1)}, bf16[256,1536]{1,0:T(8,128)(2,1)S(1)}, u32[]{:S(2)}, u32[]{:S(2)}) %collective-permute-start.1) | collective-permute-done | bytes 786464 | tf_op jit(solution)/shard_map/ppermute | solution.py:446
  65.5 1.0 collective-permute-start.8
  66.5 2.8 %duplicate.1 = (f32[384,1024]{1,0:T(8,128)}, f32[384,1024]{1,0:T(8,128)}) custom-call(f32[384,1024]{1,0:T(8,128)} %refs_0_.3, f32[384,1024]{1,0:T(8,128)} %refs_1_.3), custom_call_target="tpu_custom_call" | custom-call | bytes 6291456 | tf_op jit(solution)/shard_map/duplicate/pallas_call | solution.py:385
  70.2 2.1 %due_columns.3 = (f32[4,384,128]{2,1,0:T(8,128)S(1)}, f32[4,384,128]{2,1,0:T(8,128)S(1)}) custom-call(s32[2]{0:T(128)S(1)} %pad_add_fusion.place_ref, f32[1536,1024]{1,0:T(8,128)} %bitcast.44, f32[1536,1024]{1,0:T(8,128)} %bitcast.45, f32[1536,1024]{1,0:T(8,128)} %bitcast.46, f32[1536,1024]{1,0:T(8,128)} %bitcast.47, f32[1536,1024]{1,0:T(8,128)} %bitcast.52, ...), custom_call_target="tpu_custom_call" | custom-call | bytes 3145728 | tf_op jit(solution)/shard_map/due_columns/pallas_call | solution.py:344
  72.3 1.9 %collective-permute-start.13 = (f32[384,128]{1,0:T(8,128)S(1)}, f32[384,128]{1,0:T(8,128)S(1)}, u32[]{:S(2)}, u32[]{:S(2)}) collective-permute-start(f32[384,128]{1,0:T(8,128)S(1)} %get-tuple-element.128.refs_3_), channel_id=1, source_target_pairs={{0,8},{8,0},{16,24},{24,16},{1,9},{9,1},{17,25},{25,17},{2,10},{10... | collective-permute-start | bytes 589832 | tf_op jit(solution)/shard_map/ppermute | solution.py:446
  74.3 1.4 collective-permute-start.21
  75.7 0.6 partial_keys.10
  76.3 0.6 partial_keys.8
  76.9 0.6 partial_keys.12
  77.5 1.8 %collective-permute-done.13.refs_4_ = f32[384,128]{1,0:T(8,128)S(1)} collective-permute-done((f32[384,128]{1,0:T(8,128)S(1)}, f32[384,128]{1,0:T(8,128)S(1)}, u32[]{:S(2)}, u32[]{:S(2)}) %collective-permute-start.13) | collective-permute-done | bytes 196640 | tf_op jit(solution)/shard_map/ppermute | solution.py:446
  79.8 3.4 %collective-permute-done.refs_0_.refs_1_.refs_2_.refs_3_ = bf16[256,1536]{1,0:T(8,128)(2,1)S(1)} collective-permute-done((bf16[256,1536]{1,0:T(8,128)(2,1)S(1)}, bf16[256,1536]{1,0:T(8,128)(2,1)S(1)}, u32[]{:S(2)}, u32[]{:S(2)}) %collective-permute-start) | collective-permute-done | bytes 786464 | tf_op jit(solution)/shard_map/ppermute | solution.py:446
  83.2 1.4 collective-permute-start.9
  85.3 3.5 %collective-permute-done.21.refs_6_ = bf16[256,512]{1,0:T(8,128)(2,1)S(1)} collective-permute-done((bf16[256,512]{1,0:T(8,128)(2,1)S(1)}, bf16[256,512]{1,0:T(8,128)(2,1)S(1)}, u32[]{:S(2)}, u32[]{:S(2)}) %collective-permute-start.21) | collective-permute-done | bytes 262176 | tf_op jit(solution)/shard_map/ppermute | solution.py:446
  88.8 1.5 collective-permute-start.26
  90.3 1.5 collective-permute-start.24
  91.8 0.9 collective-permute-done.9.refs_0_
  93.9 1.6 collective-permute-start.16
  95.4 1.5 collective-permute-start.17
  97.5 0.7 collective-permute-done.26.refs_6_
  98.3 1.1 collective-permute-done.24.refs_4_
  99.4 3.2 %gradient.4.refs_8_ = f32[1536,512]{1,0:T(8,128)S(1)} custom-call(s32[2]{0:T(128)S(1)} %pad_add_fusion.place_ref, bf16[1536,256]{1,0:T(8,128)(2,1)S(1)} %get-tuple-element.94.refs_0_, bf16[1536,256]{1,0:T(8,128)(2,1)S(1)} %get-tuple-element.95.refs_1_, bf16[1536,256]{1,0:T(8,128)(2,1)S(1)} %get-tuple-element.96.refs_2_, ...), custom_call_target="tpu_custom_call" | custom-call | flops 1610612736 | bytes 6291456 | tf_op jit(solution)/shard_map/gradient/pallas_call | solution.py:232
  102.6 1.7 %collective-permute-done.16.refs_1_ = bf16[256,512]{1,0:T(8,128)(2,1)S(1)} collective-permute-done((bf16[256,512]{1,0:T(8,128)(2,1)S(1)}, bf16[256,512]{1,0:T(8,128)(2,1)S(1)}, u32[]{:S(2)}, u32[]{:S(2)}) %collective-permute-start.16) | collective-permute-done | bytes 262176 | tf_op jit(solution)/shard_map/ppermute | solution.py:446
  104.9 2.0 %collective-permute-start.32 = (bf16[256,512]{1,0:T(8,128)(2,1)S(1)}, bf16[256,512]{1,0:T(8,128)(2,1)S(1)}, u32[]{:S(2)}, u32[]{:S(2)}) collective-permute-start(bf16[256,512]{1,0:T(8,128)(2,1)S(1)} %key_backward.1.refs_4_), channel_id=1, source_target_pairs={{0,6},{1,7},{2,4},{3,5},{4,2},{5,3},{6,0},{7,1},{8,14},{9,15},{10,... | collective-permute-start | bytes 786440 | tf_op jit(solution)/shard_map/ppermute | solution.py:446
  106.9 1.0 collective-permute-start.29
  108.5 4.8 %gradient.5 = (f32[1536,512]{1,0:T(8,128)}, f32[8,128]{1,0:T(8,128)S(1)}, f32[1536,128]{1,0:T(8,128)S(1)}) custom-call(s32[2]{0:T(128)S(1)} %pad_add_fusion.place_ref, bf16[1536,256]{1,0:T(8,128)(2,1)S(1)} %get-tuple-element.70.refs_0_, bf16[1536,256]{1,0:T(8,128)(2,1)S(1)} %get-tuple-element.71.refs_1_, bf16[1536,256]{1,0:T(8,128)(2,1)S(1)} %get-tuple-element.86.refs_2_, ...), custom_call_target="tpu_custom_call" | custom-call | flops 1610612736 | bytes 6291456 | tf_op jit(solution)/shard_map/gradient/pallas_call | solution.py:232
  113.3 1.8 %collective-permute-done.32.refs_6_ = bf16[256,512]{1,0:T(8,128)(2,1)S(1)} collective-permute-done((bf16[256,512]{1,0:T(8,128)(2,1)S(1)}, bf16[256,512]{1,0:T(8,128)(2,1)S(1)}, u32[]{:S(2)}, u32[]{:S(2)}) %collective-permute-start.32) | collective-permute-done | bytes 262176 | tf_op jit(solution)/shard_map/ppermute | solution.py:446
  115.1 3.9 %collective-permute-done.29.refs_6_ = bf16[256,512]{1,0:T(8,128)(2,1)S(1)} collective-permute-done((bf16[256,512]{1,0:T(8,128)(2,1)S(1)}, bf16[256,512]{1,0:T(8,128)(2,1)S(1)}, u32[]{:S(2)}, u32[]{:S(2)}) %collective-permute-start.29) | collective-permute-done | bytes 262176 | tf_op jit(solution)/shard_map/ppermute | solution.py:446
  119.6 3.2 %gradient.6.refs_8_ = f32[1536,512]{1,0:T(8,128)S(1)} custom-call(s32[2]{0:T(128)S(1)} %pad_add_fusion.place_ref, bf16[1536,256]{1,0:T(8,128)(2,1)S(1)} %get-tuple-element.94.refs_0_, bf16[1536,256]{1,0:T(8,128)(2,1)S(1)} %get-tuple-element.95.refs_1_, bf16[1536,256]{1,0:T(8,128)(2,1)S(1)} %get-tuple-element.96.refs_2_, ...), custom_call_target="tpu_custom_call" | custom-call | flops 1610612736 | bytes 6291456 | tf_op jit(solution)/shard_map/gradient/pallas_call | solution.py:232
  122.9 4.8 %gradient.7 = (f32[1536,512]{1,0:T(8,128)}, f32[8,128]{1,0:T(8,128)S(1)}, f32[1536,128]{1,0:T(8,128)S(1)}) custom-call(s32[2]{0:T(128)S(1)} %pad_add_fusion.place_ref, bf16[1536,256]{1,0:T(8,128)(2,1)S(1)} %get-tuple-element.70.refs_0_, bf16[1536,256]{1,0:T(8,128)(2,1)S(1)} %get-tuple-element.71.refs_1_, bf16[1536,256]{1,0:T(8,128)(2,1)S(1)} %get-tuple-element.86.refs_2_, ...), custom_call_target="tpu_custom_call" | custom-call | flops 1610612736 | bytes 6291456 | tf_op jit(solution)/shard_map/gradient/pallas_call | solution.py:232
  127.7 1.1 collective-permute-done.34
  128.9 1.8 %collective-permute-start.37 = (f32[8,128]{1,0:T(8,128)S(1)}, f32[8,128]{1,0:T(8,128)S(1)}, u32[]{:S(2)}, u32[]{:S(2)}) collective-permute-start(f32[8,128]{1,0:T(8,128)S(1)} %add.32.refs_0_), channel_id=1, source_target_pairs={{0,6},{1,7},{2,4},{3,5},{4,2},{5,3},{6,0},{7,1},{8,14},{9,15},{10,... | collective-permute-start | bytes 12296 | tf_op jit(solution)/shard_map/ppermute | solution.py:446
  130.6 1.1 collective-permute-start.36
  131.7 0.6 collective-permute-start.35
  132.3 1.0 collective-permute-done.37.refs_3_
  133.4 0.9 collective-permute-done.36.refs_2_
  134.3 1.1 collective-permute-done.35.refs_1_
  135.3 1.5 adam_frag.1
  136.9 1.6 collective-permute-start.38
  138.5 1.7 %collective-permute-start.39 = (bf16[384,128]{1,0:T(8,128)(2,1)S(1)}, bf16[384,128]{1,0:T(8,128)(2,1)S(1)}, u32[]{:S(2)}, u32[]{:S(2)}) collective-permute-start(bf16[384,128]{1,0:T(8,128)(2,1)S(1)} %get-tuple-element.117), channel_id=1, source_target_pairs={{0,16},{8,24},{16,0},{24,8},{1,17},{9,25},{17,1},{25,9},{2,18},{10... | collective-permute-start | bytes 294920 | tf_op jit(solution)/shard_map/ppermute | solution.py:446
  140.2 1.2 collective-permute-start.40
  141.4 7.3 %adam_rows.2 = (f32[1536,1024]{1,0:T(8,128)}, f32[1536,1024]{1,0:T(8,128)}, f32[1536,1024]{1,0:T(8,128)}, f32[8,128]{1,0:T(8,128)S(1)}) custom-call(f32[3]{0:T(128)S(1)} %pad_maximum_fusion.sc_ref, f32[1536,1024]{1,0:T(8,128)S(1)} %bitcast.42, f32[1536,1024]{1,0:T(8,128)S(1)} %bitcast.50, f32[1536,1024]{1,0:T(8,128)S(1)} %bitcast.58, ...), custom_call_target="tpu_custom_call" | custom-call | flops 15728640 | bytes 22020096 | tf_op jit(solution)/shard_map/adam_rows/pallas_call | solution.py:287
  148.8 2.7 %collective-permute-start.43 = (bf16[384,128]{1,0:T(8,128)(2,1)S(1)}, bf16[384,128]{1,0:T(8,128)(2,1)S(1)}, u32[]{:S(2)}, u32[]{:S(2)}) collective-permute-start(bf16[384,128]{1,0:T(8,128)(2,1)S(1)} %convert_element_type.24.refs_7_), channel_id=1, source_target_pairs={{0,24},{8,16},{16,8},{24,0},{1,25},{9,17},{17,9},{25,1},{2,26},{10... | collective-permute-start | bytes 294920 | tf_op jit(solution)/shard_map/ppermute | solution.py:446
  151.5 1.7 %collective-permute-start.41 = (bf16[384,128]{1,0:T(8,128)(2,1)S(1)}, bf16[384,128]{1,0:T(8,128)(2,1)S(1)}, u32[]{:S(2)}, u32[]{:S(2)}) collective-permute-start(bf16[384,128]{1,0:T(8,128)(2,1)S(1)} %convert_element_type.24.refs_7_), channel_id=1, source_target_pairs={{0,8},{8,0},{16,24},{24,16},{1,9},{9,1},{17,25},{25,17},{2,10},{10... | collective-permute-start | bytes 294920 | tf_op jit(solution)/shard_map/ppermute | solution.py:446
  153.3 7.3 %adam_rows.3 = (f32[1536,1024]{1,0:T(8,128)}, f32[1536,1024]{1,0:T(8,128)}, f32[1536,1024]{1,0:T(8,128)}) custom-call(f32[3]{0:T(128)S(1)} %pad_maximum_fusion.sc_ref, f32[1536,1024]{1,0:T(8,128)S(1)} %bitcast.43, f32[1536,1024]{1,0:T(8,128)S(1)} %bitcast.51, ...), custom_call_target="tpu_custom_call", output_to_operand_aliasing={{0}: (10, {}), {1}: (11, {}), {2}: (12, {})} | custom-call | flops 15728640 | bytes 22020096 | tf_op jit(solution)/shard_map/adam_rows/pallas_call | solution.py:287
  160.5 2.4 %outer_step.1 = (f32[1536,1024]{1,0:T(8,128)}, f32[384,1024]{1,0:T(8,128)}, f32[384,1024]{1,0:T(8,128)}) custom-call(s32[2]{0:T(128)S(1)} %pad_add_fusion.place_ref, f32[1536,1024]{1,0:T(8,128)} %get-tuple-element.113.refs_0_, f32[384,1024]{1,0:T(8,128)} %get-tuple-element.74.refs_1_, ...), custom_call_target="tpu_custom_call", output_to_operand_aliasing={{0}: (1, {}), {1}: (2, {}), {2}: (3, {})} | custom-call | flops 1966080 | bytes 3932160 | tf_op jit(solution)/shard_map/outer_step/pallas_call | solution.py:428
  (81 shorter events, 5.8 us)
Async XLA Ops:
  3.2 14.5 %collective-permute-start.10 = (f32[384,128]{1,0:T(8,128)S(1)}, f32[384,128]{1,0:T(8,128)S(1)}, u32[]{:S(2)}, u32[]{:S(2)}) collective-permute-start(f32[384,128]{1,0:T(8,128)S(1)} %get-tuple-element.130), channel_id=1, source_target_pairs={{0,8},{8,0},{16,24},{24,16},{1,9},{9,1},{17,25},{25,17},{2,10},{10... | collective-permute-start | bytes 589832 | tf_op jit(solution)/shard_map/ppermute | solution.py:446
  6.3 12.6 %collective-permute-start.12 = (f32[384,128]{1,0:T(8,128)S(1)}, f32[384,128]{1,0:T(8,128)S(1)}, u32[]{:S(2)}, u32[]{:S(2)}) collective-permute-start(f32[384,128]{1,0:T(8,128)S(1)} %get-tuple-element.131), channel_id=1, source_target_pairs={{0,24},{8,16},{16,8},{24,0},{1,25},{9,17},{17,9},{25,1},{2,26},{10... | collective-permute-start | bytes 589832 | tf_op jit(solution)/shard_map/ppermute | solution.py:446
  8.8 17.4 %collective-permute-start.11 = (f32[384,128]{1,0:T(8,128)S(1)}, f32[384,128]{1,0:T(8,128)S(1)}, u32[]{:S(2)}, u32[]{:S(2)}) collective-permute-start(f32[384,128]{1,0:T(8,128)S(1)} %get-tuple-element.132), channel_id=1, source_target_pairs={{0,16},{8,24},{16,0},{24,8},{1,17},{9,25},{17,1},{25,9},{2,18},{10... | collective-permute-start | bytes 589832 | tf_op jit(solution)/shard_map/ppermute | solution.py:446
  10.9 31.3 %collective-permute-start.6 = (bf16[256,1536]{1,0:T(8,128)(2,1)}, bf16[256,1536]{1,0:T(8,128)(2,1)S(1)}, u32[]{:S(2)}, u32[]{:S(2)}) collective-permute-start(bf16[256,1536]{1,0:T(8,128)(2,1)} %pack.6), channel_id=1, source_target_pairs={{0,6},{1,7},{2,4},{3,5},{4,2},{5,3},{6,0},{7,1},{8,14},{9,15},{10,... | collective-permute-start | bytes 2359304 | tf_op jit(solution)/shard_map/ppermute | solution.py:446
  16.0 32.6 %collective-permute-start.7 = (bf16[256,1536]{1,0:T(8,128)(2,1)}, bf16[256,1536]{1,0:T(8,128)(2,1)S(1)}, u32[]{:S(2)}, u32[]{:S(2)}) collective-permute-start(bf16[256,1536]{1,0:T(8,128)(2,1)} %get-tuple-element.80), channel_id=1, source_target_pairs={{0,7},{1,6},{2,5},{3,4},{4,3},{5,2},{6,1},{7,0},{8,15},{9,14},{10,... | collective-permute-start | bytes 2359304 | tf_op jit(solution)/shard_map/ppermute | solution.py:446
  26.2 16.0 %copy-start.3 = (bf16[256,1536]{1,0:T(8,128)(2,1)S(1)}, bf16[256,1536]{1,0:T(8,128)(2,1)}, u32[]{:S(2)}) copy-start(bf16[256,1536]{1,0:T(8,128)(2,1)} %get-tuple-element.67) | copy-start | bytes 2359300
  26.3 22.3 %copy-start.2 = (bf16[256,1536]{1,0:T(8,128)(2,1)S(1)}, bf16[256,1536]{1,0:T(8,128)(2,1)}, u32[]{:S(2)}) copy-start(bf16[256,1536]{1,0:T(8,128)(2,1)} %get-tuple-element.72) | copy-start | bytes 2359300
  26.3 8.2 %collective-permute-start.15 = (f32[384,128]{1,0:T(8,128)S(1)}, f32[384,128]{1,0:T(8,128)S(1)}, u32[]{:S(2)}, u32[]{:S(2)}) collective-permute-start(f32[384,128]{1,0:T(8,128)S(1)} %get-tuple-element.128.refs_3_), channel_id=1, source_target_pairs={{0,24},{8,16},{16,8},{24,0},{1,25},{9,17},{17,9},{25,1},{2,26},{10... | collective-permute-start | bytes 589832 | tf_op jit(solution)/shard_map/ppermute | solution.py:446
  31.7 33.8 %collective-permute-start.1 = (bf16[256,1536]{1,0:T(8,128)(2,1)}, bf16[256,1536]{1,0:T(8,128)(2,1)S(1)}, u32[]{:S(2)}, u32[]{:S(2)}) collective-permute-start(bf16[256,1536]{1,0:T(8,128)(2,1)} %get-tuple-element.68), channel_id=1, source_target_pairs={{0,3},{1,2},{2,1},{3,0},{4,7},{5,6},{6,5},{7,4},{8,11},{9,10},{10,... | collective-permute-start | bytes 2359304 | tf_op jit(solution)/shard_map/ppermute | solution.py:446
  31.8 40.6 %collective-permute-start.4 = (bf16[256,1536]{1,0:T(8,128)(2,1)}, bf16[256,1536]{1,0:T(8,128)(2,1)S(1)}, u32[]{:S(2)}, u32[]{:S(2)}) collective-permute-start(bf16[256,1536]{1,0:T(8,128)(2,1)} %get-tuple-element.73), channel_id=1, source_target_pairs={{0,5},{1,4},{2,7},{3,6},{4,1},{5,0},{6,3},{7,2},{8,13},{9,12},{10,... | collective-permute-start | bytes 2359304 | tf_op jit(solution)/shard_map/ppermute | solution.py:446
  34.5 7.7 %collective-permute-start.14 = (f32[384,128]{1,0:T(8,128)S(1)}, f32[384,128]{1,0:T(8,128)S(1)}, u32[]{:S(2)}, u32[]{:S(2)}) collective-permute-start(f32[384,128]{1,0:T(8,128)S(1)} %get-tuple-element.128.refs_3_), channel_id=1, source_target_pairs={{0,16},{8,24},{16,0},{24,8},{1,17},{9,25},{17,1},{25,9},{2,18},{10... | collective-permute-start | bytes 589832 | tf_op jit(solution)/shard_map/ppermute | solution.py:446
  42.2 37.1 %collective-permute-start.18 = (bf16[256,1536]{1,0:T(8,128)(2,1)}, bf16[256,1536]{1,0:T(8,128)(2,1)S(1)}, u32[]{:S(2)}, u32[]{:S(2)}) collective-permute-start(bf16[256,1536]{1,0:T(8,128)(2,1)} %get-tuple-element.91), channel_id=1, source_target_pairs={{0,1},{1,0},{2,3},{3,2},{4,5},{5,4},{6,7},{7,6},{8,9},{9,8},{10,11... | collective-permute-start | bytes 2359304 | tf_op jit(solution)/shard_map/ppermute | solution.py:446
  42.2 41.0 %collective-permute-start = (bf16[256,1536]{1,0:T(8,128)(2,1)S(1)}, bf16[256,1536]{1,0:T(8,128)(2,1)S(1)}, u32[]{:S(2)}, u32[]{:S(2)}) collective-permute-start(bf16[256,1536]{1,0:T(8,128)(2,1)S(1)} %copy-done.3), channel_id=1, source_target_pairs={{0,2},{1,3},{2,0},{3,1},{4,6},{5,7},{6,4},{7,5},{8,10},{9,11},{10,... | collective-permute-start | bytes 2359304 | tf_op jit(solution)/shard_map/ppermute | solution.py:446
  48.6 21.5 %copy-start.1 = (bf16[1,256,1024]{2,1,0:T(8,128)(2,1)S(1)}, bf16[1,256,1024]{2,1,0:T(8,128)(2,1)}, u32[]{:S(2)}) copy-start(bf16[1,256,1024]{2,1,0:T(8,128)(2,1)} %param.10) | copy-start | bytes 1572868
  48.6 36.6 %collective-permute-start.3 = (bf16[256,1536]{1,0:T(8,128)(2,1)S(1)}, bf16[256,1536]{1,0:T(8,128)(2,1)S(1)}, u32[]{:S(2)}, u32[]{:S(2)}) collective-permute-start(bf16[256,1536]{1,0:T(8,128)(2,1)S(1)} %copy-done.2), channel_id=1, source_target_pairs={{0,4},{1,5},{2,6},{3,7},{4,0},{5,1},{6,2},{7,3},{8,12},{9,13},{10,... | collective-permute-start | bytes 2359304 | tf_op jit(solution)/shard_map/ppermute | solution.py:446
  65.5 8.8 %collective-permute-start.8 = (bf16[256,512]{1,0:T(8,128)(2,1)S(1)}, bf16[256,512]{1,0:T(8,128)(2,1)S(1)}, u32[]{:S(2)}, u32[]{:S(2)}) collective-permute-start(bf16[256,512]{1,0:T(8,128)(2,1)S(1)} %get-tuple-element.81), channel_id=1, source_target_pairs={{0,1},{1,0},{2,3},{3,2},{4,5},{5,4},{6,7},{7,6},{8,9},{9,8},{10,11... | collective-permute-start | bytes 786440 | tf_op jit(solution)/shard_map/ppermute | solution.py:446
  72.3 6.9 %collective-permute-start.13 = (f32[384,128]{1,0:T(8,128)S(1)}, f32[384,128]{1,0:T(8,128)S(1)}, u32[]{:S(2)}, u32[]{:S(2)}) collective-permute-start(f32[384,128]{1,0:T(8,128)S(1)} %get-tuple-element.128.refs_3_), channel_id=1, source_target_pairs={{0,8},{8,0},{16,24},{24,16},{1,9},{9,1},{17,25},{25,17},{2,10},{10... | collective-permute-start | bytes 589832 | tf_op jit(solution)/shard_map/ppermute | solution.py:446
  74.3 14.5 %collective-permute-start.21 = (bf16[256,512]{1,0:T(8,128)(2,1)S(1)}, bf16[256,512]{1,0:T(8,128)(2,1)S(1)}, u32[]{:S(2)}, u32[]{:S(2)}) collective-permute-start(bf16[256,512]{1,0:T(8,128)(2,1)S(1)} %slice.24.refs_4_), channel_id=1, source_target_pairs={{0,6},{1,7},{2,4},{3,5},{4,2},{5,3},{6,0},{7,1},{8,14},{9,15},{10,... | collective-permute-start | bytes 786440 | tf_op jit(solution)/shard_map/ppermute | solution.py:446
  79.3 9.5 %collective-permute-start.2 = (bf16[256,512]{1,0:T(8,128)(2,1)S(1)}, bf16[256,512]{1,0:T(8,128)(2,1)S(1)}, u32[]{:S(2)}, u32[]{:S(2)}) collective-permute-start(bf16[256,512]{1,0:T(8,128)(2,1)S(1)} %get-tuple-element.69), channel_id=1, source_target_pairs={{0,1},{1,0},{2,3},{3,2},{4,5},{5,4},{6,7},{7,6},{8,9},{9,8},{10,11... | collective-permute-start | bytes 786440 | tf_op jit(solution)/shard_map/ppermute | solution.py:446
  79.3 11.0 %collective-permute-start.5 = (bf16[256,512]{1,0:T(8,128)(2,1)S(1)}, bf16[256,512]{1,0:T(8,128)(2,1)S(1)}, u32[]{:S(2)}, u32[]{:S(2)}) collective-permute-start(bf16[256,512]{1,0:T(8,128)(2,1)S(1)} %get-tuple-element.79), channel_id=1, source_target_pairs={{0,1},{1,0},{2,3},{3,2},{4,5},{5,4},{6,7},{7,6},{8,9},{9,8},{10,11... | collective-permute-start | bytes 786440 | tf_op jit(solution)/shard_map/ppermute | solution.py:446
  83.2 13.8 %copy-start = (bf16[256,1536]{1,0:T(8,128)(2,1)S(1)}, bf16[256,1536]{1,0:T(8,128)(2,1)}, u32[]{:S(2)}) copy-start(bf16[256,1536]{1,0:T(8,128)(2,1)} %get-tuple-element.90.refs_0_.refs_1_.refs_2_.refs_3_) | copy-start | bytes 2359300
  83.2 9.5 %collective-permute-start.9 = (bf16[256,512]{1,0:T(8,128)(2,1)S(1)}, bf16[256,512]{1,0:T(8,128)(2,1)S(1)}, u32[]{:S(2)}, u32[]{:S(2)}) collective-permute-start(bf16[256,512]{1,0:T(8,128)(2,1)S(1)} %get-tuple-element.82), channel_id=1, source_target_pairs={{0,6},{1,7},{2,4},{3,5},{4,2},{5,3},{6,0},{7,1},{8,14},{9,15},{10,... | collective-permute-start | bytes 786440 | tf_op jit(solution)/shard_map/ppermute | solution.py:446
  85.2 8.6 %collective-permute-start.20 = (bf16[256,512]{1,0:T(8,128)(2,1)S(1)}, bf16[256,512]{1,0:T(8,128)(2,1)S(1)}, u32[]{:S(2)}, u32[]{:S(2)}) collective-permute-start(bf16[256,512]{1,0:T(8,128)(2,1)S(1)} %slice.24.refs_4_), channel_id=1, source_target_pairs={{0,1},{1,0},{2,3},{3,2},{4,5},{5,4},{6,7},{7,6},{8,9},{9,8},{10,11... | collective-permute-start | bytes 786440 | tf_op jit(solution)/shard_map/ppermute | solution.py:446
  88.8 6.7 %collective-permute-start.19 = (bf16[256,512]{1,0:T(8,128)(2,1)S(1)}, bf16[256,512]{1,0:T(8,128)(2,1)S(1)}, u32[]{:S(2)}, u32[]{:S(2)}) collective-permute-start(bf16[256,512]{1,0:T(8,128)(2,1)S(1)} %get-tuple-element.92), channel_id=1, source_target_pairs={{0,1},{1,0},{2,3},{3,2},{4,5},{5,4},{6,7},{7,6},{8,9},{9,8},{10,11... | collective-permute-start | bytes 786440 | tf_op jit(solution)/shard_map/ppermute | solution.py:446
  88.8 9.5 %collective-permute-start.26 = (bf16[256,512]{1,0:T(8,128)(2,1)S(1)}, bf16[256,512]{1,0:T(8,128)(2,1)S(1)}, u32[]{:S(2)}, u32[]{:S(2)}) collective-permute-start(bf16[256,512]{1,0:T(8,128)(2,1)S(1)} %slice.24.refs_4_), channel_id=1, source_target_pairs={{0,4},{1,5},{2,6},{3,7},{4,0},{5,1},{6,2},{7,3},{8,12},{9,13},{10,... | collective-permute-start | bytes 786440 | tf_op jit(solution)/shard_map/ppermute | solution.py:446
  90.3 9.1 %collective-permute-start.24 = (bf16[256,512]{1,0:T(8,128)(2,1)S(1)}, bf16[256,512]{1,0:T(8,128)(2,1)S(1)}, u32[]{:S(2)}, u32[]{:S(2)}) collective-permute-start(bf16[256,512]{1,0:T(8,128)(2,1)S(1)} %slice.24.refs_4_), channel_id=1, source_target_pairs={{0,2},{1,3},{2,0},{3,1},{4,6},{5,7},{6,4},{7,5},{8,10},{9,11},{10,... | collective-permute-start | bytes 786440 | tf_op jit(solution)/shard_map/ppermute | solution.py:446
  92.7 6.7 %collective-permute-start.22 = (bf16[256,512]{1,0:T(8,128)(2,1)S(1)}, bf16[256,512]{1,0:T(8,128)(2,1)S(1)}, u32[]{:S(2)}, u32[]{:S(2)}) collective-permute-start(bf16[256,512]{1,0:T(8,128)(2,1)S(1)} %collective-permute-done.21.refs_6_), channel_id=1, source_target_pairs={{0,1},{1,0},{2,3},{3,2},{4,5},{5,4},{6,7},{7,6},{8,9},{9,8},{10,11... | collective-permute-start | bytes 786440 | tf_op jit(solution)/shard_map/ppermute | solution.py:446
  93.9 10.5 %collective-permute-start.16 = (bf16[256,512]{1,0:T(8,128)(2,1)S(1)}, bf16[256,512]{1,0:T(8,128)(2,1)S(1)}, u32[]{:S(2)}, u32[]{:S(2)}) collective-permute-start(bf16[256,512]{1,0:T(8,128)(2,1)S(1)} %get-tuple-element.88), channel_id=1, source_target_pairs={{0,2},{1,3},{2,0},{3,1},{4,6},{5,7},{6,4},{7,5},{8,10},{9,11},{10,... | collective-permute-start | bytes 786440 | tf_op jit(solution)/shard_map/ppermute | solution.py:446
  95.4 8.9 %collective-permute-start.17 = (bf16[256,512]{1,0:T(8,128)(2,1)S(1)}, bf16[256,512]{1,0:T(8,128)(2,1)S(1)}, u32[]{:S(2)}, u32[]{:S(2)}) collective-permute-start(bf16[256,512]{1,0:T(8,128)(2,1)S(1)} %get-tuple-element.89), channel_id=1, source_target_pairs={{0,4},{1,5},{2,6},{3,7},{4,0},{5,1},{6,2},{7,3},{8,12},{9,13},{10,... | collective-permute-start | bytes 786440 | tf_op jit(solution)/shard_map/ppermute | solution.py:446
  97.0 44.4 %slice-start.4 = ((s8[6291456]{0:T(1024)(128)(4,1)}), s8[4194304]{0:T(1024)(128)(4,1)S(1)}, s32[]{:S(2)}) async-start(s8[6291456]{0:T(1024)(128)(4,1)} %bitcast.56), calls=%async_computation.4 | async-start | bytes 8388608
  98.2 10.2 %collective-permute-start.27 = (bf16[256,512]{1,0:T(8,128)(2,1)S(1)}, bf16[256,512]{1,0:T(8,128)(2,1)S(1)}, u32[]{:S(2)}, u32[]{:S(2)}) collective-permute-start(bf16[256,512]{1,0:T(8,128)(2,1)S(1)} %collective-permute-done.26.refs_6_), channel_id=1, source_target_pairs={{0,1},{1,0},{2,3},{3,2},{4,5},{5,4},{6,7},{7,6},{8,9},{9,8},{10,11... | collective-permute-start | bytes 786440 | tf_op jit(solution)/shard_map/ppermute | solution.py:446
  99.4 9.0 %collective-permute-start.25 = (bf16[256,512]{1,0:T(8,128)(2,1)S(1)}, bf16[256,512]{1,0:T(8,128)(2,1)S(1)}, u32[]{:S(2)}, u32[]{:S(2)}) collective-permute-start(bf16[256,512]{1,0:T(8,128)(2,1)S(1)} %collective-permute-done.24.refs_4_), channel_id=1, source_target_pairs={{0,1},{1,0},{2,3},{3,2},{4,5},{5,4},{6,7},{7,6},{8,9},{9,8},{10,11... | collective-permute-start | bytes 786440 | tf_op jit(solution)/shard_map/ppermute | solution.py:446
  104.9 10.3 %collective-permute-start.32 = (bf16[256,512]{1,0:T(8,128)(2,1)S(1)}, bf16[256,512]{1,0:T(8,128)(2,1)S(1)}, u32[]{:S(2)}, u32[]{:S(2)}) collective-permute-start(bf16[256,512]{1,0:T(8,128)(2,1)S(1)} %key_backward.1.refs_4_), channel_id=1, source_target_pairs={{0,6},{1,7},{2,4},{3,5},{4,2},{5,3},{6,0},{7,1},{8,14},{9,15},{10,... | collective-permute-start | bytes 786440 | tf_op jit(solution)/shard_map/ppermute | solution.py:446
  106.9 12.2 %collective-permute-start.29 = (bf16[256,512]{1,0:T(8,128)(2,1)S(1)}, bf16[256,512]{1,0:T(8,128)(2,1)S(1)}, u32[]{:S(2)}, u32[]{:S(2)}) collective-permute-start(bf16[256,512]{1,0:T(8,128)(2,1)S(1)} %key_backward.1.refs_4_), channel_id=1, source_target_pairs={{0,4},{1,5},{2,6},{3,7},{4,0},{5,1},{6,2},{7,3},{8,12},{9,13},{10,... | collective-permute-start | bytes 786440 | tf_op jit(solution)/shard_map/ppermute | solution.py:446
  107.9 11.2 %collective-permute-start.23 = (bf16[256,512]{1,0:T(8,128)(2,1)S(1)}, bf16[256,512]{1,0:T(8,128)(2,1)S(1)}, u32[]{:S(2)}, u32[]{:S(2)}) collective-permute-start(bf16[256,512]{1,0:T(8,128)(2,1)S(1)} %key_backward.1.refs_4_), channel_id=1, source_target_pairs={{0,2},{1,3},{2,0},{3,1},{4,6},{5,7},{6,4},{7,5},{8,10},{9,11},{10,... | collective-permute-start | bytes 786440 | tf_op jit(solution)/shard_map/ppermute | solution.py:446
  108.5 32.9 %slice-start.5 = ((s8[6291456]{0:T(1024)(128)(4,1)}), s8[2097152]{0:T(1024)(128)(4,1)S(1)}, s32[]{:S(2)}) async-start(s8[6291456]{0:T(1024)(128)(4,1)} %bitcast.56), calls=%async_computation.5 | async-start | bytes 4194304
  113.3 6.3 %collective-permute-start.31 = (bf16[256,512]{1,0:T(8,128)(2,1)S(1)}, bf16[256,512]{1,0:T(8,128)(2,1)S(1)}, u32[]{:S(2)}, u32[]{:S(2)}) collective-permute-start(bf16[256,512]{1,0:T(8,128)(2,1)S(1)} %key_backward.1.refs_4_), channel_id=1, source_target_pairs={{0,1},{1,0},{2,3},{3,2},{4,5},{5,4},{6,7},{7,6},{8,9},{9,8},{10,11... | collective-permute-start | bytes 786440 | tf_op jit(solution)/shard_map/ppermute | solution.py:446
  115.1 4.5 %collective-permute-start.33 = (bf16[256,512]{1,0:T(8,128)(2,1)S(1)}, bf16[256,512]{1,0:T(8,128)(2,1)S(1)}, u32[]{:S(2)}, u32[]{:S(2)}) collective-permute-start(bf16[256,512]{1,0:T(8,128)(2,1)S(1)} %collective-permute-done.32.refs_6_), channel_id=1, source_target_pairs={{0,1},{1,0},{2,3},{3,2},{4,5},{5,4},{6,7},{7,6},{8,9},{9,8},{10,11... | collective-permute-start | bytes 786440 | tf_op jit(solution)/shard_map/ppermute | solution.py:446
  119.1 3.7 %collective-permute-start.30 = (bf16[256,512]{1,0:T(8,128)(2,1)S(1)}, bf16[256,512]{1,0:T(8,128)(2,1)S(1)}, u32[]{:S(2)}, u32[]{:S(2)}) collective-permute-start(bf16[256,512]{1,0:T(8,128)(2,1)S(1)} %collective-permute-done.29.refs_6_), channel_id=1, source_target_pairs={{0,1},{1,0},{2,3},{3,2},{4,5},{5,4},{6,7},{7,6},{8,9},{9,8},{10,11... | collective-permute-start | bytes 786440 | tf_op jit(solution)/shard_map/ppermute | solution.py:446
  119.1 3.7 %collective-permute-start.28 = (bf16[256,512]{1,0:T(8,128)(2,1)S(1)}, bf16[256,512]{1,0:T(8,128)(2,1)S(1)}, u32[]{:S(2)}, u32[]{:S(2)}) collective-permute-start(bf16[256,512]{1,0:T(8,128)(2,1)S(1)} %collective-permute-done.23.refs_4_), channel_id=1, source_target_pairs={{0,1},{1,0},{2,3},{3,2},{4,5},{5,4},{6,7},{7,6},{8,9},{9,8},{10,11... | collective-permute-start | bytes 786440 | tf_op jit(solution)/shard_map/ppermute | solution.py:446
  119.6 21.7 %slice-start = ((s8[6291456]{0:T(1024)(128)(4,1)}), s8[4194304]{0:T(1024)(128)(4,1)S(1)}, s32[]{:S(2)}) async-start(s8[6291456]{0:T(1024)(128)(4,1)} %bitcast.40), calls=%async_computation | async-start | bytes 8388608
  119.6 21.7 %slice-start.2 = ((s8[6291456]{0:T(1024)(128)(4,1)}), s8[4194304]{0:T(1024)(128)(4,1)S(1)}, s32[]{:S(2)}) async-start(s8[6291456]{0:T(1024)(128)(4,1)} %bitcast.48), calls=%async_computation.2 | async-start | bytes 8388608
  122.8 18.5 %slice-start.1 = ((s8[6291456]{0:T(1024)(128)(4,1)}), s8[2097152]{0:T(1024)(128)(4,1)S(1)}, s32[]{:S(2)}) async-start(s8[6291456]{0:T(1024)(128)(4,1)} %bitcast.40), calls=%async_computation.1 | async-start | bytes 4194304
  122.9 18.5 %slice-start.3 = ((s8[6291456]{0:T(1024)(128)(4,1)}), s8[2097152]{0:T(1024)(128)(4,1)S(1)}, s32[]{:S(2)}) async-start(s8[6291456]{0:T(1024)(128)(4,1)} %bitcast.48), calls=%async_computation.3 | async-start | bytes 4194304
  127.7 1.2 collective-permute-start.34
  128.9 4.5 %collective-permute-start.37 = (f32[8,128]{1,0:T(8,128)S(1)}, f32[8,128]{1,0:T(8,128)S(1)}, u32[]{:S(2)}, u32[]{:S(2)}) collective-permute-start(f32[8,128]{1,0:T(8,128)S(1)} %add.32.refs_0_), channel_id=1, source_target_pairs={{0,6},{1,7},{2,4},{3,5},{4,2},{5,3},{6,0},{7,1},{8,14},{9,15},{10,... | collective-permute-start | bytes 12296 | tf_op jit(solution)/shard_map/ppermute | solution.py:446
  130.6 3.6 %collective-permute-start.36 = (f32[8,128]{1,0:T(8,128)S(1)}, f32[8,128]{1,0:T(8,128)S(1)}, u32[]{:S(2)}, u32[]{:S(2)}) collective-permute-start(f32[8,128]{1,0:T(8,128)S(1)} %add.32.refs_0_), channel_id=1, source_target_pairs={{0,4},{1,5},{2,6},{3,7},{4,0},{5,1},{6,2},{7,3},{8,12},{9,13},{10,... | collective-permute-start | bytes 12296 | tf_op jit(solution)/shard_map/ppermute | solution.py:446
  131.7 3.6 %collective-permute-start.35 = (f32[8,128]{1,0:T(8,128)S(1)}, f32[8,128]{1,0:T(8,128)S(1)}, u32[]{:S(2)}, u32[]{:S(2)}) collective-permute-start(f32[8,128]{1,0:T(8,128)S(1)} %add.32.refs_0_), channel_id=1, source_target_pairs={{0,2},{1,3},{2,0},{3,1},{4,6},{5,7},{6,4},{7,5},{8,10},{9,11},{10,... | collective-permute-start | bytes 12296 | tf_op jit(solution)/shard_map/ppermute | solution.py:446
  136.9 11.8 %collective-permute-start.38 = (bf16[384,128]{1,0:T(8,128)(2,1)S(1)}, bf16[384,128]{1,0:T(8,128)(2,1)S(1)}, u32[]{:S(2)}, u32[]{:S(2)}) collective-permute-start(bf16[384,128]{1,0:T(8,128)(2,1)S(1)} %get-tuple-element.116), channel_id=1, source_target_pairs={{0,8},{8,0},{16,24},{24,16},{1,9},{9,1},{17,25},{25,17},{2,10},{10... | collective-permute-start | bytes 294920 | tf_op jit(solution)/shard_map/ppermute | solution.py:446
  138.5 10.2 %collective-permute-start.39 = (bf16[384,128]{1,0:T(8,128)(2,1)S(1)}, bf16[384,128]{1,0:T(8,128)(2,1)S(1)}, u32[]{:S(2)}, u32[]{:S(2)}) collective-permute-start(bf16[384,128]{1,0:T(8,128)(2,1)S(1)} %get-tuple-element.117), channel_id=1, source_target_pairs={{0,16},{8,24},{16,0},{24,8},{1,17},{9,25},{17,1},{25,9},{2,18},{10... | collective-permute-start | bytes 294920 | tf_op jit(solution)/shard_map/ppermute | solution.py:446
  140.2 8.6 %collective-permute-start.40 = (bf16[384,128]{1,0:T(8,128)(2,1)S(1)}, bf16[384,128]{1,0:T(8,128)(2,1)S(1)}, u32[]{:S(2)}, u32[]{:S(2)}) collective-permute-start(bf16[384,128]{1,0:T(8,128)(2,1)S(1)} %get-tuple-element.118), channel_id=1, source_target_pairs={{0,24},{8,16},{16,8},{24,0},{1,25},{9,17},{17,9},{25,1},{2,26},{10... | collective-permute-start | bytes 294920 | tf_op jit(solution)/shard_map/ppermute | solution.py:446
  148.8 11.7 %collective-permute-start.43 = (bf16[384,128]{1,0:T(8,128)(2,1)S(1)}, bf16[384,128]{1,0:T(8,128)(2,1)S(1)}, u32[]{:S(2)}, u32[]{:S(2)}) collective-permute-start(bf16[384,128]{1,0:T(8,128)(2,1)S(1)} %convert_element_type.24.refs_7_), channel_id=1, source_target_pairs={{0,24},{8,16},{16,8},{24,0},{1,25},{9,17},{17,9},{25,1},{2,26},{10... | collective-permute-start | bytes 294920 | tf_op jit(solution)/shard_map/ppermute | solution.py:446
  151.5 9.0 %collective-permute-start.42 = (bf16[384,128]{1,0:T(8,128)(2,1)S(1)}, bf16[384,128]{1,0:T(8,128)(2,1)S(1)}, u32[]{:S(2)}, u32[]{:S(2)}) collective-permute-start(bf16[384,128]{1,0:T(8,128)(2,1)S(1)} %convert_element_type.24.refs_7_), channel_id=1, source_target_pairs={{0,16},{8,24},{16,0},{24,8},{1,17},{9,25},{17,1},{25,9},{2,18},{10... | collective-permute-start | bytes 294920 | tf_op jit(solution)/shard_map/ppermute | solution.py:446
  151.5 9.0 %collective-permute-start.41 = (bf16[384,128]{1,0:T(8,128)(2,1)S(1)}, bf16[384,128]{1,0:T(8,128)(2,1)S(1)}, u32[]{:S(2)}, u32[]{:S(2)}) collective-permute-start(bf16[384,128]{1,0:T(8,128)(2,1)S(1)} %convert_element_type.24.refs_7_), channel_id=1, source_target_pairs={{0,8},{8,0},{16,24},{24,16},{1,9},{9,1},{17,25},{25,17},{2,10},{10... | collective-permute-start | bytes 294920 | tf_op jit(solution)/shard_map/ppermute | solution.py:446

commit v13 on v12

--- a/solution.py
+++ b/solution.py
@@ -24,6 +24,7 @@
 MIX_LOCAL = 0.5
 
 MIB = 1 << 20
+ADAM_ROWS = 128
 
 
 def in_hbm(*arrays):
@@ -220,7 +221,7 @@
         specs += [fixed, row_block(FRAG_COLS)]
     if last:
         shapes = [
-            pltpu.HBM((rows, width), jnp.float32),
+            jax.ShapeDtypeStruct((rows, width), jnp.float32),
             jax.ShapeDtypeStruct((8, HEAD), jnp.float32),
             jax.ShapeDtypeStruct((rows, FRAG_COLS), jnp.float32),
         ]
@@ -235,7 +236,7 @@
         grid_spec=pltpu.PrefetchScalarGridSpec(
             num_scalar_prefetch=1, grid=(rows // step,), in_specs=specs, out_specs=outs
         ),
-        compiler_params=params_of(20),
+        compiler_params=params_of(12),
         cost_estimate=cost(2 * rows * width * depth, 2 * rows * depth + 4 * rows * width),
         name="gradient",
     )(place, *args)
@@ -275,7 +276,7 @@
 
 def adam_rows(scalars, squares, state, first, last, into=()):
     rows, width = state[0].shape
-    step = 256
+    step = ADAM_ROWS
     full = pl.BlockSpec((step, width), lambda i: (i + first, 0))
     half = pl.BlockSpec((step, width // 2), lambda i: (i + first, 0))
     shapes = [pltpu.HBM((rows, width), jnp.float32)] * 3
@@ -293,10 +294,10 @@
         + [pl.BlockSpec(memory_space=pl.ANY)] * len(into),
         out_specs=outs,
         input_output_aliases={6 + len(squares) + i: i for i in range(len(into))},
-        compiler_params=params_of(24),
+        compiler_params=params_of(12),
         cost_estimate=cost(20 * count * width, 28 * count * width),
         name="adam_rows",
-    )(scalars, *state[:3], *in_hbm(*state[3:]), *squares, *in_hbm(*into))
+    )(scalars, *state, *squares, *in_hbm(*into))
 
 
 def frag_kernel(squares, place_ref, sc_ref, w_ref, m_ref, v_ref, g_ref, *refs):
@@ -475,14 +476,14 @@
     order = [k for k in far[:-2] for k in (k, k + 1)]
     order += far[-2:] + [k + 1 for k in far[-2:]]
 
-    (old,) = due_columns(place, part, params)
-    old_sums = [old[0]] + [swap(old[k], "rep", k) for k in range(1, replicas)]
-
     packed = {}
     for offsets in (order[:1], order[1:4], order[4:], (0, 1)):
         packed |= pack(inputs, me, rows, tuple(offsets))
     blocks = {k: swap(packed[k], "fsdp", k) for k in order}
     blocks[0], blocks[1] = packed[0], swap(packed[1], "fsdp", 1)
+
+    (old,) = due_columns(after(place, blocks[order[0]]), part, params)
+    old_sums = [old[0]] + [swap(old[k], "rep", k) for k in range(1, replicas)]
 
     values = {0: incoming[:, kv_width:]}
     for i, k in enumerate(far):
@@ -543,7 +544,7 @@
 
     state = (params, first_moment[0], second_moment[0], grad_keys, grad_values)
     inner, *update = adam_frag(place, scalars, squares, old, old_first, old_second, due)
-    steps = rows // 256
+    steps = rows // ADAM_ROWS
     *results, ticket = adam_rows(scalars, squares, state, 0, steps // 2)
     own_sum = update[0].astype(jnp.float32)
     for k in range(1, replicas):

time: 165 us -> 169 us (1.024)
  waiting for transfers between devices: 50.4 us -> 55.8 us
  Pallas kernels: 60.7 us -> 58 us
    ppermute x44, waiting for transfers between devices: 50.4 us -> 55.8 us  [swap(): return lax.ppermute(block, axis, [(i, i ^ offset) for i in range(count)])]
    pallas_call x2, Pallas kernels: 14.6 us -> 12 us  [adam_rows(): pl.pallas_call(functools.partial(adam_kernel, len(squares), len(into)), o...]
    pallas_call x4, Pallas kernels: 16 us -> 13.5 us  [gradient(): pl.pallas_call(functools.partial(grad_kernel, len(flipped), base is not N...]
    pallas_call x8, Pallas kernels: 4.66 us -> 7.02 us  [partial_keys(): pl.pallas_call(functools.partial(partial_kernel, pieces), out_shape=[jax....]
  transfers between devices with their start and end apart: 44 -> 44, of which waited for: 18 -> 14; matrix products, arithmetic and copies ran while one was open for 0% -> 1% of each run, Pallas kernels for 31% -> 29%
where the time goes in v13:
time: 169 us
  Pallas kernels  58 us (34%)
  waiting for transfers between devices  55.8 us (33%)
  starting transfers between devices  49.7 us (29%)
  between operations  3.75 us (2%)
    ppermute x44, waiting for transfers between devices, swap(): return lax.ppermute(block, axis, [(i, i ^ offset) for i in range(count)])  55.8 us
    ppermute x44, starting transfers between devices, swap(): return lax.ppermute(block, axis, [(i, i ^ offset) for i in range(count)])  49.7 us
    pallas_call x4, Pallas kernels, gradient(): pl.pallas_call(functools.partial(grad_kernel, len(flipped), base is not N...  13.5 us
    pallas_call x2, Pallas kernels, adam_rows(): pl.pallas_call(functools.partial(adam_kernel, len(squares), len(into)), o...  12 us
    pallas_call x4, Pallas kernels, pack(): pl.pallas_call(functools.partial(pack_kernel, offsets), out_shape=[pltpu....  9.22 us
    pallas_call x8, Pallas kernels, partial_keys(): pl.pallas_call(functools.partial(partial_kernel, pieces), out_shape=[jax....  7.02 us
    pallas_call x3, Pallas kernels, due_columns(): pl.pallas_call(functools.partial(pick_kernel, blocks), out_shape=[jax.Sha...  5.56 us
    pallas_call x1, Pallas kernels, cast_left(): pl.pallas_call(cast_kernel, out_shape=jax.ShapeDtypeStruct((rows, width),...  3.47 us
  transfers between devices with their start and end apart: 44, of which 14 were waited for; matrix products, arithmetic and copies ran while one was open for 1% of the time, Pallas kernels for 29%

profile of v13, /device:TPU:0, one launch (start us, length us, event | category | flops | bytes accessed | tf_op | source)
XLA Modules:
  0.0 168.7 jit_solution(2344561784509170438)
XLA Ops:
  0.6 2.0 %pack.6 = bf16[256,1536]{1,0:T(8,128)(2,1)} custom-call(s32[1]{0:T(128)} %bitcast.4.me_ref, bf16[256,12288]{1,0:T(8,128)(2,1)} %bitcast.64), custom_call_target="tpu_custom_call" | custom-call | bytes 1572864 | tf_op jit(solution)/shard_map/pack/pallas_call | solution.py:69
  2.6 4.0 %collective-permute-start.6 = (bf16[256,1536]{1,0:T(8,128)(2,1)}, bf16[256,1536]{1,0:T(8,128)(2,1)S(1)}, u32[]{:S(2)}, u32[]{:S(2)}) collective-permute-start(bf16[256,1536]{1,0:T(8,128)(2,1)} %pack.6), channel_id=1, source_target_pairs={{0,6},{1,7},{2,4},{3,5},{4,2},{5,3},{6,0},{7,1},{8,14},{9,15},{10,... | collective-permute-start | bytes 2359304 | tf_op jit(solution)/shard_map/ppermute | solution.py:447
  6.6 2.3 %pack.7 = (bf16[256,1536]{1,0:T(8,128)(2,1)}, bf16[256,1536]{1,0:T(8,128)(2,1)}) custom-call(s32[1]{0:T(128)} %bitcast.4.me_ref, bf16[256,12288]{1,0:T(8,128)(2,1)} %bitcast.65), custom_call_target="tpu_custom_call" | custom-call | bytes 3145728 | tf_op jit(solution)/shard_map/pack/pallas_call | solution.py:69
  8.9 2.3 %pack.5 = (bf16[256,1536]{1,0:T(8,128)(2,1)}, bf16[256,1536]{1,0:T(8,128)(2,1)}) custom-call(s32[1]{0:T(128)} %bitcast.4.me_ref, bf16[256,12288]{1,0:T(8,128)(2,1)} %bitcast.66), custom_call_target="tpu_custom_call" | custom-call | bytes 3145728 | tf_op jit(solution)/shard_map/pack/pallas_call | solution.py:69
  11.3 0.7 collective-permute-start.1
  12.1 2.6 %pack.4 = (bf16[256,1536]{1,0:T(8,128)(2,1)}, bf16[256,1536]{1,0:T(8,128)(2,1)}, bf16[256,1536]{1,0:T(8,128)(2,1)}) custom-call(s32[1]{0:T(128)} %bitcast.4.me_ref, bf16[256,12288]{1,0:T(8,128)(2,1)} %bitcast.67), custom_call_target="tpu_custom_call" | custom-call | bytes 4718592 | tf_op jit(solution)/shard_map/pack/pallas_call | solution.py:69
  14.7 2.7 %collective-permute-start.7 = (bf16[256,1536]{1,0:T(8,128)(2,1)}, bf16[256,1536]{1,0:T(8,128)(2,1)}, u32[]{:S(2)}, u32[]{:S(2)}) collective-permute-start(bf16[256,1536]{1,0:T(8,128)(2,1)} %get-tuple-element.81), channel_id=1, source_target_pairs={{0,7},{1,6},{2,5},{3,4},{4,3},{5,2},{6,1},{7,0},{8,15},{9,14},{10,... | collective-permute-start | bytes 2359304 | tf_op jit(solution)/shard_map/ppermute | solution.py:447
  17.4 7.8 %collective-permute-done.6.refs_0_.refs_1_.refs_2_.refs_3_ = bf16[256,1536]{1,0:T(8,128)(2,1)S(1)} collective-permute-done((bf16[256,1536]{1,0:T(8,128)(2,1)}, bf16[256,1536]{1,0:T(8,128)(2,1)S(1)}, u32[]{:S(2)}, u32[]{:S(2)}) %collective-permute-start.6) | collective-permute-done | bytes 786464 | tf_op jit(solution)/shard_map/ppermute | solution.py:447
  25.2 2.0 %collective-permute-start = (bf16[256,1536]{1,0:T(8,128)(2,1)}, bf16[256,1536]{1,0:T(8,128)(2,1)S(1)}, u32[]{:S(2)}, u32[]{:S(2)}) collective-permute-start(bf16[256,1536]{1,0:T(8,128)(2,1)} %get-tuple-element.68), channel_id=1, source_target_pairs={{0,2},{1,3},{2,0},{3,1},{4,6},{5,7},{6,4},{7,5},{8,10},{9,11},{10,... | collective-permute-start | bytes 2359304 | tf_op jit(solution)/shard_map/ppermute | solution.py:447
  27.9 1.6 collective-permute-start.3
  30.4 1.0 slice.24.refs_4_
  31.4 2.8 %duplicate.1 = (f32[384,1024]{1,0:T(8,128)}, f32[384,1024]{1,0:T(8,128)}) custom-call(f32[384,1024]{1,0:T(8,128)} %refs_0_.3, f32[384,1024]{1,0:T(8,128)} %refs_1_.3), custom_call_target="tpu_custom_call" | custom-call | bytes 6291456 | tf_op jit(solution)/shard_map/duplicate/pallas_call | solution.py:386
  34.2 1.6 due_columns.4
  35.8 3.5 %cast_left.1.refs_4_ = bf16[1536,512]{1,0:T(8,128)(2,1)S(1)} custom-call(f32[1536,1024]{1,0:T(8,128)} %bitcast.35), custom_call_target="tpu_custom_call" | custom-call | bytes 4718592 | tf_op jit(solution)/shard_map/cast_left/pallas_call | solution.py:93
  39.3 2.1 %due_columns.3 = (f32[4,384,128]{2,1,0:T(8,128)S(1)}, f32[4,384,128]{2,1,0:T(8,128)S(1)}) custom-call(s32[2]{0:T(128)S(1)} %pad_add_fusion.place_ref, f32[1536,1024]{1,0:T(8,128)} %bitcast.44, f32[1536,1024]{1,0:T(8,128)} %bitcast.45, f32[1536,1024]{1,0:T(8,128)} %bitcast.46, f32[1536,1024]{1,0:T(8,128)} %bitcast.47, f32[1536,1024]{1,0:T(8,128)} %bitcast.52, ...), custom_call_target="tpu_custom_call" | custom-call | bytes 3145728 | tf_op jit(solution)/shard_map/due_columns/pallas_call | solution.py:345
  41.4 1.8 %due_columns.5.w_ref = f32[4,384,128]{2,1,0:T(8,128)S(1)} custom-call(s32[2]{0:T(128)S(1)} %pad_add_fusion.place_ref, f32[1536,1024]{1,0:T(8,128)} %bitcast.36, f32[1536,1024]{1,0:T(8,128)} %bitcast.37, f32[1536,1024]{1,0:T(8,128)} %bitcast.38, f32[1536,1024]{1,0:T(8,128)} %bitcast.39), custom_call_target="tpu_custom_call" | custom-call | bytes 1572864 | tf_op jit(solution)/shard_map/due_columns/pallas_call | solution.py:345
  43.3 1.6 collective-permute-start.10
  44.9 2.5 %collective-permute-start.12 = (f32[384,128]{1,0:T(8,128)S(1)}, f32[384,128]{1,0:T(8,128)S(1)}, u32[]{:S(2)}, u32[]{:S(2)}) collective-permute-start(f32[384,128]{1,0:T(8,128)S(1)} %get-tuple-element.133), channel_id=1, source_target_pairs={{0,24},{8,16},{16,8},{24,0},{1,25},{9,17},{17,9},{25,1},{2,26},{10... | collective-permute-start | bytes 589832 | tf_op jit(solution)/shard_map/ppermute | solution.py:447
  47.4 11.2 %collective-permute-done.7.refs_0_.refs_1_.refs_2_.refs_3_ = bf16[256,1536]{1,0:T(8,128)(2,1)} collective-permute-done((bf16[256,1536]{1,0:T(8,128)(2,1)}, bf16[256,1536]{1,0:T(8,128)(2,1)}, u32[]{:S(2)}, u32[]{:S(2)}) %collective-permute-start.7) | collective-permute-done | bytes 786464 | tf_op jit(solution)/shard_map/ppermute | solution.py:447
  58.6 2.6 %collective-permute-start.11 = (f32[384,128]{1,0:T(8,128)S(1)}, f32[384,128]{1,0:T(8,128)S(1)}, u32[]{:S(2)}, u32[]{:S(2)}) collective-permute-start(f32[384,128]{1,0:T(8,128)S(1)} %get-tuple-element.134), channel_id=1, source_target_pairs={{0,16},{8,24},{16,0},{24,8},{1,17},{9,25},{17,1},{25,9},{2,18},{10... | collective-permute-start | bytes 589832 | tf_op jit(solution)/shard_map/ppermute | solution.py:447
  61.3 1.8 %partial_keys.10 = (bf16[256,512]{1,0:T(8,128)(2,1)S(1)}, bf16[1536,256]{1,0:T(8,128)(2,1)S(1)}) custom-call(bf16[256,1536]{1,0:T(8,128)(2,1)} %collective-permute-done.4.refs_0_.refs_1_.refs_2_.refs_3_, bf16[256,1536]{1,0:T(8,128)(2,1)} %collective-permute-done.4.refs_0_.refs_1_.refs_2_.refs_3_, ...), custom_call_target="tpu_custom_call" | custom-call | flops 402653184 | bytes 1572864 | tf_op jit(solution)/shard_map/partial_keys/pallas_call | solution.py:122
  63.1 0.6 partial_keys.8
  63.7 1.8 %partial_keys.11 = (bf16[256,512]{1,0:T(8,128)(2,1)S(1)}, bf16[1536,256]{1,0:T(8,128)(2,1)S(1)}) custom-call(bf16[256,1536]{1,0:T(8,128)(2,1)} %collective-permute-done.7.refs_0_.refs_1_.refs_2_.refs_3_, bf16[256,1536]{1,0:T(8,128)(2,1)} %collective-permute-done.7.refs_0_.refs_1_.refs_2_.refs_3_, ...), custom_call_target="tpu_custom_call" | custom-call | flops 402653184 | bytes 1572864 | tf_op jit(solution)/shard_map/partial_keys/pallas_call | solution.py:122
  65.5 9.7 %collective-permute-done.refs_0_.refs_1_.refs_2_.refs_3_ = bf16[256,1536]{1,0:T(8,128)(2,1)S(1)} collective-permute-done((bf16[256,1536]{1,0:T(8,128)(2,1)}, bf16[256,1536]{1,0:T(8,128)(2,1)S(1)}, u32[]{:S(2)}, u32[]{:S(2)}) %collective-permute-start) | collective-permute-done | bytes 786464 | tf_op jit(solution)/shard_map/ppermute | solution.py:447
  75.2 1.4 collective-permute-start.21
  77.4 1.2 collective-permute-done.8.refs_5_
  78.6 3.6 %collective-permute-start.15 = (f32[384,128]{1,0:T(8,128)S(1)}, f32[384,128]{1,0:T(8,128)S(1)}, u32[]{:S(2)}, u32[]{:S(2)}) collective-permute-start(f32[384,128]{1,0:T(8,128)S(1)} %get-tuple-element.130.refs_3_), channel_id=1, source_target_pairs={{0,24},{8,16},{16,8},{24,0},{1,25},{9,17},{17,9},{25,1},{2,26},{10... | collective-permute-start | bytes 589832 | tf_op jit(solution)/shard_map/ppermute | solution.py:447
  82.2 0.6 partial_keys.12
  82.8 1.6 collective-permute-start.9
  84.3 1.7 %collective-permute-start.14 = (f32[384,128]{1,0:T(8,128)S(1)}, f32[384,128]{1,0:T(8,128)S(1)}, u32[]{:S(2)}, u32[]{:S(2)}) collective-permute-start(f32[384,128]{1,0:T(8,128)S(1)} %get-tuple-element.130.refs_3_), channel_id=1, source_target_pairs={{0,16},{8,24},{16,0},{24,8},{1,17},{9,25},{17,1},{25,9},{2,18},{10... | collective-permute-start | bytes 589832 | tf_op jit(solution)/shard_map/ppermute | solution.py:447
  86.1 1.7 %collective-permute-start.13 = (f32[384,128]{1,0:T(8,128)S(1)}, f32[384,128]{1,0:T(8,128)S(1)}, u32[]{:S(2)}, u32[]{:S(2)}) collective-permute-start(f32[384,128]{1,0:T(8,128)S(1)} %get-tuple-element.130.refs_3_), channel_id=1, source_target_pairs={{0,8},{8,0},{16,24},{24,16},{1,9},{9,1},{17,25},{25,17},{2,10},{10... | collective-permute-start | bytes 589832 | tf_op jit(solution)/shard_map/ppermute | solution.py:447
  87.8 0.6 partial_keys.14
  89.0 10.2 %collective-permute-done.14.refs_5_ = f32[384,128]{1,0:T(8,128)S(1)} collective-permute-done((f32[384,128]{1,0:T(8,128)S(1)}, f32[384,128]{1,0:T(8,128)S(1)}, u32[]{:S(2)}, u32[]{:S(2)}) %collective-permute-start.14) | collective-permute-done | bytes 196640 | tf_op jit(solution)/shard_map/ppermute | solution.py:447
  99.2 1.5 collective-permute-start.26
  101.2 0.6 partial_keys.9
  101.8 0.6 partial_keys.13
  102.4 1.6 collective-permute-start.16
  104.5 0.6 partial_keys.15
  105.1 1.6 collective-permute-done.26.refs_6_
  106.7 3.2 %collective-permute-done.24.refs_4_ = bf16[256,512]{1,0:T(8,128)(2,1)S(1)} collective-permute-done((bf16[256,512]{1,0:T(8,128)(2,1)S(1)}, bf16[256,512]{1,0:T(8,128)(2,1)S(1)}, u32[]{:S(2)}, u32[]{:S(2)}) %collective-permute-start.24) | collective-permute-done | bytes 262176 | tf_op jit(solution)/shard_map/ppermute | solution.py:447
  109.9 3.2 %gradient.4.refs_8_ = f32[1536,512]{1,0:T(8,128)S(1)} custom-call(s32[2]{0:T(128)S(1)} %pad_add_fusion.place_ref, bf16[1536,256]{1,0:T(8,128)(2,1)S(1)} %get-tuple-element.96.refs_0_, bf16[1536,256]{1,0:T(8,128)(2,1)S(1)} %get-tuple-element.97.refs_1_, bf16[1536,256]{1,0:T(8,128)(2,1)S(1)} %get-tuple-element.98.refs_2_, ...), custom_call_target="tpu_custom_call" | custom-call | flops 1610612736 | bytes 6291456 | tf_op jit(solution)/shard_map/gradient/pallas_call | solution.py:233
  113.6 0.5 key_backward.1.refs_4_
  114.1 0.5 collective-permute-start.32
  114.6 1.5 collective-permute-start.29
  116.2 1.5 collective-permute-start.23
  117.7 3.6 %gradient.5 = (f32[1536,512]{1,0:T(8,128)S(1)}, f32[8,128]{1,0:T(8,128)S(1)}, f32[1536,128]{1,0:T(8,128)S(1)}) custom-call(s32[2]{0:T(128)S(1)} %pad_add_fusion.place_ref, bf16[1536,256]{1,0:T(8,128)(2,1)S(1)} %get-tuple-element.71.refs_0_, bf16[1536,256]{1,0:T(8,128)(2,1)S(1)} %get-tuple-element.72.refs_1_, ...), custom_call_target="tpu_custom_call" | custom-call | flops 1610612736 | bytes 6291456 | tf_op jit(solution)/shard_map/gradient/pallas_call | solution.py:233
  121.3 2.9 %collective-permute-done.32.refs_6_ = bf16[256,512]{1,0:T(8,128)(2,1)S(1)} collective-permute-done((bf16[256,512]{1,0:T(8,128)(2,1)S(1)}, bf16[256,512]{1,0:T(8,128)(2,1)S(1)}, u32[]{:S(2)}, u32[]{:S(2)}) %collective-permute-start.32) | collective-permute-done | bytes 262176 | tf_op jit(solution)/shard_map/ppermute | solution.py:447
  124.3 3.9 %collective-permute-done.29.refs_6_ = bf16[256,512]{1,0:T(8,128)(2,1)S(1)} collective-permute-done((bf16[256,512]{1,0:T(8,128)(2,1)S(1)}, bf16[256,512]{1,0:T(8,128)(2,1)S(1)}, u32[]{:S(2)}, u32[]{:S(2)}) %collective-permute-start.29) | collective-permute-done | bytes 262176 | tf_op jit(solution)/shard_map/ppermute | solution.py:447
  128.7 3.2 %gradient.6.refs_8_ = f32[1536,512]{1,0:T(8,128)S(1)} custom-call(s32[2]{0:T(128)S(1)} %pad_add_fusion.place_ref, bf16[1536,256]{1,0:T(8,128)(2,1)S(1)} %get-tuple-element.96.refs_0_, bf16[1536,256]{1,0:T(8,128)(2,1)S(1)} %get-tuple-element.97.refs_1_, bf16[1536,256]{1,0:T(8,128)(2,1)S(1)} %get-tuple-element.98.refs_2_, ...), custom_call_target="tpu_custom_call" | custom-call | flops 1610612736 | bytes 6291456 | tf_op jit(solution)/shard_map/gradient/pallas_call | solution.py:233
  132.0 3.6 %gradient.7 = (f32[1536,512]{1,0:T(8,128)S(1)}, f32[8,128]{1,0:T(8,128)S(1)}, f32[1536,128]{1,0:T(8,128)S(1)}) custom-call(s32[2]{0:T(128)S(1)} %pad_add_fusion.place_ref, bf16[1536,256]{1,0:T(8,128)(2,1)S(1)} %get-tuple-element.71.refs_0_, bf16[1536,256]{1,0:T(8,128)(2,1)S(1)} %get-tuple-element.72.refs_1_, ...), custom_call_target="tpu_custom_call" | custom-call | flops 1610612736 | bytes 6291456 | tf_op jit(solution)/shard_map/gradient/pallas_call | solution.py:233
  135.6 1.1 collective-permute-done.34
  136.8 1.1 collective-permute-start.37
  137.9 1.0 collective-permute-start.36
  138.9 1.3 collective-permute-start.35
  140.3 1.0 collective-permute-done.37.refs_3_
  141.5 1.0 collective-permute-done.35.refs_1_
  142.5 1.5 adam_frag.1
  144.2 3.0 %collective-permute-start.39 = (bf16[384,128]{1,0:T(8,128)(2,1)S(1)}, bf16[384,128]{1,0:T(8,128)(2,1)S(1)}, u32[]{:S(2)}, u32[]{:S(2)}) collective-permute-start(bf16[384,128]{1,0:T(8,128)(2,1)S(1)} %get-tuple-element.119), channel_id=1, source_target_pairs={{0,16},{8,24},{16,0},{24,8},{1,17},{9,25},{17,1},{25,9},{2,18},{10... | collective-permute-start | bytes 294920 | tf_op jit(solution)/shard_map/ppermute | solution.py:447
  147.2 1.3 collective-permute-start.40
  148.6 6.0 %adam_rows.2 = (f32[1536,1024]{1,0:T(8,128)}, f32[1536,1024]{1,0:T(8,128)}, f32[1536,1024]{1,0:T(8,128)}, f32[8,128]{1,0:T(8,128)S(1)}) custom-call(f32[3]{0:T(128)S(1)} %pad_maximum_fusion.sc_ref, f32[1536,1024]{1,0:T(8,128)S(1)} %bitcast.42, f32[1536,1024]{1,0:T(8,128)S(1)} %bitcast.50, f32[1536,1024]{1,0:T(8,128)S(1)} %bitcast.58, ...), custom_call_target="tpu_custom_call" | custom-call | flops 15728640 | bytes 22020096 | tf_op jit(solution)/shard_map/adam_rows/pallas_call | solution.py:288
  154.7 2.5 %collective-permute-start.43 = (bf16[384,128]{1,0:T(8,128)(2,1)S(1)}, bf16[384,128]{1,0:T(8,128)(2,1)S(1)}, u32[]{:S(2)}, u32[]{:S(2)}) collective-permute-start(bf16[384,128]{1,0:T(8,128)(2,1)S(1)} %convert_element_type.24.refs_7_), channel_id=1, source_target_pairs={{0,24},{8,16},{16,8},{24,0},{1,25},{9,17},{17,9},{25,1},{2,26},{10... | collective-permute-start | bytes 294920 | tf_op jit(solution)/shard_map/ppermute | solution.py:447
  157.3 1.9 %collective-permute-start.41 = (bf16[384,128]{1,0:T(8,128)(2,1)S(1)}, bf16[384,128]{1,0:T(8,128)(2,1)S(1)}, u32[]{:S(2)}, u32[]{:S(2)}) collective-permute-start(bf16[384,128]{1,0:T(8,128)(2,1)S(1)} %convert_element_type.24.refs_7_), channel_id=1, source_target_pairs={{0,8},{8,0},{16,24},{24,16},{1,9},{9,1},{17,25},{25,17},{2,10},{10... | collective-permute-start | bytes 294920 | tf_op jit(solution)/shard_map/ppermute | solution.py:447
  159.2 6.0 %adam_rows.3 = (f32[1536,1024]{1,0:T(8,128)}, f32[1536,1024]{1,0:T(8,128)}, f32[1536,1024]{1,0:T(8,128)}) custom-call(f32[3]{0:T(128)S(1)} %pad_maximum_fusion.sc_ref, f32[1536,1024]{1,0:T(8,128)S(1)} %bitcast.43, f32[1536,1024]{1,0:T(8,128)S(1)} %bitcast.51, ...), custom_call_target="tpu_custom_call", output_to_operand_aliasing={{0}: (10, {}), {1}: (11, {}), {2}: (12, {})} | custom-call | flops 15728640 | bytes 22020096 | tf_op jit(solution)/shard_map/adam_rows/pallas_call | solution.py:288
  165.2 2.4 %outer_step.1 = (f32[1536,1024]{1,0:T(8,128)}, f32[384,1024]{1,0:T(8,128)}, f32[384,1024]{1,0:T(8,128)}) custom-call(s32[2]{0:T(128)S(1)} %pad_add_fusion.place_ref, f32[1536,1024]{1,0:T(8,128)} %get-tuple-element.115.refs_0_, f32[384,1024]{1,0:T(8,128)} %get-tuple-element.75.refs_1_, ...), custom_call_target="tpu_custom_call", output_to_operand_aliasing={{0}: (1, {}), {1}: (2, {}), {2}: (3, {})} | custom-call | flops 1966080 | bytes 3932160 | tf_op jit(solution)/shard_map/outer_step/pallas_call | solution.py:429
  (77 shorter events, 4.2 us)
Async XLA Ops:
  2.6 22.6 %collective-permute-start.6 = (bf16[256,1536]{1,0:T(8,128)(2,1)}, bf16[256,1536]{1,0:T(8,128)(2,1)S(1)}, u32[]{:S(2)}, u32[]{:S(2)}) collective-permute-start(bf16[256,1536]{1,0:T(8,128)(2,1)} %pack.6), channel_id=1, source_target_pairs={{0,6},{1,7},{2,4},{3,5},{4,2},{5,3},{6,0},{7,1},{8,14},{9,15},{10,... | collective-permute-start | bytes 2359304 | tf_op jit(solution)/shard_map/ppermute | solution.py:447
  8.9 19.0 %collective-permute-start.18 = (bf16[256,1536]{1,0:T(8,128)(2,1)}, bf16[256,1536]{1,0:T(8,128)(2,1)S(1)}, u32[]{:S(2)}, u32[]{:S(2)}) collective-permute-start(bf16[256,1536]{1,0:T(8,128)(2,1)} %get-tuple-element.93), channel_id=1, source_target_pairs={{0,1},{1,0},{2,3},{3,2},{4,5},{5,4},{6,7},{7,6},{8,9},{9,8},{10,11... | collective-permute-start | bytes 2359304 | tf_op jit(solution)/shard_map/ppermute | solution.py:447
  11.3 32.0 %collective-permute-start.1 = (bf16[256,1536]{1,0:T(8,128)(2,1)}, bf16[256,1536]{1,0:T(8,128)(2,1)S(1)}, u32[]{:S(2)}, u32[]{:S(2)}) collective-permute-start(bf16[256,1536]{1,0:T(8,128)(2,1)} %get-tuple-element.69), channel_id=1, source_target_pairs={{0,3},{1,2},{2,1},{3,0},{4,7},{5,6},{6,5},{7,4},{8,11},{9,10},{10,... | collective-permute-start | bytes 2359304 | tf_op jit(solution)/shard_map/ppermute | solution.py:447
  12.0 33.0 %collective-permute-start.4 = (bf16[256,1536]{1,0:T(8,128)(2,1)}, bf16[256,1536]{1,0:T(8,128)(2,1)}, u32[]{:S(2)}, u32[]{:S(2)}) collective-permute-start(bf16[256,1536]{1,0:T(8,128)(2,1)} %get-tuple-element.74), channel_id=1, source_target_pairs={{0,5},{1,4},{2,7},{3,6},{4,1},{5,0},{6,3},{7,2},{8,13},{9,12},{10,... | collective-permute-start | bytes 2359304 | tf_op jit(solution)/shard_map/ppermute | solution.py:447
  14.7 43.9 %collective-permute-start.7 = (bf16[256,1536]{1,0:T(8,128)(2,1)}, bf16[256,1536]{1,0:T(8,128)(2,1)}, u32[]{:S(2)}, u32[]{:S(2)}) collective-permute-start(bf16[256,1536]{1,0:T(8,128)(2,1)} %get-tuple-element.81), channel_id=1, source_target_pairs={{0,7},{1,6},{2,5},{3,4},{4,3},{5,2},{6,1},{7,0},{8,15},{9,14},{10,... | collective-permute-start | bytes 2359304 | tf_op jit(solution)/shard_map/ppermute | solution.py:447
  25.2 50.0 %collective-permute-start = (bf16[256,1536]{1,0:T(8,128)(2,1)}, bf16[256,1536]{1,0:T(8,128)(2,1)S(1)}, u32[]{:S(2)}, u32[]{:S(2)}) collective-permute-start(bf16[256,1536]{1,0:T(8,128)(2,1)} %get-tuple-element.68), channel_id=1, source_target_pairs={{0,2},{1,3},{2,0},{3,1},{4,6},{5,7},{6,4},{7,5},{8,10},{9,11},{10,... | collective-permute-start | bytes 2359304 | tf_op jit(solution)/shard_map/ppermute | solution.py:447
  27.9 54.9 %collective-permute-start.3 = (bf16[256,1536]{1,0:T(8,128)(2,1)}, bf16[256,1536]{1,0:T(8,128)(2,1)S(1)}, u32[]{:S(2)}, u32[]{:S(2)}) collective-permute-start(bf16[256,1536]{1,0:T(8,128)(2,1)} %get-tuple-element.73), channel_id=1, source_target_pairs={{0,4},{1,5},{2,6},{3,7},{4,0},{5,1},{6,2},{7,3},{8,12},{9,13},{10,... | collective-permute-start | bytes 2359304 | tf_op jit(solution)/shard_map/ppermute | solution.py:447
  43.3 33.4 %collective-permute-start.10 = (f32[384,128]{1,0:T(8,128)S(1)}, f32[384,128]{1,0:T(8,128)S(1)}, u32[]{:S(2)}, u32[]{:S(2)}) collective-permute-start(f32[384,128]{1,0:T(8,128)S(1)} %get-tuple-element.132), channel_id=1, source_target_pairs={{0,8},{8,0},{16,24},{24,16},{1,9},{9,1},{17,25},{25,17},{2,10},{10... | collective-permute-start | bytes 589832 | tf_op jit(solution)/shard_map/ppermute | solution.py:447
  44.9 31.7 %collective-permute-start.12 = (f32[384,128]{1,0:T(8,128)S(1)}, f32[384,128]{1,0:T(8,128)S(1)}, u32[]{:S(2)}, u32[]{:S(2)}) collective-permute-start(f32[384,128]{1,0:T(8,128)S(1)} %get-tuple-element.133), channel_id=1, source_target_pairs={{0,24},{8,16},{16,8},{24,0},{1,25},{9,17},{17,9},{25,1},{2,26},{10... | collective-permute-start | bytes 589832 | tf_op jit(solution)/shard_map/ppermute | solution.py:447
  58.6 18.5 %collective-permute-start.11 = (f32[384,128]{1,0:T(8,128)S(1)}, f32[384,128]{1,0:T(8,128)S(1)}, u32[]{:S(2)}, u32[]{:S(2)}) collective-permute-start(f32[384,128]{1,0:T(8,128)S(1)} %get-tuple-element.134), channel_id=1, source_target_pairs={{0,16},{8,24},{16,0},{24,8},{1,17},{9,25},{17,1},{25,9},{2,18},{10... | collective-permute-start | bytes 589832 | tf_op jit(solution)/shard_map/ppermute | solution.py:447
  75.2 9.1 %collective-permute-start.21 = (bf16[256,512]{1,0:T(8,128)(2,1)S(1)}, bf16[256,512]{1,0:T(8,128)(2,1)S(1)}, u32[]{:S(2)}, u32[]{:S(2)}) collective-permute-start(bf16[256,512]{1,0:T(8,128)(2,1)S(1)} %slice.24.refs_4_), channel_id=1, source_target_pairs={{0,6},{1,7},{2,4},{3,5},{4,2},{5,3},{6,0},{7,1},{8,14},{9,15},{10,... | collective-permute-start | bytes 786440 | tf_op jit(solution)/shard_map/ppermute | solution.py:447
  76.7 9.4 %collective-permute-start.2 = (bf16[256,512]{1,0:T(8,128)(2,1)S(1)}, bf16[256,512]{1,0:T(8,128)(2,1)S(1)}, u32[]{:S(2)}, u32[]{:S(2)}) collective-permute-start(bf16[256,512]{1,0:T(8,128)(2,1)S(1)} %get-tuple-element.70), channel_id=1, source_target_pairs={{0,1},{1,0},{2,3},{3,2},{4,5},{5,4},{6,7},{7,6},{8,9},{9,8},{10,11... | collective-permute-start | bytes 786440 | tf_op jit(solution)/shard_map/ppermute | solution.py:447
  76.7 1.9 %collective-permute-start.8 = (bf16[256,512]{1,0:T(8,128)(2,1)S(1)}, bf16[256,512]{1,0:T(8,128)(2,1)S(1)}, u32[]{:S(2)}, u32[]{:S(2)}) collective-permute-start(bf16[256,512]{1,0:T(8,128)(2,1)S(1)} %get-tuple-element.82), channel_id=1, source_target_pairs={{0,1},{1,0},{2,3},{3,2},{4,5},{5,4},{6,7},{7,6},{8,9},{9,8},{10,11... | collective-permute-start | bytes 786440 | tf_op jit(solution)/shard_map/ppermute | solution.py:447
  77.2 11.2 %collective-permute-start.5 = (bf16[256,512]{1,0:T(8,128)(2,1)S(1)}, bf16[256,512]{1,0:T(8,128)(2,1)S(1)}, u32[]{:S(2)}, u32[]{:S(2)}) collective-permute-start(bf16[256,512]{1,0:T(8,128)(2,1)S(1)} %get-tuple-element.80), channel_id=1, source_target_pairs={{0,1},{1,0},{2,3},{3,2},{4,5},{5,4},{6,7},{7,6},{8,9},{9,8},{10,11... | collective-permute-start | bytes 786440 | tf_op jit(solution)/shard_map/ppermute | solution.py:447
  78.6 9.9 %collective-permute-start.15 = (f32[384,128]{1,0:T(8,128)S(1)}, f32[384,128]{1,0:T(8,128)S(1)}, u32[]{:S(2)}, u32[]{:S(2)}) collective-permute-start(f32[384,128]{1,0:T(8,128)S(1)} %get-tuple-element.130.refs_3_), channel_id=1, source_target_pairs={{0,24},{8,16},{16,8},{24,0},{1,25},{9,17},{17,9},{25,1},{2,26},{10... | collective-permute-start | bytes 589832 | tf_op jit(solution)/shard_map/ppermute | solution.py:447
  82.8 21.7 %copy-start = (bf16[256,1536]{1,0:T(8,128)(2,1)S(1)}, bf16[256,1536]{1,0:T(8,128)(2,1)}, u32[]{:S(2)}) copy-start(bf16[256,1536]{1,0:T(8,128)(2,1)} %get-tuple-element.92.refs_0_.refs_1_.refs_2_.refs_3_) | copy-start | bytes 2359300
  82.8 18.5 %collective-permute-start.9 = (bf16[256,512]{1,0:T(8,128)(2,1)S(1)}, bf16[256,512]{1,0:T(8,128)(2,1)S(1)}, u32[]{:S(2)}, u32[]{:S(2)}) collective-permute-start(bf16[256,512]{1,0:T(8,128)(2,1)S(1)} %get-tuple-element.83), channel_id=1, source_target_pairs={{0,6},{1,7},{2,4},{3,5},{4,2},{5,3},{6,0},{7,1},{8,14},{9,15},{10,... | collective-permute-start | bytes 786440 | tf_op jit(solution)/shard_map/ppermute | solution.py:447
  84.3 14.8 %collective-permute-start.14 = (f32[384,128]{1,0:T(8,128)S(1)}, f32[384,128]{1,0:T(8,128)S(1)}, u32[]{:S(2)}, u32[]{:S(2)}) collective-permute-start(f32[384,128]{1,0:T(8,128)S(1)} %get-tuple-element.130.refs_3_), channel_id=1, source_target_pairs={{0,16},{8,24},{16,0},{24,8},{1,17},{9,25},{17,1},{25,9},{2,18},{10... | collective-permute-start | bytes 589832 | tf_op jit(solution)/shard_map/ppermute | solution.py:447
  86.1 14.6 %collective-permute-start.13 = (f32[384,128]{1,0:T(8,128)S(1)}, f32[384,128]{1,0:T(8,128)S(1)}, u32[]{:S(2)}, u32[]{:S(2)}) collective-permute-start(f32[384,128]{1,0:T(8,128)S(1)} %get-tuple-element.130.refs_3_), channel_id=1, source_target_pairs={{0,8},{8,0},{16,24},{24,16},{1,9},{9,1},{17,25},{25,17},{2,10},{10... | collective-permute-start | bytes 589832 | tf_op jit(solution)/shard_map/ppermute | solution.py:447
  88.4 14.0 %collective-permute-start.20 = (bf16[256,512]{1,0:T(8,128)(2,1)S(1)}, bf16[256,512]{1,0:T(8,128)(2,1)S(1)}, u32[]{:S(2)}, u32[]{:S(2)}) collective-permute-start(bf16[256,512]{1,0:T(8,128)(2,1)S(1)} %slice.24.refs_4_), channel_id=1, source_target_pairs={{0,1},{1,0},{2,3},{3,2},{4,5},{5,4},{6,7},{7,6},{8,9},{9,8},{10,11... | collective-permute-start | bytes 786440 | tf_op jit(solution)/shard_map/ppermute | solution.py:447
  88.5 15.5 %collective-permute-start.19 = (bf16[256,512]{1,0:T(8,128)(2,1)S(1)}, bf16[256,512]{1,0:T(8,128)(2,1)S(1)}, u32[]{:S(2)}, u32[]{:S(2)}) collective-permute-start(bf16[256,512]{1,0:T(8,128)(2,1)S(1)} %get-tuple-element.94), channel_id=1, source_target_pairs={{0,1},{1,0},{2,3},{3,2},{4,5},{5,4},{6,7},{7,6},{8,9},{9,8},{10,11... | collective-permute-start | bytes 786440 | tf_op jit(solution)/shard_map/ppermute | solution.py:447
  99.2 7.5 %collective-permute-start.26 = (bf16[256,512]{1,0:T(8,128)(2,1)S(1)}, bf16[256,512]{1,0:T(8,128)(2,1)S(1)}, u32[]{:S(2)}, u32[]{:S(2)}) collective-permute-start(bf16[256,512]{1,0:T(8,128)(2,1)S(1)} %slice.24.refs_4_), channel_id=1, source_target_pairs={{0,4},{1,5},{2,6},{3,7},{4,0},{5,1},{6,2},{7,3},{8,12},{9,13},{10,... | collective-permute-start | bytes 786440 | tf_op jit(solution)/shard_map/ppermute | solution.py:447
  100.7 9.2 %collective-permute-start.24 = (bf16[256,512]{1,0:T(8,128)(2,1)S(1)}, bf16[256,512]{1,0:T(8,128)(2,1)S(1)}, u32[]{:S(2)}, u32[]{:S(2)}) collective-permute-start(bf16[256,512]{1,0:T(8,128)(2,1)S(1)} %slice.24.refs_4_), channel_id=1, source_target_pairs={{0,2},{1,3},{2,0},{3,1},{4,6},{5,7},{6,4},{7,5},{8,10},{9,11},{10,... | collective-permute-start | bytes 786440 | tf_op jit(solution)/shard_map/ppermute | solution.py:447
  101.2 8.7 %collective-permute-start.22 = (bf16[256,512]{1,0:T(8,128)(2,1)S(1)}, bf16[256,512]{1,0:T(8,128)(2,1)S(1)}, u32[]{:S(2)}, u32[]{:S(2)}) collective-permute-start(bf16[256,512]{1,0:T(8,128)(2,1)S(1)} %collective-permute-done.21.refs_6_), channel_id=1, source_target_pairs={{0,1},{1,0},{2,3},{3,2},{4,5},{5,4},{6,7},{7,6},{8,9},{9,8},{10,11... | collective-permute-start | bytes 786440 | tf_op jit(solution)/shard_map/ppermute | solution.py:447
  102.4 11.2 %copy-start.1 = (bf16[1,256,1024]{2,1,0:T(8,128)(2,1)S(1)}, bf16[1,256,1024]{2,1,0:T(8,128)(2,1)}, u32[]{:S(2)}) copy-start(bf16[1,256,1024]{2,1,0:T(8,128)(2,1)} %param.10) | copy-start | bytes 1572868
  102.4 11.1 %collective-permute-start.16 = (bf16[256,512]{1,0:T(8,128)(2,1)S(1)}, bf16[256,512]{1,0:T(8,128)(2,1)S(1)}, u32[]{:S(2)}, u32[]{:S(2)}) collective-permute-start(bf16[256,512]{1,0:T(8,128)(2,1)S(1)} %get-tuple-element.90), channel_id=1, source_target_pairs={{0,2},{1,3},{2,0},{3,1},{4,6},{5,7},{6,4},{7,5},{8,10},{9,11},{10,... | collective-permute-start | bytes 786440 | tf_op jit(solution)/shard_map/ppermute | solution.py:447
  104.0 9.6 %collective-permute-start.17 = (bf16[256,512]{1,0:T(8,128)(2,1)S(1)}, bf16[256,512]{1,0:T(8,128)(2,1)S(1)}, u32[]{:S(2)}, u32[]{:S(2)}) collective-permute-start(bf16[256,512]{1,0:T(8,128)(2,1)S(1)} %get-tuple-element.91), channel_id=1, source_target_pairs={{0,4},{1,5},{2,6},{3,7},{4,0},{5,1},{6,2},{7,3},{8,12},{9,13},{10,... | collective-permute-start | bytes 786440 | tf_op jit(solution)/shard_map/ppermute | solution.py:447
  104.5 44.1 %slice-start.4 = ((s8[6291456]{0:T(1024)(128)(4,1)}), s8[4194304]{0:T(1024)(128)(4,1)S(1)}, s32[]{:S(2)}) async-start(s8[6291456]{0:T(1024)(128)(4,1)} %bitcast.56), calls=%async_computation.4 | async-start | bytes 8388608
  106.7 11.0 %collective-permute-start.27 = (bf16[256,512]{1,0:T(8,128)(2,1)S(1)}, bf16[256,512]{1,0:T(8,128)(2,1)S(1)}, u32[]{:S(2)}, u32[]{:S(2)}) collective-permute-start(bf16[256,512]{1,0:T(8,128)(2,1)S(1)} %collective-permute-done.26.refs_6_), channel_id=1, source_target_pairs={{0,1},{1,0},{2,3},{3,2},{4,5},{5,4},{6,7},{7,6},{8,9},{9,8},{10,11... | collective-permute-start | bytes 786440 | tf_op jit(solution)/shard_map/ppermute | solution.py:447
  109.9 7.7 %collective-permute-start.25 = (bf16[256,512]{1,0:T(8,128)(2,1)S(1)}, bf16[256,512]{1,0:T(8,128)(2,1)S(1)}, u32[]{:S(2)}, u32[]{:S(2)}) collective-permute-start(bf16[256,512]{1,0:T(8,128)(2,1)S(1)} %collective-permute-done.24.refs_4_), channel_id=1, source_target_pairs={{0,1},{1,0},{2,3},{3,2},{4,5},{5,4},{6,7},{7,6},{8,9},{9,8},{10,11... | collective-permute-start | bytes 786440 | tf_op jit(solution)/shard_map/ppermute | solution.py:447
  114.1 10.2 %collective-permute-start.32 = (bf16[256,512]{1,0:T(8,128)(2,1)S(1)}, bf16[256,512]{1,0:T(8,128)(2,1)S(1)}, u32[]{:S(2)}, u32[]{:S(2)}) collective-permute-start(bf16[256,512]{1,0:T(8,128)(2,1)S(1)} %key_backward.1.refs_4_), channel_id=1, source_target_pairs={{0,6},{1,7},{2,4},{3,5},{4,2},{5,3},{6,0},{7,1},{8,14},{9,15},{10,... | collective-permute-start | bytes 786440 | tf_op jit(solution)/shard_map/ppermute | solution.py:447
  114.6 13.5 %collective-permute-start.29 = (bf16[256,512]{1,0:T(8,128)(2,1)S(1)}, bf16[256,512]{1,0:T(8,128)(2,1)S(1)}, u32[]{:S(2)}, u32[]{:S(2)}) collective-permute-start(bf16[256,512]{1,0:T(8,128)(2,1)S(1)} %key_backward.1.refs_4_), channel_id=1, source_target_pairs={{0,4},{1,5},{2,6},{3,7},{4,0},{5,1},{6,2},{7,3},{8,12},{9,13},{10,... | collective-permute-start | bytes 786440 | tf_op jit(solution)/shard_map/ppermute | solution.py:447
  116.2 12.0 %collective-permute-start.23 = (bf16[256,512]{1,0:T(8,128)(2,1)S(1)}, bf16[256,512]{1,0:T(8,128)(2,1)S(1)}, u32[]{:S(2)}, u32[]{:S(2)}) collective-permute-start(bf16[256,512]{1,0:T(8,128)(2,1)S(1)} %key_backward.1.refs_4_), channel_id=1, source_target_pairs={{0,2},{1,3},{2,0},{3,1},{4,6},{5,7},{6,4},{7,5},{8,10},{9,11},{10,... | collective-permute-start | bytes 786440 | tf_op jit(solution)/shard_map/ppermute | solution.py:447
  117.7 30.9 %slice-start.5 = ((s8[6291456]{0:T(1024)(128)(4,1)}), s8[2097152]{0:T(1024)(128)(4,1)S(1)}, s32[]{:S(2)}) async-start(s8[6291456]{0:T(1024)(128)(4,1)} %bitcast.56), calls=%async_computation.5 | async-start | bytes 4194304
  121.3 7.5 %collective-permute-start.31 = (bf16[256,512]{1,0:T(8,128)(2,1)S(1)}, bf16[256,512]{1,0:T(8,128)(2,1)S(1)}, u32[]{:S(2)}, u32[]{:S(2)}) collective-permute-start(bf16[256,512]{1,0:T(8,128)(2,1)S(1)} %key_backward.1.refs_4_), channel_id=1, source_target_pairs={{0,1},{1,0},{2,3},{3,2},{4,5},{5,4},{6,7},{7,6},{8,9},{9,8},{10,11... | collective-permute-start | bytes 786440 | tf_op jit(solution)/shard_map/ppermute | solution.py:447
  124.3 4.4 %collective-permute-start.33 = (bf16[256,512]{1,0:T(8,128)(2,1)S(1)}, bf16[256,512]{1,0:T(8,128)(2,1)S(1)}, u32[]{:S(2)}, u32[]{:S(2)}) collective-permute-start(bf16[256,512]{1,0:T(8,128)(2,1)S(1)} %collective-permute-done.32.refs_6_), channel_id=1, source_target_pairs={{0,1},{1,0},{2,3},{3,2},{4,5},{5,4},{6,7},{7,6},{8,9},{9,8},{10,11... | collective-permute-start | bytes 786440 | tf_op jit(solution)/shard_map/ppermute | solution.py:447
  128.2 3.7 %collective-permute-start.30 = (bf16[256,512]{1,0:T(8,128)(2,1)S(1)}, bf16[256,512]{1,0:T(8,128)(2,1)S(1)}, u32[]{:S(2)}, u32[]{:S(2)}) collective-permute-start(bf16[256,512]{1,0:T(8,128)(2,1)S(1)} %collective-permute-done.29.refs_6_), channel_id=1, source_target_pairs={{0,1},{1,0},{2,3},{3,2},{4,5},{5,4},{6,7},{7,6},{8,9},{9,8},{10,11... | collective-permute-start | bytes 786440 | tf_op jit(solution)/shard_map/ppermute | solution.py:447
  128.2 3.7 %collective-permute-start.28 = (bf16[256,512]{1,0:T(8,128)(2,1)S(1)}, bf16[256,512]{1,0:T(8,128)(2,1)S(1)}, u32[]{:S(2)}, u32[]{:S(2)}) collective-permute-start(bf16[256,512]{1,0:T(8,128)(2,1)S(1)} %collective-permute-done.23.refs_4_), channel_id=1, source_target_pairs={{0,1},{1,0},{2,3},{3,2},{4,5},{5,4},{6,7},{7,6},{8,9},{9,8},{10,11... | collective-permute-start | bytes 786440 | tf_op jit(solution)/shard_map/ppermute | solution.py:447
  128.7 19.8 %slice-start = ((s8[6291456]{0:T(1024)(128)(4,1)}), s8[4194304]{0:T(1024)(128)(4,1)S(1)}, s32[]{:S(2)}) async-start(s8[6291456]{0:T(1024)(128)(4,1)} %bitcast.40), calls=%async_computation | async-start | bytes 8388608
  128.7 19.8 %slice-start.2 = ((s8[6291456]{0:T(1024)(128)(4,1)}), s8[4194304]{0:T(1024)(128)(4,1)S(1)}, s32[]{:S(2)}) async-start(s8[6291456]{0:T(1024)(128)(4,1)} %bitcast.48), calls=%async_computation.2 | async-start | bytes 8388608
  131.9 16.6 %slice-start.1 = ((s8[6291456]{0:T(1024)(128)(4,1)}), s8[2097152]{0:T(1024)(128)(4,1)S(1)}, s32[]{:S(2)}) async-start(s8[6291456]{0:T(1024)(128)(4,1)} %bitcast.40), calls=%async_computation.1 | async-start | bytes 4194304
  131.9 16.6 %slice-start.3 = ((s8[6291456]{0:T(1024)(128)(4,1)}), s8[2097152]{0:T(1024)(128)(4,1)S(1)}, s32[]{:S(2)}) async-start(s8[6291456]{0:T(1024)(128)(4,1)} %bitcast.48), calls=%async_computation.3 | async-start | bytes 4194304
  135.6 1.2 collective-permute-start.34
  136.8 4.5 %collective-permute-start.37 = (f32[8,128]{1,0:T(8,128)S(1)}, f32[8,128]{1,0:T(8,128)S(1)}, u32[]{:S(2)}, u32[]{:S(2)}) collective-permute-start(f32[8,128]{1,0:T(8,128)S(1)} %add.32.refs_0_), channel_id=1, source_target_pairs={{0,6},{1,7},{2,4},{3,5},{4,2},{5,3},{6,0},{7,1},{8,14},{9,15},{10,... | collective-permute-start | bytes 12296 | tf_op jit(solution)/shard_map/ppermute | solution.py:447
  137.9 3.6 %collective-permute-start.36 = (f32[8,128]{1,0:T(8,128)S(1)}, f32[8,128]{1,0:T(8,128)S(1)}, u32[]{:S(2)}, u32[]{:S(2)}) collective-permute-start(f32[8,128]{1,0:T(8,128)S(1)} %add.32.refs_0_), channel_id=1, source_target_pairs={{0,4},{1,5},{2,6},{3,7},{4,0},{5,1},{6,2},{7,3},{8,12},{9,13},{10,... | collective-permute-start | bytes 12296 | tf_op jit(solution)/shard_map/ppermute | solution.py:447
  138.9 3.6 %collective-permute-start.35 = (f32[8,128]{1,0:T(8,128)S(1)}, f32[8,128]{1,0:T(8,128)S(1)}, u32[]{:S(2)}, u32[]{:S(2)}) collective-permute-start(f32[8,128]{1,0:T(8,128)S(1)} %add.32.refs_0_), channel_id=1, source_target_pairs={{0,2},{1,3},{2,0},{3,1},{4,6},{5,7},{6,4},{7,5},{8,10},{9,11},{10,... | collective-permute-start | bytes 12296 | tf_op jit(solution)/shard_map/ppermute | solution.py:447
  144.1 10.5 %collective-permute-start.38 = (bf16[384,128]{1,0:T(8,128)(2,1)S(1)}, bf16[384,128]{1,0:T(8,128)(2,1)S(1)}, u32[]{:S(2)}, u32[]{:S(2)}) collective-permute-start(bf16[384,128]{1,0:T(8,128)(2,1)S(1)} %get-tuple-element.118), channel_id=1, source_target_pairs={{0,8},{8,0},{16,24},{24,16},{1,9},{9,1},{17,25},{25,17},{2,10},{10... | collective-permute-start | bytes 294920 | tf_op jit(solution)/shard_map/ppermute | solution.py:447
  144.2 10.5 %collective-permute-start.39 = (bf16[384,128]{1,0:T(8,128)(2,1)S(1)}, bf16[384,128]{1,0:T(8,128)(2,1)S(1)}, u32[]{:S(2)}, u32[]{:S(2)}) collective-permute-start(bf16[384,128]{1,0:T(8,128)(2,1)S(1)} %get-tuple-element.119), channel_id=1, source_target_pairs={{0,16},{8,24},{16,0},{24,8},{1,17},{9,25},{17,1},{25,9},{2,18},{10... | collective-permute-start | bytes 294920 | tf_op jit(solution)/shard_map/ppermute | solution.py:447
  147.2 7.4 %collective-permute-start.40 = (bf16[384,128]{1,0:T(8,128)(2,1)S(1)}, bf16[384,128]{1,0:T(8,128)(2,1)S(1)}, u32[]{:S(2)}, u32[]{:S(2)}) collective-permute-start(bf16[384,128]{1,0:T(8,128)(2,1)S(1)} %get-tuple-element.120), channel_id=1, source_target_pairs={{0,24},{8,16},{16,8},{24,0},{1,25},{9,17},{17,9},{25,1},{2,26},{10... | collective-permute-start | bytes 294920 | tf_op jit(solution)/shard_map/ppermute | solution.py:447
  154.7 10.5 %collective-permute-start.43 = (bf16[384,128]{1,0:T(8,128)(2,1)S(1)}, bf16[384,128]{1,0:T(8,128)(2,1)S(1)}, u32[]{:S(2)}, u32[]{:S(2)}) collective-permute-start(bf16[384,128]{1,0:T(8,128)(2,1)S(1)} %convert_element_type.24.refs_7_), channel_id=1, source_target_pairs={{0,24},{8,16},{16,8},{24,0},{1,25},{9,17},{17,9},{25,1},{2,26},{10... | collective-permute-start | bytes 294920 | tf_op jit(solution)/shard_map/ppermute | solution.py:447
  157.3 7.9 %collective-permute-start.42 = (bf16[384,128]{1,0:T(8,128)(2,1)S(1)}, bf16[384,128]{1,0:T(8,128)(2,1)S(1)}, u32[]{:S(2)}, u32[]{:S(2)}) collective-permute-start(bf16[384,128]{1,0:T(8,128)(2,1)S(1)} %convert_element_type.24.refs_7_), channel_id=1, source_target_pairs={{0,16},{8,24},{16,0},{24,8},{1,17},{9,25},{17,1},{25,9},{2,18},{10... | collective-permute-start | bytes 294920 | tf_op jit(solution)/shard_map/ppermute | solution.py:447
  157.3 7.9 %collective-permute-start.41 = (bf16[384,128]{1,0:T(8,128)(2,1)S(1)}, bf16[384,128]{1,0:T(8,128)(2,1)S(1)}, u32[]{:S(2)}, u32[]{:S(2)}) collective-permute-start(bf16[384,128]{1,0:T(8,128)(2,1)S(1)} %convert_element_type.24.refs_7_), channel_id=1, source_target_pairs={{0,8},{8,0},{16,24},{24,16},{1,9},{9,1},{17,25},{25,17},{2,10},{10... | collective-permute-start | bytes 294920 | tf_op jit(solution)/shard_map/ppermute | solution.py:447

commit v14 on v13

--- a/solution.py
+++ b/solution.py
@@ -305,9 +305,10 @@
     factor = clip_factor(refs[:squares])
     inner_ref, *out_refs = refs[squares:]
     for j in range(blocks):
-        at = pl.multiple_of((place_ref[1] ^ j) * part, 8)
-        old = w_ref[j]
-        update, _, _ = adam(old, m_ref[j], v_ref[j], g_ref[pl.ds(at, part), :], factor, sc_ref)
+        d = place_ref[1] ^ j
+        at = pl.multiple_of(d * part, 8)
+        old = w_ref[d]
+        update, _, _ = adam(old, m_ref[d], v_ref[d], g_ref[pl.ds(at, part), :], factor, sc_ref)
         inner_ref[j] = old - update
         out_refs[j][...] = update.astype(out_refs[j].dtype)
 
@@ -339,8 +340,7 @@
     blocks = arrays[0].shape[0] // part
     specs = []
     for j in range(blocks):
-        at = (lambda i, p, j=j: (p[1] ^ j, p[0])) if blocks > 1 else (lambda i, p: (0, p[0]))
-        specs.append(pl.BlockSpec((part, FRAG_COLS), at))
+        specs.append(pl.BlockSpec((part, FRAG_COLS), lambda i, p, j=j: (j, p[0])))
     shape = (blocks, part, FRAG_COLS)
     return pl.pallas_call(
         functools.partial(pick_kernel, blocks),
@@ -401,14 +401,14 @@
 
 def outer_kernel(replicas, place_ref, *refs):
     share = 1.0 / replicas
-    base_refs, sum_refs = refs[3:3 + replicas], refs[3 + replicas:3 + 2 * replicas]
-    inner_ref, a_ref, p_ref, m_ref, own_ref, _, w_out, a_out, m_out = refs[3 + 2 * replicas:]
+    base_ref, sum_refs = refs[3], refs[4:4 + replicas]
+    inner_ref, a_ref, p_ref, m_ref, own_ref, _, w_out, a_out, m_out = refs[4 + replicas:]
     scale = share * (1.0 + OUTER_MU) * OUTER_RATE
     for j in range(replicas):
 
         @pl.when(pl.program_id(0) == j)
         def _():
-            fresh = base_refs[j][...] - scale * sum_refs[j][...].astype(jnp.float32)
+            fresh = base_ref[0] - scale * sum_refs[j][...].astype(jnp.float32)
             w_out[...] = MIX_LOCAL * inner_ref[0] + (1.0 - MIX_LOCAL) * fresh
 
     @pl.when(pl.program_id(0) == 0)
@@ -423,6 +423,7 @@
     replicas, part = inner.shape[0], inner.shape[1]
     mixed = pl.BlockSpec((part, FRAG_COLS), lambda j, p: (p[1] ^ j, p[0]))
     pieces = pl.BlockSpec((1, part, FRAG_COLS), lambda j, p: (j, 0, 0))
+    placed = pl.BlockSpec((1, part, FRAG_COLS), lambda j, p: (p[1] ^ j, 0, 0))
     due = pl.BlockSpec((part, FRAG_COLS), lambda j, p: (0, p[0]))
     plain = pl.BlockSpec((part, FRAG_COLS), lambda j, p: (0, 0))
     whole = pl.BlockSpec(memory_space=pl.ANY)
@@ -432,14 +433,14 @@
         grid_spec=pltpu.PrefetchScalarGridSpec(
             num_scalar_prefetch=1,
             grid=(replicas,),
-            in_specs=[whole] * 3 + [plain] * (2 * replicas) + [pieces] + [plain] * 4 + [whole],
+            in_specs=[whole] * 3 + [placed] + [plain] * replicas + [pieces] + [plain] * 4 + [whole],
             out_specs=[mixed, due, due],
         ),
         input_output_aliases={1: 0, 2: 1, 3: 2},
         compiler_params=params_of(12),
         cost_estimate=cost(10 * replicas * part * FRAG_COLS, 20 * replicas * part * FRAG_COLS),
         name="outer_step",
-    )(place, *in_hbm(*outputs), *base, *sums, inner, anchor, pseudo, momentum, own_sum, ticket)
+    )(place, *in_hbm(*outputs), base, *sums, inner, anchor, pseudo, momentum, own_sum, ticket)
 
 
 def swap(block, axis, offset):
@@ -482,8 +483,11 @@
     blocks = {k: swap(packed[k], "fsdp", k) for k in order}
     blocks[0], blocks[1] = packed[0], swap(packed[1], "fsdp", 1)
 
+    def to_all(pieces):
+        return lax.all_to_all(pieces, "rep", 0, 0, tiled=True)
+
     (old,) = due_columns(after(place, blocks[order[0]]), part, params)
-    old_sums = [old[0]] + [swap(old[k], "rep", k) for k in range(1, replicas)]
+    old_sums = to_all(old)
 
     values = {0: incoming[:, kv_width:]}
     for i, k in enumerate(far):
@@ -501,9 +505,9 @@
     scalars = jnp.stack([rate, inv_one, inv_two])
     old_first, old_second = due_columns(place, part, first_moment[0], second_moment[0])
     anchor_cols, moment_cols = (c[0] for c in due_columns(place, part, anchor, momentum))
-    pseudo_old = anchor_cols - sum(old_sums[1:], old_sums[0]) / replicas
+    pseudo_old = anchor_cols - jnp.sum(old_sums, axis=0) / replicas
     base = anchor_cols - OUTER_RATE * (OUTER_MU * (OUTER_MU * moment_cols + pseudo_old) + pseudo_old)
-    base = [base] + [swap(base, "rep", k) for k in range(1, replicas)]
+    base = to_all(jnp.broadcast_to(base[None], (replicas,) + base.shape))
     anchor_copy, momentum_copy = duplicate(anchor, momentum)
     key_weights = cast_left(params, kv_width)
 
@@ -514,7 +518,7 @@
         theirs, flipped[k + 1] = partial_keys(blocks[k + 1], key_weights)
         theirs = swap(theirs, "fsdp", 1)
         if k == last:
-            theirs = after(theirs, *parts[:1], *base)
+            theirs = after(theirs, *parts[:1], base)
         part_k, flipped[k] = partial_keys(blocks[k], key_weights, theirs)
         parts.append(swap(part_k, "fsdp", k) if k else part_k)
     spread = [0, 1] + [k + odd for k in far for odd in range(2)]

time: 169 us -> 174 us (1.030)
  local copies, waits for them, and re-layouts: 1.06 us -> 11 us
  waiting for transfers between devices: 55.8 us -> 47.3 us
  Pallas kernels: 58 us -> 65.7 us
  starting transfers between devices: 49.7 us -> 45.2 us
    ppermute x44 -> x38, waiting for transfers between devices: 55.8 us -> 37.5 us  [swap(): return lax.ppermute(block, axis, [(i, i ^ offset) for i in range(count)])]
    ppermute x44 -> x38, starting transfers between devices: 49.7 us -> 35.9 us  [swap(): return lax.ppermute(block, axis, [(i, i ^ offset) for i in range(count)])]
    all_to_all x0 -> x2, waiting for transfers between devices: none -> 9.8 us  [to_all(): return lax.all_to_all(pieces, 'rep', 0, 0, tiled=True)]
    unnamed x16 -> x70, local copies, waits for them, and re-layouts: 0.04 us -> 9.37 us
    all_to_all x0 -> x2, starting transfers between devices: none -> 9.26 us  [to_all(): return lax.all_to_all(pieces, 'rep', 0, 0, tiled=True)]
    pallas_call x4, Pallas kernels: 13.5 us -> 15.9 us  [gradient(): pl.pallas_call(functools.partial(grad_kernel, len(flipped), base is not N...]
    pallas_call x8, Pallas kernels: 7.02 us -> 8.93 us  [partial_keys(): pl.pallas_call(functools.partial(partial_kernel, pieces), out_shape=[jax....]
    pallas_call x1, Pallas kernels: 2.36 us -> 4.12 us  [outer_step(): pl.pallas_call(functools.partial(outer_kernel, replicas), out_shape=[pltp...]
  transfers between devices with their start and end apart: 44 -> 40, of which waited for: 14 -> 13; matrix products, arithmetic and copies ran while one was open for 1% -> 1% of each run, Pallas kernels for 29% -> 29%
where the time goes in v14:
time: 174 us; the launch traced here: 173 us
  Pallas kernels  65.7 us (38%)
  waiting for transfers between devices  47.3 us (27%)
  starting transfers between devices  45.2 us (26%)
  local copies, waits for them, and re-layouts  11 us (6%)
  between operations  3.84 us (2%)
    ppermute x38, waiting for transfers between devices, swap(): return lax.ppermute(block, axis, [(i, i ^ offset) for i in range(count)])  37.5 us
    ppermute x38, starting transfers between devices, swap(): return lax.ppermute(block, axis, [(i, i ^ offset) for i in range(count)])  35.9 us
    pallas_call x4, Pallas kernels, gradient(): pl.pallas_call(functools.partial(grad_kernel, len(flipped), base is not N...  15.9 us
    pallas_call x2, Pallas kernels, adam_rows(): pl.pallas_call(functools.partial(adam_kernel, len(squares), len(into)), o...  12 us
    all_to_all x2, waiting for transfers between devices, to_all(): return lax.all_to_all(pieces, 'rep', 0, 0, tiled=True)  9.8 us
    unnamed x70, local copies, waits for them, and re-layouts  9.37 us
    pallas_call x4, Pallas kernels, pack(): pl.pallas_call(functools.partial(pack_kernel, offsets), out_shape=[pltpu....  9.34 us
    all_to_all x2, starting transfers between devices, to_all(): return lax.all_to_all(pieces, 'rep', 0, 0, tiled=True)  9.26 us
  transfers between devices with their start and end apart: 40, of which 13 were waited for; matrix products, arithmetic and copies ran while one was open for 1% of the time, Pallas kernels for 29%

profile of v14, /device:TPU:0, one launch (start us, length us, event | category | flops | bytes accessed | tf_op | source)
XLA Modules:
  0.0 173.3 jit_solution(16638340573872107396)
XLA Ops:
  0.6 2.0 %pack.6 = bf16[256,1536]{1,0:T(8,128)(2,1)} custom-call(s32[1]{0:T(128)} %bitcast.4.me_ref, bf16[256,12288]{1,0:T(8,128)(2,1)} %bitcast.48), custom_call_target="tpu_custom_call" | custom-call | bytes 1572864 | tf_op jit(solution)/shard_map/pack/pallas_call | solution.py:69
  2.6 4.0 %collective-permute-start.6 = (bf16[256,1536]{1,0:T(8,128)(2,1)}, bf16[256,1536]{1,0:T(8,128)(2,1)S(1)}, u32[]{:S(2)}, u32[]{:S(2)}) collective-permute-start(bf16[256,1536]{1,0:T(8,128)(2,1)} %pack.6), channel_id=1, source_target_pairs={{0,6},{1,7},{2,4},{3,5},{4,2},{5,3},{6,0},{7,1},{8,14},{9,15},{10,... | collective-permute-start | bytes 2359304 | tf_op jit(solution)/shard_map/ppermute | solution.py:448
  7.3 17.0 %collective-permute-done.6.refs_0_.refs_1_.refs_2_.refs_3_ = bf16[256,1536]{1,0:T(8,128)(2,1)S(1)} collective-permute-done((bf16[256,1536]{1,0:T(8,128)(2,1)}, bf16[256,1536]{1,0:T(8,128)(2,1)S(1)}, u32[]{:S(2)}, u32[]{:S(2)}) %collective-permute-start.6) | collective-permute-done | bytes 786464 | tf_op jit(solution)/shard_map/ppermute | solution.py:448
  24.3 2.7 %due_columns.5.w_ref = f32[4,384,128]{2,1,0:T(8,128)} custom-call(s32[2]{0:T(128)S(1)} %pad_add_fusion.place_ref, f32[1536,1024]{1,0:T(8,128)} %bitcast.19, f32[1536,1024]{1,0:T(8,128)} %bitcast.20, f32[1536,1024]{1,0:T(8,128)} %bitcast.21, f32[1536,1024]{1,0:T(8,128)} %bitcast.22), custom_call_target="tpu_custom_call" | custom-call | bytes 1572864 | tf_op jit(solution)/shard_map/due_columns/pallas_call | solution.py:345
  27.0 5.1 %all-to-all-start = ((f32[4,384,128]{2,1,0:T(8,128)}), f32[4,384,128]{2,1,0:T(8,128)S(1)}, u32[]{:S(2)}, u32[]{:S(2)}) async-start(f32[4,384,128]{2,1,0:T(8,128)} %due_columns.5.w_ref), calls=%async_computation | async-start | bytes 1572864 | tf_op jit(solution)/shard_map/all_to_all | solution.py:487
  32.1 2.6 %pack.4 = (bf16[256,1536]{1,0:T(8,128)(2,1)}, bf16[256,1536]{1,0:T(8,128)(2,1)}, bf16[256,1536]{1,0:T(8,128)(2,1)}) custom-call(s32[1]{0:T(128)} %bitcast.4.me_ref, bf16[256,12288]{1,0:T(8,128)(2,1)} %bitcast.49), custom_call_target="tpu_custom_call" | custom-call | bytes 4718592 | tf_op jit(solution)/shard_map/pack/pallas_call | solution.py:69
  34.7 0.8 collective-permute-start.7
  35.5 2.3 %pack.5 = (bf16[256,1536]{1,0:T(8,128)(2,1)}, bf16[256,1536]{1,0:T(8,128)(2,1)}) custom-call(s32[1]{0:T(128)} %bitcast.4.me_ref, bf16[256,12288]{1,0:T(8,128)(2,1)} %bitcast.50), custom_call_target="tpu_custom_call" | custom-call | bytes 3145728 | tf_op jit(solution)/shard_map/pack/pallas_call | solution.py:69
  37.8 2.0 %collective-permute-start.4 = (bf16[256,1536]{1,0:T(8,128)(2,1)}, bf16[256,1536]{1,0:T(8,128)(2,1)}, u32[]{:S(2)}, u32[]{:S(2)}) collective-permute-start(bf16[256,1536]{1,0:T(8,128)(2,1)} %get-tuple-element.74), channel_id=1, source_target_pairs={{0,5},{1,4},{2,7},{3,6},{4,1},{5,0},{6,3},{7,2},{8,13},{9,12},{10,... | collective-permute-start | bytes 2359304 | tf_op jit(solution)/shard_map/ppermute | solution.py:448
  40.0 1.6 due_columns.4
  41.5 9.8 %all-to-all-done = f32[4,384,128]{2,1,0:T(8,128)S(1)} async-done(((f32[4,384,128]{2,1,0:T(8,128)}), f32[4,384,128]{2,1,0:T(8,128)S(1)}, u32[]{:S(2)}, u32[]{:S(2)}) %all-to-all-start) | async-done | bytes 786464 | tf_op jit(solution)/shard_map/all_to_all | solution.py:487
  51.5 0.9 broadcast_in_dim.18
  52.4 4.2 %all-to-all-start.1 = ((f32[4,384,128]{2,1,0:T(8,128)}), f32[4,384,128]{2,1,0:T(8,128)}, u32[]{:S(2)}, u32[]{:S(2)}) async-start(f32[4,384,128]{2,1,0:T(8,128)} %broadcast_in_dim.18), calls=%async_computation.1 | async-start | bytes 1572864 | tf_op jit(solution)/shard_map/all_to_all | solution.py:487
  56.6 2.5 %pack.7 = (bf16[256,1536]{1,0:T(8,128)(2,1)}, bf16[256,1536]{1,0:T(8,128)(2,1)}) custom-call(s32[1]{0:T(128)} %bitcast.4.me_ref, bf16[256,12288]{1,0:T(8,128)(2,1)} %bitcast.51), custom_call_target="tpu_custom_call" | custom-call | bytes 3145728 | tf_op jit(solution)/shard_map/pack/pallas_call | solution.py:69
  59.2 1.6 collective-permute-start
  60.7 0.9 copy-done.1
  61.6 1.5 collective-permute-start.3
  63.1 3.5 %cast_left.1.refs_4_ = bf16[1536,512]{1,0:T(8,128)(2,1)S(1)} custom-call(f32[1536,1024]{1,0:T(8,128)} %bitcast.23), custom_call_target="tpu_custom_call" | custom-call | bytes 4718592 | tf_op jit(solution)/shard_map/cast_left/pallas_call | solution.py:93
  67.2 5.4 %collective-permute-done.4.refs_0_.refs_1_.refs_2_.refs_3_ = bf16[256,1536]{1,0:T(8,128)(2,1)} collective-permute-done((bf16[256,1536]{1,0:T(8,128)(2,1)}, bf16[256,1536]{1,0:T(8,128)(2,1)}, u32[]{:S(2)}, u32[]{:S(2)}) %collective-permute-start.4) | collective-permute-done | bytes 786464 | tf_op jit(solution)/shard_map/ppermute | solution.py:448
  72.9 2.8 %duplicate.1 = (f32[384,1024]{1,0:T(8,128)}, f32[384,1024]{1,0:T(8,128)}) custom-call(f32[384,1024]{1,0:T(8,128)} %refs_0_.3, f32[384,1024]{1,0:T(8,128)} %refs_1_.3), custom_call_target="tpu_custom_call" | custom-call | bytes 6291456 | tf_op jit(solution)/shard_map/duplicate/pallas_call | solution.py:386
  76.6 0.7 slice.4.refs_4_
  77.3 2.1 %due_columns.3 = (f32[4,384,128]{2,1,0:T(8,128)S(1)}, f32[4,384,128]{2,1,0:T(8,128)S(1)}) custom-call(s32[2]{0:T(128)S(1)} %pad_add_fusion.place_ref, f32[1536,1024]{1,0:T(8,128)} %bitcast.28, f32[1536,1024]{1,0:T(8,128)} %bitcast.29, f32[1536,1024]{1,0:T(8,128)} %bitcast.30, f32[1536,1024]{1,0:T(8,128)} %bitcast.31, f32[1536,1024]{1,0:T(8,128)} %bitcast.36, ...), custom_call_target="tpu_custom_call" | custom-call | bytes 3145728 | tf_op jit(solution)/shard_map/due_columns/pallas_call | solution.py:345
  79.5 0.9 copy-done.19
  80.4 1.3 collective-permute-start.15
  81.7 1.8 %partial_keys.10 = (bf16[256,512]{1,0:T(8,128)(2,1)S(1)}, bf16[1536,256]{1,0:T(8,128)(2,1)S(1)}) custom-call(bf16[256,1536]{1,0:T(8,128)(2,1)} %collective-permute-done.4.refs_0_.refs_1_.refs_2_.refs_3_, bf16[256,1536]{1,0:T(8,128)(2,1)} %collective-permute-done.4.refs_0_.refs_1_.refs_2_.refs_3_, ...), custom_call_target="tpu_custom_call" | custom-call | flops 402653184 | bytes 1572864 | tf_op jit(solution)/shard_map/partial_keys/pallas_call | solution.py:122
  83.5 0.9 copy-done.9
  84.4 1.8 %partial_keys.8 = (bf16[256,512]{1,0:T(8,128)(2,1)S(1)}, bf16[1536,256]{1,0:T(8,128)(2,1)S(1)}) custom-call(bf16[256,1536]{1,0:T(8,128)(2,1)} %collective-permute-done.1.refs_0_.refs_1_.refs_2_.refs_3_, bf16[256,1536]{1,0:T(8,128)(2,1)} %collective-permute-done.1.refs_0_.refs_1_.refs_2_.refs_3_, ...), custom_call_target="tpu_custom_call" | custom-call | flops 402653184 | bytes 1572864 | tf_op jit(solution)/shard_map/partial_keys/pallas_call | solution.py:122
  86.2 0.9 copy-done.11
  87.7 0.9 copy-done.5
  89.1 1.6 collective-permute-start.9
  90.7 1.3 partial_keys.14
  92.0 1.0 copy-done.7
  93.2 2.2 %collective-permute-done.15.refs_6_ = bf16[256,512]{1,0:T(8,128)(2,1)} collective-permute-done((bf16[256,512]{1,0:T(8,128)(2,1)}, bf16[256,512]{1,0:T(8,128)(2,1)}, u32[]{:S(2)}, u32[]{:S(2)}) %collective-permute-start.15) | collective-permute-done | bytes 262176 | tf_op jit(solution)/shard_map/ppermute | solution.py:448
  95.3 1.4 collective-permute-start.20
  96.7 0.7 copy-done.23
  97.5 1.5 collective-permute-start.18
  99.0 1.9 %collective-permute-done.9.refs_0_ = bf16[256,512]{1,0:T(8,128)(2,1)S(1)} collective-permute-done((bf16[256,512]{1,0:T(8,128)(2,1)S(1)}, bf16[256,512]{1,0:T(8,128)(2,1)S(1)}, u32[]{:S(2)}, u32[]{:S(2)}) %collective-permute-start.9) | collective-permute-done | bytes 262176 | tf_op jit(solution)/shard_map/ppermute | solution.py:448
  102.2 0.9 copy-done.13
  103.8 0.9 copy-done.24
  105.8 1.2 collective-permute-start.11
  107.1 1.7 %partial_keys.15 = (bf16[256,512]{1,0:T(8,128)(2,1)S(1)}, bf16[1536,256]{1,0:T(8,128)(2,1)S(1)}) custom-call(bf16[256,1536]{1,0:T(8,128)(2,1)S(1)} %copy-done, bf16[256,1536]{1,0:T(8,128)(2,1)S(1)} %copy-done, bf16[256,1536]{1,0:T(8,128)(2,1)S(1)} %copy-done, bf16[256,1536]{1,0:T(8,128)(2,1)S(1)} %copy-done, bf16[1536,512]{1,0:T(8,128)(2,1)S(1)} %cast_left.1.refs_4_, ...), custom_call_target="tpu_custom_call" | custom-call | flops 402653184 | bytes 1572864 | tf_op jit(solution)/shard_map/partial_keys/pallas_call | solution.py:122
  109.4 4.4 %gradient.4.refs_8_ = f32[1536,512]{1,0:T(8,128)S(1)} custom-call(s32[2]{0:T(128)S(1)} %pad_add_fusion.place_ref, bf16[1536,256]{1,0:T(8,128)(2,1)S(1)} %get-tuple-element.96.refs_0_, bf16[1536,256]{1,0:T(8,128)(2,1)S(1)} %copy-done.8, bf16[1536,256]{1,0:T(8,128)(2,1)S(1)} %copy-done.6, bf16[1536,256]{1,0:T(8,128)(2,1)S(1)} %copy-done.4, ...), custom_call_target="tpu_custom_call" | custom-call | flops 1610612736 | bytes 6291456 | tf_op jit(solution)/shard_map/gradient/pallas_call | solution.py:233
  114.9 1.5 collective-permute-start.26
  116.3 1.6 collective-permute-start.23
  118.5 4.7 %gradient.5 = (f32[1536,512]{1,0:T(8,128)S(1)}, f32[8,128]{1,0:T(8,128)S(1)}, f32[1536,128]{1,0:T(8,128)S(1)}) custom-call(s32[2]{0:T(128)S(1)} %pad_add_fusion.place_ref, bf16[1536,256]{1,0:T(8,128)(2,1)S(1)} %copy-done.14, bf16[1536,256]{1,0:T(8,128)(2,1)S(1)} %copy-done.12, bf16[1536,256]{1,0:T(8,128)(2,1)S(1)} %get-tuple-element.88.refs_2_, ...), custom_call_target="tpu_custom_call" | custom-call | flops 1610612736 | bytes 6291456 | tf_op jit(solution)/shard_map/gradient/pallas_call | solution.py:233
  123.3 1.8 %collective-permute-done.26.refs_6_ = bf16[256,512]{1,0:T(8,128)(2,1)S(1)} collective-permute-done((bf16[256,512]{1,0:T(8,128)(2,1)S(1)}, bf16[256,512]{1,0:T(8,128)(2,1)S(1)}, u32[]{:S(2)}, u32[]{:S(2)}) %collective-permute-start.26) | collective-permute-done | bytes 262176 | tf_op jit(solution)/shard_map/ppermute | solution.py:448
  125.1 4.3 %collective-permute-done.23.refs_6_ = bf16[256,512]{1,0:T(8,128)(2,1)S(1)} collective-permute-done((bf16[256,512]{1,0:T(8,128)(2,1)S(1)}, bf16[256,512]{1,0:T(8,128)(2,1)S(1)}, u32[]{:S(2)}, u32[]{:S(2)}) %collective-permute-start.23) | collective-permute-done | bytes 262176 | tf_op jit(solution)/shard_map/ppermute | solution.py:448
  129.9 3.2 %gradient.6.refs_8_ = f32[1536,512]{1,0:T(8,128)S(1)} custom-call(s32[2]{0:T(128)S(1)} %pad_add_fusion.place_ref, bf16[1536,256]{1,0:T(8,128)(2,1)S(1)} %get-tuple-element.96.refs_0_, bf16[1536,256]{1,0:T(8,128)(2,1)S(1)} %copy-done.8, bf16[1536,256]{1,0:T(8,128)(2,1)S(1)} %copy-done.6, bf16[1536,256]{1,0:T(8,128)(2,1)S(1)} %copy-done.4, ...), custom_call_target="tpu_custom_call" | custom-call | flops 1610612736 | bytes 6291456 | tf_op jit(solution)/shard_map/gradient/pallas_call | solution.py:233
  133.2 3.6 %gradient.7 = (f32[1536,512]{1,0:T(8,128)S(1)}, f32[8,128]{1,0:T(8,128)S(1)}, f32[1536,128]{1,0:T(8,128)S(1)}) custom-call(s32[2]{0:T(128)S(1)} %pad_add_fusion.place_ref, bf16[1536,256]{1,0:T(8,128)(2,1)S(1)} %copy-done.14, bf16[1536,256]{1,0:T(8,128)(2,1)S(1)} %copy-done.12, bf16[1536,256]{1,0:T(8,128)(2,1)S(1)} %get-tuple-element.88.refs_2_, ...), custom_call_target="tpu_custom_call" | custom-call | flops 1610612736 | bytes 6291456 | tf_op jit(solution)/shard_map/gradient/pallas_call | solution.py:233
  136.9 1.1 collective-permute-done.28
  138.0 1.7 %collective-permute-start.31 = (f32[8,128]{1,0:T(8,128)S(1)}, f32[8,128]{1,0:T(8,128)S(1)}, u32[]{:S(2)}, u32[]{:S(2)}) collective-permute-start(f32[8,128]{1,0:T(8,128)S(1)} %add.22.refs_0_), channel_id=1, source_target_pairs={{0,6},{1,7},{2,4},{3,5},{4,2},{5,3},{6,0},{7,1},{8,14},{9,15},{10,... | collective-permute-start | bytes 12296 | tf_op jit(solution)/shard_map/ppermute | solution.py:448
  139.7 0.7 collective-permute-start.30
  140.5 1.0 collective-permute-start.29
  141.5 1.0 collective-permute-done.31.refs_3_
  142.5 0.8 collective-permute-done.30.refs_2_
  143.4 0.7 collective-permute-done.29.refs_1_
  144.1 2.1 %adam_frag.1 = (f32[4,384,128]{2,1,0:T(8,128)S(1)}, bf16[384,128]{1,0:T(8,128)(2,1)S(1)}, bf16[384,128]{1,0:T(8,128)(2,1)S(1)}, bf16[384,128]{1,0:T(8,128)(2,1)S(1)}, bf16[384,128]{1,0:T(8,128)(2,1)S(1)}) custom-call(s32[2]{0:T(128)S(1)} %pad_add_fusion.place_ref, f32[3]{0:T(128)S(1)} %pad_maximum_fusion.sc_ref, f32[4,384,128]{2,1,0:T(8,128)} %due_columns.5.w_ref, ...), custom_call_target="tpu_custom_call" | custom-call | flops 3932160 | bytes 4325376 | tf_op jit(solution)/shard_map/adam_frag/pallas_call | solution.py:320
  146.2 2.1 %collective-permute-start.32 = (bf16[384,128]{1,0:T(8,128)(2,1)S(1)}, bf16[384,128]{1,0:T(8,128)(2,1)S(1)}, u32[]{:S(2)}, u32[]{:S(2)}) collective-permute-start(bf16[384,128]{1,0:T(8,128)(2,1)S(1)} %get-tuple-element.118), channel_id=1, source_target_pairs={{0,8},{8,0},{16,24},{24,16},{1,9},{9,1},{17,25},{25,17},{2,10},{10... | collective-permute-start | bytes 294920 | tf_op jit(solution)/shard_map/ppermute | solution.py:448
  148.3 2.4 %collective-permute-start.33 = (bf16[384,128]{1,0:T(8,128)(2,1)S(1)}, bf16[384,128]{1,0:T(8,128)(2,1)S(1)}, u32[]{:S(2)}, u32[]{:S(2)}) collective-permute-start(bf16[384,128]{1,0:T(8,128)(2,1)S(1)} %get-tuple-element.119), channel_id=1, source_target_pairs={{0,16},{8,24},{16,0},{24,8},{1,17},{9,25},{17,1},{25,9},{2,18},{10... | collective-permute-start | bytes 294920 | tf_op jit(solution)/shard_map/ppermute | solution.py:448
  150.8 6.0 %adam_rows.2 = (f32[1536,1024]{1,0:T(8,128)}, f32[1536,1024]{1,0:T(8,128)}, f32[1536,1024]{1,0:T(8,128)}, f32[8,128]{1,0:T(8,128)S(1)}) custom-call(f32[3]{0:T(128)S(1)} %pad_maximum_fusion.sc_ref, f32[1536,1024]{1,0:T(8,128)S(1)} %bitcast.26, f32[1536,1024]{1,0:T(8,128)S(1)} %bitcast.34, f32[1536,1024]{1,0:T(8,128)S(1)} %bitcast.42, ...), custom_call_target="tpu_custom_call" | custom-call | flops 15728640 | bytes 22020096 | tf_op jit(solution)/shard_map/adam_rows/pallas_call | solution.py:288
  157.5 3.2 %collective-permute-start.37 = (bf16[384,128]{1,0:T(8,128)(2,1)S(1)}, bf16[384,128]{1,0:T(8,128)(2,1)S(1)}, u32[]{:S(2)}, u32[]{:S(2)}) collective-permute-start(bf16[384,128]{1,0:T(8,128)(2,1)S(1)} %convert_element_type.24.refs_4_), channel_id=1, source_target_pairs={{0,24},{8,16},{16,8},{24,0},{1,25},{9,17},{17,9},{25,1},{2,26},{10... | collective-permute-start | bytes 294920 | tf_op jit(solution)/shard_map/ppermute | solution.py:448
  160.8 1.2 collective-permute-start.35
  162.0 6.0 %adam_rows.3 = (f32[1536,1024]{1,0:T(8,128)}, f32[1536,1024]{1,0:T(8,128)}, f32[1536,1024]{1,0:T(8,128)}) custom-call(f32[3]{0:T(128)S(1)} %pad_maximum_fusion.sc_ref, f32[1536,1024]{1,0:T(8,128)S(1)} %bitcast.27, f32[1536,1024]{1,0:T(8,128)S(1)} %bitcast.35, ...), custom_call_target="tpu_custom_call", output_to_operand_aliasing={{0}: (10, {}), {1}: (11, {}), {2}: (12, {})} | custom-call | flops 15728640 | bytes 22020096 | tf_op jit(solution)/shard_map/adam_rows/pallas_call | solution.py:288
  168.1 4.1 %outer_step.1 = (f32[1536,1024]{1,0:T(8,128)}, f32[384,1024]{1,0:T(8,128)}, f32[384,1024]{1,0:T(8,128)}) custom-call(s32[2]{0:T(128)S(1)} %pad_add_fusion.place_ref, f32[1536,1024]{1,0:T(8,128)} %get-tuple-element.115.refs_0_, f32[384,1024]{1,0:T(8,128)} %get-tuple-element.75.refs_1_, ...), custom_call_target="tpu_custom_call", output_to_operand_aliasing={{0}: (1, {}), {1}: (2, {}), {2}: (3, {})} | custom-call | flops 1966080 | bytes 3932160 | tf_op jit(solution)/shard_map/outer_step/pallas_call | solution.py:430
  (125 shorter events, 9.4 us)
Async XLA Ops:
  2.6 21.7 %collective-permute-start.6 = (bf16[256,1536]{1,0:T(8,128)(2,1)}, bf16[256,1536]{1,0:T(8,128)(2,1)S(1)}, u32[]{:S(2)}, u32[]{:S(2)}) collective-permute-start(bf16[256,1536]{1,0:T(8,128)(2,1)} %pack.6), channel_id=1, source_target_pairs={{0,6},{1,7},{2,4},{3,5},{4,2},{5,3},{6,0},{7,1},{8,14},{9,15},{10,... | collective-permute-start | bytes 2359304 | tf_op jit(solution)/shard_map/ppermute | solution.py:448
  27.0 24.3 %all-to-all-start = ((f32[4,384,128]{2,1,0:T(8,128)}), f32[4,384,128]{2,1,0:T(8,128)S(1)}, u32[]{:S(2)}, u32[]{:S(2)}) async-start(f32[4,384,128]{2,1,0:T(8,128)} %due_columns.5.w_ref), calls=%async_computation | async-start | bytes 1572864 | tf_op jit(solution)/shard_map/all_to_all | solution.py:487
  34.7 26.0 %collective-permute-start.7 = (bf16[256,1536]{1,0:T(8,128)(2,1)}, bf16[256,1536]{1,0:T(8,128)(2,1)S(1)}, u32[]{:S(2)}, u32[]{:S(2)}) collective-permute-start(bf16[256,1536]{1,0:T(8,128)(2,1)} %get-tuple-element.81), channel_id=1, source_target_pairs={{0,7},{1,6},{2,5},{3,4},{4,3},{5,2},{6,1},{7,0},{8,15},{9,14},{10,... | collective-permute-start | bytes 2359304 | tf_op jit(solution)/shard_map/ppermute | solution.py:448
  37.8 34.8 %collective-permute-start.4 = (bf16[256,1536]{1,0:T(8,128)(2,1)}, bf16[256,1536]{1,0:T(8,128)(2,1)}, u32[]{:S(2)}, u32[]{:S(2)}) collective-permute-start(bf16[256,1536]{1,0:T(8,128)(2,1)} %get-tuple-element.74), channel_id=1, source_target_pairs={{0,5},{1,4},{2,7},{3,6},{4,1},{5,0},{6,3},{7,2},{8,13},{9,12},{10,... | collective-permute-start | bytes 2359304 | tf_op jit(solution)/shard_map/ppermute | solution.py:448
  39.8 40.6 %collective-permute-start.1 = (bf16[256,1536]{1,0:T(8,128)(2,1)}, bf16[256,1536]{1,0:T(8,128)(2,1)}, u32[]{:S(2)}, u32[]{:S(2)}) collective-permute-start(bf16[256,1536]{1,0:T(8,128)(2,1)} %get-tuple-element.69), channel_id=1, source_target_pairs={{0,3},{1,2},{2,1},{3,0},{4,7},{5,6},{6,5},{7,4},{8,11},{9,10},{10,... | collective-permute-start | bytes 2359304 | tf_op jit(solution)/shard_map/ppermute | solution.py:448
  51.4 9.3 %copy-start.26 = (f32[384,128]{1,0:T(8,128)}, f32[384,128]{1,0:T(8,128)S(1)}, u32[]{:S(2)}) copy-start(f32[384,128]{1,0:T(8,128)S(1)} %reduce_sum.9) | copy-start | bytes 589828
  52.4 51.4 %all-to-all-start.1 = ((f32[4,384,128]{2,1,0:T(8,128)}), f32[4,384,128]{2,1,0:T(8,128)}, u32[]{:S(2)}, u32[]{:S(2)}) async-start(f32[4,384,128]{2,1,0:T(8,128)} %broadcast_in_dim.18), calls=%async_computation.1 | async-start | bytes 1572864 | tf_op jit(solution)/shard_map/all_to_all | solution.py:487
  56.6 5.0 %copy-start.28 = (bf16[256,1536]{1,0:T(8,128)(2,1)S(1)}, bf16[256,1536]{1,0:T(8,128)(2,1)}, u32[]{:S(2)}) copy-start(bf16[256,1536]{1,0:T(8,128)(2,1)} %get-tuple-element.73) | copy-start | bytes 2359300
  59.1 29.5 %collective-permute-start.12 = (bf16[256,1536]{1,0:T(8,128)(2,1)}, bf16[256,1536]{1,0:T(8,128)(2,1)S(1)}, u32[]{:S(2)}, u32[]{:S(2)}) collective-permute-start(bf16[256,1536]{1,0:T(8,128)(2,1)} %get-tuple-element.93), channel_id=1, source_target_pairs={{0,1},{1,0},{2,3},{3,2},{4,5},{5,4},{6,7},{7,6},{8,9},{9,8},{10,11... | collective-permute-start | bytes 2359304 | tf_op jit(solution)/shard_map/ppermute | solution.py:448
  59.2 29.9 %collective-permute-start = (bf16[256,1536]{1,0:T(8,128)(2,1)}, bf16[256,1536]{1,0:T(8,128)(2,1)S(1)}, u32[]{:S(2)}, u32[]{:S(2)}) collective-permute-start(bf16[256,1536]{1,0:T(8,128)(2,1)} %get-tuple-element.68), channel_id=1, source_target_pairs={{0,2},{1,3},{2,0},{3,1},{4,6},{5,7},{6,4},{7,5},{8,10},{9,11},{10,... | collective-permute-start | bytes 2359304 | tf_op jit(solution)/shard_map/ppermute | solution.py:448
  61.6 5.0 %copy-start.2 = (bf16[256,1536]{1,0:T(8,128)(2,1)S(1)}, bf16[256,1536]{1,0:T(8,128)(2,1)}, u32[]{:S(2)}) copy-start(bf16[256,1536]{1,0:T(8,128)(2,1)} %copy-done.1) | copy-start | bytes 2359300
  61.6 15.0 %copy-start.15 = (bf16[1,256,1024]{2,1,0:T(8,128)(2,1)S(1)}, bf16[1,256,1024]{2,1,0:T(8,128)(2,1)}, u32[]{:S(2)}) copy-start(bf16[1,256,1024]{2,1,0:T(8,128)(2,1)} %param.10) | copy-start | bytes 1572868
  61.6 31.3 %collective-permute-start.3 = (bf16[256,1536]{1,0:T(8,128)(2,1)S(1)}, bf16[256,1536]{1,0:T(8,128)(2,1)S(1)}, u32[]{:S(2)}, u32[]{:S(2)}) collective-permute-start(bf16[256,1536]{1,0:T(8,128)(2,1)S(1)} %copy-done.28), channel_id=1, source_target_pairs={{0,4},{1,5},{2,6},{3,7},{4,0},{5,1},{6,2},{7,3},{8,12},{9,13},{10,... | collective-permute-start | bytes 2359304 | tf_op jit(solution)/shard_map/ppermute | solution.py:448
  67.2 12.3 %copy-start.3 = (bf16[1536,256]{1,0:T(8,128)(2,1)}, bf16[1536,256]{1,0:T(8,128)(2,1)S(1)}, u32[]{:S(2)}) copy-start(bf16[1536,256]{1,0:T(8,128)(2,1)S(1)} %get-tuple-element.99.refs_3_) | copy-start | bytes 2359300
  72.6 14.5 %collective-permute-start.8 = (bf16[256,512]{1,0:T(8,128)(2,1)S(1)}, bf16[256,512]{1,0:T(8,128)(2,1)S(1)}, u32[]{:S(2)}, u32[]{:S(2)}) collective-permute-start(bf16[256,512]{1,0:T(8,128)(2,1)S(1)} %get-tuple-element.82), channel_id=1, source_target_pairs={{0,1},{1,0},{2,3},{3,2},{4,5},{5,4},{6,7},{7,6},{8,9},{9,8},{10,11... | collective-permute-start | bytes 786440 | tf_op jit(solution)/shard_map/ppermute | solution.py:448
  80.3 7.3 %copy-start.17 = (f32[4,384,128]{2,1,0:T(8,128)}, f32[4,384,128]{2,1,0:T(8,128)S(1)}, u32[]{:S(2)}) copy-start(f32[4,384,128]{2,1,0:T(8,128)S(1)} %get-tuple-element.77.m_ref) | copy-start | bytes 2359300
  80.4 14.9 %collective-permute-start.15 = (bf16[256,512]{1,0:T(8,128)(2,1)}, bf16[256,512]{1,0:T(8,128)(2,1)}, u32[]{:S(2)}, u32[]{:S(2)}) collective-permute-start(bf16[256,512]{1,0:T(8,128)(2,1)} %slice.4.refs_4_), channel_id=1, source_target_pairs={{0,6},{1,7},{2,4},{3,5},{4,2},{5,3},{6,0},{7,1},{8,14},{9,15},{10,... | collective-permute-start | bytes 786440 | tf_op jit(solution)/shard_map/ppermute | solution.py:448
  87.1 8.3 %collective-permute-start.2 = (bf16[256,512]{1,0:T(8,128)(2,1)S(1)}, bf16[256,512]{1,0:T(8,128)(2,1)S(1)}, u32[]{:S(2)}, u32[]{:S(2)}) collective-permute-start(bf16[256,512]{1,0:T(8,128)(2,1)S(1)} %get-tuple-element.70), channel_id=1, source_target_pairs={{0,1},{1,0},{2,3},{3,2},{4,5},{5,4},{6,7},{7,6},{8,9},{9,8},{10,11... | collective-permute-start | bytes 786440 | tf_op jit(solution)/shard_map/ppermute | solution.py:448
  88.5 8.2 %collective-permute-start.5 = (bf16[256,512]{1,0:T(8,128)(2,1)S(1)}, bf16[256,512]{1,0:T(8,128)(2,1)S(1)}, u32[]{:S(2)}, u32[]{:S(2)}) collective-permute-start(bf16[256,512]{1,0:T(8,128)(2,1)S(1)} %get-tuple-element.80), channel_id=1, source_target_pairs={{0,1},{1,0},{2,3},{3,2},{4,5},{5,4},{6,7},{7,6},{8,9},{9,8},{10,11... | collective-permute-start | bytes 786440 | tf_op jit(solution)/shard_map/ppermute | solution.py:448
  89.1 18.0 %copy-start = (bf16[256,1536]{1,0:T(8,128)(2,1)S(1)}, bf16[256,1536]{1,0:T(8,128)(2,1)}, u32[]{:S(2)}) copy-start(bf16[256,1536]{1,0:T(8,128)(2,1)} %get-tuple-element.92.refs_0_.refs_1_.refs_2_.refs_3_) | copy-start | bytes 2359300
  89.1 11.8 %collective-permute-start.9 = (bf16[256,512]{1,0:T(8,128)(2,1)S(1)}, bf16[256,512]{1,0:T(8,128)(2,1)S(1)}, u32[]{:S(2)}, u32[]{:S(2)}) collective-permute-start(bf16[256,512]{1,0:T(8,128)(2,1)S(1)} %get-tuple-element.83), channel_id=1, source_target_pairs={{0,6},{1,7},{2,4},{3,5},{4,2},{5,3},{6,0},{7,1},{8,14},{9,15},{10,... | collective-permute-start | bytes 786440 | tf_op jit(solution)/shard_map/ppermute | solution.py:448
  92.9 12.4 %collective-permute-start.14 = (bf16[256,512]{1,0:T(8,128)(2,1)}, bf16[256,512]{1,0:T(8,128)(2,1)}, u32[]{:S(2)}, u32[]{:S(2)}) collective-permute-start(bf16[256,512]{1,0:T(8,128)(2,1)} %slice.4.refs_4_), channel_id=1, source_target_pairs={{0,1},{1,0},{2,3},{3,2},{4,5},{5,4},{6,7},{7,6},{8,9},{9,8},{10,11... | collective-permute-start | bytes 786440 | tf_op jit(solution)/shard_map/ppermute | solution.py:448
  95.3 10.5 %collective-permute-start.13 = (bf16[256,512]{1,0:T(8,128)(2,1)}, bf16[256,512]{1,0:T(8,128)(2,1)}, u32[]{:S(2)}, u32[]{:S(2)}) collective-permute-start(bf16[256,512]{1,0:T(8,128)(2,1)} %get-tuple-element.94), channel_id=1, source_target_pairs={{0,1},{1,0},{2,3},{3,2},{4,5},{5,4},{6,7},{7,6},{8,9},{9,8},{10,11... | collective-permute-start | bytes 786440 | tf_op jit(solution)/shard_map/ppermute | solution.py:448
  95.3 13.5 %collective-permute-start.20 = (bf16[256,512]{1,0:T(8,128)(2,1)}, bf16[256,512]{1,0:T(8,128)(2,1)}, u32[]{:S(2)}, u32[]{:S(2)}) collective-permute-start(bf16[256,512]{1,0:T(8,128)(2,1)} %slice.4.refs_4_), channel_id=1, source_target_pairs={{0,4},{1,5},{2,6},{3,7},{4,0},{5,1},{6,2},{7,3},{8,12},{9,13},{10,... | collective-permute-start | bytes 786440 | tf_op jit(solution)/shard_map/ppermute | solution.py:448
  97.5 11.5 %collective-permute-start.18 = (bf16[256,512]{1,0:T(8,128)(2,1)}, bf16[256,512]{1,0:T(8,128)(2,1)}, u32[]{:S(2)}, u32[]{:S(2)}) collective-permute-start(bf16[256,512]{1,0:T(8,128)(2,1)} %slice.4.refs_4_), channel_id=1, source_target_pairs={{0,2},{1,3},{2,0},{3,1},{4,6},{5,7},{6,4},{7,5},{8,10},{9,11},{10,... | collective-permute-start | bytes 786440 | tf_op jit(solution)/shard_map/ppermute | solution.py:448
  101.6 7.8 %collective-permute-start.16 = (bf16[256,512]{1,0:T(8,128)(2,1)}, bf16[256,512]{1,0:T(8,128)(2,1)}, u32[]{:S(2)}, u32[]{:S(2)}) collective-permute-start(bf16[256,512]{1,0:T(8,128)(2,1)} %collective-permute-done.15.refs_6_), channel_id=1, source_target_pairs={{0,1},{1,0},{2,3},{3,2},{4,5},{5,4},{6,7},{7,6},{8,9},{9,8},{10,11... | collective-permute-start | bytes 786440 | tf_op jit(solution)/shard_map/ppermute | solution.py:448
  104.7 4.7 %copy-start.4 = (bf16[1536,256]{1,0:T(8,128)(2,1)S(1)}, bf16[1536,256]{1,0:T(8,128)(2,1)}, u32[]{:S(2)}) copy-start(bf16[1536,256]{1,0:T(8,128)(2,1)} %copy-done.3) | copy-start | bytes 2359300
  104.7 4.7 %copy-start.6 = (bf16[1536,256]{1,0:T(8,128)(2,1)S(1)}, bf16[1536,256]{1,0:T(8,128)(2,1)}, u32[]{:S(2)}) copy-start(bf16[1536,256]{1,0:T(8,128)(2,1)} %copy-done.5) | copy-start | bytes 2359300
  104.7 4.7 %copy-start.8 = (bf16[1536,256]{1,0:T(8,128)(2,1)S(1)}, bf16[1536,256]{1,0:T(8,128)(2,1)}, u32[]{:S(2)}) copy-start(bf16[1536,256]{1,0:T(8,128)(2,1)} %copy-done.7) | copy-start | bytes 2359300
  105.3 9.0 %copy-start.16 = (bf16[1,256,1024]{2,1,0:T(8,128)(2,1)S(1)}, bf16[1,256,1024]{2,1,0:T(8,128)(2,1)}, u32[]{:S(2)}) copy-start(bf16[1,256,1024]{2,1,0:T(8,128)(2,1)} %param.10) | copy-start | bytes 1572868
  105.3 9.0 %copy-start.22 = (bf16[256,512]{1,0:T(8,128)(2,1)S(1)}, bf16[256,512]{1,0:T(8,128)(2,1)}, u32[]{:S(2)}) copy-start(bf16[256,512]{1,0:T(8,128)(2,1)} %copy-done.21) | copy-start | bytes 786436
  105.3 9.0 %collective-permute-start.10 = (bf16[256,512]{1,0:T(8,128)(2,1)}, bf16[256,512]{1,0:T(8,128)(2,1)S(1)}, u32[]{:S(2)}, u32[]{:S(2)}) collective-permute-start(bf16[256,512]{1,0:T(8,128)(2,1)} %copy-done.25), channel_id=1, source_target_pairs={{0,2},{1,3},{2,0},{3,1},{4,6},{5,7},{6,4},{7,5},{8,10},{9,11},{10,... | collective-permute-start | bytes 786440 | tf_op jit(solution)/shard_map/ppermute | solution.py:448
  105.8 8.5 %collective-permute-start.11 = (bf16[256,512]{1,0:T(8,128)(2,1)S(1)}, bf16[256,512]{1,0:T(8,128)(2,1)S(1)}, u32[]{:S(2)}, u32[]{:S(2)}) collective-permute-start(bf16[256,512]{1,0:T(8,128)(2,1)S(1)} %get-tuple-element.91), channel_id=1, source_target_pairs={{0,4},{1,5},{2,6},{3,7},{4,0},{5,1},{6,2},{7,3},{8,12},{9,13},{10,... | collective-permute-start | bytes 786440 | tf_op jit(solution)/shard_map/ppermute | solution.py:448
  107.1 11.4 %copy-start.10 = (bf16[1536,256]{1,0:T(8,128)(2,1)S(1)}, bf16[1536,256]{1,0:T(8,128)(2,1)}, u32[]{:S(2)}) copy-start(bf16[1536,256]{1,0:T(8,128)(2,1)} %copy-done.9) | copy-start | bytes 2359300
  107.1 11.4 %copy-start.12 = (bf16[1536,256]{1,0:T(8,128)(2,1)S(1)}, bf16[1536,256]{1,0:T(8,128)(2,1)}, u32[]{:S(2)}) copy-start(bf16[1536,256]{1,0:T(8,128)(2,1)} %copy-done.11) | copy-start | bytes 2359300
  107.1 11.4 %copy-start.14 = (bf16[1536,256]{1,0:T(8,128)(2,1)S(1)}, bf16[1536,256]{1,0:T(8,128)(2,1)}, u32[]{:S(2)}) copy-start(bf16[1536,256]{1,0:T(8,128)(2,1)} %copy-done.13) | copy-start | bytes 2359300
  107.1 43.7 %slice-start.4 = ((s8[6291456]{0:T(1024)(128)(4,1)}), s8[4194304]{0:T(1024)(128)(4,1)S(1)}, s32[]{:S(2)}) async-start(s8[6291456]{0:T(1024)(128)(4,1)} %bitcast.40), calls=%async_computation.6 | async-start | bytes 8388608
  108.8 9.6 %collective-permute-start.21 = (bf16[256,512]{1,0:T(8,128)(2,1)}, bf16[256,512]{1,0:T(8,128)(2,1)S(1)}, u32[]{:S(2)}, u32[]{:S(2)}) collective-permute-start(bf16[256,512]{1,0:T(8,128)(2,1)} %collective-permute-done.20.refs_6_), channel_id=1, source_target_pairs={{0,1},{1,0},{2,3},{3,2},{4,5},{5,4},{6,7},{7,6},{8,9},{9,8},{10,11... | collective-permute-start | bytes 786440 | tf_op jit(solution)/shard_map/ppermute | solution.py:448
  108.9 9.5 %collective-permute-start.19 = (bf16[256,512]{1,0:T(8,128)(2,1)}, bf16[256,512]{1,0:T(8,128)(2,1)S(1)}, u32[]{:S(2)}, u32[]{:S(2)}) collective-permute-start(bf16[256,512]{1,0:T(8,128)(2,1)} %collective-permute-done.18.refs_4_), channel_id=1, source_target_pairs={{0,1},{1,0},{2,3},{3,2},{4,5},{5,4},{6,7},{7,6},{8,9},{9,8},{10,11... | collective-permute-start | bytes 786440 | tf_op jit(solution)/shard_map/ppermute | solution.py:448
  114.9 10.2 %collective-permute-start.26 = (bf16[256,512]{1,0:T(8,128)(2,1)S(1)}, bf16[256,512]{1,0:T(8,128)(2,1)S(1)}, u32[]{:S(2)}, u32[]{:S(2)}) collective-permute-start(bf16[256,512]{1,0:T(8,128)(2,1)S(1)} %key_backward.1.refs_4_), channel_id=1, source_target_pairs={{0,6},{1,7},{2,4},{3,5},{4,2},{5,3},{6,0},{7,1},{8,14},{9,15},{10,... | collective-permute-start | bytes 786440 | tf_op jit(solution)/shard_map/ppermute | solution.py:448
  116.3 13.1 %collective-permute-start.23 = (bf16[256,512]{1,0:T(8,128)(2,1)S(1)}, bf16[256,512]{1,0:T(8,128)(2,1)S(1)}, u32[]{:S(2)}, u32[]{:S(2)}) collective-permute-start(bf16[256,512]{1,0:T(8,128)(2,1)S(1)} %key_backward.1.refs_4_), channel_id=1, source_target_pairs={{0,4},{1,5},{2,6},{3,7},{4,0},{5,1},{6,2},{7,3},{8,12},{9,13},{10,... | collective-permute-start | bytes 786440 | tf_op jit(solution)/shard_map/ppermute | solution.py:448
  117.9 11.5 %collective-permute-start.17 = (bf16[256,512]{1,0:T(8,128)(2,1)S(1)}, bf16[256,512]{1,0:T(8,128)(2,1)S(1)}, u32[]{:S(2)}, u32[]{:S(2)}) collective-permute-start(bf16[256,512]{1,0:T(8,128)(2,1)S(1)} %key_backward.1.refs_4_), channel_id=1, source_target_pairs={{0,2},{1,3},{2,0},{3,1},{4,6},{5,7},{6,4},{7,5},{8,10},{9,11},{10,... | collective-permute-start | bytes 786440 | tf_op jit(solution)/shard_map/ppermute | solution.py:448
  118.5 32.3 %slice-start.5 = ((s8[6291456]{0:T(1024)(128)(4,1)}), s8[2097152]{0:T(1024)(128)(4,1)S(1)}, s32[]{:S(2)}) async-start(s8[6291456]{0:T(1024)(128)(4,1)} %bitcast.40), calls=%async_computation.7 | async-start | bytes 4194304
  123.2 6.7 %collective-permute-start.25 = (bf16[256,512]{1,0:T(8,128)(2,1)S(1)}, bf16[256,512]{1,0:T(8,128)(2,1)S(1)}, u32[]{:S(2)}, u32[]{:S(2)}) collective-permute-start(bf16[256,512]{1,0:T(8,128)(2,1)S(1)} %key_backward.1.refs_4_), channel_id=1, source_target_pairs={{0,1},{1,0},{2,3},{3,2},{4,5},{5,4},{6,7},{7,6},{8,9},{9,8},{10,11... | collective-permute-start | bytes 786440 | tf_op jit(solution)/shard_map/ppermute | solution.py:448
  125.1 19.0 %copy-start.18 = (f32[4,384,128]{2,1,0:T(8,128)S(1)}, f32[4,384,128]{2,1,0:T(8,128)}, u32[]{:S(2)}) copy-start(f32[4,384,128]{2,1,0:T(8,128)} %copy-done.17) | copy-start | bytes 2359300
  125.1 19.0 %copy-start.20 = (f32[4,384,128]{2,1,0:T(8,128)S(1)}, f32[4,384,128]{2,1,0:T(8,128)}, u32[]{:S(2)}) copy-start(f32[4,384,128]{2,1,0:T(8,128)} %copy-done.19) | copy-start | bytes 2359300
  125.1 4.8 %collective-permute-start.27 = (bf16[256,512]{1,0:T(8,128)(2,1)S(1)}, bf16[256,512]{1,0:T(8,128)(2,1)S(1)}, u32[]{:S(2)}, u32[]{:S(2)}) collective-permute-start(bf16[256,512]{1,0:T(8,128)(2,1)S(1)} %collective-permute-done.26.refs_6_), channel_id=1, source_target_pairs={{0,1},{1,0},{2,3},{3,2},{4,5},{5,4},{6,7},{7,6},{8,9},{9,8},{10,11... | collective-permute-start | bytes 786440 | tf_op jit(solution)/shard_map/ppermute | solution.py:448
  129.4 3.7 %collective-permute-start.24 = (bf16[256,512]{1,0:T(8,128)(2,1)S(1)}, bf16[256,512]{1,0:T(8,128)(2,1)S(1)}, u32[]{:S(2)}, u32[]{:S(2)}) collective-permute-start(bf16[256,512]{1,0:T(8,128)(2,1)S(1)} %collective-permute-done.23.refs_6_), channel_id=1, source_target_pairs={{0,1},{1,0},{2,3},{3,2},{4,5},{5,4},{6,7},{7,6},{8,9},{9,8},{10,11... | collective-permute-start | bytes 786440 | tf_op jit(solution)/shard_map/ppermute | solution.py:448
  129.4 3.7 %collective-permute-start.22 = (bf16[256,512]{1,0:T(8,128)(2,1)S(1)}, bf16[256,512]{1,0:T(8,128)(2,1)S(1)}, u32[]{:S(2)}, u32[]{:S(2)}) collective-permute-start(bf16[256,512]{1,0:T(8,128)(2,1)S(1)} %collective-permute-done.17.refs_4_), channel_id=1, source_target_pairs={{0,1},{1,0},{2,3},{3,2},{4,5},{5,4},{6,7},{7,6},{8,9},{9,8},{10,11... | collective-permute-start | bytes 786440 | tf_op jit(solution)/shard_map/ppermute | solution.py:448
  129.9 20.8 %slice-start = ((s8[6291456]{0:T(1024)(128)(4,1)}), s8[4194304]{0:T(1024)(128)(4,1)S(1)}, s32[]{:S(2)}) async-start(s8[6291456]{0:T(1024)(128)(4,1)} %bitcast.24), calls=%async_computation.2 | async-start | bytes 8388608
  129.9 20.8 %slice-start.2 = ((s8[6291456]{0:T(1024)(128)(4,1)}), s8[4194304]{0:T(1024)(128)(4,1)S(1)}, s32[]{:S(2)}) async-start(s8[6291456]{0:T(1024)(128)(4,1)} %bitcast.32), calls=%async_computation.4 | async-start | bytes 8388608
  133.1 17.6 %slice-start.1 = ((s8[6291456]{0:T(1024)(128)(4,1)}), s8[2097152]{0:T(1024)(128)(4,1)S(1)}, s32[]{:S(2)}) async-start(s8[6291456]{0:T(1024)(128)(4,1)} %bitcast.24), calls=%async_computation.3 | async-start | bytes 4194304
  133.2 17.6 %slice-start.3 = ((s8[6291456]{0:T(1024)(128)(4,1)}), s8[2097152]{0:T(1024)(128)(4,1)S(1)}, s32[]{:S(2)}) async-start(s8[6291456]{0:T(1024)(128)(4,1)} %bitcast.32), calls=%async_computation.5 | async-start | bytes 4194304
  136.8 1.2 collective-permute-start.28
  138.0 4.5 %collective-permute-start.31 = (f32[8,128]{1,0:T(8,128)S(1)}, f32[8,128]{1,0:T(8,128)S(1)}, u32[]{:S(2)}, u32[]{:S(2)}) collective-permute-start(f32[8,128]{1,0:T(8,128)S(1)} %add.22.refs_0_), channel_id=1, source_target_pairs={{0,6},{1,7},{2,4},{3,5},{4,2},{5,3},{6,0},{7,1},{8,14},{9,15},{10,... | collective-permute-start | bytes 12296 | tf_op jit(solution)/shard_map/ppermute | solution.py:448
  139.7 3.6 %collective-permute-start.30 = (f32[8,128]{1,0:T(8,128)S(1)}, f32[8,128]{1,0:T(8,128)S(1)}, u32[]{:S(2)}, u32[]{:S(2)}) collective-permute-start(f32[8,128]{1,0:T(8,128)S(1)} %add.22.refs_0_), channel_id=1, source_target_pairs={{0,4},{1,5},{2,6},{3,7},{4,0},{5,1},{6,2},{7,3},{8,12},{9,13},{10,... | collective-permute-start | bytes 12296 | tf_op jit(solution)/shard_map/ppermute | solution.py:448
  140.5 3.6 %collective-permute-start.29 = (f32[8,128]{1,0:T(8,128)S(1)}, f32[8,128]{1,0:T(8,128)S(1)}, u32[]{:S(2)}, u32[]{:S(2)}) collective-permute-start(f32[8,128]{1,0:T(8,128)S(1)} %add.22.refs_0_), channel_id=1, source_target_pairs={{0,2},{1,3},{2,0},{3,1},{4,6},{5,7},{6,4},{7,5},{8,10},{9,11},{10,... | collective-permute-start | bytes 12296 | tf_op jit(solution)/shard_map/ppermute | solution.py:448
  146.2 10.6 %collective-permute-start.32 = (bf16[384,128]{1,0:T(8,128)(2,1)S(1)}, bf16[384,128]{1,0:T(8,128)(2,1)S(1)}, u32[]{:S(2)}, u32[]{:S(2)}) collective-permute-start(bf16[384,128]{1,0:T(8,128)(2,1)S(1)} %get-tuple-element.118), channel_id=1, source_target_pairs={{0,8},{8,0},{16,24},{24,16},{1,9},{9,1},{17,25},{25,17},{2,10},{10... | collective-permute-start | bytes 294920 | tf_op jit(solution)/shard_map/ppermute | solution.py:448
  148.3 9.1 %collective-permute-start.33 = (bf16[384,128]{1,0:T(8,128)(2,1)S(1)}, bf16[384,128]{1,0:T(8,128)(2,1)S(1)}, u32[]{:S(2)}, u32[]{:S(2)}) collective-permute-start(bf16[384,128]{1,0:T(8,128)(2,1)S(1)} %get-tuple-element.119), channel_id=1, source_target_pairs={{0,16},{8,24},{16,0},{24,8},{1,17},{9,25},{17,1},{25,9},{2,18},{10... | collective-permute-start | bytes 294920 | tf_op jit(solution)/shard_map/ppermute | solution.py:448
  150.7 6.8 %collective-permute-start.34 = (bf16[384,128]{1,0:T(8,128)(2,1)S(1)}, bf16[384,128]{1,0:T(8,128)(2,1)S(1)}, u32[]{:S(2)}, u32[]{:S(2)}) collective-permute-start(bf16[384,128]{1,0:T(8,128)(2,1)S(1)} %get-tuple-element.120), channel_id=1, source_target_pairs={{0,24},{8,16},{16,8},{24,0},{1,25},{9,17},{17,9},{25,1},{2,26},{10... | collective-permute-start | bytes 294920 | tf_op jit(solution)/shard_map/ppermute | solution.py:448
  150.8 11.2 %copy-start.27 = (f32[384,128]{1,0:T(8,128)S(1)}, f32[384,128]{1,0:T(8,128)}, u32[]{:S(2)}) copy-start(f32[384,128]{1,0:T(8,128)} %copy-done.26) | copy-start | bytes 589828
  157.5 10.5 %collective-permute-start.37 = (bf16[384,128]{1,0:T(8,128)(2,1)S(1)}, bf16[384,128]{1,0:T(8,128)(2,1)S(1)}, u32[]{:S(2)}, u32[]{:S(2)}) collective-permute-start(bf16[384,128]{1,0:T(8,128)(2,1)S(1)} %convert_element_type.24.refs_4_), channel_id=1, source_target_pairs={{0,24},{8,16},{16,8},{24,0},{1,25},{9,17},{17,9},{25,1},{2,26},{10... | collective-permute-start | bytes 294920 | tf_op jit(solution)/shard_map/ppermute | solution.py:448
  160.7 7.3 %collective-permute-start.36 = (bf16[384,128]{1,0:T(8,128)(2,1)S(1)}, bf16[384,128]{1,0:T(8,128)(2,1)S(1)}, u32[]{:S(2)}, u32[]{:S(2)}) collective-permute-start(bf16[384,128]{1,0:T(8,128)(2,1)S(1)} %convert_element_type.24.refs_4_), channel_id=1, source_target_pairs={{0,16},{8,24},{16,0},{24,8},{1,17},{9,25},{17,1},{25,9},{2,18},{10... | collective-permute-start | bytes 294920 | tf_op jit(solution)/shard_map/ppermute | solution.py:448
  160.8 7.3 %collective-permute-start.35 = (bf16[384,128]{1,0:T(8,128)(2,1)S(1)}, bf16[384,128]{1,0:T(8,128)(2,1)S(1)}, u32[]{:S(2)}, u32[]{:S(2)}) collective-permute-start(bf16[384,128]{1,0:T(8,128)(2,1)S(1)} %convert_element_type.24.refs_4_), channel_id=1, source_target_pairs={{0,8},{8,0},{16,24},{24,16},{1,9},{9,1},{17,25},{25,17},{2,10},{10... | collective-permute-start | bytes 294920 | tf_op jit(solution)/shard_map/ppermute | solution.py:448
  (11 other events, 9.3 us)

commit v15 on v13

--- a/solution.py
+++ b/solution.py
@@ -514,7 +514,7 @@
         theirs, flipped[k + 1] = partial_keys(blocks[k + 1], key_weights)
         theirs = swap(theirs, "fsdp", 1)
         if k == last:
-            theirs = after(theirs, *parts[:1], *base)
+            theirs = after(theirs, *parts[:1], pseudo_old)
         part_k, flipped[k] = partial_keys(blocks[k], key_weights, theirs)
         parts.append(swap(part_k, "fsdp", k) if k else part_k)
     spread = [0, 1] + [k + odd for k in far for odd in range(2)]
@@ -536,7 +536,7 @@
     for k in rest[::2]:
         keys[k + 1] = swap(after(keys[k], square), "fsdp", 1)
     grad_keys, square, due = gradient(
-        place, pick(flipped, rest), pick(keys, rest), keys_first, square, due
+        after(place, *base), pick(flipped, rest), pick(keys, rest), keys_first, square, due
     )
 
     square = square + swap(square, "fsdp", 1)

time: 169 us -> 172 us (1.018)
  waiting for transfers between devices: 55.8 us -> 65 us
  starting transfers between devices: 49.7 us -> 42.9 us
    ppermute x44, waiting for transfers between devices: 55.8 us -> 65 us  [swap(): return lax.ppermute(block, axis, [(i, i ^ offset) for i in range(count)])]
    ppermute x44, starting transfers between devices: 49.7 us -> 42.9 us  [swap(): return lax.ppermute(block, axis, [(i, i ^ offset) for i in range(count)])]
  transfers between devices with their start and end apart: 44 -> 44, of which waited for: 14 -> 16; matrix products, arithmetic and copies ran while one was open for 1% -> 0% of each run, Pallas kernels for 29% -> 28%
where the time goes in v15:
time: 172 us; the launch traced here: 171 us
  waiting for transfers between devices  65 us (38%)
  Pallas kernels  58.1 us (34%)
  starting transfers between devices  42.9 us (25%)
  between operations  3.8 us (2%)
    ppermute x44, waiting for transfers between devices, swap(): return lax.ppermute(block, axis, [(i, i ^ offset) for i in range(count)])  65 us
    ppermute x44, starting transfers between devices, swap(): return lax.ppermute(block, axis, [(i, i ^ offset) for i in range(count)])  42.9 us
    pallas_call x4, Pallas kernels, gradient(): pl.pallas_call(functools.partial(grad_kernel, len(flipped), base is not N...  13.5 us
    pallas_call x2, Pallas kernels, adam_rows(): pl.pallas_call(functools.partial(adam_kernel, len(squares), len(into)), o...  12 us
    pallas_call x4, Pallas kernels, pack(): pl.pallas_call(functools.partial(pack_kernel, offsets), out_shape=[pltpu....  9.23 us
    pallas_call x8, Pallas kernels, partial_keys(): pl.pallas_call(functools.partial(partial_kernel, pieces), out_shape=[jax....  7.05 us
    pallas_call x3, Pallas kernels, due_columns(): pl.pallas_call(functools.partial(pick_kernel, blocks), out_shape=[jax.Sha...  5.56 us
    pallas_call x1, Pallas kernels, cast_left(): pl.pallas_call(cast_kernel, out_shape=jax.ShapeDtypeStruct((rows, width),...  3.47 us
  transfers between devices with their start and end apart: 44, of which 16 were waited for; matrix products, arithmetic and copies ran while one was open for 0% of the time, Pallas kernels for 28%

profile of v15, /device:TPU:0, one launch (start us, length us, event | category | flops | bytes accessed | tf_op | source)
XLA Modules:
  0.0 171.1 jit_solution(17774251148374829502)
XLA Ops:
  0.6 2.0 %pack.4 = bf16[256,1536]{1,0:T(8,128)(2,1)} custom-call(s32[1]{0:T(128)} %bitcast.6.me_ref, bf16[256,12288]{1,0:T(8,128)(2,1)} %bitcast.64), custom_call_target="tpu_custom_call" | custom-call | bytes 1572864 | tf_op jit(solution)/shard_map/pack/pallas_call | solution.py:69
  2.6 4.0 %collective-permute-start = (bf16[256,1536]{1,0:T(8,128)(2,1)}, bf16[256,1536]{1,0:T(8,128)(2,1)S(1)}, u32[]{:S(2)}, u32[]{:S(2)}) collective-permute-start(bf16[256,1536]{1,0:T(8,128)(2,1)} %pack.4), channel_id=1, source_target_pairs={{0,6},{1,7},{2,4},{3,5},{4,2},{5,3},{6,0},{7,1},{8,14},{9,15},{10,... | collective-permute-start | bytes 2359304 | tf_op jit(solution)/shard_map/ppermute | solution.py:447
  6.6 2.6 %pack.5 = (bf16[256,1536]{1,0:T(8,128)(2,1)}, bf16[256,1536]{1,0:T(8,128)(2,1)}, bf16[256,1536]{1,0:T(8,128)(2,1)}) custom-call(s32[1]{0:T(128)} %bitcast.6.me_ref, bf16[256,12288]{1,0:T(8,128)(2,1)} %bitcast.65), custom_call_target="tpu_custom_call" | custom-call | bytes 4718592 | tf_op jit(solution)/shard_map/pack/pallas_call | solution.py:69
  9.3 2.3 %pack.6 = (bf16[256,1536]{1,0:T(8,128)(2,1)}, bf16[256,1536]{1,0:T(8,128)(2,1)}) custom-call(s32[1]{0:T(128)} %bitcast.6.me_ref, bf16[256,12288]{1,0:T(8,128)(2,1)} %bitcast.66), custom_call_target="tpu_custom_call" | custom-call | bytes 3145728 | tf_op jit(solution)/shard_map/pack/pallas_call | solution.py:69
  11.6 1.7 %collective-permute-start.8 = (bf16[256,1536]{1,0:T(8,128)(2,1)}, bf16[256,1536]{1,0:T(8,128)(2,1)}, u32[]{:S(2)}, u32[]{:S(2)}) collective-permute-start(bf16[256,1536]{1,0:T(8,128)(2,1)} %get-tuple-element.74), channel_id=1, source_target_pairs={{0,3},{1,2},{2,1},{3,0},{4,7},{5,6},{6,5},{7,4},{8,11},{9,10},{10,... | collective-permute-start | bytes 2359304 | tf_op jit(solution)/shard_map/ppermute | solution.py:447
  13.3 0.7 collective-permute-start.11
  14.0 2.3 %pack.7 = (bf16[256,1536]{1,0:T(8,128)(2,1)}, bf16[256,1536]{1,0:T(8,128)(2,1)}) custom-call(s32[1]{0:T(128)} %bitcast.6.me_ref, bf16[256,12288]{1,0:T(8,128)(2,1)} %bitcast.67), custom_call_target="tpu_custom_call" | custom-call | bytes 3145728 | tf_op jit(solution)/shard_map/pack/pallas_call | solution.py:69
  16.3 1.0 collective-permute-start.18
  17.4 7.9 %collective-permute-done.refs_0_.refs_1_.refs_2_.refs_3_ = bf16[256,1536]{1,0:T(8,128)(2,1)S(1)} collective-permute-done((bf16[256,1536]{1,0:T(8,128)(2,1)}, bf16[256,1536]{1,0:T(8,128)(2,1)S(1)}, u32[]{:S(2)}, u32[]{:S(2)}) %collective-permute-start) | collective-permute-done | bytes 786464 | tf_op jit(solution)/shard_map/ppermute | solution.py:447
  25.3 2.0 %collective-permute-start.7 = (bf16[256,1536]{1,0:T(8,128)(2,1)}, bf16[256,1536]{1,0:T(8,128)(2,1)S(1)}, u32[]{:S(2)}, u32[]{:S(2)}) collective-permute-start(bf16[256,1536]{1,0:T(8,128)(2,1)} %get-tuple-element.73), channel_id=1, source_target_pairs={{0,2},{1,3},{2,0},{3,1},{4,6},{5,7},{6,4},{7,5},{8,10},{9,11},{10,... | collective-permute-start | bytes 2359304 | tf_op jit(solution)/shard_map/ppermute | solution.py:447
  27.3 14.5 %collective-permute-done.13.refs_0_.refs_1_.refs_2_.refs_3_ = bf16[256,1536]{1,0:T(8,128)(2,1)S(1)} collective-permute-done((bf16[256,1536]{1,0:T(8,128)(2,1)}, bf16[256,1536]{1,0:T(8,128)(2,1)S(1)}, u32[]{:S(2)}, u32[]{:S(2)}) %collective-permute-start.13) | collective-permute-done | bytes 786464 | tf_op jit(solution)/shard_map/ppermute | solution.py:447
  41.7 0.9 copy-done.1
  43.9 3.5 %cast_left.1.refs_4_ = bf16[1536,512]{1,0:T(8,128)(2,1)S(1)} custom-call(f32[1536,1024]{1,0:T(8,128)} %bitcast.35), custom_call_target="tpu_custom_call" | custom-call | bytes 4718592 | tf_op jit(solution)/shard_map/cast_left/pallas_call | solution.py:93
  47.3 0.6 partial_keys.11
  47.9 10.7 %collective-permute-done.8.refs_0_.refs_1_.refs_2_.refs_3_ = bf16[256,1536]{1,0:T(8,128)(2,1)} collective-permute-done((bf16[256,1536]{1,0:T(8,128)(2,1)}, bf16[256,1536]{1,0:T(8,128)(2,1)}, u32[]{:S(2)}, u32[]{:S(2)}) %collective-permute-start.8) | collective-permute-done | bytes 786464 | tf_op jit(solution)/shard_map/ppermute | solution.py:447
  58.6 1.0 collective-permute-start.14
  60.6 1.8 %due_columns.4.w_ref = f32[4,384,128]{2,1,0:T(8,128)S(1)} custom-call(s32[2]{0:T(128)S(1)} %pad_add_fusion.place_ref, f32[1536,1024]{1,0:T(8,128)} %bitcast.36, f32[1536,1024]{1,0:T(8,128)} %bitcast.37, f32[1536,1024]{1,0:T(8,128)} %bitcast.38, f32[1536,1024]{1,0:T(8,128)} %bitcast.39), custom_call_target="tpu_custom_call" | custom-call | bytes 1572864 | tf_op jit(solution)/shard_map/due_columns/pallas_call | solution.py:345
  62.5 1.6 collective-permute-start.1
  64.1 2.5 %collective-permute-start.3 = (f32[384,128]{1,0:T(8,128)S(1)}, f32[384,128]{1,0:T(8,128)S(1)}, u32[]{:S(2)}, u32[]{:S(2)}) collective-permute-start(f32[384,128]{1,0:T(8,128)S(1)} %get-tuple-element.135), channel_id=1, source_target_pairs={{0,24},{8,16},{16,8},{24,0},{1,25},{9,17},{17,9},{25,1},{2,26},{10... | collective-permute-start | bytes 589832 | tf_op jit(solution)/shard_map/ppermute | solution.py:447
  66.7 2.1 %due_columns.5 = (f32[4,384,128]{2,1,0:T(8,128)S(1)}, f32[4,384,128]{2,1,0:T(8,128)S(1)}) custom-call(s32[2]{0:T(128)S(1)} %pad_add_fusion.place_ref, f32[1536,1024]{1,0:T(8,128)} %bitcast.44, f32[1536,1024]{1,0:T(8,128)} %bitcast.45, f32[1536,1024]{1,0:T(8,128)} %bitcast.46, f32[1536,1024]{1,0:T(8,128)} %bitcast.47, f32[1536,1024]{1,0:T(8,128)} %bitcast.52, ...), custom_call_target="tpu_custom_call" | custom-call | bytes 3145728 | tf_op jit(solution)/shard_map/due_columns/pallas_call | solution.py:345
  68.8 2.8 %duplicate.1 = (f32[384,1024]{1,0:T(8,128)}, f32[384,1024]{1,0:T(8,128)}) custom-call(f32[384,1024]{1,0:T(8,128)} %refs_0_.3, f32[384,1024]{1,0:T(8,128)} %refs_1_.3), custom_call_target="tpu_custom_call" | custom-call | bytes 6291456 | tf_op jit(solution)/shard_map/duplicate/pallas_call | solution.py:386
  71.6 1.8 %partial_keys.10 = (bf16[256,512]{1,0:T(8,128)(2,1)S(1)}, bf16[1536,256]{1,0:T(8,128)(2,1)S(1)}) custom-call(bf16[256,1536]{1,0:T(8,128)(2,1)} %collective-permute-done.11.refs_0_.refs_1_.refs_2_.refs_3_, bf16[256,1536]{1,0:T(8,128)(2,1)} %collective-permute-done.11.refs_0_.refs_1_.refs_2_.refs_3_, ...), custom_call_target="tpu_custom_call" | custom-call | flops 402653184 | bytes 1572864 | tf_op jit(solution)/shard_map/partial_keys/pallas_call | solution.py:122
  73.4 1.8 %partial_keys.8 = (bf16[256,512]{1,0:T(8,128)(2,1)S(1)}, bf16[1536,256]{1,0:T(8,128)(2,1)S(1)}) custom-call(bf16[256,1536]{1,0:T(8,128)(2,1)} %collective-permute-done.8.refs_0_.refs_1_.refs_2_.refs_3_, bf16[256,1536]{1,0:T(8,128)(2,1)} %collective-permute-done.8.refs_0_.refs_1_.refs_2_.refs_3_, ...), custom_call_target="tpu_custom_call" | custom-call | flops 402653184 | bytes 1572864 | tf_op jit(solution)/shard_map/partial_keys/pallas_call | solution.py:122
  75.2 0.6 partial_keys.12
  75.8 1.5 collective-permute-start.21
  77.8 1.5 collective-permute-start.15
  79.3 0.9 collective-permute-start.2
  80.2 1.6 due_columns.3
  81.8 0.6 partial_keys.14
  82.4 8.6 %collective-permute-done.2 = f32[384,128]{1,0:T(8,128)S(1)} collective-permute-done((f32[384,128]{1,0:T(8,128)S(1)}, f32[384,128]{1,0:T(8,128)S(1)}, u32[]{:S(2)}, u32[]{:S(2)}) %collective-permute-start.2) | collective-permute-done | bytes 196640 | tf_op jit(solution)/shard_map/ppermute | solution.py:447
  92.1 1.5 collective-permute-start.24
  93.7 0.6 partial_keys.9
  94.3 0.6 partial_keys.13
  94.8 0.6 collective-permute-start.16
  95.5 1.5 collective-permute-start.17
  97.0 0.6 partial_keys.15
  97.6 3.2 %collective-permute-done.26.refs_6_ = bf16[256,512]{1,0:T(8,128)(2,1)S(1)} collective-permute-done((bf16[256,512]{1,0:T(8,128)(2,1)S(1)}, bf16[256,512]{1,0:T(8,128)(2,1)S(1)}, u32[]{:S(2)}, u32[]{:S(2)}) %collective-permute-start.26) | collective-permute-done | bytes 262176 | tf_op jit(solution)/shard_map/ppermute | solution.py:447
  100.7 0.5 collective-permute-done.24.refs_4_
  101.3 3.2 %gradient.4.refs_8_ = f32[1536,512]{1,0:T(8,128)S(1)} custom-call(s32[2]{0:T(128)S(1)} %pad_add_fusion.place_ref, bf16[1536,256]{1,0:T(8,128)(2,1)S(1)} %get-tuple-element.98.refs_0_, bf16[1536,256]{1,0:T(8,128)(2,1)S(1)} %get-tuple-element.99.refs_1_, bf16[1536,256]{1,0:T(8,128)(2,1)S(1)} %get-tuple-element.100.refs_2_, ...), custom_call_target="tpu_custom_call" | custom-call | flops 1610612736 | bytes 6291456 | tf_op jit(solution)/shard_map/gradient/pallas_call | solution.py:233
  104.5 1.2 collective-permute-done.16.refs_1_
  106.2 2.5 %collective-permute-start.32 = (bf16[256,512]{1,0:T(8,128)(2,1)S(1)}, bf16[256,512]{1,0:T(8,128)(2,1)S(1)}, u32[]{:S(2)}, u32[]{:S(2)}) collective-permute-start(bf16[256,512]{1,0:T(8,128)(2,1)S(1)} %key_backward.1.refs_4_), channel_id=1, source_target_pairs={{0,6},{1,7},{2,4},{3,5},{4,2},{5,3},{6,0},{7,1},{8,14},{9,15},{10,... | collective-permute-start | bytes 786440 | tf_op jit(solution)/shard_map/ppermute | solution.py:447
  109.8 2.3 %collective-permute-start.6 = (f32[384,128]{1,0:T(8,128)S(1)}, f32[384,128]{1,0:T(8,128)S(1)}, u32[]{:S(2)}, u32[]{:S(2)}) collective-permute-start(f32[384,128]{1,0:T(8,128)S(1)} %get-tuple-element.132.refs_3_), channel_id=1, source_target_pairs={{0,24},{8,16},{16,8},{24,0},{1,25},{9,17},{17,9},{25,1},{2,26},{10... | collective-permute-start | bytes 589832 | tf_op jit(solution)/shard_map/ppermute | solution.py:447
  112.1 3.6 %gradient.5 = (f32[1536,512]{1,0:T(8,128)S(1)}, f32[8,128]{1,0:T(8,128)S(1)}, f32[1536,128]{1,0:T(8,128)S(1)}) custom-call(s32[2]{0:T(128)S(1)} %pad_add_fusion.place_ref, bf16[1536,256]{1,0:T(8,128)(2,1)S(1)} %get-tuple-element.76.refs_0_, bf16[1536,256]{1,0:T(8,128)(2,1)S(1)} %get-tuple-element.77.refs_1_, ...), custom_call_target="tpu_custom_call" | custom-call | flops 1610612736 | bytes 6291456 | tf_op jit(solution)/shard_map/gradient/pallas_call | solution.py:233
  115.7 0.8 collective-permute-done.32.refs_6_
  116.5 3.8 %collective-permute-done.29.refs_6_ = bf16[256,512]{1,0:T(8,128)(2,1)S(1)} collective-permute-done((bf16[256,512]{1,0:T(8,128)(2,1)S(1)}, bf16[256,512]{1,0:T(8,128)(2,1)S(1)}, u32[]{:S(2)}, u32[]{:S(2)}) %collective-permute-start.29) | collective-permute-done | bytes 262176 | tf_op jit(solution)/shard_map/ppermute | solution.py:447
  120.9 6.2 %collective-permute-done.5.refs_5_ = f32[384,128]{1,0:T(8,128)S(1)} collective-permute-done((f32[384,128]{1,0:T(8,128)S(1)}, f32[384,128]{1,0:T(8,128)S(1)}, u32[]{:S(2)}, u32[]{:S(2)}) %collective-permute-start.5) | collective-permute-done | bytes 196640 | tf_op jit(solution)/shard_map/ppermute | solution.py:447
  127.1 3.6 %collective-permute-done.4.refs_4_ = f32[384,128]{1,0:T(8,128)S(1)} collective-permute-done((f32[384,128]{1,0:T(8,128)S(1)}, f32[384,128]{1,0:T(8,128)S(1)}, u32[]{:S(2)}, u32[]{:S(2)}) %collective-permute-start.4) | collective-permute-done | bytes 196640 | tf_op jit(solution)/shard_map/ppermute | solution.py:447
  130.8 3.2 %gradient.6.refs_8_ = f32[1536,512]{1,0:T(8,128)S(1)} custom-call(s32[2]{0:T(128)S(1)} %pad_add_fusion.place_ref, bf16[1536,256]{1,0:T(8,128)(2,1)S(1)} %get-tuple-element.98.refs_0_, bf16[1536,256]{1,0:T(8,128)(2,1)S(1)} %get-tuple-element.99.refs_1_, bf16[1536,256]{1,0:T(8,128)(2,1)S(1)} %get-tuple-element.100.refs_2_, ...), custom_call_target="tpu_custom_call" | custom-call | flops 1610612736 | bytes 6291456 | tf_op jit(solution)/shard_map/gradient/pallas_call | solution.py:233
  134.0 3.6 %gradient.7 = (f32[1536,512]{1,0:T(8,128)S(1)}, f32[8,128]{1,0:T(8,128)S(1)}, f32[1536,128]{1,0:T(8,128)S(1)}) custom-call(s32[2]{0:T(128)S(1)} %pad_add_fusion.place_ref, bf16[1536,256]{1,0:T(8,128)(2,1)S(1)} %get-tuple-element.76.refs_0_, bf16[1536,256]{1,0:T(8,128)(2,1)S(1)} %get-tuple-element.77.refs_1_, ...), custom_call_target="tpu_custom_call" | custom-call | flops 1610612736 | bytes 6291456 | tf_op jit(solution)/shard_map/gradient/pallas_call | solution.py:233
  137.7 1.2 collective-permute-done.34
  138.9 1.8 %collective-permute-start.37 = (f32[8,128]{1,0:T(8,128)S(1)}, f32[8,128]{1,0:T(8,128)S(1)}, u32[]{:S(2)}, u32[]{:S(2)}) collective-permute-start(f32[8,128]{1,0:T(8,128)S(1)} %add.32.refs_0_), channel_id=1, source_target_pairs={{0,6},{1,7},{2,4},{3,5},{4,2},{5,3},{6,0},{7,1},{8,14},{9,15},{10,... | collective-permute-start | bytes 12296 | tf_op jit(solution)/shard_map/ppermute | solution.py:447
  140.7 0.7 collective-permute-start.36
  141.3 1.0 collective-permute-start.35
  142.3 1.0 collective-permute-done.37.refs_3_
  143.4 0.9 collective-permute-done.36.refs_2_
  144.3 0.7 collective-permute-done.35.refs_1_
  144.9 1.5 adam_frag.1
  146.6 2.3 %collective-permute-start.39 = (bf16[384,128]{1,0:T(8,128)(2,1)S(1)}, bf16[384,128]{1,0:T(8,128)(2,1)S(1)}, u32[]{:S(2)}, u32[]{:S(2)}) collective-permute-start(bf16[384,128]{1,0:T(8,128)(2,1)S(1)} %get-tuple-element.121), channel_id=1, source_target_pairs={{0,16},{8,24},{16,0},{24,8},{1,17},{9,25},{17,1},{25,9},{2,18},{10... | collective-permute-start | bytes 294920 | tf_op jit(solution)/shard_map/ppermute | solution.py:447
  148.9 2.0 %collective-permute-start.40 = (bf16[384,128]{1,0:T(8,128)(2,1)S(1)}, bf16[384,128]{1,0:T(8,128)(2,1)S(1)}, u32[]{:S(2)}, u32[]{:S(2)}) collective-permute-start(bf16[384,128]{1,0:T(8,128)(2,1)S(1)} %get-tuple-element.122), channel_id=1, source_target_pairs={{0,24},{8,16},{16,8},{24,0},{1,25},{9,17},{17,9},{25,1},{2,26},{10... | collective-permute-start | bytes 294920 | tf_op jit(solution)/shard_map/ppermute | solution.py:447
  151.0 6.0 %adam_rows.2 = (f32[1536,1024]{1,0:T(8,128)}, f32[1536,1024]{1,0:T(8,128)}, f32[1536,1024]{1,0:T(8,128)}, f32[8,128]{1,0:T(8,128)S(1)}) custom-call(f32[3]{0:T(128)S(1)} %pad_maximum_fusion.sc_ref, f32[1536,1024]{1,0:T(8,128)S(1)} %bitcast.42, f32[1536,1024]{1,0:T(8,128)S(1)} %bitcast.50, f32[1536,1024]{1,0:T(8,128)S(1)} %bitcast.58, ...), custom_call_target="tpu_custom_call" | custom-call | flops 15728640 | bytes 22020096 | tf_op jit(solution)/shard_map/adam_rows/pallas_call | solution.py:288
  157.1 1.9 %collective-permute-start.43 = (bf16[384,128]{1,0:T(8,128)(2,1)S(1)}, bf16[384,128]{1,0:T(8,128)(2,1)S(1)}, u32[]{:S(2)}, u32[]{:S(2)}) collective-permute-start(bf16[384,128]{1,0:T(8,128)(2,1)S(1)} %convert_element_type.24.refs_7_), channel_id=1, source_target_pairs={{0,24},{8,16},{16,8},{24,0},{1,25},{9,17},{17,9},{25,1},{2,26},{10... | collective-permute-start | bytes 294920 | tf_op jit(solution)/shard_map/ppermute | solution.py:447
  159.3 2.3 %collective-permute-start.41 = (bf16[384,128]{1,0:T(8,128)(2,1)S(1)}, bf16[384,128]{1,0:T(8,128)(2,1)S(1)}, u32[]{:S(2)}, u32[]{:S(2)}) collective-permute-start(bf16[384,128]{1,0:T(8,128)(2,1)S(1)} %convert_element_type.24.refs_7_), channel_id=1, source_target_pairs={{0,8},{8,0},{16,24},{24,16},{1,9},{9,1},{17,25},{25,17},{2,10},{10... | collective-permute-start | bytes 294920 | tf_op jit(solution)/shard_map/ppermute | solution.py:447
  161.6 6.0 %adam_rows.3 = (f32[1536,1024]{1,0:T(8,128)}, f32[1536,1024]{1,0:T(8,128)}, f32[1536,1024]{1,0:T(8,128)}) custom-call(f32[3]{0:T(128)S(1)} %pad_maximum_fusion.sc_ref, f32[1536,1024]{1,0:T(8,128)S(1)} %bitcast.43, f32[1536,1024]{1,0:T(8,128)S(1)} %bitcast.51, ...), custom_call_target="tpu_custom_call", output_to_operand_aliasing={{0}: (10, {}), {1}: (11, {}), {2}: (12, {})} | custom-call | flops 15728640 | bytes 22020096 | tf_op jit(solution)/shard_map/adam_rows/pallas_call | solution.py:288
  167.6 2.4 %outer_step.1 = (f32[1536,1024]{1,0:T(8,128)}, f32[384,1024]{1,0:T(8,128)}, f32[384,1024]{1,0:T(8,128)}) custom-call(s32[2]{0:T(128)S(1)} %pad_add_fusion.place_ref, f32[1536,1024]{1,0:T(8,128)} %get-tuple-element.117.refs_0_, f32[384,1024]{1,0:T(8,128)} %get-tuple-element.80.refs_1_, ...), custom_call_target="tpu_custom_call", output_to_operand_aliasing={{0}: (1, {}), {1}: (2, {}), {2}: (3, {})} | custom-call | flops 1966080 | bytes 3932160 | tf_op jit(solution)/shard_map/outer_step/pallas_call | solution.py:429
  (81 shorter events, 5.2 us)
Async XLA Ops:
  2.6 22.6 %collective-permute-start = (bf16[256,1536]{1,0:T(8,128)(2,1)}, bf16[256,1536]{1,0:T(8,128)(2,1)S(1)}, u32[]{:S(2)}, u32[]{:S(2)}) collective-permute-start(bf16[256,1536]{1,0:T(8,128)(2,1)} %pack.4), channel_id=1, source_target_pairs={{0,6},{1,7},{2,4},{3,5},{4,2},{5,3},{6,0},{7,1},{8,14},{9,15},{10,... | collective-permute-start | bytes 2359304 | tf_op jit(solution)/shard_map/ppermute | solution.py:447
  9.2 32.5 %collective-permute-start.13 = (bf16[256,1536]{1,0:T(8,128)(2,1)}, bf16[256,1536]{1,0:T(8,128)(2,1)S(1)}, u32[]{:S(2)}, u32[]{:S(2)}) collective-permute-start(bf16[256,1536]{1,0:T(8,128)(2,1)} %get-tuple-element.86), channel_id=1, source_target_pairs={{0,7},{1,6},{2,5},{3,4},{4,3},{5,2},{6,1},{7,0},{8,15},{9,14},{10,... | collective-permute-start | bytes 2359304 | tf_op jit(solution)/shard_map/ppermute | solution.py:447
  11.6 47.0 %collective-permute-start.8 = (bf16[256,1536]{1,0:T(8,128)(2,1)}, bf16[256,1536]{1,0:T(8,128)(2,1)}, u32[]{:S(2)}, u32[]{:S(2)}) collective-permute-start(bf16[256,1536]{1,0:T(8,128)(2,1)} %get-tuple-element.74), channel_id=1, source_target_pairs={{0,3},{1,2},{2,1},{3,0},{4,7},{5,6},{6,5},{7,4},{8,11},{9,10},{10,... | collective-permute-start | bytes 2359304 | tf_op jit(solution)/shard_map/ppermute | solution.py:447
  13.3 49.1 %collective-permute-start.11 = (bf16[256,1536]{1,0:T(8,128)(2,1)}, bf16[256,1536]{1,0:T(8,128)(2,1)}, u32[]{:S(2)}, u32[]{:S(2)}) collective-permute-start(bf16[256,1536]{1,0:T(8,128)(2,1)} %get-tuple-element.79), channel_id=1, source_target_pairs={{0,5},{1,4},{2,7},{3,6},{4,1},{5,0},{6,3},{7,2},{8,13},{9,12},{10,... | collective-permute-start | bytes 2359304 | tf_op jit(solution)/shard_map/ppermute | solution.py:447
  16.3 59.5 %collective-permute-start.18 = (bf16[256,1536]{1,0:T(8,128)(2,1)}, bf16[256,1536]{1,0:T(8,128)(2,1)S(1)}, u32[]{:S(2)}, u32[]{:S(2)}) collective-permute-start(bf16[256,1536]{1,0:T(8,128)(2,1)} %get-tuple-element.95), channel_id=1, source_target_pairs={{0,1},{1,0},{2,3},{3,2},{4,5},{5,4},{6,7},{7,6},{8,9},{9,8},{10,11... | collective-permute-start | bytes 2359304 | tf_op jit(solution)/shard_map/ppermute | solution.py:447
  25.3 52.1 %collective-permute-start.7 = (bf16[256,1536]{1,0:T(8,128)(2,1)}, bf16[256,1536]{1,0:T(8,128)(2,1)S(1)}, u32[]{:S(2)}, u32[]{:S(2)}) collective-permute-start(bf16[256,1536]{1,0:T(8,128)(2,1)} %get-tuple-element.73), channel_id=1, source_target_pairs={{0,2},{1,3},{2,0},{3,1},{4,6},{5,7},{6,4},{7,5},{8,10},{9,11},{10,... | collective-permute-start | bytes 2359304 | tf_op jit(solution)/shard_map/ppermute | solution.py:447
  41.7 0.9 copy-start.1
  42.6 34.7 %collective-permute-start.10 = (bf16[256,1536]{1,0:T(8,128)(2,1)}, bf16[256,1536]{1,0:T(8,128)(2,1)S(1)}, u32[]{:S(2)}, u32[]{:S(2)}) collective-permute-start(bf16[256,1536]{1,0:T(8,128)(2,1)} %get-tuple-element.78), channel_id=1, source_target_pairs={{0,4},{1,5},{2,6},{3,7},{4,0},{5,1},{6,2},{7,3},{8,12},{9,13},{10,... | collective-permute-start | bytes 2359304 | tf_op jit(solution)/shard_map/ppermute | solution.py:447
  43.1 4.2 %copy-start.2 = (bf16[256,1536]{1,0:T(8,128)(2,1)S(1)}, bf16[256,1536]{1,0:T(8,128)(2,1)}, u32[]{:S(2)}) copy-start(bf16[256,1536]{1,0:T(8,128)(2,1)} %copy-done.1) | copy-start | bytes 2359300
  58.6 5.5 %collective-permute-start.14 = (bf16[256,512]{1,0:T(8,128)(2,1)S(1)}, bf16[256,512]{1,0:T(8,128)(2,1)S(1)}, u32[]{:S(2)}, u32[]{:S(2)}) collective-permute-start(bf16[256,512]{1,0:T(8,128)(2,1)S(1)} %get-tuple-element.87), channel_id=1, source_target_pairs={{0,1},{1,0},{2,3},{3,2},{4,5},{5,4},{6,7},{7,6},{8,9},{9,8},{10,11... | collective-permute-start | bytes 786440 | tf_op jit(solution)/shard_map/ppermute | solution.py:447
  60.6 6.1 %copy-start.3 = (bf16[1,256,1024]{2,1,0:T(8,128)(2,1)S(1)}, bf16[1,256,1024]{2,1,0:T(8,128)(2,1)}, u32[]{:S(2)}) copy-start(bf16[1,256,1024]{2,1,0:T(8,128)(2,1)} %param.10) | copy-start | bytes 1572868
  62.5 15.4 %collective-permute-start.1 = (f32[384,128]{1,0:T(8,128)S(1)}, f32[384,128]{1,0:T(8,128)S(1)}, u32[]{:S(2)}, u32[]{:S(2)}) collective-permute-start(f32[384,128]{1,0:T(8,128)S(1)} %get-tuple-element.134), channel_id=1, source_target_pairs={{0,8},{8,0},{16,24},{24,16},{1,9},{9,1},{17,25},{25,17},{2,10},{10... | collective-permute-start | bytes 589832 | tf_op jit(solution)/shard_map/ppermute | solution.py:447
  64.1 15.2 %collective-permute-start.3 = (f32[384,128]{1,0:T(8,128)S(1)}, f32[384,128]{1,0:T(8,128)S(1)}, u32[]{:S(2)}, u32[]{:S(2)}) collective-permute-start(f32[384,128]{1,0:T(8,128)S(1)} %get-tuple-element.135), channel_id=1, source_target_pairs={{0,24},{8,16},{16,8},{24,0},{1,25},{9,17},{17,9},{25,1},{2,26},{10... | collective-permute-start | bytes 589832 | tf_op jit(solution)/shard_map/ppermute | solution.py:447
  75.8 15.2 %collective-permute-start.21 = (bf16[256,512]{1,0:T(8,128)(2,1)S(1)}, bf16[256,512]{1,0:T(8,128)(2,1)S(1)}, u32[]{:S(2)}, u32[]{:S(2)}) collective-permute-start(bf16[256,512]{1,0:T(8,128)(2,1)S(1)} %slice.24.refs_4_), channel_id=1, source_target_pairs={{0,6},{1,7},{2,4},{3,5},{4,2},{5,3},{6,0},{7,1},{8,14},{9,15},{10,... | collective-permute-start | bytes 786440 | tf_op jit(solution)/shard_map/ppermute | solution.py:447
  77.3 14.2 %collective-permute-start.9 = (bf16[256,512]{1,0:T(8,128)(2,1)S(1)}, bf16[256,512]{1,0:T(8,128)(2,1)S(1)}, u32[]{:S(2)}, u32[]{:S(2)}) collective-permute-start(bf16[256,512]{1,0:T(8,128)(2,1)S(1)} %get-tuple-element.75), channel_id=1, source_target_pairs={{0,1},{1,0},{2,3},{3,2},{4,5},{5,4},{6,7},{7,6},{8,9},{9,8},{10,11... | collective-permute-start | bytes 786440 | tf_op jit(solution)/shard_map/ppermute | solution.py:447
  77.3 14.7 %collective-permute-start.12 = (bf16[256,512]{1,0:T(8,128)(2,1)S(1)}, bf16[256,512]{1,0:T(8,128)(2,1)S(1)}, u32[]{:S(2)}, u32[]{:S(2)}) collective-permute-start(bf16[256,512]{1,0:T(8,128)(2,1)S(1)} %get-tuple-element.85), channel_id=1, source_target_pairs={{0,1},{1,0},{2,3},{3,2},{4,5},{5,4},{6,7},{7,6},{8,9},{9,8},{10,11... | collective-permute-start | bytes 786440 | tf_op jit(solution)/shard_map/ppermute | solution.py:447
  77.8 15.7 %collective-permute-start.15 = (bf16[256,512]{1,0:T(8,128)(2,1)S(1)}, bf16[256,512]{1,0:T(8,128)(2,1)S(1)}, u32[]{:S(2)}, u32[]{:S(2)}) collective-permute-start(bf16[256,512]{1,0:T(8,128)(2,1)S(1)} %get-tuple-element.88), channel_id=1, source_target_pairs={{0,6},{1,7},{2,4},{3,5},{4,2},{5,3},{6,0},{7,1},{8,14},{9,15},{10,... | collective-permute-start | bytes 786440 | tf_op jit(solution)/shard_map/ppermute | solution.py:447
  79.3 11.7 %collective-permute-start.2 = (f32[384,128]{1,0:T(8,128)S(1)}, f32[384,128]{1,0:T(8,128)S(1)}, u32[]{:S(2)}, u32[]{:S(2)}) collective-permute-start(f32[384,128]{1,0:T(8,128)S(1)} %get-tuple-element.136), channel_id=1, source_target_pairs={{0,16},{8,24},{16,0},{24,8},{1,17},{9,25},{17,1},{25,9},{2,18},{10... | collective-permute-start | bytes 589832 | tf_op jit(solution)/shard_map/ppermute | solution.py:447
  82.4 14.6 %copy-start = (bf16[256,1536]{1,0:T(8,128)(2,1)S(1)}, bf16[256,1536]{1,0:T(8,128)(2,1)}, u32[]{:S(2)}) copy-start(bf16[256,1536]{1,0:T(8,128)(2,1)} %get-tuple-element.94.refs_0_.refs_1_.refs_2_.refs_3_) | copy-start | bytes 2359300
  91.0 3.8 %collective-permute-start.20 = (bf16[256,512]{1,0:T(8,128)(2,1)S(1)}, bf16[256,512]{1,0:T(8,128)(2,1)S(1)}, u32[]{:S(2)}, u32[]{:S(2)}) collective-permute-start(bf16[256,512]{1,0:T(8,128)(2,1)S(1)} %slice.24.refs_4_), channel_id=1, source_target_pairs={{0,1},{1,0},{2,3},{3,2},{4,5},{5,4},{6,7},{7,6},{8,9},{9,8},{10,11... | collective-permute-start | bytes 786440 | tf_op jit(solution)/shard_map/ppermute | solution.py:447
  91.1 4.4 %collective-permute-start.19 = (bf16[256,512]{1,0:T(8,128)(2,1)S(1)}, bf16[256,512]{1,0:T(8,128)(2,1)S(1)}, u32[]{:S(2)}, u32[]{:S(2)}) collective-permute-start(bf16[256,512]{1,0:T(8,128)(2,1)S(1)} %get-tuple-element.96), channel_id=1, source_target_pairs={{0,1},{1,0},{2,3},{3,2},{4,5},{5,4},{6,7},{7,6},{8,9},{9,8},{10,11... | collective-permute-start | bytes 786440 | tf_op jit(solution)/shard_map/ppermute | solution.py:447
  91.6 9.2 %collective-permute-start.26 = (bf16[256,512]{1,0:T(8,128)(2,1)S(1)}, bf16[256,512]{1,0:T(8,128)(2,1)S(1)}, u32[]{:S(2)}, u32[]{:S(2)}) collective-permute-start(bf16[256,512]{1,0:T(8,128)(2,1)S(1)} %slice.24.refs_4_), channel_id=1, source_target_pairs={{0,4},{1,5},{2,6},{3,7},{4,0},{5,1},{6,2},{7,3},{8,12},{9,13},{10,... | collective-permute-start | bytes 786440 | tf_op jit(solution)/shard_map/ppermute | solution.py:447
  92.1 9.2 %collective-permute-start.24 = (bf16[256,512]{1,0:T(8,128)(2,1)S(1)}, bf16[256,512]{1,0:T(8,128)(2,1)S(1)}, u32[]{:S(2)}, u32[]{:S(2)}) collective-permute-start(bf16[256,512]{1,0:T(8,128)(2,1)S(1)} %slice.24.refs_4_), channel_id=1, source_target_pairs={{0,2},{1,3},{2,0},{3,1},{4,6},{5,7},{6,4},{7,5},{8,10},{9,11},{10,... | collective-permute-start | bytes 786440 | tf_op jit(solution)/shard_map/ppermute | solution.py:447
  93.6 7.7 %collective-permute-start.22 = (bf16[256,512]{1,0:T(8,128)(2,1)S(1)}, bf16[256,512]{1,0:T(8,128)(2,1)S(1)}, u32[]{:S(2)}, u32[]{:S(2)}) collective-permute-start(bf16[256,512]{1,0:T(8,128)(2,1)S(1)} %collective-permute-done.21.refs_6_), channel_id=1, source_target_pairs={{0,1},{1,0},{2,3},{3,2},{4,5},{5,4},{6,7},{7,6},{8,9},{9,8},{10,11... | collective-permute-start | bytes 786440 | tf_op jit(solution)/shard_map/ppermute | solution.py:447
  94.8 10.8 %collective-permute-start.16 = (bf16[256,512]{1,0:T(8,128)(2,1)S(1)}, bf16[256,512]{1,0:T(8,128)(2,1)S(1)}, u32[]{:S(2)}, u32[]{:S(2)}) collective-permute-start(bf16[256,512]{1,0:T(8,128)(2,1)S(1)} %get-tuple-element.92), channel_id=1, source_target_pairs={{0,2},{1,3},{2,0},{3,1},{4,6},{5,7},{6,4},{7,5},{8,10},{9,11},{10,... | collective-permute-start | bytes 786440 | tf_op jit(solution)/shard_map/ppermute | solution.py:447
  95.5 10.2 %collective-permute-start.17 = (bf16[256,512]{1,0:T(8,128)(2,1)S(1)}, bf16[256,512]{1,0:T(8,128)(2,1)S(1)}, u32[]{:S(2)}, u32[]{:S(2)}) collective-permute-start(bf16[256,512]{1,0:T(8,128)(2,1)S(1)} %get-tuple-element.93), channel_id=1, source_target_pairs={{0,4},{1,5},{2,6},{3,7},{4,0},{5,1},{6,2},{7,3},{8,12},{9,13},{10,... | collective-permute-start | bytes 786440 | tf_op jit(solution)/shard_map/ppermute | solution.py:447
  97.0 54.0 %slice-start.4 = ((s8[6291456]{0:T(1024)(128)(4,1)}), s8[4194304]{0:T(1024)(128)(4,1)S(1)}, s32[]{:S(2)}) async-start(s8[6291456]{0:T(1024)(128)(4,1)} %bitcast.56), calls=%async_computation.4 | async-start | bytes 8388608
  100.7 9.1 %collective-permute-start.27 = (bf16[256,512]{1,0:T(8,128)(2,1)S(1)}, bf16[256,512]{1,0:T(8,128)(2,1)S(1)}, u32[]{:S(2)}, u32[]{:S(2)}) collective-permute-start(bf16[256,512]{1,0:T(8,128)(2,1)S(1)} %collective-permute-done.26.refs_6_), channel_id=1, source_target_pairs={{0,1},{1,0},{2,3},{3,2},{4,5},{5,4},{6,7},{7,6},{8,9},{9,8},{10,11... | collective-permute-start | bytes 786440 | tf_op jit(solution)/shard_map/ppermute | solution.py:447
  101.3 10.8 %collective-permute-start.25 = (bf16[256,512]{1,0:T(8,128)(2,1)S(1)}, bf16[256,512]{1,0:T(8,128)(2,1)S(1)}, u32[]{:S(2)}, u32[]{:S(2)}) collective-permute-start(bf16[256,512]{1,0:T(8,128)(2,1)S(1)} %collective-permute-done.24.refs_4_), channel_id=1, source_target_pairs={{0,1},{1,0},{2,3},{3,2},{4,5},{5,4},{6,7},{7,6},{8,9},{9,8},{10,11... | collective-permute-start | bytes 786440 | tf_op jit(solution)/shard_map/ppermute | solution.py:447
  106.2 10.3 %collective-permute-start.32 = (bf16[256,512]{1,0:T(8,128)(2,1)S(1)}, bf16[256,512]{1,0:T(8,128)(2,1)S(1)}, u32[]{:S(2)}, u32[]{:S(2)}) collective-permute-start(bf16[256,512]{1,0:T(8,128)(2,1)S(1)} %key_backward.1.refs_4_), channel_id=1, source_target_pairs={{0,6},{1,7},{2,4},{3,5},{4,2},{5,3},{6,0},{7,1},{8,14},{9,15},{10,... | collective-permute-start | bytes 786440 | tf_op jit(solution)/shard_map/ppermute | solution.py:447
  108.7 11.6 %collective-permute-start.29 = (bf16[256,512]{1,0:T(8,128)(2,1)S(1)}, bf16[256,512]{1,0:T(8,128)(2,1)S(1)}, u32[]{:S(2)}, u32[]{:S(2)}) collective-permute-start(bf16[256,512]{1,0:T(8,128)(2,1)S(1)} %key_backward.1.refs_4_), channel_id=1, source_target_pairs={{0,4},{1,5},{2,6},{3,7},{4,0},{5,1},{6,2},{7,3},{8,12},{9,13},{10,... | collective-permute-start | bytes 786440 | tf_op jit(solution)/shard_map/ppermute | solution.py:447
  109.2 11.2 %collective-permute-start.23 = (bf16[256,512]{1,0:T(8,128)(2,1)S(1)}, bf16[256,512]{1,0:T(8,128)(2,1)S(1)}, u32[]{:S(2)}, u32[]{:S(2)}) collective-permute-start(bf16[256,512]{1,0:T(8,128)(2,1)S(1)} %key_backward.1.refs_4_), channel_id=1, source_target_pairs={{0,2},{1,3},{2,0},{3,1},{4,6},{5,7},{6,4},{7,5},{8,10},{9,11},{10,... | collective-permute-start | bytes 786440 | tf_op jit(solution)/shard_map/ppermute | solution.py:447
  109.8 10.6 %collective-permute-start.6 = (f32[384,128]{1,0:T(8,128)S(1)}, f32[384,128]{1,0:T(8,128)S(1)}, u32[]{:S(2)}, u32[]{:S(2)}) collective-permute-start(f32[384,128]{1,0:T(8,128)S(1)} %get-tuple-element.132.refs_3_), channel_id=1, source_target_pairs={{0,24},{8,16},{16,8},{24,0},{1,25},{9,17},{17,9},{25,1},{2,26},{10... | collective-permute-start | bytes 589832 | tf_op jit(solution)/shard_map/ppermute | solution.py:447
  112.1 15.0 %collective-permute-start.5 = (f32[384,128]{1,0:T(8,128)S(1)}, f32[384,128]{1,0:T(8,128)S(1)}, u32[]{:S(2)}, u32[]{:S(2)}) collective-permute-start(f32[384,128]{1,0:T(8,128)S(1)} %get-tuple-element.132.refs_3_), channel_id=1, source_target_pairs={{0,16},{8,24},{16,0},{24,8},{1,17},{9,25},{17,1},{25,9},{2,18},{10... | collective-permute-start | bytes 589832 | tf_op jit(solution)/shard_map/ppermute | solution.py:447
  112.1 38.8 %slice-start.5 = ((s8[6291456]{0:T(1024)(128)(4,1)}), s8[2097152]{0:T(1024)(128)(4,1)S(1)}, s32[]{:S(2)}) async-start(s8[6291456]{0:T(1024)(128)(4,1)} %bitcast.56), calls=%async_computation.5 | async-start | bytes 4194304
  116.5 14.3 %collective-permute-start.31 = (bf16[256,512]{1,0:T(8,128)(2,1)S(1)}, bf16[256,512]{1,0:T(8,128)(2,1)S(1)}, u32[]{:S(2)}, u32[]{:S(2)}) collective-permute-start(bf16[256,512]{1,0:T(8,128)(2,1)S(1)} %key_backward.1.refs_4_), channel_id=1, source_target_pairs={{0,1},{1,0},{2,3},{3,2},{4,5},{5,4},{6,7},{7,6},{8,9},{9,8},{10,11... | collective-permute-start | bytes 786440 | tf_op jit(solution)/shard_map/ppermute | solution.py:447
  120.3 10.4 %collective-permute-start.33 = (bf16[256,512]{1,0:T(8,128)(2,1)S(1)}, bf16[256,512]{1,0:T(8,128)(2,1)S(1)}, u32[]{:S(2)}, u32[]{:S(2)}) collective-permute-start(bf16[256,512]{1,0:T(8,128)(2,1)S(1)} %collective-permute-done.32.refs_6_), channel_id=1, source_target_pairs={{0,1},{1,0},{2,3},{3,2},{4,5},{5,4},{6,7},{7,6},{8,9},{9,8},{10,11... | collective-permute-start | bytes 786440 | tf_op jit(solution)/shard_map/ppermute | solution.py:447
  120.4 10.3 %collective-permute-start.4 = (f32[384,128]{1,0:T(8,128)S(1)}, f32[384,128]{1,0:T(8,128)S(1)}, u32[]{:S(2)}, u32[]{:S(2)}) collective-permute-start(f32[384,128]{1,0:T(8,128)S(1)} %get-tuple-element.132.refs_3_), channel_id=1, source_target_pairs={{0,8},{8,0},{16,24},{24,16},{1,9},{9,1},{17,25},{25,17},{2,10},{10... | collective-permute-start | bytes 589832 | tf_op jit(solution)/shard_map/ppermute | solution.py:447
  120.4 13.5 %collective-permute-start.30 = (bf16[256,512]{1,0:T(8,128)(2,1)S(1)}, bf16[256,512]{1,0:T(8,128)(2,1)S(1)}, u32[]{:S(2)}, u32[]{:S(2)}) collective-permute-start(bf16[256,512]{1,0:T(8,128)(2,1)S(1)} %collective-permute-done.29.refs_6_), channel_id=1, source_target_pairs={{0,1},{1,0},{2,3},{3,2},{4,5},{5,4},{6,7},{7,6},{8,9},{9,8},{10,11... | collective-permute-start | bytes 786440 | tf_op jit(solution)/shard_map/ppermute | solution.py:447
  127.1 6.9 %collective-permute-start.28 = (bf16[256,512]{1,0:T(8,128)(2,1)S(1)}, bf16[256,512]{1,0:T(8,128)(2,1)S(1)}, u32[]{:S(2)}, u32[]{:S(2)}) collective-permute-start(bf16[256,512]{1,0:T(8,128)(2,1)S(1)} %collective-permute-done.23.refs_4_), channel_id=1, source_target_pairs={{0,1},{1,0},{2,3},{3,2},{4,5},{5,4},{6,7},{7,6},{8,9},{9,8},{10,11... | collective-permute-start | bytes 786440 | tf_op jit(solution)/shard_map/ppermute | solution.py:447
  130.8 20.2 %slice-start = ((s8[6291456]{0:T(1024)(128)(4,1)}), s8[4194304]{0:T(1024)(128)(4,1)S(1)}, s32[]{:S(2)}) async-start(s8[6291456]{0:T(1024)(128)(4,1)} %bitcast.40), calls=%async_computation | async-start | bytes 8388608
  130.8 20.2 %slice-start.2 = ((s8[6291456]{0:T(1024)(128)(4,1)}), s8[4194304]{0:T(1024)(128)(4,1)S(1)}, s32[]{:S(2)}) async-start(s8[6291456]{0:T(1024)(128)(4,1)} %bitcast.48), calls=%async_computation.2 | async-start | bytes 8388608
  134.0 17.0 %slice-start.1 = ((s8[6291456]{0:T(1024)(128)(4,1)}), s8[2097152]{0:T(1024)(128)(4,1)S(1)}, s32[]{:S(2)}) async-start(s8[6291456]{0:T(1024)(128)(4,1)} %bitcast.40), calls=%async_computation.1 | async-start | bytes 4194304
  134.0 16.9 %slice-start.3 = ((s8[6291456]{0:T(1024)(128)(4,1)}), s8[2097152]{0:T(1024)(128)(4,1)S(1)}, s32[]{:S(2)}) async-start(s8[6291456]{0:T(1024)(128)(4,1)} %bitcast.48), calls=%async_computation.3 | async-start | bytes 4194304
  137.6 1.2 collective-permute-start.34
  138.9 4.5 %collective-permute-start.37 = (f32[8,128]{1,0:T(8,128)S(1)}, f32[8,128]{1,0:T(8,128)S(1)}, u32[]{:S(2)}, u32[]{:S(2)}) collective-permute-start(f32[8,128]{1,0:T(8,128)S(1)} %add.32.refs_0_), channel_id=1, source_target_pairs={{0,6},{1,7},{2,4},{3,5},{4,2},{5,3},{6,0},{7,1},{8,14},{9,15},{10,... | collective-permute-start | bytes 12296 | tf_op jit(solution)/shard_map/ppermute | solution.py:447
  140.7 3.6 %collective-permute-start.36 = (f32[8,128]{1,0:T(8,128)S(1)}, f32[8,128]{1,0:T(8,128)S(1)}, u32[]{:S(2)}, u32[]{:S(2)}) collective-permute-start(f32[8,128]{1,0:T(8,128)S(1)} %add.32.refs_0_), channel_id=1, source_target_pairs={{0,4},{1,5},{2,6},{3,7},{4,0},{5,1},{6,2},{7,3},{8,12},{9,13},{10,... | collective-permute-start | bytes 12296 | tf_op jit(solution)/shard_map/ppermute | solution.py:447
  141.3 3.6 %collective-permute-start.35 = (f32[8,128]{1,0:T(8,128)S(1)}, f32[8,128]{1,0:T(8,128)S(1)}, u32[]{:S(2)}, u32[]{:S(2)}) collective-permute-start(f32[8,128]{1,0:T(8,128)S(1)} %add.32.refs_0_), channel_id=1, source_target_pairs={{0,2},{1,3},{2,0},{3,1},{4,6},{5,7},{6,4},{7,5},{8,10},{9,11},{10,... | collective-permute-start | bytes 12296 | tf_op jit(solution)/shard_map/ppermute | solution.py:447
  146.5 10.5 %collective-permute-start.38 = (bf16[384,128]{1,0:T(8,128)(2,1)S(1)}, bf16[384,128]{1,0:T(8,128)(2,1)S(1)}, u32[]{:S(2)}, u32[]{:S(2)}) collective-permute-start(bf16[384,128]{1,0:T(8,128)(2,1)S(1)} %get-tuple-element.120), channel_id=1, source_target_pairs={{0,8},{8,0},{16,24},{24,16},{1,9},{9,1},{17,25},{25,17},{2,10},{10... | collective-permute-start | bytes 294920 | tf_op jit(solution)/shard_map/ppermute | solution.py:447
  146.6 10.5 %collective-permute-start.39 = (bf16[384,128]{1,0:T(8,128)(2,1)S(1)}, bf16[384,128]{1,0:T(8,128)(2,1)S(1)}, u32[]{:S(2)}, u32[]{:S(2)}) collective-permute-start(bf16[384,128]{1,0:T(8,128)(2,1)S(1)} %get-tuple-element.121), channel_id=1, source_target_pairs={{0,16},{8,24},{16,0},{24,8},{1,17},{9,25},{17,1},{25,9},{2,18},{10... | collective-permute-start | bytes 294920 | tf_op jit(solution)/shard_map/ppermute | solution.py:447
  148.9 8.1 %collective-permute-start.40 = (bf16[384,128]{1,0:T(8,128)(2,1)S(1)}, bf16[384,128]{1,0:T(8,128)(2,1)S(1)}, u32[]{:S(2)}, u32[]{:S(2)}) collective-permute-start(bf16[384,128]{1,0:T(8,128)(2,1)S(1)} %get-tuple-element.122), channel_id=1, source_target_pairs={{0,24},{8,16},{16,8},{24,0},{1,25},{9,17},{17,9},{25,1},{2,26},{10... | collective-permute-start | bytes 294920 | tf_op jit(solution)/shard_map/ppermute | solution.py:447
  157.1 10.5 %collective-permute-start.43 = (bf16[384,128]{1,0:T(8,128)(2,1)S(1)}, bf16[384,128]{1,0:T(8,128)(2,1)S(1)}, u32[]{:S(2)}, u32[]{:S(2)}) collective-permute-start(bf16[384,128]{1,0:T(8,128)(2,1)S(1)} %convert_element_type.24.refs_7_), channel_id=1, source_target_pairs={{0,24},{8,16},{16,8},{24,0},{1,25},{9,17},{17,9},{25,1},{2,26},{10... | collective-permute-start | bytes 294920 | tf_op jit(solution)/shard_map/ppermute | solution.py:447
  159.0 8.6 %collective-permute-start.42 = (bf16[384,128]{1,0:T(8,128)(2,1)S(1)}, bf16[384,128]{1,0:T(8,128)(2,1)S(1)}, u32[]{:S(2)}, u32[]{:S(2)}) collective-permute-start(bf16[384,128]{1,0:T(8,128)(2,1)S(1)} %convert_element_type.24.refs_7_), channel_id=1, source_target_pairs={{0,16},{8,24},{16,0},{24,8},{1,17},{9,25},{17,1},{25,9},{2,18},{10... | collective-permute-start | bytes 294920 | tf_op jit(solution)/shard_map/ppermute | solution.py:447
  159.3 8.3 %collective-permute-start.41 = (bf16[384,128]{1,0:T(8,128)(2,1)S(1)}, bf16[384,128]{1,0:T(8,128)(2,1)S(1)}, u32[]{:S(2)}, u32[]{:S(2)}) collective-permute-start(bf16[384,128]{1,0:T(8,128)(2,1)S(1)} %convert_element_type.24.refs_7_), channel_id=1, source_target_pairs={{0,8},{8,0},{16,24},{24,16},{1,9},{9,1},{17,25},{25,17},{2,10},{10... | collective-permute-start | bytes 294920 | tf_op jit(solution)/shard_map/ppermute | solution.py:447

commit v16 on v13

--- a/solution.py
+++ b/solution.py
@@ -102,41 +102,44 @@
     )(*in_hbm(array))
 
 
-def partial_kernel(pieces, *refs):
-    x_refs, w_ref, (*add_refs, out_ref, flip_ref) = refs[:pieces], refs[pieces], refs[pieces + 1:]
+def partial_kernel(pieces, firsts, splits, *refs):
+    x_refs, w_ref, refs = refs[:pieces], refs[pieces], refs[pieces + 1:]
+    add_refs, out_refs, flip_ref = refs[:len(firsts)], refs[len(firsts):-1], refs[-1]
     x = jnp.concatenate([ref[...] for ref in x_refs], axis=1)
     total = jnp.dot(x, w_ref[...], preferred_element_type=jnp.float32)
-    for ref in add_refs:
-        total = total + ref[...].astype(jnp.float32)
-    out_ref[...] = total.astype(out_ref.dtype)
+    count = total.shape[0]
+    for ref, first in zip(add_refs, firsts):
+        last = first + ref.shape[0]
+        rows = [total[:first], total[first:last] + ref[...].astype(jnp.float32), total[last:]]
+        total = jnp.concatenate([r for r in rows if r.shape[0]], axis=0)
+    height = count // splits
+    for i, ref in enumerate(out_refs):
+        ref[...] = total[i * height:(i + 1) * height].astype(ref.dtype)
     step = x_refs[0].shape[1]
     for i, ref in enumerate(x_refs):
         flip_ref[i * step:(i + 1) * step, :] = ref[...].T
 
 
-def partial_keys(block, key_weights, *others):
+def partial_keys(block, key_weights, adds=(), splits=1):
     count, rows = block.shape
     width = key_weights.shape[1]
     pieces = 4 if rows % (4 * HEAD) == 0 else 2
     fixed = lambda a: pl.BlockSpec(a.shape, lambda i: (0, 0))
-    return pl.pallas_call(
-        functools.partial(partial_kernel, pieces),
-        out_shape=[
-            jax.ShapeDtypeStruct((count, width), jnp.bfloat16),
-            jax.ShapeDtypeStruct((rows, count), jnp.bfloat16),
-        ],
+    *parts, flipped = pl.pallas_call(
+        functools.partial(partial_kernel, pieces, [first for _, first in adds], splits),
+        out_shape=[jax.ShapeDtypeStruct((count // splits, width), jnp.bfloat16)] * splits
+        + [jax.ShapeDtypeStruct((rows, count), jnp.bfloat16)],
         grid=(1,),
         in_specs=[pl.BlockSpec((count, rows // pieces), lambda i, c=c: (0, c)) for c in range(pieces)]
         + [fixed(key_weights)]
-        + [fixed(o) for o in others],
-        out_specs=[
-            pl.BlockSpec((count, width), lambda i: (0, 0)),
-            pl.BlockSpec((rows, count), lambda i: (0, 0)),
-        ],
+        + [fixed(a) for a, _ in adds],
+        out_specs=[pl.BlockSpec((count // splits, width), lambda i: (0, 0))] * splits
+        + [pl.BlockSpec((rows, count), lambda i: (0, 0))],
         compiler_params=params_of(12),
         cost_estimate=cost(2 * count * rows * width, 4 * count * rows),
         name="partial_keys",
-    )(*[block] * pieces, key_weights, *others)
+    )(*[block] * pieces, key_weights, *[a for a, _ in adds])
+    return parts if splits > 1 else parts[0], flipped
 
 
 def key_kernel(first, *refs):
@@ -476,20 +479,24 @@
     order = [k for k in far[:-2] for k in (k, k + 1)]
     order += far[-2:] + [k + 1 for k in far[-2:]]
 
+    (old,) = due_columns(place, part, params)
+    old_sums = [old[0]] + [swap(old[k], "rep", k) for k in range(1, replicas)]
+
     packed = {}
     for offsets in (order[:1], order[1:4], order[4:], (0, 1)):
         packed |= pack(inputs, me, rows, tuple(offsets))
     blocks = {k: swap(packed[k], "fsdp", k) for k in order}
     blocks[0], blocks[1] = packed[0], swap(packed[1], "fsdp", 1)
 
-    (old,) = due_columns(after(place, blocks[order[0]]), part, params)
-    old_sums = [old[0]] + [swap(old[k], "rep", k) for k in range(1, replicas)]
-
+    relay = len(far) == 3 and far[0] == far[1] ^ far[2]
+    half = inputs.shape[0] // 2
     values = {0: incoming[:, kv_width:]}
-    for i, k in enumerate(far):
+    for i, k in enumerate(far[1:] if relay else far):
         values[k] = swap(after(values[0], blocks[order[i]]), "fsdp", k)
-    for k in range(0, shards, 2):
-        values[k + 1] = swap(values[k], "fsdp", 1)
+    if relay:
+        upper = swap(values[far[1]][:half], "fsdp", far[2])
+        lower = swap(values[far[2]][half:], "fsdp", far[1])
+        values[far[0]] = jnp.concatenate([upper, lower], axis=0)
 
     steps_now = step_count[0].astype(jnp.float32)
     plan = jnp.minimum(1.0, steps_now / WARMUP) * (
@@ -509,19 +516,27 @@
 
     last = far[-1]
     blocks[last + 1] = after(blocks[last + 1], anchor_copy, momentum_copy, scalars, old_first, old_second)
-    parts, flipped = [], {}
+    parts, flipped, relayed = [], {}, {}
     for k in far + [0]:
         theirs, flipped[k + 1] = partial_keys(blocks[k + 1], key_weights)
         theirs = swap(theirs, "fsdp", 1)
         if k == last:
-            theirs = after(theirs, *parts[:1], *base)
-        part_k, flipped[k] = partial_keys(blocks[k], key_weights, theirs)
+            theirs = after(theirs, *base)
+        adds = [(theirs, 0)] + relayed.get(k, [])
+        if relay and k == far[0]:
+            (upper, lower), flipped[k] = partial_keys(blocks[k], key_weights, adds, 2)
+            relayed[far[2]] = [(swap(upper, "fsdp", far[1]), 0)]
+            relayed[far[1]] = [(swap(lower, "fsdp", far[2]), half)]
+            continue
+        part_k, flipped[k] = partial_keys(blocks[k], key_weights, adds)
+        if k == last:
+            for j in range(0, shards, 2):
+                values[j + 1] = swap(after(values[j], part_k), "fsdp", 1)
         parts.append(swap(part_k, "fsdp", k) if k else part_k)
     spread = [0, 1] + [k + odd for k in far for odd in range(2)]
     near, rest = spread[:shards // 2], spread[shards // 2:]
     pick = lambda table, which: [table[k] for k in which]
     (values_first,) = gradient(place, pick(flipped, near), pick(values, near), last=False)
-    parts[-1] = after(parts[-1], values_first)
     keys = {0: key_backward(parts, incoming, 0)}
     for k in far:
         keys[k] = swap(keys[0], "fsdp", k)

time: 169 us -> 162 us (0.959)
  starting transfers between devices: 49.7 us -> 43.6 us
  Pallas kernels: 58 us -> 55.6 us
  waiting for transfers between devices: 55.8 us -> 57.6 us
    ppermute x44 -> x46, starting transfers between devices: 49.7 us -> 43.6 us  [swap(): return lax.ppermute(block, axis, [(i, i ^ offset) for i in range(count)])]
    pallas_call x8, Pallas kernels: 7.02 us -> 4.64 us  [partial_keys(): pl.pallas_call(functools.partial(partial_kernel, pieces, [first for _, fi...]
    ppermute x44 -> x46, waiting for transfers between devices: 55.8 us -> 57.6 us  [swap(): return lax.ppermute(block, axis, [(i, i ^ offset) for i in range(count)])]
  transfers between devices with their start and end apart: 44 -> 46, of which waited for: 14 -> 17; matrix products, arithmetic and copies ran while one was open for 1% -> 0% of each run, Pallas kernels for 29% -> 29%
where the time goes in v16:
time: 162 us; the launch traced here: 161 us
  waiting for transfers between devices  57.6 us (36%)
  Pallas kernels  55.6 us (34%)
  starting transfers between devices  43.6 us (27%)
  between operations  3.79 us (2%)
    ppermute x46, waiting for transfers between devices, swap(): return lax.ppermute(block, axis, [(i, i ^ offset) for i in range(count)])  57.6 us
    ppermute x46, starting transfers between devices, swap(): return lax.ppermute(block, axis, [(i, i ^ offset) for i in range(count)])  43.6 us
    pallas_call x4, Pallas kernels, gradient(): pl.pallas_call(functools.partial(grad_kernel, len(flipped), base is not N...  13.5 us
    pallas_call x2, Pallas kernels, adam_rows(): pl.pallas_call(functools.partial(adam_kernel, len(squares), len(into)), o...  12 us
    pallas_call x4, Pallas kernels, pack(): pl.pallas_call(functools.partial(pack_kernel, offsets), out_shape=[pltpu....  9.19 us
    pallas_call x3, Pallas kernels, due_columns(): pl.pallas_call(functools.partial(pick_kernel, blocks), out_shape=[jax.Sha...  5.55 us
    pallas_call x8, Pallas kernels, partial_keys(): pl.pallas_call(functools.partial(partial_kernel, pieces, [first for _, fi...  4.64 us
    pallas_call x1, Pallas kernels, cast_left(): pl.pallas_call(cast_kernel, out_shape=jax.ShapeDtypeStruct((rows, width),...  3.46 us
  transfers between devices with their start and end apart: 46, of which 17 were waited for; matrix products, arithmetic and copies ran while one was open for 0% of the time, Pallas kernels for 29%

profile of v16, /device:TPU:0, one launch (start us, length us, event | category | flops | bytes accessed | tf_op | source)
XLA Modules:
  0.0 161.1 jit_solution(5636038564644287418)
XLA Ops:
  1.4 1.8 %due_columns.5.w_ref = f32[4,384,128]{2,1,0:T(8,128)S(1)} custom-call(s32[2]{0:T(128)S(1)} %pad_add_fusion.place_ref, f32[1536,1024]{1,0:T(8,128)} %bitcast.35, f32[1536,1024]{1,0:T(8,128)} %bitcast.36, f32[1536,1024]{1,0:T(8,128)} %bitcast.37, f32[1536,1024]{1,0:T(8,128)} %bitcast.38), custom_call_target="tpu_custom_call" | custom-call | bytes 1572864 | tf_op jit(solution)/shard_map/due_columns/pallas_call | solution.py:348
  3.2 3.1 %collective-permute-start.10 = (f32[384,128]{1,0:T(8,128)S(1)}, f32[384,128]{1,0:T(8,128)S(1)}, u32[]{:S(2)}, u32[]{:S(2)}) collective-permute-start(f32[384,128]{1,0:T(8,128)S(1)} %get-tuple-element.136), channel_id=1, source_target_pairs={{0,8},{8,0},{16,24},{24,16},{1,9},{9,1},{17,25},{25,17},{2,10},{10... | collective-permute-start | bytes 589832 | tf_op jit(solution)/shard_map/ppermute | solution.py:450
  6.3 2.5 %collective-permute-start.12 = (f32[384,128]{1,0:T(8,128)S(1)}, f32[384,128]{1,0:T(8,128)S(1)}, u32[]{:S(2)}, u32[]{:S(2)}) collective-permute-start(f32[384,128]{1,0:T(8,128)S(1)} %get-tuple-element.137), channel_id=1, source_target_pairs={{0,24},{8,16},{16,8},{24,0},{1,25},{9,17},{17,9},{25,1},{2,26},{10... | collective-permute-start | bytes 589832 | tf_op jit(solution)/shard_map/ppermute | solution.py:450
  8.9 2.0 %pack.6 = bf16[256,1536]{1,0:T(8,128)(2,1)} custom-call(s32[1]{0:T(128)} %bitcast.4.me_ref, bf16[256,12288]{1,0:T(8,128)(2,1)} %bitcast.64), custom_call_target="tpu_custom_call" | custom-call | bytes 1572864 | tf_op jit(solution)/shard_map/pack/pallas_call | solution.py:69
  10.9 2.5 %collective-permute-start.3 = (bf16[256,1536]{1,0:T(8,128)(2,1)}, bf16[256,1536]{1,0:T(8,128)(2,1)S(1)}, u32[]{:S(2)}, u32[]{:S(2)}) collective-permute-start(bf16[256,1536]{1,0:T(8,128)(2,1)} %pack.6), channel_id=1, source_target_pairs={{0,6},{1,7},{2,4},{3,5},{4,2},{5,3},{6,0},{7,1},{8,14},{9,15},{10,... | collective-permute-start | bytes 2359304 | tf_op jit(solution)/shard_map/ppermute | solution.py:450
  13.4 2.6 %pack.4 = (bf16[256,1536]{1,0:T(8,128)(2,1)}, bf16[256,1536]{1,0:T(8,128)(2,1)}, bf16[256,1536]{1,0:T(8,128)(2,1)}) custom-call(s32[1]{0:T(128)} %bitcast.4.me_ref, bf16[256,12288]{1,0:T(8,128)(2,1)} %bitcast.65), custom_call_target="tpu_custom_call" | custom-call | bytes 4718592 | tf_op jit(solution)/shard_map/pack/pallas_call | solution.py:69
  16.1 1.6 due_columns.4
  17.7 1.2 collective-permute-done.12
  18.9 7.3 %collective-permute-done.11 = f32[384,128]{1,0:T(8,128)S(1)} collective-permute-done((f32[384,128]{1,0:T(8,128)S(1)}, f32[384,128]{1,0:T(8,128)S(1)}, u32[]{:S(2)}, u32[]{:S(2)}) %collective-permute-start.11) | collective-permute-done | bytes 196640 | tf_op jit(solution)/shard_map/ppermute | solution.py:450
  26.3 3.1 %collective-permute-start.15 = (f32[384,128]{1,0:T(8,128)S(1)}, f32[384,128]{1,0:T(8,128)S(1)}, u32[]{:S(2)}, u32[]{:S(2)}) collective-permute-start(f32[384,128]{1,0:T(8,128)S(1)} %get-tuple-element.134.refs_3_), channel_id=1, source_target_pairs={{0,24},{8,16},{16,8},{24,0},{1,25},{9,17},{17,9},{25,1},{2,26},{10... | collective-permute-start | bytes 589832 | tf_op jit(solution)/shard_map/ppermute | solution.py:450
  29.4 1.4 collective-permute-start.13
  30.7 2.3 %pack.7 = (bf16[256,1536]{1,0:T(8,128)(2,1)}, bf16[256,1536]{1,0:T(8,128)(2,1)}) custom-call(s32[1]{0:T(128)} %bitcast.4.me_ref, bf16[256,12288]{1,0:T(8,128)(2,1)} %bitcast.66), custom_call_target="tpu_custom_call" | custom-call | bytes 3145728 | tf_op jit(solution)/shard_map/pack/pallas_call | solution.py:69
  33.1 3.0 %collective-permute-done.15.refs_6_ = f32[384,128]{1,0:T(8,128)S(1)} collective-permute-done((f32[384,128]{1,0:T(8,128)S(1)}, f32[384,128]{1,0:T(8,128)S(1)}, u32[]{:S(2)}, u32[]{:S(2)}) %collective-permute-start.15) | collective-permute-done | bytes 196640 | tf_op jit(solution)/shard_map/ppermute | solution.py:450
  36.1 2.3 %pack.5 = (bf16[256,1536]{1,0:T(8,128)(2,1)}, bf16[256,1536]{1,0:T(8,128)(2,1)}) custom-call(s32[1]{0:T(128)} %bitcast.4.me_ref, bf16[256,12288]{1,0:T(8,128)(2,1)} %bitcast.67), custom_call_target="tpu_custom_call" | custom-call | bytes 3145728 | tf_op jit(solution)/shard_map/pack/pallas_call | solution.py:69
  38.4 6.0 %collective-permute-done.14.refs_5_ = f32[384,128]{1,0:T(8,128)S(1)} collective-permute-done((f32[384,128]{1,0:T(8,128)S(1)}, f32[384,128]{1,0:T(8,128)S(1)}, u32[]{:S(2)}, u32[]{:S(2)}) %collective-permute-start.14) | collective-permute-done | bytes 196640 | tf_op jit(solution)/shard_map/ppermute | solution.py:450
  44.4 2.7 %collective-permute-start.1 = (bf16[256,1536]{1,0:T(8,128)(2,1)}, bf16[256,1536]{1,0:T(8,128)(2,1)S(1)}, u32[]{:S(2)}, u32[]{:S(2)}) collective-permute-start(bf16[256,1536]{1,0:T(8,128)(2,1)} %get-tuple-element.71), channel_id=1, source_target_pairs={{0,3},{1,2},{2,1},{3,0},{4,7},{5,6},{6,5},{7,4},{8,11},{9,10},{10,... | collective-permute-start | bytes 2359304 | tf_op jit(solution)/shard_map/ppermute | solution.py:450
  48.2 3.5 %cast_left.1.refs_4_ = bf16[1536,512]{1,0:T(8,128)(2,1)S(1)} custom-call(f32[1536,1024]{1,0:T(8,128)} %bitcast.39), custom_call_target="tpu_custom_call" | custom-call | bytes 4718592 | tf_op jit(solution)/shard_map/cast_left/pallas_call | solution.py:93
  51.7 0.6 partial_keys.9
  52.3 0.7 collective-permute-start.5
  53.9 10.6 %collective-permute-done.8.refs_0_.refs_1_.refs_2_.refs_3_ = bf16[256,1536]{1,0:T(8,128)(2,1)S(1)} collective-permute-done((bf16[256,1536]{1,0:T(8,128)(2,1)}, bf16[256,1536]{1,0:T(8,128)(2,1)S(1)}, u32[]{:S(2)}, u32[]{:S(2)}) %collective-permute-start.8) | collective-permute-done | bytes 786464 | tf_op jit(solution)/shard_map/ppermute | solution.py:450
  64.5 1.5 collective-permute-start.22
  66.0 2.8 %duplicate.1 = (f32[384,1024]{1,0:T(8,128)}, f32[384,1024]{1,0:T(8,128)}) custom-call(f32[384,1024]{1,0:T(8,128)} %refs_0_.3, f32[384,1024]{1,0:T(8,128)} %refs_1_.3), custom_call_target="tpu_custom_call" | custom-call | bytes 6291456 | tf_op jit(solution)/shard_map/duplicate/pallas_call | solution.py:389
  68.8 2.1 %due_columns.3 = (f32[4,384,128]{2,1,0:T(8,128)S(1)}, f32[4,384,128]{2,1,0:T(8,128)S(1)}) custom-call(s32[2]{0:T(128)S(1)} %pad_add_fusion.place_ref, f32[1536,1024]{1,0:T(8,128)} %bitcast.44, f32[1536,1024]{1,0:T(8,128)} %bitcast.45, f32[1536,1024]{1,0:T(8,128)} %bitcast.46, f32[1536,1024]{1,0:T(8,128)} %bitcast.47, f32[1536,1024]{1,0:T(8,128)} %bitcast.52, ...), custom_call_target="tpu_custom_call" | custom-call | bytes 3145728 | tf_op jit(solution)/shard_map/due_columns/pallas_call | solution.py:348
  71.0 1.7 %collective-permute-start.24 = (bf16[256,512]{1,0:T(8,128)(2,1)S(1)}, bf16[256,512]{1,0:T(8,128)(2,1)S(1)}, u32[]{:S(2)}, u32[]{:S(2)}) collective-permute-start(bf16[256,512]{1,0:T(8,128)(2,1)S(1)} %slice.32.refs_4_), channel_id=1, source_target_pairs={{0,4},{1,5},{2,6},{3,7},{4,0},{5,1},{6,2},{7,3},{8,12},{9,13},{10,... | collective-permute-start | bytes 786440 | tf_op jit(solution)/shard_map/ppermute | solution.py:450
  72.7 0.6 partial_keys.12
  73.2 9.8 %collective-permute-done.refs_0_.refs_1_.refs_2_.refs_3_ = bf16[256,1536]{1,0:T(8,128)(2,1)S(1)} collective-permute-done((bf16[256,1536]{1,0:T(8,128)(2,1)S(1)}, bf16[256,1536]{1,0:T(8,128)(2,1)S(1)}, u32[]{:S(2)}, u32[]{:S(2)}) %collective-permute-start) | collective-permute-done | bytes 786464 | tf_op jit(solution)/shard_map/ppermute | solution.py:450
  83.1 0.6 partial_keys.8
  84.2 0.6 partial_keys.10
  84.8 3.1 %collective-permute-done.22.refs_4_ = bf16[256,512]{1,0:T(8,128)(2,1)S(1)} collective-permute-done((bf16[256,512]{1,0:T(8,128)(2,1)S(1)}, bf16[256,512]{1,0:T(8,128)(2,1)S(1)}, u32[]{:S(2)}, u32[]{:S(2)}) %collective-permute-start.22) | collective-permute-done | bytes 262176 | tf_op jit(solution)/shard_map/ppermute | solution.py:450
  88.4 1.5 collective-permute-start.16
  89.9 0.7 collective-permute-start.27
  90.6 0.6 partial_keys.14
  91.3 2.9 %collective-permute-done.6.refs_6_ = bf16[128,512]{1,0:T(8,128)(2,1)S(1)} collective-permute-done((bf16[128,512]{1,0:T(8,128)(2,1)S(1)}, bf16[128,512]{1,0:T(8,128)(2,1)S(1)}, u32[]{:S(2)}, u32[]{:S(2)}) %collective-permute-start.6) | collective-permute-done | bytes 131104 | tf_op jit(solution)/shard_map/ppermute | solution.py:450
  94.7 0.6 partial_keys.11
  95.3 1.6 collective-permute-start.17
  96.9 0.6 partial_keys.13
  97.8 2.6 %collective-permute-done.28 = bf16[128,512]{1,0:T(8,128)(2,1)S(1)} collective-permute-done((bf16[128,512]{1,0:T(8,128)(2,1)S(1)}, bf16[128,512]{1,0:T(8,128)(2,1)S(1)}, u32[]{:S(2)}, u32[]{:S(2)}) %collective-permute-start.28) | collective-permute-done | bytes 131104 | tf_op jit(solution)/shard_map/ppermute | solution.py:450
  101.1 2.1 %collective-permute-done.17.refs_0_ = bf16[256,512]{1,0:T(8,128)(2,1)S(1)} collective-permute-done((bf16[256,512]{1,0:T(8,128)(2,1)S(1)}, bf16[256,512]{1,0:T(8,128)(2,1)S(1)}, u32[]{:S(2)}, u32[]{:S(2)}) %collective-permute-start.17) | collective-permute-done | bytes 262176 | tf_op jit(solution)/shard_map/ppermute | solution.py:450
  103.2 0.6 partial_keys.15
  104.4 1.5 collective-permute-start.34
  106.1 1.0 collective-permute-start.31
  107.1 3.2 %gradient.4.refs_8_ = f32[1536,512]{1,0:T(8,128)S(1)} custom-call(s32[2]{0:T(128)S(1)} %pad_add_fusion.place_ref, bf16[1536,256]{1,0:T(8,128)(2,1)S(1)} %get-tuple-element.102.refs_0_, bf16[1536,256]{1,0:T(8,128)(2,1)S(1)} %get-tuple-element.103.refs_1_, bf16[1536,256]{1,0:T(8,128)(2,1)S(1)} %get-tuple-element.104.refs_2_, ...), custom_call_target="tpu_custom_call" | custom-call | flops 1610612736 | bytes 6291456 | tf_op jit(solution)/shard_map/gradient/pallas_call | solution.py:236
  110.3 1.1 collective-permute-start.21
  111.4 3.6 %gradient.5 = (f32[1536,512]{1,0:T(8,128)S(1)}, f32[8,128]{1,0:T(8,128)S(1)}, f32[1536,128]{1,0:T(8,128)S(1)}) custom-call(s32[2]{0:T(128)S(1)} %pad_add_fusion.place_ref, bf16[1536,256]{1,0:T(8,128)(2,1)S(1)} %get-tuple-element.76.refs_0_, bf16[1536,256]{1,0:T(8,128)(2,1)S(1)} %get-tuple-element.77.refs_1_, ...), custom_call_target="tpu_custom_call" | custom-call | flops 1610612736 | bytes 6291456 | tf_op jit(solution)/shard_map/gradient/pallas_call | solution.py:236
  115.1 4.6 %collective-permute-done.31.refs_6_ = bf16[256,512]{1,0:T(8,128)(2,1)S(1)} collective-permute-done((bf16[256,512]{1,0:T(8,128)(2,1)S(1)}, bf16[256,512]{1,0:T(8,128)(2,1)S(1)}, u32[]{:S(2)}, u32[]{:S(2)}) %collective-permute-start.31) | collective-permute-done | bytes 262176 | tf_op jit(solution)/shard_map/ppermute | solution.py:450
  120.2 3.2 %gradient.6.refs_8_ = f32[1536,512]{1,0:T(8,128)S(1)} custom-call(s32[2]{0:T(128)S(1)} %pad_add_fusion.place_ref, bf16[1536,256]{1,0:T(8,128)(2,1)S(1)} %get-tuple-element.102.refs_0_, bf16[1536,256]{1,0:T(8,128)(2,1)S(1)} %get-tuple-element.103.refs_1_, bf16[1536,256]{1,0:T(8,128)(2,1)S(1)} %get-tuple-element.104.refs_2_, ...), custom_call_target="tpu_custom_call" | custom-call | flops 1610612736 | bytes 6291456 | tf_op jit(solution)/shard_map/gradient/pallas_call | solution.py:236
  123.4 3.6 %gradient.7 = (f32[1536,512]{1,0:T(8,128)S(1)}, f32[8,128]{1,0:T(8,128)S(1)}, f32[1536,128]{1,0:T(8,128)S(1)}) custom-call(s32[2]{0:T(128)S(1)} %pad_add_fusion.place_ref, bf16[1536,256]{1,0:T(8,128)(2,1)S(1)} %get-tuple-element.76.refs_0_, bf16[1536,256]{1,0:T(8,128)(2,1)S(1)} %get-tuple-element.77.refs_1_, ...), custom_call_target="tpu_custom_call" | custom-call | flops 1610612736 | bytes 6291456 | tf_op jit(solution)/shard_map/gradient/pallas_call | solution.py:236
  127.1 1.1 collective-permute-done.36
  128.3 1.5 collective-permute-start.39
  129.7 1.0 collective-permute-start.38
  130.7 1.0 collective-permute-start.37
  131.8 1.0 collective-permute-done.39.refs_3_
  133.3 1.0 collective-permute-done.37.refs_1_
  134.3 1.6 adam_frag.1
  135.9 1.9 %collective-permute-start.40 = (bf16[384,128]{1,0:T(8,128)(2,1)S(1)}, bf16[384,128]{1,0:T(8,128)(2,1)S(1)}, u32[]{:S(2)}, u32[]{:S(2)}) collective-permute-start(bf16[384,128]{1,0:T(8,128)(2,1)S(1)} %get-tuple-element.122), channel_id=1, source_target_pairs={{0,8},{8,0},{16,24},{24,16},{1,9},{9,1},{17,25},{25,17},{2,10},{10... | collective-permute-start | bytes 294920 | tf_op jit(solution)/shard_map/ppermute | solution.py:450
  137.8 1.0 collective-permute-start.41
  138.8 1.6 collective-permute-start.42
  140.4 6.0 %adam_rows.2 = (f32[1536,1024]{1,0:T(8,128)}, f32[1536,1024]{1,0:T(8,128)}, f32[1536,1024]{1,0:T(8,128)}, f32[8,128]{1,0:T(8,128)S(1)}) custom-call(f32[3]{0:T(128)S(1)} %pad_maximum_fusion.sc_ref, f32[1536,1024]{1,0:T(8,128)S(1)} %bitcast.42, f32[1536,1024]{1,0:T(8,128)S(1)} %bitcast.50, f32[1536,1024]{1,0:T(8,128)S(1)} %bitcast.58, ...), custom_call_target="tpu_custom_call" | custom-call | flops 15728640 | bytes 22020096 | tf_op jit(solution)/shard_map/adam_rows/pallas_call | solution.py:291
  146.4 0.6 collective-permute-done.41
  147.1 1.8 %collective-permute-start.45 = (bf16[384,128]{1,0:T(8,128)(2,1)S(1)}, bf16[384,128]{1,0:T(8,128)(2,1)S(1)}, u32[]{:S(2)}, u32[]{:S(2)}) collective-permute-start(bf16[384,128]{1,0:T(8,128)(2,1)S(1)} %convert_element_type.24.refs_7_), channel_id=1, source_target_pairs={{0,24},{8,16},{16,8},{24,0},{1,25},{9,17},{17,9},{25,1},{2,26},{10... | collective-permute-start | bytes 294920 | tf_op jit(solution)/shard_map/ppermute | solution.py:450
  149.0 1.3 collective-permute-start.44
  150.3 1.3 collective-permute-start.43
  151.6 6.0 %adam_rows.3 = (f32[1536,1024]{1,0:T(8,128)}, f32[1536,1024]{1,0:T(8,128)}, f32[1536,1024]{1,0:T(8,128)}) custom-call(f32[3]{0:T(128)S(1)} %pad_maximum_fusion.sc_ref, f32[1536,1024]{1,0:T(8,128)S(1)} %bitcast.43, f32[1536,1024]{1,0:T(8,128)S(1)} %bitcast.51, ...), custom_call_target="tpu_custom_call", output_to_operand_aliasing={{0}: (10, {}), {1}: (11, {}), {2}: (12, {})} | custom-call | flops 15728640 | bytes 22020096 | tf_op jit(solution)/shard_map/adam_rows/pallas_call | solution.py:291
  157.6 2.4 %outer_step.1 = (f32[1536,1024]{1,0:T(8,128)}, f32[384,1024]{1,0:T(8,128)}, f32[384,1024]{1,0:T(8,128)}) custom-call(s32[2]{0:T(128)S(1)} %pad_add_fusion.place_ref, f32[1536,1024]{1,0:T(8,128)} %get-tuple-element.119.refs_0_, f32[384,1024]{1,0:T(8,128)} %get-tuple-element.80.refs_1_, ...), custom_call_target="tpu_custom_call", output_to_operand_aliasing={{0}: (1, {}), {1}: (2, {}), {2}: (3, {})} | custom-call | flops 1966080 | bytes 3932160 | tf_op jit(solution)/shard_map/outer_step/pallas_call | solution.py:432
  (89 shorter events, 6.6 us)
Async XLA Ops:
  3.2 14.5 %collective-permute-start.10 = (f32[384,128]{1,0:T(8,128)S(1)}, f32[384,128]{1,0:T(8,128)S(1)}, u32[]{:S(2)}, u32[]{:S(2)}) collective-permute-start(f32[384,128]{1,0:T(8,128)S(1)} %get-tuple-element.136), channel_id=1, source_target_pairs={{0,8},{8,0},{16,24},{24,16},{1,9},{9,1},{17,25},{25,17},{2,10},{10... | collective-permute-start | bytes 589832 | tf_op jit(solution)/shard_map/ppermute | solution.py:450
  6.3 12.6 %collective-permute-start.12 = (f32[384,128]{1,0:T(8,128)S(1)}, f32[384,128]{1,0:T(8,128)S(1)}, u32[]{:S(2)}, u32[]{:S(2)}) collective-permute-start(f32[384,128]{1,0:T(8,128)S(1)} %get-tuple-element.137), channel_id=1, source_target_pairs={{0,24},{8,16},{16,8},{24,0},{1,25},{9,17},{17,9},{25,1},{2,26},{10... | collective-permute-start | bytes 589832 | tf_op jit(solution)/shard_map/ppermute | solution.py:450
  8.8 17.4 %collective-permute-start.11 = (f32[384,128]{1,0:T(8,128)S(1)}, f32[384,128]{1,0:T(8,128)S(1)}, u32[]{:S(2)}, u32[]{:S(2)}) collective-permute-start(f32[384,128]{1,0:T(8,128)S(1)} %get-tuple-element.138), channel_id=1, source_target_pairs={{0,16},{8,24},{16,0},{24,8},{1,17},{9,25},{17,1},{25,9},{2,18},{10... | collective-permute-start | bytes 589832 | tf_op jit(solution)/shard_map/ppermute | solution.py:450
  10.9 36.2 %collective-permute-start.3 = (bf16[256,1536]{1,0:T(8,128)(2,1)}, bf16[256,1536]{1,0:T(8,128)(2,1)S(1)}, u32[]{:S(2)}, u32[]{:S(2)}) collective-permute-start(bf16[256,1536]{1,0:T(8,128)(2,1)} %pack.6), channel_id=1, source_target_pairs={{0,6},{1,7},{2,4},{3,5},{4,2},{5,3},{6,0},{7,1},{8,14},{9,15},{10,... | collective-permute-start | bytes 2359304 | tf_op jit(solution)/shard_map/ppermute | solution.py:450
  16.0 31.6 %collective-permute-start.4 = (bf16[256,1536]{1,0:T(8,128)(2,1)}, bf16[256,1536]{1,0:T(8,128)(2,1)S(1)}, u32[]{:S(2)}, u32[]{:S(2)}) collective-permute-start(bf16[256,1536]{1,0:T(8,128)(2,1)} %get-tuple-element.73), channel_id=1, source_target_pairs={{0,7},{1,6},{2,5},{3,4},{4,3},{5,2},{6,1},{7,0},{8,15},{9,14},{10,... | collective-permute-start | bytes 2359304 | tf_op jit(solution)/shard_map/ppermute | solution.py:450
  26.3 20.8 %copy-start.3 = (bf16[256,1536]{1,0:T(8,128)(2,1)S(1)}, bf16[256,1536]{1,0:T(8,128)(2,1)}, u32[]{:S(2)}) copy-start(bf16[256,1536]{1,0:T(8,128)(2,1)} %get-tuple-element.70) | copy-start | bytes 2359300
  26.3 21.4 %copy-start.2 = (bf16[256,1536]{1,0:T(8,128)(2,1)S(1)}, bf16[256,1536]{1,0:T(8,128)(2,1)}, u32[]{:S(2)}) copy-start(bf16[256,1536]{1,0:T(8,128)(2,1)} %get-tuple-element.78) | copy-start | bytes 2359300
  26.3 9.8 %collective-permute-start.15 = (f32[384,128]{1,0:T(8,128)S(1)}, f32[384,128]{1,0:T(8,128)S(1)}, u32[]{:S(2)}, u32[]{:S(2)}) collective-permute-start(f32[384,128]{1,0:T(8,128)S(1)} %get-tuple-element.134.refs_3_), channel_id=1, source_target_pairs={{0,24},{8,16},{16,8},{24,0},{1,25},{9,17},{17,9},{25,1},{2,26},{10... | collective-permute-start | bytes 589832 | tf_op jit(solution)/shard_map/ppermute | solution.py:450
  29.4 15.0 %collective-permute-start.14 = (f32[384,128]{1,0:T(8,128)S(1)}, f32[384,128]{1,0:T(8,128)S(1)}, u32[]{:S(2)}, u32[]{:S(2)}) collective-permute-start(f32[384,128]{1,0:T(8,128)S(1)} %get-tuple-element.134.refs_3_), channel_id=1, source_target_pairs={{0,16},{8,24},{16,0},{24,8},{1,17},{9,25},{17,1},{25,9},{2,18},{10... | collective-permute-start | bytes 589832 | tf_op jit(solution)/shard_map/ppermute | solution.py:450
  29.4 15.0 %collective-permute-start.13 = (f32[384,128]{1,0:T(8,128)S(1)}, f32[384,128]{1,0:T(8,128)S(1)}, u32[]{:S(2)}, u32[]{:S(2)}) collective-permute-start(f32[384,128]{1,0:T(8,128)S(1)} %get-tuple-element.134.refs_3_), channel_id=1, source_target_pairs={{0,8},{8,0},{16,24},{24,16},{1,9},{9,1},{17,25},{25,17},{2,10},{10... | collective-permute-start | bytes 589832 | tf_op jit(solution)/shard_map/ppermute | solution.py:450
  36.1 16.2 %collective-permute-start.19 = (bf16[256,1536]{1,0:T(8,128)(2,1)}, bf16[256,1536]{1,0:T(8,128)(2,1)S(1)}, u32[]{:S(2)}, u32[]{:S(2)}) collective-permute-start(bf16[256,1536]{1,0:T(8,128)(2,1)} %get-tuple-element.95), channel_id=1, source_target_pairs={{0,1},{1,0},{2,3},{3,2},{4,5},{5,4},{6,7},{7,6},{8,9},{9,8},{10,11... | collective-permute-start | bytes 2359304 | tf_op jit(solution)/shard_map/ppermute | solution.py:450
  44.4 20.1 %collective-permute-start.8 = (bf16[256,1536]{1,0:T(8,128)(2,1)}, bf16[256,1536]{1,0:T(8,128)(2,1)S(1)}, u32[]{:S(2)}, u32[]{:S(2)}) collective-permute-start(bf16[256,1536]{1,0:T(8,128)(2,1)} %get-tuple-element.79), channel_id=1, source_target_pairs={{0,5},{1,4},{2,7},{3,6},{4,1},{5,0},{6,3},{7,2},{8,13},{9,12},{10,... | collective-permute-start | bytes 2359304 | tf_op jit(solution)/shard_map/ppermute | solution.py:450
  44.4 26.6 %collective-permute-start.1 = (bf16[256,1536]{1,0:T(8,128)(2,1)}, bf16[256,1536]{1,0:T(8,128)(2,1)S(1)}, u32[]{:S(2)}, u32[]{:S(2)}) collective-permute-start(bf16[256,1536]{1,0:T(8,128)(2,1)} %get-tuple-element.71), channel_id=1, source_target_pairs={{0,3},{1,2},{2,1},{3,0},{4,7},{5,6},{6,5},{7,4},{8,11},{9,10},{10,... | collective-permute-start | bytes 2359304 | tf_op jit(solution)/shard_map/ppermute | solution.py:450
  47.1 36.0 %collective-permute-start = (bf16[256,1536]{1,0:T(8,128)(2,1)S(1)}, bf16[256,1536]{1,0:T(8,128)(2,1)S(1)}, u32[]{:S(2)}, u32[]{:S(2)}) collective-permute-start(bf16[256,1536]{1,0:T(8,128)(2,1)S(1)} %copy-done.3), channel_id=1, source_target_pairs={{0,2},{1,3},{2,0},{3,1},{4,6},{5,7},{6,4},{7,5},{8,10},{9,11},{10,... | collective-permute-start | bytes 2359304 | tf_op jit(solution)/shard_map/ppermute | solution.py:450
  47.6 6.2 %copy-start.1 = (bf16[1,256,1024]{2,1,0:T(8,128)(2,1)S(1)}, bf16[1,256,1024]{2,1,0:T(8,128)(2,1)}, u32[]{:S(2)}) copy-start(bf16[1,256,1024]{2,1,0:T(8,128)(2,1)} %param.10) | copy-start | bytes 1572868
  47.6 47.7 %collective-permute-start.7 = (bf16[256,1536]{1,0:T(8,128)(2,1)S(1)}, bf16[256,1536]{1,0:T(8,128)(2,1)S(1)}, u32[]{:S(2)}, u32[]{:S(2)}) collective-permute-start(bf16[256,1536]{1,0:T(8,128)(2,1)S(1)} %copy-done.2), channel_id=1, source_target_pairs={{0,4},{1,5},{2,6},{3,7},{4,0},{5,1},{6,2},{7,3},{8,12},{9,13},{10,... | collective-permute-start | bytes 2359304 | tf_op jit(solution)/shard_map/ppermute | solution.py:450
  52.3 31.4 %collective-permute-start.5 = (bf16[256,512]{1,0:T(8,128)(2,1)S(1)}, bf16[256,512]{1,0:T(8,128)(2,1)S(1)}, u32[]{:S(2)}, u32[]{:S(2)}) collective-permute-start(bf16[256,512]{1,0:T(8,128)(2,1)S(1)} %get-tuple-element.74), channel_id=1, source_target_pairs={{0,1},{1,0},{2,3},{3,2},{4,5},{5,4},{6,7},{7,6},{8,9},{9,8},{10,11... | collective-permute-start | bytes 786440 | tf_op jit(solution)/shard_map/ppermute | solution.py:450
  64.5 23.4 %collective-permute-start.22 = (bf16[256,512]{1,0:T(8,128)(2,1)S(1)}, bf16[256,512]{1,0:T(8,128)(2,1)S(1)}, u32[]{:S(2)}, u32[]{:S(2)}) collective-permute-start(bf16[256,512]{1,0:T(8,128)(2,1)S(1)} %slice.32.refs_4_), channel_id=1, source_target_pairs={{0,2},{1,3},{2,0},{3,1},{4,6},{5,7},{6,4},{7,5},{8,10},{9,11},{10,... | collective-permute-start | bytes 786440 | tf_op jit(solution)/shard_map/ppermute | solution.py:450
  71.0 17.4 %collective-permute-start.24 = (bf16[256,512]{1,0:T(8,128)(2,1)S(1)}, bf16[256,512]{1,0:T(8,128)(2,1)S(1)}, u32[]{:S(2)}, u32[]{:S(2)}) collective-permute-start(bf16[256,512]{1,0:T(8,128)(2,1)S(1)} %slice.32.refs_4_), channel_id=1, source_target_pairs={{0,4},{1,5},{2,6},{3,7},{4,0},{5,1},{6,2},{7,3},{8,12},{9,13},{10,... | collective-permute-start | bytes 786440 | tf_op jit(solution)/shard_map/ppermute | solution.py:450
  83.1 6.9 %collective-permute-start.9 = (bf16[256,512]{1,0:T(8,128)(2,1)S(1)}, bf16[256,512]{1,0:T(8,128)(2,1)S(1)}, u32[]{:S(2)}, u32[]{:S(2)}) collective-permute-start(bf16[256,512]{1,0:T(8,128)(2,1)S(1)} %get-tuple-element.85), channel_id=1, source_target_pairs={{0,1},{1,0},{2,3},{3,2},{4,5},{5,4},{6,7},{7,6},{8,9},{9,8},{10,11... | collective-permute-start | bytes 786440 | tf_op jit(solution)/shard_map/ppermute | solution.py:450
  83.6 7.6 %collective-permute-start.2 = (bf16[256,512]{1,0:T(8,128)(2,1)S(1)}, bf16[256,512]{1,0:T(8,128)(2,1)S(1)}, u32[]{:S(2)}, u32[]{:S(2)}) collective-permute-start(bf16[256,512]{1,0:T(8,128)(2,1)S(1)} %get-tuple-element.72), channel_id=1, source_target_pairs={{0,1},{1,0},{2,3},{3,2},{4,5},{5,4},{6,7},{7,6},{8,9},{9,8},{10,11... | collective-permute-start | bytes 786440 | tf_op jit(solution)/shard_map/ppermute | solution.py:450
  87.9 6.3 %collective-permute-start.6 = (bf16[128,512]{1,0:T(8,128)(2,1)S(1)}, bf16[128,512]{1,0:T(8,128)(2,1)S(1)}, u32[]{:S(2)}, u32[]{:S(2)}) collective-permute-start(bf16[128,512]{1,0:T(8,128)(2,1)S(1)} %get-tuple-element.75), channel_id=1, source_target_pairs={{0,4},{1,5},{2,6},{3,7},{4,0},{5,1},{6,2},{7,3},{8,12},{9,13},{10,... | collective-permute-start | bytes 393224 | tf_op jit(solution)/shard_map/ppermute | solution.py:450
  88.4 8.5 %collective-permute-start.16 = (bf16[128,512]{1,0:T(8,128)(2,1)S(1)}, bf16[128,512]{1,0:T(8,128)(2,1)S(1)}, u32[]{:S(2)}, u32[]{:S(2)}) collective-permute-start(bf16[128,512]{1,0:T(8,128)(2,1)S(1)} %get-tuple-element.89), channel_id=1, source_target_pairs={{0,2},{1,3},{2,0},{3,1},{4,6},{5,7},{6,4},{7,5},{8,10},{9,11},{10,... | collective-permute-start | bytes 393224 | tf_op jit(solution)/shard_map/ppermute | solution.py:450
  89.9 7.8 %collective-permute-start.27 = (bf16[128,512]{1,0:T(8,128)(2,1)S(1)}, bf16[128,512]{1,0:T(8,128)(2,1)S(1)}, u32[]{:S(2)}, u32[]{:S(2)}) collective-permute-start(bf16[128,512]{1,0:T(8,128)(2,1)S(1)} %slice.33), channel_id=1, source_target_pairs={{0,4},{1,5},{2,6},{3,7},{4,0},{5,1},{6,2},{7,3},{8,12},{9,13},{10,... | collective-permute-start | bytes 393224 | tf_op jit(solution)/shard_map/ppermute | solution.py:450
  91.2 12.0 %copy-start = (bf16[256,1536]{1,0:T(8,128)(2,1)S(1)}, bf16[256,1536]{1,0:T(8,128)(2,1)}, u32[]{:S(2)}) copy-start(bf16[256,1536]{1,0:T(8,128)(2,1)} %get-tuple-element.94.refs_0_.refs_1_.refs_2_.refs_3_) | copy-start | bytes 2359300
  91.2 9.8 %collective-permute-start.20 = (bf16[256,512]{1,0:T(8,128)(2,1)S(1)}, bf16[256,512]{1,0:T(8,128)(2,1)S(1)}, u32[]{:S(2)}, u32[]{:S(2)}) collective-permute-start(bf16[256,512]{1,0:T(8,128)(2,1)S(1)} %get-tuple-element.96), channel_id=1, source_target_pairs={{0,1},{1,0},{2,3},{3,2},{4,5},{5,4},{6,7},{7,6},{8,9},{9,8},{10,11... | collective-permute-start | bytes 786440 | tf_op jit(solution)/shard_map/ppermute | solution.py:450
  94.2 6.2 %collective-permute-start.28 = (bf16[128,512]{1,0:T(8,128)(2,1)S(1)}, bf16[128,512]{1,0:T(8,128)(2,1)S(1)}, u32[]{:S(2)}, u32[]{:S(2)}) collective-permute-start(bf16[128,512]{1,0:T(8,128)(2,1)S(1)} %slice.34), channel_id=1, source_target_pairs={{0,2},{1,3},{2,0},{3,1},{4,6},{5,7},{6,4},{7,5},{8,10},{9,11},{10,... | collective-permute-start | bytes 393224 | tf_op jit(solution)/shard_map/ppermute | solution.py:450
  95.3 7.9 %collective-permute-start.17 = (bf16[256,512]{1,0:T(8,128)(2,1)S(1)}, bf16[256,512]{1,0:T(8,128)(2,1)S(1)}, u32[]{:S(2)}, u32[]{:S(2)}) collective-permute-start(bf16[256,512]{1,0:T(8,128)(2,1)S(1)} %get-tuple-element.92), channel_id=1, source_target_pairs={{0,2},{1,3},{2,0},{3,1},{4,6},{5,7},{6,4},{7,5},{8,10},{9,11},{10,... | collective-permute-start | bytes 786440 | tf_op jit(solution)/shard_map/ppermute | solution.py:450
  97.5 6.4 %collective-permute-start.18 = (bf16[256,512]{1,0:T(8,128)(2,1)S(1)}, bf16[256,512]{1,0:T(8,128)(2,1)S(1)}, u32[]{:S(2)}, u32[]{:S(2)}) collective-permute-start(bf16[256,512]{1,0:T(8,128)(2,1)S(1)} %get-tuple-element.93), channel_id=1, source_target_pairs={{0,4},{1,5},{2,6},{3,7},{4,0},{5,1},{6,2},{7,3},{8,12},{9,13},{10,... | collective-permute-start | bytes 786440 | tf_op jit(solution)/shard_map/ppermute | solution.py:450
  100.4 5.5 %collective-permute-start.26 = (bf16[256,512]{1,0:T(8,128)(2,1)S(1)}, bf16[256,512]{1,0:T(8,128)(2,1)S(1)}, u32[]{:S(2)}, u32[]{:S(2)}) collective-permute-start(bf16[256,512]{1,0:T(8,128)(2,1)S(1)} %slice.32.refs_4_), channel_id=1, source_target_pairs={{0,1},{1,0},{2,3},{3,2},{4,5},{5,4},{6,7},{7,6},{8,9},{9,8},{10,11... | collective-permute-start | bytes 786440 | tf_op jit(solution)/shard_map/ppermute | solution.py:450
  100.5 5.6 %collective-permute-start.29 = (bf16[256,512]{1,0:T(8,128)(2,1)S(1)}, bf16[256,512]{1,0:T(8,128)(2,1)S(1)}, u32[]{:S(2)}, u32[]{:S(2)}) collective-permute-start(bf16[256,512]{1,0:T(8,128)(2,1)S(1)} %constant_dynamic-update-slice_fusion.refs_6_), channel_id=1, source_target_pairs={{0,1},{1,0},{2,3},{3,2},{4,5},{5,4},{6,7},{7,6},{8,9},{9,8},{10,11... | collective-permute-start | bytes 786440 | tf_op jit(solution)/shard_map/ppermute | solution.py:450
  101.0 9.3 %collective-permute-start.23 = (bf16[256,512]{1,0:T(8,128)(2,1)S(1)}, bf16[256,512]{1,0:T(8,128)(2,1)S(1)}, u32[]{:S(2)}, u32[]{:S(2)}) collective-permute-start(bf16[256,512]{1,0:T(8,128)(2,1)S(1)} %collective-permute-done.22.refs_4_), channel_id=1, source_target_pairs={{0,1},{1,0},{2,3},{3,2},{4,5},{5,4},{6,7},{7,6},{8,9},{9,8},{10,11... | collective-permute-start | bytes 786440 | tf_op jit(solution)/shard_map/ppermute | solution.py:450
  103.2 8.2 %collective-permute-start.25 = (bf16[256,512]{1,0:T(8,128)(2,1)S(1)}, bf16[256,512]{1,0:T(8,128)(2,1)S(1)}, u32[]{:S(2)}, u32[]{:S(2)}) collective-permute-start(bf16[256,512]{1,0:T(8,128)(2,1)S(1)} %collective-permute-done.24.refs_6_), channel_id=1, source_target_pairs={{0,1},{1,0},{2,3},{3,2},{4,5},{5,4},{6,7},{7,6},{8,9},{9,8},{10,11... | collective-permute-start | bytes 786440 | tf_op jit(solution)/shard_map/ppermute | solution.py:450
  103.2 37.1 %slice-start.4 = ((s8[6291456]{0:T(1024)(128)(4,1)}), s8[4194304]{0:T(1024)(128)(4,1)S(1)}, s32[]{:S(2)}) async-start(s8[6291456]{0:T(1024)(128)(4,1)} %bitcast.56), calls=%async_computation.4 | async-start | bytes 8388608
  104.4 10.6 %collective-permute-start.34 = (bf16[256,512]{1,0:T(8,128)(2,1)S(1)}, bf16[256,512]{1,0:T(8,128)(2,1)S(1)}, u32[]{:S(2)}, u32[]{:S(2)}) collective-permute-start(bf16[256,512]{1,0:T(8,128)(2,1)S(1)} %key_backward.1.refs_4_), channel_id=1, source_target_pairs={{0,6},{1,7},{2,4},{3,5},{4,2},{5,3},{6,0},{7,1},{8,14},{9,15},{10,... | collective-permute-start | bytes 786440 | tf_op jit(solution)/shard_map/ppermute | solution.py:450
  105.9 14.2 %collective-permute-start.33 = (bf16[256,512]{1,0:T(8,128)(2,1)S(1)}, bf16[256,512]{1,0:T(8,128)(2,1)S(1)}, u32[]{:S(2)}, u32[]{:S(2)}) collective-permute-start(bf16[256,512]{1,0:T(8,128)(2,1)S(1)} %key_backward.1.refs_4_), channel_id=1, source_target_pairs={{0,1},{1,0},{2,3},{3,2},{4,5},{5,4},{6,7},{7,6},{8,9},{9,8},{10,11... | collective-permute-start | bytes 786440 | tf_op jit(solution)/shard_map/ppermute | solution.py:450
  106.1 13.5 %collective-permute-start.31 = (bf16[256,512]{1,0:T(8,128)(2,1)S(1)}, bf16[256,512]{1,0:T(8,128)(2,1)S(1)}, u32[]{:S(2)}, u32[]{:S(2)}) collective-permute-start(bf16[256,512]{1,0:T(8,128)(2,1)S(1)} %key_backward.1.refs_4_), channel_id=1, source_target_pairs={{0,4},{1,5},{2,6},{3,7},{4,0},{5,1},{6,2},{7,3},{8,12},{9,13},{10,... | collective-permute-start | bytes 786440 | tf_op jit(solution)/shard_map/ppermute | solution.py:450
  110.3 9.3 %collective-permute-start.21 = (bf16[256,512]{1,0:T(8,128)(2,1)S(1)}, bf16[256,512]{1,0:T(8,128)(2,1)S(1)}, u32[]{:S(2)}, u32[]{:S(2)}) collective-permute-start(bf16[256,512]{1,0:T(8,128)(2,1)S(1)} %key_backward.1.refs_4_), channel_id=1, source_target_pairs={{0,2},{1,3},{2,0},{3,1},{4,6},{5,7},{6,4},{7,5},{8,10},{9,11},{10,... | collective-permute-start | bytes 786440 | tf_op jit(solution)/shard_map/ppermute | solution.py:450
  111.4 29.0 %slice-start.5 = ((s8[6291456]{0:T(1024)(128)(4,1)}), s8[2097152]{0:T(1024)(128)(4,1)S(1)}, s32[]{:S(2)}) async-start(s8[6291456]{0:T(1024)(128)(4,1)} %bitcast.56), calls=%async_computation.5 | async-start | bytes 4194304
  115.0 5.2 %collective-permute-start.35 = (bf16[256,512]{1,0:T(8,128)(2,1)S(1)}, bf16[256,512]{1,0:T(8,128)(2,1)S(1)}, u32[]{:S(2)}, u32[]{:S(2)}) collective-permute-start(bf16[256,512]{1,0:T(8,128)(2,1)S(1)} %collective-permute-done.34.refs_6_), channel_id=1, source_target_pairs={{0,1},{1,0},{2,3},{3,2},{4,5},{5,4},{6,7},{7,6},{8,9},{9,8},{10,11... | collective-permute-start | bytes 786440 | tf_op jit(solution)/shard_map/ppermute | solution.py:450
  119.7 3.7 %collective-permute-start.30 = (bf16[256,512]{1,0:T(8,128)(2,1)S(1)}, bf16[256,512]{1,0:T(8,128)(2,1)S(1)}, u32[]{:S(2)}, u32[]{:S(2)}) collective-permute-start(bf16[256,512]{1,0:T(8,128)(2,1)S(1)} %collective-permute-done.21.refs_4_), channel_id=1, source_target_pairs={{0,1},{1,0},{2,3},{3,2},{4,5},{5,4},{6,7},{7,6},{8,9},{9,8},{10,11... | collective-permute-start | bytes 786440 | tf_op jit(solution)/shard_map/ppermute | solution.py:450
  119.7 3.7 %collective-permute-start.32 = (bf16[256,512]{1,0:T(8,128)(2,1)S(1)}, bf16[256,512]{1,0:T(8,128)(2,1)S(1)}, u32[]{:S(2)}, u32[]{:S(2)}) collective-permute-start(bf16[256,512]{1,0:T(8,128)(2,1)S(1)} %collective-permute-done.31.refs_6_), channel_id=1, source_target_pairs={{0,1},{1,0},{2,3},{3,2},{4,5},{5,4},{6,7},{7,6},{8,9},{9,8},{10,11... | collective-permute-start | bytes 786440 | tf_op jit(solution)/shard_map/ppermute | solution.py:450
  120.2 20.2 %slice-start = ((s8[6291456]{0:T(1024)(128)(4,1)}), s8[4194304]{0:T(1024)(128)(4,1)S(1)}, s32[]{:S(2)}) async-start(s8[6291456]{0:T(1024)(128)(4,1)} %bitcast.40), calls=%async_computation | async-start | bytes 8388608
  120.2 20.2 %slice-start.2 = ((s8[6291456]{0:T(1024)(128)(4,1)}), s8[4194304]{0:T(1024)(128)(4,1)S(1)}, s32[]{:S(2)}) async-start(s8[6291456]{0:T(1024)(128)(4,1)} %bitcast.48), calls=%async_computation.2 | async-start | bytes 8388608
  123.4 17.0 %slice-start.1 = ((s8[6291456]{0:T(1024)(128)(4,1)}), s8[2097152]{0:T(1024)(128)(4,1)S(1)}, s32[]{:S(2)}) async-start(s8[6291456]{0:T(1024)(128)(4,1)} %bitcast.40), calls=%async_computation.1 | async-start | bytes 4194304
  123.4 17.0 %slice-start.3 = ((s8[6291456]{0:T(1024)(128)(4,1)}), s8[2097152]{0:T(1024)(128)(4,1)S(1)}, s32[]{:S(2)}) async-start(s8[6291456]{0:T(1024)(128)(4,1)} %bitcast.48), calls=%async_computation.3 | async-start | bytes 4194304
  127.0 1.2 collective-permute-start.36
  128.3 4.5 %collective-permute-start.39 = (f32[8,128]{1,0:T(8,128)S(1)}, f32[8,128]{1,0:T(8,128)S(1)}, u32[]{:S(2)}, u32[]{:S(2)}) collective-permute-start(f32[8,128]{1,0:T(8,128)S(1)} %add.32.refs_0_), channel_id=1, source_target_pairs={{0,6},{1,7},{2,4},{3,5},{4,2},{5,3},{6,0},{7,1},{8,14},{9,15},{10,... | collective-permute-start | bytes 12296 | tf_op jit(solution)/shard_map/ppermute | solution.py:450
  129.7 3.6 %collective-permute-start.38 = (f32[8,128]{1,0:T(8,128)S(1)}, f32[8,128]{1,0:T(8,128)S(1)}, u32[]{:S(2)}, u32[]{:S(2)}) collective-permute-start(f32[8,128]{1,0:T(8,128)S(1)} %add.32.refs_0_), channel_id=1, source_target_pairs={{0,4},{1,5},{2,6},{3,7},{4,0},{5,1},{6,2},{7,3},{8,12},{9,13},{10,... | collective-permute-start | bytes 12296 | tf_op jit(solution)/shard_map/ppermute | solution.py:450
  130.7 3.6 %collective-permute-start.37 = (f32[8,128]{1,0:T(8,128)S(1)}, f32[8,128]{1,0:T(8,128)S(1)}, u32[]{:S(2)}, u32[]{:S(2)}) collective-permute-start(f32[8,128]{1,0:T(8,128)S(1)} %add.32.refs_0_), channel_id=1, source_target_pairs={{0,2},{1,3},{2,0},{3,1},{4,6},{5,7},{6,4},{7,5},{8,10},{9,11},{10,... | collective-permute-start | bytes 12296 | tf_op jit(solution)/shard_map/ppermute | solution.py:450
  135.9 10.5 %collective-permute-start.40 = (bf16[384,128]{1,0:T(8,128)(2,1)S(1)}, bf16[384,128]{1,0:T(8,128)(2,1)S(1)}, u32[]{:S(2)}, u32[]{:S(2)}) collective-permute-start(bf16[384,128]{1,0:T(8,128)(2,1)S(1)} %get-tuple-element.122), channel_id=1, source_target_pairs={{0,8},{8,0},{16,24},{24,16},{1,9},{9,1},{17,25},{25,17},{2,10},{10... | collective-permute-start | bytes 294920 | tf_op jit(solution)/shard_map/ppermute | solution.py:450
  137.8 9.3 %collective-permute-start.41 = (bf16[384,128]{1,0:T(8,128)(2,1)S(1)}, bf16[384,128]{1,0:T(8,128)(2,1)S(1)}, u32[]{:S(2)}, u32[]{:S(2)}) collective-permute-start(bf16[384,128]{1,0:T(8,128)(2,1)S(1)} %get-tuple-element.123), channel_id=1, source_target_pairs={{0,16},{8,24},{16,0},{24,8},{1,17},{9,25},{17,1},{25,9},{2,18},{10... | collective-permute-start | bytes 294920 | tf_op jit(solution)/shard_map/ppermute | solution.py:450
  138.8 8.3 %collective-permute-start.42 = (bf16[384,128]{1,0:T(8,128)(2,1)S(1)}, bf16[384,128]{1,0:T(8,128)(2,1)S(1)}, u32[]{:S(2)}, u32[]{:S(2)}) collective-permute-start(bf16[384,128]{1,0:T(8,128)(2,1)S(1)} %get-tuple-element.124), channel_id=1, source_target_pairs={{0,24},{8,16},{16,8},{24,0},{1,25},{9,17},{17,9},{25,1},{2,26},{10... | collective-permute-start | bytes 294920 | tf_op jit(solution)/shard_map/ppermute | solution.py:450
  147.1 10.4 %collective-permute-start.45 = (bf16[384,128]{1,0:T(8,128)(2,1)S(1)}, bf16[384,128]{1,0:T(8,128)(2,1)S(1)}, u32[]{:S(2)}, u32[]{:S(2)}) collective-permute-start(bf16[384,128]{1,0:T(8,128)(2,1)S(1)} %convert_element_type.24.refs_7_), channel_id=1, source_target_pairs={{0,24},{8,16},{16,8},{24,0},{1,25},{9,17},{17,9},{25,1},{2,26},{10... | collective-permute-start | bytes 294920 | tf_op jit(solution)/shard_map/ppermute | solution.py:450
  149.0 8.6 %collective-permute-start.44 = (bf16[384,128]{1,0:T(8,128)(2,1)S(1)}, bf16[384,128]{1,0:T(8,128)(2,1)S(1)}, u32[]{:S(2)}, u32[]{:S(2)}) collective-permute-start(bf16[384,128]{1,0:T(8,128)(2,1)S(1)} %convert_element_type.24.refs_7_), channel_id=1, source_target_pairs={{0,16},{8,24},{16,0},{24,8},{1,17},{9,25},{17,1},{25,9},{2,18},{10... | collective-permute-start | bytes 294920 | tf_op jit(solution)/shard_map/ppermute | solution.py:450
  150.3 7.3 %collective-permute-start.43 = (bf16[384,128]{1,0:T(8,128)(2,1)S(1)}, bf16[384,128]{1,0:T(8,128)(2,1)S(1)}, u32[]{:S(2)}, u32[]{:S(2)}) collective-permute-start(bf16[384,128]{1,0:T(8,128)(2,1)S(1)} %convert_element_type.24.refs_7_), channel_id=1, source_target_pairs={{0,8},{8,0},{16,24},{24,16},{1,9},{9,1},{17,25},{25,17},{2,10},{10... | collective-permute-start | bytes 294920 | tf_op jit(solution)/shard_map/ppermute | solution.py:450

commit v17 on v16

--- a/solution.py
+++ b/solution.py
@@ -405,39 +405,47 @@
 def outer_kernel(replicas, place_ref, *refs):
     share = 1.0 / replicas
     base_refs, sum_refs = refs[3:3 + replicas], refs[3 + replicas:3 + 2 * replicas]
-    inner_ref, a_ref, p_ref, m_ref, own_ref, _, w_out, a_out, m_out = refs[3 + 2 * replicas:]
+    inner_ref, a_ref, p_ref, m_ref, own_ref, _, *refs = refs[3 + 2 * replicas:]
+    w_out, a_out, m_out, mixed, new_a, new_m, sems = refs
+    part = a_ref.shape[0]
     scale = share * (1.0 + OUTER_MU) * OUTER_RATE
+    columns = pl.ds(pl.multiple_of(place_ref[0] * FRAG_COLS, FRAG_COLS), FRAG_COLS)
+    copies = []
     for j in range(replicas):
-
-        @pl.when(pl.program_id(0) == j)
-        def _():
-            fresh = base_refs[j][...] - scale * sum_refs[j][...].astype(jnp.float32)
-            w_out[...] = MIX_LOCAL * inner_ref[0] + (1.0 - MIX_LOCAL) * fresh
-
-    @pl.when(pl.program_id(0) == 0)
-    def _():
-        pseudo = p_ref[...] + share * own_ref[...]
-        new_moment = OUTER_MU * m_ref[...] + pseudo
-        m_out[...] = new_moment
-        a_out[...] = a_ref[...] - OUTER_RATE * (OUTER_MU * new_moment + pseudo)
+        fresh = base_refs[j][...] - scale * sum_refs[j][...].astype(jnp.float32)
+        mixed[j] = MIX_LOCAL * inner_ref[j] + (1.0 - MIX_LOCAL) * fresh
+        rows = pl.ds(pl.multiple_of((place_ref[1] ^ j) * part, 8), part)
+        copies.append(pltpu.make_async_copy(mixed.at[j], w_out.at[rows, columns], sems.at[j]))
+        copies[-1].start()
+    pseudo = p_ref[...] + share * own_ref[...]
+    new_moment = OUTER_MU * m_ref[...] + pseudo
+    new_m[...] = new_moment
+    new_a[...] = a_ref[...] - OUTER_RATE * (OUTER_MU * new_moment + pseudo)
+    for i, (src, dst) in enumerate(((new_a, a_out), (new_m, m_out))):
+        copies.append(pltpu.make_async_copy(src, dst.at[:, columns], sems.at[replicas + i]))
+        copies[-1].start()
+    for copy in copies:
+        copy.wait()
 
 
 def outer_step(place, outputs, base, sums, inner, anchor, pseudo, momentum, own_sum, ticket):
     replicas, part = inner.shape[0], inner.shape[1]
-    mixed = pl.BlockSpec((part, FRAG_COLS), lambda j, p: (p[1] ^ j, p[0]))
-    pieces = pl.BlockSpec((1, part, FRAG_COLS), lambda j, p: (j, 0, 0))
-    due = pl.BlockSpec((part, FRAG_COLS), lambda j, p: (0, p[0]))
-    plain = pl.BlockSpec((part, FRAG_COLS), lambda j, p: (0, 0))
     whole = pl.BlockSpec(memory_space=pl.ANY)
+    held = pl.BlockSpec(memory_space=pltpu.VMEM)
     return pl.pallas_call(
         functools.partial(outer_kernel, replicas),
         out_shape=[pltpu.HBM(a.shape, a.dtype) for a in outputs],
-        grid_spec=pltpu.PrefetchScalarGridSpec(
-            num_scalar_prefetch=1,
-            grid=(replicas,),
-            in_specs=[whole] * 3 + [plain] * (2 * replicas) + [pieces] + [plain] * 4 + [whole],
-            out_specs=[mixed, due, due],
-        ),
+        in_specs=[pl.BlockSpec(memory_space=pltpu.SMEM)]
+        + [whole] * 3
+        + [held] * (2 * replicas + 5)
+        + [whole],
+        out_specs=[whole] * 3,
+        scratch_shapes=[
+            pltpu.VMEM((replicas, part, FRAG_COLS), jnp.float32),
+            pltpu.VMEM((part, FRAG_COLS), jnp.float32),
+            pltpu.VMEM((part, FRAG_COLS), jnp.float32),
+            pltpu.SemaphoreType.DMA((replicas + 2,)),
+        ],
         input_output_aliases={1: 0, 2: 1, 3: 2},
         compiler_params=params_of(12),
         cost_estimate=cost(10 * replicas * part * FRAG_COLS, 20 * replicas * part * FRAG_COLS),
@@ -452,6 +460,15 @@
 
 def after(value, *others):
     return lax.optimization_barrier((value,) + others)[0]
+
+
+class Line:
+    def __init__(self, axis):
+        self.axis, self.ended = axis, []
+
+    def swap(self, block, offset):
+        self.ended = [swap(after(block, *self.ended), self.axis, offset)]
+        return self.ended[0]
 
 
 def body(
@@ -480,7 +497,8 @@
     order += far[-2:] + [k + 1 for k in far[-2:]]
 
     (old,) = due_columns(place, part, params)
-    old_sums = [old[0]] + [swap(old[k], "rep", k) for k in range(1, replicas)]
+    line = Line("rep")
+    old_sums = [old[0]] + [line.swap(old[k], k) for k in range(1, replicas)]
 
     packed = {}
     for offsets in (order[:1], order[1:4], order[4:], (0, 1)):
@@ -493,10 +511,6 @@
     values = {0: incoming[:, kv_width:]}
     for i, k in enumerate(far[1:] if relay else far):
         values[k] = swap(after(values[0], blocks[order[i]]), "fsdp", k)
-    if relay:
-        upper = swap(values[far[1]][:half], "fsdp", far[2])
-        lower = swap(values[far[2]][half:], "fsdp", far[1])
-        values[far[0]] = jnp.concatenate([upper, lower], axis=0)
 
     steps_now = step_count[0].astype(jnp.float32)
     plan = jnp.minimum(1.0, steps_now / WARMUP) * (
@@ -510,7 +524,7 @@
     anchor_cols, moment_cols = (c[0] for c in due_columns(place, part, anchor, momentum))
     pseudo_old = anchor_cols - sum(old_sums[1:], old_sums[0]) / replicas
     base = anchor_cols - OUTER_RATE * (OUTER_MU * (OUTER_MU * moment_cols + pseudo_old) + pseudo_old)
-    base = [base] + [swap(base, "rep", k) for k in range(1, replicas)]
+    base = [base] + [line.swap(base, k) for k in range(1, replicas)]
     anchor_copy, momentum_copy = duplicate(anchor, momentum)
     key_weights = cast_left(params, kv_width)
 
@@ -530,8 +544,14 @@
             continue
         part_k, flipped[k] = partial_keys(blocks[k], key_weights, adds)
         if k == last:
+            for j in [0] + [j for j in far if j in values]:
+                values[j] = after(values[j], part_k)
+            if relay:
+                upper = swap(values[far[1]][:half], "fsdp", far[2])
+                lower = swap(values[far[2]][half:], "fsdp", far[1])
+                values[far[0]] = jnp.concatenate([upper, lower], axis=0)
             for j in range(0, shards, 2):
-                values[j + 1] = swap(after(values[j], part_k), "fsdp", 1)
+                values[j + 1] = swap(values[j], "fsdp", 1)
         parts.append(swap(part_k, "fsdp", k) if k else part_k)
     spread = [0, 1] + [k + odd for k in far for odd in range(2)]
     near, rest = spread[:shards // 2], spread[shards // 2:]

time: 162 us -> 186 us (1.15)
  waiting for transfers between devices: 57.6 us -> 80.5 us
  starting transfers between devices: 43.6 us -> 45.5 us
    ppermute x46, waiting for transfers between devices: 57.6 us -> 80.5 us  [swap(): return lax.ppermute(block, axis, [(i, i ^ offset) for i in range(count)])]
  transfers between devices with their start and end apart: 46 -> 46, of which waited for: 17 -> 17; matrix products, arithmetic and copies ran while one was open for 0% -> 0% of each run, Pallas kernels for 29% -> 25%
where the time goes in v17:
time: 186 us; the launch traced here: 185 us
  waiting for transfers between devices  80.5 us (43%)
  Pallas kernels  54.8 us (29%)
  starting transfers between devices  45.5 us (24%)
  between operations  3.85 us (2%)
    ppermute x46, waiting for transfers between devices, swap(): return lax.ppermute(block, axis, [(i, i ^ offset) for i in range(count)])  80.5 us
    ppermute x46, starting transfers between devices, swap(): return lax.ppermute(block, axis, [(i, i ^ offset) for i in range(count)])  45.5 us
    pallas_call x4, Pallas kernels, gradient(): pl.pallas_call(functools.partial(grad_kernel, len(flipped), base is not N...  13.5 us
    pallas_call x2, Pallas kernels, adam_rows(): pl.pallas_call(functools.partial(adam_kernel, len(squares), len(into)), o...  12 us
    pallas_call x4, Pallas kernels, pack(): pl.pallas_call(functools.partial(pack_kernel, offsets), out_shape=[pltpu....  9.16 us
    pallas_call x3, Pallas kernels, due_columns(): pl.pallas_call(functools.partial(pick_kernel, blocks), out_shape=[jax.Sha...  5.55 us
    pallas_call x8, Pallas kernels, partial_keys(): pl.pallas_call(functools.partial(partial_kernel, pieces, [first for _, fi...  4.64 us
  transfers between devices with their start and end apart: 46, of which 17 were waited for; matrix products, arithmetic and copies ran while one was open for 0% of the time, Pallas kernels for 25%

profile of v17, /device:TPU:0, one launch (start us, length us, event | category | flops | bytes accessed | tf_op | source)
XLA Modules:
  0.0 185.1 jit_solution(5181545608959390058)
XLA Ops:
  1.4 1.8 due_columns.5.w_ref
  3.2 3.1 %collective-permute-start.10 = (f32[384,128]{1,0:T(8,128)S(1)}, f32[384,128]{1,0:T(8,128)S(1)}, u32[]{:S(2)}, u32[]{:S(2)}) collective-permute-start(f32[384,128]{1,0:T(8,128)S(1)} %get-tuple-element.144), channel_id=1, source_target_pairs={{0,8},{8,0},{16,24},{24,16},{1,9},{9,1},{17,25},{25,17},{2,10},{10... | collective-permute-start | bytes 589832 | tf_op jit(solution)/shard_map/ppermute | solution.py:458
  6.3 4.9 %collective-permute-done.10 = f32[384,128]{1,0:T(8,128)S(1)} collective-permute-done((f32[384,128]{1,0:T(8,128)S(1)}, f32[384,128]{1,0:T(8,128)S(1)}, u32[]{:S(2)}, u32[]{:S(2)}) %collective-permute-start.10) | collective-permute-done | bytes 196640 | tf_op jit(solution)/shard_map/ppermute | solution.py:458
  11.2 2.8 %collective-permute-start.11 = (f32[384,128]{1,0:T(8,128)S(1)}, f32[384,128]{1,0:T(8,128)S(1)}, u32[]{:S(2)}, u32[]{:S(2)}) collective-permute-start(f32[384,128]{1,0:T(8,128)S(1)} %get-tuple-element.92), channel_id=1, source_target_pairs={{0,16},{8,24},{16,0},{24,8},{1,17},{9,25},{17,1},{25,9},{2,18},{10... | collective-permute-start | bytes 589832 | tf_op jit(solution)/shard_map/ppermute | solution.py:458
  14.0 8.4 %collective-permute-done.11 = f32[384,128]{1,0:T(8,128)S(1)} collective-permute-done((f32[384,128]{1,0:T(8,128)S(1)}, f32[384,128]{1,0:T(8,128)S(1)}, u32[]{:S(2)}, u32[]{:S(2)}) %collective-permute-start.11) | collective-permute-done | bytes 196640 | tf_op jit(solution)/shard_map/ppermute | solution.py:458
  22.4 3.3 %collective-permute-start.12 = (f32[384,128]{1,0:T(8,128)S(1)}, f32[384,128]{1,0:T(8,128)S(1)}, u32[]{:S(2)}, u32[]{:S(2)}) collective-permute-start(f32[384,128]{1,0:T(8,128)S(1)} %get-tuple-element.93), channel_id=1, source_target_pairs={{0,24},{8,16},{16,8},{24,0},{1,25},{9,17},{17,9},{25,1},{2,26},{10... | collective-permute-start | bytes 589832 | tf_op jit(solution)/shard_map/ppermute | solution.py:458
  25.8 2.0 %pack.6 = bf16[256,1536]{1,0:T(8,128)(2,1)} custom-call(s32[1]{0:T(128)} %bitcast.4.me_ref, bf16[256,12288]{1,0:T(8,128)(2,1)} %bitcast.64), custom_call_target="tpu_custom_call" | custom-call | bytes 1572864 | tf_op jit(solution)/shard_map/pack/pallas_call | solution.py:69
  27.7 2.5 %collective-permute-start.3 = (bf16[256,1536]{1,0:T(8,128)(2,1)}, bf16[256,1536]{1,0:T(8,128)(2,1)S(1)}, u32[]{:S(2)}, u32[]{:S(2)}) collective-permute-start(bf16[256,1536]{1,0:T(8,128)(2,1)} %pack.6), channel_id=1, source_target_pairs={{0,6},{1,7},{2,4},{3,5},{4,2},{5,3},{6,0},{7,1},{8,14},{9,15},{10,... | collective-permute-start | bytes 2359304 | tf_op jit(solution)/shard_map/ppermute | solution.py:458
  30.2 2.3 %pack.5 = (bf16[256,1536]{1,0:T(8,128)(2,1)}, bf16[256,1536]{1,0:T(8,128)(2,1)}) custom-call(s32[1]{0:T(128)} %bitcast.4.me_ref, bf16[256,12288]{1,0:T(8,128)(2,1)} %bitcast.65), custom_call_target="tpu_custom_call" | custom-call | bytes 3145728 | tf_op jit(solution)/shard_map/pack/pallas_call | solution.py:69
  32.6 1.6 due_columns.4
  34.4 2.6 %pack.4 = (bf16[256,1536]{1,0:T(8,128)(2,1)}, bf16[256,1536]{1,0:T(8,128)(2,1)}, bf16[256,1536]{1,0:T(8,128)(2,1)}) custom-call(s32[1]{0:T(128)} %bitcast.4.me_ref, bf16[256,12288]{1,0:T(8,128)(2,1)} %bitcast.66), custom_call_target="tpu_custom_call" | custom-call | bytes 4718592 | tf_op jit(solution)/shard_map/pack/pallas_call | solution.py:69
  37.0 1.7 collective-permute-start.4
  38.8 0.7 collective-permute-start.8
  39.5 2.3 %collective-permute-done.13.refs_4_ = f32[384,128]{1,0:T(8,128)S(1)} collective-permute-done((f32[384,128]{1,0:T(8,128)S(1)}, f32[384,128]{1,0:T(8,128)S(1)}, u32[]{:S(2)}, u32[]{:S(2)}) %collective-permute-start.13) | collective-permute-done | bytes 196640 | tf_op jit(solution)/shard_map/ppermute | solution.py:458
  42.3 2.3 %pack.7 = (bf16[256,1536]{1,0:T(8,128)(2,1)}, bf16[256,1536]{1,0:T(8,128)(2,1)}) custom-call(s32[1]{0:T(128)} %bitcast.4.me_ref, bf16[256,12288]{1,0:T(8,128)(2,1)} %bitcast.67), custom_call_target="tpu_custom_call" | custom-call | bytes 3145728 | tf_op jit(solution)/shard_map/pack/pallas_call | solution.py:69
  44.6 4.8 %collective-permute-done.3.refs_0_.refs_1_.refs_2_.refs_3_ = bf16[256,1536]{1,0:T(8,128)(2,1)S(1)} collective-permute-done((bf16[256,1536]{1,0:T(8,128)(2,1)}, bf16[256,1536]{1,0:T(8,128)(2,1)S(1)}, u32[]{:S(2)}, u32[]{:S(2)}) %collective-permute-start.3) | collective-permute-done | bytes 786464 | tf_op jit(solution)/shard_map/ppermute | solution.py:458
  49.4 16.0 %collective-permute-done.1.refs_0_.refs_1_.refs_2_.refs_3_ = bf16[256,1536]{1,0:T(8,128)(2,1)S(1)} collective-permute-done((bf16[256,1536]{1,0:T(8,128)(2,1)}, bf16[256,1536]{1,0:T(8,128)(2,1)S(1)}, u32[]{:S(2)}, u32[]{:S(2)}) %collective-permute-start.1) | collective-permute-done | bytes 786464 | tf_op jit(solution)/shard_map/ppermute | solution.py:458
  66.0 3.5 %cast_left.1.refs_4_ = bf16[1536,512]{1,0:T(8,128)(2,1)S(1)} custom-call(f32[1536,1024]{1,0:T(8,128)} %bitcast.39), custom_call_target="tpu_custom_call" | custom-call | bytes 4718592 | tf_op jit(solution)/shard_map/cast_left/pallas_call | solution.py:93
  69.4 12.9 %collective-permute-done.4.refs_0_.refs_1_.refs_2_.refs_3_ = bf16[256,1536]{1,0:T(8,128)(2,1)S(1)} collective-permute-done((bf16[256,1536]{1,0:T(8,128)(2,1)}, bf16[256,1536]{1,0:T(8,128)(2,1)S(1)}, u32[]{:S(2)}, u32[]{:S(2)}) %collective-permute-start.4) | collective-permute-done | bytes 786464 | tf_op jit(solution)/shard_map/ppermute | solution.py:458
  82.3 0.6 partial_keys.9
  82.9 0.7 collective-permute-start.5
  83.6 2.8 %duplicate.1 = (f32[384,1024]{1,0:T(8,128)}, f32[384,1024]{1,0:T(8,128)}) custom-call(f32[384,1024]{1,0:T(8,128)} %refs_0_.3, f32[384,1024]{1,0:T(8,128)} %refs_1_.3), custom_call_target="tpu_custom_call" | custom-call | bytes 6291456 | tf_op jit(solution)/shard_map/duplicate/pallas_call | solution.py:389
  87.3 2.1 %due_columns.3 = (f32[4,384,128]{2,1,0:T(8,128)S(1)}, f32[4,384,128]{2,1,0:T(8,128)S(1)}) custom-call(s32[2]{0:T(128)S(1)} %pad_add_fusion.place_ref, f32[1536,1024]{1,0:T(8,128)} %bitcast.44, f32[1536,1024]{1,0:T(8,128)} %bitcast.45, f32[1536,1024]{1,0:T(8,128)} %bitcast.46, f32[1536,1024]{1,0:T(8,128)} %bitcast.47, f32[1536,1024]{1,0:T(8,128)} %bitcast.52, ...), custom_call_target="tpu_custom_call" | custom-call | bytes 3145728 | tf_op jit(solution)/shard_map/due_columns/pallas_call | solution.py:348
  89.6 0.6 partial_keys.12
  90.1 8.5 %collective-permute-done.7.refs_0_.refs_1_.refs_2_.refs_3_ = bf16[256,1536]{1,0:T(8,128)(2,1)S(1)} collective-permute-done((bf16[256,1536]{1,0:T(8,128)(2,1)}, bf16[256,1536]{1,0:T(8,128)(2,1)S(1)}, u32[]{:S(2)}, u32[]{:S(2)}) %collective-permute-start.7) | collective-permute-done | bytes 786464 | tf_op jit(solution)/shard_map/ppermute | solution.py:458
  98.6 1.5 collective-permute-start.22
  100.5 0.6 partial_keys.10
  101.1 5.8 %collective-permute-done.22.refs_4_ = bf16[256,512]{1,0:T(8,128)(2,1)S(1)} collective-permute-done((bf16[256,512]{1,0:T(8,128)(2,1)S(1)}, bf16[256,512]{1,0:T(8,128)(2,1)S(1)}, u32[]{:S(2)}, u32[]{:S(2)}) %collective-permute-start.22) | collective-permute-done | bytes 262176 | tf_op jit(solution)/shard_map/ppermute | solution.py:458
  106.9 1.6 collective-permute-start.24
  108.5 1.5 collective-permute-start.16
  110.0 0.6 partial_keys.8
  110.6 2.8 %collective-permute-done.16.refs_6_ = bf16[128,512]{1,0:T(8,128)(2,1)S(1)} collective-permute-done((bf16[128,512]{1,0:T(8,128)(2,1)S(1)}, bf16[128,512]{1,0:T(8,128)(2,1)S(1)}, u32[]{:S(2)}, u32[]{:S(2)}) %collective-permute-start.16) | collective-permute-done | bytes 131104 | tf_op jit(solution)/shard_map/ppermute | solution.py:458
  114.5 1.6 collective-permute-start.27
  116.1 0.6 partial_keys.14
  116.9 1.6 collective-permute-start.28
  118.5 0.6 partial_keys.11
  119.1 1.6 collective-permute-start.17
  120.7 1.7 collective-permute-start.18
  122.4 0.9 collective-permute-done.28
  123.8 4.6 %collective-permute-done.17.refs_0_ = bf16[256,512]{1,0:T(8,128)(2,1)S(1)} collective-permute-done((bf16[256,512]{1,0:T(8,128)(2,1)S(1)}, bf16[256,512]{1,0:T(8,128)(2,1)S(1)}, u32[]{:S(2)}, u32[]{:S(2)}) %collective-permute-start.17) | collective-permute-done | bytes 262176 | tf_op jit(solution)/shard_map/ppermute | solution.py:458
  128.4 0.6 partial_keys.15
  129.6 1.6 collective-permute-start.34
  131.4 1.5 collective-permute-start.31
  132.8 3.2 %gradient.4.refs_8_ = f32[1536,512]{1,0:T(8,128)S(1)} custom-call(s32[2]{0:T(128)S(1)} %pad_add_fusion.place_ref, bf16[1536,256]{1,0:T(8,128)(2,1)S(1)} %get-tuple-element.111.refs_0_, bf16[1536,256]{1,0:T(8,128)(2,1)S(1)} %get-tuple-element.112.refs_1_, bf16[1536,256]{1,0:T(8,128)(2,1)S(1)} %get-tuple-element.113.refs_2_, ...), custom_call_target="tpu_custom_call" | custom-call | flops 1610612736 | bytes 6291456 | tf_op jit(solution)/shard_map/gradient/pallas_call | solution.py:236
  136.0 0.6 collective-permute-start.21
  136.6 3.6 %gradient.5 = (f32[1536,512]{1,0:T(8,128)S(1)}, f32[8,128]{1,0:T(8,128)S(1)}, f32[1536,128]{1,0:T(8,128)S(1)}) custom-call(s32[2]{0:T(128)S(1)} %pad_add_fusion.place_ref, bf16[1536,256]{1,0:T(8,128)(2,1)S(1)} %get-tuple-element.80.refs_0_, bf16[1536,256]{1,0:T(8,128)(2,1)S(1)} %get-tuple-element.81.refs_1_, ...), custom_call_target="tpu_custom_call" | custom-call | flops 1610612736 | bytes 6291456 | tf_op jit(solution)/shard_map/gradient/pallas_call | solution.py:236
  140.3 4.6 %collective-permute-done.31.refs_6_ = bf16[256,512]{1,0:T(8,128)(2,1)S(1)} collective-permute-done((bf16[256,512]{1,0:T(8,128)(2,1)S(1)}, bf16[256,512]{1,0:T(8,128)(2,1)S(1)}, u32[]{:S(2)}, u32[]{:S(2)}) %collective-permute-start.31) | collective-permute-done | bytes 262176 | tf_op jit(solution)/shard_map/ppermute | solution.py:458
  145.4 3.2 %gradient.6.refs_8_ = f32[1536,512]{1,0:T(8,128)S(1)} custom-call(s32[2]{0:T(128)S(1)} %pad_add_fusion.place_ref, bf16[1536,256]{1,0:T(8,128)(2,1)S(1)} %get-tuple-element.111.refs_0_, bf16[1536,256]{1,0:T(8,128)(2,1)S(1)} %get-tuple-element.112.refs_1_, bf16[1536,256]{1,0:T(8,128)(2,1)S(1)} %get-tuple-element.113.refs_2_, ...), custom_call_target="tpu_custom_call" | custom-call | flops 1610612736 | bytes 6291456 | tf_op jit(solution)/shard_map/gradient/pallas_call | solution.py:236
  148.6 3.6 %gradient.7 = (f32[1536,512]{1,0:T(8,128)S(1)}, f32[8,128]{1,0:T(8,128)S(1)}, f32[1536,128]{1,0:T(8,128)S(1)}) custom-call(s32[2]{0:T(128)S(1)} %pad_add_fusion.place_ref, bf16[1536,256]{1,0:T(8,128)(2,1)S(1)} %get-tuple-element.80.refs_0_, bf16[1536,256]{1,0:T(8,128)(2,1)S(1)} %get-tuple-element.81.refs_1_, ...), custom_call_target="tpu_custom_call" | custom-call | flops 1610612736 | bytes 6291456 | tf_op jit(solution)/shard_map/gradient/pallas_call | solution.py:236
  152.4 1.1 collective-permute-done.36
  153.5 1.6 collective-permute-start.39
  155.0 1.1 collective-permute-start.38
  156.1 0.9 collective-permute-start.37
  157.0 1.0 collective-permute-done.39.refs_3_
  158.0 0.7 collective-permute-done.38.refs_2_
  158.6 1.1 collective-permute-done.37.refs_1_
  159.7 1.5 adam_frag.1
  161.3 0.7 collective-permute-start.41
  162.1 3.6 %collective-permute-start.42 = (bf16[384,128]{1,0:T(8,128)(2,1)S(1)}, bf16[384,128]{1,0:T(8,128)(2,1)S(1)}, u32[]{:S(2)}, u32[]{:S(2)}) collective-permute-start(bf16[384,128]{1,0:T(8,128)(2,1)S(1)} %get-tuple-element.132), channel_id=1, source_target_pairs={{0,24},{8,16},{16,8},{24,0},{1,25},{9,17},{17,9},{25,1},{2,26},{10... | collective-permute-start | bytes 294920 | tf_op jit(solution)/shard_map/ppermute | solution.py:458
  165.8 6.0 %adam_rows.2 = (f32[1536,1024]{1,0:T(8,128)}, f32[1536,1024]{1,0:T(8,128)}, f32[1536,1024]{1,0:T(8,128)}, f32[8,128]{1,0:T(8,128)S(1)}) custom-call(f32[3]{0:T(128)S(1)} %pad_maximum_fusion.sc_ref, f32[1536,1024]{1,0:T(8,128)S(1)} %bitcast.42, f32[1536,1024]{1,0:T(8,128)S(1)} %bitcast.50, f32[1536,1024]{1,0:T(8,128)S(1)} %bitcast.58, ...), custom_call_target="tpu_custom_call" | custom-call | flops 15728640 | bytes 22020096 | tf_op jit(solution)/shard_map/adam_rows/pallas_call | solution.py:291
  172.4 1.6 collective-permute-start.44
  174.0 2.4 %collective-permute-start.43 = (bf16[384,128]{1,0:T(8,128)(2,1)S(1)}, bf16[384,128]{1,0:T(8,128)(2,1)S(1)}, u32[]{:S(2)}, u32[]{:S(2)}) collective-permute-start(bf16[384,128]{1,0:T(8,128)(2,1)S(1)} %convert_element_type.24.refs_7_), channel_id=1, source_target_pairs={{0,8},{8,0},{16,24},{24,16},{1,9},{9,1},{17,25},{25,17},{2,10},{10... | collective-permute-start | bytes 294920 | tf_op jit(solution)/shard_map/ppermute | solution.py:458
  176.3 6.0 %adam_rows.3 = (f32[1536,1024]{1,0:T(8,128)}, f32[1536,1024]{1,0:T(8,128)}, f32[1536,1024]{1,0:T(8,128)}) custom-call(f32[3]{0:T(128)S(1)} %pad_maximum_fusion.sc_ref, f32[1536,1024]{1,0:T(8,128)S(1)} %bitcast.43, f32[1536,1024]{1,0:T(8,128)S(1)} %bitcast.51, ...), custom_call_target="tpu_custom_call", output_to_operand_aliasing={{0}: (10, {}), {1}: (11, {}), {2}: (12, {})} | custom-call | flops 15728640 | bytes 22020096 | tf_op jit(solution)/shard_map/adam_rows/pallas_call | solution.py:291
  182.3 1.6 outer_step.1
  (89 shorter events, 5.9 us)
Async XLA Ops:
  3.2 8.0 %collective-permute-start.10 = (f32[384,128]{1,0:T(8,128)S(1)}, f32[384,128]{1,0:T(8,128)S(1)}, u32[]{:S(2)}, u32[]{:S(2)}) collective-permute-start(f32[384,128]{1,0:T(8,128)S(1)} %get-tuple-element.144), channel_id=1, source_target_pairs={{0,8},{8,0},{16,24},{24,16},{1,9},{9,1},{17,25},{25,17},{2,10},{10... | collective-permute-start | bytes 589832 | tf_op jit(solution)/shard_map/ppermute | solution.py:458
  11.2 11.2 %collective-permute-start.11 = (f32[384,128]{1,0:T(8,128)S(1)}, f32[384,128]{1,0:T(8,128)S(1)}, u32[]{:S(2)}, u32[]{:S(2)}) collective-permute-start(f32[384,128]{1,0:T(8,128)S(1)} %get-tuple-element.92), channel_id=1, source_target_pairs={{0,16},{8,24},{16,0},{24,8},{1,17},{9,25},{17,1},{25,9},{2,18},{10... | collective-permute-start | bytes 589832 | tf_op jit(solution)/shard_map/ppermute | solution.py:458
  22.4 11.8 %collective-permute-start.12 = (f32[384,128]{1,0:T(8,128)S(1)}, f32[384,128]{1,0:T(8,128)S(1)}, u32[]{:S(2)}, u32[]{:S(2)}) collective-permute-start(f32[384,128]{1,0:T(8,128)S(1)} %get-tuple-element.93), channel_id=1, source_target_pairs={{0,24},{8,16},{16,8},{24,0},{1,25},{9,17},{17,9},{25,1},{2,26},{10... | collective-permute-start | bytes 589832 | tf_op jit(solution)/shard_map/ppermute | solution.py:458
  27.7 21.7 %collective-permute-start.3 = (bf16[256,1536]{1,0:T(8,128)(2,1)}, bf16[256,1536]{1,0:T(8,128)(2,1)S(1)}, u32[]{:S(2)}, u32[]{:S(2)}) collective-permute-start(bf16[256,1536]{1,0:T(8,128)(2,1)} %pack.6), channel_id=1, source_target_pairs={{0,6},{1,7},{2,4},{3,5},{4,2},{5,3},{6,0},{7,1},{8,14},{9,15},{10,... | collective-permute-start | bytes 2359304 | tf_op jit(solution)/shard_map/ppermute | solution.py:458
  32.5 6.3 %copy-start.3 = (bf16[256,1536]{1,0:T(8,128)(2,1)S(1)}, bf16[256,1536]{1,0:T(8,128)(2,1)}, u32[]{:S(2)}) copy-start(bf16[256,1536]{1,0:T(8,128)(2,1)} %get-tuple-element.83) | copy-start | bytes 2359300
  32.5 32.9 %collective-permute-start.1 = (bf16[256,1536]{1,0:T(8,128)(2,1)}, bf16[256,1536]{1,0:T(8,128)(2,1)S(1)}, u32[]{:S(2)}, u32[]{:S(2)}) collective-permute-start(bf16[256,1536]{1,0:T(8,128)(2,1)} %get-tuple-element.75), channel_id=1, source_target_pairs={{0,3},{1,2},{2,1},{3,0},{4,7},{5,6},{6,5},{7,4},{8,11},{9,10},{10,... | collective-permute-start | bytes 2359304 | tf_op jit(solution)/shard_map/ppermute | solution.py:458
  34.3 7.5 %collective-permute-start.13 = (f32[384,128]{1,0:T(8,128)S(1)}, f32[384,128]{1,0:T(8,128)S(1)}, u32[]{:S(2)}, u32[]{:S(2)}) collective-permute-start(f32[384,128]{1,0:T(8,128)S(1)} %get-tuple-element.96.refs_3_), channel_id=1, source_target_pairs={{0,8},{8,0},{16,24},{24,16},{1,9},{9,1},{17,25},{25,17},{2,10},{10... | collective-permute-start | bytes 589832 | tf_op jit(solution)/shard_map/ppermute | solution.py:458
  37.0 28.4 %copy-start.2 = (bf16[256,1536]{1,0:T(8,128)(2,1)S(1)}, bf16[256,1536]{1,0:T(8,128)(2,1)}, u32[]{:S(2)}) copy-start(bf16[256,1536]{1,0:T(8,128)(2,1)} %get-tuple-element.74) | copy-start | bytes 2359300
  37.0 45.3 %collective-permute-start.4 = (bf16[256,1536]{1,0:T(8,128)(2,1)}, bf16[256,1536]{1,0:T(8,128)(2,1)S(1)}, u32[]{:S(2)}, u32[]{:S(2)}) collective-permute-start(bf16[256,1536]{1,0:T(8,128)(2,1)} %get-tuple-element.77), channel_id=1, source_target_pairs={{0,7},{1,6},{2,5},{3,4},{4,3},{5,2},{6,1},{7,0},{8,15},{9,14},{10,... | collective-permute-start | bytes 2359304 | tf_op jit(solution)/shard_map/ppermute | solution.py:458
  38.8 44.1 %collective-permute-start.8 = (bf16[256,1536]{1,0:T(8,128)(2,1)S(1)}, bf16[256,1536]{1,0:T(8,128)(2,1)S(1)}, u32[]{:S(2)}, u32[]{:S(2)}) collective-permute-start(bf16[256,1536]{1,0:T(8,128)(2,1)S(1)} %copy-done.3), channel_id=1, source_target_pairs={{0,5},{1,4},{2,7},{3,6},{4,1},{5,0},{6,3},{7,2},{8,13},{9,12},{10,... | collective-permute-start | bytes 2359304 | tf_op jit(solution)/shard_map/ppermute | solution.py:458
  41.8 56.8 %collective-permute-start.7 = (bf16[256,1536]{1,0:T(8,128)(2,1)}, bf16[256,1536]{1,0:T(8,128)(2,1)S(1)}, u32[]{:S(2)}, u32[]{:S(2)}) collective-permute-start(bf16[256,1536]{1,0:T(8,128)(2,1)} %get-tuple-element.82), channel_id=1, source_target_pairs={{0,4},{1,5},{2,6},{3,7},{4,0},{5,1},{6,2},{7,3},{8,12},{9,13},{10,... | collective-permute-start | bytes 2359304 | tf_op jit(solution)/shard_map/ppermute | solution.py:458
  49.4 65.1 %collective-permute-start.19 = (bf16[256,1536]{1,0:T(8,128)(2,1)}, bf16[256,1536]{1,0:T(8,128)(2,1)S(1)}, u32[]{:S(2)}, u32[]{:S(2)}) collective-permute-start(bf16[256,1536]{1,0:T(8,128)(2,1)} %get-tuple-element.104), channel_id=1, source_target_pairs={{0,1},{1,0},{2,3},{3,2},{4,5},{5,4},{6,7},{7,6},{8,9},{9,8},{10,11... | collective-permute-start | bytes 2359304 | tf_op jit(solution)/shard_map/ppermute | solution.py:458
  65.4 21.9 %copy-start.1 = (bf16[1,256,1024]{2,1,0:T(8,128)(2,1)S(1)}, bf16[1,256,1024]{2,1,0:T(8,128)(2,1)}, u32[]{:S(2)}) copy-start(bf16[1,256,1024]{2,1,0:T(8,128)(2,1)} %param.10) | copy-start | bytes 1572868
  65.4 51.4 %collective-permute-start = (bf16[256,1536]{1,0:T(8,128)(2,1)S(1)}, bf16[256,1536]{1,0:T(8,128)(2,1)S(1)}, u32[]{:S(2)}, u32[]{:S(2)}) collective-permute-start(bf16[256,1536]{1,0:T(8,128)(2,1)S(1)} %copy-done.2), channel_id=1, source_target_pairs={{0,2},{1,3},{2,0},{3,1},{4,6},{5,7},{6,4},{7,5},{8,10},{9,11},{10,... | collective-permute-start | bytes 2359304 | tf_op jit(solution)/shard_map/ppermute | solution.py:458
  82.3 17.8 %collective-permute-start.14 = (f32[384,128]{1,0:T(8,128)S(1)}, f32[384,128]{1,0:T(8,128)S(1)}, u32[]{:S(2)}, u32[]{:S(2)}) collective-permute-start(f32[384,128]{1,0:T(8,128)S(1)} %get-tuple-element.96.refs_3_), channel_id=1, source_target_pairs={{0,16},{8,24},{16,0},{24,8},{1,17},{9,25},{17,1},{25,9},{2,18},{10... | collective-permute-start | bytes 589832 | tf_op jit(solution)/shard_map/ppermute | solution.py:458
  82.9 17.2 %collective-permute-start.5 = (bf16[256,512]{1,0:T(8,128)(2,1)S(1)}, bf16[256,512]{1,0:T(8,128)(2,1)S(1)}, u32[]{:S(2)}, u32[]{:S(2)}) collective-permute-start(bf16[256,512]{1,0:T(8,128)(2,1)S(1)} %get-tuple-element.78), channel_id=1, source_target_pairs={{0,1},{1,0},{2,3},{3,2},{4,5},{5,4},{6,7},{7,6},{8,9},{9,8},{10,11... | collective-permute-start | bytes 786440 | tf_op jit(solution)/shard_map/ppermute | solution.py:458
  98.6 8.2 %collective-permute-start.22 = (bf16[256,512]{1,0:T(8,128)(2,1)S(1)}, bf16[256,512]{1,0:T(8,128)(2,1)S(1)}, u32[]{:S(2)}, u32[]{:S(2)}) collective-permute-start(bf16[256,512]{1,0:T(8,128)(2,1)S(1)} %slice.32.refs_4_), channel_id=1, source_target_pairs={{0,2},{1,3},{2,0},{3,1},{4,6},{5,7},{6,4},{7,5},{8,10},{9,11},{10,... | collective-permute-start | bytes 786440 | tf_op jit(solution)/shard_map/ppermute | solution.py:458
  100.1 8.3 %collective-permute-start.9 = (bf16[256,512]{1,0:T(8,128)(2,1)S(1)}, bf16[256,512]{1,0:T(8,128)(2,1)S(1)}, u32[]{:S(2)}, u32[]{:S(2)}) collective-permute-start(bf16[256,512]{1,0:T(8,128)(2,1)S(1)} %get-tuple-element.89), channel_id=1, source_target_pairs={{0,1},{1,0},{2,3},{3,2},{4,5},{5,4},{6,7},{7,6},{8,9},{9,8},{10,11... | collective-permute-start | bytes 786440 | tf_op jit(solution)/shard_map/ppermute | solution.py:458
  100.1 10.4 %collective-permute-start.15 = (f32[384,128]{1,0:T(8,128)S(1)}, f32[384,128]{1,0:T(8,128)S(1)}, u32[]{:S(2)}, u32[]{:S(2)}) collective-permute-start(f32[384,128]{1,0:T(8,128)S(1)} %get-tuple-element.96.refs_3_), channel_id=1, source_target_pairs={{0,24},{8,16},{16,8},{24,0},{1,25},{9,17},{17,9},{25,1},{2,26},{10... | collective-permute-start | bytes 589832 | tf_op jit(solution)/shard_map/ppermute | solution.py:458
  106.9 9.8 %collective-permute-start.24 = (bf16[256,512]{1,0:T(8,128)(2,1)S(1)}, bf16[256,512]{1,0:T(8,128)(2,1)S(1)}, u32[]{:S(2)}, u32[]{:S(2)}) collective-permute-start(bf16[256,512]{1,0:T(8,128)(2,1)S(1)} %slice.32.refs_4_), channel_id=1, source_target_pairs={{0,4},{1,5},{2,6},{3,7},{4,0},{5,1},{6,2},{7,3},{8,12},{9,13},{10,... | collective-permute-start | bytes 786440 | tf_op jit(solution)/shard_map/ppermute | solution.py:458
  108.5 5.0 %collective-permute-start.16 = (bf16[128,512]{1,0:T(8,128)(2,1)S(1)}, bf16[128,512]{1,0:T(8,128)(2,1)S(1)}, u32[]{:S(2)}, u32[]{:S(2)}) collective-permute-start(bf16[128,512]{1,0:T(8,128)(2,1)S(1)} %get-tuple-element.98), channel_id=1, source_target_pairs={{0,2},{1,3},{2,0},{3,1},{4,6},{5,7},{6,4},{7,5},{8,10},{9,11},{10,... | collective-permute-start | bytes 393224 | tf_op jit(solution)/shard_map/ppermute | solution.py:458
  110.6 7.9 %collective-permute-start.2 = (bf16[256,512]{1,0:T(8,128)(2,1)S(1)}, bf16[256,512]{1,0:T(8,128)(2,1)S(1)}, u32[]{:S(2)}, u32[]{:S(2)}) collective-permute-start(bf16[256,512]{1,0:T(8,128)(2,1)S(1)} %get-tuple-element.76), channel_id=1, source_target_pairs={{0,1},{1,0},{2,3},{3,2},{4,5},{5,4},{6,7},{7,6},{8,9},{9,8},{10,11... | collective-permute-start | bytes 786440 | tf_op jit(solution)/shard_map/ppermute | solution.py:458
  113.4 5.1 %collective-permute-start.6 = (bf16[128,512]{1,0:T(8,128)(2,1)S(1)}, bf16[128,512]{1,0:T(8,128)(2,1)S(1)}, u32[]{:S(2)}, u32[]{:S(2)}) collective-permute-start(bf16[128,512]{1,0:T(8,128)(2,1)S(1)} %get-tuple-element.79), channel_id=1, source_target_pairs={{0,4},{1,5},{2,6},{3,7},{4,0},{5,1},{6,2},{7,3},{8,12},{9,13},{10,... | collective-permute-start | bytes 393224 | tf_op jit(solution)/shard_map/ppermute | solution.py:458
  114.5 14.0 %copy-start = (bf16[256,1536]{1,0:T(8,128)(2,1)S(1)}, bf16[256,1536]{1,0:T(8,128)(2,1)}, u32[]{:S(2)}) copy-start(bf16[256,1536]{1,0:T(8,128)(2,1)} %get-tuple-element.103.refs_0_.refs_1_.refs_2_.refs_3_) | copy-start | bytes 2359300
  114.5 7.8 %collective-permute-start.27 = (bf16[128,512]{1,0:T(8,128)(2,1)S(1)}, bf16[128,512]{1,0:T(8,128)(2,1)S(1)}, u32[]{:S(2)}, u32[]{:S(2)}) collective-permute-start(bf16[128,512]{1,0:T(8,128)(2,1)S(1)} %slice.26), channel_id=1, source_target_pairs={{0,4},{1,5},{2,6},{3,7},{4,0},{5,1},{6,2},{7,3},{8,12},{9,13},{10,... | collective-permute-start | bytes 393224 | tf_op jit(solution)/shard_map/ppermute | solution.py:458
  116.7 6.6 %collective-permute-start.20 = (bf16[256,512]{1,0:T(8,128)(2,1)S(1)}, bf16[256,512]{1,0:T(8,128)(2,1)S(1)}, u32[]{:S(2)}, u32[]{:S(2)}) collective-permute-start(bf16[256,512]{1,0:T(8,128)(2,1)S(1)} %get-tuple-element.105), channel_id=1, source_target_pairs={{0,1},{1,0},{2,3},{3,2},{4,5},{5,4},{6,7},{7,6},{8,9},{9,8},{10,11... | collective-permute-start | bytes 786440 | tf_op jit(solution)/shard_map/ppermute | solution.py:458
  116.9 6.4 %collective-permute-start.28 = (bf16[128,512]{1,0:T(8,128)(2,1)S(1)}, bf16[128,512]{1,0:T(8,128)(2,1)S(1)}, u32[]{:S(2)}, u32[]{:S(2)}) collective-permute-start(bf16[128,512]{1,0:T(8,128)(2,1)S(1)} %slice.27), channel_id=1, source_target_pairs={{0,2},{1,3},{2,0},{3,1},{4,6},{5,7},{6,4},{7,5},{8,10},{9,11},{10,... | collective-permute-start | bytes 393224 | tf_op jit(solution)/shard_map/ppermute | solution.py:458
  119.1 9.3 %collective-permute-start.17 = (bf16[256,512]{1,0:T(8,128)(2,1)S(1)}, bf16[256,512]{1,0:T(8,128)(2,1)S(1)}, u32[]{:S(2)}, u32[]{:S(2)}) collective-permute-start(bf16[256,512]{1,0:T(8,128)(2,1)S(1)} %get-tuple-element.101), channel_id=1, source_target_pairs={{0,2},{1,3},{2,0},{3,1},{4,6},{5,7},{6,4},{7,5},{8,10},{9,11},{10,... | collective-permute-start | bytes 786440 | tf_op jit(solution)/shard_map/ppermute | solution.py:458
  120.7 8.4 %collective-permute-start.18 = (bf16[256,512]{1,0:T(8,128)(2,1)S(1)}, bf16[256,512]{1,0:T(8,128)(2,1)S(1)}, u32[]{:S(2)}, u32[]{:S(2)}) collective-permute-start(bf16[256,512]{1,0:T(8,128)(2,1)S(1)} %get-tuple-element.102), channel_id=1, source_target_pairs={{0,4},{1,5},{2,6},{3,7},{4,0},{5,1},{6,2},{7,3},{8,12},{9,13},{10,... | collective-permute-start | bytes 786440 | tf_op jit(solution)/shard_map/ppermute | solution.py:458
  122.3 8.8 %collective-permute-start.26 = (bf16[256,512]{1,0:T(8,128)(2,1)S(1)}, bf16[256,512]{1,0:T(8,128)(2,1)S(1)}, u32[]{:S(2)}, u32[]{:S(2)}) collective-permute-start(bf16[256,512]{1,0:T(8,128)(2,1)S(1)} %slice.32.refs_4_), channel_id=1, source_target_pairs={{0,1},{1,0},{2,3},{3,2},{4,5},{5,4},{6,7},{7,6},{8,9},{9,8},{10,11... | collective-permute-start | bytes 786440 | tf_op jit(solution)/shard_map/ppermute | solution.py:458
  123.2 8.2 %collective-permute-start.29 = (bf16[256,512]{1,0:T(8,128)(2,1)S(1)}, bf16[256,512]{1,0:T(8,128)(2,1)S(1)}, u32[]{:S(2)}, u32[]{:S(2)}) collective-permute-start(bf16[256,512]{1,0:T(8,128)(2,1)S(1)} %constant_dynamic-update-slice_fusion.refs_6_), channel_id=1, source_target_pairs={{0,1},{1,0},{2,3},{3,2},{4,5},{5,4},{6,7},{7,6},{8,9},{9,8},{10,11... | collective-permute-start | bytes 786440 | tf_op jit(solution)/shard_map/ppermute | solution.py:458
  123.3 12.7 %collective-permute-start.23 = (bf16[256,512]{1,0:T(8,128)(2,1)S(1)}, bf16[256,512]{1,0:T(8,128)(2,1)S(1)}, u32[]{:S(2)}, u32[]{:S(2)}) collective-permute-start(bf16[256,512]{1,0:T(8,128)(2,1)S(1)} %collective-permute-done.22.refs_4_), channel_id=1, source_target_pairs={{0,1},{1,0},{2,3},{3,2},{4,5},{5,4},{6,7},{7,6},{8,9},{9,8},{10,11... | collective-permute-start | bytes 786440 | tf_op jit(solution)/shard_map/ppermute | solution.py:458
  128.4 8.2 %collective-permute-start.25 = (bf16[256,512]{1,0:T(8,128)(2,1)S(1)}, bf16[256,512]{1,0:T(8,128)(2,1)S(1)}, u32[]{:S(2)}, u32[]{:S(2)}) collective-permute-start(bf16[256,512]{1,0:T(8,128)(2,1)S(1)} %collective-permute-done.24.refs_6_), channel_id=1, source_target_pairs={{0,1},{1,0},{2,3},{3,2},{4,5},{5,4},{6,7},{7,6},{8,9},{9,8},{10,11... | collective-permute-start | bytes 786440 | tf_op jit(solution)/shard_map/ppermute | solution.py:458
  128.4 37.3 %slice-start.4 = ((s8[6291456]{0:T(1024)(128)(4,1)}), s8[4194304]{0:T(1024)(128)(4,1)S(1)}, s32[]{:S(2)}) async-start(s8[6291456]{0:T(1024)(128)(4,1)} %bitcast.56), calls=%async_computation.4 | async-start | bytes 8388608
  129.6 10.6 %collective-permute-start.34 = (bf16[256,512]{1,0:T(8,128)(2,1)S(1)}, bf16[256,512]{1,0:T(8,128)(2,1)S(1)}, u32[]{:S(2)}, u32[]{:S(2)}) collective-permute-start(bf16[256,512]{1,0:T(8,128)(2,1)S(1)} %key_backward.1.refs_4_), channel_id=1, source_target_pairs={{0,6},{1,7},{2,4},{3,5},{4,2},{5,3},{6,0},{7,1},{8,14},{9,15},{10,... | collective-permute-start | bytes 786440 | tf_op jit(solution)/shard_map/ppermute | solution.py:458
  131.1 14.2 %collective-permute-start.33 = (bf16[256,512]{1,0:T(8,128)(2,1)S(1)}, bf16[256,512]{1,0:T(8,128)(2,1)S(1)}, u32[]{:S(2)}, u32[]{:S(2)}) collective-permute-start(bf16[256,512]{1,0:T(8,128)(2,1)S(1)} %key_backward.1.refs_4_), channel_id=1, source_target_pairs={{0,1},{1,0},{2,3},{3,2},{4,5},{5,4},{6,7},{7,6},{8,9},{9,8},{10,11... | collective-permute-start | bytes 786440 | tf_op jit(solution)/shard_map/ppermute | solution.py:458
  131.4 13.5 %collective-permute-start.31 = (bf16[256,512]{1,0:T(8,128)(2,1)S(1)}, bf16[256,512]{1,0:T(8,128)(2,1)S(1)}, u32[]{:S(2)}, u32[]{:S(2)}) collective-permute-start(bf16[256,512]{1,0:T(8,128)(2,1)S(1)} %key_backward.1.refs_4_), channel_id=1, source_target_pairs={{0,4},{1,5},{2,6},{3,7},{4,0},{5,1},{6,2},{7,3},{8,12},{9,13},{10,... | collective-permute-start | bytes 786440 | tf_op jit(solution)/shard_map/ppermute | solution.py:458
  136.0 8.8 %collective-permute-start.21 = (bf16[256,512]{1,0:T(8,128)(2,1)S(1)}, bf16[256,512]{1,0:T(8,128)(2,1)S(1)}, u32[]{:S(2)}, u32[]{:S(2)}) collective-permute-start(bf16[256,512]{1,0:T(8,128)(2,1)S(1)} %key_backward.1.refs_4_), channel_id=1, source_target_pairs={{0,2},{1,3},{2,0},{3,1},{4,6},{5,7},{6,4},{7,5},{8,10},{9,11},{10,... | collective-permute-start | bytes 786440 | tf_op jit(solution)/shard_map/ppermute | solution.py:458
  136.6 29.1 %slice-start.5 = ((s8[6291456]{0:T(1024)(128)(4,1)}), s8[2097152]{0:T(1024)(128)(4,1)S(1)}, s32[]{:S(2)}) async-start(s8[6291456]{0:T(1024)(128)(4,1)} %bitcast.56), calls=%async_computation.5 | async-start | bytes 4194304
  140.2 5.2 %collective-permute-start.35 = (bf16[256,512]{1,0:T(8,128)(2,1)S(1)}, bf16[256,512]{1,0:T(8,128)(2,1)S(1)}, u32[]{:S(2)}, u32[]{:S(2)}) collective-permute-start(bf16[256,512]{1,0:T(8,128)(2,1)S(1)} %collective-permute-done.34.refs_6_), channel_id=1, source_target_pairs={{0,1},{1,0},{2,3},{3,2},{4,5},{5,4},{6,7},{7,6},{8,9},{9,8},{10,11... | collective-permute-start | bytes 786440 | tf_op jit(solution)/shard_map/ppermute | solution.py:458
  144.9 3.7 %collective-permute-start.30 = (bf16[256,512]{1,0:T(8,128)(2,1)S(1)}, bf16[256,512]{1,0:T(8,128)(2,1)S(1)}, u32[]{:S(2)}, u32[]{:S(2)}) collective-permute-start(bf16[256,512]{1,0:T(8,128)(2,1)S(1)} %collective-permute-done.21.refs_4_), channel_id=1, source_target_pairs={{0,1},{1,0},{2,3},{3,2},{4,5},{5,4},{6,7},{7,6},{8,9},{9,8},{10,11... | collective-permute-start | bytes 786440 | tf_op jit(solution)/shard_map/ppermute | solution.py:458
  144.9 3.7 %collective-permute-start.32 = (bf16[256,512]{1,0:T(8,128)(2,1)S(1)}, bf16[256,512]{1,0:T(8,128)(2,1)S(1)}, u32[]{:S(2)}, u32[]{:S(2)}) collective-permute-start(bf16[256,512]{1,0:T(8,128)(2,1)S(1)} %collective-permute-done.31.refs_6_), channel_id=1, source_target_pairs={{0,1},{1,0},{2,3},{3,2},{4,5},{5,4},{6,7},{7,6},{8,9},{9,8},{10,11... | collective-permute-start | bytes 786440 | tf_op jit(solution)/shard_map/ppermute | solution.py:458
  145.4 20.3 %slice-start = ((s8[6291456]{0:T(1024)(128)(4,1)}), s8[4194304]{0:T(1024)(128)(4,1)S(1)}, s32[]{:S(2)}) async-start(s8[6291456]{0:T(1024)(128)(4,1)} %bitcast.40), calls=%async_computation | async-start | bytes 8388608
  145.4 20.3 %slice-start.2 = ((s8[6291456]{0:T(1024)(128)(4,1)}), s8[4194304]{0:T(1024)(128)(4,1)S(1)}, s32[]{:S(2)}) async-start(s8[6291456]{0:T(1024)(128)(4,1)} %bitcast.48), calls=%async_computation.2 | async-start | bytes 8388608
  148.6 17.1 %slice-start.1 = ((s8[6291456]{0:T(1024)(128)(4,1)}), s8[2097152]{0:T(1024)(128)(4,1)S(1)}, s32[]{:S(2)}) async-start(s8[6291456]{0:T(1024)(128)(4,1)} %bitcast.40), calls=%async_computation.1 | async-start | bytes 4194304
  148.6 17.1 %slice-start.3 = ((s8[6291456]{0:T(1024)(128)(4,1)}), s8[2097152]{0:T(1024)(128)(4,1)S(1)}, s32[]{:S(2)}) async-start(s8[6291456]{0:T(1024)(128)(4,1)} %bitcast.48), calls=%async_computation.3 | async-start | bytes 4194304
  152.2 1.2 collective-permute-start.36
  153.5 4.5 %collective-permute-start.39 = (f32[8,128]{1,0:T(8,128)S(1)}, f32[8,128]{1,0:T(8,128)S(1)}, u32[]{:S(2)}, u32[]{:S(2)}) collective-permute-start(f32[8,128]{1,0:T(8,128)S(1)} %add.32.refs_0_), channel_id=1, source_target_pairs={{0,6},{1,7},{2,4},{3,5},{4,2},{5,3},{6,0},{7,1},{8,14},{9,15},{10,... | collective-permute-start | bytes 12296 | tf_op jit(solution)/shard_map/ppermute | solution.py:458
  155.0 3.6 %collective-permute-start.38 = (f32[8,128]{1,0:T(8,128)S(1)}, f32[8,128]{1,0:T(8,128)S(1)}, u32[]{:S(2)}, u32[]{:S(2)}) collective-permute-start(f32[8,128]{1,0:T(8,128)S(1)} %add.32.refs_0_), channel_id=1, source_target_pairs={{0,4},{1,5},{2,6},{3,7},{4,0},{5,1},{6,2},{7,3},{8,12},{9,13},{10,... | collective-permute-start | bytes 12296 | tf_op jit(solution)/shard_map/ppermute | solution.py:458
  156.1 3.6 %collective-permute-start.37 = (f32[8,128]{1,0:T(8,128)S(1)}, f32[8,128]{1,0:T(8,128)S(1)}, u32[]{:S(2)}, u32[]{:S(2)}) collective-permute-start(f32[8,128]{1,0:T(8,128)S(1)} %add.32.refs_0_), channel_id=1, source_target_pairs={{0,2},{1,3},{2,0},{3,1},{4,6},{5,7},{6,4},{7,5},{8,10},{9,11},{10,... | collective-permute-start | bytes 12296 | tf_op jit(solution)/shard_map/ppermute | solution.py:458
  161.3 10.5 %collective-permute-start.40 = (bf16[384,128]{1,0:T(8,128)(2,1)S(1)}, bf16[384,128]{1,0:T(8,128)(2,1)S(1)}, u32[]{:S(2)}, u32[]{:S(2)}) collective-permute-start(bf16[384,128]{1,0:T(8,128)(2,1)S(1)} %get-tuple-element.130), channel_id=1, source_target_pairs={{0,8},{8,0},{16,24},{24,16},{1,9},{9,1},{17,25},{25,17},{2,10},{10... | collective-permute-start | bytes 294920 | tf_op jit(solution)/shard_map/ppermute | solution.py:458
  161.3 10.5 %collective-permute-start.41 = (bf16[384,128]{1,0:T(8,128)(2,1)S(1)}, bf16[384,128]{1,0:T(8,128)(2,1)S(1)}, u32[]{:S(2)}, u32[]{:S(2)}) collective-permute-start(bf16[384,128]{1,0:T(8,128)(2,1)S(1)} %get-tuple-element.131), channel_id=1, source_target_pairs={{0,16},{8,24},{16,0},{24,8},{1,17},{9,25},{17,1},{25,9},{2,18},{10... | collective-permute-start | bytes 294920 | tf_op jit(solution)/shard_map/ppermute | solution.py:458
  162.1 9.7 %collective-permute-start.42 = (bf16[384,128]{1,0:T(8,128)(2,1)S(1)}, bf16[384,128]{1,0:T(8,128)(2,1)S(1)}, u32[]{:S(2)}, u32[]{:S(2)}) collective-permute-start(bf16[384,128]{1,0:T(8,128)(2,1)S(1)} %get-tuple-element.132), channel_id=1, source_target_pairs={{0,24},{8,16},{16,8},{24,0},{1,25},{9,17},{17,9},{25,1},{2,26},{10... | collective-permute-start | bytes 294920 | tf_op jit(solution)/shard_map/ppermute | solution.py:458
  171.9 10.4 %collective-permute-start.45 = (bf16[384,128]{1,0:T(8,128)(2,1)S(1)}, bf16[384,128]{1,0:T(8,128)(2,1)S(1)}, u32[]{:S(2)}, u32[]{:S(2)}) collective-permute-start(bf16[384,128]{1,0:T(8,128)(2,1)S(1)} %convert_element_type.24.refs_7_), channel_id=1, source_target_pairs={{0,24},{8,16},{16,8},{24,0},{1,25},{9,17},{17,9},{25,1},{2,26},{10... | collective-permute-start | bytes 294920 | tf_op jit(solution)/shard_map/ppermute | solution.py:458
  172.4 10.0 %collective-permute-start.44 = (bf16[384,128]{1,0:T(8,128)(2,1)S(1)}, bf16[384,128]{1,0:T(8,128)(2,1)S(1)}, u32[]{:S(2)}, u32[]{:S(2)}) collective-permute-start(bf16[384,128]{1,0:T(8,128)(2,1)S(1)} %convert_element_type.24.refs_7_), channel_id=1, source_target_pairs={{0,16},{8,24},{16,0},{24,8},{1,17},{9,25},{17,1},{25,9},{2,18},{10... | collective-permute-start | bytes 294920 | tf_op jit(solution)/shard_map/ppermute | solution.py:458
  174.0 8.4 %collective-permute-start.43 = (bf16[384,128]{1,0:T(8,128)(2,1)S(1)}, bf16[384,128]{1,0:T(8,128)(2,1)S(1)}, u32[]{:S(2)}, u32[]{:S(2)}) collective-permute-start(bf16[384,128]{1,0:T(8,128)(2,1)S(1)} %convert_element_type.24.refs_7_), channel_id=1, source_target_pairs={{0,8},{8,0},{16,24},{24,16},{1,9},{9,1},{17,25},{25,17},{2,10},{10... | collective-permute-start | bytes 294920 | tf_op jit(solution)/shard_map/ppermute | solution.py:458

commit v18 on v17

--- a/solution.py
+++ b/solution.py
@@ -462,15 +462,6 @@
     return lax.optimization_barrier((value,) + others)[0]
 
 
-class Line:
-    def __init__(self, axis):
-        self.axis, self.ended = axis, []
-
-    def swap(self, block, offset):
-        self.ended = [swap(after(block, *self.ended), self.axis, offset)]
-        return self.ended[0]
-
-
 def body(
     tokens,
     cotangent,
@@ -497,8 +488,7 @@
     order += far[-2:] + [k + 1 for k in far[-2:]]
 
     (old,) = due_columns(place, part, params)
-    line = Line("rep")
-    old_sums = [old[0]] + [line.swap(old[k], k) for k in range(1, replicas)]
+    old_sums = [old[0]] + [swap(old[k], "rep", k) for k in range(1, replicas)]
 
     packed = {}
     for offsets in (order[:1], order[1:4], order[4:], (0, 1)):
@@ -524,7 +514,7 @@
     anchor_cols, moment_cols = (c[0] for c in due_columns(place, part, anchor, momentum))
     pseudo_old = anchor_cols - sum(old_sums[1:], old_sums[0]) / replicas
     base = anchor_cols - OUTER_RATE * (OUTER_MU * (OUTER_MU * moment_cols + pseudo_old) + pseudo_old)
-    base = [base] + [line.swap(base, k) for k in range(1, replicas)]
+    base = [base] + [swap(base, "rep", k) for k in range(1, replicas)]
     anchor_copy, momentum_copy = duplicate(anchor, momentum)
     key_weights = cast_left(params, kv_width)
 

time: 186 us -> 168 us (0.903)
  waiting for transfers between devices: 80.5 us -> 64.4 us
    ppermute x46, waiting for transfers between devices: 80.5 us -> 64.4 us  [swap(): return lax.ppermute(block, axis, [(i, i ^ offset) for i in range(count)])]
  transfers between devices with their start and end apart: 46 -> 46, of which waited for: 17 -> 17; matrix products, arithmetic and copies ran while one was open for 0% -> 0% of each run, Pallas kernels for 25% -> 28%
where the time goes in v18:
time: 168 us
  waiting for transfers between devices  64.4 us (38%)
  Pallas kernels  55 us (33%)
  starting transfers between devices  43.8 us (26%)
  between operations  3.85 us (2%)
    ppermute x46, waiting for transfers between devices, swap(): return lax.ppermute(block, axis, [(i, i ^ offset) for i in range(count)])  64.4 us
    ppermute x46, starting transfers between devices, swap(): return lax.ppermute(block, axis, [(i, i ^ offset) for i in range(count)])  43.8 us
    pallas_call x4, Pallas kernels, gradient(): pl.pallas_call(functools.partial(grad_kernel, len(flipped), base is not N...  13.5 us
    pallas_call x2, Pallas kernels, adam_rows(): pl.pallas_call(functools.partial(adam_kernel, len(squares), len(into)), o...  12 us
    pallas_call x4, Pallas kernels, pack(): pl.pallas_call(functools.partial(pack_kernel, offsets), out_shape=[pltpu....  9.21 us
    pallas_call x3, Pallas kernels, due_columns(): pl.pallas_call(functools.partial(pick_kernel, blocks), out_shape=[jax.Sha...  5.55 us
    pallas_call x8, Pallas kernels, partial_keys(): pl.pallas_call(functools.partial(partial_kernel, pieces, [first for _, fi...  4.64 us
    pallas_call x1, Pallas kernels, cast_left(): pl.pallas_call(cast_kernel, out_shape=jax.ShapeDtypeStruct((rows, width),...  3.55 us
  transfers between devices with their start and end apart: 46, of which 17 were waited for; matrix products, arithmetic and copies ran while one was open for 0% of the time, Pallas kernels for 28%

profile of v18, /device:TPU:0, one launch (start us, length us, event | category | flops | bytes accessed | tf_op | source)
XLA Modules:
  0.0 167.6 jit_solution(12666628084994822970)
XLA Ops:
  1.4 1.8 %due_columns.5.w_ref = f32[4,384,128]{2,1,0:T(8,128)S(1)} custom-call(s32[2]{0:T(128)S(1)} %pad_add_fusion.place_ref, f32[1536,1024]{1,0:T(8,128)} %bitcast.35, f32[1536,1024]{1,0:T(8,128)} %bitcast.36, f32[1536,1024]{1,0:T(8,128)} %bitcast.37, f32[1536,1024]{1,0:T(8,128)} %bitcast.38), custom_call_target="tpu_custom_call" | custom-call | bytes 1572864 | tf_op jit(solution)/shard_map/due_columns/pallas_call | solution.py:348
  3.2 3.1 %collective-permute-start.10 = (f32[384,128]{1,0:T(8,128)S(1)}, f32[384,128]{1,0:T(8,128)S(1)}, u32[]{:S(2)}, u32[]{:S(2)}) collective-permute-start(f32[384,128]{1,0:T(8,128)S(1)} %get-tuple-element.134), channel_id=1, source_target_pairs={{0,8},{8,0},{16,24},{24,16},{1,9},{9,1},{17,25},{25,17},{2,10},{10... | collective-permute-start | bytes 589832 | tf_op jit(solution)/shard_map/ppermute | solution.py:458
  6.3 2.5 %collective-permute-start.12 = (f32[384,128]{1,0:T(8,128)S(1)}, f32[384,128]{1,0:T(8,128)S(1)}, u32[]{:S(2)}, u32[]{:S(2)}) collective-permute-start(f32[384,128]{1,0:T(8,128)S(1)} %get-tuple-element.135), channel_id=1, source_target_pairs={{0,24},{8,16},{16,8},{24,0},{1,25},{9,17},{17,9},{25,1},{2,26},{10... | collective-permute-start | bytes 589832 | tf_op jit(solution)/shard_map/ppermute | solution.py:458
  8.9 2.0 %pack.6 = bf16[256,1536]{1,0:T(8,128)(2,1)} custom-call(s32[1]{0:T(128)} %bitcast.4.me_ref, bf16[256,12288]{1,0:T(8,128)(2,1)} %bitcast.64), custom_call_target="tpu_custom_call" | custom-call | bytes 1572864 | tf_op jit(solution)/shard_map/pack/pallas_call | solution.py:69
  10.9 2.5 %collective-permute-start.3 = (bf16[256,1536]{1,0:T(8,128)(2,1)}, bf16[256,1536]{1,0:T(8,128)(2,1)S(1)}, u32[]{:S(2)}, u32[]{:S(2)}) collective-permute-start(bf16[256,1536]{1,0:T(8,128)(2,1)} %pack.6), channel_id=1, source_target_pairs={{0,6},{1,7},{2,4},{3,5},{4,2},{5,3},{6,0},{7,1},{8,14},{9,15},{10,... | collective-permute-start | bytes 2359304 | tf_op jit(solution)/shard_map/ppermute | solution.py:458
  13.4 2.3 %pack.5 = (bf16[256,1536]{1,0:T(8,128)(2,1)}, bf16[256,1536]{1,0:T(8,128)(2,1)}) custom-call(s32[1]{0:T(128)} %bitcast.4.me_ref, bf16[256,12288]{1,0:T(8,128)(2,1)} %bitcast.65), custom_call_target="tpu_custom_call" | custom-call | bytes 3145728 | tf_op jit(solution)/shard_map/pack/pallas_call | solution.py:69
  15.8 2.7 %pack.4 = (bf16[256,1536]{1,0:T(8,128)(2,1)}, bf16[256,1536]{1,0:T(8,128)(2,1)}, bf16[256,1536]{1,0:T(8,128)(2,1)}) custom-call(s32[1]{0:T(128)} %bitcast.4.me_ref, bf16[256,12288]{1,0:T(8,128)(2,1)} %bitcast.66), custom_call_target="tpu_custom_call" | custom-call | bytes 4718592 | tf_op jit(solution)/shard_map/pack/pallas_call | solution.py:69
  18.5 1.6 due_columns.4
  20.1 1.7 %collective-permute-start.4 = (bf16[256,1536]{1,0:T(8,128)(2,1)}, bf16[256,1536]{1,0:T(8,128)(2,1)S(1)}, u32[]{:S(2)}, u32[]{:S(2)}) collective-permute-start(bf16[256,1536]{1,0:T(8,128)(2,1)} %get-tuple-element.72), channel_id=1, source_target_pairs={{0,7},{1,6},{2,5},{3,4},{4,3},{5,2},{6,1},{7,0},{8,15},{9,14},{10,... | collective-permute-start | bytes 2359304 | tf_op jit(solution)/shard_map/ppermute | solution.py:458
  21.8 4.4 %collective-permute-done.11 = f32[384,128]{1,0:T(8,128)S(1)} collective-permute-done((f32[384,128]{1,0:T(8,128)S(1)}, f32[384,128]{1,0:T(8,128)S(1)}, u32[]{:S(2)}, u32[]{:S(2)}) %collective-permute-start.11) | collective-permute-done | bytes 196640 | tf_op jit(solution)/shard_map/ppermute | solution.py:458
  26.3 3.1 %collective-permute-start.15 = (f32[384,128]{1,0:T(8,128)S(1)}, f32[384,128]{1,0:T(8,128)S(1)}, u32[]{:S(2)}, u32[]{:S(2)}) collective-permute-start(f32[384,128]{1,0:T(8,128)S(1)} %get-tuple-element.132.refs_3_), channel_id=1, source_target_pairs={{0,24},{8,16},{16,8},{24,0},{1,25},{9,17},{17,9},{25,1},{2,26},{10... | collective-permute-start | bytes 589832 | tf_op jit(solution)/shard_map/ppermute | solution.py:458
  29.4 6.6 %collective-permute-done.15.refs_6_ = f32[384,128]{1,0:T(8,128)S(1)} collective-permute-done((f32[384,128]{1,0:T(8,128)S(1)}, f32[384,128]{1,0:T(8,128)S(1)}, u32[]{:S(2)}, u32[]{:S(2)}) %collective-permute-start.15) | collective-permute-done | bytes 196640 | tf_op jit(solution)/shard_map/ppermute | solution.py:458
  36.0 8.3 %collective-permute-done.14.refs_5_ = f32[384,128]{1,0:T(8,128)S(1)} collective-permute-done((f32[384,128]{1,0:T(8,128)S(1)}, f32[384,128]{1,0:T(8,128)S(1)}, u32[]{:S(2)}, u32[]{:S(2)}) %collective-permute-start.14) | collective-permute-done | bytes 196640 | tf_op jit(solution)/shard_map/ppermute | solution.py:458
  44.3 5.7 %collective-permute-done.13.refs_4_ = f32[384,128]{1,0:T(8,128)S(1)} collective-permute-done((f32[384,128]{1,0:T(8,128)S(1)}, f32[384,128]{1,0:T(8,128)S(1)}, u32[]{:S(2)}, u32[]{:S(2)}) %collective-permute-start.13) | collective-permute-done | bytes 196640 | tf_op jit(solution)/shard_map/ppermute | solution.py:458
  50.0 1.5 collective-permute-start.7
  51.5 2.3 %pack.7 = (bf16[256,1536]{1,0:T(8,128)(2,1)}, bf16[256,1536]{1,0:T(8,128)(2,1)}) custom-call(s32[1]{0:T(128)} %bitcast.4.me_ref, bf16[256,12288]{1,0:T(8,128)(2,1)} %bitcast.67), custom_call_target="tpu_custom_call" | custom-call | bytes 3145728 | tf_op jit(solution)/shard_map/pack/pallas_call | solution.py:69
  53.9 3.5 %cast_left.1.refs_4_ = bf16[1536,512]{1,0:T(8,128)(2,1)S(1)} custom-call(f32[1536,1024]{1,0:T(8,128)} %bitcast.39), custom_call_target="tpu_custom_call" | custom-call | bytes 4718592 | tf_op jit(solution)/shard_map/cast_left/pallas_call | solution.py:93
  57.5 0.6 partial_keys.9
  58.5 6.0 %collective-permute-done.8.refs_0_.refs_1_.refs_2_.refs_3_ = bf16[256,1536]{1,0:T(8,128)(2,1)S(1)} collective-permute-done((bf16[256,1536]{1,0:T(8,128)(2,1)}, bf16[256,1536]{1,0:T(8,128)(2,1)S(1)}, u32[]{:S(2)}, u32[]{:S(2)}) %collective-permute-start.8) | collective-permute-done | bytes 786464 | tf_op jit(solution)/shard_map/ppermute | solution.py:458
  64.6 1.5 collective-permute-start
  66.0 2.8 %duplicate.1 = (f32[384,1024]{1,0:T(8,128)}, f32[384,1024]{1,0:T(8,128)}) custom-call(f32[384,1024]{1,0:T(8,128)} %refs_0_.3, f32[384,1024]{1,0:T(8,128)} %refs_1_.3), custom_call_target="tpu_custom_call" | custom-call | bytes 6291456 | tf_op jit(solution)/shard_map/duplicate/pallas_call | solution.py:389
  69.8 2.1 %due_columns.3 = (f32[4,384,128]{2,1,0:T(8,128)S(1)}, f32[4,384,128]{2,1,0:T(8,128)S(1)}) custom-call(s32[2]{0:T(128)S(1)} %pad_add_fusion.place_ref, f32[1536,1024]{1,0:T(8,128)} %bitcast.44, f32[1536,1024]{1,0:T(8,128)} %bitcast.45, f32[1536,1024]{1,0:T(8,128)} %bitcast.46, f32[1536,1024]{1,0:T(8,128)} %bitcast.47, f32[1536,1024]{1,0:T(8,128)} %bitcast.52, ...), custom_call_target="tpu_custom_call" | custom-call | bytes 3145728 | tf_op jit(solution)/shard_map/due_columns/pallas_call | solution.py:348
  72.5 0.6 partial_keys.12
  73.2 0.6 partial_keys.10
  73.8 7.5 %collective-permute-done.7.refs_0_.refs_1_.refs_2_.refs_3_ = bf16[256,1536]{1,0:T(8,128)(2,1)S(1)} collective-permute-done((bf16[256,1536]{1,0:T(8,128)(2,1)}, bf16[256,1536]{1,0:T(8,128)(2,1)S(1)}, u32[]{:S(2)}, u32[]{:S(2)}) %collective-permute-start.7) | collective-permute-done | bytes 786464 | tf_op jit(solution)/shard_map/ppermute | solution.py:458
  81.3 1.6 collective-permute-start.24
  82.9 6.7 %collective-permute-done.22.refs_4_ = bf16[256,512]{1,0:T(8,128)(2,1)S(1)} collective-permute-done((bf16[256,512]{1,0:T(8,128)(2,1)S(1)}, bf16[256,512]{1,0:T(8,128)(2,1)S(1)}, u32[]{:S(2)}, u32[]{:S(2)}) %collective-permute-start.22) | collective-permute-done | bytes 262176 | tf_op jit(solution)/shard_map/ppermute | solution.py:458
  89.6 1.5 collective-permute-start.16
  91.1 0.6 partial_keys.8
  91.8 2.8 %collective-permute-done.16.refs_6_ = bf16[128,512]{1,0:T(8,128)(2,1)S(1)} collective-permute-done((bf16[128,512]{1,0:T(8,128)(2,1)S(1)}, bf16[128,512]{1,0:T(8,128)(2,1)S(1)}, u32[]{:S(2)}, u32[]{:S(2)}) %collective-permute-start.16) | collective-permute-done | bytes 131104 | tf_op jit(solution)/shard_map/ppermute | solution.py:458
  94.6 1.6 collective-permute-start.6
  97.3 0.6 partial_keys.14
  98.0 1.7 collective-permute-start.18
  99.6 1.5 collective-permute-start.28
  101.1 0.6 partial_keys.11
  101.7 0.6 collective-permute-start.17
  102.5 3.4 %collective-permute-done.28 = bf16[128,512]{1,0:T(8,128)(2,1)S(1)} collective-permute-done((bf16[128,512]{1,0:T(8,128)(2,1)S(1)}, bf16[128,512]{1,0:T(8,128)(2,1)S(1)}, u32[]{:S(2)}, u32[]{:S(2)}) %collective-permute-start.28) | collective-permute-done | bytes 131104 | tf_op jit(solution)/shard_map/ppermute | solution.py:458
  106.6 4.3 %collective-permute-done.17.refs_0_ = bf16[256,512]{1,0:T(8,128)(2,1)S(1)} collective-permute-done((bf16[256,512]{1,0:T(8,128)(2,1)S(1)}, bf16[256,512]{1,0:T(8,128)(2,1)S(1)}, u32[]{:S(2)}, u32[]{:S(2)}) %collective-permute-start.17) | collective-permute-done | bytes 262176 | tf_op jit(solution)/shard_map/ppermute | solution.py:458
  110.9 0.6 partial_keys.15
  112.0 1.4 collective-permute-start.34
  113.7 1.6 collective-permute-start.31
  115.3 3.2 %gradient.4.refs_8_ = f32[1536,512]{1,0:T(8,128)S(1)} custom-call(s32[2]{0:T(128)S(1)} %pad_add_fusion.place_ref, bf16[1536,256]{1,0:T(8,128)(2,1)S(1)} %get-tuple-element.101.refs_0_, bf16[1536,256]{1,0:T(8,128)(2,1)S(1)} %get-tuple-element.102.refs_1_, bf16[1536,256]{1,0:T(8,128)(2,1)S(1)} %get-tuple-element.103.refs_2_, ...), custom_call_target="tpu_custom_call" | custom-call | flops 1610612736 | bytes 6291456 | tf_op jit(solution)/shard_map/gradient/pallas_call | solution.py:236
  118.4 0.6 collective-permute-start.21
  119.1 3.6 %gradient.5 = (f32[1536,512]{1,0:T(8,128)S(1)}, f32[8,128]{1,0:T(8,128)S(1)}, f32[1536,128]{1,0:T(8,128)S(1)}) custom-call(s32[2]{0:T(128)S(1)} %pad_add_fusion.place_ref, bf16[1536,256]{1,0:T(8,128)(2,1)S(1)} %get-tuple-element.75.refs_0_, bf16[1536,256]{1,0:T(8,128)(2,1)S(1)} %get-tuple-element.76.refs_1_, ...), custom_call_target="tpu_custom_call" | custom-call | flops 1610612736 | bytes 6291456 | tf_op jit(solution)/shard_map/gradient/pallas_call | solution.py:236
  122.7 4.6 %collective-permute-done.31.refs_6_ = bf16[256,512]{1,0:T(8,128)(2,1)S(1)} collective-permute-done((bf16[256,512]{1,0:T(8,128)(2,1)S(1)}, bf16[256,512]{1,0:T(8,128)(2,1)S(1)}, u32[]{:S(2)}, u32[]{:S(2)}) %collective-permute-start.31) | collective-permute-done | bytes 262176 | tf_op jit(solution)/shard_map/ppermute | solution.py:458
  127.8 3.2 %gradient.6.refs_8_ = f32[1536,512]{1,0:T(8,128)S(1)} custom-call(s32[2]{0:T(128)S(1)} %pad_add_fusion.place_ref, bf16[1536,256]{1,0:T(8,128)(2,1)S(1)} %get-tuple-element.101.refs_0_, bf16[1536,256]{1,0:T(8,128)(2,1)S(1)} %get-tuple-element.102.refs_1_, bf16[1536,256]{1,0:T(8,128)(2,1)S(1)} %get-tuple-element.103.refs_2_, ...), custom_call_target="tpu_custom_call" | custom-call | flops 1610612736 | bytes 6291456 | tf_op jit(solution)/shard_map/gradient/pallas_call | solution.py:236
  131.1 3.6 %gradient.7 = (f32[1536,512]{1,0:T(8,128)S(1)}, f32[8,128]{1,0:T(8,128)S(1)}, f32[1536,128]{1,0:T(8,128)S(1)}) custom-call(s32[2]{0:T(128)S(1)} %pad_add_fusion.place_ref, bf16[1536,256]{1,0:T(8,128)(2,1)S(1)} %get-tuple-element.75.refs_0_, bf16[1536,256]{1,0:T(8,128)(2,1)S(1)} %get-tuple-element.76.refs_1_, ...), custom_call_target="tpu_custom_call" | custom-call | flops 1610612736 | bytes 6291456 | tf_op jit(solution)/shard_map/gradient/pallas_call | solution.py:236
  134.8 1.1 collective-permute-done.36
  135.9 1.5 collective-permute-start.39
  137.4 0.9 collective-permute-start.38
  138.4 1.0 collective-permute-start.37
  139.4 1.0 collective-permute-done.39.refs_3_
  140.4 0.6 collective-permute-done.38.refs_2_
  141.0 0.9 collective-permute-done.37.refs_1_
  142.0 1.5 adam_frag.1
  143.5 1.6 collective-permute-start.40
  145.1 1.7 %collective-permute-start.41 = (bf16[384,128]{1,0:T(8,128)(2,1)S(1)}, bf16[384,128]{1,0:T(8,128)(2,1)S(1)}, u32[]{:S(2)}, u32[]{:S(2)}) collective-permute-start(bf16[384,128]{1,0:T(8,128)(2,1)S(1)} %get-tuple-element.121), channel_id=1, source_target_pairs={{0,16},{8,24},{16,0},{24,8},{1,17},{9,25},{17,1},{25,9},{2,18},{10... | collective-permute-start | bytes 294920 | tf_op jit(solution)/shard_map/ppermute | solution.py:458
  146.8 1.2 collective-permute-start.42
  148.0 6.0 %adam_rows.2 = (f32[1536,1024]{1,0:T(8,128)}, f32[1536,1024]{1,0:T(8,128)}, f32[1536,1024]{1,0:T(8,128)}, f32[8,128]{1,0:T(8,128)S(1)}) custom-call(f32[3]{0:T(128)S(1)} %pad_maximum_fusion.sc_ref, f32[1536,1024]{1,0:T(8,128)S(1)} %bitcast.42, f32[1536,1024]{1,0:T(8,128)S(1)} %bitcast.50, f32[1536,1024]{1,0:T(8,128)S(1)} %bitcast.58, ...), custom_call_target="tpu_custom_call" | custom-call | flops 15728640 | bytes 22020096 | tf_op jit(solution)/shard_map/adam_rows/pallas_call | solution.py:291
  154.3 2.5 %collective-permute-start.45 = (bf16[384,128]{1,0:T(8,128)(2,1)S(1)}, bf16[384,128]{1,0:T(8,128)(2,1)S(1)}, u32[]{:S(2)}, u32[]{:S(2)}) collective-permute-start(bf16[384,128]{1,0:T(8,128)(2,1)S(1)} %convert_element_type.24.refs_7_), channel_id=1, source_target_pairs={{0,24},{8,16},{16,8},{24,0},{1,25},{9,17},{17,9},{25,1},{2,26},{10... | collective-permute-start | bytes 294920 | tf_op jit(solution)/shard_map/ppermute | solution.py:458
  156.9 0.6 collective-permute-start.44
  157.5 1.3 collective-permute-start.43
  158.8 6.0 %adam_rows.3 = (f32[1536,1024]{1,0:T(8,128)}, f32[1536,1024]{1,0:T(8,128)}, f32[1536,1024]{1,0:T(8,128)}) custom-call(f32[3]{0:T(128)S(1)} %pad_maximum_fusion.sc_ref, f32[1536,1024]{1,0:T(8,128)S(1)} %bitcast.43, f32[1536,1024]{1,0:T(8,128)S(1)} %bitcast.51, ...), custom_call_target="tpu_custom_call", output_to_operand_aliasing={{0}: (10, {}), {1}: (11, {}), {2}: (12, {})} | custom-call | flops 15728640 | bytes 22020096 | tf_op jit(solution)/shard_map/adam_rows/pallas_call | solution.py:291
  164.8 1.7 outer_step.1
  (89 shorter events, 5.5 us)
Async XLA Ops:
  3.2 16.8 %collective-permute-start.10 = (f32[384,128]{1,0:T(8,128)S(1)}, f32[384,128]{1,0:T(8,128)S(1)}, u32[]{:S(2)}, u32[]{:S(2)}) collective-permute-start(f32[384,128]{1,0:T(8,128)S(1)} %get-tuple-element.134), channel_id=1, source_target_pairs={{0,8},{8,0},{16,24},{24,16},{1,9},{9,1},{17,25},{25,17},{2,10},{10... | collective-permute-start | bytes 589832 | tf_op jit(solution)/shard_map/ppermute | solution.py:458
  6.3 15.5 %collective-permute-start.12 = (f32[384,128]{1,0:T(8,128)S(1)}, f32[384,128]{1,0:T(8,128)S(1)}, u32[]{:S(2)}, u32[]{:S(2)}) collective-permute-start(f32[384,128]{1,0:T(8,128)S(1)} %get-tuple-element.135), channel_id=1, source_target_pairs={{0,24},{8,16},{16,8},{24,0},{1,25},{9,17},{17,9},{25,1},{2,26},{10... | collective-permute-start | bytes 589832 | tf_op jit(solution)/shard_map/ppermute | solution.py:458
  8.8 17.4 %collective-permute-start.11 = (f32[384,128]{1,0:T(8,128)S(1)}, f32[384,128]{1,0:T(8,128)S(1)}, u32[]{:S(2)}, u32[]{:S(2)}) collective-permute-start(f32[384,128]{1,0:T(8,128)S(1)} %get-tuple-element.136), channel_id=1, source_target_pairs={{0,16},{8,24},{16,0},{24,8},{1,17},{9,25},{17,1},{25,9},{2,18},{10... | collective-permute-start | bytes 589832 | tf_op jit(solution)/shard_map/ppermute | solution.py:458
  10.9 47.2 %collective-permute-start.3 = (bf16[256,1536]{1,0:T(8,128)(2,1)}, bf16[256,1536]{1,0:T(8,128)(2,1)S(1)}, u32[]{:S(2)}, u32[]{:S(2)}) collective-permute-start(bf16[256,1536]{1,0:T(8,128)(2,1)} %pack.6), channel_id=1, source_target_pairs={{0,6},{1,7},{2,4},{3,5},{4,2},{5,3},{6,0},{7,1},{8,14},{9,15},{10,... | collective-permute-start | bytes 2359304 | tf_op jit(solution)/shard_map/ppermute | solution.py:458
  15.7 20.3 %copy-start.3 = (bf16[256,1536]{1,0:T(8,128)(2,1)S(1)}, bf16[256,1536]{1,0:T(8,128)(2,1)}, u32[]{:S(2)}) copy-start(bf16[256,1536]{1,0:T(8,128)(2,1)} %get-tuple-element.70) | copy-start | bytes 2359300
  15.7 48.8 %collective-permute-start.8 = (bf16[256,1536]{1,0:T(8,128)(2,1)}, bf16[256,1536]{1,0:T(8,128)(2,1)S(1)}, u32[]{:S(2)}, u32[]{:S(2)}) collective-permute-start(bf16[256,1536]{1,0:T(8,128)(2,1)} %get-tuple-element.78), channel_id=1, source_target_pairs={{0,5},{1,4},{2,7},{3,6},{4,1},{5,0},{6,3},{7,2},{8,13},{9,12},{10,... | collective-permute-start | bytes 2359304 | tf_op jit(solution)/shard_map/ppermute | solution.py:458
  20.1 33.7 %collective-permute-start.4 = (bf16[256,1536]{1,0:T(8,128)(2,1)}, bf16[256,1536]{1,0:T(8,128)(2,1)S(1)}, u32[]{:S(2)}, u32[]{:S(2)}) collective-permute-start(bf16[256,1536]{1,0:T(8,128)(2,1)} %get-tuple-element.72), channel_id=1, source_target_pairs={{0,7},{1,6},{2,5},{3,4},{4,3},{5,2},{6,1},{7,0},{8,15},{9,14},{10,... | collective-permute-start | bytes 2359304 | tf_op jit(solution)/shard_map/ppermute | solution.py:458
  26.3 9.8 %collective-permute-start.15 = (f32[384,128]{1,0:T(8,128)S(1)}, f32[384,128]{1,0:T(8,128)S(1)}, u32[]{:S(2)}, u32[]{:S(2)}) collective-permute-start(f32[384,128]{1,0:T(8,128)S(1)} %get-tuple-element.132.refs_3_), channel_id=1, source_target_pairs={{0,24},{8,16},{16,8},{24,0},{1,25},{9,17},{17,9},{25,1},{2,26},{10... | collective-permute-start | bytes 589832 | tf_op jit(solution)/shard_map/ppermute | solution.py:458
  29.4 14.9 %collective-permute-start.14 = (f32[384,128]{1,0:T(8,128)S(1)}, f32[384,128]{1,0:T(8,128)S(1)}, u32[]{:S(2)}, u32[]{:S(2)}) collective-permute-start(f32[384,128]{1,0:T(8,128)S(1)} %get-tuple-element.132.refs_3_), channel_id=1, source_target_pairs={{0,16},{8,24},{16,0},{24,8},{1,17},{9,25},{17,1},{25,9},{2,18},{10... | collective-permute-start | bytes 589832 | tf_op jit(solution)/shard_map/ppermute | solution.py:458
  36.0 36.0 %collective-permute-start.1 = (bf16[256,1536]{1,0:T(8,128)(2,1)S(1)}, bf16[256,1536]{1,0:T(8,128)(2,1)S(1)}, u32[]{:S(2)}, u32[]{:S(2)}) collective-permute-start(bf16[256,1536]{1,0:T(8,128)(2,1)S(1)} %copy-done.3), channel_id=1, source_target_pairs={{0,3},{1,2},{2,1},{3,0},{4,7},{5,6},{6,5},{7,4},{8,11},{9,10},{10,... | collective-permute-start | bytes 2359304 | tf_op jit(solution)/shard_map/ppermute | solution.py:458
  44.3 5.7 %collective-permute-start.13 = (f32[384,128]{1,0:T(8,128)S(1)}, f32[384,128]{1,0:T(8,128)S(1)}, u32[]{:S(2)}, u32[]{:S(2)}) collective-permute-start(f32[384,128]{1,0:T(8,128)S(1)} %get-tuple-element.132.refs_3_), channel_id=1, source_target_pairs={{0,8},{8,0},{16,24},{24,16},{1,9},{9,1},{17,25},{25,17},{2,10},{10... | collective-permute-start | bytes 589832 | tf_op jit(solution)/shard_map/ppermute | solution.py:458
  50.0 31.3 %collective-permute-start.7 = (bf16[256,1536]{1,0:T(8,128)(2,1)}, bf16[256,1536]{1,0:T(8,128)(2,1)S(1)}, u32[]{:S(2)}, u32[]{:S(2)}) collective-permute-start(bf16[256,1536]{1,0:T(8,128)(2,1)} %get-tuple-element.77), channel_id=1, source_target_pairs={{0,4},{1,5},{2,6},{3,7},{4,0},{5,1},{6,2},{7,3},{8,12},{9,13},{10,... | collective-permute-start | bytes 2359304 | tf_op jit(solution)/shard_map/ppermute | solution.py:458
  53.8 10.7 %copy-start.2 = (bf16[256,1536]{1,0:T(8,128)(2,1)S(1)}, bf16[256,1536]{1,0:T(8,128)(2,1)}, u32[]{:S(2)}) copy-start(bf16[256,1536]{1,0:T(8,128)(2,1)} %get-tuple-element.69) | copy-start | bytes 2359300
  53.8 15.9 %copy-start.1 = (bf16[1,256,1024]{2,1,0:T(8,128)(2,1)S(1)}, bf16[1,256,1024]{2,1,0:T(8,128)(2,1)}, u32[]{:S(2)}) copy-start(bf16[1,256,1024]{2,1,0:T(8,128)(2,1)} %param.10) | copy-start | bytes 1572868
  53.8 42.9 %collective-permute-start.19 = (bf16[256,1536]{1,0:T(8,128)(2,1)}, bf16[256,1536]{1,0:T(8,128)(2,1)S(1)}, u32[]{:S(2)}, u32[]{:S(2)}) collective-permute-start(bf16[256,1536]{1,0:T(8,128)(2,1)} %get-tuple-element.94), channel_id=1, source_target_pairs={{0,1},{1,0},{2,3},{3,2},{4,5},{5,4},{6,7},{7,6},{8,9},{9,8},{10,11... | collective-permute-start | bytes 2359304 | tf_op jit(solution)/shard_map/ppermute | solution.py:458
  58.1 15.1 %collective-permute-start.5 = (bf16[256,512]{1,0:T(8,128)(2,1)S(1)}, bf16[256,512]{1,0:T(8,128)(2,1)S(1)}, u32[]{:S(2)}, u32[]{:S(2)}) collective-permute-start(bf16[256,512]{1,0:T(8,128)(2,1)S(1)} %get-tuple-element.73), channel_id=1, source_target_pairs={{0,1},{1,0},{2,3},{3,2},{4,5},{5,4},{6,7},{7,6},{8,9},{9,8},{10,11... | collective-permute-start | bytes 786440 | tf_op jit(solution)/shard_map/ppermute | solution.py:458
  64.6 33.4 %collective-permute-start = (bf16[256,1536]{1,0:T(8,128)(2,1)S(1)}, bf16[256,1536]{1,0:T(8,128)(2,1)S(1)}, u32[]{:S(2)}, u32[]{:S(2)}) collective-permute-start(bf16[256,1536]{1,0:T(8,128)(2,1)S(1)} %copy-done.2), channel_id=1, source_target_pairs={{0,2},{1,3},{2,0},{3,1},{4,6},{5,7},{6,4},{7,5},{8,10},{9,11},{10,... | collective-permute-start | bytes 2359304 | tf_op jit(solution)/shard_map/ppermute | solution.py:458
  72.0 17.6 %collective-permute-start.22 = (bf16[256,512]{1,0:T(8,128)(2,1)S(1)}, bf16[256,512]{1,0:T(8,128)(2,1)S(1)}, u32[]{:S(2)}, u32[]{:S(2)}) collective-permute-start(bf16[256,512]{1,0:T(8,128)(2,1)S(1)} %slice.32.refs_4_), channel_id=1, source_target_pairs={{0,2},{1,3},{2,0},{3,1},{4,6},{5,7},{6,4},{7,5},{8,10},{9,11},{10,... | collective-permute-start | bytes 786440 | tf_op jit(solution)/shard_map/ppermute | solution.py:458
  73.1 18.5 %collective-permute-start.9 = (bf16[256,512]{1,0:T(8,128)(2,1)S(1)}, bf16[256,512]{1,0:T(8,128)(2,1)S(1)}, u32[]{:S(2)}, u32[]{:S(2)}) collective-permute-start(bf16[256,512]{1,0:T(8,128)(2,1)S(1)} %get-tuple-element.84), channel_id=1, source_target_pairs={{0,1},{1,0},{2,3},{3,2},{4,5},{5,4},{6,7},{7,6},{8,9},{9,8},{10,11... | collective-permute-start | bytes 786440 | tf_op jit(solution)/shard_map/ppermute | solution.py:458
  81.3 16.6 %collective-permute-start.24 = (bf16[256,512]{1,0:T(8,128)(2,1)S(1)}, bf16[256,512]{1,0:T(8,128)(2,1)S(1)}, u32[]{:S(2)}, u32[]{:S(2)}) collective-permute-start(bf16[256,512]{1,0:T(8,128)(2,1)S(1)} %slice.32.refs_4_), channel_id=1, source_target_pairs={{0,4},{1,5},{2,6},{3,7},{4,0},{5,1},{6,2},{7,3},{8,12},{9,13},{10,... | collective-permute-start | bytes 786440 | tf_op jit(solution)/shard_map/ppermute | solution.py:458
  89.6 5.0 %collective-permute-start.16 = (bf16[128,512]{1,0:T(8,128)(2,1)S(1)}, bf16[128,512]{1,0:T(8,128)(2,1)S(1)}, u32[]{:S(2)}, u32[]{:S(2)}) collective-permute-start(bf16[128,512]{1,0:T(8,128)(2,1)S(1)} %get-tuple-element.88), channel_id=1, source_target_pairs={{0,2},{1,3},{2,0},{3,1},{4,6},{5,7},{6,4},{7,5},{8,10},{9,11},{10,... | collective-permute-start | bytes 393224 | tf_op jit(solution)/shard_map/ppermute | solution.py:458
  91.7 8.0 %collective-permute-start.2 = (bf16[256,512]{1,0:T(8,128)(2,1)S(1)}, bf16[256,512]{1,0:T(8,128)(2,1)S(1)}, u32[]{:S(2)}, u32[]{:S(2)}) collective-permute-start(bf16[256,512]{1,0:T(8,128)(2,1)S(1)} %get-tuple-element.71), channel_id=1, source_target_pairs={{0,1},{1,0},{2,3},{3,2},{4,5},{5,4},{6,7},{7,6},{8,9},{9,8},{10,11... | collective-permute-start | bytes 786440 | tf_op jit(solution)/shard_map/ppermute | solution.py:458
  94.6 6.6 %collective-permute-start.6 = (bf16[128,512]{1,0:T(8,128)(2,1)S(1)}, bf16[128,512]{1,0:T(8,128)(2,1)S(1)}, u32[]{:S(2)}, u32[]{:S(2)}) collective-permute-start(bf16[128,512]{1,0:T(8,128)(2,1)S(1)} %get-tuple-element.74), channel_id=1, source_target_pairs={{0,4},{1,5},{2,6},{3,7},{4,0},{5,1},{6,2},{7,3},{8,12},{9,13},{10,... | collective-permute-start | bytes 393224 | tf_op jit(solution)/shard_map/ppermute | solution.py:458
  96.7 14.1 %copy-start = (bf16[256,1536]{1,0:T(8,128)(2,1)S(1)}, bf16[256,1536]{1,0:T(8,128)(2,1)}, u32[]{:S(2)}) copy-start(bf16[256,1536]{1,0:T(8,128)(2,1)} %get-tuple-element.93.refs_0_.refs_1_.refs_2_.refs_3_) | copy-start | bytes 2359300
  96.8 5.8 %collective-permute-start.27 = (bf16[128,512]{1,0:T(8,128)(2,1)S(1)}, bf16[128,512]{1,0:T(8,128)(2,1)S(1)}, u32[]{:S(2)}, u32[]{:S(2)}) collective-permute-start(bf16[128,512]{1,0:T(8,128)(2,1)S(1)} %slice.26), channel_id=1, source_target_pairs={{0,4},{1,5},{2,6},{3,7},{4,0},{5,1},{6,2},{7,3},{8,12},{9,13},{10,... | collective-permute-start | bytes 393224 | tf_op jit(solution)/shard_map/ppermute | solution.py:458
  97.9 8.2 %collective-permute-start.20 = (bf16[256,512]{1,0:T(8,128)(2,1)S(1)}, bf16[256,512]{1,0:T(8,128)(2,1)S(1)}, u32[]{:S(2)}, u32[]{:S(2)}) collective-permute-start(bf16[256,512]{1,0:T(8,128)(2,1)S(1)} %get-tuple-element.95), channel_id=1, source_target_pairs={{0,1},{1,0},{2,3},{3,2},{4,5},{5,4},{6,7},{7,6},{8,9},{9,8},{10,11... | collective-permute-start | bytes 786440 | tf_op jit(solution)/shard_map/ppermute | solution.py:458
  98.0 13.5 %collective-permute-start.18 = (bf16[256,512]{1,0:T(8,128)(2,1)S(1)}, bf16[256,512]{1,0:T(8,128)(2,1)S(1)}, u32[]{:S(2)}, u32[]{:S(2)}) collective-permute-start(bf16[256,512]{1,0:T(8,128)(2,1)S(1)} %get-tuple-element.92), channel_id=1, source_target_pairs={{0,4},{1,5},{2,6},{3,7},{4,0},{5,1},{6,2},{7,3},{8,12},{9,13},{10,... | collective-permute-start | bytes 786440 | tf_op jit(solution)/shard_map/ppermute | solution.py:458
  99.6 6.3 %collective-permute-start.28 = (bf16[128,512]{1,0:T(8,128)(2,1)S(1)}, bf16[128,512]{1,0:T(8,128)(2,1)S(1)}, u32[]{:S(2)}, u32[]{:S(2)}) collective-permute-start(bf16[128,512]{1,0:T(8,128)(2,1)S(1)} %slice.27), channel_id=1, source_target_pairs={{0,2},{1,3},{2,0},{3,1},{4,6},{5,7},{6,4},{7,5},{8,10},{9,11},{10,... | collective-permute-start | bytes 393224 | tf_op jit(solution)/shard_map/ppermute | solution.py:458
  101.7 9.1 %collective-permute-start.17 = (bf16[256,512]{1,0:T(8,128)(2,1)S(1)}, bf16[256,512]{1,0:T(8,128)(2,1)S(1)}, u32[]{:S(2)}, u32[]{:S(2)}) collective-permute-start(bf16[256,512]{1,0:T(8,128)(2,1)S(1)} %get-tuple-element.91), channel_id=1, source_target_pairs={{0,2},{1,3},{2,0},{3,1},{4,6},{5,7},{6,4},{7,5},{8,10},{9,11},{10,... | collective-permute-start | bytes 786440 | tf_op jit(solution)/shard_map/ppermute | solution.py:458
  102.5 10.9 %collective-permute-start.26 = (bf16[256,512]{1,0:T(8,128)(2,1)S(1)}, bf16[256,512]{1,0:T(8,128)(2,1)S(1)}, u32[]{:S(2)}, u32[]{:S(2)}) collective-permute-start(bf16[256,512]{1,0:T(8,128)(2,1)S(1)} %slice.32.refs_4_), channel_id=1, source_target_pairs={{0,1},{1,0},{2,3},{3,2},{4,5},{5,4},{6,7},{7,6},{8,9},{9,8},{10,11... | collective-permute-start | bytes 786440 | tf_op jit(solution)/shard_map/ppermute | solution.py:458
  106.0 7.7 %collective-permute-start.29 = (bf16[256,512]{1,0:T(8,128)(2,1)S(1)}, bf16[256,512]{1,0:T(8,128)(2,1)S(1)}, u32[]{:S(2)}, u32[]{:S(2)}) collective-permute-start(bf16[256,512]{1,0:T(8,128)(2,1)S(1)} %constant_dynamic-update-slice_fusion.refs_6_), channel_id=1, source_target_pairs={{0,1},{1,0},{2,3},{3,2},{4,5},{5,4},{6,7},{7,6},{8,9},{9,8},{10,11... | collective-permute-start | bytes 786440 | tf_op jit(solution)/shard_map/ppermute | solution.py:458
  106.1 12.4 %collective-permute-start.23 = (bf16[256,512]{1,0:T(8,128)(2,1)S(1)}, bf16[256,512]{1,0:T(8,128)(2,1)S(1)}, u32[]{:S(2)}, u32[]{:S(2)}) collective-permute-start(bf16[256,512]{1,0:T(8,128)(2,1)S(1)} %collective-permute-done.22.refs_4_), channel_id=1, source_target_pairs={{0,1},{1,0},{2,3},{3,2},{4,5},{5,4},{6,7},{7,6},{8,9},{9,8},{10,11... | collective-permute-start | bytes 786440 | tf_op jit(solution)/shard_map/ppermute | solution.py:458
  110.9 8.2 %collective-permute-start.25 = (bf16[256,512]{1,0:T(8,128)(2,1)S(1)}, bf16[256,512]{1,0:T(8,128)(2,1)S(1)}, u32[]{:S(2)}, u32[]{:S(2)}) collective-permute-start(bf16[256,512]{1,0:T(8,128)(2,1)S(1)} %collective-permute-done.24.refs_6_), channel_id=1, source_target_pairs={{0,1},{1,0},{2,3},{3,2},{4,5},{5,4},{6,7},{7,6},{8,9},{9,8},{10,11... | collective-permute-start | bytes 786440 | tf_op jit(solution)/shard_map/ppermute | solution.py:458
  110.9 37.1 %slice-start.4 = ((s8[6291456]{0:T(1024)(128)(4,1)}), s8[4194304]{0:T(1024)(128)(4,1)S(1)}, s32[]{:S(2)}) async-start(s8[6291456]{0:T(1024)(128)(4,1)} %bitcast.56), calls=%async_computation.4 | async-start | bytes 8388608
  112.0 10.6 %collective-permute-start.34 = (bf16[256,512]{1,0:T(8,128)(2,1)S(1)}, bf16[256,512]{1,0:T(8,128)(2,1)S(1)}, u32[]{:S(2)}, u32[]{:S(2)}) collective-permute-start(bf16[256,512]{1,0:T(8,128)(2,1)S(1)} %key_backward.1.refs_4_), channel_id=1, source_target_pairs={{0,6},{1,7},{2,4},{3,5},{4,2},{5,3},{6,0},{7,1},{8,14},{9,15},{10,... | collective-permute-start | bytes 786440 | tf_op jit(solution)/shard_map/ppermute | solution.py:458
  113.4 14.4 %collective-permute-start.33 = (bf16[256,512]{1,0:T(8,128)(2,1)S(1)}, bf16[256,512]{1,0:T(8,128)(2,1)S(1)}, u32[]{:S(2)}, u32[]{:S(2)}) collective-permute-start(bf16[256,512]{1,0:T(8,128)(2,1)S(1)} %key_backward.1.refs_4_), channel_id=1, source_target_pairs={{0,1},{1,0},{2,3},{3,2},{4,5},{5,4},{6,7},{7,6},{8,9},{9,8},{10,11... | collective-permute-start | bytes 786440 | tf_op jit(solution)/shard_map/ppermute | solution.py:458
  113.7 13.6 %collective-permute-start.31 = (bf16[256,512]{1,0:T(8,128)(2,1)S(1)}, bf16[256,512]{1,0:T(8,128)(2,1)S(1)}, u32[]{:S(2)}, u32[]{:S(2)}) collective-permute-start(bf16[256,512]{1,0:T(8,128)(2,1)S(1)} %key_backward.1.refs_4_), channel_id=1, source_target_pairs={{0,4},{1,5},{2,6},{3,7},{4,0},{5,1},{6,2},{7,3},{8,12},{9,13},{10,... | collective-permute-start | bytes 786440 | tf_op jit(solution)/shard_map/ppermute | solution.py:458
  118.4 8.9 %collective-permute-start.21 = (bf16[256,512]{1,0:T(8,128)(2,1)S(1)}, bf16[256,512]{1,0:T(8,128)(2,1)S(1)}, u32[]{:S(2)}, u32[]{:S(2)}) collective-permute-start(bf16[256,512]{1,0:T(8,128)(2,1)S(1)} %key_backward.1.refs_4_), channel_id=1, source_target_pairs={{0,2},{1,3},{2,0},{3,1},{4,6},{5,7},{6,4},{7,5},{8,10},{9,11},{10,... | collective-permute-start | bytes 786440 | tf_op jit(solution)/shard_map/ppermute | solution.py:458
  119.0 28.9 %slice-start.5 = ((s8[6291456]{0:T(1024)(128)(4,1)}), s8[2097152]{0:T(1024)(128)(4,1)S(1)}, s32[]{:S(2)}) async-start(s8[6291456]{0:T(1024)(128)(4,1)} %bitcast.56), calls=%async_computation.5 | async-start | bytes 4194304
  122.6 5.2 %collective-permute-start.35 = (bf16[256,512]{1,0:T(8,128)(2,1)S(1)}, bf16[256,512]{1,0:T(8,128)(2,1)S(1)}, u32[]{:S(2)}, u32[]{:S(2)}) collective-permute-start(bf16[256,512]{1,0:T(8,128)(2,1)S(1)} %collective-permute-done.34.refs_6_), channel_id=1, source_target_pairs={{0,1},{1,0},{2,3},{3,2},{4,5},{5,4},{6,7},{7,6},{8,9},{9,8},{10,11... | collective-permute-start | bytes 786440 | tf_op jit(solution)/shard_map/ppermute | solution.py:458
  127.3 3.7 %collective-permute-start.30 = (bf16[256,512]{1,0:T(8,128)(2,1)S(1)}, bf16[256,512]{1,0:T(8,128)(2,1)S(1)}, u32[]{:S(2)}, u32[]{:S(2)}) collective-permute-start(bf16[256,512]{1,0:T(8,128)(2,1)S(1)} %collective-permute-done.21.refs_4_), channel_id=1, source_target_pairs={{0,1},{1,0},{2,3},{3,2},{4,5},{5,4},{6,7},{7,6},{8,9},{9,8},{10,11... | collective-permute-start | bytes 786440 | tf_op jit(solution)/shard_map/ppermute | solution.py:458
  127.4 3.7 %collective-permute-start.32 = (bf16[256,512]{1,0:T(8,128)(2,1)S(1)}, bf16[256,512]{1,0:T(8,128)(2,1)S(1)}, u32[]{:S(2)}, u32[]{:S(2)}) collective-permute-start(bf16[256,512]{1,0:T(8,128)(2,1)S(1)} %collective-permute-done.31.refs_6_), channel_id=1, source_target_pairs={{0,1},{1,0},{2,3},{3,2},{4,5},{5,4},{6,7},{7,6},{8,9},{9,8},{10,11... | collective-permute-start | bytes 786440 | tf_op jit(solution)/shard_map/ppermute | solution.py:458
  127.8 20.2 %slice-start = ((s8[6291456]{0:T(1024)(128)(4,1)}), s8[4194304]{0:T(1024)(128)(4,1)S(1)}, s32[]{:S(2)}) async-start(s8[6291456]{0:T(1024)(128)(4,1)} %bitcast.40), calls=%async_computation | async-start | bytes 8388608
  127.8 20.2 %slice-start.2 = ((s8[6291456]{0:T(1024)(128)(4,1)}), s8[4194304]{0:T(1024)(128)(4,1)S(1)}, s32[]{:S(2)}) async-start(s8[6291456]{0:T(1024)(128)(4,1)} %bitcast.48), calls=%async_computation.2 | async-start | bytes 8388608
  131.0 17.0 %slice-start.1 = ((s8[6291456]{0:T(1024)(128)(4,1)}), s8[2097152]{0:T(1024)(128)(4,1)S(1)}, s32[]{:S(2)}) async-start(s8[6291456]{0:T(1024)(128)(4,1)} %bitcast.40), calls=%async_computation.1 | async-start | bytes 4194304
  131.1 17.0 %slice-start.3 = ((s8[6291456]{0:T(1024)(128)(4,1)}), s8[2097152]{0:T(1024)(128)(4,1)S(1)}, s32[]{:S(2)}) async-start(s8[6291456]{0:T(1024)(128)(4,1)} %bitcast.48), calls=%async_computation.3 | async-start | bytes 4194304
  134.7 1.2 collective-permute-start.36
  135.9 4.5 %collective-permute-start.39 = (f32[8,128]{1,0:T(8,128)S(1)}, f32[8,128]{1,0:T(8,128)S(1)}, u32[]{:S(2)}, u32[]{:S(2)}) collective-permute-start(f32[8,128]{1,0:T(8,128)S(1)} %add.32.refs_0_), channel_id=1, source_target_pairs={{0,6},{1,7},{2,4},{3,5},{4,2},{5,3},{6,0},{7,1},{8,14},{9,15},{10,... | collective-permute-start | bytes 12296 | tf_op jit(solution)/shard_map/ppermute | solution.py:458
  137.4 3.6 %collective-permute-start.38 = (f32[8,128]{1,0:T(8,128)S(1)}, f32[8,128]{1,0:T(8,128)S(1)}, u32[]{:S(2)}, u32[]{:S(2)}) collective-permute-start(f32[8,128]{1,0:T(8,128)S(1)} %add.32.refs_0_), channel_id=1, source_target_pairs={{0,4},{1,5},{2,6},{3,7},{4,0},{5,1},{6,2},{7,3},{8,12},{9,13},{10,... | collective-permute-start | bytes 12296 | tf_op jit(solution)/shard_map/ppermute | solution.py:458
  138.4 3.6 %collective-permute-start.37 = (f32[8,128]{1,0:T(8,128)S(1)}, f32[8,128]{1,0:T(8,128)S(1)}, u32[]{:S(2)}, u32[]{:S(2)}) collective-permute-start(f32[8,128]{1,0:T(8,128)S(1)} %add.32.refs_0_), channel_id=1, source_target_pairs={{0,2},{1,3},{2,0},{3,1},{4,6},{5,7},{6,4},{7,5},{8,10},{9,11},{10,... | collective-permute-start | bytes 12296 | tf_op jit(solution)/shard_map/ppermute | solution.py:458
  143.5 10.5 %collective-permute-start.40 = (bf16[384,128]{1,0:T(8,128)(2,1)S(1)}, bf16[384,128]{1,0:T(8,128)(2,1)S(1)}, u32[]{:S(2)}, u32[]{:S(2)}) collective-permute-start(bf16[384,128]{1,0:T(8,128)(2,1)S(1)} %get-tuple-element.120), channel_id=1, source_target_pairs={{0,8},{8,0},{16,24},{24,16},{1,9},{9,1},{17,25},{25,17},{2,10},{10... | collective-permute-start | bytes 294920 | tf_op jit(solution)/shard_map/ppermute | solution.py:458
  145.1 9.1 %collective-permute-start.41 = (bf16[384,128]{1,0:T(8,128)(2,1)S(1)}, bf16[384,128]{1,0:T(8,128)(2,1)S(1)}, u32[]{:S(2)}, u32[]{:S(2)}) collective-permute-start(bf16[384,128]{1,0:T(8,128)(2,1)S(1)} %get-tuple-element.121), channel_id=1, source_target_pairs={{0,16},{8,24},{16,0},{24,8},{1,17},{9,25},{17,1},{25,9},{2,18},{10... | collective-permute-start | bytes 294920 | tf_op jit(solution)/shard_map/ppermute | solution.py:458
  146.8 7.5 %collective-permute-start.42 = (bf16[384,128]{1,0:T(8,128)(2,1)S(1)}, bf16[384,128]{1,0:T(8,128)(2,1)S(1)}, u32[]{:S(2)}, u32[]{:S(2)}) collective-permute-start(bf16[384,128]{1,0:T(8,128)(2,1)S(1)} %get-tuple-element.122), channel_id=1, source_target_pairs={{0,24},{8,16},{16,8},{24,0},{1,25},{9,17},{17,9},{25,1},{2,26},{10... | collective-permute-start | bytes 294920 | tf_op jit(solution)/shard_map/ppermute | solution.py:458
  154.3 10.4 %collective-permute-start.45 = (bf16[384,128]{1,0:T(8,128)(2,1)S(1)}, bf16[384,128]{1,0:T(8,128)(2,1)S(1)}, u32[]{:S(2)}, u32[]{:S(2)}) collective-permute-start(bf16[384,128]{1,0:T(8,128)(2,1)S(1)} %convert_element_type.24.refs_7_), channel_id=1, source_target_pairs={{0,24},{8,16},{16,8},{24,0},{1,25},{9,17},{17,9},{25,1},{2,26},{10... | collective-permute-start | bytes 294920 | tf_op jit(solution)/shard_map/ppermute | solution.py:458
  156.9 7.9 %collective-permute-start.44 = (bf16[384,128]{1,0:T(8,128)(2,1)S(1)}, bf16[384,128]{1,0:T(8,128)(2,1)S(1)}, u32[]{:S(2)}, u32[]{:S(2)}) collective-permute-start(bf16[384,128]{1,0:T(8,128)(2,1)S(1)} %convert_element_type.24.refs_7_), channel_id=1, source_target_pairs={{0,16},{8,24},{16,0},{24,8},{1,17},{9,25},{17,1},{25,9},{2,18},{10... | collective-permute-start | bytes 294920 | tf_op jit(solution)/shard_map/ppermute | solution.py:458
  157.5 7.3 %collective-permute-start.43 = (bf16[384,128]{1,0:T(8,128)(2,1)S(1)}, bf16[384,128]{1,0:T(8,128)(2,1)S(1)}, u32[]{:S(2)}, u32[]{:S(2)}) collective-permute-start(bf16[384,128]{1,0:T(8,128)(2,1)S(1)} %convert_element_type.24.refs_7_), channel_id=1, source_target_pairs={{0,8},{8,0},{16,24},{24,16},{1,9},{9,1},{17,25},{25,17},{2,10},{10... | collective-permute-start | bytes 294920 | tf_op jit(solution)/shard_map/ppermute | solution.py:458

commit v19 on v18

--- a/solution.py
+++ b/solution.py
@@ -499,8 +499,6 @@
     relay = len(far) == 3 and far[0] == far[1] ^ far[2]
     half = inputs.shape[0] // 2
     values = {0: incoming[:, kv_width:]}
-    for i, k in enumerate(far[1:] if relay else far):
-        values[k] = swap(after(values[0], blocks[order[i]]), "fsdp", k)
 
     steps_now = step_count[0].astype(jnp.float32)
     plan = jnp.minimum(1.0, steps_now / WARMUP) * (
@@ -527,12 +525,19 @@
         if k == last:
             theirs = after(theirs, *base)
         adds = [(theirs, 0)] + relayed.get(k, [])
+        if k == far[0]:
+            blocks[k] = after(blocks[k], blocks[1])
         if relay and k == far[0]:
             (upper, lower), flipped[k] = partial_keys(blocks[k], key_weights, adds, 2)
+            for j in far[1:]:
+                values[j] = swap(after(values[0], upper), "fsdp", j)
             relayed[far[2]] = [(swap(upper, "fsdp", far[1]), 0)]
             relayed[far[1]] = [(swap(lower, "fsdp", far[2]), half)]
             continue
         part_k, flipped[k] = partial_keys(blocks[k], key_weights, adds)
+        if k == far[0]:
+            for j in far:
+                values[j] = swap(after(values[0], part_k), "fsdp", j)
         if k == last:
             for j in [0] + [j for j in far if j in values]:
                 values[j] = after(values[j], part_k)

time: 168 us -> 168 us (level)
  waiting for transfers between devices: 64.4 us -> 59.9 us
  starting transfers between devices: 43.8 us -> 48.2 us
    ppermute x46, waiting for transfers between devices: 64.4 us -> 59.9 us  [swap(): return lax.ppermute(block, axis, [(i, i ^ offset) for i in range(count)])]
    ppermute x46, starting transfers between devices: 43.8 us -> 48.2 us  [swap(): return lax.ppermute(block, axis, [(i, i ^ offset) for i in range(count)])]
  transfers between devices with their start and end apart: 46 -> 46, of which waited for: 17 -> 18; matrix products, arithmetic and copies ran while one was open for 0% -> 0% of each run, Pallas kernels for 28% -> 28%
where the time goes in v19:
time: 168 us; the launch traced here: 167 us
  waiting for transfers between devices  59.9 us (36%)
  Pallas kernels  54.9 us (33%)
  starting transfers between devices  48.2 us (29%)
  between operations  3.84 us (2%)
    ppermute x46, waiting for transfers between devices, swap(): return lax.ppermute(block, axis, [(i, i ^ offset) for i in range(count)])  59.9 us
    ppermute x46, starting transfers between devices, swap(): return lax.ppermute(block, axis, [(i, i ^ offset) for i in range(count)])  48.2 us
    pallas_call x4, Pallas kernels, gradient(): pl.pallas_call(functools.partial(grad_kernel, len(flipped), base is not N...  13.5 us
    pallas_call x2, Pallas kernels, adam_rows(): pl.pallas_call(functools.partial(adam_kernel, len(squares), len(into)), o...  12 us
    pallas_call x4, Pallas kernels, pack(): pl.pallas_call(functools.partial(pack_kernel, offsets), out_shape=[pltpu....  9.19 us
    pallas_call x3, Pallas kernels, due_columns(): pl.pallas_call(functools.partial(pick_kernel, blocks), out_shape=[jax.Sha...  5.55 us
    pallas_call x8, Pallas kernels, partial_keys(): pl.pallas_call(functools.partial(partial_kernel, pieces, [first for _, fi...  4.64 us
    pallas_call x1, Pallas kernels, cast_left(): pl.pallas_call(cast_kernel, out_shape=jax.ShapeDtypeStruct((rows, width),...  3.46 us
  transfers between devices with their start and end apart: 46, of which 18 were waited for; matrix products, arithmetic and copies ran while one was open for 0% of the time, Pallas kernels for 28%

profile of v19, /device:TPU:0, one launch (start us, length us, event | category | flops | bytes accessed | tf_op | source)
XLA Modules:
  0.0 167.2 jit_solution(14509955363505414688)
XLA Ops:
  1.4 1.8 %due_columns.5.w_ref = f32[4,384,128]{2,1,0:T(8,128)S(1)} custom-call(s32[2]{0:T(128)S(1)} %pad_add_fusion.place_ref, f32[1536,1024]{1,0:T(8,128)} %bitcast.35, f32[1536,1024]{1,0:T(8,128)} %bitcast.36, f32[1536,1024]{1,0:T(8,128)} %bitcast.37, f32[1536,1024]{1,0:T(8,128)} %bitcast.38), custom_call_target="tpu_custom_call" | custom-call | bytes 1572864 | tf_op jit(solution)/shard_map/due_columns/pallas_call | solution.py:348
  3.2 3.1 %collective-permute-start.11 = (f32[384,128]{1,0:T(8,128)S(1)}, f32[384,128]{1,0:T(8,128)S(1)}, u32[]{:S(2)}, u32[]{:S(2)}) collective-permute-start(f32[384,128]{1,0:T(8,128)S(1)} %get-tuple-element.134), channel_id=1, source_target_pairs={{0,8},{8,0},{16,24},{24,16},{1,9},{9,1},{17,25},{25,17},{2,10},{10... | collective-permute-start | bytes 589832 | tf_op jit(solution)/shard_map/ppermute | solution.py:458
  6.3 2.5 %collective-permute-start.13 = (f32[384,128]{1,0:T(8,128)S(1)}, f32[384,128]{1,0:T(8,128)S(1)}, u32[]{:S(2)}, u32[]{:S(2)}) collective-permute-start(f32[384,128]{1,0:T(8,128)S(1)} %get-tuple-element.135), channel_id=1, source_target_pairs={{0,24},{8,16},{16,8},{24,0},{1,25},{9,17},{17,9},{25,1},{2,26},{10... | collective-permute-start | bytes 589832 | tf_op jit(solution)/shard_map/ppermute | solution.py:458
  8.9 2.6 %pack.4 = (bf16[256,1536]{1,0:T(8,128)(2,1)}, bf16[256,1536]{1,0:T(8,128)(2,1)}, bf16[256,1536]{1,0:T(8,128)(2,1)}) custom-call(s32[1]{0:T(128)} %bitcast.4.me_ref, bf16[256,12288]{1,0:T(8,128)(2,1)} %bitcast.64), custom_call_target="tpu_custom_call" | custom-call | bytes 4718592 | tf_op jit(solution)/shard_map/pack/pallas_call | solution.py:69
  11.5 1.4 collective-permute-start.5
  12.9 2.0 %pack.6 = bf16[256,1536]{1,0:T(8,128)(2,1)} custom-call(s32[1]{0:T(128)} %bitcast.4.me_ref, bf16[256,12288]{1,0:T(8,128)(2,1)} %bitcast.65), custom_call_target="tpu_custom_call" | custom-call | bytes 1572864 | tf_op jit(solution)/shard_map/pack/pallas_call | solution.py:69
  14.9 1.2 collective-permute-start.3
  16.1 2.3 %pack.5 = (bf16[256,1536]{1,0:T(8,128)(2,1)}, bf16[256,1536]{1,0:T(8,128)(2,1)}) custom-call(s32[1]{0:T(128)} %bitcast.4.me_ref, bf16[256,12288]{1,0:T(8,128)(2,1)} %bitcast.66), custom_call_target="tpu_custom_call" | custom-call | bytes 3145728 | tf_op jit(solution)/shard_map/pack/pallas_call | solution.py:69
  18.4 1.6 due_columns.4
  20.0 1.5 collective-permute-start.9
  21.5 4.6 %collective-permute-done.12 = f32[384,128]{1,0:T(8,128)S(1)} collective-permute-done((f32[384,128]{1,0:T(8,128)S(1)}, f32[384,128]{1,0:T(8,128)S(1)}, u32[]{:S(2)}, u32[]{:S(2)}) %collective-permute-start.12) | collective-permute-done | bytes 196640 | tf_op jit(solution)/shard_map/ppermute | solution.py:458
  26.2 3.1 %collective-permute-start.16 = (f32[384,128]{1,0:T(8,128)S(1)}, f32[384,128]{1,0:T(8,128)S(1)}, u32[]{:S(2)}, u32[]{:S(2)}) collective-permute-start(f32[384,128]{1,0:T(8,128)S(1)} %get-tuple-element.132.refs_3_), channel_id=1, source_target_pairs={{0,24},{8,16},{16,8},{24,0},{1,25},{9,17},{17,9},{25,1},{2,26},{10... | collective-permute-start | bytes 589832 | tf_op jit(solution)/shard_map/ppermute | solution.py:458
  29.4 2.3 %pack.7 = (bf16[256,1536]{1,0:T(8,128)(2,1)}, bf16[256,1536]{1,0:T(8,128)(2,1)}) custom-call(s32[1]{0:T(128)} %bitcast.4.me_ref, bf16[256,12288]{1,0:T(8,128)(2,1)} %bitcast.67), custom_call_target="tpu_custom_call" | custom-call | bytes 3145728 | tf_op jit(solution)/shard_map/pack/pallas_call | solution.py:69
  31.8 2.2 %collective-permute-done.16.refs_6_ = f32[384,128]{1,0:T(8,128)S(1)} collective-permute-done((f32[384,128]{1,0:T(8,128)S(1)}, f32[384,128]{1,0:T(8,128)S(1)}, u32[]{:S(2)}, u32[]{:S(2)}) %collective-permute-start.16) | collective-permute-done | bytes 196640 | tf_op jit(solution)/shard_map/ppermute | solution.py:458
  34.0 4.6 %collective-permute-start.15 = (f32[384,128]{1,0:T(8,128)S(1)}, f32[384,128]{1,0:T(8,128)S(1)}, u32[]{:S(2)}, u32[]{:S(2)}) collective-permute-start(f32[384,128]{1,0:T(8,128)S(1)} %get-tuple-element.132.refs_3_), channel_id=1, source_target_pairs={{0,16},{8,24},{16,0},{24,8},{1,17},{9,25},{17,1},{25,9},{2,18},{10... | collective-permute-start | bytes 589832 | tf_op jit(solution)/shard_map/ppermute | solution.py:458
  38.6 3.6 %collective-permute-done.15.refs_5_ = f32[384,128]{1,0:T(8,128)S(1)} collective-permute-done((f32[384,128]{1,0:T(8,128)S(1)}, f32[384,128]{1,0:T(8,128)S(1)}, u32[]{:S(2)}, u32[]{:S(2)}) %collective-permute-start.15) | collective-permute-done | bytes 196640 | tf_op jit(solution)/shard_map/ppermute | solution.py:458
  42.3 1.6 collective-permute-start.8
  43.9 3.5 %cast_left.1.refs_4_ = bf16[1536,512]{1,0:T(8,128)(2,1)S(1)} custom-call(f32[1536,1024]{1,0:T(8,128)} %bitcast.39), custom_call_target="tpu_custom_call" | custom-call | bytes 4718592 | tf_op jit(solution)/shard_map/cast_left/pallas_call | solution.py:93
  47.3 0.6 partial_keys.9
  47.9 1.6 collective-permute-done.3.refs_0_.refs_1_.refs_2_.refs_3_
  49.6 16.7 %collective-permute-done.9.refs_0_.refs_1_.refs_2_.refs_3_ = bf16[256,1536]{1,0:T(8,128)(2,1)S(1)} collective-permute-done((bf16[256,1536]{1,0:T(8,128)(2,1)}, bf16[256,1536]{1,0:T(8,128)(2,1)S(1)}, u32[]{:S(2)}, u32[]{:S(2)}) %collective-permute-start.9) | collective-permute-done | bytes 786464 | tf_op jit(solution)/shard_map/ppermute | solution.py:458
  66.2 0.9 collective-permute-start
  67.1 2.8 %duplicate.1 = (f32[384,1024]{1,0:T(8,128)}, f32[384,1024]{1,0:T(8,128)}) custom-call(f32[384,1024]{1,0:T(8,128)} %refs_0_.3, f32[384,1024]{1,0:T(8,128)} %refs_1_.3), custom_call_target="tpu_custom_call" | custom-call | bytes 6291456 | tf_op jit(solution)/shard_map/duplicate/pallas_call | solution.py:389
  70.8 2.1 %due_columns.3 = (f32[4,384,128]{2,1,0:T(8,128)S(1)}, f32[4,384,128]{2,1,0:T(8,128)S(1)}) custom-call(s32[2]{0:T(128)S(1)} %pad_add_fusion.place_ref, f32[1536,1024]{1,0:T(8,128)} %bitcast.44, f32[1536,1024]{1,0:T(8,128)} %bitcast.45, f32[1536,1024]{1,0:T(8,128)} %bitcast.46, f32[1536,1024]{1,0:T(8,128)} %bitcast.47, f32[1536,1024]{1,0:T(8,128)} %bitcast.52, ...), custom_call_target="tpu_custom_call" | custom-call | bytes 3145728 | tf_op jit(solution)/shard_map/due_columns/pallas_call | solution.py:348
  73.1 1.5 collective-permute-start.14
  75.3 0.6 partial_keys.10
  75.9 4.0 %collective-permute-done.14.refs_4_ = f32[384,128]{1,0:T(8,128)S(1)} collective-permute-done((f32[384,128]{1,0:T(8,128)S(1)}, f32[384,128]{1,0:T(8,128)S(1)}, u32[]{:S(2)}, u32[]{:S(2)}) %collective-permute-start.14) | collective-permute-done | bytes 196640 | tf_op jit(solution)/shard_map/ppermute | solution.py:458
  79.9 1.0 collective-permute-start.22
  80.9 1.0 collective-permute-start.17
  81.9 1.2 collective-permute-done.8.refs_0_.refs_1_.refs_2_.refs_3_
  83.1 1.0 collective-permute-start.24
  84.8 9.4 %collective-permute-done.17.refs_6_ = bf16[128,512]{1,0:T(8,128)(2,1)S(1)} collective-permute-done((bf16[128,512]{1,0:T(8,128)(2,1)S(1)}, bf16[128,512]{1,0:T(8,128)(2,1)S(1)}, u32[]{:S(2)}, u32[]{:S(2)}) %collective-permute-start.17) | collective-permute-done | bytes 131104 | tf_op jit(solution)/shard_map/ppermute | solution.py:458
  94.2 0.9 collective-permute-start.7
  95.8 1.2 collective-permute-start.27
  97.6 1.0 collective-permute-start.19
  98.6 1.5 collective-permute-start.28
  100.3 0.6 partial_keys.11
  100.9 1.3 collective-permute-start.18
  102.6 2.4 %collective-permute-done.28 = bf16[128,512]{1,0:T(8,128)(2,1)S(1)} collective-permute-done((bf16[128,512]{1,0:T(8,128)(2,1)S(1)}, bf16[128,512]{1,0:T(8,128)(2,1)S(1)}, u32[]{:S(2)}, u32[]{:S(2)}) %collective-permute-start.28) | collective-permute-done | bytes 131104 | tf_op jit(solution)/shard_map/ppermute | solution.py:458
  105.5 4.3 %collective-permute-done.18.refs_0_ = bf16[256,512]{1,0:T(8,128)(2,1)S(1)} collective-permute-done((bf16[256,512]{1,0:T(8,128)(2,1)S(1)}, bf16[256,512]{1,0:T(8,128)(2,1)S(1)}, u32[]{:S(2)}, u32[]{:S(2)}) %collective-permute-start.18) | collective-permute-done | bytes 262176 | tf_op jit(solution)/shard_map/ppermute | solution.py:458
  111.0 1.7 %collective-permute-start.34 = (bf16[256,512]{1,0:T(8,128)(2,1)S(1)}, bf16[256,512]{1,0:T(8,128)(2,1)S(1)}, u32[]{:S(2)}, u32[]{:S(2)}) collective-permute-start(bf16[256,512]{1,0:T(8,128)(2,1)S(1)} %key_backward.1.refs_4_), channel_id=1, source_target_pairs={{0,6},{1,7},{2,4},{3,5},{4,2},{5,3},{6,0},{7,1},{8,14},{9,15},{10,... | collective-permute-start | bytes 786440 | tf_op jit(solution)/shard_map/ppermute | solution.py:458
  112.9 1.3 collective-permute-start.31
  114.2 3.2 %gradient.4.refs_8_ = f32[1536,512]{1,0:T(8,128)S(1)} custom-call(s32[2]{0:T(128)S(1)} %pad_add_fusion.place_ref, bf16[1536,256]{1,0:T(8,128)(2,1)S(1)} %get-tuple-element.101.refs_0_, bf16[1536,256]{1,0:T(8,128)(2,1)S(1)} %get-tuple-element.102.refs_1_, bf16[1536,256]{1,0:T(8,128)(2,1)S(1)} %get-tuple-element.103.refs_2_, ...), custom_call_target="tpu_custom_call" | custom-call | flops 1610612736 | bytes 6291456 | tf_op jit(solution)/shard_map/gradient/pallas_call | solution.py:236
  117.4 0.6 collective-permute-start.21
  118.0 3.6 %gradient.5 = (f32[1536,512]{1,0:T(8,128)S(1)}, f32[8,128]{1,0:T(8,128)S(1)}, f32[1536,128]{1,0:T(8,128)S(1)}) custom-call(s32[2]{0:T(128)S(1)} %pad_add_fusion.place_ref, bf16[1536,256]{1,0:T(8,128)(2,1)S(1)} %get-tuple-element.77.refs_0_, bf16[1536,256]{1,0:T(8,128)(2,1)S(1)} %get-tuple-element.78.refs_1_, ...), custom_call_target="tpu_custom_call" | custom-call | flops 1610612736 | bytes 6291456 | tf_op jit(solution)/shard_map/gradient/pallas_call | solution.py:236
  121.7 4.6 %collective-permute-done.31.refs_6_ = bf16[256,512]{1,0:T(8,128)(2,1)S(1)} collective-permute-done((bf16[256,512]{1,0:T(8,128)(2,1)S(1)}, bf16[256,512]{1,0:T(8,128)(2,1)S(1)}, u32[]{:S(2)}, u32[]{:S(2)}) %collective-permute-start.31) | collective-permute-done | bytes 262176 | tf_op jit(solution)/shard_map/ppermute | solution.py:458
  126.8 3.2 %gradient.6.refs_8_ = f32[1536,512]{1,0:T(8,128)S(1)} custom-call(s32[2]{0:T(128)S(1)} %pad_add_fusion.place_ref, bf16[1536,256]{1,0:T(8,128)(2,1)S(1)} %get-tuple-element.101.refs_0_, bf16[1536,256]{1,0:T(8,128)(2,1)S(1)} %get-tuple-element.102.refs_1_, bf16[1536,256]{1,0:T(8,128)(2,1)S(1)} %get-tuple-element.103.refs_2_, ...), custom_call_target="tpu_custom_call" | custom-call | flops 1610612736 | bytes 6291456 | tf_op jit(solution)/shard_map/gradient/pallas_call | solution.py:236
  130.1 3.6 %gradient.7 = (f32[1536,512]{1,0:T(8,128)S(1)}, f32[8,128]{1,0:T(8,128)S(1)}, f32[1536,128]{1,0:T(8,128)S(1)}) custom-call(s32[2]{0:T(128)S(1)} %pad_add_fusion.place_ref, bf16[1536,256]{1,0:T(8,128)(2,1)S(1)} %get-tuple-element.77.refs_0_, bf16[1536,256]{1,0:T(8,128)(2,1)S(1)} %get-tuple-element.78.refs_1_, ...), custom_call_target="tpu_custom_call" | custom-call | flops 1610612736 | bytes 6291456 | tf_op jit(solution)/shard_map/gradient/pallas_call | solution.py:236
  133.8 1.1 collective-permute-done.36
  134.9 1.6 collective-permute-start.39
  136.5 1.3 collective-permute-start.38
  138.4 1.0 collective-permute-done.39.refs_3_
  139.4 0.7 collective-permute-done.38.refs_2_
  140.1 1.3 collective-permute-done.37.refs_1_
  141.4 1.5 adam_frag.1
  143.0 1.6 collective-permute-start.40
  144.6 1.7 %collective-permute-start.41 = (bf16[384,128]{1,0:T(8,128)(2,1)S(1)}, bf16[384,128]{1,0:T(8,128)(2,1)S(1)}, u32[]{:S(2)}, u32[]{:S(2)}) collective-permute-start(bf16[384,128]{1,0:T(8,128)(2,1)S(1)} %get-tuple-element.121), channel_id=1, source_target_pairs={{0,16},{8,24},{16,0},{24,8},{1,17},{9,25},{17,1},{25,9},{2,18},{10... | collective-permute-start | bytes 294920 | tf_op jit(solution)/shard_map/ppermute | solution.py:458
  146.3 1.2 collective-permute-start.42
  147.5 6.0 %adam_rows.2 = (f32[1536,1024]{1,0:T(8,128)}, f32[1536,1024]{1,0:T(8,128)}, f32[1536,1024]{1,0:T(8,128)}, f32[8,128]{1,0:T(8,128)S(1)}) custom-call(f32[3]{0:T(128)S(1)} %pad_maximum_fusion.sc_ref, f32[1536,1024]{1,0:T(8,128)S(1)} %bitcast.42, f32[1536,1024]{1,0:T(8,128)S(1)} %bitcast.50, f32[1536,1024]{1,0:T(8,128)S(1)} %bitcast.58, ...), custom_call_target="tpu_custom_call" | custom-call | flops 15728640 | bytes 22020096 | tf_op jit(solution)/shard_map/adam_rows/pallas_call | solution.py:291
  154.0 2.5 %collective-permute-start.45 = (bf16[384,128]{1,0:T(8,128)(2,1)S(1)}, bf16[384,128]{1,0:T(8,128)(2,1)S(1)}, u32[]{:S(2)}, u32[]{:S(2)}) collective-permute-start(bf16[384,128]{1,0:T(8,128)(2,1)S(1)} %convert_element_type.24.refs_7_), channel_id=1, source_target_pairs={{0,24},{8,16},{16,8},{24,0},{1,25},{9,17},{17,9},{25,1},{2,26},{10... | collective-permute-start | bytes 294920 | tf_op jit(solution)/shard_map/ppermute | solution.py:458
  156.5 0.7 collective-permute-start.44
  157.1 1.3 collective-permute-start.43
  158.4 6.0 %adam_rows.3 = (f32[1536,1024]{1,0:T(8,128)}, f32[1536,1024]{1,0:T(8,128)}, f32[1536,1024]{1,0:T(8,128)}) custom-call(f32[3]{0:T(128)S(1)} %pad_maximum_fusion.sc_ref, f32[1536,1024]{1,0:T(8,128)S(1)} %bitcast.43, f32[1536,1024]{1,0:T(8,128)S(1)} %bitcast.51, ...), custom_call_target="tpu_custom_call", output_to_operand_aliasing={{0}: (10, {}), {1}: (11, {}), {2}: (12, {})} | custom-call | flops 15728640 | bytes 22020096 | tf_op jit(solution)/shard_map/adam_rows/pallas_call | solution.py:291
  164.4 1.7 outer_step.1
  (91 shorter events, 7.3 us)
Async XLA Ops:
  3.2 16.8 %collective-permute-start.11 = (f32[384,128]{1,0:T(8,128)S(1)}, f32[384,128]{1,0:T(8,128)S(1)}, u32[]{:S(2)}, u32[]{:S(2)}) collective-permute-start(f32[384,128]{1,0:T(8,128)S(1)} %get-tuple-element.134), channel_id=1, source_target_pairs={{0,8},{8,0},{16,24},{24,16},{1,9},{9,1},{17,25},{25,17},{2,10},{10... | collective-permute-start | bytes 589832 | tf_op jit(solution)/shard_map/ppermute | solution.py:458
  6.3 15.2 %collective-permute-start.13 = (f32[384,128]{1,0:T(8,128)S(1)}, f32[384,128]{1,0:T(8,128)S(1)}, u32[]{:S(2)}, u32[]{:S(2)}) collective-permute-start(f32[384,128]{1,0:T(8,128)S(1)} %get-tuple-element.135), channel_id=1, source_target_pairs={{0,24},{8,16},{16,8},{24,0},{1,25},{9,17},{17,9},{25,1},{2,26},{10... | collective-permute-start | bytes 589832 | tf_op jit(solution)/shard_map/ppermute | solution.py:458
  8.8 17.4 %collective-permute-start.12 = (f32[384,128]{1,0:T(8,128)S(1)}, f32[384,128]{1,0:T(8,128)S(1)}, u32[]{:S(2)}, u32[]{:S(2)}) collective-permute-start(f32[384,128]{1,0:T(8,128)S(1)} %get-tuple-element.136), channel_id=1, source_target_pairs={{0,16},{8,24},{16,0},{24,8},{1,17},{9,25},{17,1},{25,9},{2,18},{10... | collective-permute-start | bytes 589832 | tf_op jit(solution)/shard_map/ppermute | solution.py:458
  11.5 30.7 %collective-permute-start.5 = (bf16[256,1536]{1,0:T(8,128)(2,1)}, bf16[256,1536]{1,0:T(8,128)(2,1)S(1)}, u32[]{:S(2)}, u32[]{:S(2)}) collective-permute-start(bf16[256,1536]{1,0:T(8,128)(2,1)} %get-tuple-element.74), channel_id=1, source_target_pairs={{0,7},{1,6},{2,5},{3,4},{4,3},{5,2},{6,1},{7,0},{8,15},{9,14},{10,... | collective-permute-start | bytes 2359304 | tf_op jit(solution)/shard_map/ppermute | solution.py:458
  14.9 34.6 %collective-permute-start.3 = (bf16[256,1536]{1,0:T(8,128)(2,1)}, bf16[256,1536]{1,0:T(8,128)(2,1)S(1)}, u32[]{:S(2)}, u32[]{:S(2)}) collective-permute-start(bf16[256,1536]{1,0:T(8,128)(2,1)} %pack.6), channel_id=1, source_target_pairs={{0,6},{1,7},{2,4},{3,5},{4,2},{5,3},{6,0},{7,1},{8,14},{9,15},{10,... | collective-permute-start | bytes 2359304 | tf_op jit(solution)/shard_map/ppermute | solution.py:458
  18.4 23.8 %copy-start.4 = (bf16[256,1536]{1,0:T(8,128)(2,1)S(1)}, bf16[256,1536]{1,0:T(8,128)(2,1)}, u32[]{:S(2)}) copy-start(bf16[256,1536]{1,0:T(8,128)(2,1)} %get-tuple-element.70) | copy-start | bytes 2359300
  18.4 23.8 %copy-start.3 = (bf16[256,1536]{1,0:T(8,128)(2,1)S(1)}, bf16[256,1536]{1,0:T(8,128)(2,1)}, u32[]{:S(2)}) copy-start(bf16[256,1536]{1,0:T(8,128)(2,1)} %get-tuple-element.79) | copy-start | bytes 2359300
  20.0 46.2 %collective-permute-start.9 = (bf16[256,1536]{1,0:T(8,128)(2,1)}, bf16[256,1536]{1,0:T(8,128)(2,1)S(1)}, u32[]{:S(2)}, u32[]{:S(2)}) collective-permute-start(bf16[256,1536]{1,0:T(8,128)(2,1)} %get-tuple-element.80), channel_id=1, source_target_pairs={{0,5},{1,4},{2,7},{3,6},{4,1},{5,0},{6,3},{7,2},{8,13},{9,12},{10,... | collective-permute-start | bytes 2359304 | tf_op jit(solution)/shard_map/ppermute | solution.py:458
  26.2 7.7 %collective-permute-start.16 = (f32[384,128]{1,0:T(8,128)S(1)}, f32[384,128]{1,0:T(8,128)S(1)}, u32[]{:S(2)}, u32[]{:S(2)}) collective-permute-start(f32[384,128]{1,0:T(8,128)S(1)} %get-tuple-element.132.refs_3_), channel_id=1, source_target_pairs={{0,24},{8,16},{16,8},{24,0},{1,25},{9,17},{17,9},{25,1},{2,26},{10... | collective-permute-start | bytes 589832 | tf_op jit(solution)/shard_map/ppermute | solution.py:458
  31.7 41.3 %collective-permute-start.4 = (bf16[256,1536]{1,0:T(8,128)(2,1)}, bf16[256,1536]{1,0:T(8,128)(2,1)S(1)}, u32[]{:S(2)}, u32[]{:S(2)}) collective-permute-start(bf16[256,1536]{1,0:T(8,128)(2,1)} %get-tuple-element.72), channel_id=1, source_target_pairs={{0,1},{1,0},{2,3},{3,2},{4,5},{5,4},{6,7},{7,6},{8,9},{9,8},{10,11... | collective-permute-start | bytes 2359304 | tf_op jit(solution)/shard_map/ppermute | solution.py:458
  34.0 8.3 %collective-permute-start.15 = (f32[384,128]{1,0:T(8,128)S(1)}, f32[384,128]{1,0:T(8,128)S(1)}, u32[]{:S(2)}, u32[]{:S(2)}) collective-permute-start(f32[384,128]{1,0:T(8,128)S(1)} %get-tuple-element.132.refs_3_), channel_id=1, source_target_pairs={{0,16},{8,24},{16,0},{24,8},{1,17},{9,25},{17,1},{25,9},{2,18},{10... | collective-permute-start | bytes 589832 | tf_op jit(solution)/shard_map/ppermute | solution.py:458
  42.3 38.6 %collective-permute-start.1 = (bf16[256,1536]{1,0:T(8,128)(2,1)S(1)}, bf16[256,1536]{1,0:T(8,128)(2,1)S(1)}, u32[]{:S(2)}, u32[]{:S(2)}) collective-permute-start(bf16[256,1536]{1,0:T(8,128)(2,1)S(1)} %copy-done.4), channel_id=1, source_target_pairs={{0,3},{1,2},{2,1},{3,0},{4,7},{5,6},{6,5},{7,4},{8,11},{9,10},{10,... | collective-permute-start | bytes 2359304 | tf_op jit(solution)/shard_map/ppermute | solution.py:458
  42.3 23.9 %copy-start.2 = (bf16[256,1536]{1,0:T(8,128)(2,1)S(1)}, bf16[256,1536]{1,0:T(8,128)(2,1)}, u32[]{:S(2)}) copy-start(bf16[256,1536]{1,0:T(8,128)(2,1)} %get-tuple-element.69) | copy-start | bytes 2359300
  42.3 40.8 %collective-permute-start.8 = (bf16[256,1536]{1,0:T(8,128)(2,1)S(1)}, bf16[256,1536]{1,0:T(8,128)(2,1)S(1)}, u32[]{:S(2)}, u32[]{:S(2)}) collective-permute-start(bf16[256,1536]{1,0:T(8,128)(2,1)S(1)} %copy-done.3), channel_id=1, source_target_pairs={{0,4},{1,5},{2,6},{3,7},{4,0},{5,1},{6,2},{7,3},{8,12},{9,13},{10,... | collective-permute-start | bytes 2359304 | tf_op jit(solution)/shard_map/ppermute | solution.py:458
  49.6 25.6 %collective-permute-start.6 = (bf16[256,512]{1,0:T(8,128)(2,1)S(1)}, bf16[256,512]{1,0:T(8,128)(2,1)S(1)}, u32[]{:S(2)}, u32[]{:S(2)}) collective-permute-start(bf16[256,512]{1,0:T(8,128)(2,1)S(1)} %get-tuple-element.75), channel_id=1, source_target_pairs={{0,1},{1,0},{2,3},{3,2},{4,5},{5,4},{6,7},{7,6},{8,9},{9,8},{10,11... | collective-permute-start | bytes 786440 | tf_op jit(solution)/shard_map/ppermute | solution.py:458
  66.2 31.4 %collective-permute-start = (bf16[256,1536]{1,0:T(8,128)(2,1)S(1)}, bf16[256,1536]{1,0:T(8,128)(2,1)S(1)}, u32[]{:S(2)}, u32[]{:S(2)}) collective-permute-start(bf16[256,1536]{1,0:T(8,128)(2,1)S(1)} %copy-done.2), channel_id=1, source_target_pairs={{0,2},{1,3},{2,0},{3,1},{4,6},{5,7},{6,4},{7,5},{8,10},{9,11},{10,... | collective-permute-start | bytes 2359304 | tf_op jit(solution)/shard_map/ppermute | solution.py:458
  70.8 4.4 %copy-start.1 = (bf16[1,256,1024]{2,1,0:T(8,128)(2,1)S(1)}, bf16[1,256,1024]{2,1,0:T(8,128)(2,1)}, u32[]{:S(2)}) copy-start(bf16[1,256,1024]{2,1,0:T(8,128)(2,1)} %param.10) | copy-start | bytes 1572868
  73.1 6.8 %collective-permute-start.14 = (f32[384,128]{1,0:T(8,128)S(1)}, f32[384,128]{1,0:T(8,128)S(1)}, u32[]{:S(2)}, u32[]{:S(2)}) collective-permute-start(f32[384,128]{1,0:T(8,128)S(1)} %get-tuple-element.132.refs_3_), channel_id=1, source_target_pairs={{0,8},{8,0},{16,24},{24,16},{1,9},{9,1},{17,25},{25,17},{2,10},{10... | collective-permute-start | bytes 589832 | tf_op jit(solution)/shard_map/ppermute | solution.py:458
  75.2 9.5 %collective-permute-start.10 = (bf16[256,512]{1,0:T(8,128)(2,1)S(1)}, bf16[256,512]{1,0:T(8,128)(2,1)S(1)}, u32[]{:S(2)}, u32[]{:S(2)}) collective-permute-start(bf16[256,512]{1,0:T(8,128)(2,1)S(1)} %get-tuple-element.86), channel_id=1, source_target_pairs={{0,1},{1,0},{2,3},{3,2},{4,5},{5,4},{6,7},{7,6},{8,9},{9,8},{10,11... | collective-permute-start | bytes 786440 | tf_op jit(solution)/shard_map/ppermute | solution.py:458
  79.9 15.9 %collective-permute-start.22 = (bf16[256,512]{1,0:T(8,128)(2,1)S(1)}, bf16[256,512]{1,0:T(8,128)(2,1)S(1)}, u32[]{:S(2)}, u32[]{:S(2)}) collective-permute-start(bf16[256,512]{1,0:T(8,128)(2,1)S(1)} %slice.32.refs_4_), channel_id=1, source_target_pairs={{0,2},{1,3},{2,0},{3,1},{4,6},{5,7},{6,4},{7,5},{8,10},{9,11},{10,... | collective-permute-start | bytes 786440 | tf_op jit(solution)/shard_map/ppermute | solution.py:458
  80.9 13.3 %collective-permute-start.17 = (bf16[128,512]{1,0:T(8,128)(2,1)S(1)}, bf16[128,512]{1,0:T(8,128)(2,1)S(1)}, u32[]{:S(2)}, u32[]{:S(2)}) collective-permute-start(bf16[128,512]{1,0:T(8,128)(2,1)S(1)} %get-tuple-element.90), channel_id=1, source_target_pairs={{0,2},{1,3},{2,0},{3,1},{4,6},{5,7},{6,4},{7,5},{8,10},{9,11},{10,... | collective-permute-start | bytes 393224 | tf_op jit(solution)/shard_map/ppermute | solution.py:458
  83.1 14.4 %collective-permute-start.24 = (bf16[256,512]{1,0:T(8,128)(2,1)S(1)}, bf16[256,512]{1,0:T(8,128)(2,1)S(1)}, u32[]{:S(2)}, u32[]{:S(2)}) collective-permute-start(bf16[256,512]{1,0:T(8,128)(2,1)S(1)} %slice.32.refs_4_), channel_id=1, source_target_pairs={{0,4},{1,5},{2,6},{3,7},{4,0},{5,1},{6,2},{7,3},{8,12},{9,13},{10,... | collective-permute-start | bytes 786440 | tf_op jit(solution)/shard_map/ppermute | solution.py:458
  84.7 13.9 %collective-permute-start.2 = (bf16[256,512]{1,0:T(8,128)(2,1)S(1)}, bf16[256,512]{1,0:T(8,128)(2,1)S(1)}, u32[]{:S(2)}, u32[]{:S(2)}) collective-permute-start(bf16[256,512]{1,0:T(8,128)(2,1)S(1)} %get-tuple-element.71), channel_id=1, source_target_pairs={{0,1},{1,0},{2,3},{3,2},{4,5},{5,4},{6,7},{7,6},{8,9},{9,8},{10,11... | collective-permute-start | bytes 786440 | tf_op jit(solution)/shard_map/ppermute | solution.py:458
  94.2 6.1 %collective-permute-start.7 = (bf16[128,512]{1,0:T(8,128)(2,1)S(1)}, bf16[128,512]{1,0:T(8,128)(2,1)S(1)}, u32[]{:S(2)}, u32[]{:S(2)}) collective-permute-start(bf16[128,512]{1,0:T(8,128)(2,1)S(1)} %get-tuple-element.76), channel_id=1, source_target_pairs={{0,4},{1,5},{2,6},{3,7},{4,0},{5,1},{6,2},{7,3},{8,12},{9,13},{10,... | collective-permute-start | bytes 393224 | tf_op jit(solution)/shard_map/ppermute | solution.py:458
  95.7 14.1 %copy-start = (bf16[256,1536]{1,0:T(8,128)(2,1)S(1)}, bf16[256,1536]{1,0:T(8,128)(2,1)}, u32[]{:S(2)}) copy-start(bf16[256,1536]{1,0:T(8,128)(2,1)} %get-tuple-element.95.refs_0_.refs_1_.refs_2_.refs_3_) | copy-start | bytes 2359300
  95.8 6.8 %collective-permute-start.27 = (bf16[128,512]{1,0:T(8,128)(2,1)S(1)}, bf16[128,512]{1,0:T(8,128)(2,1)S(1)}, u32[]{:S(2)}, u32[]{:S(2)}) collective-permute-start(bf16[128,512]{1,0:T(8,128)(2,1)S(1)} %slice.26), channel_id=1, source_target_pairs={{0,4},{1,5},{2,6},{3,7},{4,0},{5,1},{6,2},{7,3},{8,12},{9,13},{10,... | collective-permute-start | bytes 393224 | tf_op jit(solution)/shard_map/ppermute | solution.py:458
  97.5 7.5 %collective-permute-start.20 = (bf16[256,512]{1,0:T(8,128)(2,1)S(1)}, bf16[256,512]{1,0:T(8,128)(2,1)S(1)}, u32[]{:S(2)}, u32[]{:S(2)}) collective-permute-start(bf16[256,512]{1,0:T(8,128)(2,1)S(1)} %get-tuple-element.96), channel_id=1, source_target_pairs={{0,1},{1,0},{2,3},{3,2},{4,5},{5,4},{6,7},{7,6},{8,9},{9,8},{10,11... | collective-permute-start | bytes 786440 | tf_op jit(solution)/shard_map/ppermute | solution.py:458
  97.6 12.8 %collective-permute-start.19 = (bf16[256,512]{1,0:T(8,128)(2,1)S(1)}, bf16[256,512]{1,0:T(8,128)(2,1)S(1)}, u32[]{:S(2)}, u32[]{:S(2)}) collective-permute-start(bf16[256,512]{1,0:T(8,128)(2,1)S(1)} %get-tuple-element.94), channel_id=1, source_target_pairs={{0,4},{1,5},{2,6},{3,7},{4,0},{5,1},{6,2},{7,3},{8,12},{9,13},{10,... | collective-permute-start | bytes 786440 | tf_op jit(solution)/shard_map/ppermute | solution.py:458
  98.6 6.3 %collective-permute-start.28 = (bf16[128,512]{1,0:T(8,128)(2,1)S(1)}, bf16[128,512]{1,0:T(8,128)(2,1)S(1)}, u32[]{:S(2)}, u32[]{:S(2)}) collective-permute-start(bf16[128,512]{1,0:T(8,128)(2,1)S(1)} %slice.27), channel_id=1, source_target_pairs={{0,2},{1,3},{2,0},{3,1},{4,6},{5,7},{6,4},{7,5},{8,10},{9,11},{10,... | collective-permute-start | bytes 393224 | tf_op jit(solution)/shard_map/ppermute | solution.py:458
  100.9 8.9 %collective-permute-start.18 = (bf16[256,512]{1,0:T(8,128)(2,1)S(1)}, bf16[256,512]{1,0:T(8,128)(2,1)S(1)}, u32[]{:S(2)}, u32[]{:S(2)}) collective-permute-start(bf16[256,512]{1,0:T(8,128)(2,1)S(1)} %get-tuple-element.93), channel_id=1, source_target_pairs={{0,2},{1,3},{2,0},{3,1},{4,6},{5,7},{6,4},{7,5},{8,10},{9,11},{10,... | collective-permute-start | bytes 786440 | tf_op jit(solution)/shard_map/ppermute | solution.py:458
  102.6 10.1 %collective-permute-start.26 = (bf16[256,512]{1,0:T(8,128)(2,1)S(1)}, bf16[256,512]{1,0:T(8,128)(2,1)S(1)}, u32[]{:S(2)}, u32[]{:S(2)}) collective-permute-start(bf16[256,512]{1,0:T(8,128)(2,1)S(1)} %slice.32.refs_4_), channel_id=1, source_target_pairs={{0,1},{1,0},{2,3},{3,2},{4,5},{5,4},{6,7},{7,6},{8,9},{9,8},{10,11... | collective-permute-start | bytes 786440 | tf_op jit(solution)/shard_map/ppermute | solution.py:458
  105.0 7.9 %collective-permute-start.29 = (bf16[256,512]{1,0:T(8,128)(2,1)S(1)}, bf16[256,512]{1,0:T(8,128)(2,1)S(1)}, u32[]{:S(2)}, u32[]{:S(2)}) collective-permute-start(bf16[256,512]{1,0:T(8,128)(2,1)S(1)} %constant_dynamic-update-slice_fusion.refs_6_), channel_id=1, source_target_pairs={{0,1},{1,0},{2,3},{3,2},{4,5},{5,4},{6,7},{7,6},{8,9},{9,8},{10,11... | collective-permute-start | bytes 786440 | tf_op jit(solution)/shard_map/ppermute | solution.py:458
  105.0 12.4 %collective-permute-start.23 = (bf16[256,512]{1,0:T(8,128)(2,1)S(1)}, bf16[256,512]{1,0:T(8,128)(2,1)S(1)}, u32[]{:S(2)}, u32[]{:S(2)}) collective-permute-start(bf16[256,512]{1,0:T(8,128)(2,1)S(1)} %collective-permute-done.22.refs_4_), channel_id=1, source_target_pairs={{0,1},{1,0},{2,3},{3,2},{4,5},{5,4},{6,7},{7,6},{8,9},{9,8},{10,11... | collective-permute-start | bytes 786440 | tf_op jit(solution)/shard_map/ppermute | solution.py:458
  109.8 8.2 %collective-permute-start.25 = (bf16[256,512]{1,0:T(8,128)(2,1)S(1)}, bf16[256,512]{1,0:T(8,128)(2,1)S(1)}, u32[]{:S(2)}, u32[]{:S(2)}) collective-permute-start(bf16[256,512]{1,0:T(8,128)(2,1)S(1)} %collective-permute-done.24.refs_6_), channel_id=1, source_target_pairs={{0,1},{1,0},{2,3},{3,2},{4,5},{5,4},{6,7},{7,6},{8,9},{9,8},{10,11... | collective-permute-start | bytes 786440 | tf_op jit(solution)/shard_map/ppermute | solution.py:458
  109.9 37.6 %slice-start.4 = ((s8[6291456]{0:T(1024)(128)(4,1)}), s8[4194304]{0:T(1024)(128)(4,1)S(1)}, s32[]{:S(2)}) async-start(s8[6291456]{0:T(1024)(128)(4,1)} %bitcast.56), calls=%async_computation.4 | async-start | bytes 8388608
  111.0 10.6 %collective-permute-start.34 = (bf16[256,512]{1,0:T(8,128)(2,1)S(1)}, bf16[256,512]{1,0:T(8,128)(2,1)S(1)}, u32[]{:S(2)}, u32[]{:S(2)}) collective-permute-start(bf16[256,512]{1,0:T(8,128)(2,1)S(1)} %key_backward.1.refs_4_), channel_id=1, source_target_pairs={{0,6},{1,7},{2,4},{3,5},{4,2},{5,3},{6,0},{7,1},{8,14},{9,15},{10,... | collective-permute-start | bytes 786440 | tf_op jit(solution)/shard_map/ppermute | solution.py:458
  112.7 14.1 %collective-permute-start.33 = (bf16[256,512]{1,0:T(8,128)(2,1)S(1)}, bf16[256,512]{1,0:T(8,128)(2,1)S(1)}, u32[]{:S(2)}, u32[]{:S(2)}) collective-permute-start(bf16[256,512]{1,0:T(8,128)(2,1)S(1)} %key_backward.1.refs_4_), channel_id=1, source_target_pairs={{0,1},{1,0},{2,3},{3,2},{4,5},{5,4},{6,7},{7,6},{8,9},{9,8},{10,11... | collective-permute-start | bytes 786440 | tf_op jit(solution)/shard_map/ppermute | solution.py:458
  112.9 13.4 %collective-permute-start.31 = (bf16[256,512]{1,0:T(8,128)(2,1)S(1)}, bf16[256,512]{1,0:T(8,128)(2,1)S(1)}, u32[]{:S(2)}, u32[]{:S(2)}) collective-permute-start(bf16[256,512]{1,0:T(8,128)(2,1)S(1)} %key_backward.1.refs_4_), channel_id=1, source_target_pairs={{0,4},{1,5},{2,6},{3,7},{4,0},{5,1},{6,2},{7,3},{8,12},{9,13},{10,... | collective-permute-start | bytes 786440 | tf_op jit(solution)/shard_map/ppermute | solution.py:458
  117.4 8.9 %collective-permute-start.21 = (bf16[256,512]{1,0:T(8,128)(2,1)S(1)}, bf16[256,512]{1,0:T(8,128)(2,1)S(1)}, u32[]{:S(2)}, u32[]{:S(2)}) collective-permute-start(bf16[256,512]{1,0:T(8,128)(2,1)S(1)} %key_backward.1.refs_4_), channel_id=1, source_target_pairs={{0,2},{1,3},{2,0},{3,1},{4,6},{5,7},{6,4},{7,5},{8,10},{9,11},{10,... | collective-permute-start | bytes 786440 | tf_op jit(solution)/shard_map/ppermute | solution.py:458
  118.0 29.4 %slice-start.5 = ((s8[6291456]{0:T(1024)(128)(4,1)}), s8[2097152]{0:T(1024)(128)(4,1)S(1)}, s32[]{:S(2)}) async-start(s8[6291456]{0:T(1024)(128)(4,1)} %bitcast.56), calls=%async_computation.5 | async-start | bytes 4194304
  121.6 5.2 %collective-permute-start.35 = (bf16[256,512]{1,0:T(8,128)(2,1)S(1)}, bf16[256,512]{1,0:T(8,128)(2,1)S(1)}, u32[]{:S(2)}, u32[]{:S(2)}) collective-permute-start(bf16[256,512]{1,0:T(8,128)(2,1)S(1)} %collective-permute-done.34.refs_6_), channel_id=1, source_target_pairs={{0,1},{1,0},{2,3},{3,2},{4,5},{5,4},{6,7},{7,6},{8,9},{9,8},{10,11... | collective-permute-start | bytes 786440 | tf_op jit(solution)/shard_map/ppermute | solution.py:458
  126.3 3.7 %collective-permute-start.30 = (bf16[256,512]{1,0:T(8,128)(2,1)S(1)}, bf16[256,512]{1,0:T(8,128)(2,1)S(1)}, u32[]{:S(2)}, u32[]{:S(2)}) collective-permute-start(bf16[256,512]{1,0:T(8,128)(2,1)S(1)} %collective-permute-done.21.refs_4_), channel_id=1, source_target_pairs={{0,1},{1,0},{2,3},{3,2},{4,5},{5,4},{6,7},{7,6},{8,9},{9,8},{10,11... | collective-permute-start | bytes 786440 | tf_op jit(solution)/shard_map/ppermute | solution.py:458
  126.3 3.7 %collective-permute-start.32 = (bf16[256,512]{1,0:T(8,128)(2,1)S(1)}, bf16[256,512]{1,0:T(8,128)(2,1)S(1)}, u32[]{:S(2)}, u32[]{:S(2)}) collective-permute-start(bf16[256,512]{1,0:T(8,128)(2,1)S(1)} %collective-permute-done.31.refs_6_), channel_id=1, source_target_pairs={{0,1},{1,0},{2,3},{3,2},{4,5},{5,4},{6,7},{7,6},{8,9},{9,8},{10,11... | collective-permute-start | bytes 786440 | tf_op jit(solution)/shard_map/ppermute | solution.py:458
  126.8 20.7 %slice-start = ((s8[6291456]{0:T(1024)(128)(4,1)}), s8[4194304]{0:T(1024)(128)(4,1)S(1)}, s32[]{:S(2)}) async-start(s8[6291456]{0:T(1024)(128)(4,1)} %bitcast.40), calls=%async_computation | async-start | bytes 8388608
  126.8 20.7 %slice-start.2 = ((s8[6291456]{0:T(1024)(128)(4,1)}), s8[4194304]{0:T(1024)(128)(4,1)S(1)}, s32[]{:S(2)}) async-start(s8[6291456]{0:T(1024)(128)(4,1)} %bitcast.48), calls=%async_computation.2 | async-start | bytes 8388608
  130.0 17.4 %slice-start.1 = ((s8[6291456]{0:T(1024)(128)(4,1)}), s8[2097152]{0:T(1024)(128)(4,1)S(1)}, s32[]{:S(2)}) async-start(s8[6291456]{0:T(1024)(128)(4,1)} %bitcast.40), calls=%async_computation.1 | async-start | bytes 4194304
  130.0 17.4 %slice-start.3 = ((s8[6291456]{0:T(1024)(128)(4,1)}), s8[2097152]{0:T(1024)(128)(4,1)S(1)}, s32[]{:S(2)}) async-start(s8[6291456]{0:T(1024)(128)(4,1)} %bitcast.48), calls=%async_computation.3 | async-start | bytes 4194304
  133.6 1.2 collective-permute-start.36
  134.9 4.5 %collective-permute-start.39 = (f32[8,128]{1,0:T(8,128)S(1)}, f32[8,128]{1,0:T(8,128)S(1)}, u32[]{:S(2)}, u32[]{:S(2)}) collective-permute-start(f32[8,128]{1,0:T(8,128)S(1)} %add.32.refs_0_), channel_id=1, source_target_pairs={{0,6},{1,7},{2,4},{3,5},{4,2},{5,3},{6,0},{7,1},{8,14},{9,15},{10,... | collective-permute-start | bytes 12296 | tf_op jit(solution)/shard_map/ppermute | solution.py:458
  136.5 3.6 %collective-permute-start.38 = (f32[8,128]{1,0:T(8,128)S(1)}, f32[8,128]{1,0:T(8,128)S(1)}, u32[]{:S(2)}, u32[]{:S(2)}) collective-permute-start(f32[8,128]{1,0:T(8,128)S(1)} %add.32.refs_0_), channel_id=1, source_target_pairs={{0,4},{1,5},{2,6},{3,7},{4,0},{5,1},{6,2},{7,3},{8,12},{9,13},{10,... | collective-permute-start | bytes 12296 | tf_op jit(solution)/shard_map/ppermute | solution.py:458
  137.8 3.6 %collective-permute-start.37 = (f32[8,128]{1,0:T(8,128)S(1)}, f32[8,128]{1,0:T(8,128)S(1)}, u32[]{:S(2)}, u32[]{:S(2)}) collective-permute-start(f32[8,128]{1,0:T(8,128)S(1)} %add.32.refs_0_), channel_id=1, source_target_pairs={{0,2},{1,3},{2,0},{3,1},{4,6},{5,7},{6,4},{7,5},{8,10},{9,11},{10,... | collective-permute-start | bytes 12296 | tf_op jit(solution)/shard_map/ppermute | solution.py:458
  143.0 10.5 %collective-permute-start.40 = (bf16[384,128]{1,0:T(8,128)(2,1)S(1)}, bf16[384,128]{1,0:T(8,128)(2,1)S(1)}, u32[]{:S(2)}, u32[]{:S(2)}) collective-permute-start(bf16[384,128]{1,0:T(8,128)(2,1)S(1)} %get-tuple-element.120), channel_id=1, source_target_pairs={{0,8},{8,0},{16,24},{24,16},{1,9},{9,1},{17,25},{25,17},{2,10},{10... | collective-permute-start | bytes 294920 | tf_op jit(solution)/shard_map/ppermute | solution.py:458
  144.6 9.3 %collective-permute-start.41 = (bf16[384,128]{1,0:T(8,128)(2,1)S(1)}, bf16[384,128]{1,0:T(8,128)(2,1)S(1)}, u32[]{:S(2)}, u32[]{:S(2)}) collective-permute-start(bf16[384,128]{1,0:T(8,128)(2,1)S(1)} %get-tuple-element.121), channel_id=1, source_target_pairs={{0,16},{8,24},{16,0},{24,8},{1,17},{9,25},{17,1},{25,9},{2,18},{10... | collective-permute-start | bytes 294920 | tf_op jit(solution)/shard_map/ppermute | solution.py:458
  146.3 7.7 %collective-permute-start.42 = (bf16[384,128]{1,0:T(8,128)(2,1)S(1)}, bf16[384,128]{1,0:T(8,128)(2,1)S(1)}, u32[]{:S(2)}, u32[]{:S(2)}) collective-permute-start(bf16[384,128]{1,0:T(8,128)(2,1)S(1)} %get-tuple-element.122), channel_id=1, source_target_pairs={{0,24},{8,16},{16,8},{24,0},{1,25},{9,17},{17,9},{25,1},{2,26},{10... | collective-permute-start | bytes 294920 | tf_op jit(solution)/shard_map/ppermute | solution.py:458
  154.0 10.4 %collective-permute-start.45 = (bf16[384,128]{1,0:T(8,128)(2,1)S(1)}, bf16[384,128]{1,0:T(8,128)(2,1)S(1)}, u32[]{:S(2)}, u32[]{:S(2)}) collective-permute-start(bf16[384,128]{1,0:T(8,128)(2,1)S(1)} %convert_element_type.24.refs_7_), channel_id=1, source_target_pairs={{0,24},{8,16},{16,8},{24,0},{1,25},{9,17},{17,9},{25,1},{2,26},{10... | collective-permute-start | bytes 294920 | tf_op jit(solution)/shard_map/ppermute | solution.py:458
  156.5 8.0 %collective-permute-start.44 = (bf16[384,128]{1,0:T(8,128)(2,1)S(1)}, bf16[384,128]{1,0:T(8,128)(2,1)S(1)}, u32[]{:S(2)}, u32[]{:S(2)}) collective-permute-start(bf16[384,128]{1,0:T(8,128)(2,1)S(1)} %convert_element_type.24.refs_7_), channel_id=1, source_target_pairs={{0,16},{8,24},{16,0},{24,8},{1,17},{9,25},{17,1},{25,9},{2,18},{10... | collective-permute-start | bytes 294920 | tf_op jit(solution)/shard_map/ppermute | solution.py:458
  157.1 7.3 %collective-permute-start.43 = (bf16[384,128]{1,0:T(8,128)(2,1)S(1)}, bf16[384,128]{1,0:T(8,128)(2,1)S(1)}, u32[]{:S(2)}, u32[]{:S(2)}) collective-permute-start(bf16[384,128]{1,0:T(8,128)(2,1)S(1)} %convert_element_type.24.refs_7_), channel_id=1, source_target_pairs={{0,8},{8,0},{16,24},{24,16},{1,9},{9,1},{17,25},{25,17},{2,10},{10... | collective-permute-start | bytes 294920 | tf_op jit(solution)/shard_map/ppermute | solution.py:458

commit v20 on v18

--- a/solution.py
+++ b/solution.py
@@ -496,12 +496,6 @@
     blocks = {k: swap(packed[k], "fsdp", k) for k in order}
     blocks[0], blocks[1] = packed[0], swap(packed[1], "fsdp", 1)
 
-    relay = len(far) == 3 and far[0] == far[1] ^ far[2]
-    half = inputs.shape[0] // 2
-    values = {0: incoming[:, kv_width:]}
-    for i, k in enumerate(far[1:] if relay else far):
-        values[k] = swap(after(values[0], blocks[order[i]]), "fsdp", k)
-
     steps_now = step_count[0].astype(jnp.float32)
     plan = jnp.minimum(1.0, steps_now / WARMUP) * (
         0.55 + 0.45 * jnp.cos(jnp.pi * steps_now / STEPS_TOTAL)
@@ -520,6 +514,8 @@
 
     last = far[-1]
     blocks[last + 1] = after(blocks[last + 1], anchor_copy, momentum_copy, scalars, old_first, old_second)
+    relay = len(far) == 3 and far[0] == far[1] ^ far[2]
+    half = inputs.shape[0] // 2
     parts, flipped, relayed = [], {}, {}
     for k in far + [0]:
         theirs, flipped[k + 1] = partial_keys(blocks[k + 1], key_weights)
@@ -534,8 +530,9 @@
             continue
         part_k, flipped[k] = partial_keys(blocks[k], key_weights, adds)
         if k == last:
-            for j in [0] + [j for j in far if j in values]:
-                values[j] = after(values[j], part_k)
+            values = {0: after(incoming[:, kv_width:], part_k)}
+            for j in far[1:] if relay else far:
+                values[j] = swap(values[0], "fsdp", j)
             if relay:
                 upper = swap(values[far[1]][:half], "fsdp", far[2])
                 lower = swap(values[far[2]][half:], "fsdp", far[1])

time: 168 us -> 176 us (1.048)
  starting transfers between devices: 43.8 us -> 51.2 us
    ppermute x46, starting transfers between devices: 43.8 us -> 51.2 us  [swap(): return lax.ppermute(block, axis, [(i, i ^ offset) for i in range(count)])]
  transfers between devices with their start and end apart: 46 -> 46, of which waited for: 17 -> 16; matrix products, arithmetic and copies ran while one was open for 0% -> 0% of each run, Pallas kernels for 28% -> 26%
where the time goes in v20:
time: 176 us; the launch traced here: 175 us
  waiting for transfers between devices  65.1 us (37%)
  Pallas kernels  54.8 us (31%)
  starting transfers between devices  51.2 us (29%)
  between operations  3.84 us (2%)
    ppermute x46, waiting for transfers between devices, swap(): return lax.ppermute(block, axis, [(i, i ^ offset) for i in range(count)])  65.1 us
    ppermute x46, starting transfers between devices, swap(): return lax.ppermute(block, axis, [(i, i ^ offset) for i in range(count)])  51.2 us
    pallas_call x4, Pallas kernels, gradient(): pl.pallas_call(functools.partial(grad_kernel, len(flipped), base is not N...  13.5 us
    pallas_call x2, Pallas kernels, adam_rows(): pl.pallas_call(functools.partial(adam_kernel, len(squares), len(into)), o...  12 us
    pallas_call x4, Pallas kernels, pack(): pl.pallas_call(functools.partial(pack_kernel, offsets), out_shape=[pltpu....  9.16 us
    pallas_call x3, Pallas kernels, due_columns(): pl.pallas_call(functools.partial(pick_kernel, blocks), out_shape=[jax.Sha...  5.55 us
    pallas_call x8, Pallas kernels, partial_keys(): pl.pallas_call(functools.partial(partial_kernel, pieces, [first for _, fi...  4.6 us
  transfers between devices with their start and end apart: 46, of which 16 were waited for; matrix products, arithmetic and copies ran while one was open for 0% of the time, Pallas kernels for 26%

profile of v20, /device:TPU:0, one launch (start us, length us, event | category | flops | bytes accessed | tf_op | source)
XLA Modules:
  0.0 175.4 jit_solution(5138337232237834698)
XLA Ops:
  1.4 1.8 %due_columns.5.w_ref = f32[4,384,128]{2,1,0:T(8,128)S(1)} custom-call(s32[2]{0:T(128)S(1)} %pad_add_fusion.place_ref, f32[1536,1024]{1,0:T(8,128)} %bitcast.35, f32[1536,1024]{1,0:T(8,128)} %bitcast.36, f32[1536,1024]{1,0:T(8,128)} %bitcast.37, f32[1536,1024]{1,0:T(8,128)} %bitcast.38), custom_call_target="tpu_custom_call" | custom-call | bytes 1572864 | tf_op jit(solution)/shard_map/due_columns/pallas_call | solution.py:348
  3.2 3.1 %collective-permute-start.10 = (f32[384,128]{1,0:T(8,128)S(1)}, f32[384,128]{1,0:T(8,128)S(1)}, u32[]{:S(2)}, u32[]{:S(2)}) collective-permute-start(f32[384,128]{1,0:T(8,128)S(1)} %get-tuple-element.126), channel_id=1, source_target_pairs={{0,8},{8,0},{16,24},{24,16},{1,9},{9,1},{17,25},{25,17},{2,10},{10... | collective-permute-start | bytes 589832 | tf_op jit(solution)/shard_map/ppermute | solution.py:458
  6.3 2.5 %collective-permute-start.12 = (f32[384,128]{1,0:T(8,128)S(1)}, f32[384,128]{1,0:T(8,128)S(1)}, u32[]{:S(2)}, u32[]{:S(2)}) collective-permute-start(f32[384,128]{1,0:T(8,128)S(1)} %get-tuple-element.127), channel_id=1, source_target_pairs={{0,24},{8,16},{16,8},{24,0},{1,25},{9,17},{17,9},{25,1},{2,26},{10... | collective-permute-start | bytes 589832 | tf_op jit(solution)/shard_map/ppermute | solution.py:458
  8.9 2.6 %pack.4 = (bf16[256,1536]{1,0:T(8,128)(2,1)}, bf16[256,1536]{1,0:T(8,128)(2,1)}, bf16[256,1536]{1,0:T(8,128)(2,1)}) custom-call(s32[1]{0:T(128)} %bitcast.4.me_ref, bf16[256,12288]{1,0:T(8,128)(2,1)} %bitcast.64), custom_call_target="tpu_custom_call" | custom-call | bytes 4718592 | tf_op jit(solution)/shard_map/pack/pallas_call | solution.py:69
  11.5 1.4 collective-permute-start.4
  12.9 2.3 %pack.5 = (bf16[256,1536]{1,0:T(8,128)(2,1)}, bf16[256,1536]{1,0:T(8,128)(2,1)}) custom-call(s32[1]{0:T(128)} %bitcast.4.me_ref, bf16[256,12288]{1,0:T(8,128)(2,1)} %bitcast.65), custom_call_target="tpu_custom_call" | custom-call | bytes 3145728 | tf_op jit(solution)/shard_map/pack/pallas_call | solution.py:69
  15.2 1.4 collective-permute-start.8
  16.7 2.0 %pack.6 = bf16[256,1536]{1,0:T(8,128)(2,1)} custom-call(s32[1]{0:T(128)} %bitcast.4.me_ref, bf16[256,12288]{1,0:T(8,128)(2,1)} %bitcast.66), custom_call_target="tpu_custom_call" | custom-call | bytes 1572864 | tf_op jit(solution)/shard_map/pack/pallas_call | solution.py:69
  18.6 1.6 due_columns.4
  20.2 1.6 collective-permute-start.3
  21.8 4.4 %collective-permute-done.11 = f32[384,128]{1,0:T(8,128)S(1)} collective-permute-done((f32[384,128]{1,0:T(8,128)S(1)}, f32[384,128]{1,0:T(8,128)S(1)}, u32[]{:S(2)}, u32[]{:S(2)}) %collective-permute-start.11) | collective-permute-done | bytes 196640 | tf_op jit(solution)/shard_map/ppermute | solution.py:458
  26.3 3.1 %collective-permute-start.15 = (f32[384,128]{1,0:T(8,128)S(1)}, f32[384,128]{1,0:T(8,128)S(1)}, u32[]{:S(2)}, u32[]{:S(2)}) collective-permute-start(f32[384,128]{1,0:T(8,128)S(1)} %get-tuple-element.124.refs_3_), channel_id=1, source_target_pairs={{0,24},{8,16},{16,8},{24,0},{1,25},{9,17},{17,9},{25,1},{2,26},{10... | collective-permute-start | bytes 589832 | tf_op jit(solution)/shard_map/ppermute | solution.py:458
  29.4 6.6 %collective-permute-done.15.refs_6_ = f32[384,128]{1,0:T(8,128)S(1)} collective-permute-done((f32[384,128]{1,0:T(8,128)S(1)}, f32[384,128]{1,0:T(8,128)S(1)}, u32[]{:S(2)}, u32[]{:S(2)}) %collective-permute-start.15) | collective-permute-done | bytes 196640 | tf_op jit(solution)/shard_map/ppermute | solution.py:458
  36.0 6.5 %collective-permute-start.13 = (f32[384,128]{1,0:T(8,128)S(1)}, f32[384,128]{1,0:T(8,128)S(1)}, u32[]{:S(2)}, u32[]{:S(2)}) collective-permute-start(f32[384,128]{1,0:T(8,128)S(1)} %get-tuple-element.124.refs_3_), channel_id=1, source_target_pairs={{0,8},{8,0},{16,24},{24,16},{1,9},{9,1},{17,25},{25,17},{2,10},{10... | collective-permute-start | bytes 589832 | tf_op jit(solution)/shard_map/ppermute | solution.py:458
  42.5 1.8 %collective-permute-done.14.refs_5_ = f32[384,128]{1,0:T(8,128)S(1)} collective-permute-done((f32[384,128]{1,0:T(8,128)S(1)}, f32[384,128]{1,0:T(8,128)S(1)}, u32[]{:S(2)}, u32[]{:S(2)}) %collective-permute-start.14) | collective-permute-done | bytes 196640 | tf_op jit(solution)/shard_map/ppermute | solution.py:458
  44.3 1.5 collective-permute-start.7
  45.9 3.5 %cast_left.1.refs_4_ = bf16[1536,512]{1,0:T(8,128)(2,1)S(1)} custom-call(f32[1536,1024]{1,0:T(8,128)} %bitcast.39), custom_call_target="tpu_custom_call" | custom-call | bytes 4718592 | tf_op jit(solution)/shard_map/cast_left/pallas_call | solution.py:93
  49.4 0.6 partial_keys.9
  50.0 1.7 collective-permute-start.5
  51.7 2.3 %pack.7 = (bf16[256,1536]{1,0:T(8,128)(2,1)}, bf16[256,1536]{1,0:T(8,128)(2,1)}) custom-call(s32[1]{0:T(128)} %bitcast.4.me_ref, bf16[256,12288]{1,0:T(8,128)(2,1)} %bitcast.67), custom_call_target="tpu_custom_call" | custom-call | bytes 3145728 | tf_op jit(solution)/shard_map/pack/pallas_call | solution.py:69
  54.9 11.3 %collective-permute-done.8.refs_0_.refs_1_.refs_2_.refs_3_ = bf16[256,1536]{1,0:T(8,128)(2,1)S(1)} collective-permute-done((bf16[256,1536]{1,0:T(8,128)(2,1)}, bf16[256,1536]{1,0:T(8,128)(2,1)S(1)}, u32[]{:S(2)}, u32[]{:S(2)}) %collective-permute-start.8) | collective-permute-done | bytes 786464 | tf_op jit(solution)/shard_map/ppermute | solution.py:458
  66.5 2.8 %duplicate.1 = (f32[384,1024]{1,0:T(8,128)}, f32[384,1024]{1,0:T(8,128)}) custom-call(f32[384,1024]{1,0:T(8,128)} %refs_0_.3, f32[384,1024]{1,0:T(8,128)} %refs_1_.3), custom_call_target="tpu_custom_call" | custom-call | bytes 6291456 | tf_op jit(solution)/shard_map/duplicate/pallas_call | solution.py:389
  69.4 2.1 %due_columns.3 = (f32[4,384,128]{2,1,0:T(8,128)S(1)}, f32[4,384,128]{2,1,0:T(8,128)S(1)}) custom-call(s32[2]{0:T(128)S(1)} %pad_add_fusion.place_ref, f32[1536,1024]{1,0:T(8,128)} %bitcast.44, f32[1536,1024]{1,0:T(8,128)} %bitcast.45, f32[1536,1024]{1,0:T(8,128)} %bitcast.46, f32[1536,1024]{1,0:T(8,128)} %bitcast.47, f32[1536,1024]{1,0:T(8,128)} %bitcast.52, ...), custom_call_target="tpu_custom_call" | custom-call | bytes 3145728 | tf_op jit(solution)/shard_map/due_columns/pallas_call | solution.py:348
  71.5 0.6 partial_keys.12
  72.4 0.9 collective-permute-start
  73.9 1.1 collective-permute-start.16
  75.1 8.0 %collective-permute-done.7.refs_0_.refs_1_.refs_2_.refs_3_ = bf16[256,1536]{1,0:T(8,128)(2,1)S(1)} collective-permute-done((bf16[256,1536]{1,0:T(8,128)(2,1)S(1)}, bf16[256,1536]{1,0:T(8,128)(2,1)S(1)}, u32[]{:S(2)}, u32[]{:S(2)}) %collective-permute-start.7) | collective-permute-done | bytes 786464 | tf_op jit(solution)/shard_map/ppermute | solution.py:458
  83.1 11.8 %collective-permute-done.16.refs_6_ = bf16[128,512]{1,0:T(8,128)(2,1)S(1)} collective-permute-done((bf16[128,512]{1,0:T(8,128)(2,1)S(1)}, bf16[128,512]{1,0:T(8,128)(2,1)S(1)}, u32[]{:S(2)}, u32[]{:S(2)}) %collective-permute-start.16) | collective-permute-done | bytes 131104 | tf_op jit(solution)/shard_map/ppermute | solution.py:458
  95.5 1.0 collective-permute-start.22
  96.5 1.5 collective-permute-start.24
  98.7 4.6 %collective-permute-done.22.refs_4_ = bf16[256,512]{1,0:T(8,128)(2,1)S(1)} collective-permute-done((bf16[256,512]{1,0:T(8,128)(2,1)S(1)}, bf16[256,512]{1,0:T(8,128)(2,1)S(1)}, u32[]{:S(2)}, u32[]{:S(2)}) %collective-permute-start.22) | collective-permute-done | bytes 262176 | tf_op jit(solution)/shard_map/ppermute | solution.py:458
  103.3 0.9 collective-permute-start.6
  104.2 1.2 collective-permute-start.27
  106.7 0.9 collective-permute-start.18
  107.6 1.1 collective-permute-done.6.refs_6_
  108.7 0.9 collective-permute-start.28
  109.6 0.6 partial_keys.11
  110.8 0.9 collective-permute-start.17
  111.7 3.3 %collective-permute-done.28 = bf16[128,512]{1,0:T(8,128)(2,1)S(1)} collective-permute-done((bf16[128,512]{1,0:T(8,128)(2,1)S(1)}, bf16[128,512]{1,0:T(8,128)(2,1)S(1)}, u32[]{:S(2)}, u32[]{:S(2)}) %collective-permute-start.28) | collective-permute-done | bytes 131104 | tf_op jit(solution)/shard_map/ppermute | solution.py:458
  115.6 3.3 %collective-permute-done.17.refs_0_ = bf16[256,512]{1,0:T(8,128)(2,1)S(1)} collective-permute-done((bf16[256,512]{1,0:T(8,128)(2,1)S(1)}, bf16[256,512]{1,0:T(8,128)(2,1)S(1)}, u32[]{:S(2)}, u32[]{:S(2)}) %collective-permute-start.17) | collective-permute-done | bytes 262176 | tf_op jit(solution)/shard_map/ppermute | solution.py:458
  118.8 0.6 partial_keys.15
  120.0 1.2 collective-permute-start.34
  121.4 1.4 collective-permute-start.31
  122.7 3.2 %gradient.4.refs_8_ = f32[1536,512]{1,0:T(8,128)S(1)} custom-call(s32[2]{0:T(128)S(1)} %pad_add_fusion.place_ref, bf16[1536,256]{1,0:T(8,128)(2,1)S(1)} %get-tuple-element.94.refs_0_, bf16[1536,256]{1,0:T(8,128)(2,1)S(1)} %get-tuple-element.95.refs_1_, bf16[1536,256]{1,0:T(8,128)(2,1)S(1)} %get-tuple-element.96.refs_2_, ...), custom_call_target="tpu_custom_call" | custom-call | flops 1610612736 | bytes 6291456 | tf_op jit(solution)/shard_map/gradient/pallas_call | solution.py:236
  125.9 1.1 collective-permute-start.21
  127.0 3.6 %gradient.5 = (f32[1536,512]{1,0:T(8,128)S(1)}, f32[8,128]{1,0:T(8,128)S(1)}, f32[1536,128]{1,0:T(8,128)S(1)}) custom-call(s32[2]{0:T(128)S(1)} %pad_add_fusion.place_ref, bf16[1536,256]{1,0:T(8,128)(2,1)S(1)} %get-tuple-element.71.refs_0_, bf16[1536,256]{1,0:T(8,128)(2,1)S(1)} %get-tuple-element.72.refs_1_, ...), custom_call_target="tpu_custom_call" | custom-call | flops 1610612736 | bytes 6291456 | tf_op jit(solution)/shard_map/gradient/pallas_call | solution.py:236
  130.7 4.6 %collective-permute-done.31.refs_6_ = bf16[256,512]{1,0:T(8,128)(2,1)S(1)} collective-permute-done((bf16[256,512]{1,0:T(8,128)(2,1)S(1)}, bf16[256,512]{1,0:T(8,128)(2,1)S(1)}, u32[]{:S(2)}, u32[]{:S(2)}) %collective-permute-start.31) | collective-permute-done | bytes 262176 | tf_op jit(solution)/shard_map/ppermute | solution.py:458
  135.8 3.2 %gradient.6.refs_8_ = f32[1536,512]{1,0:T(8,128)S(1)} custom-call(s32[2]{0:T(128)S(1)} %pad_add_fusion.place_ref, bf16[1536,256]{1,0:T(8,128)(2,1)S(1)} %get-tuple-element.94.refs_0_, bf16[1536,256]{1,0:T(8,128)(2,1)S(1)} %get-tuple-element.95.refs_1_, bf16[1536,256]{1,0:T(8,128)(2,1)S(1)} %get-tuple-element.96.refs_2_, ...), custom_call_target="tpu_custom_call" | custom-call | flops 1610612736 | bytes 6291456 | tf_op jit(solution)/shard_map/gradient/pallas_call | solution.py:236
  139.0 3.6 %gradient.7 = (f32[1536,512]{1,0:T(8,128)S(1)}, f32[8,128]{1,0:T(8,128)S(1)}, f32[1536,128]{1,0:T(8,128)S(1)}) custom-call(s32[2]{0:T(128)S(1)} %pad_add_fusion.place_ref, bf16[1536,256]{1,0:T(8,128)(2,1)S(1)} %get-tuple-element.71.refs_0_, bf16[1536,256]{1,0:T(8,128)(2,1)S(1)} %get-tuple-element.72.refs_1_, ...), custom_call_target="tpu_custom_call" | custom-call | flops 1610612736 | bytes 6291456 | tf_op jit(solution)/shard_map/gradient/pallas_call | solution.py:236
  142.7 1.1 collective-permute-done.36
  143.9 1.1 collective-permute-start.39
  145.0 1.4 collective-permute-start.38
  146.4 1.0 collective-permute-start.37
  147.4 1.0 collective-permute-done.39.refs_3_
  148.6 1.4 collective-permute-done.37.refs_1_
  150.0 1.5 adam_frag.1
  151.5 1.3 collective-permute-start.40
  152.8 2.0 %collective-permute-start.41 = (bf16[384,128]{1,0:T(8,128)(2,1)S(1)}, bf16[384,128]{1,0:T(8,128)(2,1)S(1)}, u32[]{:S(2)}, u32[]{:S(2)}) collective-permute-start(bf16[384,128]{1,0:T(8,128)(2,1)S(1)} %get-tuple-element.113), channel_id=1, source_target_pairs={{0,16},{8,24},{16,0},{24,8},{1,17},{9,25},{17,1},{25,9},{2,18},{10... | collective-permute-start | bytes 294920 | tf_op jit(solution)/shard_map/ppermute | solution.py:458
  154.8 1.2 collective-permute-start.42
  156.0 6.0 %adam_rows.2 = (f32[1536,1024]{1,0:T(8,128)}, f32[1536,1024]{1,0:T(8,128)}, f32[1536,1024]{1,0:T(8,128)}, f32[8,128]{1,0:T(8,128)S(1)}) custom-call(f32[3]{0:T(128)S(1)} %pad_maximum_fusion.sc_ref, f32[1536,1024]{1,0:T(8,128)S(1)} %bitcast.42, f32[1536,1024]{1,0:T(8,128)S(1)} %bitcast.50, f32[1536,1024]{1,0:T(8,128)S(1)} %bitcast.58, ...), custom_call_target="tpu_custom_call" | custom-call | flops 15728640 | bytes 22020096 | tf_op jit(solution)/shard_map/adam_rows/pallas_call | solution.py:291
  162.1 2.7 %collective-permute-start.45 = (bf16[384,128]{1,0:T(8,128)(2,1)S(1)}, bf16[384,128]{1,0:T(8,128)(2,1)S(1)}, u32[]{:S(2)}, u32[]{:S(2)}) collective-permute-start(bf16[384,128]{1,0:T(8,128)(2,1)S(1)} %convert_element_type.24.refs_7_), channel_id=1, source_target_pairs={{0,24},{8,16},{16,8},{24,0},{1,25},{9,17},{17,9},{25,1},{2,26},{10... | collective-permute-start | bytes 294920 | tf_op jit(solution)/shard_map/ppermute | solution.py:458
  165.1 1.5 collective-permute-start.43
  166.6 6.0 %adam_rows.3 = (f32[1536,1024]{1,0:T(8,128)}, f32[1536,1024]{1,0:T(8,128)}, f32[1536,1024]{1,0:T(8,128)}) custom-call(f32[3]{0:T(128)S(1)} %pad_maximum_fusion.sc_ref, f32[1536,1024]{1,0:T(8,128)S(1)} %bitcast.43, f32[1536,1024]{1,0:T(8,128)S(1)} %bitcast.51, ...), custom_call_target="tpu_custom_call", output_to_operand_aliasing={{0}: (10, {}), {1}: (11, {}), {2}: (12, {})} | custom-call | flops 15728640 | bytes 22020096 | tf_op jit(solution)/shard_map/adam_rows/pallas_call | solution.py:291
  172.6 1.6 outer_step.1
  (91 shorter events, 7.3 us)
Async XLA Ops:
  3.2 17.0 %collective-permute-start.10 = (f32[384,128]{1,0:T(8,128)S(1)}, f32[384,128]{1,0:T(8,128)S(1)}, u32[]{:S(2)}, u32[]{:S(2)}) collective-permute-start(f32[384,128]{1,0:T(8,128)S(1)} %get-tuple-element.126), channel_id=1, source_target_pairs={{0,8},{8,0},{16,24},{24,16},{1,9},{9,1},{17,25},{25,17},{2,10},{10... | collective-permute-start | bytes 589832 | tf_op jit(solution)/shard_map/ppermute | solution.py:458
  6.3 15.5 %collective-permute-start.12 = (f32[384,128]{1,0:T(8,128)S(1)}, f32[384,128]{1,0:T(8,128)S(1)}, u32[]{:S(2)}, u32[]{:S(2)}) collective-permute-start(f32[384,128]{1,0:T(8,128)S(1)} %get-tuple-element.127), channel_id=1, source_target_pairs={{0,24},{8,16},{16,8},{24,0},{1,25},{9,17},{17,9},{25,1},{2,26},{10... | collective-permute-start | bytes 589832 | tf_op jit(solution)/shard_map/ppermute | solution.py:458
  8.8 17.4 %collective-permute-start.11 = (f32[384,128]{1,0:T(8,128)S(1)}, f32[384,128]{1,0:T(8,128)S(1)}, u32[]{:S(2)}, u32[]{:S(2)}) collective-permute-start(f32[384,128]{1,0:T(8,128)S(1)} %get-tuple-element.128), channel_id=1, source_target_pairs={{0,16},{8,24},{16,0},{24,8},{1,17},{9,25},{17,1},{25,9},{2,18},{10... | collective-permute-start | bytes 589832 | tf_op jit(solution)/shard_map/ppermute | solution.py:458
  11.5 37.8 %collective-permute-start.4 = (bf16[256,1536]{1,0:T(8,128)(2,1)}, bf16[256,1536]{1,0:T(8,128)(2,1)S(1)}, u32[]{:S(2)}, u32[]{:S(2)}) collective-permute-start(bf16[256,1536]{1,0:T(8,128)(2,1)} %get-tuple-element.68), channel_id=1, source_target_pairs={{0,7},{1,6},{2,5},{3,4},{4,3},{5,2},{6,1},{7,0},{8,15},{9,14},{10,... | collective-permute-start | bytes 2359304 | tf_op jit(solution)/shard_map/ppermute | solution.py:458
  15.2 29.1 %copy-start.4 = (bf16[256,1536]{1,0:T(8,128)(2,1)S(1)}, bf16[256,1536]{1,0:T(8,128)(2,1)}, u32[]{:S(2)}) copy-start(bf16[256,1536]{1,0:T(8,128)(2,1)} %get-tuple-element.73) | copy-start | bytes 2359300
  15.2 50.9 %collective-permute-start.8 = (bf16[256,1536]{1,0:T(8,128)(2,1)}, bf16[256,1536]{1,0:T(8,128)(2,1)S(1)}, u32[]{:S(2)}, u32[]{:S(2)}) collective-permute-start(bf16[256,1536]{1,0:T(8,128)(2,1)} %get-tuple-element.74), channel_id=1, source_target_pairs={{0,5},{1,4},{2,7},{3,6},{4,1},{5,0},{6,3},{7,2},{8,13},{9,12},{10,... | collective-permute-start | bytes 2359304 | tf_op jit(solution)/shard_map/ppermute | solution.py:458
  18.6 30.7 %copy-start.3 = (bf16[256,1536]{1,0:T(8,128)(2,1)S(1)}, bf16[256,1536]{1,0:T(8,128)(2,1)}, u32[]{:S(2)}) copy-start(bf16[256,1536]{1,0:T(8,128)(2,1)} %get-tuple-element.66) | copy-start | bytes 2359300
  20.2 51.8 %collective-permute-start.3 = (bf16[256,1536]{1,0:T(8,128)(2,1)}, bf16[256,1536]{1,0:T(8,128)(2,1)S(1)}, u32[]{:S(2)}, u32[]{:S(2)}) collective-permute-start(bf16[256,1536]{1,0:T(8,128)(2,1)} %pack.6), channel_id=1, source_target_pairs={{0,6},{1,7},{2,4},{3,5},{4,2},{5,3},{6,0},{7,1},{8,14},{9,15},{10,... | collective-permute-start | bytes 2359304 | tf_op jit(solution)/shard_map/ppermute | solution.py:458
  26.3 9.8 %collective-permute-start.15 = (f32[384,128]{1,0:T(8,128)S(1)}, f32[384,128]{1,0:T(8,128)S(1)}, u32[]{:S(2)}, u32[]{:S(2)}) collective-permute-start(f32[384,128]{1,0:T(8,128)S(1)} %get-tuple-element.124.refs_3_), channel_id=1, source_target_pairs={{0,24},{8,16},{16,8},{24,0},{1,25},{9,17},{17,9},{25,1},{2,26},{10... | collective-permute-start | bytes 589832 | tf_op jit(solution)/shard_map/ppermute | solution.py:458
  29.4 15.0 %collective-permute-start.14 = (f32[384,128]{1,0:T(8,128)S(1)}, f32[384,128]{1,0:T(8,128)S(1)}, u32[]{:S(2)}, u32[]{:S(2)}) collective-permute-start(f32[384,128]{1,0:T(8,128)S(1)} %get-tuple-element.124.refs_3_), channel_id=1, source_target_pairs={{0,16},{8,24},{16,0},{24,8},{1,17},{9,25},{17,1},{25,9},{2,18},{10... | collective-permute-start | bytes 589832 | tf_op jit(solution)/shard_map/ppermute | solution.py:458
  36.0 14.0 %collective-permute-start.13 = (f32[384,128]{1,0:T(8,128)S(1)}, f32[384,128]{1,0:T(8,128)S(1)}, u32[]{:S(2)}, u32[]{:S(2)}) collective-permute-start(f32[384,128]{1,0:T(8,128)S(1)} %get-tuple-element.124.refs_3_), channel_id=1, source_target_pairs={{0,8},{8,0},{16,24},{24,16},{1,9},{9,1},{17,25},{25,17},{2,10},{10... | collective-permute-start | bytes 589832 | tf_op jit(solution)/shard_map/ppermute | solution.py:458
  44.3 38.8 %collective-permute-start.7 = (bf16[256,1536]{1,0:T(8,128)(2,1)S(1)}, bf16[256,1536]{1,0:T(8,128)(2,1)S(1)}, u32[]{:S(2)}, u32[]{:S(2)}) collective-permute-start(bf16[256,1536]{1,0:T(8,128)(2,1)S(1)} %copy-done.4), channel_id=1, source_target_pairs={{0,4},{1,5},{2,6},{3,7},{4,0},{5,1},{6,2},{7,3},{8,12},{9,13},{10,... | collective-permute-start | bytes 2359304 | tf_op jit(solution)/shard_map/ppermute | solution.py:458
  49.3 48.7 %collective-permute-start.1 = (bf16[256,1536]{1,0:T(8,128)(2,1)S(1)}, bf16[256,1536]{1,0:T(8,128)(2,1)S(1)}, u32[]{:S(2)}, u32[]{:S(2)}) collective-permute-start(bf16[256,1536]{1,0:T(8,128)(2,1)S(1)} %copy-done.3), channel_id=1, source_target_pairs={{0,3},{1,2},{2,1},{3,0},{4,7},{5,6},{6,5},{7,4},{8,11},{9,10},{10,... | collective-permute-start | bytes 2359304 | tf_op jit(solution)/shard_map/ppermute | solution.py:458
  50.0 22.3 %collective-permute-start.5 = (bf16[256,512]{1,0:T(8,128)(2,1)S(1)}, bf16[256,512]{1,0:T(8,128)(2,1)S(1)}, u32[]{:S(2)}, u32[]{:S(2)}) collective-permute-start(bf16[256,512]{1,0:T(8,128)(2,1)S(1)} %get-tuple-element.69), channel_id=1, source_target_pairs={{0,1},{1,0},{2,3},{3,2},{4,5},{5,4},{6,7},{7,6},{8,9},{9,8},{10,11... | collective-permute-start | bytes 786440 | tf_op jit(solution)/shard_map/ppermute | solution.py:458
  66.2 38.0 %collective-permute-start.19 = (bf16[256,1536]{1,0:T(8,128)(2,1)}, bf16[256,1536]{1,0:T(8,128)(2,1)S(1)}, u32[]{:S(2)}, u32[]{:S(2)}) collective-permute-start(bf16[256,1536]{1,0:T(8,128)(2,1)} %get-tuple-element.90), channel_id=1, source_target_pairs={{0,1},{1,0},{2,3},{3,2},{4,5},{5,4},{6,7},{7,6},{8,9},{9,8},{10,11... | collective-permute-start | bytes 2359304 | tf_op jit(solution)/shard_map/ppermute | solution.py:458
  69.3 3.0 %copy-start.2 = (bf16[256,1536]{1,0:T(8,128)(2,1)S(1)}, bf16[256,1536]{1,0:T(8,128)(2,1)}, u32[]{:S(2)}) copy-start(bf16[256,1536]{1,0:T(8,128)(2,1)} %get-tuple-element.65) | copy-start | bytes 2359300
  71.5 3.6 %copy-start.1 = (bf16[1,256,1024]{2,1,0:T(8,128)(2,1)S(1)}, bf16[1,256,1024]{2,1,0:T(8,128)(2,1)}, u32[]{:S(2)}) copy-start(bf16[1,256,1024]{2,1,0:T(8,128)(2,1)} %param.10) | copy-start | bytes 1572868
  72.1 1.8 %collective-permute-start.9 = (bf16[256,512]{1,0:T(8,128)(2,1)S(1)}, bf16[256,512]{1,0:T(8,128)(2,1)S(1)}, u32[]{:S(2)}, u32[]{:S(2)}) collective-permute-start(bf16[256,512]{1,0:T(8,128)(2,1)S(1)} %get-tuple-element.80), channel_id=1, source_target_pairs={{0,1},{1,0},{2,3},{3,2},{4,5},{5,4},{6,7},{7,6},{8,9},{9,8},{10,11... | collective-permute-start | bytes 786440 | tf_op jit(solution)/shard_map/ppermute | solution.py:458
  72.4 33.7 %collective-permute-start = (bf16[256,1536]{1,0:T(8,128)(2,1)S(1)}, bf16[256,1536]{1,0:T(8,128)(2,1)S(1)}, u32[]{:S(2)}, u32[]{:S(2)}) collective-permute-start(bf16[256,1536]{1,0:T(8,128)(2,1)S(1)} %copy-done.2), channel_id=1, source_target_pairs={{0,2},{1,3},{2,0},{3,1},{4,6},{5,7},{6,4},{7,5},{8,10},{9,11},{10,... | collective-permute-start | bytes 2359304 | tf_op jit(solution)/shard_map/ppermute | solution.py:458
  73.9 21.0 %collective-permute-start.16 = (bf16[128,512]{1,0:T(8,128)(2,1)S(1)}, bf16[128,512]{1,0:T(8,128)(2,1)S(1)}, u32[]{:S(2)}, u32[]{:S(2)}) collective-permute-start(bf16[128,512]{1,0:T(8,128)(2,1)S(1)} %get-tuple-element.84), channel_id=1, source_target_pairs={{0,2},{1,3},{2,0},{3,1},{4,6},{5,7},{6,4},{7,5},{8,10},{9,11},{10,... | collective-permute-start | bytes 393224 | tf_op jit(solution)/shard_map/ppermute | solution.py:458
  95.5 7.8 %collective-permute-start.22 = (bf16[256,512]{1,0:T(8,128)(2,1)S(1)}, bf16[256,512]{1,0:T(8,128)(2,1)S(1)}, u32[]{:S(2)}, u32[]{:S(2)}) collective-permute-start(bf16[256,512]{1,0:T(8,128)(2,1)S(1)} %slice.32.refs_4_), channel_id=1, source_target_pairs={{0,2},{1,3},{2,0},{3,1},{4,6},{5,7},{6,4},{7,5},{8,10},{9,11},{10,... | collective-permute-start | bytes 786440 | tf_op jit(solution)/shard_map/ppermute | solution.py:458
  96.5 9.5 %collective-permute-start.24 = (bf16[256,512]{1,0:T(8,128)(2,1)S(1)}, bf16[256,512]{1,0:T(8,128)(2,1)S(1)}, u32[]{:S(2)}, u32[]{:S(2)}) collective-permute-start(bf16[256,512]{1,0:T(8,128)(2,1)S(1)} %slice.32.refs_4_), channel_id=1, source_target_pairs={{0,4},{1,5},{2,6},{3,7},{4,0},{5,1},{6,2},{7,3},{8,12},{9,13},{10,... | collective-permute-start | bytes 786440 | tf_op jit(solution)/shard_map/ppermute | solution.py:458
  98.6 20.3 %copy-start = (bf16[256,1536]{1,0:T(8,128)(2,1)S(1)}, bf16[256,1536]{1,0:T(8,128)(2,1)}, u32[]{:S(2)}) copy-start(bf16[256,1536]{1,0:T(8,128)(2,1)} %get-tuple-element.89.refs_0_.refs_1_.refs_2_.refs_3_) | copy-start | bytes 2359300
  98.6 8.1 %collective-permute-start.2 = (bf16[256,512]{1,0:T(8,128)(2,1)S(1)}, bf16[256,512]{1,0:T(8,128)(2,1)S(1)}, u32[]{:S(2)}, u32[]{:S(2)}) collective-permute-start(bf16[256,512]{1,0:T(8,128)(2,1)S(1)} %get-tuple-element.67), channel_id=1, source_target_pairs={{0,1},{1,0},{2,3},{3,2},{4,5},{5,4},{6,7},{7,6},{8,9},{9,8},{10,11... | collective-permute-start | bytes 786440 | tf_op jit(solution)/shard_map/ppermute | solution.py:458
  103.3 5.4 %collective-permute-start.6 = (bf16[128,512]{1,0:T(8,128)(2,1)S(1)}, bf16[128,512]{1,0:T(8,128)(2,1)S(1)}, u32[]{:S(2)}, u32[]{:S(2)}) collective-permute-start(bf16[128,512]{1,0:T(8,128)(2,1)S(1)} %get-tuple-element.70), channel_id=1, source_target_pairs={{0,4},{1,5},{2,6},{3,7},{4,0},{5,1},{6,2},{7,3},{8,12},{9,13},{10,... | collective-permute-start | bytes 393224 | tf_op jit(solution)/shard_map/ppermute | solution.py:458
  104.2 6.5 %collective-permute-start.27 = (bf16[128,512]{1,0:T(8,128)(2,1)S(1)}, bf16[128,512]{1,0:T(8,128)(2,1)S(1)}, u32[]{:S(2)}, u32[]{:S(2)}) collective-permute-start(bf16[128,512]{1,0:T(8,128)(2,1)S(1)} %slice.33), channel_id=1, source_target_pairs={{0,4},{1,5},{2,6},{3,7},{4,0},{5,1},{6,2},{7,3},{8,12},{9,13},{10,... | collective-permute-start | bytes 393224 | tf_op jit(solution)/shard_map/ppermute | solution.py:458
  106.0 9.1 %collective-permute-start.20 = (bf16[256,512]{1,0:T(8,128)(2,1)S(1)}, bf16[256,512]{1,0:T(8,128)(2,1)S(1)}, u32[]{:S(2)}, u32[]{:S(2)}) collective-permute-start(bf16[256,512]{1,0:T(8,128)(2,1)S(1)} %get-tuple-element.91), channel_id=1, source_target_pairs={{0,1},{1,0},{2,3},{3,2},{4,5},{5,4},{6,7},{7,6},{8,9},{9,8},{10,11... | collective-permute-start | bytes 786440 | tf_op jit(solution)/shard_map/ppermute | solution.py:458
  106.1 15.0 %collective-permute-start.26 = (bf16[256,512]{1,0:T(8,128)(2,1)S(1)}, bf16[256,512]{1,0:T(8,128)(2,1)S(1)}, u32[]{:S(2)}, u32[]{:S(2)}) collective-permute-start(bf16[256,512]{1,0:T(8,128)(2,1)S(1)} %slice.32.refs_4_), channel_id=1, source_target_pairs={{0,1},{1,0},{2,3},{3,2},{4,5},{5,4},{6,7},{7,6},{8,9},{9,8},{10,11... | collective-permute-start | bytes 786440 | tf_op jit(solution)/shard_map/ppermute | solution.py:458
  106.7 12.8 %collective-permute-start.18 = (bf16[256,512]{1,0:T(8,128)(2,1)S(1)}, bf16[256,512]{1,0:T(8,128)(2,1)S(1)}, u32[]{:S(2)}, u32[]{:S(2)}) collective-permute-start(bf16[256,512]{1,0:T(8,128)(2,1)S(1)} %get-tuple-element.88), channel_id=1, source_target_pairs={{0,4},{1,5},{2,6},{3,7},{4,0},{5,1},{6,2},{7,3},{8,12},{9,13},{10,... | collective-permute-start | bytes 786440 | tf_op jit(solution)/shard_map/ppermute | solution.py:458
  108.7 6.3 %collective-permute-start.28 = (bf16[128,512]{1,0:T(8,128)(2,1)S(1)}, bf16[128,512]{1,0:T(8,128)(2,1)S(1)}, u32[]{:S(2)}, u32[]{:S(2)}) collective-permute-start(bf16[128,512]{1,0:T(8,128)(2,1)S(1)} %slice.34), channel_id=1, source_target_pairs={{0,2},{1,3},{2,0},{3,1},{4,6},{5,7},{6,4},{7,5},{8,10},{9,11},{10,... | collective-permute-start | bytes 393224 | tf_op jit(solution)/shard_map/ppermute | solution.py:458
  110.8 8.1 %collective-permute-start.17 = (bf16[256,512]{1,0:T(8,128)(2,1)S(1)}, bf16[256,512]{1,0:T(8,128)(2,1)S(1)}, u32[]{:S(2)}, u32[]{:S(2)}) collective-permute-start(bf16[256,512]{1,0:T(8,128)(2,1)S(1)} %get-tuple-element.87), channel_id=1, source_target_pairs={{0,2},{1,3},{2,0},{3,1},{4,6},{5,7},{6,4},{7,5},{8,10},{9,11},{10,... | collective-permute-start | bytes 786440 | tf_op jit(solution)/shard_map/ppermute | solution.py:458
  115.0 6.4 %collective-permute-start.29 = (bf16[256,512]{1,0:T(8,128)(2,1)S(1)}, bf16[256,512]{1,0:T(8,128)(2,1)S(1)}, u32[]{:S(2)}, u32[]{:S(2)}) collective-permute-start(bf16[256,512]{1,0:T(8,128)(2,1)S(1)} %constant_dynamic-update-slice_fusion.refs_6_), channel_id=1, source_target_pairs={{0,1},{1,0},{2,3},{3,2},{4,5},{5,4},{6,7},{7,6},{8,9},{9,8},{10,11... | collective-permute-start | bytes 786440 | tf_op jit(solution)/shard_map/ppermute | solution.py:458
  115.1 10.9 %collective-permute-start.25 = (bf16[256,512]{1,0:T(8,128)(2,1)S(1)}, bf16[256,512]{1,0:T(8,128)(2,1)S(1)}, u32[]{:S(2)}, u32[]{:S(2)}) collective-permute-start(bf16[256,512]{1,0:T(8,128)(2,1)S(1)} %collective-permute-done.24.refs_6_), channel_id=1, source_target_pairs={{0,1},{1,0},{2,3},{3,2},{4,5},{5,4},{6,7},{7,6},{8,9},{9,8},{10,11... | collective-permute-start | bytes 786440 | tf_op jit(solution)/shard_map/ppermute | solution.py:458
  118.8 8.2 %collective-permute-start.23 = (bf16[256,512]{1,0:T(8,128)(2,1)S(1)}, bf16[256,512]{1,0:T(8,128)(2,1)S(1)}, u32[]{:S(2)}, u32[]{:S(2)}) collective-permute-start(bf16[256,512]{1,0:T(8,128)(2,1)S(1)} %collective-permute-done.22.refs_4_), channel_id=1, source_target_pairs={{0,1},{1,0},{2,3},{3,2},{4,5},{5,4},{6,7},{7,6},{8,9},{9,8},{10,11... | collective-permute-start | bytes 786440 | tf_op jit(solution)/shard_map/ppermute | solution.py:458
  118.8 37.1 %slice-start.4 = ((s8[6291456]{0:T(1024)(128)(4,1)}), s8[4194304]{0:T(1024)(128)(4,1)S(1)}, s32[]{:S(2)}) async-start(s8[6291456]{0:T(1024)(128)(4,1)} %bitcast.56), calls=%async_computation.4 | async-start | bytes 8388608
  120.0 10.6 %collective-permute-start.34 = (bf16[256,512]{1,0:T(8,128)(2,1)S(1)}, bf16[256,512]{1,0:T(8,128)(2,1)S(1)}, u32[]{:S(2)}, u32[]{:S(2)}) collective-permute-start(bf16[256,512]{1,0:T(8,128)(2,1)S(1)} %key_backward.1.refs_4_), channel_id=1, source_target_pairs={{0,6},{1,7},{2,4},{3,5},{4,2},{5,3},{6,0},{7,1},{8,14},{9,15},{10,... | collective-permute-start | bytes 786440 | tf_op jit(solution)/shard_map/ppermute | solution.py:458
  121.1 14.6 %collective-permute-start.33 = (bf16[256,512]{1,0:T(8,128)(2,1)S(1)}, bf16[256,512]{1,0:T(8,128)(2,1)S(1)}, u32[]{:S(2)}, u32[]{:S(2)}) collective-permute-start(bf16[256,512]{1,0:T(8,128)(2,1)S(1)} %key_backward.1.refs_4_), channel_id=1, source_target_pairs={{0,1},{1,0},{2,3},{3,2},{4,5},{5,4},{6,7},{7,6},{8,9},{9,8},{10,11... | collective-permute-start | bytes 786440 | tf_op jit(solution)/shard_map/ppermute | solution.py:458
  121.4 13.9 %collective-permute-start.31 = (bf16[256,512]{1,0:T(8,128)(2,1)S(1)}, bf16[256,512]{1,0:T(8,128)(2,1)S(1)}, u32[]{:S(2)}, u32[]{:S(2)}) collective-permute-start(bf16[256,512]{1,0:T(8,128)(2,1)S(1)} %key_backward.1.refs_4_), channel_id=1, source_target_pairs={{0,4},{1,5},{2,6},{3,7},{4,0},{5,1},{6,2},{7,3},{8,12},{9,13},{10,... | collective-permute-start | bytes 786440 | tf_op jit(solution)/shard_map/ppermute | solution.py:458
  125.9 9.3 %collective-permute-start.21 = (bf16[256,512]{1,0:T(8,128)(2,1)S(1)}, bf16[256,512]{1,0:T(8,128)(2,1)S(1)}, u32[]{:S(2)}, u32[]{:S(2)}) collective-permute-start(bf16[256,512]{1,0:T(8,128)(2,1)S(1)} %key_backward.1.refs_4_), channel_id=1, source_target_pairs={{0,2},{1,3},{2,0},{3,1},{4,6},{5,7},{6,4},{7,5},{8,10},{9,11},{10,... | collective-permute-start | bytes 786440 | tf_op jit(solution)/shard_map/ppermute | solution.py:458
  127.0 29.0 %slice-start.5 = ((s8[6291456]{0:T(1024)(128)(4,1)}), s8[2097152]{0:T(1024)(128)(4,1)S(1)}, s32[]{:S(2)}) async-start(s8[6291456]{0:T(1024)(128)(4,1)} %bitcast.56), calls=%async_computation.5 | async-start | bytes 4194304
  130.6 5.2 %collective-permute-start.35 = (bf16[256,512]{1,0:T(8,128)(2,1)S(1)}, bf16[256,512]{1,0:T(8,128)(2,1)S(1)}, u32[]{:S(2)}, u32[]{:S(2)}) collective-permute-start(bf16[256,512]{1,0:T(8,128)(2,1)S(1)} %collective-permute-done.34.refs_6_), channel_id=1, source_target_pairs={{0,1},{1,0},{2,3},{3,2},{4,5},{5,4},{6,7},{7,6},{8,9},{9,8},{10,11... | collective-permute-start | bytes 786440 | tf_op jit(solution)/shard_map/ppermute | solution.py:458
  135.3 3.7 %collective-permute-start.30 = (bf16[256,512]{1,0:T(8,128)(2,1)S(1)}, bf16[256,512]{1,0:T(8,128)(2,1)S(1)}, u32[]{:S(2)}, u32[]{:S(2)}) collective-permute-start(bf16[256,512]{1,0:T(8,128)(2,1)S(1)} %collective-permute-done.21.refs_4_), channel_id=1, source_target_pairs={{0,1},{1,0},{2,3},{3,2},{4,5},{5,4},{6,7},{7,6},{8,9},{9,8},{10,11... | collective-permute-start | bytes 786440 | tf_op jit(solution)/shard_map/ppermute | solution.py:458
  135.3 3.7 %collective-permute-start.32 = (bf16[256,512]{1,0:T(8,128)(2,1)S(1)}, bf16[256,512]{1,0:T(8,128)(2,1)S(1)}, u32[]{:S(2)}, u32[]{:S(2)}) collective-permute-start(bf16[256,512]{1,0:T(8,128)(2,1)S(1)} %collective-permute-done.31.refs_6_), channel_id=1, source_target_pairs={{0,1},{1,0},{2,3},{3,2},{4,5},{5,4},{6,7},{7,6},{8,9},{9,8},{10,11... | collective-permute-start | bytes 786440 | tf_op jit(solution)/shard_map/ppermute | solution.py:458
  135.8 20.2 %slice-start = ((s8[6291456]{0:T(1024)(128)(4,1)}), s8[4194304]{0:T(1024)(128)(4,1)S(1)}, s32[]{:S(2)}) async-start(s8[6291456]{0:T(1024)(128)(4,1)} %bitcast.40), calls=%async_computation | async-start | bytes 8388608
  135.8 20.2 %slice-start.2 = ((s8[6291456]{0:T(1024)(128)(4,1)}), s8[4194304]{0:T(1024)(128)(4,1)S(1)}, s32[]{:S(2)}) async-start(s8[6291456]{0:T(1024)(128)(4,1)} %bitcast.48), calls=%async_computation.2 | async-start | bytes 8388608
  139.0 17.0 %slice-start.1 = ((s8[6291456]{0:T(1024)(128)(4,1)}), s8[2097152]{0:T(1024)(128)(4,1)S(1)}, s32[]{:S(2)}) async-start(s8[6291456]{0:T(1024)(128)(4,1)} %bitcast.40), calls=%async_computation.1 | async-start | bytes 4194304
  139.0 17.0 %slice-start.3 = ((s8[6291456]{0:T(1024)(128)(4,1)}), s8[2097152]{0:T(1024)(128)(4,1)S(1)}, s32[]{:S(2)}) async-start(s8[6291456]{0:T(1024)(128)(4,1)} %bitcast.48), calls=%async_computation.3 | async-start | bytes 4194304
  142.6 1.2 collective-permute-start.36
  143.9 4.5 %collective-permute-start.39 = (f32[8,128]{1,0:T(8,128)S(1)}, f32[8,128]{1,0:T(8,128)S(1)}, u32[]{:S(2)}, u32[]{:S(2)}) collective-permute-start(f32[8,128]{1,0:T(8,128)S(1)} %add.32.refs_0_), channel_id=1, source_target_pairs={{0,6},{1,7},{2,4},{3,5},{4,2},{5,3},{6,0},{7,1},{8,14},{9,15},{10,... | collective-permute-start | bytes 12296 | tf_op jit(solution)/shard_map/ppermute | solution.py:458
  145.0 3.6 %collective-permute-start.38 = (f32[8,128]{1,0:T(8,128)S(1)}, f32[8,128]{1,0:T(8,128)S(1)}, u32[]{:S(2)}, u32[]{:S(2)}) collective-permute-start(f32[8,128]{1,0:T(8,128)S(1)} %add.32.refs_0_), channel_id=1, source_target_pairs={{0,4},{1,5},{2,6},{3,7},{4,0},{5,1},{6,2},{7,3},{8,12},{9,13},{10,... | collective-permute-start | bytes 12296 | tf_op jit(solution)/shard_map/ppermute | solution.py:458
  146.4 3.6 %collective-permute-start.37 = (f32[8,128]{1,0:T(8,128)S(1)}, f32[8,128]{1,0:T(8,128)S(1)}, u32[]{:S(2)}, u32[]{:S(2)}) collective-permute-start(f32[8,128]{1,0:T(8,128)S(1)} %add.32.refs_0_), channel_id=1, source_target_pairs={{0,2},{1,3},{2,0},{3,1},{4,6},{5,7},{6,4},{7,5},{8,10},{9,11},{10,... | collective-permute-start | bytes 12296 | tf_op jit(solution)/shard_map/ppermute | solution.py:458
  151.5 10.5 %collective-permute-start.40 = (bf16[384,128]{1,0:T(8,128)(2,1)S(1)}, bf16[384,128]{1,0:T(8,128)(2,1)S(1)}, u32[]{:S(2)}, u32[]{:S(2)}) collective-permute-start(bf16[384,128]{1,0:T(8,128)(2,1)S(1)} %get-tuple-element.112), channel_id=1, source_target_pairs={{0,8},{8,0},{16,24},{24,16},{1,9},{9,1},{17,25},{25,17},{2,10},{10... | collective-permute-start | bytes 294920 | tf_op jit(solution)/shard_map/ppermute | solution.py:458
  152.8 9.3 %collective-permute-start.41 = (bf16[384,128]{1,0:T(8,128)(2,1)S(1)}, bf16[384,128]{1,0:T(8,128)(2,1)S(1)}, u32[]{:S(2)}, u32[]{:S(2)}) collective-permute-start(bf16[384,128]{1,0:T(8,128)(2,1)S(1)} %get-tuple-element.113), channel_id=1, source_target_pairs={{0,16},{8,24},{16,0},{24,8},{1,17},{9,25},{17,1},{25,9},{2,18},{10... | collective-permute-start | bytes 294920 | tf_op jit(solution)/shard_map/ppermute | solution.py:458
  154.8 7.3 %collective-permute-start.42 = (bf16[384,128]{1,0:T(8,128)(2,1)S(1)}, bf16[384,128]{1,0:T(8,128)(2,1)S(1)}, u32[]{:S(2)}, u32[]{:S(2)}) collective-permute-start(bf16[384,128]{1,0:T(8,128)(2,1)S(1)} %get-tuple-element.114), channel_id=1, source_target_pairs={{0,24},{8,16},{16,8},{24,0},{1,25},{9,17},{17,9},{25,1},{2,26},{10... | collective-permute-start | bytes 294920 | tf_op jit(solution)/shard_map/ppermute | solution.py:458
  162.1 10.5 %collective-permute-start.45 = (bf16[384,128]{1,0:T(8,128)(2,1)S(1)}, bf16[384,128]{1,0:T(8,128)(2,1)S(1)}, u32[]{:S(2)}, u32[]{:S(2)}) collective-permute-start(bf16[384,128]{1,0:T(8,128)(2,1)S(1)} %convert_element_type.24.refs_7_), channel_id=1, source_target_pairs={{0,24},{8,16},{16,8},{24,0},{1,25},{9,17},{17,9},{25,1},{2,26},{10... | collective-permute-start | bytes 294920 | tf_op jit(solution)/shard_map/ppermute | solution.py:458
  164.8 7.8 %collective-permute-start.44 = (bf16[384,128]{1,0:T(8,128)(2,1)S(1)}, bf16[384,128]{1,0:T(8,128)(2,1)S(1)}, u32[]{:S(2)}, u32[]{:S(2)}) collective-permute-start(bf16[384,128]{1,0:T(8,128)(2,1)S(1)} %convert_element_type.24.refs_7_), channel_id=1, source_target_pairs={{0,16},{8,24},{16,0},{24,8},{1,17},{9,25},{17,1},{25,9},{2,18},{10... | collective-permute-start | bytes 294920 | tf_op jit(solution)/shard_map/ppermute | solution.py:458
  165.1 7.5 %collective-permute-start.43 = (bf16[384,128]{1,0:T(8,128)(2,1)S(1)}, bf16[384,128]{1,0:T(8,128)(2,1)S(1)}, u32[]{:S(2)}, u32[]{:S(2)}) collective-permute-start(bf16[384,128]{1,0:T(8,128)(2,1)S(1)} %convert_element_type.24.refs_7_), channel_id=1, source_target_pairs={{0,8},{8,0},{16,24},{24,16},{1,9},{9,1},{17,25},{25,17},{2,10},{10... | collective-permute-start | bytes 294920 | tf_op jit(solution)/shard_map/ppermute | solution.py:458

commit v21 on v18

--- a/solution.py
+++ b/solution.py
@@ -487,20 +487,34 @@
     order = [k for k in far[:-2] for k in (k, k + 1)]
     order += far[-2:] + [k + 1 for k in far[-2:]]
 
-    (old,) = due_columns(place, part, params)
-    old_sums = [old[0]] + [swap(old[k], "rep", k) for k in range(1, replicas)]
-
     packed = {}
     for offsets in (order[:1], order[1:4], order[4:], (0, 1)):
         packed |= pack(inputs, me, rows, tuple(offsets))
-    blocks = {k: swap(packed[k], "fsdp", k) for k in order}
+    blocks = {}
+    for i, k in enumerate(order[:-4]):
+        blocks[k] = swap(after(packed[k], *[blocks[j] for j in order[max(i - 2, 0):max(i - 1, 0)]]), "fsdp", k)
     blocks[0], blocks[1] = packed[0], swap(packed[1], "fsdp", 1)
+
+    (old,) = due_columns(place, part, params)
+    old_sums = [old[0]] + [swap(old[k], "rep", k) for k in range(1, replicas)]
+    anchor_cols, moment_cols = (c[0] for c in due_columns(place, part, anchor, momentum))
+    pseudo_old = anchor_cols - sum(old_sums[1:], old_sums[0]) / replicas
+    base = anchor_cols - OUTER_RATE * (OUTER_MU * (OUTER_MU * moment_cols + pseudo_old) + pseudo_old)
+    base = [base] + [swap(base, "rep", k) for k in range(1, replicas)]
+
+    for ready, i in (((pseudo_old,), len(order) - 4), (tuple(base), len(order) - 2)):
+        for k, before in zip(order[i:i + 2], order[i - 2:i]):
+            blocks[k] = swap(after(packed[k], blocks[before], *ready), "fsdp", k)
 
     relay = len(far) == 3 and far[0] == far[1] ^ far[2]
     half = inputs.shape[0] // 2
     values = {0: incoming[:, kv_width:]}
     for i, k in enumerate(far[1:] if relay else far):
         values[k] = swap(after(values[0], blocks[order[i]]), "fsdp", k)
+    if relay:
+        upper = swap(values[far[1]][:half], "fsdp", far[2])
+        lower = swap(values[far[2]][half:], "fsdp", far[1])
+        values[far[0]] = jnp.concatenate([upper, lower], axis=0)
 
     steps_now = step_count[0].astype(jnp.float32)
     plan = jnp.minimum(1.0, steps_now / WARMUP) * (
@@ -511,10 +525,6 @@
     inv_two = 1.0 / (1.0 - jnp.power(BETA_TWO, steps_now))
     scalars = jnp.stack([rate, inv_one, inv_two])
     old_first, old_second = due_columns(place, part, first_moment[0], second_moment[0])
-    anchor_cols, moment_cols = (c[0] for c in due_columns(place, part, anchor, momentum))
-    pseudo_old = anchor_cols - sum(old_sums[1:], old_sums[0]) / replicas
-    base = anchor_cols - OUTER_RATE * (OUTER_MU * (OUTER_MU * moment_cols + pseudo_old) + pseudo_old)
-    base = [base] + [swap(base, "rep", k) for k in range(1, replicas)]
     anchor_copy, momentum_copy = duplicate(anchor, momentum)
     key_weights = cast_left(params, kv_width)
 
@@ -524,8 +534,6 @@
     for k in far + [0]:
         theirs, flipped[k + 1] = partial_keys(blocks[k + 1], key_weights)
         theirs = swap(theirs, "fsdp", 1)
-        if k == last:
-            theirs = after(theirs, *base)
         adds = [(theirs, 0)] + relayed.get(k, [])
         if relay and k == far[0]:
             (upper, lower), flipped[k] = partial_keys(blocks[k], key_weights, adds, 2)
@@ -534,14 +542,8 @@
             continue
         part_k, flipped[k] = partial_keys(blocks[k], key_weights, adds)
         if k == last:
-            for j in [0] + [j for j in far if j in values]:
-                values[j] = after(values[j], part_k)
-            if relay:
-                upper = swap(values[far[1]][:half], "fsdp", far[2])
-                lower = swap(values[far[2]][half:], "fsdp", far[1])
-                values[far[0]] = jnp.concatenate([upper, lower], axis=0)
             for j in range(0, shards, 2):
-                values[j + 1] = swap(values[j], "fsdp", 1)
+                values[j + 1] = swap(after(values[j], part_k), "fsdp", 1)
         parts.append(swap(part_k, "fsdp", k) if k else part_k)
     spread = [0, 1] + [k + odd for k in far for odd in range(2)]
     near, rest = spread[:shards // 2], spread[shards // 2:]

time: 168 us -> 169 us (level)
  waiting for transfers between devices: 64.4 us -> 67.6 us
  starting transfers between devices: 43.8 us -> 41.6 us
    ppermute x46, waiting for transfers between devices: 64.4 us -> 67.6 us  [swap(): return lax.ppermute(block, axis, [(i, i ^ offset) for i in range(count)])]
    ppermute x46, starting transfers between devices: 43.8 us -> 41.6 us  [swap(): return lax.ppermute(block, axis, [(i, i ^ offset) for i in range(count)])]
  transfers between devices with their start and end apart: 46 -> 46, of which waited for: 17 -> 18; matrix products, arithmetic and copies ran while one was open for 0% -> 0% of each run, Pallas kernels for 28% -> 27%
where the time goes in v21:
time: 169 us; the launch traced here: 168 us
  waiting for transfers between devices  67.6 us (40%)
  Pallas kernels  54.8 us (32%)
  starting transfers between devices  41.6 us (25%)
  between operations  3.78 us (2%)
    ppermute x46, waiting for transfers between devices, swap(): return lax.ppermute(block, axis, [(i, i ^ offset) for i in range(count)])  67.6 us
    ppermute x46, starting transfers between devices, swap(): return lax.ppermute(block, axis, [(i, i ^ offset) for i in range(count)])  41.6 us
    pallas_call x4, Pallas kernels, gradient(): pl.pallas_call(functools.partial(grad_kernel, len(flipped), base is not N...  13.5 us
    pallas_call x2, Pallas kernels, adam_rows(): pl.pallas_call(functools.partial(adam_kernel, len(squares), len(into)), o...  12 us
    pallas_call x4, Pallas kernels, pack(): pl.pallas_call(functools.partial(pack_kernel, offsets), out_shape=[pltpu....  9.16 us
    pallas_call x3, Pallas kernels, due_columns(): pl.pallas_call(functools.partial(pick_kernel, blocks), out_shape=[jax.Sha...  5.55 us
    pallas_call x8, Pallas kernels, partial_keys(): pl.pallas_call(functools.partial(partial_kernel, pieces, [first for _, fi...  4.58 us
    pallas_call x1, Pallas kernels, cast_left(): pl.pallas_call(cast_kernel, out_shape=jax.ShapeDtypeStruct((rows, width),...  3.46 us
  transfers between devices with their start and end apart: 46, of which 18 were waited for; matrix products, arithmetic and copies ran while one was open for 0% of the time, Pallas kernels for 27%

profile of v21, /device:TPU:0, one launch (start us, length us, event | category | flops | bytes accessed | tf_op | source)
XLA Modules:
  0.0 168.2 jit_solution(19607934306304635)
XLA Ops:
  0.6 2.0 %pack.5 = bf16[256,1536]{1,0:T(8,128)(2,1)} custom-call(s32[1]{0:T(128)} %bitcast.4.me_ref, bf16[256,12288]{1,0:T(8,128)(2,1)} %bitcast.64), custom_call_target="tpu_custom_call" | custom-call | bytes 1572864 | tf_op jit(solution)/shard_map/pack/pallas_call | solution.py:69
  2.6 4.0 %collective-permute-start = (bf16[256,1536]{1,0:T(8,128)(2,1)}, bf16[256,1536]{1,0:T(8,128)(2,1)S(1)}, u32[]{:S(2)}, u32[]{:S(2)}) collective-permute-start(bf16[256,1536]{1,0:T(8,128)(2,1)} %pack.5), channel_id=1, source_target_pairs={{0,6},{1,7},{2,4},{3,5},{4,2},{5,3},{6,0},{7,1},{8,14},{9,15},{10,... | collective-permute-start | bytes 2359304 | tf_op jit(solution)/shard_map/ppermute | solution.py:458
  6.6 2.6 %pack.4 = (bf16[256,1536]{1,0:T(8,128)(2,1)}, bf16[256,1536]{1,0:T(8,128)(2,1)}, bf16[256,1536]{1,0:T(8,128)(2,1)}) custom-call(s32[1]{0:T(128)} %bitcast.4.me_ref, bf16[256,12288]{1,0:T(8,128)(2,1)} %bitcast.65), custom_call_target="tpu_custom_call" | custom-call | bytes 4718592 | tf_op jit(solution)/shard_map/pack/pallas_call | solution.py:69
  10.0 1.8 %due_columns.4.w_ref = f32[4,384,128]{2,1,0:T(8,128)S(1)} custom-call(s32[2]{0:T(128)S(1)} %pad_add_fusion.place_ref, f32[1536,1024]{1,0:T(8,128)} %bitcast.35, f32[1536,1024]{1,0:T(8,128)} %bitcast.36, f32[1536,1024]{1,0:T(8,128)} %bitcast.37, f32[1536,1024]{1,0:T(8,128)} %bitcast.38), custom_call_target="tpu_custom_call" | custom-call | bytes 1572864 | tf_op jit(solution)/shard_map/due_columns/pallas_call | solution.py:348
  11.9 1.6 collective-permute-start.1
  13.5 2.5 %collective-permute-start.3 = (f32[384,128]{1,0:T(8,128)S(1)}, f32[384,128]{1,0:T(8,128)S(1)}, u32[]{:S(2)}, u32[]{:S(2)}) collective-permute-start(f32[384,128]{1,0:T(8,128)S(1)} %get-tuple-element.143), channel_id=1, source_target_pairs={{0,24},{8,16},{16,8},{24,0},{1,25},{9,17},{17,9},{25,1},{2,26},{10... | collective-permute-start | bytes 589832 | tf_op jit(solution)/shard_map/ppermute | solution.py:458
  16.1 1.6 due_columns.3
  17.7 1.5 collective-permute-done.1
  19.2 6.8 %collective-permute-done.3 = f32[384,128]{1,0:T(8,128)S(1)} collective-permute-done((f32[384,128]{1,0:T(8,128)S(1)}, f32[384,128]{1,0:T(8,128)S(1)}, u32[]{:S(2)}, u32[]{:S(2)}) %collective-permute-start.3) | collective-permute-done | bytes 196640 | tf_op jit(solution)/shard_map/ppermute | solution.py:458
  26.0 8.1 %collective-permute-done.2 = f32[384,128]{1,0:T(8,128)S(1)} collective-permute-done((f32[384,128]{1,0:T(8,128)S(1)}, f32[384,128]{1,0:T(8,128)S(1)}, u32[]{:S(2)}, u32[]{:S(2)}) %collective-permute-start.2) | collective-permute-done | bytes 196640 | tf_op jit(solution)/shard_map/ppermute | solution.py:458
  34.2 1.6 collective-permute-start.4
  35.8 5.9 %collective-permute-done.10.refs_0_.refs_1_.refs_2_.refs_3_ = bf16[256,1536]{1,0:T(8,128)(2,1)S(1)} collective-permute-done((bf16[256,1536]{1,0:T(8,128)(2,1)}, bf16[256,1536]{1,0:T(8,128)(2,1)S(1)}, u32[]{:S(2)}, u32[]{:S(2)}) %collective-permute-start.10) | collective-permute-done | bytes 786464 | tf_op jit(solution)/shard_map/ppermute | solution.py:458
  42.2 3.6 %collective-permute-start.7 = (f32[384,128]{1,0:T(8,128)S(1)}, f32[384,128]{1,0:T(8,128)S(1)}, u32[]{:S(2)}, u32[]{:S(2)}) collective-permute-start(f32[384,128]{1,0:T(8,128)S(1)} %get-tuple-element.140.refs_3_), channel_id=1, source_target_pairs={{0,24},{8,16},{16,8},{24,0},{1,25},{9,17},{17,9},{25,1},{2,26},{10... | collective-permute-start | bytes 589832 | tf_op jit(solution)/shard_map/ppermute | solution.py:458
  45.8 0.8 collective-permute-start.5
  46.6 2.3 %pack.6 = (bf16[256,1536]{1,0:T(8,128)(2,1)}, bf16[256,1536]{1,0:T(8,128)(2,1)}) custom-call(s32[1]{0:T(128)} %bitcast.4.me_ref, bf16[256,12288]{1,0:T(8,128)(2,1)} %bitcast.66), custom_call_target="tpu_custom_call" | custom-call | bytes 3145728 | tf_op jit(solution)/shard_map/pack/pallas_call | solution.py:69
  48.9 2.7 %collective-permute-done.7.refs_6_ = f32[384,128]{1,0:T(8,128)S(1)} collective-permute-done((f32[384,128]{1,0:T(8,128)S(1)}, f32[384,128]{1,0:T(8,128)S(1)}, u32[]{:S(2)}, u32[]{:S(2)}) %collective-permute-start.7) | collective-permute-done | bytes 196640 | tf_op jit(solution)/shard_map/ppermute | solution.py:458
  51.6 11.7 %collective-permute-done.6.refs_5_ = f32[384,128]{1,0:T(8,128)S(1)} collective-permute-done((f32[384,128]{1,0:T(8,128)S(1)}, f32[384,128]{1,0:T(8,128)S(1)}, u32[]{:S(2)}, u32[]{:S(2)}) %collective-permute-start.6) | collective-permute-done | bytes 196640 | tf_op jit(solution)/shard_map/ppermute | solution.py:458
  63.3 0.8 collective-permute-start.8
  64.1 1.1 collective-permute-start.14
  65.2 2.3 %pack.7 = (bf16[256,1536]{1,0:T(8,128)(2,1)}, bf16[256,1536]{1,0:T(8,128)(2,1)}) custom-call(s32[1]{0:T(128)} %bitcast.4.me_ref, bf16[256,12288]{1,0:T(8,128)(2,1)} %bitcast.67), custom_call_target="tpu_custom_call" | custom-call | bytes 3145728 | tf_op jit(solution)/shard_map/pack/pallas_call | solution.py:69
  67.7 1.1 collective-permute-start.22
  68.8 3.5 %cast_left.1.refs_4_ = bf16[1536,512]{1,0:T(8,128)(2,1)S(1)} custom-call(f32[1536,1024]{1,0:T(8,128)} %bitcast.39), custom_call_target="tpu_custom_call" | custom-call | bytes 4718592 | tf_op jit(solution)/shard_map/cast_left/pallas_call | solution.py:93
  72.2 0.6 partial_keys.9
  73.1 2.8 %duplicate.1 = (f32[384,1024]{1,0:T(8,128)}, f32[384,1024]{1,0:T(8,128)}) custom-call(f32[384,1024]{1,0:T(8,128)} %refs_0_.3, f32[384,1024]{1,0:T(8,128)} %refs_1_.3), custom_call_target="tpu_custom_call" | custom-call | bytes 6291456 | tf_op jit(solution)/shard_map/duplicate/pallas_call | solution.py:389
  76.8 2.1 %due_columns.5 = (f32[4,384,128]{2,1,0:T(8,128)S(1)}, f32[4,384,128]{2,1,0:T(8,128)S(1)}) custom-call(s32[2]{0:T(128)S(1)} %pad_add_fusion.place_ref, f32[1536,1024]{1,0:T(8,128)} %bitcast.44, f32[1536,1024]{1,0:T(8,128)} %bitcast.45, f32[1536,1024]{1,0:T(8,128)} %bitcast.46, f32[1536,1024]{1,0:T(8,128)} %bitcast.47, f32[1536,1024]{1,0:T(8,128)} %bitcast.52, ...), custom_call_target="tpu_custom_call" | custom-call | bytes 3145728 | tf_op jit(solution)/shard_map/due_columns/pallas_call | solution.py:348
  78.9 10.1 %collective-permute-done.22.refs_4_ = bf16[256,512]{1,0:T(8,128)(2,1)S(1)} collective-permute-done((bf16[256,512]{1,0:T(8,128)(2,1)S(1)}, bf16[256,512]{1,0:T(8,128)(2,1)S(1)}, u32[]{:S(2)}, u32[]{:S(2)}) %collective-permute-start.22) | collective-permute-done | bytes 262176 | tf_op jit(solution)/shard_map/ppermute | solution.py:458
  89.0 0.7 collective-permute-start.24
  89.8 1.4 collective-permute-start.27
  91.8 0.6 partial_keys.12
  93.6 0.8 collective-permute-start.12
  94.9 3.2 %collective-permute-done.24.refs_6_ = bf16[256,512]{1,0:T(8,128)(2,1)S(1)} collective-permute-done((bf16[256,512]{1,0:T(8,128)(2,1)S(1)}, bf16[256,512]{1,0:T(8,128)(2,1)S(1)}, u32[]{:S(2)}, u32[]{:S(2)}) %collective-permute-start.24) | collective-permute-done | bytes 262176 | tf_op jit(solution)/shard_map/ppermute | solution.py:458
  98.2 0.6 collective-permute-start.28
  98.8 2.2 %collective-permute-done.27 = bf16[128,512]{1,0:T(8,128)(2,1)S(1)} collective-permute-done((bf16[128,512]{1,0:T(8,128)(2,1)S(1)}, bf16[128,512]{1,0:T(8,128)(2,1)S(1)}, u32[]{:S(2)}, u32[]{:S(2)}) %collective-permute-start.27) | collective-permute-done | bytes 131104 | tf_op jit(solution)/shard_map/ppermute | solution.py:458
  101.5 1.0 collective-permute-done.12.refs_6_
  102.6 0.6 partial_keys.11
  103.2 0.6 collective-permute-start.17
  103.8 2.2 %collective-permute-done.16.refs_6_ = bf16[128,512]{1,0:T(8,128)(2,1)S(1)} collective-permute-done((bf16[128,512]{1,0:T(8,128)(2,1)S(1)}, bf16[128,512]{1,0:T(8,128)(2,1)S(1)}, u32[]{:S(2)}, u32[]{:S(2)}) %collective-permute-start.16) | collective-permute-done | bytes 131104 | tf_op jit(solution)/shard_map/ppermute | solution.py:458
  106.0 0.6 partial_keys.13
  106.5 0.8 collective-permute-start.18
  108.0 3.9 %collective-permute-done.17.refs_0_ = bf16[256,512]{1,0:T(8,128)(2,1)S(1)} collective-permute-done((bf16[256,512]{1,0:T(8,128)(2,1)S(1)}, bf16[256,512]{1,0:T(8,128)(2,1)S(1)}, u32[]{:S(2)}, u32[]{:S(2)}) %collective-permute-start.17) | collective-permute-done | bytes 262176 | tf_op jit(solution)/shard_map/ppermute | solution.py:458
  112.0 0.6 partial_keys.15
  113.5 1.9 %collective-permute-start.34 = (bf16[256,512]{1,0:T(8,128)(2,1)S(1)}, bf16[256,512]{1,0:T(8,128)(2,1)S(1)}, u32[]{:S(2)}, u32[]{:S(2)}) collective-permute-start(bf16[256,512]{1,0:T(8,128)(2,1)S(1)} %key_backward.1.refs_4_), channel_id=1, source_target_pairs={{0,6},{1,7},{2,4},{3,5},{4,2},{5,3},{6,0},{7,1},{8,14},{9,15},{10,... | collective-permute-start | bytes 786440 | tf_op jit(solution)/shard_map/ppermute | solution.py:458
  115.4 1.1 collective-permute-start.31
  116.5 3.2 %gradient.4.refs_8_ = f32[1536,512]{1,0:T(8,128)S(1)} custom-call(s32[2]{0:T(128)S(1)} %pad_add_fusion.place_ref, bf16[1536,256]{1,0:T(8,128)(2,1)S(1)} %get-tuple-element.108.refs_0_, bf16[1536,256]{1,0:T(8,128)(2,1)S(1)} %get-tuple-element.109.refs_1_, bf16[1536,256]{1,0:T(8,128)(2,1)S(1)} %get-tuple-element.110.refs_2_, ...), custom_call_target="tpu_custom_call" | custom-call | flops 1610612736 | bytes 6291456 | tf_op jit(solution)/shard_map/gradient/pallas_call | solution.py:236
  119.7 0.7 collective-permute-start.21
  120.4 3.6 %gradient.5 = (f32[1536,512]{1,0:T(8,128)S(1)}, f32[8,128]{1,0:T(8,128)S(1)}, f32[1536,128]{1,0:T(8,128)S(1)}) custom-call(s32[2]{0:T(128)S(1)} %pad_add_fusion.place_ref, bf16[1536,256]{1,0:T(8,128)(2,1)S(1)} %get-tuple-element.83.refs_0_, bf16[1536,256]{1,0:T(8,128)(2,1)S(1)} %get-tuple-element.84.refs_1_, ...), custom_call_target="tpu_custom_call" | custom-call | flops 1610612736 | bytes 6291456 | tf_op jit(solution)/shard_map/gradient/pallas_call | solution.py:236
  124.1 4.3 %collective-permute-done.31.refs_6_ = bf16[256,512]{1,0:T(8,128)(2,1)S(1)} collective-permute-done((bf16[256,512]{1,0:T(8,128)(2,1)S(1)}, bf16[256,512]{1,0:T(8,128)(2,1)S(1)}, u32[]{:S(2)}, u32[]{:S(2)}) %collective-permute-start.31) | collective-permute-done | bytes 262176 | tf_op jit(solution)/shard_map/ppermute | solution.py:458
  128.9 3.2 %gradient.6.refs_8_ = f32[1536,512]{1,0:T(8,128)S(1)} custom-call(s32[2]{0:T(128)S(1)} %pad_add_fusion.place_ref, bf16[1536,256]{1,0:T(8,128)(2,1)S(1)} %get-tuple-element.108.refs_0_, bf16[1536,256]{1,0:T(8,128)(2,1)S(1)} %get-tuple-element.109.refs_1_, bf16[1536,256]{1,0:T(8,128)(2,1)S(1)} %get-tuple-element.110.refs_2_, ...), custom_call_target="tpu_custom_call" | custom-call | flops 1610612736 | bytes 6291456 | tf_op jit(solution)/shard_map/gradient/pallas_call | solution.py:236
  132.2 3.6 %gradient.7 = (f32[1536,512]{1,0:T(8,128)S(1)}, f32[8,128]{1,0:T(8,128)S(1)}, f32[1536,128]{1,0:T(8,128)S(1)}) custom-call(s32[2]{0:T(128)S(1)} %pad_add_fusion.place_ref, bf16[1536,256]{1,0:T(8,128)(2,1)S(1)} %get-tuple-element.83.refs_0_, bf16[1536,256]{1,0:T(8,128)(2,1)S(1)} %get-tuple-element.84.refs_1_, ...), custom_call_target="tpu_custom_call" | custom-call | flops 1610612736 | bytes 6291456 | tf_op jit(solution)/shard_map/gradient/pallas_call | solution.py:236
  135.9 1.1 collective-permute-done.36
  137.0 1.6 collective-permute-start.39
  138.6 0.6 collective-permute-start.38
  139.2 1.3 collective-permute-start.37
  140.5 1.0 collective-permute-done.39.refs_3_
  141.5 0.7 collective-permute-done.38.refs_2_
  142.2 0.6 collective-permute-done.37.refs_1_
  142.8 1.5 adam_frag.1
  144.4 3.0 %collective-permute-start.41 = (bf16[384,128]{1,0:T(8,128)(2,1)S(1)}, bf16[384,128]{1,0:T(8,128)(2,1)S(1)}, u32[]{:S(2)}, u32[]{:S(2)}) collective-permute-start(bf16[384,128]{1,0:T(8,128)(2,1)S(1)} %get-tuple-element.129), channel_id=1, source_target_pairs={{0,16},{8,24},{16,0},{24,8},{1,17},{9,25},{17,1},{25,9},{2,18},{10... | collective-permute-start | bytes 294920 | tf_op jit(solution)/shard_map/ppermute | solution.py:458
  147.5 1.3 collective-permute-start.42
  148.9 6.0 %adam_rows.2 = (f32[1536,1024]{1,0:T(8,128)}, f32[1536,1024]{1,0:T(8,128)}, f32[1536,1024]{1,0:T(8,128)}, f32[8,128]{1,0:T(8,128)S(1)}) custom-call(f32[3]{0:T(128)S(1)} %pad_maximum_fusion.sc_ref, f32[1536,1024]{1,0:T(8,128)S(1)} %bitcast.42, f32[1536,1024]{1,0:T(8,128)S(1)} %bitcast.50, f32[1536,1024]{1,0:T(8,128)S(1)} %bitcast.58, ...), custom_call_target="tpu_custom_call" | custom-call | flops 15728640 | bytes 22020096 | tf_op jit(solution)/shard_map/adam_rows/pallas_call | solution.py:291
  155.0 2.5 %collective-permute-start.45 = (bf16[384,128]{1,0:T(8,128)(2,1)S(1)}, bf16[384,128]{1,0:T(8,128)(2,1)S(1)}, u32[]{:S(2)}, u32[]{:S(2)}) collective-permute-start(bf16[384,128]{1,0:T(8,128)(2,1)S(1)} %convert_element_type.24.refs_7_), channel_id=1, source_target_pairs={{0,24},{8,16},{16,8},{24,0},{1,25},{9,17},{17,9},{25,1},{2,26},{10... | collective-permute-start | bytes 294920 | tf_op jit(solution)/shard_map/ppermute | solution.py:458
  157.5 1.9 %collective-permute-start.43 = (bf16[384,128]{1,0:T(8,128)(2,1)S(1)}, bf16[384,128]{1,0:T(8,128)(2,1)S(1)}, u32[]{:S(2)}, u32[]{:S(2)}) collective-permute-start(bf16[384,128]{1,0:T(8,128)(2,1)S(1)} %convert_element_type.24.refs_7_), channel_id=1, source_target_pairs={{0,8},{8,0},{16,24},{24,16},{1,9},{9,1},{17,25},{25,17},{2,10},{10... | collective-permute-start | bytes 294920 | tf_op jit(solution)/shard_map/ppermute | solution.py:458
  159.4 6.0 %adam_rows.3 = (f32[1536,1024]{1,0:T(8,128)}, f32[1536,1024]{1,0:T(8,128)}, f32[1536,1024]{1,0:T(8,128)}) custom-call(f32[3]{0:T(128)S(1)} %pad_maximum_fusion.sc_ref, f32[1536,1024]{1,0:T(8,128)S(1)} %bitcast.43, f32[1536,1024]{1,0:T(8,128)S(1)} %bitcast.51, ...), custom_call_target="tpu_custom_call", output_to_operand_aliasing={{0}: (10, {}), {1}: (11, {}), {2}: (12, {})} | custom-call | flops 15728640 | bytes 22020096 | tf_op jit(solution)/shard_map/adam_rows/pallas_call | solution.py:291
  165.5 1.7 outer_step.1
  (89 shorter events, 6.9 us)
Async XLA Ops:
  2.6 31.6 %collective-permute-start = (bf16[256,1536]{1,0:T(8,128)(2,1)}, bf16[256,1536]{1,0:T(8,128)(2,1)S(1)}, u32[]{:S(2)}, u32[]{:S(2)}) collective-permute-start(bf16[256,1536]{1,0:T(8,128)(2,1)} %pack.5), channel_id=1, source_target_pairs={{0,6},{1,7},{2,4},{3,5},{4,2},{5,3},{6,0},{7,1},{8,14},{9,15},{10,... | collective-permute-start | bytes 2359304 | tf_op jit(solution)/shard_map/ppermute | solution.py:458
  9.2 32.5 %collective-permute-start.10 = (bf16[256,1536]{1,0:T(8,128)(2,1)}, bf16[256,1536]{1,0:T(8,128)(2,1)S(1)}, u32[]{:S(2)}, u32[]{:S(2)}) collective-permute-start(bf16[256,1536]{1,0:T(8,128)(2,1)} %get-tuple-element.80), channel_id=1, source_target_pairs={{0,7},{1,6},{2,5},{3,4},{4,3},{5,2},{6,1},{7,0},{8,15},{9,14},{10,... | collective-permute-start | bytes 2359304 | tf_op jit(solution)/shard_map/ppermute | solution.py:458
  10.0 24.2 %copy-start.3 = (bf16[256,1536]{1,0:T(8,128)(2,1)S(1)}, bf16[256,1536]{1,0:T(8,128)(2,1)}, u32[]{:S(2)}) copy-start(bf16[256,1536]{1,0:T(8,128)(2,1)} %get-tuple-element.75) | copy-start | bytes 2359300
  10.0 31.7 %copy-start.2 = (bf16[256,1536]{1,0:T(8,128)(2,1)S(1)}, bf16[256,1536]{1,0:T(8,128)(2,1)}, u32[]{:S(2)}) copy-start(bf16[256,1536]{1,0:T(8,128)(2,1)} %get-tuple-element.86) | copy-start | bytes 2359300
  11.9 7.3 %collective-permute-start.1 = (f32[384,128]{1,0:T(8,128)S(1)}, f32[384,128]{1,0:T(8,128)S(1)}, u32[]{:S(2)}, u32[]{:S(2)}) collective-permute-start(f32[384,128]{1,0:T(8,128)S(1)} %get-tuple-element.142), channel_id=1, source_target_pairs={{0,8},{8,0},{16,24},{24,16},{1,9},{9,1},{17,25},{25,17},{2,10},{10... | collective-permute-start | bytes 589832 | tf_op jit(solution)/shard_map/ppermute | solution.py:458
  13.5 12.4 %collective-permute-start.3 = (f32[384,128]{1,0:T(8,128)S(1)}, f32[384,128]{1,0:T(8,128)S(1)}, u32[]{:S(2)}, u32[]{:S(2)}) collective-permute-start(f32[384,128]{1,0:T(8,128)S(1)} %get-tuple-element.143), channel_id=1, source_target_pairs={{0,24},{8,16},{16,8},{24,0},{1,25},{9,17},{17,9},{25,1},{2,26},{10... | collective-permute-start | bytes 589832 | tf_op jit(solution)/shard_map/ppermute | solution.py:458
  16.0 18.1 %collective-permute-start.2 = (f32[384,128]{1,0:T(8,128)S(1)}, f32[384,128]{1,0:T(8,128)S(1)}, u32[]{:S(2)}, u32[]{:S(2)}) collective-permute-start(f32[384,128]{1,0:T(8,128)S(1)} %get-tuple-element.144), channel_id=1, source_target_pairs={{0,16},{8,24},{16,0},{24,8},{1,17},{9,25},{17,1},{25,9},{2,18},{10... | collective-permute-start | bytes 589832 | tf_op jit(solution)/shard_map/ppermute | solution.py:458
  34.2 29.1 %collective-permute-start.4 = (bf16[256,1536]{1,0:T(8,128)(2,1)S(1)}, bf16[256,1536]{1,0:T(8,128)(2,1)S(1)}, u32[]{:S(2)}, u32[]{:S(2)}) collective-permute-start(bf16[256,1536]{1,0:T(8,128)(2,1)S(1)} %copy-done.3), channel_id=1, source_target_pairs={{0,2},{1,3},{2,0},{3,1},{4,6},{5,7},{6,4},{7,5},{8,10},{9,11},{10,... | collective-permute-start | bytes 2359304 | tf_op jit(solution)/shard_map/ppermute | solution.py:458
  41.7 22.4 %collective-permute-start.13 = (bf16[256,1536]{1,0:T(8,128)(2,1)S(1)}, bf16[256,1536]{1,0:T(8,128)(2,1)S(1)}, u32[]{:S(2)}, u32[]{:S(2)}) collective-permute-start(bf16[256,1536]{1,0:T(8,128)(2,1)S(1)} %copy-done.2), channel_id=1, source_target_pairs={{0,4},{1,5},{2,6},{3,7},{4,0},{5,1},{6,2},{7,3},{8,12},{9,13},{10,... | collective-permute-start | bytes 2359304 | tf_op jit(solution)/shard_map/ppermute | solution.py:458
  42.2 25.4 %copy-start.1 = (bf16[1,256,1024]{2,1,0:T(8,128)(2,1)S(1)}, bf16[1,256,1024]{2,1,0:T(8,128)(2,1)}, u32[]{:S(2)}) copy-start(bf16[1,256,1024]{2,1,0:T(8,128)(2,1)} %param.10) | copy-start | bytes 1572868
  42.2 9.4 %collective-permute-start.7 = (f32[384,128]{1,0:T(8,128)S(1)}, f32[384,128]{1,0:T(8,128)S(1)}, u32[]{:S(2)}, u32[]{:S(2)}) collective-permute-start(f32[384,128]{1,0:T(8,128)S(1)} %get-tuple-element.140.refs_3_), channel_id=1, source_target_pairs={{0,24},{8,16},{16,8},{24,0},{1,25},{9,17},{17,9},{25,1},{2,26},{10... | collective-permute-start | bytes 589832 | tf_op jit(solution)/shard_map/ppermute | solution.py:458
  45.8 17.5 %collective-permute-start.6 = (f32[384,128]{1,0:T(8,128)S(1)}, f32[384,128]{1,0:T(8,128)S(1)}, u32[]{:S(2)}, u32[]{:S(2)}) collective-permute-start(f32[384,128]{1,0:T(8,128)S(1)} %get-tuple-element.140.refs_3_), channel_id=1, source_target_pairs={{0,16},{8,24},{16,0},{24,8},{1,17},{9,25},{17,1},{25,9},{2,18},{10... | collective-permute-start | bytes 589832 | tf_op jit(solution)/shard_map/ppermute | solution.py:458
  45.8 17.5 %collective-permute-start.5 = (f32[384,128]{1,0:T(8,128)S(1)}, f32[384,128]{1,0:T(8,128)S(1)}, u32[]{:S(2)}, u32[]{:S(2)}) collective-permute-start(f32[384,128]{1,0:T(8,128)S(1)} %get-tuple-element.140.refs_3_), channel_id=1, source_target_pairs={{0,8},{8,0},{16,24},{24,16},{1,9},{9,1},{17,25},{25,17},{2,10},{10... | collective-permute-start | bytes 589832 | tf_op jit(solution)/shard_map/ppermute | solution.py:458
  63.3 26.5 %collective-permute-start.8 = (bf16[256,1536]{1,0:T(8,128)(2,1)}, bf16[256,1536]{1,0:T(8,128)(2,1)S(1)}, u32[]{:S(2)}, u32[]{:S(2)}) collective-permute-start(bf16[256,1536]{1,0:T(8,128)(2,1)} %get-tuple-element.78), channel_id=1, source_target_pairs={{0,3},{1,2},{2,1},{3,0},{4,7},{5,6},{6,5},{7,4},{8,11},{9,10},{10,... | collective-permute-start | bytes 2359304 | tf_op jit(solution)/shard_map/ppermute | solution.py:458
  64.1 27.6 %collective-permute-start.14 = (bf16[256,1536]{1,0:T(8,128)(2,1)}, bf16[256,1536]{1,0:T(8,128)(2,1)S(1)}, u32[]{:S(2)}, u32[]{:S(2)}) collective-permute-start(bf16[256,1536]{1,0:T(8,128)(2,1)} %get-tuple-element.88), channel_id=1, source_target_pairs={{0,5},{1,4},{2,7},{3,6},{4,1},{5,0},{6,3},{7,2},{8,13},{9,12},{10,... | collective-permute-start | bytes 2359304 | tf_op jit(solution)/shard_map/ppermute | solution.py:458
  67.5 26.1 %collective-permute-start.19 = (bf16[256,1536]{1,0:T(8,128)(2,1)}, bf16[256,1536]{1,0:T(8,128)(2,1)S(1)}, u32[]{:S(2)}, u32[]{:S(2)}) collective-permute-start(bf16[256,1536]{1,0:T(8,128)(2,1)} %get-tuple-element.101), channel_id=1, source_target_pairs={{0,1},{1,0},{2,3},{3,2},{4,5},{5,4},{6,7},{7,6},{8,9},{9,8},{10,11... | collective-permute-start | bytes 2359304 | tf_op jit(solution)/shard_map/ppermute | solution.py:458
  67.7 21.3 %collective-permute-start.22 = (bf16[256,512]{1,0:T(8,128)(2,1)S(1)}, bf16[256,512]{1,0:T(8,128)(2,1)S(1)}, u32[]{:S(2)}, u32[]{:S(2)}) collective-permute-start(bf16[256,512]{1,0:T(8,128)(2,1)S(1)} %slice.32.refs_4_), channel_id=1, source_target_pairs={{0,2},{1,3},{2,0},{3,1},{4,6},{5,7},{6,4},{7,5},{8,10},{9,11},{10,... | collective-permute-start | bytes 786440 | tf_op jit(solution)/shard_map/ppermute | solution.py:458
  72.8 19.6 %collective-permute-start.11 = (bf16[256,512]{1,0:T(8,128)(2,1)S(1)}, bf16[256,512]{1,0:T(8,128)(2,1)S(1)}, u32[]{:S(2)}, u32[]{:S(2)}) collective-permute-start(bf16[256,512]{1,0:T(8,128)(2,1)S(1)} %get-tuple-element.81), channel_id=1, source_target_pairs={{0,1},{1,0},{2,3},{3,2},{4,5},{5,4},{6,7},{7,6},{8,9},{9,8},{10,11... | collective-permute-start | bytes 786440 | tf_op jit(solution)/shard_map/ppermute | solution.py:458
  89.0 9.2 %collective-permute-start.24 = (bf16[256,512]{1,0:T(8,128)(2,1)S(1)}, bf16[256,512]{1,0:T(8,128)(2,1)S(1)}, u32[]{:S(2)}, u32[]{:S(2)}) collective-permute-start(bf16[256,512]{1,0:T(8,128)(2,1)S(1)} %slice.32.refs_4_), channel_id=1, source_target_pairs={{0,4},{1,5},{2,6},{3,7},{4,0},{5,1},{6,2},{7,3},{8,12},{9,13},{10,... | collective-permute-start | bytes 786440 | tf_op jit(solution)/shard_map/ppermute | solution.py:458
  89.8 11.2 %collective-permute-start.27 = (bf16[128,512]{1,0:T(8,128)(2,1)S(1)}, bf16[128,512]{1,0:T(8,128)(2,1)S(1)}, u32[]{:S(2)}, u32[]{:S(2)}) collective-permute-start(bf16[128,512]{1,0:T(8,128)(2,1)S(1)} %slice.33), channel_id=1, source_target_pairs={{0,4},{1,5},{2,6},{3,7},{4,0},{5,1},{6,2},{7,3},{8,12},{9,13},{10,... | collective-permute-start | bytes 393224 | tf_op jit(solution)/shard_map/ppermute | solution.py:458
  91.7 10.8 %collective-permute-start.9 = (bf16[256,512]{1,0:T(8,128)(2,1)S(1)}, bf16[256,512]{1,0:T(8,128)(2,1)S(1)}, u32[]{:S(2)}, u32[]{:S(2)}) collective-permute-start(bf16[256,512]{1,0:T(8,128)(2,1)S(1)} %get-tuple-element.79), channel_id=1, source_target_pairs={{0,1},{1,0},{2,3},{3,2},{4,5},{5,4},{6,7},{7,6},{8,9},{9,8},{10,11... | collective-permute-start | bytes 786440 | tf_op jit(solution)/shard_map/ppermute | solution.py:458
  92.4 13.5 %collective-permute-start.15 = (bf16[256,512]{1,0:T(8,128)(2,1)S(1)}, bf16[256,512]{1,0:T(8,128)(2,1)S(1)}, u32[]{:S(2)}, u32[]{:S(2)}) collective-permute-start(bf16[256,512]{1,0:T(8,128)(2,1)S(1)} %get-tuple-element.94), channel_id=1, source_target_pairs={{0,1},{1,0},{2,3},{3,2},{4,5},{5,4},{6,7},{7,6},{8,9},{9,8},{10,11... | collective-permute-start | bytes 786440 | tf_op jit(solution)/shard_map/ppermute | solution.py:458
  93.6 9.0 %collective-permute-start.12 = (bf16[128,512]{1,0:T(8,128)(2,1)S(1)}, bf16[128,512]{1,0:T(8,128)(2,1)S(1)}, u32[]{:S(2)}, u32[]{:S(2)}) collective-permute-start(bf16[128,512]{1,0:T(8,128)(2,1)S(1)} %get-tuple-element.82), channel_id=1, source_target_pairs={{0,4},{1,5},{2,6},{3,7},{4,0},{5,1},{6,2},{7,3},{8,12},{9,13},{10,... | collective-permute-start | bytes 393224 | tf_op jit(solution)/shard_map/ppermute | solution.py:458
  94.9 17.1 %copy-start = (bf16[256,1536]{1,0:T(8,128)(2,1)S(1)}, bf16[256,1536]{1,0:T(8,128)(2,1)}, u32[]{:S(2)}) copy-start(bf16[256,1536]{1,0:T(8,128)(2,1)} %get-tuple-element.100.refs_0_.refs_1_.refs_2_.refs_3_) | copy-start | bytes 2359300
  98.2 9.2 %collective-permute-start.28 = (bf16[128,512]{1,0:T(8,128)(2,1)S(1)}, bf16[128,512]{1,0:T(8,128)(2,1)S(1)}, u32[]{:S(2)}, u32[]{:S(2)}) collective-permute-start(bf16[128,512]{1,0:T(8,128)(2,1)S(1)} %slice.34), channel_id=1, source_target_pairs={{0,2},{1,3},{2,0},{3,1},{4,6},{5,7},{6,4},{7,5},{8,10},{9,11},{10,... | collective-permute-start | bytes 393224 | tf_op jit(solution)/shard_map/ppermute | solution.py:458
  101.0 5.0 %collective-permute-start.16 = (bf16[128,512]{1,0:T(8,128)(2,1)S(1)}, bf16[128,512]{1,0:T(8,128)(2,1)S(1)}, u32[]{:S(2)}, u32[]{:S(2)}) collective-permute-start(bf16[128,512]{1,0:T(8,128)(2,1)S(1)} %get-tuple-element.95), channel_id=1, source_target_pairs={{0,2},{1,3},{2,0},{3,1},{4,6},{5,7},{6,4},{7,5},{8,10},{9,11},{10,... | collective-permute-start | bytes 393224 | tf_op jit(solution)/shard_map/ppermute | solution.py:458
  102.6 5.4 %collective-permute-start.20 = (bf16[256,512]{1,0:T(8,128)(2,1)S(1)}, bf16[256,512]{1,0:T(8,128)(2,1)S(1)}, u32[]{:S(2)}, u32[]{:S(2)}) collective-permute-start(bf16[256,512]{1,0:T(8,128)(2,1)S(1)} %get-tuple-element.102), channel_id=1, source_target_pairs={{0,1},{1,0},{2,3},{3,2},{4,5},{5,4},{6,7},{7,6},{8,9},{9,8},{10,11... | collective-permute-start | bytes 786440 | tf_op jit(solution)/shard_map/ppermute | solution.py:458
  103.2 8.8 %collective-permute-start.17 = (bf16[256,512]{1,0:T(8,128)(2,1)S(1)}, bf16[256,512]{1,0:T(8,128)(2,1)S(1)}, u32[]{:S(2)}, u32[]{:S(2)}) collective-permute-start(bf16[256,512]{1,0:T(8,128)(2,1)S(1)} %get-tuple-element.98), channel_id=1, source_target_pairs={{0,2},{1,3},{2,0},{3,1},{4,6},{5,7},{6,4},{7,5},{8,10},{9,11},{10,... | collective-permute-start | bytes 786440 | tf_op jit(solution)/shard_map/ppermute | solution.py:458
  106.5 6.4 %collective-permute-start.18 = (bf16[256,512]{1,0:T(8,128)(2,1)S(1)}, bf16[256,512]{1,0:T(8,128)(2,1)S(1)}, u32[]{:S(2)}, u32[]{:S(2)}) collective-permute-start(bf16[256,512]{1,0:T(8,128)(2,1)S(1)} %get-tuple-element.99), channel_id=1, source_target_pairs={{0,4},{1,5},{2,6},{3,7},{4,0},{5,1},{6,2},{7,3},{8,12},{9,13},{10,... | collective-permute-start | bytes 786440 | tf_op jit(solution)/shard_map/ppermute | solution.py:458
  107.4 8.1 %collective-permute-start.26 = (bf16[256,512]{1,0:T(8,128)(2,1)S(1)}, bf16[256,512]{1,0:T(8,128)(2,1)S(1)}, u32[]{:S(2)}, u32[]{:S(2)}) collective-permute-start(bf16[256,512]{1,0:T(8,128)(2,1)S(1)} %slice.32.refs_4_), channel_id=1, source_target_pairs={{0,1},{1,0},{2,3},{3,2},{4,5},{5,4},{6,7},{7,6},{8,9},{9,8},{10,11... | collective-permute-start | bytes 786440 | tf_op jit(solution)/shard_map/ppermute | solution.py:458
  107.4 8.0 %collective-permute-start.29 = (bf16[256,512]{1,0:T(8,128)(2,1)S(1)}, bf16[256,512]{1,0:T(8,128)(2,1)S(1)}, u32[]{:S(2)}, u32[]{:S(2)}) collective-permute-start(bf16[256,512]{1,0:T(8,128)(2,1)S(1)} %constant_dynamic-update-slice_fusion.refs_6_), channel_id=1, source_target_pairs={{0,1},{1,0},{2,3},{3,2},{4,5},{5,4},{6,7},{7,6},{8,9},{9,8},{10,11... | collective-permute-start | bytes 786440 | tf_op jit(solution)/shard_map/ppermute | solution.py:458
  107.9 11.7 %collective-permute-start.23 = (bf16[256,512]{1,0:T(8,128)(2,1)S(1)}, bf16[256,512]{1,0:T(8,128)(2,1)S(1)}, u32[]{:S(2)}, u32[]{:S(2)}) collective-permute-start(bf16[256,512]{1,0:T(8,128)(2,1)S(1)} %collective-permute-done.22.refs_4_), channel_id=1, source_target_pairs={{0,1},{1,0},{2,3},{3,2},{4,5},{5,4},{6,7},{7,6},{8,9},{9,8},{10,11... | collective-permute-start | bytes 786440 | tf_op jit(solution)/shard_map/ppermute | solution.py:458
  112.0 8.4 %collective-permute-start.25 = (bf16[256,512]{1,0:T(8,128)(2,1)S(1)}, bf16[256,512]{1,0:T(8,128)(2,1)S(1)}, u32[]{:S(2)}, u32[]{:S(2)}) collective-permute-start(bf16[256,512]{1,0:T(8,128)(2,1)S(1)} %collective-permute-done.24.refs_6_), channel_id=1, source_target_pairs={{0,1},{1,0},{2,3},{3,2},{4,5},{5,4},{6,7},{7,6},{8,9},{9,8},{10,11... | collective-permute-start | bytes 786440 | tf_op jit(solution)/shard_map/ppermute | solution.py:458
  112.0 36.8 %slice-start.4 = ((s8[6291456]{0:T(1024)(128)(4,1)}), s8[4194304]{0:T(1024)(128)(4,1)S(1)}, s32[]{:S(2)}) async-start(s8[6291456]{0:T(1024)(128)(4,1)} %bitcast.56), calls=%async_computation.4 | async-start | bytes 8388608
  113.5 10.5 %collective-permute-start.34 = (bf16[256,512]{1,0:T(8,128)(2,1)S(1)}, bf16[256,512]{1,0:T(8,128)(2,1)S(1)}, u32[]{:S(2)}, u32[]{:S(2)}) collective-permute-start(bf16[256,512]{1,0:T(8,128)(2,1)S(1)} %key_backward.1.refs_4_), channel_id=1, source_target_pairs={{0,6},{1,7},{2,4},{3,5},{4,2},{5,3},{6,0},{7,1},{8,14},{9,15},{10,... | collective-permute-start | bytes 786440 | tf_op jit(solution)/shard_map/ppermute | solution.py:458
  115.4 13.5 %collective-permute-start.33 = (bf16[256,512]{1,0:T(8,128)(2,1)S(1)}, bf16[256,512]{1,0:T(8,128)(2,1)S(1)}, u32[]{:S(2)}, u32[]{:S(2)}) collective-permute-start(bf16[256,512]{1,0:T(8,128)(2,1)S(1)} %key_backward.1.refs_4_), channel_id=1, source_target_pairs={{0,1},{1,0},{2,3},{3,2},{4,5},{5,4},{6,7},{7,6},{8,9},{9,8},{10,11... | collective-permute-start | bytes 786440 | tf_op jit(solution)/shard_map/ppermute | solution.py:458
  115.4 12.9 %collective-permute-start.31 = (bf16[256,512]{1,0:T(8,128)(2,1)S(1)}, bf16[256,512]{1,0:T(8,128)(2,1)S(1)}, u32[]{:S(2)}, u32[]{:S(2)}) collective-permute-start(bf16[256,512]{1,0:T(8,128)(2,1)S(1)} %key_backward.1.refs_4_), channel_id=1, source_target_pairs={{0,4},{1,5},{2,6},{3,7},{4,0},{5,1},{6,2},{7,3},{8,12},{9,13},{10,... | collective-permute-start | bytes 786440 | tf_op jit(solution)/shard_map/ppermute | solution.py:458
  119.7 8.7 %collective-permute-start.21 = (bf16[256,512]{1,0:T(8,128)(2,1)S(1)}, bf16[256,512]{1,0:T(8,128)(2,1)S(1)}, u32[]{:S(2)}, u32[]{:S(2)}) collective-permute-start(bf16[256,512]{1,0:T(8,128)(2,1)S(1)} %key_backward.1.refs_4_), channel_id=1, source_target_pairs={{0,2},{1,3},{2,0},{3,1},{4,6},{5,7},{6,4},{7,5},{8,10},{9,11},{10,... | collective-permute-start | bytes 786440 | tf_op jit(solution)/shard_map/ppermute | solution.py:458
  120.4 28.4 %slice-start.5 = ((s8[6291456]{0:T(1024)(128)(4,1)}), s8[2097152]{0:T(1024)(128)(4,1)S(1)}, s32[]{:S(2)}) async-start(s8[6291456]{0:T(1024)(128)(4,1)} %bitcast.56), calls=%async_computation.5 | async-start | bytes 4194304
  124.0 4.9 %collective-permute-start.35 = (bf16[256,512]{1,0:T(8,128)(2,1)S(1)}, bf16[256,512]{1,0:T(8,128)(2,1)S(1)}, u32[]{:S(2)}, u32[]{:S(2)}) collective-permute-start(bf16[256,512]{1,0:T(8,128)(2,1)S(1)} %collective-permute-done.34.refs_6_), channel_id=1, source_target_pairs={{0,1},{1,0},{2,3},{3,2},{4,5},{5,4},{6,7},{7,6},{8,9},{9,8},{10,11... | collective-permute-start | bytes 786440 | tf_op jit(solution)/shard_map/ppermute | solution.py:458
  128.4 3.7 %collective-permute-start.30 = (bf16[256,512]{1,0:T(8,128)(2,1)S(1)}, bf16[256,512]{1,0:T(8,128)(2,1)S(1)}, u32[]{:S(2)}, u32[]{:S(2)}) collective-permute-start(bf16[256,512]{1,0:T(8,128)(2,1)S(1)} %collective-permute-done.21.refs_4_), channel_id=1, source_target_pairs={{0,1},{1,0},{2,3},{3,2},{4,5},{5,4},{6,7},{7,6},{8,9},{9,8},{10,11... | collective-permute-start | bytes 786440 | tf_op jit(solution)/shard_map/ppermute | solution.py:458
  128.4 3.7 %collective-permute-start.32 = (bf16[256,512]{1,0:T(8,128)(2,1)S(1)}, bf16[256,512]{1,0:T(8,128)(2,1)S(1)}, u32[]{:S(2)}, u32[]{:S(2)}) collective-permute-start(bf16[256,512]{1,0:T(8,128)(2,1)S(1)} %collective-permute-done.31.refs_6_), channel_id=1, source_target_pairs={{0,1},{1,0},{2,3},{3,2},{4,5},{5,4},{6,7},{7,6},{8,9},{9,8},{10,11... | collective-permute-start | bytes 786440 | tf_op jit(solution)/shard_map/ppermute | solution.py:458
  128.9 19.9 %slice-start = ((s8[6291456]{0:T(1024)(128)(4,1)}), s8[4194304]{0:T(1024)(128)(4,1)S(1)}, s32[]{:S(2)}) async-start(s8[6291456]{0:T(1024)(128)(4,1)} %bitcast.40), calls=%async_computation | async-start | bytes 8388608
  128.9 19.9 %slice-start.2 = ((s8[6291456]{0:T(1024)(128)(4,1)}), s8[4194304]{0:T(1024)(128)(4,1)S(1)}, s32[]{:S(2)}) async-start(s8[6291456]{0:T(1024)(128)(4,1)} %bitcast.48), calls=%async_computation.2 | async-start | bytes 8388608
  132.1 16.7 %slice-start.1 = ((s8[6291456]{0:T(1024)(128)(4,1)}), s8[2097152]{0:T(1024)(128)(4,1)S(1)}, s32[]{:S(2)}) async-start(s8[6291456]{0:T(1024)(128)(4,1)} %bitcast.40), calls=%async_computation.1 | async-start | bytes 4194304
  132.1 16.7 %slice-start.3 = ((s8[6291456]{0:T(1024)(128)(4,1)}), s8[2097152]{0:T(1024)(128)(4,1)S(1)}, s32[]{:S(2)}) async-start(s8[6291456]{0:T(1024)(128)(4,1)} %bitcast.48), calls=%async_computation.3 | async-start | bytes 4194304
  135.8 1.2 collective-permute-start.36
  137.0 4.5 %collective-permute-start.39 = (f32[8,128]{1,0:T(8,128)S(1)}, f32[8,128]{1,0:T(8,128)S(1)}, u32[]{:S(2)}, u32[]{:S(2)}) collective-permute-start(f32[8,128]{1,0:T(8,128)S(1)} %add.32.refs_0_), channel_id=1, source_target_pairs={{0,6},{1,7},{2,4},{3,5},{4,2},{5,3},{6,0},{7,1},{8,14},{9,15},{10,... | collective-permute-start | bytes 12296 | tf_op jit(solution)/shard_map/ppermute | solution.py:458
  138.6 3.6 %collective-permute-start.38 = (f32[8,128]{1,0:T(8,128)S(1)}, f32[8,128]{1,0:T(8,128)S(1)}, u32[]{:S(2)}, u32[]{:S(2)}) collective-permute-start(f32[8,128]{1,0:T(8,128)S(1)} %add.32.refs_0_), channel_id=1, source_target_pairs={{0,4},{1,5},{2,6},{3,7},{4,0},{5,1},{6,2},{7,3},{8,12},{9,13},{10,... | collective-permute-start | bytes 12296 | tf_op jit(solution)/shard_map/ppermute | solution.py:458
  139.2 3.6 %collective-permute-start.37 = (f32[8,128]{1,0:T(8,128)S(1)}, f32[8,128]{1,0:T(8,128)S(1)}, u32[]{:S(2)}, u32[]{:S(2)}) collective-permute-start(f32[8,128]{1,0:T(8,128)S(1)} %add.32.refs_0_), channel_id=1, source_target_pairs={{0,2},{1,3},{2,0},{3,1},{4,6},{5,7},{6,4},{7,5},{8,10},{9,11},{10,... | collective-permute-start | bytes 12296 | tf_op jit(solution)/shard_map/ppermute | solution.py:458
  144.3 10.5 %collective-permute-start.40 = (bf16[384,128]{1,0:T(8,128)(2,1)S(1)}, bf16[384,128]{1,0:T(8,128)(2,1)S(1)}, u32[]{:S(2)}, u32[]{:S(2)}) collective-permute-start(bf16[384,128]{1,0:T(8,128)(2,1)S(1)} %get-tuple-element.128), channel_id=1, source_target_pairs={{0,8},{8,0},{16,24},{24,16},{1,9},{9,1},{17,25},{25,17},{2,10},{10... | collective-permute-start | bytes 294920 | tf_op jit(solution)/shard_map/ppermute | solution.py:458
  144.4 10.5 %collective-permute-start.41 = (bf16[384,128]{1,0:T(8,128)(2,1)S(1)}, bf16[384,128]{1,0:T(8,128)(2,1)S(1)}, u32[]{:S(2)}, u32[]{:S(2)}) collective-permute-start(bf16[384,128]{1,0:T(8,128)(2,1)S(1)} %get-tuple-element.129), channel_id=1, source_target_pairs={{0,16},{8,24},{16,0},{24,8},{1,17},{9,25},{17,1},{25,9},{2,18},{10... | collective-permute-start | bytes 294920 | tf_op jit(solution)/shard_map/ppermute | solution.py:458
  147.5 7.4 %collective-permute-start.42 = (bf16[384,128]{1,0:T(8,128)(2,1)S(1)}, bf16[384,128]{1,0:T(8,128)(2,1)S(1)}, u32[]{:S(2)}, u32[]{:S(2)}) collective-permute-start(bf16[384,128]{1,0:T(8,128)(2,1)S(1)} %get-tuple-element.130), channel_id=1, source_target_pairs={{0,24},{8,16},{16,8},{24,0},{1,25},{9,17},{17,9},{25,1},{2,26},{10... | collective-permute-start | bytes 294920 | tf_op jit(solution)/shard_map/ppermute | solution.py:458
  155.0 10.5 %collective-permute-start.45 = (bf16[384,128]{1,0:T(8,128)(2,1)S(1)}, bf16[384,128]{1,0:T(8,128)(2,1)S(1)}, u32[]{:S(2)}, u32[]{:S(2)}) collective-permute-start(bf16[384,128]{1,0:T(8,128)(2,1)S(1)} %convert_element_type.24.refs_7_), channel_id=1, source_target_pairs={{0,24},{8,16},{16,8},{24,0},{1,25},{9,17},{17,9},{25,1},{2,26},{10... | collective-permute-start | bytes 294920 | tf_op jit(solution)/shard_map/ppermute | solution.py:458
  157.5 7.9 %collective-permute-start.44 = (bf16[384,128]{1,0:T(8,128)(2,1)S(1)}, bf16[384,128]{1,0:T(8,128)(2,1)S(1)}, u32[]{:S(2)}, u32[]{:S(2)}) collective-permute-start(bf16[384,128]{1,0:T(8,128)(2,1)S(1)} %convert_element_type.24.refs_7_), channel_id=1, source_target_pairs={{0,16},{8,24},{16,0},{24,8},{1,17},{9,25},{17,1},{25,9},{2,18},{10... | collective-permute-start | bytes 294920 | tf_op jit(solution)/shard_map/ppermute | solution.py:458
  157.5 7.9 %collective-permute-start.43 = (bf16[384,128]{1,0:T(8,128)(2,1)S(1)}, bf16[384,128]{1,0:T(8,128)(2,1)S(1)}, u32[]{:S(2)}, u32[]{:S(2)}) collective-permute-start(bf16[384,128]{1,0:T(8,128)(2,1)S(1)} %convert_element_type.24.refs_7_), channel_id=1, source_target_pairs={{0,8},{8,0},{16,24},{24,16},{1,9},{9,1},{17,25},{25,17},{2,10},{10... | collective-permute-start | bytes 294920 | tf_op jit(solution)/shard_map/ppermute | solution.py:458

commit v22 on v21

--- a/solution.py
+++ b/solution.py
@@ -506,16 +506,6 @@
         for k, before in zip(order[i:i + 2], order[i - 2:i]):
             blocks[k] = swap(after(packed[k], blocks[before], *ready), "fsdp", k)
 
-    relay = len(far) == 3 and far[0] == far[1] ^ far[2]
-    half = inputs.shape[0] // 2
-    values = {0: incoming[:, kv_width:]}
-    for i, k in enumerate(far[1:] if relay else far):
-        values[k] = swap(after(values[0], blocks[order[i]]), "fsdp", k)
-    if relay:
-        upper = swap(values[far[1]][:half], "fsdp", far[2])
-        lower = swap(values[far[2]][half:], "fsdp", far[1])
-        values[far[0]] = jnp.concatenate([upper, lower], axis=0)
-
     steps_now = step_count[0].astype(jnp.float32)
     plan = jnp.minimum(1.0, steps_now / WARMUP) * (
         0.55 + 0.45 * jnp.cos(jnp.pi * steps_now / STEPS_TOTAL)
@@ -530,6 +520,8 @@
 
     last = far[-1]
     blocks[last + 1] = after(blocks[last + 1], anchor_copy, momentum_copy, scalars, old_first, old_second)
+    relay = len(far) == 3 and far[0] == far[1] ^ far[2]
+    half = inputs.shape[0] // 2
     parts, flipped, relayed = [], {}, {}
     for k in far + [0]:
         theirs, flipped[k + 1] = partial_keys(blocks[k + 1], key_weights)
@@ -542,8 +534,15 @@
             continue
         part_k, flipped[k] = partial_keys(blocks[k], key_weights, adds)
         if k == last:
+            values = {0: after(incoming[:, kv_width:], part_k)}
+            for j in far[1:] if relay else far:
+                values[j] = swap(values[0], "fsdp", j)
+            if relay:
+                upper = swap(values[far[1]][:half], "fsdp", far[2])
+                lower = swap(values[far[2]][half:], "fsdp", far[1])
+                values[far[0]] = jnp.concatenate([upper, lower], axis=0)
             for j in range(0, shards, 2):
-                values[j + 1] = swap(after(values[j], part_k), "fsdp", 1)
+                values[j + 1] = swap(values[j], "fsdp", 1)
         parts.append(swap(part_k, "fsdp", k) if k else part_k)
     spread = [0, 1] + [k + odd for k in far for odd in range(2)]
     near, rest = spread[:shards // 2], spread[shards // 2:]

time: 169 us -> 172 us (1.018)
  starting transfers between devices: 41.6 us -> 43.7 us
    ppermute x46, starting transfers between devices: 41.6 us -> 43.7 us  [swap(): return lax.ppermute(block, axis, [(i, i ^ offset) for i in range(count)])]
  transfers between devices with their start and end apart: 46 -> 46, of which waited for: 18 -> 16; matrix products, arithmetic and copies ran while one was open for 0% -> 0% of each run, Pallas kernels for 27% -> 27%
where the time goes in v22:
time: 172 us; the launch traced here: 171 us
  waiting for transfers between devices  68.5 us (40%)
  Pallas kernels  54.8 us (32%)
  starting transfers between devices  43.7 us (25%)
  between operations  3.81 us (2%)
    ppermute x46, waiting for transfers between devices, swap(): return lax.ppermute(block, axis, [(i, i ^ offset) for i in range(count)])  68.5 us
    ppermute x46, starting transfers between devices, swap(): return lax.ppermute(block, axis, [(i, i ^ offset) for i in range(count)])  43.7 us
    pallas_call x4, Pallas kernels, gradient(): pl.pallas_call(functools.partial(grad_kernel, len(flipped), base is not N...  13.5 us
    pallas_call x2, Pallas kernels, adam_rows(): pl.pallas_call(functools.partial(adam_kernel, len(squares), len(into)), o...  12 us
    pallas_call x4, Pallas kernels, pack(): pl.pallas_call(functools.partial(pack_kernel, offsets), out_shape=[pltpu....  9.16 us
    pallas_call x3, Pallas kernels, due_columns(): pl.pallas_call(functools.partial(pick_kernel, blocks), out_shape=[jax.Sha...  5.55 us
    pallas_call x8, Pallas kernels, partial_keys(): pl.pallas_call(functools.partial(partial_kernel, pieces, [first for _, fi...  4.64 us
    pallas_call x1, Pallas kernels, cast_left(): pl.pallas_call(cast_kernel, out_shape=jax.ShapeDtypeStruct((rows, width),...  3.47 us
  transfers between devices with their start and end apart: 46, of which 16 were waited for; matrix products, arithmetic and copies ran while one was open for 0% of the time, Pallas kernels for 27%

profile of v22, /device:TPU:0, one launch (start us, length us, event | category | flops | bytes accessed | tf_op | source)
XLA Modules:
  0.0 171.3 jit_solution(539194243762088032)
XLA Ops:
  0.6 2.6 %pack.4 = (bf16[256,1536]{1,0:T(8,128)(2,1)}, bf16[256,1536]{1,0:T(8,128)(2,1)}, bf16[256,1536]{1,0:T(8,128)(2,1)}) custom-call(s32[1]{0:T(128)} %bitcast.4.me_ref, bf16[256,12288]{1,0:T(8,128)(2,1)} %bitcast.64), custom_call_target="tpu_custom_call" | custom-call | bytes 4718592 | tf_op jit(solution)/shard_map/pack/pallas_call | solution.py:69
  3.3 3.4 %collective-permute-start.10 = (bf16[256,1536]{1,0:T(8,128)(2,1)}, bf16[256,1536]{1,0:T(8,128)(2,1)S(1)}, u32[]{:S(2)}, u32[]{:S(2)}) collective-permute-start(bf16[256,1536]{1,0:T(8,128)(2,1)} %get-tuple-element.75), channel_id=1, source_target_pairs={{0,7},{1,6},{2,5},{3,4},{4,3},{5,2},{6,1},{7,0},{8,15},{9,14},{10,... | collective-permute-start | bytes 2359304 | tf_op jit(solution)/shard_map/ppermute | solution.py:458
  7.4 1.8 %due_columns.4.w_ref = f32[4,384,128]{2,1,0:T(8,128)S(1)} custom-call(s32[2]{0:T(128)S(1)} %pad_add_fusion.place_ref, f32[1536,1024]{1,0:T(8,128)} %bitcast.35, f32[1536,1024]{1,0:T(8,128)} %bitcast.36, f32[1536,1024]{1,0:T(8,128)} %bitcast.37, f32[1536,1024]{1,0:T(8,128)} %bitcast.38), custom_call_target="tpu_custom_call" | custom-call | bytes 1572864 | tf_op jit(solution)/shard_map/due_columns/pallas_call | solution.py:348
  9.3 1.6 collective-permute-start.1
  10.9 2.5 %collective-permute-start.3 = (f32[384,128]{1,0:T(8,128)S(1)}, f32[384,128]{1,0:T(8,128)S(1)}, u32[]{:S(2)}, u32[]{:S(2)}) collective-permute-start(f32[384,128]{1,0:T(8,128)S(1)} %get-tuple-element.133), channel_id=1, source_target_pairs={{0,24},{8,16},{16,8},{24,0},{1,25},{9,17},{17,9},{25,1},{2,26},{10... | collective-permute-start | bytes 589832 | tf_op jit(solution)/shard_map/ppermute | solution.py:458
  13.5 2.0 %pack.5 = bf16[256,1536]{1,0:T(8,128)(2,1)} custom-call(s32[1]{0:T(128)} %bitcast.4.me_ref, bf16[256,12288]{1,0:T(8,128)(2,1)} %bitcast.65), custom_call_target="tpu_custom_call" | custom-call | bytes 1572864 | tf_op jit(solution)/shard_map/pack/pallas_call | solution.py:69
  15.5 0.6 collective-permute-start
  16.1 1.6 due_columns.3
  17.7 5.7 %collective-permute-done.3 = f32[384,128]{1,0:T(8,128)S(1)} collective-permute-done((f32[384,128]{1,0:T(8,128)S(1)}, f32[384,128]{1,0:T(8,128)S(1)}, u32[]{:S(2)}, u32[]{:S(2)}) %collective-permute-start.3) | collective-permute-done | bytes 196640 | tf_op jit(solution)/shard_map/ppermute | solution.py:458
  23.5 8.2 %collective-permute-done.2 = f32[384,128]{1,0:T(8,128)S(1)} collective-permute-done((f32[384,128]{1,0:T(8,128)S(1)}, f32[384,128]{1,0:T(8,128)S(1)}, u32[]{:S(2)}, u32[]{:S(2)}) %collective-permute-start.2) | collective-permute-done | bytes 196640 | tf_op jit(solution)/shard_map/ppermute | solution.py:458
  32.3 9.6 %collective-permute-done.refs_0_.refs_1_.refs_2_.refs_3_ = bf16[256,1536]{1,0:T(8,128)(2,1)S(1)} collective-permute-done((bf16[256,1536]{1,0:T(8,128)(2,1)}, bf16[256,1536]{1,0:T(8,128)(2,1)S(1)}, u32[]{:S(2)}, u32[]{:S(2)}) %collective-permute-start) | collective-permute-done | bytes 786464 | tf_op jit(solution)/shard_map/ppermute | solution.py:458
  41.9 2.2 %collective-permute-start.4 = (bf16[256,1536]{1,0:T(8,128)(2,1)S(1)}, bf16[256,1536]{1,0:T(8,128)(2,1)S(1)}, u32[]{:S(2)}, u32[]{:S(2)}) collective-permute-start(bf16[256,1536]{1,0:T(8,128)(2,1)S(1)} %copy-done.2), channel_id=1, source_target_pairs={{0,2},{1,3},{2,0},{3,1},{4,6},{5,7},{6,4},{7,5},{8,10},{9,11},{10,... | collective-permute-start | bytes 2359304 | tf_op jit(solution)/shard_map/ppermute | solution.py:458
  44.2 3.6 %collective-permute-start.7 = (f32[384,128]{1,0:T(8,128)S(1)}, f32[384,128]{1,0:T(8,128)S(1)}, u32[]{:S(2)}, u32[]{:S(2)}) collective-permute-start(f32[384,128]{1,0:T(8,128)S(1)} %get-tuple-element.130.refs_3_), channel_id=1, source_target_pairs={{0,24},{8,16},{16,8},{24,0},{1,25},{9,17},{17,9},{25,1},{2,26},{10... | collective-permute-start | bytes 589832 | tf_op jit(solution)/shard_map/ppermute | solution.py:458
  47.8 0.8 collective-permute-start.5
  48.6 2.3 %pack.6 = (bf16[256,1536]{1,0:T(8,128)(2,1)}, bf16[256,1536]{1,0:T(8,128)(2,1)}) custom-call(s32[1]{0:T(128)} %bitcast.4.me_ref, bf16[256,12288]{1,0:T(8,128)(2,1)} %bitcast.66), custom_call_target="tpu_custom_call" | custom-call | bytes 3145728 | tf_op jit(solution)/shard_map/pack/pallas_call | solution.py:69
  50.9 3.0 %collective-permute-done.7.refs_6_ = f32[384,128]{1,0:T(8,128)S(1)} collective-permute-done((f32[384,128]{1,0:T(8,128)S(1)}, f32[384,128]{1,0:T(8,128)S(1)}, u32[]{:S(2)}, u32[]{:S(2)}) %collective-permute-start.7) | collective-permute-done | bytes 196640 | tf_op jit(solution)/shard_map/ppermute | solution.py:458
  53.9 10.5 %collective-permute-done.6.refs_5_ = f32[384,128]{1,0:T(8,128)S(1)} collective-permute-done((f32[384,128]{1,0:T(8,128)S(1)}, f32[384,128]{1,0:T(8,128)S(1)}, u32[]{:S(2)}, u32[]{:S(2)}) %collective-permute-start.6) | collective-permute-done | bytes 196640 | tf_op jit(solution)/shard_map/ppermute | solution.py:458
  64.7 1.5 collective-permute-start.8
  66.2 2.3 %pack.7 = (bf16[256,1536]{1,0:T(8,128)(2,1)}, bf16[256,1536]{1,0:T(8,128)(2,1)}) custom-call(s32[1]{0:T(128)} %bitcast.4.me_ref, bf16[256,12288]{1,0:T(8,128)(2,1)} %bitcast.67), custom_call_target="tpu_custom_call" | custom-call | bytes 3145728 | tf_op jit(solution)/shard_map/pack/pallas_call | solution.py:69
  68.6 3.5 %cast_left.1.refs_4_ = bf16[1536,512]{1,0:T(8,128)(2,1)S(1)} custom-call(f32[1536,1024]{1,0:T(8,128)} %bitcast.39), custom_call_target="tpu_custom_call" | custom-call | bytes 4718592 | tf_op jit(solution)/shard_map/cast_left/pallas_call | solution.py:93
  72.0 0.6 partial_keys.9
  73.2 2.8 %duplicate.1 = (f32[384,1024]{1,0:T(8,128)}, f32[384,1024]{1,0:T(8,128)}) custom-call(f32[384,1024]{1,0:T(8,128)} %refs_0_.3, f32[384,1024]{1,0:T(8,128)} %refs_1_.3), custom_call_target="tpu_custom_call" | custom-call | bytes 6291456 | tf_op jit(solution)/shard_map/duplicate/pallas_call | solution.py:389
  76.9 2.1 %due_columns.5 = (f32[4,384,128]{2,1,0:T(8,128)S(1)}, f32[4,384,128]{2,1,0:T(8,128)S(1)}) custom-call(s32[2]{0:T(128)S(1)} %pad_add_fusion.place_ref, f32[1536,1024]{1,0:T(8,128)} %bitcast.44, f32[1536,1024]{1,0:T(8,128)} %bitcast.45, f32[1536,1024]{1,0:T(8,128)} %bitcast.46, f32[1536,1024]{1,0:T(8,128)} %bitcast.47, f32[1536,1024]{1,0:T(8,128)} %bitcast.52, ...), custom_call_target="tpu_custom_call" | custom-call | bytes 3145728 | tf_op jit(solution)/shard_map/due_columns/pallas_call | solution.py:348
  79.1 5.3 %collective-permute-done.14.refs_0_.refs_1_.refs_2_.refs_3_ = bf16[256,1536]{1,0:T(8,128)(2,1)S(1)} collective-permute-done((bf16[256,1536]{1,0:T(8,128)(2,1)}, bf16[256,1536]{1,0:T(8,128)(2,1)S(1)}, u32[]{:S(2)}, u32[]{:S(2)}) %collective-permute-start.14) | collective-permute-done | bytes 786464 | tf_op jit(solution)/shard_map/ppermute | solution.py:458
  84.4 0.6 partial_keys.12
  85.7 0.6 collective-permute-start.16
  86.4 5.2 %collective-permute-done.16.refs_6_ = bf16[128,512]{1,0:T(8,128)(2,1)S(1)} collective-permute-done((bf16[128,512]{1,0:T(8,128)(2,1)S(1)}, bf16[128,512]{1,0:T(8,128)(2,1)S(1)}, u32[]{:S(2)}, u32[]{:S(2)}) %collective-permute-start.16) | collective-permute-done | bytes 131104 | tf_op jit(solution)/shard_map/ppermute | solution.py:458
  92.6 1.1 collective-permute-start.24
  93.7 0.6 partial_keys.8
  94.4 1.0 collective-permute-start.12
  95.4 4.6 %collective-permute-done.22.refs_4_ = bf16[256,512]{1,0:T(8,128)(2,1)S(1)} collective-permute-done((bf16[256,512]{1,0:T(8,128)(2,1)S(1)}, bf16[256,512]{1,0:T(8,128)(2,1)S(1)}, u32[]{:S(2)}, u32[]{:S(2)}) %collective-permute-start.22) | collective-permute-done | bytes 262176 | tf_op jit(solution)/shard_map/ppermute | solution.py:458
  100.0 1.1 collective-permute-start.27
  101.2 0.6 partial_keys.14
  102.3 2.0 %collective-permute-done.12.refs_6_ = bf16[128,512]{1,0:T(8,128)(2,1)S(1)} collective-permute-done((bf16[128,512]{1,0:T(8,128)(2,1)S(1)}, bf16[128,512]{1,0:T(8,128)(2,1)S(1)}, u32[]{:S(2)}, u32[]{:S(2)}) %collective-permute-start.12) | collective-permute-done | bytes 131104 | tf_op jit(solution)/shard_map/ppermute | solution.py:458
  104.3 1.2 collective-permute-start.18
  105.6 1.5 collective-permute-start.28
  107.0 0.6 partial_keys.11
  107.7 0.6 collective-permute-start.17
  108.3 3.7 %collective-permute-done.28 = bf16[128,512]{1,0:T(8,128)(2,1)S(1)} collective-permute-done((bf16[128,512]{1,0:T(8,128)(2,1)S(1)}, bf16[128,512]{1,0:T(8,128)(2,1)S(1)}, u32[]{:S(2)}, u32[]{:S(2)}) %collective-permute-start.28) | collective-permute-done | bytes 131104 | tf_op jit(solution)/shard_map/ppermute | solution.py:458
  112.6 2.2 %collective-permute-done.17.refs_0_ = bf16[256,512]{1,0:T(8,128)(2,1)S(1)} collective-permute-done((bf16[256,512]{1,0:T(8,128)(2,1)S(1)}, bf16[256,512]{1,0:T(8,128)(2,1)S(1)}, u32[]{:S(2)}, u32[]{:S(2)}) %collective-permute-start.17) | collective-permute-done | bytes 262176 | tf_op jit(solution)/shard_map/ppermute | solution.py:458
  114.8 0.6 partial_keys.15
  115.9 1.6 collective-permute-start.34
  117.8 0.9 collective-permute-start.31
  118.7 3.2 %gradient.4.refs_8_ = f32[1536,512]{1,0:T(8,128)S(1)} custom-call(s32[2]{0:T(128)S(1)} %pad_add_fusion.place_ref, bf16[1536,256]{1,0:T(8,128)(2,1)S(1)} %get-tuple-element.100.refs_0_, bf16[1536,256]{1,0:T(8,128)(2,1)S(1)} %get-tuple-element.101.refs_1_, bf16[1536,256]{1,0:T(8,128)(2,1)S(1)} %get-tuple-element.102.refs_2_, ...), custom_call_target="tpu_custom_call" | custom-call | flops 1610612736 | bytes 6291456 | tf_op jit(solution)/shard_map/gradient/pallas_call | solution.py:236
  121.9 1.1 collective-permute-start.21
  123.0 3.6 %gradient.5 = (f32[1536,512]{1,0:T(8,128)S(1)}, f32[8,128]{1,0:T(8,128)S(1)}, f32[1536,128]{1,0:T(8,128)S(1)}) custom-call(s32[2]{0:T(128)S(1)} %pad_add_fusion.place_ref, bf16[1536,256]{1,0:T(8,128)(2,1)S(1)} %get-tuple-element.78.refs_0_, bf16[1536,256]{1,0:T(8,128)(2,1)S(1)} %get-tuple-element.79.refs_1_, ...), custom_call_target="tpu_custom_call" | custom-call | flops 1610612736 | bytes 6291456 | tf_op jit(solution)/shard_map/gradient/pallas_call | solution.py:236
  126.6 4.6 %collective-permute-done.31.refs_6_ = bf16[256,512]{1,0:T(8,128)(2,1)S(1)} collective-permute-done((bf16[256,512]{1,0:T(8,128)(2,1)S(1)}, bf16[256,512]{1,0:T(8,128)(2,1)S(1)}, u32[]{:S(2)}, u32[]{:S(2)}) %collective-permute-start.31) | collective-permute-done | bytes 262176 | tf_op jit(solution)/shard_map/ppermute | solution.py:458
  131.7 3.2 %gradient.6.refs_8_ = f32[1536,512]{1,0:T(8,128)S(1)} custom-call(s32[2]{0:T(128)S(1)} %pad_add_fusion.place_ref, bf16[1536,256]{1,0:T(8,128)(2,1)S(1)} %get-tuple-element.100.refs_0_, bf16[1536,256]{1,0:T(8,128)(2,1)S(1)} %get-tuple-element.101.refs_1_, bf16[1536,256]{1,0:T(8,128)(2,1)S(1)} %get-tuple-element.102.refs_2_, ...), custom_call_target="tpu_custom_call" | custom-call | flops 1610612736 | bytes 6291456 | tf_op jit(solution)/shard_map/gradient/pallas_call | solution.py:236
  135.0 3.6 %gradient.7 = (f32[1536,512]{1,0:T(8,128)S(1)}, f32[8,128]{1,0:T(8,128)S(1)}, f32[1536,128]{1,0:T(8,128)S(1)}) custom-call(s32[2]{0:T(128)S(1)} %pad_add_fusion.place_ref, bf16[1536,256]{1,0:T(8,128)(2,1)S(1)} %get-tuple-element.78.refs_0_, bf16[1536,256]{1,0:T(8,128)(2,1)S(1)} %get-tuple-element.79.refs_1_, ...), custom_call_target="tpu_custom_call" | custom-call | flops 1610612736 | bytes 6291456 | tf_op jit(solution)/shard_map/gradient/pallas_call | solution.py:236
  138.7 1.1 collective-permute-done.36
  139.8 1.6 collective-permute-start.39
  141.4 0.9 collective-permute-start.38
  142.3 1.0 collective-permute-start.37
  143.3 1.0 collective-permute-done.39.refs_3_
  144.3 0.7 collective-permute-done.38.refs_2_
  145.0 0.9 collective-permute-done.37.refs_1_
  145.9 1.5 adam_frag.1
  147.5 2.8 %collective-permute-start.41 = (bf16[384,128]{1,0:T(8,128)(2,1)S(1)}, bf16[384,128]{1,0:T(8,128)(2,1)S(1)}, u32[]{:S(2)}, u32[]{:S(2)}) collective-permute-start(bf16[384,128]{1,0:T(8,128)(2,1)S(1)} %get-tuple-element.119), channel_id=1, source_target_pairs={{0,16},{8,24},{16,0},{24,8},{1,17},{9,25},{17,1},{25,9},{2,18},{10... | collective-permute-start | bytes 294920 | tf_op jit(solution)/shard_map/ppermute | solution.py:458
  150.3 1.6 collective-permute-start.42
  152.0 6.0 %adam_rows.2 = (f32[1536,1024]{1,0:T(8,128)}, f32[1536,1024]{1,0:T(8,128)}, f32[1536,1024]{1,0:T(8,128)}, f32[8,128]{1,0:T(8,128)S(1)}) custom-call(f32[3]{0:T(128)S(1)} %pad_maximum_fusion.sc_ref, f32[1536,1024]{1,0:T(8,128)S(1)} %bitcast.42, f32[1536,1024]{1,0:T(8,128)S(1)} %bitcast.50, f32[1536,1024]{1,0:T(8,128)S(1)} %bitcast.58, ...), custom_call_target="tpu_custom_call" | custom-call | flops 15728640 | bytes 22020096 | tf_op jit(solution)/shard_map/adam_rows/pallas_call | solution.py:291
  158.1 2.3 %collective-permute-start.45 = (bf16[384,128]{1,0:T(8,128)(2,1)S(1)}, bf16[384,128]{1,0:T(8,128)(2,1)S(1)}, u32[]{:S(2)}, u32[]{:S(2)}) collective-permute-start(bf16[384,128]{1,0:T(8,128)(2,1)S(1)} %convert_element_type.24.refs_7_), channel_id=1, source_target_pairs={{0,24},{8,16},{16,8},{24,0},{1,25},{9,17},{17,9},{25,1},{2,26},{10... | collective-permute-start | bytes 294920 | tf_op jit(solution)/shard_map/ppermute | solution.py:458
  160.4 2.1 %collective-permute-start.43 = (bf16[384,128]{1,0:T(8,128)(2,1)S(1)}, bf16[384,128]{1,0:T(8,128)(2,1)S(1)}, u32[]{:S(2)}, u32[]{:S(2)}) collective-permute-start(bf16[384,128]{1,0:T(8,128)(2,1)S(1)} %convert_element_type.24.refs_7_), channel_id=1, source_target_pairs={{0,8},{8,0},{16,24},{24,16},{1,9},{9,1},{17,25},{25,17},{2,10},{10... | collective-permute-start | bytes 294920 | tf_op jit(solution)/shard_map/ppermute | solution.py:458
  162.5 6.0 %adam_rows.3 = (f32[1536,1024]{1,0:T(8,128)}, f32[1536,1024]{1,0:T(8,128)}, f32[1536,1024]{1,0:T(8,128)}) custom-call(f32[3]{0:T(128)S(1)} %pad_maximum_fusion.sc_ref, f32[1536,1024]{1,0:T(8,128)S(1)} %bitcast.43, f32[1536,1024]{1,0:T(8,128)S(1)} %bitcast.51, ...), custom_call_target="tpu_custom_call", output_to_operand_aliasing={{0}: (10, {}), {1}: (11, {}), {2}: (12, {})} | custom-call | flops 15728640 | bytes 22020096 | tf_op jit(solution)/shard_map/adam_rows/pallas_call | solution.py:291
  168.5 1.7 outer_step.1
  (89 shorter events, 6.6 us)
Async XLA Ops:
  3.3 28.4 %collective-permute-start.10 = (bf16[256,1536]{1,0:T(8,128)(2,1)}, bf16[256,1536]{1,0:T(8,128)(2,1)S(1)}, u32[]{:S(2)}, u32[]{:S(2)}) collective-permute-start(bf16[256,1536]{1,0:T(8,128)(2,1)} %get-tuple-element.75), channel_id=1, source_target_pairs={{0,7},{1,6},{2,5},{3,4},{4,3},{5,2},{6,1},{7,0},{8,15},{9,14},{10,... | collective-permute-start | bytes 2359304 | tf_op jit(solution)/shard_map/ppermute | solution.py:458
  9.2 22.5 %copy-start.3 = (bf16[256,1536]{1,0:T(8,128)(2,1)S(1)}, bf16[256,1536]{1,0:T(8,128)(2,1)}, u32[]{:S(2)}) copy-start(bf16[256,1536]{1,0:T(8,128)(2,1)} %get-tuple-element.81) | copy-start | bytes 2359300
  9.2 32.7 %copy-start.2 = (bf16[256,1536]{1,0:T(8,128)(2,1)S(1)}, bf16[256,1536]{1,0:T(8,128)(2,1)}, u32[]{:S(2)}) copy-start(bf16[256,1536]{1,0:T(8,128)(2,1)} %get-tuple-element.70) | copy-start | bytes 2359300
  9.3 8.4 %collective-permute-start.1 = (f32[384,128]{1,0:T(8,128)S(1)}, f32[384,128]{1,0:T(8,128)S(1)}, u32[]{:S(2)}, u32[]{:S(2)}) collective-permute-start(f32[384,128]{1,0:T(8,128)S(1)} %get-tuple-element.132), channel_id=1, source_target_pairs={{0,8},{8,0},{16,24},{24,16},{1,9},{9,1},{17,25},{25,17},{2,10},{10... | collective-permute-start | bytes 589832 | tf_op jit(solution)/shard_map/ppermute | solution.py:458
  10.9 12.5 %collective-permute-start.3 = (f32[384,128]{1,0:T(8,128)S(1)}, f32[384,128]{1,0:T(8,128)S(1)}, u32[]{:S(2)}, u32[]{:S(2)}) collective-permute-start(f32[384,128]{1,0:T(8,128)S(1)} %get-tuple-element.133), channel_id=1, source_target_pairs={{0,24},{8,16},{16,8},{24,0},{1,25},{9,17},{17,9},{25,1},{2,26},{10... | collective-permute-start | bytes 589832 | tf_op jit(solution)/shard_map/ppermute | solution.py:458
  13.4 18.2 %collective-permute-start.2 = (f32[384,128]{1,0:T(8,128)S(1)}, f32[384,128]{1,0:T(8,128)S(1)}, u32[]{:S(2)}, u32[]{:S(2)}) collective-permute-start(f32[384,128]{1,0:T(8,128)S(1)} %get-tuple-element.134), channel_id=1, source_target_pairs={{0,16},{8,24},{16,0},{24,8},{1,17},{9,25},{17,1},{25,9},{2,18},{10... | collective-permute-start | bytes 589832 | tf_op jit(solution)/shard_map/ppermute | solution.py:458
  15.5 26.4 %collective-permute-start = (bf16[256,1536]{1,0:T(8,128)(2,1)}, bf16[256,1536]{1,0:T(8,128)(2,1)S(1)}, u32[]{:S(2)}, u32[]{:S(2)}) collective-permute-start(bf16[256,1536]{1,0:T(8,128)(2,1)} %pack.5), channel_id=1, source_target_pairs={{0,6},{1,7},{2,4},{3,5},{4,2},{5,3},{6,0},{7,1},{8,14},{9,15},{10,... | collective-permute-start | bytes 2359304 | tf_op jit(solution)/shard_map/ppermute | solution.py:458
  31.7 32.7 %collective-permute-start.13 = (bf16[256,1536]{1,0:T(8,128)(2,1)S(1)}, bf16[256,1536]{1,0:T(8,128)(2,1)S(1)}, u32[]{:S(2)}, u32[]{:S(2)}) collective-permute-start(bf16[256,1536]{1,0:T(8,128)(2,1)S(1)} %copy-done.3), channel_id=1, source_target_pairs={{0,4},{1,5},{2,6},{3,7},{4,0},{5,1},{6,2},{7,3},{8,12},{9,13},{10,... | collective-permute-start | bytes 2359304 | tf_op jit(solution)/shard_map/ppermute | solution.py:458
  41.9 22.7 %collective-permute-start.4 = (bf16[256,1536]{1,0:T(8,128)(2,1)S(1)}, bf16[256,1536]{1,0:T(8,128)(2,1)S(1)}, u32[]{:S(2)}, u32[]{:S(2)}) collective-permute-start(bf16[256,1536]{1,0:T(8,128)(2,1)S(1)} %copy-done.2), channel_id=1, source_target_pairs={{0,2},{1,3},{2,0},{3,1},{4,6},{5,7},{6,4},{7,5},{8,10},{9,11},{10,... | collective-permute-start | bytes 2359304 | tf_op jit(solution)/shard_map/ppermute | solution.py:458
  44.2 9.7 %collective-permute-start.7 = (f32[384,128]{1,0:T(8,128)S(1)}, f32[384,128]{1,0:T(8,128)S(1)}, u32[]{:S(2)}, u32[]{:S(2)}) collective-permute-start(f32[384,128]{1,0:T(8,128)S(1)} %get-tuple-element.130.refs_3_), channel_id=1, source_target_pairs={{0,24},{8,16},{16,8},{24,0},{1,25},{9,17},{17,9},{25,1},{2,26},{10... | collective-permute-start | bytes 589832 | tf_op jit(solution)/shard_map/ppermute | solution.py:458
  47.8 16.6 %collective-permute-start.6 = (f32[384,128]{1,0:T(8,128)S(1)}, f32[384,128]{1,0:T(8,128)S(1)}, u32[]{:S(2)}, u32[]{:S(2)}) collective-permute-start(f32[384,128]{1,0:T(8,128)S(1)} %get-tuple-element.130.refs_3_), channel_id=1, source_target_pairs={{0,16},{8,24},{16,0},{24,8},{1,17},{9,25},{17,1},{25,9},{2,18},{10... | collective-permute-start | bytes 589832 | tf_op jit(solution)/shard_map/ppermute | solution.py:458
  47.8 16.6 %collective-permute-start.5 = (f32[384,128]{1,0:T(8,128)S(1)}, f32[384,128]{1,0:T(8,128)S(1)}, u32[]{:S(2)}, u32[]{:S(2)}) collective-permute-start(f32[384,128]{1,0:T(8,128)S(1)} %get-tuple-element.130.refs_3_), channel_id=1, source_target_pairs={{0,8},{8,0},{16,24},{24,16},{1,9},{9,1},{17,25},{25,17},{2,10},{10... | collective-permute-start | bytes 589832 | tf_op jit(solution)/shard_map/ppermute | solution.py:458
  64.4 20.0 %collective-permute-start.14 = (bf16[256,1536]{1,0:T(8,128)(2,1)}, bf16[256,1536]{1,0:T(8,128)(2,1)S(1)}, u32[]{:S(2)}, u32[]{:S(2)}) collective-permute-start(bf16[256,1536]{1,0:T(8,128)(2,1)} %get-tuple-element.83), channel_id=1, source_target_pairs={{0,5},{1,4},{2,7},{3,6},{4,1},{5,0},{6,3},{7,2},{8,13},{9,12},{10,... | collective-permute-start | bytes 2359304 | tf_op jit(solution)/shard_map/ppermute | solution.py:458
  64.7 29.0 %collective-permute-start.8 = (bf16[256,1536]{1,0:T(8,128)(2,1)}, bf16[256,1536]{1,0:T(8,128)(2,1)S(1)}, u32[]{:S(2)}, u32[]{:S(2)}) collective-permute-start(bf16[256,1536]{1,0:T(8,128)(2,1)} %get-tuple-element.73), channel_id=1, source_target_pairs={{0,3},{1,2},{2,1},{3,0},{4,7},{5,6},{6,5},{7,4},{8,11},{9,10},{10,... | collective-permute-start | bytes 2359304 | tf_op jit(solution)/shard_map/ppermute | solution.py:458
  68.5 32.7 %collective-permute-start.19 = (bf16[256,1536]{1,0:T(8,128)(2,1)}, bf16[256,1536]{1,0:T(8,128)(2,1)S(1)}, u32[]{:S(2)}, u32[]{:S(2)}) collective-permute-start(bf16[256,1536]{1,0:T(8,128)(2,1)} %get-tuple-element.96), channel_id=1, source_target_pairs={{0,1},{1,0},{2,3},{3,2},{4,5},{5,4},{6,7},{7,6},{8,9},{9,8},{10,11... | collective-permute-start | bytes 2359304 | tf_op jit(solution)/shard_map/ppermute | solution.py:458
  72.6 12.5 %collective-permute-start.11 = (bf16[256,512]{1,0:T(8,128)(2,1)S(1)}, bf16[256,512]{1,0:T(8,128)(2,1)S(1)}, u32[]{:S(2)}, u32[]{:S(2)}) collective-permute-start(bf16[256,512]{1,0:T(8,128)(2,1)S(1)} %get-tuple-element.76), channel_id=1, source_target_pairs={{0,1},{1,0},{2,3},{3,2},{4,5},{5,4},{6,7},{7,6},{8,9},{9,8},{10,11... | collective-permute-start | bytes 786440 | tf_op jit(solution)/shard_map/ppermute | solution.py:458
  79.0 7.3 %copy-start.1 = (bf16[1,256,1024]{2,1,0:T(8,128)(2,1)S(1)}, bf16[1,256,1024]{2,1,0:T(8,128)(2,1)}, u32[]{:S(2)}) copy-start(bf16[1,256,1024]{2,1,0:T(8,128)(2,1)} %param.10) | copy-start | bytes 1572868
  85.0 6.6 %collective-permute-start.15 = (bf16[256,512]{1,0:T(8,128)(2,1)S(1)}, bf16[256,512]{1,0:T(8,128)(2,1)S(1)}, u32[]{:S(2)}, u32[]{:S(2)}) collective-permute-start(bf16[256,512]{1,0:T(8,128)(2,1)S(1)} %get-tuple-element.89), channel_id=1, source_target_pairs={{0,1},{1,0},{2,3},{3,2},{4,5},{5,4},{6,7},{7,6},{8,9},{9,8},{10,11... | collective-permute-start | bytes 786440 | tf_op jit(solution)/shard_map/ppermute | solution.py:458
  85.7 5.9 %collective-permute-start.16 = (bf16[128,512]{1,0:T(8,128)(2,1)S(1)}, bf16[128,512]{1,0:T(8,128)(2,1)S(1)}, u32[]{:S(2)}, u32[]{:S(2)}) collective-permute-start(bf16[128,512]{1,0:T(8,128)(2,1)S(1)} %get-tuple-element.90), channel_id=1, source_target_pairs={{0,2},{1,3},{2,0},{3,1},{4,6},{5,7},{6,4},{7,5},{8,10},{9,11},{10,... | collective-permute-start | bytes 393224 | tf_op jit(solution)/shard_map/ppermute | solution.py:458
  92.2 7.8 %collective-permute-start.22 = (bf16[256,512]{1,0:T(8,128)(2,1)S(1)}, bf16[256,512]{1,0:T(8,128)(2,1)S(1)}, u32[]{:S(2)}, u32[]{:S(2)}) collective-permute-start(bf16[256,512]{1,0:T(8,128)(2,1)S(1)} %slice.32.refs_4_), channel_id=1, source_target_pairs={{0,2},{1,3},{2,0},{3,1},{4,6},{5,7},{6,4},{7,5},{8,10},{9,11},{10,... | collective-permute-start | bytes 786440 | tf_op jit(solution)/shard_map/ppermute | solution.py:458
  92.6 9.2 %collective-permute-start.24 = (bf16[256,512]{1,0:T(8,128)(2,1)S(1)}, bf16[256,512]{1,0:T(8,128)(2,1)S(1)}, u32[]{:S(2)}, u32[]{:S(2)}) collective-permute-start(bf16[256,512]{1,0:T(8,128)(2,1)S(1)} %slice.32.refs_4_), channel_id=1, source_target_pairs={{0,4},{1,5},{2,6},{3,7},{4,0},{5,1},{6,2},{7,3},{8,12},{9,13},{10,... | collective-permute-start | bytes 786440 | tf_op jit(solution)/shard_map/ppermute | solution.py:458
  94.3 20.5 %copy-start = (bf16[256,1536]{1,0:T(8,128)(2,1)S(1)}, bf16[256,1536]{1,0:T(8,128)(2,1)}, u32[]{:S(2)}) copy-start(bf16[256,1536]{1,0:T(8,128)(2,1)} %get-tuple-element.95.refs_0_.refs_1_.refs_2_.refs_3_) | copy-start | bytes 2359300
  94.3 11.3 %collective-permute-start.9 = (bf16[256,512]{1,0:T(8,128)(2,1)S(1)}, bf16[256,512]{1,0:T(8,128)(2,1)S(1)}, u32[]{:S(2)}, u32[]{:S(2)}) collective-permute-start(bf16[256,512]{1,0:T(8,128)(2,1)S(1)} %get-tuple-element.74), channel_id=1, source_target_pairs={{0,1},{1,0},{2,3},{3,2},{4,5},{5,4},{6,7},{7,6},{8,9},{9,8},{10,11... | collective-permute-start | bytes 786440 | tf_op jit(solution)/shard_map/ppermute | solution.py:458
  94.4 9.9 %collective-permute-start.12 = (bf16[128,512]{1,0:T(8,128)(2,1)S(1)}, bf16[128,512]{1,0:T(8,128)(2,1)S(1)}, u32[]{:S(2)}, u32[]{:S(2)}) collective-permute-start(bf16[128,512]{1,0:T(8,128)(2,1)S(1)} %get-tuple-element.77), channel_id=1, source_target_pairs={{0,4},{1,5},{2,6},{3,7},{4,0},{5,1},{6,2},{7,3},{8,12},{9,13},{10,... | collective-permute-start | bytes 393224 | tf_op jit(solution)/shard_map/ppermute | solution.py:458
  100.0 7.6 %collective-permute-start.27 = (bf16[128,512]{1,0:T(8,128)(2,1)S(1)}, bf16[128,512]{1,0:T(8,128)(2,1)S(1)}, u32[]{:S(2)}, u32[]{:S(2)}) collective-permute-start(bf16[128,512]{1,0:T(8,128)(2,1)S(1)} %slice.33), channel_id=1, source_target_pairs={{0,4},{1,5},{2,6},{3,7},{4,0},{5,1},{6,2},{7,3},{8,12},{9,13},{10,... | collective-permute-start | bytes 393224 | tf_op jit(solution)/shard_map/ppermute | solution.py:458
  101.8 10.3 %collective-permute-start.20 = (bf16[256,512]{1,0:T(8,128)(2,1)S(1)}, bf16[256,512]{1,0:T(8,128)(2,1)S(1)}, u32[]{:S(2)}, u32[]{:S(2)}) collective-permute-start(bf16[256,512]{1,0:T(8,128)(2,1)S(1)} %get-tuple-element.97), channel_id=1, source_target_pairs={{0,1},{1,0},{2,3},{3,2},{4,5},{5,4},{6,7},{7,6},{8,9},{9,8},{10,11... | collective-permute-start | bytes 786440 | tf_op jit(solution)/shard_map/ppermute | solution.py:458
  101.8 15.7 %collective-permute-start.26 = (bf16[256,512]{1,0:T(8,128)(2,1)S(1)}, bf16[256,512]{1,0:T(8,128)(2,1)S(1)}, u32[]{:S(2)}, u32[]{:S(2)}) collective-permute-start(bf16[256,512]{1,0:T(8,128)(2,1)S(1)} %slice.32.refs_4_), channel_id=1, source_target_pairs={{0,1},{1,0},{2,3},{3,2},{4,5},{5,4},{6,7},{7,6},{8,9},{9,8},{10,11... | collective-permute-start | bytes 786440 | tf_op jit(solution)/shard_map/ppermute | solution.py:458
  104.3 11.1 %collective-permute-start.18 = (bf16[256,512]{1,0:T(8,128)(2,1)S(1)}, bf16[256,512]{1,0:T(8,128)(2,1)S(1)}, u32[]{:S(2)}, u32[]{:S(2)}) collective-permute-start(bf16[256,512]{1,0:T(8,128)(2,1)S(1)} %get-tuple-element.94), channel_id=1, source_target_pairs={{0,4},{1,5},{2,6},{3,7},{4,0},{5,1},{6,2},{7,3},{8,12},{9,13},{10,... | collective-permute-start | bytes 786440 | tf_op jit(solution)/shard_map/ppermute | solution.py:458
  105.6 6.4 %collective-permute-start.28 = (bf16[128,512]{1,0:T(8,128)(2,1)S(1)}, bf16[128,512]{1,0:T(8,128)(2,1)S(1)}, u32[]{:S(2)}, u32[]{:S(2)}) collective-permute-start(bf16[128,512]{1,0:T(8,128)(2,1)S(1)} %slice.34), channel_id=1, source_target_pairs={{0,2},{1,3},{2,0},{3,1},{4,6},{5,7},{6,4},{7,5},{8,10},{9,11},{10,... | collective-permute-start | bytes 393224 | tf_op jit(solution)/shard_map/ppermute | solution.py:458
  107.7 7.1 %collective-permute-start.17 = (bf16[256,512]{1,0:T(8,128)(2,1)S(1)}, bf16[256,512]{1,0:T(8,128)(2,1)S(1)}, u32[]{:S(2)}, u32[]{:S(2)}) collective-permute-start(bf16[256,512]{1,0:T(8,128)(2,1)S(1)} %get-tuple-element.93), channel_id=1, source_target_pairs={{0,2},{1,3},{2,0},{3,1},{4,6},{5,7},{6,4},{7,5},{8,10},{9,11},{10,... | collective-permute-start | bytes 786440 | tf_op jit(solution)/shard_map/ppermute | solution.py:458
  112.0 5.8 %collective-permute-start.29 = (bf16[256,512]{1,0:T(8,128)(2,1)S(1)}, bf16[256,512]{1,0:T(8,128)(2,1)S(1)}, u32[]{:S(2)}, u32[]{:S(2)}) collective-permute-start(bf16[256,512]{1,0:T(8,128)(2,1)S(1)} %constant_dynamic-update-slice_fusion.refs_6_), channel_id=1, source_target_pairs={{0,1},{1,0},{2,3},{3,2},{4,5},{5,4},{6,7},{7,6},{8,9},{9,8},{10,11... | collective-permute-start | bytes 786440 | tf_op jit(solution)/shard_map/ppermute | solution.py:458
  112.1 9.8 %collective-permute-start.25 = (bf16[256,512]{1,0:T(8,128)(2,1)S(1)}, bf16[256,512]{1,0:T(8,128)(2,1)S(1)}, u32[]{:S(2)}, u32[]{:S(2)}) collective-permute-start(bf16[256,512]{1,0:T(8,128)(2,1)S(1)} %collective-permute-done.24.refs_6_), channel_id=1, source_target_pairs={{0,1},{1,0},{2,3},{3,2},{4,5},{5,4},{6,7},{7,6},{8,9},{9,8},{10,11... | collective-permute-start | bytes 786440 | tf_op jit(solution)/shard_map/ppermute | solution.py:458
  114.8 8.2 %collective-permute-start.23 = (bf16[256,512]{1,0:T(8,128)(2,1)S(1)}, bf16[256,512]{1,0:T(8,128)(2,1)S(1)}, u32[]{:S(2)}, u32[]{:S(2)}) collective-permute-start(bf16[256,512]{1,0:T(8,128)(2,1)S(1)} %collective-permute-done.22.refs_4_), channel_id=1, source_target_pairs={{0,1},{1,0},{2,3},{3,2},{4,5},{5,4},{6,7},{7,6},{8,9},{9,8},{10,11... | collective-permute-start | bytes 786440 | tf_op jit(solution)/shard_map/ppermute | solution.py:458
  114.8 37.1 %slice-start.4 = ((s8[6291456]{0:T(1024)(128)(4,1)}), s8[4194304]{0:T(1024)(128)(4,1)S(1)}, s32[]{:S(2)}) async-start(s8[6291456]{0:T(1024)(128)(4,1)} %bitcast.56), calls=%async_computation.4 | async-start | bytes 8388608
  115.9 10.6 %collective-permute-start.34 = (bf16[256,512]{1,0:T(8,128)(2,1)S(1)}, bf16[256,512]{1,0:T(8,128)(2,1)S(1)}, u32[]{:S(2)}, u32[]{:S(2)}) collective-permute-start(bf16[256,512]{1,0:T(8,128)(2,1)S(1)} %key_backward.1.refs_4_), channel_id=1, source_target_pairs={{0,6},{1,7},{2,4},{3,5},{4,2},{5,3},{6,0},{7,1},{8,14},{9,15},{10,... | collective-permute-start | bytes 786440 | tf_op jit(solution)/shard_map/ppermute | solution.py:458
  117.5 14.2 %collective-permute-start.33 = (bf16[256,512]{1,0:T(8,128)(2,1)S(1)}, bf16[256,512]{1,0:T(8,128)(2,1)S(1)}, u32[]{:S(2)}, u32[]{:S(2)}) collective-permute-start(bf16[256,512]{1,0:T(8,128)(2,1)S(1)} %key_backward.1.refs_4_), channel_id=1, source_target_pairs={{0,1},{1,0},{2,3},{3,2},{4,5},{5,4},{6,7},{7,6},{8,9},{9,8},{10,11... | collective-permute-start | bytes 786440 | tf_op jit(solution)/shard_map/ppermute | solution.py:458
  117.8 13.4 %collective-permute-start.31 = (bf16[256,512]{1,0:T(8,128)(2,1)S(1)}, bf16[256,512]{1,0:T(8,128)(2,1)S(1)}, u32[]{:S(2)}, u32[]{:S(2)}) collective-permute-start(bf16[256,512]{1,0:T(8,128)(2,1)S(1)} %key_backward.1.refs_4_), channel_id=1, source_target_pairs={{0,4},{1,5},{2,6},{3,7},{4,0},{5,1},{6,2},{7,3},{8,12},{9,13},{10,... | collective-permute-start | bytes 786440 | tf_op jit(solution)/shard_map/ppermute | solution.py:458
  121.9 9.3 %collective-permute-start.21 = (bf16[256,512]{1,0:T(8,128)(2,1)S(1)}, bf16[256,512]{1,0:T(8,128)(2,1)S(1)}, u32[]{:S(2)}, u32[]{:S(2)}) collective-permute-start(bf16[256,512]{1,0:T(8,128)(2,1)S(1)} %key_backward.1.refs_4_), channel_id=1, source_target_pairs={{0,2},{1,3},{2,0},{3,1},{4,6},{5,7},{6,4},{7,5},{8,10},{9,11},{10,... | collective-permute-start | bytes 786440 | tf_op jit(solution)/shard_map/ppermute | solution.py:458
  123.0 28.9 %slice-start.5 = ((s8[6291456]{0:T(1024)(128)(4,1)}), s8[2097152]{0:T(1024)(128)(4,1)S(1)}, s32[]{:S(2)}) async-start(s8[6291456]{0:T(1024)(128)(4,1)} %bitcast.56), calls=%async_computation.5 | async-start | bytes 4194304
  126.5 5.2 %collective-permute-start.35 = (bf16[256,512]{1,0:T(8,128)(2,1)S(1)}, bf16[256,512]{1,0:T(8,128)(2,1)S(1)}, u32[]{:S(2)}, u32[]{:S(2)}) collective-permute-start(bf16[256,512]{1,0:T(8,128)(2,1)S(1)} %collective-permute-done.34.refs_6_), channel_id=1, source_target_pairs={{0,1},{1,0},{2,3},{3,2},{4,5},{5,4},{6,7},{7,6},{8,9},{9,8},{10,11... | collective-permute-start | bytes 786440 | tf_op jit(solution)/shard_map/ppermute | solution.py:458
  131.2 3.7 %collective-permute-start.30 = (bf16[256,512]{1,0:T(8,128)(2,1)S(1)}, bf16[256,512]{1,0:T(8,128)(2,1)S(1)}, u32[]{:S(2)}, u32[]{:S(2)}) collective-permute-start(bf16[256,512]{1,0:T(8,128)(2,1)S(1)} %collective-permute-done.21.refs_4_), channel_id=1, source_target_pairs={{0,1},{1,0},{2,3},{3,2},{4,5},{5,4},{6,7},{7,6},{8,9},{9,8},{10,11... | collective-permute-start | bytes 786440 | tf_op jit(solution)/shard_map/ppermute | solution.py:458
  131.3 3.7 %collective-permute-start.32 = (bf16[256,512]{1,0:T(8,128)(2,1)S(1)}, bf16[256,512]{1,0:T(8,128)(2,1)S(1)}, u32[]{:S(2)}, u32[]{:S(2)}) collective-permute-start(bf16[256,512]{1,0:T(8,128)(2,1)S(1)} %collective-permute-done.31.refs_6_), channel_id=1, source_target_pairs={{0,1},{1,0},{2,3},{3,2},{4,5},{5,4},{6,7},{7,6},{8,9},{9,8},{10,11... | collective-permute-start | bytes 786440 | tf_op jit(solution)/shard_map/ppermute | solution.py:458
  131.7 20.2 %slice-start = ((s8[6291456]{0:T(1024)(128)(4,1)}), s8[4194304]{0:T(1024)(128)(4,1)S(1)}, s32[]{:S(2)}) async-start(s8[6291456]{0:T(1024)(128)(4,1)} %bitcast.40), calls=%async_computation | async-start | bytes 8388608
  131.7 20.2 %slice-start.2 = ((s8[6291456]{0:T(1024)(128)(4,1)}), s8[4194304]{0:T(1024)(128)(4,1)S(1)}, s32[]{:S(2)}) async-start(s8[6291456]{0:T(1024)(128)(4,1)} %bitcast.48), calls=%async_computation.2 | async-start | bytes 8388608
  135.0 17.0 %slice-start.1 = ((s8[6291456]{0:T(1024)(128)(4,1)}), s8[2097152]{0:T(1024)(128)(4,1)S(1)}, s32[]{:S(2)}) async-start(s8[6291456]{0:T(1024)(128)(4,1)} %bitcast.40), calls=%async_computation.1 | async-start | bytes 4194304
  135.0 17.0 %slice-start.3 = ((s8[6291456]{0:T(1024)(128)(4,1)}), s8[2097152]{0:T(1024)(128)(4,1)S(1)}, s32[]{:S(2)}) async-start(s8[6291456]{0:T(1024)(128)(4,1)} %bitcast.48), calls=%async_computation.3 | async-start | bytes 4194304
  138.6 1.2 collective-permute-start.36
  139.8 4.5 %collective-permute-start.39 = (f32[8,128]{1,0:T(8,128)S(1)}, f32[8,128]{1,0:T(8,128)S(1)}, u32[]{:S(2)}, u32[]{:S(2)}) collective-permute-start(f32[8,128]{1,0:T(8,128)S(1)} %add.32.refs_0_), channel_id=1, source_target_pairs={{0,6},{1,7},{2,4},{3,5},{4,2},{5,3},{6,0},{7,1},{8,14},{9,15},{10,... | collective-permute-start | bytes 12296 | tf_op jit(solution)/shard_map/ppermute | solution.py:458
  141.4 3.6 %collective-permute-start.38 = (f32[8,128]{1,0:T(8,128)S(1)}, f32[8,128]{1,0:T(8,128)S(1)}, u32[]{:S(2)}, u32[]{:S(2)}) collective-permute-start(f32[8,128]{1,0:T(8,128)S(1)} %add.32.refs_0_), channel_id=1, source_target_pairs={{0,4},{1,5},{2,6},{3,7},{4,0},{5,1},{6,2},{7,3},{8,12},{9,13},{10,... | collective-permute-start | bytes 12296 | tf_op jit(solution)/shard_map/ppermute | solution.py:458
  142.3 3.6 %collective-permute-start.37 = (f32[8,128]{1,0:T(8,128)S(1)}, f32[8,128]{1,0:T(8,128)S(1)}, u32[]{:S(2)}, u32[]{:S(2)}) collective-permute-start(f32[8,128]{1,0:T(8,128)S(1)} %add.32.refs_0_), channel_id=1, source_target_pairs={{0,2},{1,3},{2,0},{3,1},{4,6},{5,7},{6,4},{7,5},{8,10},{9,11},{10,... | collective-permute-start | bytes 12296 | tf_op jit(solution)/shard_map/ppermute | solution.py:458
  147.4 10.5 %collective-permute-start.40 = (bf16[384,128]{1,0:T(8,128)(2,1)S(1)}, bf16[384,128]{1,0:T(8,128)(2,1)S(1)}, u32[]{:S(2)}, u32[]{:S(2)}) collective-permute-start(bf16[384,128]{1,0:T(8,128)(2,1)S(1)} %get-tuple-element.118), channel_id=1, source_target_pairs={{0,8},{8,0},{16,24},{24,16},{1,9},{9,1},{17,25},{25,17},{2,10},{10... | collective-permute-start | bytes 294920 | tf_op jit(solution)/shard_map/ppermute | solution.py:458
  147.5 10.5 %collective-permute-start.41 = (bf16[384,128]{1,0:T(8,128)(2,1)S(1)}, bf16[384,128]{1,0:T(8,128)(2,1)S(1)}, u32[]{:S(2)}, u32[]{:S(2)}) collective-permute-start(bf16[384,128]{1,0:T(8,128)(2,1)S(1)} %get-tuple-element.119), channel_id=1, source_target_pairs={{0,16},{8,24},{16,0},{24,8},{1,17},{9,25},{17,1},{25,9},{2,18},{10... | collective-permute-start | bytes 294920 | tf_op jit(solution)/shard_map/ppermute | solution.py:458
  150.3 7.7 %collective-permute-start.42 = (bf16[384,128]{1,0:T(8,128)(2,1)S(1)}, bf16[384,128]{1,0:T(8,128)(2,1)S(1)}, u32[]{:S(2)}, u32[]{:S(2)}) collective-permute-start(bf16[384,128]{1,0:T(8,128)(2,1)S(1)} %get-tuple-element.120), channel_id=1, source_target_pairs={{0,24},{8,16},{16,8},{24,0},{1,25},{9,17},{17,9},{25,1},{2,26},{10... | collective-permute-start | bytes 294920 | tf_op jit(solution)/shard_map/ppermute | solution.py:458
  158.1 10.4 %collective-permute-start.45 = (bf16[384,128]{1,0:T(8,128)(2,1)S(1)}, bf16[384,128]{1,0:T(8,128)(2,1)S(1)}, u32[]{:S(2)}, u32[]{:S(2)}) collective-permute-start(bf16[384,128]{1,0:T(8,128)(2,1)S(1)} %convert_element_type.24.refs_7_), channel_id=1, source_target_pairs={{0,24},{8,16},{16,8},{24,0},{1,25},{9,17},{17,9},{25,1},{2,26},{10... | collective-permute-start | bytes 294920 | tf_op jit(solution)/shard_map/ppermute | solution.py:458
  160.4 8.1 %collective-permute-start.44 = (bf16[384,128]{1,0:T(8,128)(2,1)S(1)}, bf16[384,128]{1,0:T(8,128)(2,1)S(1)}, u32[]{:S(2)}, u32[]{:S(2)}) collective-permute-start(bf16[384,128]{1,0:T(8,128)(2,1)S(1)} %convert_element_type.24.refs_7_), channel_id=1, source_target_pairs={{0,16},{8,24},{16,0},{24,8},{1,17},{9,25},{17,1},{25,9},{2,18},{10... | collective-permute-start | bytes 294920 | tf_op jit(solution)/shard_map/ppermute | solution.py:458
  160.4 8.1 %collective-permute-start.43 = (bf16[384,128]{1,0:T(8,128)(2,1)S(1)}, bf16[384,128]{1,0:T(8,128)(2,1)S(1)}, u32[]{:S(2)}, u32[]{:S(2)}) collective-permute-start(bf16[384,128]{1,0:T(8,128)(2,1)S(1)} %convert_element_type.24.refs_7_), channel_id=1, source_target_pairs={{0,8},{8,0},{16,24},{24,16},{1,9},{9,1},{17,25},{25,17},{2,10},{10... | collective-permute-start | bytes 294920 | tf_op jit(solution)/shard_map/ppermute | solution.py:458

commit v23 on v22

--- a/solution.py
+++ b/solution.py
@@ -522,7 +522,7 @@
     blocks[last + 1] = after(blocks[last + 1], anchor_copy, momentum_copy, scalars, old_first, old_second)
     relay = len(far) == 3 and far[0] == far[1] ^ far[2]
     half = inputs.shape[0] // 2
-    parts, flipped, relayed = [], {}, {}
+    parts, flipped, relayed, formed = [], {}, {}, []
     for k in far + [0]:
         theirs, flipped[k + 1] = partial_keys(blocks[k + 1], key_weights)
         theirs = swap(theirs, "fsdp", 1)
@@ -533,8 +533,9 @@
             relayed[far[1]] = [(swap(lower, "fsdp", far[2]), half)]
             continue
         part_k, flipped[k] = partial_keys(blocks[k], key_weights, adds)
+        formed.append(part_k)
         if k == last:
-            values = {0: after(incoming[:, kv_width:], part_k)}
+            values = {0: after(incoming[:, kv_width:], *formed)}
             for j in far[1:] if relay else far:
                 values[j] = swap(values[0], "fsdp", j)
             if relay:

time: 172 us -> 169 us (0.983)
  waiting for transfers between devices: 68.5 us -> 66.5 us
    ppermute x46, waiting for transfers between devices: 68.5 us -> 66.5 us  [swap(): return lax.ppermute(block, axis, [(i, i ^ offset) for i in range(count)])]
  transfers between devices with their start and end apart: 46 -> 46, of which waited for: 16 -> 17; matrix products, arithmetic and copies ran while one was open for 0% -> 0% of each run, Pallas kernels for 27% -> 27%
where the time goes in v23:
time: 169 us
  waiting for transfers between devices  66.5 us (39%)
  Pallas kernels  54.8 us (32%)
  starting transfers between devices  43.5 us (26%)
  between operations  3.78 us (2%)
    ppermute x46, waiting for transfers between devices, swap(): return lax.ppermute(block, axis, [(i, i ^ offset) for i in range(count)])  66.5 us
    ppermute x46, starting transfers between devices, swap(): return lax.ppermute(block, axis, [(i, i ^ offset) for i in range(count)])  43.5 us
    pallas_call x4, Pallas kernels, gradient(): pl.pallas_call(functools.partial(grad_kernel, len(flipped), base is not N...  13.5 us
    pallas_call x2, Pallas kernels, adam_rows(): pl.pallas_call(functools.partial(adam_kernel, len(squares), len(into)), o...  12 us
    pallas_call x4, Pallas kernels, pack(): pl.pallas_call(functools.partial(pack_kernel, offsets), out_shape=[pltpu....  9.16 us
    pallas_call x3, Pallas kernels, due_columns(): pl.pallas_call(functools.partial(pick_kernel, blocks), out_shape=[jax.Sha...  5.55 us
    pallas_call x8, Pallas kernels, partial_keys(): pl.pallas_call(functools.partial(partial_kernel, pieces, [first for _, fi...  4.58 us
    pallas_call x1, Pallas kernels, cast_left(): pl.pallas_call(cast_kernel, out_shape=jax.ShapeDtypeStruct((rows, width),...  3.46 us
  transfers between devices with their start and end apart: 46, of which 17 were waited for; matrix products, arithmetic and copies ran while one was open for 0% of the time, Pallas kernels for 27%

profile of v23, /device:TPU:0, one launch (start us, length us, event | category | flops | bytes accessed | tf_op | source)
XLA Modules:
  0.0 169.0 jit_solution(3599273187174239193)
XLA Ops:
  0.6 2.0 %pack.5 = bf16[256,1536]{1,0:T(8,128)(2,1)} custom-call(s32[1]{0:T(128)} %bitcast.4.me_ref, bf16[256,12288]{1,0:T(8,128)(2,1)} %bitcast.64), custom_call_target="tpu_custom_call" | custom-call | bytes 1572864 | tf_op jit(solution)/shard_map/pack/pallas_call | solution.py:69
  2.6 4.0 %collective-permute-start = (bf16[256,1536]{1,0:T(8,128)(2,1)}, bf16[256,1536]{1,0:T(8,128)(2,1)S(1)}, u32[]{:S(2)}, u32[]{:S(2)}) collective-permute-start(bf16[256,1536]{1,0:T(8,128)(2,1)} %pack.5), channel_id=1, source_target_pairs={{0,6},{1,7},{2,4},{3,5},{4,2},{5,3},{6,0},{7,1},{8,14},{9,15},{10,... | collective-permute-start | bytes 2359304 | tf_op jit(solution)/shard_map/ppermute | solution.py:458
  6.6 2.6 %pack.4 = (bf16[256,1536]{1,0:T(8,128)(2,1)}, bf16[256,1536]{1,0:T(8,128)(2,1)}, bf16[256,1536]{1,0:T(8,128)(2,1)}) custom-call(s32[1]{0:T(128)} %bitcast.4.me_ref, bf16[256,12288]{1,0:T(8,128)(2,1)} %bitcast.65), custom_call_target="tpu_custom_call" | custom-call | bytes 4718592 | tf_op jit(solution)/shard_map/pack/pallas_call | solution.py:69
  10.0 1.8 %due_columns.4.w_ref = f32[4,384,128]{2,1,0:T(8,128)S(1)} custom-call(s32[2]{0:T(128)S(1)} %pad_add_fusion.place_ref, f32[1536,1024]{1,0:T(8,128)} %bitcast.35, f32[1536,1024]{1,0:T(8,128)} %bitcast.36, f32[1536,1024]{1,0:T(8,128)} %bitcast.37, f32[1536,1024]{1,0:T(8,128)} %bitcast.38), custom_call_target="tpu_custom_call" | custom-call | bytes 1572864 | tf_op jit(solution)/shard_map/due_columns/pallas_call | solution.py:348
  11.9 1.6 collective-permute-start.1
  13.5 2.5 %collective-permute-start.3 = (f32[384,128]{1,0:T(8,128)S(1)}, f32[384,128]{1,0:T(8,128)S(1)}, u32[]{:S(2)}, u32[]{:S(2)}) collective-permute-start(f32[384,128]{1,0:T(8,128)S(1)} %get-tuple-element.133), channel_id=1, source_target_pairs={{0,24},{8,16},{16,8},{24,0},{1,25},{9,17},{17,9},{25,1},{2,26},{10... | collective-permute-start | bytes 589832 | tf_op jit(solution)/shard_map/ppermute | solution.py:458
  16.1 1.6 due_columns.3
  17.7 1.5 collective-permute-done.1
  19.2 6.8 %collective-permute-done.3 = f32[384,128]{1,0:T(8,128)S(1)} collective-permute-done((f32[384,128]{1,0:T(8,128)S(1)}, f32[384,128]{1,0:T(8,128)S(1)}, u32[]{:S(2)}, u32[]{:S(2)}) %collective-permute-start.3) | collective-permute-done | bytes 196640 | tf_op jit(solution)/shard_map/ppermute | solution.py:458
  26.0 8.1 %collective-permute-done.2 = f32[384,128]{1,0:T(8,128)S(1)} collective-permute-done((f32[384,128]{1,0:T(8,128)S(1)}, f32[384,128]{1,0:T(8,128)S(1)}, u32[]{:S(2)}, u32[]{:S(2)}) %collective-permute-start.2) | collective-permute-done | bytes 196640 | tf_op jit(solution)/shard_map/ppermute | solution.py:458
  34.2 1.6 collective-permute-start.4
  35.8 5.9 %collective-permute-done.10.refs_0_.refs_1_.refs_2_.refs_3_ = bf16[256,1536]{1,0:T(8,128)(2,1)S(1)} collective-permute-done((bf16[256,1536]{1,0:T(8,128)(2,1)}, bf16[256,1536]{1,0:T(8,128)(2,1)S(1)}, u32[]{:S(2)}, u32[]{:S(2)}) %collective-permute-start.10) | collective-permute-done | bytes 786464 | tf_op jit(solution)/shard_map/ppermute | solution.py:458
  42.2 3.6 %collective-permute-start.7 = (f32[384,128]{1,0:T(8,128)S(1)}, f32[384,128]{1,0:T(8,128)S(1)}, u32[]{:S(2)}, u32[]{:S(2)}) collective-permute-start(f32[384,128]{1,0:T(8,128)S(1)} %get-tuple-element.130.refs_3_), channel_id=1, source_target_pairs={{0,24},{8,16},{16,8},{24,0},{1,25},{9,17},{17,9},{25,1},{2,26},{10... | collective-permute-start | bytes 589832 | tf_op jit(solution)/shard_map/ppermute | solution.py:458
  45.8 0.8 collective-permute-start.5
  46.6 2.3 %pack.6 = (bf16[256,1536]{1,0:T(8,128)(2,1)}, bf16[256,1536]{1,0:T(8,128)(2,1)}) custom-call(s32[1]{0:T(128)} %bitcast.4.me_ref, bf16[256,12288]{1,0:T(8,128)(2,1)} %bitcast.66), custom_call_target="tpu_custom_call" | custom-call | bytes 3145728 | tf_op jit(solution)/shard_map/pack/pallas_call | solution.py:69
  48.9 2.7 %collective-permute-done.7.refs_6_ = f32[384,128]{1,0:T(8,128)S(1)} collective-permute-done((f32[384,128]{1,0:T(8,128)S(1)}, f32[384,128]{1,0:T(8,128)S(1)}, u32[]{:S(2)}, u32[]{:S(2)}) %collective-permute-start.7) | collective-permute-done | bytes 196640 | tf_op jit(solution)/shard_map/ppermute | solution.py:458
  51.6 11.7 %collective-permute-done.6.refs_5_ = f32[384,128]{1,0:T(8,128)S(1)} collective-permute-done((f32[384,128]{1,0:T(8,128)S(1)}, f32[384,128]{1,0:T(8,128)S(1)}, u32[]{:S(2)}, u32[]{:S(2)}) %collective-permute-start.6) | collective-permute-done | bytes 196640 | tf_op jit(solution)/shard_map/ppermute | solution.py:458
  63.3 0.8 collective-permute-start.8
  64.1 1.1 collective-permute-start.14
  65.2 3.5 %cast_left.1.refs_4_ = bf16[1536,512]{1,0:T(8,128)(2,1)S(1)} custom-call(f32[1536,1024]{1,0:T(8,128)} %bitcast.39), custom_call_target="tpu_custom_call" | custom-call | bytes 4718592 | tf_op jit(solution)/shard_map/cast_left/pallas_call | solution.py:93
  68.6 0.6 partial_keys.9
  69.4 2.3 %pack.7 = (bf16[256,1536]{1,0:T(8,128)(2,1)}, bf16[256,1536]{1,0:T(8,128)(2,1)}) custom-call(s32[1]{0:T(128)} %bitcast.4.me_ref, bf16[256,12288]{1,0:T(8,128)(2,1)} %bitcast.67), custom_call_target="tpu_custom_call" | custom-call | bytes 3145728 | tf_op jit(solution)/shard_map/pack/pallas_call | solution.py:69
  73.1 2.8 %duplicate.1 = (f32[384,1024]{1,0:T(8,128)}, f32[384,1024]{1,0:T(8,128)}) custom-call(f32[384,1024]{1,0:T(8,128)} %refs_0_.3, f32[384,1024]{1,0:T(8,128)} %refs_1_.3), custom_call_target="tpu_custom_call" | custom-call | bytes 6291456 | tf_op jit(solution)/shard_map/duplicate/pallas_call | solution.py:389
  75.9 2.1 %due_columns.5 = (f32[4,384,128]{2,1,0:T(8,128)S(1)}, f32[4,384,128]{2,1,0:T(8,128)S(1)}) custom-call(s32[2]{0:T(128)S(1)} %pad_add_fusion.place_ref, f32[1536,1024]{1,0:T(8,128)} %bitcast.44, f32[1536,1024]{1,0:T(8,128)} %bitcast.45, f32[1536,1024]{1,0:T(8,128)} %bitcast.46, f32[1536,1024]{1,0:T(8,128)} %bitcast.47, f32[1536,1024]{1,0:T(8,128)} %bitcast.52, ...), custom_call_target="tpu_custom_call" | custom-call | bytes 3145728 | tf_op jit(solution)/shard_map/due_columns/pallas_call | solution.py:348
  78.1 4.9 %collective-permute-done.8.refs_0_.refs_1_.refs_2_.refs_3_ = bf16[256,1536]{1,0:T(8,128)(2,1)S(1)} collective-permute-done((bf16[256,1536]{1,0:T(8,128)(2,1)}, bf16[256,1536]{1,0:T(8,128)(2,1)S(1)}, u32[]{:S(2)}, u32[]{:S(2)}) %collective-permute-start.8) | collective-permute-done | bytes 786464 | tf_op jit(solution)/shard_map/ppermute | solution.py:458
  84.1 0.6 partial_keys.12
  84.9 0.6 partial_keys.10
  85.5 1.3 collective-permute-start.12
  86.8 0.8 collective-permute-start.16
  87.6 3.7 %collective-permute-done.12.refs_6_ = bf16[128,512]{1,0:T(8,128)(2,1)S(1)} collective-permute-done((bf16[128,512]{1,0:T(8,128)(2,1)S(1)}, bf16[128,512]{1,0:T(8,128)(2,1)S(1)}, u32[]{:S(2)}, u32[]{:S(2)}) %collective-permute-start.12) | collective-permute-done | bytes 131104 | tf_op jit(solution)/shard_map/ppermute | solution.py:458
  91.4 0.6 partial_keys.11
  92.0 0.6 partial_keys.13
  92.5 1.0 collective-permute-start.22
  93.5 0.9 collective-permute-start.24
  94.4 6.1 %collective-permute-done.22.refs_4_ = bf16[256,512]{1,0:T(8,128)(2,1)S(1)} collective-permute-done((bf16[256,512]{1,0:T(8,128)(2,1)S(1)}, bf16[256,512]{1,0:T(8,128)(2,1)S(1)}, u32[]{:S(2)}, u32[]{:S(2)}) %collective-permute-start.22) | collective-permute-done | bytes 262176 | tf_op jit(solution)/shard_map/ppermute | solution.py:458
  100.5 0.9 collective-permute-start.27
  101.4 1.5 collective-permute-start.28
  103.6 0.6 collective-permute-start.17
  104.3 1.2 collective-permute-done.27
  105.5 0.8 collective-permute-start.18
  107.0 5.3 %collective-permute-done.17.refs_0_ = bf16[256,512]{1,0:T(8,128)(2,1)S(1)} collective-permute-done((bf16[256,512]{1,0:T(8,128)(2,1)S(1)}, bf16[256,512]{1,0:T(8,128)(2,1)S(1)}, u32[]{:S(2)}, u32[]{:S(2)}) %collective-permute-start.17) | collective-permute-done | bytes 262176 | tf_op jit(solution)/shard_map/ppermute | solution.py:458
  112.3 0.6 partial_keys.15
  113.4 1.3 collective-permute-start.34
  114.9 1.6 collective-permute-start.31
  116.5 3.2 %gradient.4.refs_8_ = f32[1536,512]{1,0:T(8,128)S(1)} custom-call(s32[2]{0:T(128)S(1)} %pad_add_fusion.place_ref, bf16[1536,256]{1,0:T(8,128)(2,1)S(1)} %get-tuple-element.100.refs_0_, bf16[1536,256]{1,0:T(8,128)(2,1)S(1)} %get-tuple-element.101.refs_1_, bf16[1536,256]{1,0:T(8,128)(2,1)S(1)} %get-tuple-element.102.refs_2_, ...), custom_call_target="tpu_custom_call" | custom-call | flops 1610612736 | bytes 6291456 | tf_op jit(solution)/shard_map/gradient/pallas_call | solution.py:236
  119.7 0.8 collective-permute-start.21
  120.5 3.6 %gradient.5 = (f32[1536,512]{1,0:T(8,128)S(1)}, f32[8,128]{1,0:T(8,128)S(1)}, f32[1536,128]{1,0:T(8,128)S(1)}) custom-call(s32[2]{0:T(128)S(1)} %pad_add_fusion.place_ref, bf16[1536,256]{1,0:T(8,128)(2,1)S(1)} %get-tuple-element.78.refs_0_, bf16[1536,256]{1,0:T(8,128)(2,1)S(1)} %get-tuple-element.79.refs_1_, ...), custom_call_target="tpu_custom_call" | custom-call | flops 1610612736 | bytes 6291456 | tf_op jit(solution)/shard_map/gradient/pallas_call | solution.py:236
  124.1 4.6 %collective-permute-done.31.refs_6_ = bf16[256,512]{1,0:T(8,128)(2,1)S(1)} collective-permute-done((bf16[256,512]{1,0:T(8,128)(2,1)S(1)}, bf16[256,512]{1,0:T(8,128)(2,1)S(1)}, u32[]{:S(2)}, u32[]{:S(2)}) %collective-permute-start.31) | collective-permute-done | bytes 262176 | tf_op jit(solution)/shard_map/ppermute | solution.py:458
  129.3 3.2 %gradient.6.refs_8_ = f32[1536,512]{1,0:T(8,128)S(1)} custom-call(s32[2]{0:T(128)S(1)} %pad_add_fusion.place_ref, bf16[1536,256]{1,0:T(8,128)(2,1)S(1)} %get-tuple-element.100.refs_0_, bf16[1536,256]{1,0:T(8,128)(2,1)S(1)} %get-tuple-element.101.refs_1_, bf16[1536,256]{1,0:T(8,128)(2,1)S(1)} %get-tuple-element.102.refs_2_, ...), custom_call_target="tpu_custom_call" | custom-call | flops 1610612736 | bytes 6291456 | tf_op jit(solution)/shard_map/gradient/pallas_call | solution.py:236
  132.5 3.6 %gradient.7 = (f32[1536,512]{1,0:T(8,128)S(1)}, f32[8,128]{1,0:T(8,128)S(1)}, f32[1536,128]{1,0:T(8,128)S(1)}) custom-call(s32[2]{0:T(128)S(1)} %pad_add_fusion.place_ref, bf16[1536,256]{1,0:T(8,128)(2,1)S(1)} %get-tuple-element.78.refs_0_, bf16[1536,256]{1,0:T(8,128)(2,1)S(1)} %get-tuple-element.79.refs_1_, ...), custom_call_target="tpu_custom_call" | custom-call | flops 1610612736 | bytes 6291456 | tf_op jit(solution)/shard_map/gradient/pallas_call | solution.py:236
  136.2 1.1 collective-permute-done.36
  137.3 1.2 collective-permute-start.39
  138.6 1.4 collective-permute-start.38
  140.0 0.8 collective-permute-start.37
  140.8 1.0 collective-permute-done.39.refs_3_
  142.2 1.4 collective-permute-done.37.refs_1_
  143.6 1.5 adam_frag.1
  145.2 2.8 %collective-permute-start.41 = (bf16[384,128]{1,0:T(8,128)(2,1)S(1)}, bf16[384,128]{1,0:T(8,128)(2,1)S(1)}, u32[]{:S(2)}, u32[]{:S(2)}) collective-permute-start(bf16[384,128]{1,0:T(8,128)(2,1)S(1)} %get-tuple-element.119), channel_id=1, source_target_pairs={{0,16},{8,24},{16,0},{24,8},{1,17},{9,25},{17,1},{25,9},{2,18},{10... | collective-permute-start | bytes 294920 | tf_op jit(solution)/shard_map/ppermute | solution.py:458
  148.1 1.5 collective-permute-start.42
  149.7 6.0 %adam_rows.2 = (f32[1536,1024]{1,0:T(8,128)}, f32[1536,1024]{1,0:T(8,128)}, f32[1536,1024]{1,0:T(8,128)}, f32[8,128]{1,0:T(8,128)S(1)}) custom-call(f32[3]{0:T(128)S(1)} %pad_maximum_fusion.sc_ref, f32[1536,1024]{1,0:T(8,128)S(1)} %bitcast.42, f32[1536,1024]{1,0:T(8,128)S(1)} %bitcast.50, f32[1536,1024]{1,0:T(8,128)S(1)} %bitcast.58, ...), custom_call_target="tpu_custom_call" | custom-call | flops 15728640 | bytes 22020096 | tf_op jit(solution)/shard_map/adam_rows/pallas_call | solution.py:291
  155.8 2.3 %collective-permute-start.45 = (bf16[384,128]{1,0:T(8,128)(2,1)S(1)}, bf16[384,128]{1,0:T(8,128)(2,1)S(1)}, u32[]{:S(2)}, u32[]{:S(2)}) collective-permute-start(bf16[384,128]{1,0:T(8,128)(2,1)S(1)} %convert_element_type.24.refs_7_), channel_id=1, source_target_pairs={{0,24},{8,16},{16,8},{24,0},{1,25},{9,17},{17,9},{25,1},{2,26},{10... | collective-permute-start | bytes 294920 | tf_op jit(solution)/shard_map/ppermute | solution.py:458
  158.1 2.1 %collective-permute-start.43 = (bf16[384,128]{1,0:T(8,128)(2,1)S(1)}, bf16[384,128]{1,0:T(8,128)(2,1)S(1)}, u32[]{:S(2)}, u32[]{:S(2)}) collective-permute-start(bf16[384,128]{1,0:T(8,128)(2,1)S(1)} %convert_element_type.24.refs_7_), channel_id=1, source_target_pairs={{0,8},{8,0},{16,24},{24,16},{1,9},{9,1},{17,25},{25,17},{2,10},{10... | collective-permute-start | bytes 294920 | tf_op jit(solution)/shard_map/ppermute | solution.py:458
  160.2 6.0 %adam_rows.3 = (f32[1536,1024]{1,0:T(8,128)}, f32[1536,1024]{1,0:T(8,128)}, f32[1536,1024]{1,0:T(8,128)}) custom-call(f32[3]{0:T(128)S(1)} %pad_maximum_fusion.sc_ref, f32[1536,1024]{1,0:T(8,128)S(1)} %bitcast.43, f32[1536,1024]{1,0:T(8,128)S(1)} %bitcast.51, ...), custom_call_target="tpu_custom_call", output_to_operand_aliasing={{0}: (10, {}), {1}: (11, {}), {2}: (12, {})} | custom-call | flops 15728640 | bytes 22020096 | tf_op jit(solution)/shard_map/adam_rows/pallas_call | solution.py:291
  166.3 1.7 outer_step.1
  (89 shorter events, 6.5 us)
Async XLA Ops:
  2.6 31.6 %collective-permute-start = (bf16[256,1536]{1,0:T(8,128)(2,1)}, bf16[256,1536]{1,0:T(8,128)(2,1)S(1)}, u32[]{:S(2)}, u32[]{:S(2)}) collective-permute-start(bf16[256,1536]{1,0:T(8,128)(2,1)} %pack.5), channel_id=1, source_target_pairs={{0,6},{1,7},{2,4},{3,5},{4,2},{5,3},{6,0},{7,1},{8,14},{9,15},{10,... | collective-permute-start | bytes 2359304 | tf_op jit(solution)/shard_map/ppermute | solution.py:458
  9.2 32.5 %collective-permute-start.10 = (bf16[256,1536]{1,0:T(8,128)(2,1)}, bf16[256,1536]{1,0:T(8,128)(2,1)S(1)}, u32[]{:S(2)}, u32[]{:S(2)}) collective-permute-start(bf16[256,1536]{1,0:T(8,128)(2,1)} %get-tuple-element.75), channel_id=1, source_target_pairs={{0,7},{1,6},{2,5},{3,4},{4,3},{5,2},{6,1},{7,0},{8,15},{9,14},{10,... | collective-permute-start | bytes 2359304 | tf_op jit(solution)/shard_map/ppermute | solution.py:458
  10.0 24.2 %copy-start.3 = (bf16[256,1536]{1,0:T(8,128)(2,1)S(1)}, bf16[256,1536]{1,0:T(8,128)(2,1)}, u32[]{:S(2)}) copy-start(bf16[256,1536]{1,0:T(8,128)(2,1)} %get-tuple-element.70) | copy-start | bytes 2359300
  10.0 31.7 %copy-start.2 = (bf16[256,1536]{1,0:T(8,128)(2,1)S(1)}, bf16[256,1536]{1,0:T(8,128)(2,1)}, u32[]{:S(2)}) copy-start(bf16[256,1536]{1,0:T(8,128)(2,1)} %get-tuple-element.81) | copy-start | bytes 2359300
  11.9 7.3 %collective-permute-start.1 = (f32[384,128]{1,0:T(8,128)S(1)}, f32[384,128]{1,0:T(8,128)S(1)}, u32[]{:S(2)}, u32[]{:S(2)}) collective-permute-start(f32[384,128]{1,0:T(8,128)S(1)} %get-tuple-element.132), channel_id=1, source_target_pairs={{0,8},{8,0},{16,24},{24,16},{1,9},{9,1},{17,25},{25,17},{2,10},{10... | collective-permute-start | bytes 589832 | tf_op jit(solution)/shard_map/ppermute | solution.py:458
  13.5 12.4 %collective-permute-start.3 = (f32[384,128]{1,0:T(8,128)S(1)}, f32[384,128]{1,0:T(8,128)S(1)}, u32[]{:S(2)}, u32[]{:S(2)}) collective-permute-start(f32[384,128]{1,0:T(8,128)S(1)} %get-tuple-element.133), channel_id=1, source_target_pairs={{0,24},{8,16},{16,8},{24,0},{1,25},{9,17},{17,9},{25,1},{2,26},{10... | collective-permute-start | bytes 589832 | tf_op jit(solution)/shard_map/ppermute | solution.py:458
  16.0 18.1 %collective-permute-start.2 = (f32[384,128]{1,0:T(8,128)S(1)}, f32[384,128]{1,0:T(8,128)S(1)}, u32[]{:S(2)}, u32[]{:S(2)}) collective-permute-start(f32[384,128]{1,0:T(8,128)S(1)} %get-tuple-element.134), channel_id=1, source_target_pairs={{0,16},{8,24},{16,0},{24,8},{1,17},{9,25},{17,1},{25,9},{2,18},{10... | collective-permute-start | bytes 589832 | tf_op jit(solution)/shard_map/ppermute | solution.py:458
  34.2 29.1 %collective-permute-start.4 = (bf16[256,1536]{1,0:T(8,128)(2,1)S(1)}, bf16[256,1536]{1,0:T(8,128)(2,1)S(1)}, u32[]{:S(2)}, u32[]{:S(2)}) collective-permute-start(bf16[256,1536]{1,0:T(8,128)(2,1)S(1)} %copy-done.3), channel_id=1, source_target_pairs={{0,2},{1,3},{2,0},{3,1},{4,6},{5,7},{6,4},{7,5},{8,10},{9,11},{10,... | collective-permute-start | bytes 2359304 | tf_op jit(solution)/shard_map/ppermute | solution.py:458
  41.7 22.4 %collective-permute-start.13 = (bf16[256,1536]{1,0:T(8,128)(2,1)S(1)}, bf16[256,1536]{1,0:T(8,128)(2,1)S(1)}, u32[]{:S(2)}, u32[]{:S(2)}) collective-permute-start(bf16[256,1536]{1,0:T(8,128)(2,1)S(1)} %copy-done.2), channel_id=1, source_target_pairs={{0,4},{1,5},{2,6},{3,7},{4,0},{5,1},{6,2},{7,3},{8,12},{9,13},{10,... | collective-permute-start | bytes 2359304 | tf_op jit(solution)/shard_map/ppermute | solution.py:458
  42.2 9.4 %collective-permute-start.7 = (f32[384,128]{1,0:T(8,128)S(1)}, f32[384,128]{1,0:T(8,128)S(1)}, u32[]{:S(2)}, u32[]{:S(2)}) collective-permute-start(f32[384,128]{1,0:T(8,128)S(1)} %get-tuple-element.130.refs_3_), channel_id=1, source_target_pairs={{0,24},{8,16},{16,8},{24,0},{1,25},{9,17},{17,9},{25,1},{2,26},{10... | collective-permute-start | bytes 589832 | tf_op jit(solution)/shard_map/ppermute | solution.py:458
  45.8 17.5 %collective-permute-start.6 = (f32[384,128]{1,0:T(8,128)S(1)}, f32[384,128]{1,0:T(8,128)S(1)}, u32[]{:S(2)}, u32[]{:S(2)}) collective-permute-start(f32[384,128]{1,0:T(8,128)S(1)} %get-tuple-element.130.refs_3_), channel_id=1, source_target_pairs={{0,16},{8,24},{16,0},{24,8},{1,17},{9,25},{17,1},{25,9},{2,18},{10... | collective-permute-start | bytes 589832 | tf_op jit(solution)/shard_map/ppermute | solution.py:458
  45.8 17.5 %collective-permute-start.5 = (f32[384,128]{1,0:T(8,128)S(1)}, f32[384,128]{1,0:T(8,128)S(1)}, u32[]{:S(2)}, u32[]{:S(2)}) collective-permute-start(f32[384,128]{1,0:T(8,128)S(1)} %get-tuple-element.130.refs_3_), channel_id=1, source_target_pairs={{0,8},{8,0},{16,24},{24,16},{1,9},{9,1},{17,25},{25,17},{2,10},{10... | collective-permute-start | bytes 589832 | tf_op jit(solution)/shard_map/ppermute | solution.py:458
  63.3 19.7 %collective-permute-start.8 = (bf16[256,1536]{1,0:T(8,128)(2,1)}, bf16[256,1536]{1,0:T(8,128)(2,1)S(1)}, u32[]{:S(2)}, u32[]{:S(2)}) collective-permute-start(bf16[256,1536]{1,0:T(8,128)(2,1)} %get-tuple-element.73), channel_id=1, source_target_pairs={{0,3},{1,2},{2,1},{3,0},{4,7},{5,6},{6,5},{7,4},{8,11},{9,10},{10,... | collective-permute-start | bytes 2359304 | tf_op jit(solution)/shard_map/ppermute | solution.py:458
  64.1 20.0 %collective-permute-start.14 = (bf16[256,1536]{1,0:T(8,128)(2,1)}, bf16[256,1536]{1,0:T(8,128)(2,1)S(1)}, u32[]{:S(2)}, u32[]{:S(2)}) collective-permute-start(bf16[256,1536]{1,0:T(8,128)(2,1)} %get-tuple-element.83), channel_id=1, source_target_pairs={{0,5},{1,4},{2,7},{3,6},{4,1},{5,0},{6,3},{7,2},{8,13},{9,12},{10,... | collective-permute-start | bytes 2359304 | tf_op jit(solution)/shard_map/ppermute | solution.py:458
  69.2 15.6 %collective-permute-start.11 = (bf16[256,512]{1,0:T(8,128)(2,1)S(1)}, bf16[256,512]{1,0:T(8,128)(2,1)S(1)}, u32[]{:S(2)}, u32[]{:S(2)}) collective-permute-start(bf16[256,512]{1,0:T(8,128)(2,1)S(1)} %get-tuple-element.76), channel_id=1, source_target_pairs={{0,1},{1,0},{2,3},{3,2},{4,5},{5,4},{6,7},{7,6},{8,9},{9,8},{10,11... | collective-permute-start | bytes 786440 | tf_op jit(solution)/shard_map/ppermute | solution.py:458
  71.7 31.2 %collective-permute-start.19 = (bf16[256,1536]{1,0:T(8,128)(2,1)}, bf16[256,1536]{1,0:T(8,128)(2,1)S(1)}, u32[]{:S(2)}, u32[]{:S(2)}) collective-permute-start(bf16[256,1536]{1,0:T(8,128)(2,1)} %get-tuple-element.96), channel_id=1, source_target_pairs={{0,1},{1,0},{2,3},{3,2},{4,5},{5,4},{6,7},{7,6},{8,9},{9,8},{10,11... | collective-permute-start | bytes 2359304 | tf_op jit(solution)/shard_map/ppermute | solution.py:458
  78.1 9.6 %copy-start.1 = (bf16[1,256,1024]{2,1,0:T(8,128)(2,1)S(1)}, bf16[1,256,1024]{2,1,0:T(8,128)(2,1)}, u32[]{:S(2)}) copy-start(bf16[1,256,1024]{2,1,0:T(8,128)(2,1)} %param.10) | copy-start | bytes 1572868
  83.6 7.8 %collective-permute-start.9 = (bf16[256,512]{1,0:T(8,128)(2,1)S(1)}, bf16[256,512]{1,0:T(8,128)(2,1)S(1)}, u32[]{:S(2)}, u32[]{:S(2)}) collective-permute-start(bf16[256,512]{1,0:T(8,128)(2,1)S(1)} %get-tuple-element.74), channel_id=1, source_target_pairs={{0,1},{1,0},{2,3},{3,2},{4,5},{5,4},{6,7},{7,6},{8,9},{9,8},{10,11... | collective-permute-start | bytes 786440 | tf_op jit(solution)/shard_map/ppermute | solution.py:458
  84.7 7.3 %collective-permute-start.15 = (bf16[256,512]{1,0:T(8,128)(2,1)S(1)}, bf16[256,512]{1,0:T(8,128)(2,1)S(1)}, u32[]{:S(2)}, u32[]{:S(2)}) collective-permute-start(bf16[256,512]{1,0:T(8,128)(2,1)S(1)} %get-tuple-element.89), channel_id=1, source_target_pairs={{0,1},{1,0},{2,3},{3,2},{4,5},{5,4},{6,7},{7,6},{8,9},{9,8},{10,11... | collective-permute-start | bytes 786440 | tf_op jit(solution)/shard_map/ppermute | solution.py:458
  85.5 5.9 %collective-permute-start.12 = (bf16[128,512]{1,0:T(8,128)(2,1)S(1)}, bf16[128,512]{1,0:T(8,128)(2,1)S(1)}, u32[]{:S(2)}, u32[]{:S(2)}) collective-permute-start(bf16[128,512]{1,0:T(8,128)(2,1)S(1)} %get-tuple-element.77), channel_id=1, source_target_pairs={{0,4},{1,5},{2,6},{3,7},{4,0},{5,1},{6,2},{7,3},{8,12},{9,13},{10,... | collective-permute-start | bytes 393224 | tf_op jit(solution)/shard_map/ppermute | solution.py:458
  86.8 5.2 %collective-permute-start.16 = (bf16[128,512]{1,0:T(8,128)(2,1)S(1)}, bf16[128,512]{1,0:T(8,128)(2,1)S(1)}, u32[]{:S(2)}, u32[]{:S(2)}) collective-permute-start(bf16[128,512]{1,0:T(8,128)(2,1)S(1)} %get-tuple-element.90), channel_id=1, source_target_pairs={{0,2},{1,3},{2,0},{3,1},{4,6},{5,7},{6,4},{7,5},{8,10},{9,11},{10,... | collective-permute-start | bytes 393224 | tf_op jit(solution)/shard_map/ppermute | solution.py:458
  91.9 20.4 %copy-start = (bf16[256,1536]{1,0:T(8,128)(2,1)S(1)}, bf16[256,1536]{1,0:T(8,128)(2,1)}, u32[]{:S(2)}) copy-start(bf16[256,1536]{1,0:T(8,128)(2,1)} %get-tuple-element.95.refs_0_.refs_1_.refs_2_.refs_3_) | copy-start | bytes 2359300
  92.5 7.9 %collective-permute-start.22 = (bf16[256,512]{1,0:T(8,128)(2,1)S(1)}, bf16[256,512]{1,0:T(8,128)(2,1)S(1)}, u32[]{:S(2)}, u32[]{:S(2)}) collective-permute-start(bf16[256,512]{1,0:T(8,128)(2,1)S(1)} %slice.32.refs_4_), channel_id=1, source_target_pairs={{0,2},{1,3},{2,0},{3,1},{4,6},{5,7},{6,4},{7,5},{8,10},{9,11},{10,... | collective-permute-start | bytes 786440 | tf_op jit(solution)/shard_map/ppermute | solution.py:458
  93.5 7.8 %collective-permute-start.24 = (bf16[256,512]{1,0:T(8,128)(2,1)S(1)}, bf16[256,512]{1,0:T(8,128)(2,1)S(1)}, u32[]{:S(2)}, u32[]{:S(2)}) collective-permute-start(bf16[256,512]{1,0:T(8,128)(2,1)S(1)} %slice.32.refs_4_), channel_id=1, source_target_pairs={{0,4},{1,5},{2,6},{3,7},{4,0},{5,1},{6,2},{7,3},{8,12},{9,13},{10,... | collective-permute-start | bytes 786440 | tf_op jit(solution)/shard_map/ppermute | solution.py:458
  100.5 5.0 %collective-permute-start.27 = (bf16[128,512]{1,0:T(8,128)(2,1)S(1)}, bf16[128,512]{1,0:T(8,128)(2,1)S(1)}, u32[]{:S(2)}, u32[]{:S(2)}) collective-permute-start(bf16[128,512]{1,0:T(8,128)(2,1)S(1)} %slice.33), channel_id=1, source_target_pairs={{0,4},{1,5},{2,6},{3,7},{4,0},{5,1},{6,2},{7,3},{8,12},{9,13},{10,... | collective-permute-start | bytes 393224 | tf_op jit(solution)/shard_map/ppermute | solution.py:458
  101.4 5.0 %collective-permute-start.28 = (bf16[128,512]{1,0:T(8,128)(2,1)S(1)}, bf16[128,512]{1,0:T(8,128)(2,1)S(1)}, u32[]{:S(2)}, u32[]{:S(2)}) collective-permute-start(bf16[128,512]{1,0:T(8,128)(2,1)S(1)} %slice.34), channel_id=1, source_target_pairs={{0,2},{1,3},{2,0},{3,1},{4,6},{5,7},{6,4},{7,5},{8,10},{9,11},{10,... | collective-permute-start | bytes 393224 | tf_op jit(solution)/shard_map/ppermute | solution.py:458
  103.5 3.0 %collective-permute-start.20 = (bf16[256,512]{1,0:T(8,128)(2,1)S(1)}, bf16[256,512]{1,0:T(8,128)(2,1)S(1)}, u32[]{:S(2)}, u32[]{:S(2)}) collective-permute-start(bf16[256,512]{1,0:T(8,128)(2,1)S(1)} %get-tuple-element.97), channel_id=1, source_target_pairs={{0,1},{1,0},{2,3},{3,2},{4,5},{5,4},{6,7},{7,6},{8,9},{9,8},{10,11... | collective-permute-start | bytes 786440 | tf_op jit(solution)/shard_map/ppermute | solution.py:458
  103.6 8.7 %collective-permute-start.17 = (bf16[256,512]{1,0:T(8,128)(2,1)S(1)}, bf16[256,512]{1,0:T(8,128)(2,1)S(1)}, u32[]{:S(2)}, u32[]{:S(2)}) collective-permute-start(bf16[256,512]{1,0:T(8,128)(2,1)S(1)} %get-tuple-element.93), channel_id=1, source_target_pairs={{0,2},{1,3},{2,0},{3,1},{4,6},{5,7},{6,4},{7,5},{8,10},{9,11},{10,... | collective-permute-start | bytes 786440 | tf_op jit(solution)/shard_map/ppermute | solution.py:458
  104.2 10.5 %collective-permute-start.26 = (bf16[256,512]{1,0:T(8,128)(2,1)S(1)}, bf16[256,512]{1,0:T(8,128)(2,1)S(1)}, u32[]{:S(2)}, u32[]{:S(2)}) collective-permute-start(bf16[256,512]{1,0:T(8,128)(2,1)S(1)} %slice.32.refs_4_), channel_id=1, source_target_pairs={{0,1},{1,0},{2,3},{3,2},{4,5},{5,4},{6,7},{7,6},{8,9},{9,8},{10,11... | collective-permute-start | bytes 786440 | tf_op jit(solution)/shard_map/ppermute | solution.py:458
  105.5 7.4 %collective-permute-start.18 = (bf16[256,512]{1,0:T(8,128)(2,1)S(1)}, bf16[256,512]{1,0:T(8,128)(2,1)S(1)}, u32[]{:S(2)}, u32[]{:S(2)}) collective-permute-start(bf16[256,512]{1,0:T(8,128)(2,1)S(1)} %get-tuple-element.94), channel_id=1, source_target_pairs={{0,4},{1,5},{2,6},{3,7},{4,0},{5,1},{6,2},{7,3},{8,12},{9,13},{10,... | collective-permute-start | bytes 786440 | tf_op jit(solution)/shard_map/ppermute | solution.py:458
  106.4 8.5 %collective-permute-start.29 = (bf16[256,512]{1,0:T(8,128)(2,1)S(1)}, bf16[256,512]{1,0:T(8,128)(2,1)S(1)}, u32[]{:S(2)}, u32[]{:S(2)}) collective-permute-start(bf16[256,512]{1,0:T(8,128)(2,1)S(1)} %constant_dynamic-update-slice_fusion.refs_6_), channel_id=1, source_target_pairs={{0,1},{1,0},{2,3},{3,2},{4,5},{5,4},{6,7},{7,6},{8,9},{9,8},{10,11... | collective-permute-start | bytes 786440 | tf_op jit(solution)/shard_map/ppermute | solution.py:458
  106.5 13.2 %collective-permute-start.25 = (bf16[256,512]{1,0:T(8,128)(2,1)S(1)}, bf16[256,512]{1,0:T(8,128)(2,1)S(1)}, u32[]{:S(2)}, u32[]{:S(2)}) collective-permute-start(bf16[256,512]{1,0:T(8,128)(2,1)S(1)} %collective-permute-done.24.refs_6_), channel_id=1, source_target_pairs={{0,1},{1,0},{2,3},{3,2},{4,5},{5,4},{6,7},{7,6},{8,9},{9,8},{10,11... | collective-permute-start | bytes 786440 | tf_op jit(solution)/shard_map/ppermute | solution.py:458
  112.3 8.2 %collective-permute-start.23 = (bf16[256,512]{1,0:T(8,128)(2,1)S(1)}, bf16[256,512]{1,0:T(8,128)(2,1)S(1)}, u32[]{:S(2)}, u32[]{:S(2)}) collective-permute-start(bf16[256,512]{1,0:T(8,128)(2,1)S(1)} %collective-permute-done.22.refs_4_), channel_id=1, source_target_pairs={{0,1},{1,0},{2,3},{3,2},{4,5},{5,4},{6,7},{7,6},{8,9},{9,8},{10,11... | collective-permute-start | bytes 786440 | tf_op jit(solution)/shard_map/ppermute | solution.py:458
  112.3 37.3 %slice-start.4 = ((s8[6291456]{0:T(1024)(128)(4,1)}), s8[4194304]{0:T(1024)(128)(4,1)S(1)}, s32[]{:S(2)}) async-start(s8[6291456]{0:T(1024)(128)(4,1)} %bitcast.56), calls=%async_computation.4 | async-start | bytes 8388608
  113.4 10.6 %collective-permute-start.34 = (bf16[256,512]{1,0:T(8,128)(2,1)S(1)}, bf16[256,512]{1,0:T(8,128)(2,1)S(1)}, u32[]{:S(2)}, u32[]{:S(2)}) collective-permute-start(bf16[256,512]{1,0:T(8,128)(2,1)S(1)} %key_backward.1.refs_4_), channel_id=1, source_target_pairs={{0,6},{1,7},{2,4},{3,5},{4,2},{5,3},{6,0},{7,1},{8,14},{9,15},{10,... | collective-permute-start | bytes 786440 | tf_op jit(solution)/shard_map/ppermute | solution.py:458
  114.7 14.5 %collective-permute-start.33 = (bf16[256,512]{1,0:T(8,128)(2,1)S(1)}, bf16[256,512]{1,0:T(8,128)(2,1)S(1)}, u32[]{:S(2)}, u32[]{:S(2)}) collective-permute-start(bf16[256,512]{1,0:T(8,128)(2,1)S(1)} %key_backward.1.refs_4_), channel_id=1, source_target_pairs={{0,1},{1,0},{2,3},{3,2},{4,5},{5,4},{6,7},{7,6},{8,9},{9,8},{10,11... | collective-permute-start | bytes 786440 | tf_op jit(solution)/shard_map/ppermute | solution.py:458
  114.9 13.8 %collective-permute-start.31 = (bf16[256,512]{1,0:T(8,128)(2,1)S(1)}, bf16[256,512]{1,0:T(8,128)(2,1)S(1)}, u32[]{:S(2)}, u32[]{:S(2)}) collective-permute-start(bf16[256,512]{1,0:T(8,128)(2,1)S(1)} %key_backward.1.refs_4_), channel_id=1, source_target_pairs={{0,4},{1,5},{2,6},{3,7},{4,0},{5,1},{6,2},{7,3},{8,12},{9,13},{10,... | collective-permute-start | bytes 786440 | tf_op jit(solution)/shard_map/ppermute | solution.py:458
  119.7 9.0 %collective-permute-start.21 = (bf16[256,512]{1,0:T(8,128)(2,1)S(1)}, bf16[256,512]{1,0:T(8,128)(2,1)S(1)}, u32[]{:S(2)}, u32[]{:S(2)}) collective-permute-start(bf16[256,512]{1,0:T(8,128)(2,1)S(1)} %key_backward.1.refs_4_), channel_id=1, source_target_pairs={{0,2},{1,3},{2,0},{3,1},{4,6},{5,7},{6,4},{7,5},{8,10},{9,11},{10,... | collective-permute-start | bytes 786440 | tf_op jit(solution)/shard_map/ppermute | solution.py:458
  120.5 29.1 %slice-start.5 = ((s8[6291456]{0:T(1024)(128)(4,1)}), s8[2097152]{0:T(1024)(128)(4,1)S(1)}, s32[]{:S(2)}) async-start(s8[6291456]{0:T(1024)(128)(4,1)} %bitcast.56), calls=%async_computation.5 | async-start | bytes 4194304
  124.1 5.2 %collective-permute-start.35 = (bf16[256,512]{1,0:T(8,128)(2,1)S(1)}, bf16[256,512]{1,0:T(8,128)(2,1)S(1)}, u32[]{:S(2)}, u32[]{:S(2)}) collective-permute-start(bf16[256,512]{1,0:T(8,128)(2,1)S(1)} %collective-permute-done.34.refs_6_), channel_id=1, source_target_pairs={{0,1},{1,0},{2,3},{3,2},{4,5},{5,4},{6,7},{7,6},{8,9},{9,8},{10,11... | collective-permute-start | bytes 786440 | tf_op jit(solution)/shard_map/ppermute | solution.py:458
  128.7 3.7 %collective-permute-start.30 = (bf16[256,512]{1,0:T(8,128)(2,1)S(1)}, bf16[256,512]{1,0:T(8,128)(2,1)S(1)}, u32[]{:S(2)}, u32[]{:S(2)}) collective-permute-start(bf16[256,512]{1,0:T(8,128)(2,1)S(1)} %collective-permute-done.21.refs_4_), channel_id=1, source_target_pairs={{0,1},{1,0},{2,3},{3,2},{4,5},{5,4},{6,7},{7,6},{8,9},{9,8},{10,11... | collective-permute-start | bytes 786440 | tf_op jit(solution)/shard_map/ppermute | solution.py:458
  128.8 3.7 %collective-permute-start.32 = (bf16[256,512]{1,0:T(8,128)(2,1)S(1)}, bf16[256,512]{1,0:T(8,128)(2,1)S(1)}, u32[]{:S(2)}, u32[]{:S(2)}) collective-permute-start(bf16[256,512]{1,0:T(8,128)(2,1)S(1)} %collective-permute-done.31.refs_6_), channel_id=1, source_target_pairs={{0,1},{1,0},{2,3},{3,2},{4,5},{5,4},{6,7},{7,6},{8,9},{9,8},{10,11... | collective-permute-start | bytes 786440 | tf_op jit(solution)/shard_map/ppermute | solution.py:458
  129.2 20.4 %slice-start = ((s8[6291456]{0:T(1024)(128)(4,1)}), s8[4194304]{0:T(1024)(128)(4,1)S(1)}, s32[]{:S(2)}) async-start(s8[6291456]{0:T(1024)(128)(4,1)} %bitcast.40), calls=%async_computation | async-start | bytes 8388608
  129.2 20.4 %slice-start.2 = ((s8[6291456]{0:T(1024)(128)(4,1)}), s8[4194304]{0:T(1024)(128)(4,1)S(1)}, s32[]{:S(2)}) async-start(s8[6291456]{0:T(1024)(128)(4,1)} %bitcast.48), calls=%async_computation.2 | async-start | bytes 8388608
  132.5 17.2 %slice-start.1 = ((s8[6291456]{0:T(1024)(128)(4,1)}), s8[2097152]{0:T(1024)(128)(4,1)S(1)}, s32[]{:S(2)}) async-start(s8[6291456]{0:T(1024)(128)(4,1)} %bitcast.40), calls=%async_computation.1 | async-start | bytes 4194304
  132.5 17.1 %slice-start.3 = ((s8[6291456]{0:T(1024)(128)(4,1)}), s8[2097152]{0:T(1024)(128)(4,1)S(1)}, s32[]{:S(2)}) async-start(s8[6291456]{0:T(1024)(128)(4,1)} %bitcast.48), calls=%async_computation.3 | async-start | bytes 4194304
  136.1 1.2 collective-permute-start.36
  137.3 4.5 %collective-permute-start.39 = (f32[8,128]{1,0:T(8,128)S(1)}, f32[8,128]{1,0:T(8,128)S(1)}, u32[]{:S(2)}, u32[]{:S(2)}) collective-permute-start(f32[8,128]{1,0:T(8,128)S(1)} %add.32.refs_0_), channel_id=1, source_target_pairs={{0,6},{1,7},{2,4},{3,5},{4,2},{5,3},{6,0},{7,1},{8,14},{9,15},{10,... | collective-permute-start | bytes 12296 | tf_op jit(solution)/shard_map/ppermute | solution.py:458
  138.6 3.6 %collective-permute-start.38 = (f32[8,128]{1,0:T(8,128)S(1)}, f32[8,128]{1,0:T(8,128)S(1)}, u32[]{:S(2)}, u32[]{:S(2)}) collective-permute-start(f32[8,128]{1,0:T(8,128)S(1)} %add.32.refs_0_), channel_id=1, source_target_pairs={{0,4},{1,5},{2,6},{3,7},{4,0},{5,1},{6,2},{7,3},{8,12},{9,13},{10,... | collective-permute-start | bytes 12296 | tf_op jit(solution)/shard_map/ppermute | solution.py:458
  140.0 3.6 %collective-permute-start.37 = (f32[8,128]{1,0:T(8,128)S(1)}, f32[8,128]{1,0:T(8,128)S(1)}, u32[]{:S(2)}, u32[]{:S(2)}) collective-permute-start(f32[8,128]{1,0:T(8,128)S(1)} %add.32.refs_0_), channel_id=1, source_target_pairs={{0,2},{1,3},{2,0},{3,1},{4,6},{5,7},{6,4},{7,5},{8,10},{9,11},{10,... | collective-permute-start | bytes 12296 | tf_op jit(solution)/shard_map/ppermute | solution.py:458
  145.2 10.5 %collective-permute-start.40 = (bf16[384,128]{1,0:T(8,128)(2,1)S(1)}, bf16[384,128]{1,0:T(8,128)(2,1)S(1)}, u32[]{:S(2)}, u32[]{:S(2)}) collective-permute-start(bf16[384,128]{1,0:T(8,128)(2,1)S(1)} %get-tuple-element.118), channel_id=1, source_target_pairs={{0,8},{8,0},{16,24},{24,16},{1,9},{9,1},{17,25},{25,17},{2,10},{10... | collective-permute-start | bytes 294920 | tf_op jit(solution)/shard_map/ppermute | solution.py:458
  145.2 10.5 %collective-permute-start.41 = (bf16[384,128]{1,0:T(8,128)(2,1)S(1)}, bf16[384,128]{1,0:T(8,128)(2,1)S(1)}, u32[]{:S(2)}, u32[]{:S(2)}) collective-permute-start(bf16[384,128]{1,0:T(8,128)(2,1)S(1)} %get-tuple-element.119), channel_id=1, source_target_pairs={{0,16},{8,24},{16,0},{24,8},{1,17},{9,25},{17,1},{25,9},{2,18},{10... | collective-permute-start | bytes 294920 | tf_op jit(solution)/shard_map/ppermute | solution.py:458
  148.1 7.6 %collective-permute-start.42 = (bf16[384,128]{1,0:T(8,128)(2,1)S(1)}, bf16[384,128]{1,0:T(8,128)(2,1)S(1)}, u32[]{:S(2)}, u32[]{:S(2)}) collective-permute-start(bf16[384,128]{1,0:T(8,128)(2,1)S(1)} %get-tuple-element.120), channel_id=1, source_target_pairs={{0,24},{8,16},{16,8},{24,0},{1,25},{9,17},{17,9},{25,1},{2,26},{10... | collective-permute-start | bytes 294920 | tf_op jit(solution)/shard_map/ppermute | solution.py:458
  155.8 10.5 %collective-permute-start.45 = (bf16[384,128]{1,0:T(8,128)(2,1)S(1)}, bf16[384,128]{1,0:T(8,128)(2,1)S(1)}, u32[]{:S(2)}, u32[]{:S(2)}) collective-permute-start(bf16[384,128]{1,0:T(8,128)(2,1)S(1)} %convert_element_type.24.refs_7_), channel_id=1, source_target_pairs={{0,24},{8,16},{16,8},{24,0},{1,25},{9,17},{17,9},{25,1},{2,26},{10... | collective-permute-start | bytes 294920 | tf_op jit(solution)/shard_map/ppermute | solution.py:458
  158.1 8.1 %collective-permute-start.44 = (bf16[384,128]{1,0:T(8,128)(2,1)S(1)}, bf16[384,128]{1,0:T(8,128)(2,1)S(1)}, u32[]{:S(2)}, u32[]{:S(2)}) collective-permute-start(bf16[384,128]{1,0:T(8,128)(2,1)S(1)} %convert_element_type.24.refs_7_), channel_id=1, source_target_pairs={{0,16},{8,24},{16,0},{24,8},{1,17},{9,25},{17,1},{25,9},{2,18},{10... | collective-permute-start | bytes 294920 | tf_op jit(solution)/shard_map/ppermute | solution.py:458
  158.1 8.1 %collective-permute-start.43 = (bf16[384,128]{1,0:T(8,128)(2,1)S(1)}, bf16[384,128]{1,0:T(8,128)(2,1)S(1)}, u32[]{:S(2)}, u32[]{:S(2)}) collective-permute-start(bf16[384,128]{1,0:T(8,128)(2,1)S(1)} %convert_element_type.24.refs_7_), channel_id=1, source_target_pairs={{0,8},{8,0},{16,24},{24,16},{1,9},{9,1},{17,25},{25,17},{2,10},{10... | collective-permute-start | bytes 294920 | tf_op jit(solution)/shard_map/ppermute | solution.py:458

commit v24 on v18

--- a/solution.py
+++ b/solution.py
@@ -501,6 +501,10 @@
     values = {0: incoming[:, kv_width:]}
     for i, k in enumerate(far[1:] if relay else far):
         values[k] = swap(after(values[0], blocks[order[i]]), "fsdp", k)
+    if relay:
+        upper = swap(values[far[1]][:half], "fsdp", far[2])
+        lower = swap(values[far[2]][half:], "fsdp", far[1])
+        values[far[0]] = jnp.concatenate([upper, lower], axis=0)
 
     steps_now = step_count[0].astype(jnp.float32)
     plan = jnp.minimum(1.0, steps_now / WARMUP) * (
@@ -534,14 +538,8 @@
             continue
         part_k, flipped[k] = partial_keys(blocks[k], key_weights, adds)
         if k == last:
-            for j in [0] + [j for j in far if j in values]:
-                values[j] = after(values[j], part_k)
-            if relay:
-                upper = swap(values[far[1]][:half], "fsdp", far[2])
-                lower = swap(values[far[2]][half:], "fsdp", far[1])
-                values[far[0]] = jnp.concatenate([upper, lower], axis=0)
             for j in range(0, shards, 2):
-                values[j + 1] = swap(values[j], "fsdp", 1)
+                values[j + 1] = swap(after(values[j], part_k), "fsdp", 1)
         parts.append(swap(part_k, "fsdp", k) if k else part_k)
     spread = [0, 1] + [k + odd for k in far for odd in range(2)]
     near, rest = spread[:shards // 2], spread[shards // 2:]

time: 168 us -> 161 us (0.958)
  waiting for transfers between devices: 64.4 us -> 57.6 us
    ppermute x46, waiting for transfers between devices: 64.4 us -> 57.6 us  [swap(): return lax.ppermute(block, axis, [(i, i ^ offset) for i in range(count)])]
  transfers between devices with their start and end apart: 46 -> 46, of which waited for: 17 -> 17; matrix products, arithmetic and copies ran while one was open for 0% -> 0% of each run, Pallas kernels for 28% -> 29%
where the time goes in v24:
time: 161 us; the launch traced here: 160 us
  waiting for transfers between devices  57.6 us (36%)
  Pallas kernels  54.9 us (34%)
  starting transfers between devices  43.6 us (27%)
  between operations  3.8 us (2%)
    ppermute x46, waiting for transfers between devices, swap(): return lax.ppermute(block, axis, [(i, i ^ offset) for i in range(count)])  57.6 us
    ppermute x46, starting transfers between devices, swap(): return lax.ppermute(block, axis, [(i, i ^ offset) for i in range(count)])  43.6 us
    pallas_call x4, Pallas kernels, gradient(): pl.pallas_call(functools.partial(grad_kernel, len(flipped), base is not N...  13.5 us
    pallas_call x2, Pallas kernels, adam_rows(): pl.pallas_call(functools.partial(adam_kernel, len(squares), len(into)), o...  12 us
    pallas_call x4, Pallas kernels, pack(): pl.pallas_call(functools.partial(pack_kernel, offsets), out_shape=[pltpu....  9.19 us
    pallas_call x3, Pallas kernels, due_columns(): pl.pallas_call(functools.partial(pick_kernel, blocks), out_shape=[jax.Sha...  5.55 us
    pallas_call x8, Pallas kernels, partial_keys(): pl.pallas_call(functools.partial(partial_kernel, pieces, [first for _, fi...  4.64 us
    pallas_call x1, Pallas kernels, cast_left(): pl.pallas_call(cast_kernel, out_shape=jax.ShapeDtypeStruct((rows, width),...  3.46 us
  transfers between devices with their start and end apart: 46, of which 17 were waited for; matrix products, arithmetic and copies ran while one was open for 0% of the time, Pallas kernels for 29%

profile of v24, /device:TPU:0, one launch (start us, length us, event | category | flops | bytes accessed | tf_op | source)
XLA Modules:
  0.0 160.4 jit_solution(1084690835416987064)
XLA Ops:
  1.4 1.8 %due_columns.5.w_ref = f32[4,384,128]{2,1,0:T(8,128)S(1)} custom-call(s32[2]{0:T(128)S(1)} %pad_add_fusion.place_ref, f32[1536,1024]{1,0:T(8,128)} %bitcast.35, f32[1536,1024]{1,0:T(8,128)} %bitcast.36, f32[1536,1024]{1,0:T(8,128)} %bitcast.37, f32[1536,1024]{1,0:T(8,128)} %bitcast.38), custom_call_target="tpu_custom_call" | custom-call | bytes 1572864 | tf_op jit(solution)/shard_map/due_columns/pallas_call | solution.py:348
  3.2 3.1 %collective-permute-start.10 = (f32[384,128]{1,0:T(8,128)S(1)}, f32[384,128]{1,0:T(8,128)S(1)}, u32[]{:S(2)}, u32[]{:S(2)}) collective-permute-start(f32[384,128]{1,0:T(8,128)S(1)} %get-tuple-element.136), channel_id=1, source_target_pairs={{0,8},{8,0},{16,24},{24,16},{1,9},{9,1},{17,25},{25,17},{2,10},{10... | collective-permute-start | bytes 589832 | tf_op jit(solution)/shard_map/ppermute | solution.py:458
  6.3 2.5 %collective-permute-start.12 = (f32[384,128]{1,0:T(8,128)S(1)}, f32[384,128]{1,0:T(8,128)S(1)}, u32[]{:S(2)}, u32[]{:S(2)}) collective-permute-start(f32[384,128]{1,0:T(8,128)S(1)} %get-tuple-element.137), channel_id=1, source_target_pairs={{0,24},{8,16},{16,8},{24,0},{1,25},{9,17},{17,9},{25,1},{2,26},{10... | collective-permute-start | bytes 589832 | tf_op jit(solution)/shard_map/ppermute | solution.py:458
  8.9 2.0 %pack.6 = bf16[256,1536]{1,0:T(8,128)(2,1)} custom-call(s32[1]{0:T(128)} %bitcast.4.me_ref, bf16[256,12288]{1,0:T(8,128)(2,1)} %bitcast.64), custom_call_target="tpu_custom_call" | custom-call | bytes 1572864 | tf_op jit(solution)/shard_map/pack/pallas_call | solution.py:69
  10.9 2.5 %collective-permute-start.3 = (bf16[256,1536]{1,0:T(8,128)(2,1)}, bf16[256,1536]{1,0:T(8,128)(2,1)S(1)}, u32[]{:S(2)}, u32[]{:S(2)}) collective-permute-start(bf16[256,1536]{1,0:T(8,128)(2,1)} %pack.6), channel_id=1, source_target_pairs={{0,6},{1,7},{2,4},{3,5},{4,2},{5,3},{6,0},{7,1},{8,14},{9,15},{10,... | collective-permute-start | bytes 2359304 | tf_op jit(solution)/shard_map/ppermute | solution.py:458
  13.4 2.6 %pack.4 = (bf16[256,1536]{1,0:T(8,128)(2,1)}, bf16[256,1536]{1,0:T(8,128)(2,1)}, bf16[256,1536]{1,0:T(8,128)(2,1)}) custom-call(s32[1]{0:T(128)} %bitcast.4.me_ref, bf16[256,12288]{1,0:T(8,128)(2,1)} %bitcast.65), custom_call_target="tpu_custom_call" | custom-call | bytes 4718592 | tf_op jit(solution)/shard_map/pack/pallas_call | solution.py:69
  16.1 1.6 due_columns.4
  17.7 1.2 collective-permute-done.12
  18.9 7.3 %collective-permute-done.11 = f32[384,128]{1,0:T(8,128)S(1)} collective-permute-done((f32[384,128]{1,0:T(8,128)S(1)}, f32[384,128]{1,0:T(8,128)S(1)}, u32[]{:S(2)}, u32[]{:S(2)}) %collective-permute-start.11) | collective-permute-done | bytes 196640 | tf_op jit(solution)/shard_map/ppermute | solution.py:458
  26.3 3.1 %collective-permute-start.15 = (f32[384,128]{1,0:T(8,128)S(1)}, f32[384,128]{1,0:T(8,128)S(1)}, u32[]{:S(2)}, u32[]{:S(2)}) collective-permute-start(f32[384,128]{1,0:T(8,128)S(1)} %get-tuple-element.134.refs_3_), channel_id=1, source_target_pairs={{0,24},{8,16},{16,8},{24,0},{1,25},{9,17},{17,9},{25,1},{2,26},{10... | collective-permute-start | bytes 589832 | tf_op jit(solution)/shard_map/ppermute | solution.py:458
  29.4 1.4 collective-permute-start.13
  30.7 2.3 %pack.7 = (bf16[256,1536]{1,0:T(8,128)(2,1)}, bf16[256,1536]{1,0:T(8,128)(2,1)}) custom-call(s32[1]{0:T(128)} %bitcast.4.me_ref, bf16[256,12288]{1,0:T(8,128)(2,1)} %bitcast.66), custom_call_target="tpu_custom_call" | custom-call | bytes 3145728 | tf_op jit(solution)/shard_map/pack/pallas_call | solution.py:69
  33.1 3.0 %collective-permute-done.15.refs_6_ = f32[384,128]{1,0:T(8,128)S(1)} collective-permute-done((f32[384,128]{1,0:T(8,128)S(1)}, f32[384,128]{1,0:T(8,128)S(1)}, u32[]{:S(2)}, u32[]{:S(2)}) %collective-permute-start.15) | collective-permute-done | bytes 196640 | tf_op jit(solution)/shard_map/ppermute | solution.py:458
  36.1 2.3 %pack.5 = (bf16[256,1536]{1,0:T(8,128)(2,1)}, bf16[256,1536]{1,0:T(8,128)(2,1)}) custom-call(s32[1]{0:T(128)} %bitcast.4.me_ref, bf16[256,12288]{1,0:T(8,128)(2,1)} %bitcast.67), custom_call_target="tpu_custom_call" | custom-call | bytes 3145728 | tf_op jit(solution)/shard_map/pack/pallas_call | solution.py:69
  38.4 6.0 %collective-permute-done.14.refs_5_ = f32[384,128]{1,0:T(8,128)S(1)} collective-permute-done((f32[384,128]{1,0:T(8,128)S(1)}, f32[384,128]{1,0:T(8,128)S(1)}, u32[]{:S(2)}, u32[]{:S(2)}) %collective-permute-start.14) | collective-permute-done | bytes 196640 | tf_op jit(solution)/shard_map/ppermute | solution.py:458
  44.4 2.7 %collective-permute-start.1 = (bf16[256,1536]{1,0:T(8,128)(2,1)}, bf16[256,1536]{1,0:T(8,128)(2,1)S(1)}, u32[]{:S(2)}, u32[]{:S(2)}) collective-permute-start(bf16[256,1536]{1,0:T(8,128)(2,1)} %get-tuple-element.71), channel_id=1, source_target_pairs={{0,3},{1,2},{2,1},{3,0},{4,7},{5,6},{6,5},{7,4},{8,11},{9,10},{10,... | collective-permute-start | bytes 2359304 | tf_op jit(solution)/shard_map/ppermute | solution.py:458
  48.2 3.5 %cast_left.1.refs_4_ = bf16[1536,512]{1,0:T(8,128)(2,1)S(1)} custom-call(f32[1536,1024]{1,0:T(8,128)} %bitcast.39), custom_call_target="tpu_custom_call" | custom-call | bytes 4718592 | tf_op jit(solution)/shard_map/cast_left/pallas_call | solution.py:93
  51.7 0.6 partial_keys.9
  52.3 0.7 collective-permute-start.5
  53.9 10.6 %collective-permute-done.8.refs_0_.refs_1_.refs_2_.refs_3_ = bf16[256,1536]{1,0:T(8,128)(2,1)S(1)} collective-permute-done((bf16[256,1536]{1,0:T(8,128)(2,1)}, bf16[256,1536]{1,0:T(8,128)(2,1)S(1)}, u32[]{:S(2)}, u32[]{:S(2)}) %collective-permute-start.8) | collective-permute-done | bytes 786464 | tf_op jit(solution)/shard_map/ppermute | solution.py:458
  64.5 1.5 collective-permute-start.22
  66.0 2.8 %duplicate.1 = (f32[384,1024]{1,0:T(8,128)}, f32[384,1024]{1,0:T(8,128)}) custom-call(f32[384,1024]{1,0:T(8,128)} %refs_0_.3, f32[384,1024]{1,0:T(8,128)} %refs_1_.3), custom_call_target="tpu_custom_call" | custom-call | bytes 6291456 | tf_op jit(solution)/shard_map/duplicate/pallas_call | solution.py:389
  68.8 2.1 %due_columns.3 = (f32[4,384,128]{2,1,0:T(8,128)S(1)}, f32[4,384,128]{2,1,0:T(8,128)S(1)}) custom-call(s32[2]{0:T(128)S(1)} %pad_add_fusion.place_ref, f32[1536,1024]{1,0:T(8,128)} %bitcast.44, f32[1536,1024]{1,0:T(8,128)} %bitcast.45, f32[1536,1024]{1,0:T(8,128)} %bitcast.46, f32[1536,1024]{1,0:T(8,128)} %bitcast.47, f32[1536,1024]{1,0:T(8,128)} %bitcast.52, ...), custom_call_target="tpu_custom_call" | custom-call | bytes 3145728 | tf_op jit(solution)/shard_map/due_columns/pallas_call | solution.py:348
  71.0 1.7 %collective-permute-start.24 = (bf16[256,512]{1,0:T(8,128)(2,1)S(1)}, bf16[256,512]{1,0:T(8,128)(2,1)S(1)}, u32[]{:S(2)}, u32[]{:S(2)}) collective-permute-start(bf16[256,512]{1,0:T(8,128)(2,1)S(1)} %slice.32.refs_4_), channel_id=1, source_target_pairs={{0,4},{1,5},{2,6},{3,7},{4,0},{5,1},{6,2},{7,3},{8,12},{9,13},{10,... | collective-permute-start | bytes 786440 | tf_op jit(solution)/shard_map/ppermute | solution.py:458
  72.7 0.6 partial_keys.12
  73.2 9.8 %collective-permute-done.refs_0_.refs_1_.refs_2_.refs_3_ = bf16[256,1536]{1,0:T(8,128)(2,1)S(1)} collective-permute-done((bf16[256,1536]{1,0:T(8,128)(2,1)S(1)}, bf16[256,1536]{1,0:T(8,128)(2,1)S(1)}, u32[]{:S(2)}, u32[]{:S(2)}) %collective-permute-start) | collective-permute-done | bytes 786464 | tf_op jit(solution)/shard_map/ppermute | solution.py:458
  83.1 0.6 partial_keys.8
  84.2 0.6 partial_keys.10
  84.8 3.1 %collective-permute-done.22.refs_4_ = bf16[256,512]{1,0:T(8,128)(2,1)S(1)} collective-permute-done((bf16[256,512]{1,0:T(8,128)(2,1)S(1)}, bf16[256,512]{1,0:T(8,128)(2,1)S(1)}, u32[]{:S(2)}, u32[]{:S(2)}) %collective-permute-start.22) | collective-permute-done | bytes 262176 | tf_op jit(solution)/shard_map/ppermute | solution.py:458
  88.4 1.5 collective-permute-start.16
  89.9 0.7 collective-permute-start.27
  90.6 0.6 partial_keys.14
  91.3 2.9 %collective-permute-done.6.refs_6_ = bf16[128,512]{1,0:T(8,128)(2,1)S(1)} collective-permute-done((bf16[128,512]{1,0:T(8,128)(2,1)S(1)}, bf16[128,512]{1,0:T(8,128)(2,1)S(1)}, u32[]{:S(2)}, u32[]{:S(2)}) %collective-permute-start.6) | collective-permute-done | bytes 131104 | tf_op jit(solution)/shard_map/ppermute | solution.py:458
  94.7 0.6 partial_keys.11
  95.3 1.6 collective-permute-start.17
  96.9 0.6 partial_keys.13
  97.8 2.6 %collective-permute-done.28 = bf16[128,512]{1,0:T(8,128)(2,1)S(1)} collective-permute-done((bf16[128,512]{1,0:T(8,128)(2,1)S(1)}, bf16[128,512]{1,0:T(8,128)(2,1)S(1)}, u32[]{:S(2)}, u32[]{:S(2)}) %collective-permute-start.28) | collective-permute-done | bytes 131104 | tf_op jit(solution)/shard_map/ppermute | solution.py:458
  101.1 2.1 %collective-permute-done.17.refs_0_ = bf16[256,512]{1,0:T(8,128)(2,1)S(1)} collective-permute-done((bf16[256,512]{1,0:T(8,128)(2,1)S(1)}, bf16[256,512]{1,0:T(8,128)(2,1)S(1)}, u32[]{:S(2)}, u32[]{:S(2)}) %collective-permute-start.17) | collective-permute-done | bytes 262176 | tf_op jit(solution)/shard_map/ppermute | solution.py:458
  103.2 0.6 partial_keys.15
  104.4 1.5 collective-permute-start.34
  106.1 1.0 collective-permute-start.31
  107.1 3.2 %gradient.4.refs_8_ = f32[1536,512]{1,0:T(8,128)S(1)} custom-call(s32[2]{0:T(128)S(1)} %pad_add_fusion.place_ref, bf16[1536,256]{1,0:T(8,128)(2,1)S(1)} %get-tuple-element.102.refs_0_, bf16[1536,256]{1,0:T(8,128)(2,1)S(1)} %get-tuple-element.103.refs_1_, bf16[1536,256]{1,0:T(8,128)(2,1)S(1)} %get-tuple-element.104.refs_2_, ...), custom_call_target="tpu_custom_call" | custom-call | flops 1610612736 | bytes 6291456 | tf_op jit(solution)/shard_map/gradient/pallas_call | solution.py:236
  110.3 1.1 collective-permute-start.21
  111.4 3.6 %gradient.5 = (f32[1536,512]{1,0:T(8,128)S(1)}, f32[8,128]{1,0:T(8,128)S(1)}, f32[1536,128]{1,0:T(8,128)S(1)}) custom-call(s32[2]{0:T(128)S(1)} %pad_add_fusion.place_ref, bf16[1536,256]{1,0:T(8,128)(2,1)S(1)} %get-tuple-element.76.refs_0_, bf16[1536,256]{1,0:T(8,128)(2,1)S(1)} %get-tuple-element.77.refs_1_, ...), custom_call_target="tpu_custom_call" | custom-call | flops 1610612736 | bytes 6291456 | tf_op jit(solution)/shard_map/gradient/pallas_call | solution.py:236
  115.1 4.6 %collective-permute-done.31.refs_6_ = bf16[256,512]{1,0:T(8,128)(2,1)S(1)} collective-permute-done((bf16[256,512]{1,0:T(8,128)(2,1)S(1)}, bf16[256,512]{1,0:T(8,128)(2,1)S(1)}, u32[]{:S(2)}, u32[]{:S(2)}) %collective-permute-start.31) | collective-permute-done | bytes 262176 | tf_op jit(solution)/shard_map/ppermute | solution.py:458
  120.2 3.2 %gradient.6.refs_8_ = f32[1536,512]{1,0:T(8,128)S(1)} custom-call(s32[2]{0:T(128)S(1)} %pad_add_fusion.place_ref, bf16[1536,256]{1,0:T(8,128)(2,1)S(1)} %get-tuple-element.102.refs_0_, bf16[1536,256]{1,0:T(8,128)(2,1)S(1)} %get-tuple-element.103.refs_1_, bf16[1536,256]{1,0:T(8,128)(2,1)S(1)} %get-tuple-element.104.refs_2_, ...), custom_call_target="tpu_custom_call" | custom-call | flops 1610612736 | bytes 6291456 | tf_op jit(solution)/shard_map/gradient/pallas_call | solution.py:236
  123.4 3.6 %gradient.7 = (f32[1536,512]{1,0:T(8,128)S(1)}, f32[8,128]{1,0:T(8,128)S(1)}, f32[1536,128]{1,0:T(8,128)S(1)}) custom-call(s32[2]{0:T(128)S(1)} %pad_add_fusion.place_ref, bf16[1536,256]{1,0:T(8,128)(2,1)S(1)} %get-tuple-element.76.refs_0_, bf16[1536,256]{1,0:T(8,128)(2,1)S(1)} %get-tuple-element.77.refs_1_, ...), custom_call_target="tpu_custom_call" | custom-call | flops 1610612736 | bytes 6291456 | tf_op jit(solution)/shard_map/gradient/pallas_call | solution.py:236
  127.1 1.1 collective-permute-done.36
  128.3 1.5 collective-permute-start.39
  129.7 1.0 collective-permute-start.38
  130.7 1.0 collective-permute-start.37
  131.8 1.0 collective-permute-done.39.refs_3_
  133.3 1.0 collective-permute-done.37.refs_1_
  134.3 1.6 adam_frag.1
  135.9 1.9 %collective-permute-start.40 = (bf16[384,128]{1,0:T(8,128)(2,1)S(1)}, bf16[384,128]{1,0:T(8,128)(2,1)S(1)}, u32[]{:S(2)}, u32[]{:S(2)}) collective-permute-start(bf16[384,128]{1,0:T(8,128)(2,1)S(1)} %get-tuple-element.122), channel_id=1, source_target_pairs={{0,8},{8,0},{16,24},{24,16},{1,9},{9,1},{17,25},{25,17},{2,10},{10... | collective-permute-start | bytes 294920 | tf_op jit(solution)/shard_map/ppermute | solution.py:458
  137.8 1.0 collective-permute-start.41
  138.8 1.6 collective-permute-start.42
  140.4 6.0 %adam_rows.2 = (f32[1536,1024]{1,0:T(8,128)}, f32[1536,1024]{1,0:T(8,128)}, f32[1536,1024]{1,0:T(8,128)}, f32[8,128]{1,0:T(8,128)S(1)}) custom-call(f32[3]{0:T(128)S(1)} %pad_maximum_fusion.sc_ref, f32[1536,1024]{1,0:T(8,128)S(1)} %bitcast.42, f32[1536,1024]{1,0:T(8,128)S(1)} %bitcast.50, f32[1536,1024]{1,0:T(8,128)S(1)} %bitcast.58, ...), custom_call_target="tpu_custom_call" | custom-call | flops 15728640 | bytes 22020096 | tf_op jit(solution)/shard_map/adam_rows/pallas_call | solution.py:291
  146.4 0.6 collective-permute-done.41
  147.1 1.8 %collective-permute-start.45 = (bf16[384,128]{1,0:T(8,128)(2,1)S(1)}, bf16[384,128]{1,0:T(8,128)(2,1)S(1)}, u32[]{:S(2)}, u32[]{:S(2)}) collective-permute-start(bf16[384,128]{1,0:T(8,128)(2,1)S(1)} %convert_element_type.24.refs_7_), channel_id=1, source_target_pairs={{0,24},{8,16},{16,8},{24,0},{1,25},{9,17},{17,9},{25,1},{2,26},{10... | collective-permute-start | bytes 294920 | tf_op jit(solution)/shard_map/ppermute | solution.py:458
  149.0 1.3 collective-permute-start.44
  150.3 1.3 collective-permute-start.43
  151.6 6.0 %adam_rows.3 = (f32[1536,1024]{1,0:T(8,128)}, f32[1536,1024]{1,0:T(8,128)}, f32[1536,1024]{1,0:T(8,128)}) custom-call(f32[3]{0:T(128)S(1)} %pad_maximum_fusion.sc_ref, f32[1536,1024]{1,0:T(8,128)S(1)} %bitcast.43, f32[1536,1024]{1,0:T(8,128)S(1)} %bitcast.51, ...), custom_call_target="tpu_custom_call", output_to_operand_aliasing={{0}: (10, {}), {1}: (11, {}), {2}: (12, {})} | custom-call | flops 15728640 | bytes 22020096 | tf_op jit(solution)/shard_map/adam_rows/pallas_call | solution.py:291
  157.6 1.7 %outer_step.1 = (f32[1536,1024]{1,0:T(8,128)}, f32[384,1024]{1,0:T(8,128)}, f32[384,1024]{1,0:T(8,128)}) custom-call(s32[2]{0:T(128)S(1)} %pad_add_fusion.place_ref, f32[1536,1024]{1,0:T(8,128)} %get-tuple-element.119.refs_0_, f32[384,1024]{1,0:T(8,128)} %get-tuple-element.80.refs_1_, ...), custom_call_target="tpu_custom_call", output_to_operand_aliasing={{0}: (1, {}), {1}: (2, {}), {2}: (3, {})} | custom-call | flops 1966080 | bytes 3932160 | tf_op jit(solution)/shard_map/outer_step/pallas_call | solution.py:435
  (89 shorter events, 6.6 us)
Async XLA Ops:
  3.2 14.5 %collective-permute-start.10 = (f32[384,128]{1,0:T(8,128)S(1)}, f32[384,128]{1,0:T(8,128)S(1)}, u32[]{:S(2)}, u32[]{:S(2)}) collective-permute-start(f32[384,128]{1,0:T(8,128)S(1)} %get-tuple-element.136), channel_id=1, source_target_pairs={{0,8},{8,0},{16,24},{24,16},{1,9},{9,1},{17,25},{25,17},{2,10},{10... | collective-permute-start | bytes 589832 | tf_op jit(solution)/shard_map/ppermute | solution.py:458
  6.3 12.6 %collective-permute-start.12 = (f32[384,128]{1,0:T(8,128)S(1)}, f32[384,128]{1,0:T(8,128)S(1)}, u32[]{:S(2)}, u32[]{:S(2)}) collective-permute-start(f32[384,128]{1,0:T(8,128)S(1)} %get-tuple-element.137), channel_id=1, source_target_pairs={{0,24},{8,16},{16,8},{24,0},{1,25},{9,17},{17,9},{25,1},{2,26},{10... | collective-permute-start | bytes 589832 | tf_op jit(solution)/shard_map/ppermute | solution.py:458
  8.8 17.4 %collective-permute-start.11 = (f32[384,128]{1,0:T(8,128)S(1)}, f32[384,128]{1,0:T(8,128)S(1)}, u32[]{:S(2)}, u32[]{:S(2)}) collective-permute-start(f32[384,128]{1,0:T(8,128)S(1)} %get-tuple-element.138), channel_id=1, source_target_pairs={{0,16},{8,24},{16,0},{24,8},{1,17},{9,25},{17,1},{25,9},{2,18},{10... | collective-permute-start | bytes 589832 | tf_op jit(solution)/shard_map/ppermute | solution.py:458
  10.9 36.2 %collective-permute-start.3 = (bf16[256,1536]{1,0:T(8,128)(2,1)}, bf16[256,1536]{1,0:T(8,128)(2,1)S(1)}, u32[]{:S(2)}, u32[]{:S(2)}) collective-permute-start(bf16[256,1536]{1,0:T(8,128)(2,1)} %pack.6), channel_id=1, source_target_pairs={{0,6},{1,7},{2,4},{3,5},{4,2},{5,3},{6,0},{7,1},{8,14},{9,15},{10,... | collective-permute-start | bytes 2359304 | tf_op jit(solution)/shard_map/ppermute | solution.py:458
  16.0 31.6 %collective-permute-start.4 = (bf16[256,1536]{1,0:T(8,128)(2,1)}, bf16[256,1536]{1,0:T(8,128)(2,1)S(1)}, u32[]{:S(2)}, u32[]{:S(2)}) collective-permute-start(bf16[256,1536]{1,0:T(8,128)(2,1)} %get-tuple-element.73), channel_id=1, source_target_pairs={{0,7},{1,6},{2,5},{3,4},{4,3},{5,2},{6,1},{7,0},{8,15},{9,14},{10,... | collective-permute-start | bytes 2359304 | tf_op jit(solution)/shard_map/ppermute | solution.py:458
  26.3 20.8 %copy-start.3 = (bf16[256,1536]{1,0:T(8,128)(2,1)S(1)}, bf16[256,1536]{1,0:T(8,128)(2,1)}, u32[]{:S(2)}) copy-start(bf16[256,1536]{1,0:T(8,128)(2,1)} %get-tuple-element.70) | copy-start | bytes 2359300
  26.3 21.4 %copy-start.2 = (bf16[256,1536]{1,0:T(8,128)(2,1)S(1)}, bf16[256,1536]{1,0:T(8,128)(2,1)}, u32[]{:S(2)}) copy-start(bf16[256,1536]{1,0:T(8,128)(2,1)} %get-tuple-element.78) | copy-start | bytes 2359300
  26.3 9.8 %collective-permute-start.15 = (f32[384,128]{1,0:T(8,128)S(1)}, f32[384,128]{1,0:T(8,128)S(1)}, u32[]{:S(2)}, u32[]{:S(2)}) collective-permute-start(f32[384,128]{1,0:T(8,128)S(1)} %get-tuple-element.134.refs_3_), channel_id=1, source_target_pairs={{0,24},{8,16},{16,8},{24,0},{1,25},{9,17},{17,9},{25,1},{2,26},{10... | collective-permute-start | bytes 589832 | tf_op jit(solution)/shard_map/ppermute | solution.py:458
  29.4 15.0 %collective-permute-start.14 = (f32[384,128]{1,0:T(8,128)S(1)}, f32[384,128]{1,0:T(8,128)S(1)}, u32[]{:S(2)}, u32[]{:S(2)}) collective-permute-start(f32[384,128]{1,0:T(8,128)S(1)} %get-tuple-element.134.refs_3_), channel_id=1, source_target_pairs={{0,16},{8,24},{16,0},{24,8},{1,17},{9,25},{17,1},{25,9},{2,18},{10... | collective-permute-start | bytes 589832 | tf_op jit(solution)/shard_map/ppermute | solution.py:458
  29.4 15.0 %collective-permute-start.13 = (f32[384,128]{1,0:T(8,128)S(1)}, f32[384,128]{1,0:T(8,128)S(1)}, u32[]{:S(2)}, u32[]{:S(2)}) collective-permute-start(f32[384,128]{1,0:T(8,128)S(1)} %get-tuple-element.134.refs_3_), channel_id=1, source_target_pairs={{0,8},{8,0},{16,24},{24,16},{1,9},{9,1},{17,25},{25,17},{2,10},{10... | collective-permute-start | bytes 589832 | tf_op jit(solution)/shard_map/ppermute | solution.py:458
  36.1 16.2 %collective-permute-start.19 = (bf16[256,1536]{1,0:T(8,128)(2,1)}, bf16[256,1536]{1,0:T(8,128)(2,1)S(1)}, u32[]{:S(2)}, u32[]{:S(2)}) collective-permute-start(bf16[256,1536]{1,0:T(8,128)(2,1)} %get-tuple-element.95), channel_id=1, source_target_pairs={{0,1},{1,0},{2,3},{3,2},{4,5},{5,4},{6,7},{7,6},{8,9},{9,8},{10,11... | collective-permute-start | bytes 2359304 | tf_op jit(solution)/shard_map/ppermute | solution.py:458
  44.4 20.1 %collective-permute-start.8 = (bf16[256,1536]{1,0:T(8,128)(2,1)}, bf16[256,1536]{1,0:T(8,128)(2,1)S(1)}, u32[]{:S(2)}, u32[]{:S(2)}) collective-permute-start(bf16[256,1536]{1,0:T(8,128)(2,1)} %get-tuple-element.79), channel_id=1, source_target_pairs={{0,5},{1,4},{2,7},{3,6},{4,1},{5,0},{6,3},{7,2},{8,13},{9,12},{10,... | collective-permute-start | bytes 2359304 | tf_op jit(solution)/shard_map/ppermute | solution.py:458
  44.4 26.6 %collective-permute-start.1 = (bf16[256,1536]{1,0:T(8,128)(2,1)}, bf16[256,1536]{1,0:T(8,128)(2,1)S(1)}, u32[]{:S(2)}, u32[]{:S(2)}) collective-permute-start(bf16[256,1536]{1,0:T(8,128)(2,1)} %get-tuple-element.71), channel_id=1, source_target_pairs={{0,3},{1,2},{2,1},{3,0},{4,7},{5,6},{6,5},{7,4},{8,11},{9,10},{10,... | collective-permute-start | bytes 2359304 | tf_op jit(solution)/shard_map/ppermute | solution.py:458
  47.1 36.0 %collective-permute-start = (bf16[256,1536]{1,0:T(8,128)(2,1)S(1)}, bf16[256,1536]{1,0:T(8,128)(2,1)S(1)}, u32[]{:S(2)}, u32[]{:S(2)}) collective-permute-start(bf16[256,1536]{1,0:T(8,128)(2,1)S(1)} %copy-done.3), channel_id=1, source_target_pairs={{0,2},{1,3},{2,0},{3,1},{4,6},{5,7},{6,4},{7,5},{8,10},{9,11},{10,... | collective-permute-start | bytes 2359304 | tf_op jit(solution)/shard_map/ppermute | solution.py:458
  47.6 6.2 %copy-start.1 = (bf16[1,256,1024]{2,1,0:T(8,128)(2,1)S(1)}, bf16[1,256,1024]{2,1,0:T(8,128)(2,1)}, u32[]{:S(2)}) copy-start(bf16[1,256,1024]{2,1,0:T(8,128)(2,1)} %param.10) | copy-start | bytes 1572868
  47.6 47.7 %collective-permute-start.7 = (bf16[256,1536]{1,0:T(8,128)(2,1)S(1)}, bf16[256,1536]{1,0:T(8,128)(2,1)S(1)}, u32[]{:S(2)}, u32[]{:S(2)}) collective-permute-start(bf16[256,1536]{1,0:T(8,128)(2,1)S(1)} %copy-done.2), channel_id=1, source_target_pairs={{0,4},{1,5},{2,6},{3,7},{4,0},{5,1},{6,2},{7,3},{8,12},{9,13},{10,... | collective-permute-start | bytes 2359304 | tf_op jit(solution)/shard_map/ppermute | solution.py:458
  52.3 31.4 %collective-permute-start.5 = (bf16[256,512]{1,0:T(8,128)(2,1)S(1)}, bf16[256,512]{1,0:T(8,128)(2,1)S(1)}, u32[]{:S(2)}, u32[]{:S(2)}) collective-permute-start(bf16[256,512]{1,0:T(8,128)(2,1)S(1)} %get-tuple-element.74), channel_id=1, source_target_pairs={{0,1},{1,0},{2,3},{3,2},{4,5},{5,4},{6,7},{7,6},{8,9},{9,8},{10,11... | collective-permute-start | bytes 786440 | tf_op jit(solution)/shard_map/ppermute | solution.py:458
  64.5 23.4 %collective-permute-start.22 = (bf16[256,512]{1,0:T(8,128)(2,1)S(1)}, bf16[256,512]{1,0:T(8,128)(2,1)S(1)}, u32[]{:S(2)}, u32[]{:S(2)}) collective-permute-start(bf16[256,512]{1,0:T(8,128)(2,1)S(1)} %slice.32.refs_4_), channel_id=1, source_target_pairs={{0,2},{1,3},{2,0},{3,1},{4,6},{5,7},{6,4},{7,5},{8,10},{9,11},{10,... | collective-permute-start | bytes 786440 | tf_op jit(solution)/shard_map/ppermute | solution.py:458
  71.0 17.4 %collective-permute-start.24 = (bf16[256,512]{1,0:T(8,128)(2,1)S(1)}, bf16[256,512]{1,0:T(8,128)(2,1)S(1)}, u32[]{:S(2)}, u32[]{:S(2)}) collective-permute-start(bf16[256,512]{1,0:T(8,128)(2,1)S(1)} %slice.32.refs_4_), channel_id=1, source_target_pairs={{0,4},{1,5},{2,6},{3,7},{4,0},{5,1},{6,2},{7,3},{8,12},{9,13},{10,... | collective-permute-start | bytes 786440 | tf_op jit(solution)/shard_map/ppermute | solution.py:458
  83.1 6.9 %collective-permute-start.9 = (bf16[256,512]{1,0:T(8,128)(2,1)S(1)}, bf16[256,512]{1,0:T(8,128)(2,1)S(1)}, u32[]{:S(2)}, u32[]{:S(2)}) collective-permute-start(bf16[256,512]{1,0:T(8,128)(2,1)S(1)} %get-tuple-element.85), channel_id=1, source_target_pairs={{0,1},{1,0},{2,3},{3,2},{4,5},{5,4},{6,7},{7,6},{8,9},{9,8},{10,11... | collective-permute-start | bytes 786440 | tf_op jit(solution)/shard_map/ppermute | solution.py:458
  83.6 7.6 %collective-permute-start.2 = (bf16[256,512]{1,0:T(8,128)(2,1)S(1)}, bf16[256,512]{1,0:T(8,128)(2,1)S(1)}, u32[]{:S(2)}, u32[]{:S(2)}) collective-permute-start(bf16[256,512]{1,0:T(8,128)(2,1)S(1)} %get-tuple-element.72), channel_id=1, source_target_pairs={{0,1},{1,0},{2,3},{3,2},{4,5},{5,4},{6,7},{7,6},{8,9},{9,8},{10,11... | collective-permute-start | bytes 786440 | tf_op jit(solution)/shard_map/ppermute | solution.py:458
  87.9 6.3 %collective-permute-start.6 = (bf16[128,512]{1,0:T(8,128)(2,1)S(1)}, bf16[128,512]{1,0:T(8,128)(2,1)S(1)}, u32[]{:S(2)}, u32[]{:S(2)}) collective-permute-start(bf16[128,512]{1,0:T(8,128)(2,1)S(1)} %get-tuple-element.75), channel_id=1, source_target_pairs={{0,4},{1,5},{2,6},{3,7},{4,0},{5,1},{6,2},{7,3},{8,12},{9,13},{10,... | collective-permute-start | bytes 393224 | tf_op jit(solution)/shard_map/ppermute | solution.py:458
  88.4 8.5 %collective-permute-start.16 = (bf16[128,512]{1,0:T(8,128)(2,1)S(1)}, bf16[128,512]{1,0:T(8,128)(2,1)S(1)}, u32[]{:S(2)}, u32[]{:S(2)}) collective-permute-start(bf16[128,512]{1,0:T(8,128)(2,1)S(1)} %get-tuple-element.89), channel_id=1, source_target_pairs={{0,2},{1,3},{2,0},{3,1},{4,6},{5,7},{6,4},{7,5},{8,10},{9,11},{10,... | collective-permute-start | bytes 393224 | tf_op jit(solution)/shard_map/ppermute | solution.py:458
  89.9 7.8 %collective-permute-start.27 = (bf16[128,512]{1,0:T(8,128)(2,1)S(1)}, bf16[128,512]{1,0:T(8,128)(2,1)S(1)}, u32[]{:S(2)}, u32[]{:S(2)}) collective-permute-start(bf16[128,512]{1,0:T(8,128)(2,1)S(1)} %slice.33), channel_id=1, source_target_pairs={{0,4},{1,5},{2,6},{3,7},{4,0},{5,1},{6,2},{7,3},{8,12},{9,13},{10,... | collective-permute-start | bytes 393224 | tf_op jit(solution)/shard_map/ppermute | solution.py:458
  91.2 12.0 %copy-start = (bf16[256,1536]{1,0:T(8,128)(2,1)S(1)}, bf16[256,1536]{1,0:T(8,128)(2,1)}, u32[]{:S(2)}) copy-start(bf16[256,1536]{1,0:T(8,128)(2,1)} %get-tuple-element.94.refs_0_.refs_1_.refs_2_.refs_3_) | copy-start | bytes 2359300
  91.2 9.8 %collective-permute-start.20 = (bf16[256,512]{1,0:T(8,128)(2,1)S(1)}, bf16[256,512]{1,0:T(8,128)(2,1)S(1)}, u32[]{:S(2)}, u32[]{:S(2)}) collective-permute-start(bf16[256,512]{1,0:T(8,128)(2,1)S(1)} %get-tuple-element.96), channel_id=1, source_target_pairs={{0,1},{1,0},{2,3},{3,2},{4,5},{5,4},{6,7},{7,6},{8,9},{9,8},{10,11... | collective-permute-start | bytes 786440 | tf_op jit(solution)/shard_map/ppermute | solution.py:458
  94.2 6.2 %collective-permute-start.28 = (bf16[128,512]{1,0:T(8,128)(2,1)S(1)}, bf16[128,512]{1,0:T(8,128)(2,1)S(1)}, u32[]{:S(2)}, u32[]{:S(2)}) collective-permute-start(bf16[128,512]{1,0:T(8,128)(2,1)S(1)} %slice.34), channel_id=1, source_target_pairs={{0,2},{1,3},{2,0},{3,1},{4,6},{5,7},{6,4},{7,5},{8,10},{9,11},{10,... | collective-permute-start | bytes 393224 | tf_op jit(solution)/shard_map/ppermute | solution.py:458
  95.3 7.9 %collective-permute-start.17 = (bf16[256,512]{1,0:T(8,128)(2,1)S(1)}, bf16[256,512]{1,0:T(8,128)(2,1)S(1)}, u32[]{:S(2)}, u32[]{:S(2)}) collective-permute-start(bf16[256,512]{1,0:T(8,128)(2,1)S(1)} %get-tuple-element.92), channel_id=1, source_target_pairs={{0,2},{1,3},{2,0},{3,1},{4,6},{5,7},{6,4},{7,5},{8,10},{9,11},{10,... | collective-permute-start | bytes 786440 | tf_op jit(solution)/shard_map/ppermute | solution.py:458
  97.5 6.4 %collective-permute-start.18 = (bf16[256,512]{1,0:T(8,128)(2,1)S(1)}, bf16[256,512]{1,0:T(8,128)(2,1)S(1)}, u32[]{:S(2)}, u32[]{:S(2)}) collective-permute-start(bf16[256,512]{1,0:T(8,128)(2,1)S(1)} %get-tuple-element.93), channel_id=1, source_target_pairs={{0,4},{1,5},{2,6},{3,7},{4,0},{5,1},{6,2},{7,3},{8,12},{9,13},{10,... | collective-permute-start | bytes 786440 | tf_op jit(solution)/shard_map/ppermute | solution.py:458
  100.4 5.5 %collective-permute-start.26 = (bf16[256,512]{1,0:T(8,128)(2,1)S(1)}, bf16[256,512]{1,0:T(8,128)(2,1)S(1)}, u32[]{:S(2)}, u32[]{:S(2)}) collective-permute-start(bf16[256,512]{1,0:T(8,128)(2,1)S(1)} %slice.32.refs_4_), channel_id=1, source_target_pairs={{0,1},{1,0},{2,3},{3,2},{4,5},{5,4},{6,7},{7,6},{8,9},{9,8},{10,11... | collective-permute-start | bytes 786440 | tf_op jit(solution)/shard_map/ppermute | solution.py:458
  100.5 5.6 %collective-permute-start.29 = (bf16[256,512]{1,0:T(8,128)(2,1)S(1)}, bf16[256,512]{1,0:T(8,128)(2,1)S(1)}, u32[]{:S(2)}, u32[]{:S(2)}) collective-permute-start(bf16[256,512]{1,0:T(8,128)(2,1)S(1)} %constant_dynamic-update-slice_fusion.refs_6_), channel_id=1, source_target_pairs={{0,1},{1,0},{2,3},{3,2},{4,5},{5,4},{6,7},{7,6},{8,9},{9,8},{10,11... | collective-permute-start | bytes 786440 | tf_op jit(solution)/shard_map/ppermute | solution.py:458
  101.0 9.3 %collective-permute-start.23 = (bf16[256,512]{1,0:T(8,128)(2,1)S(1)}, bf16[256,512]{1,0:T(8,128)(2,1)S(1)}, u32[]{:S(2)}, u32[]{:S(2)}) collective-permute-start(bf16[256,512]{1,0:T(8,128)(2,1)S(1)} %collective-permute-done.22.refs_4_), channel_id=1, source_target_pairs={{0,1},{1,0},{2,3},{3,2},{4,5},{5,4},{6,7},{7,6},{8,9},{9,8},{10,11... | collective-permute-start | bytes 786440 | tf_op jit(solution)/shard_map/ppermute | solution.py:458
  103.2 8.2 %collective-permute-start.25 = (bf16[256,512]{1,0:T(8,128)(2,1)S(1)}, bf16[256,512]{1,0:T(8,128)(2,1)S(1)}, u32[]{:S(2)}, u32[]{:S(2)}) collective-permute-start(bf16[256,512]{1,0:T(8,128)(2,1)S(1)} %collective-permute-done.24.refs_6_), channel_id=1, source_target_pairs={{0,1},{1,0},{2,3},{3,2},{4,5},{5,4},{6,7},{7,6},{8,9},{9,8},{10,11... | collective-permute-start | bytes 786440 | tf_op jit(solution)/shard_map/ppermute | solution.py:458
  103.2 37.1 %slice-start.4 = ((s8[6291456]{0:T(1024)(128)(4,1)}), s8[4194304]{0:T(1024)(128)(4,1)S(1)}, s32[]{:S(2)}) async-start(s8[6291456]{0:T(1024)(128)(4,1)} %bitcast.56), calls=%async_computation.4 | async-start | bytes 8388608
  104.4 10.6 %collective-permute-start.34 = (bf16[256,512]{1,0:T(8,128)(2,1)S(1)}, bf16[256,512]{1,0:T(8,128)(2,1)S(1)}, u32[]{:S(2)}, u32[]{:S(2)}) collective-permute-start(bf16[256,512]{1,0:T(8,128)(2,1)S(1)} %key_backward.1.refs_4_), channel_id=1, source_target_pairs={{0,6},{1,7},{2,4},{3,5},{4,2},{5,3},{6,0},{7,1},{8,14},{9,15},{10,... | collective-permute-start | bytes 786440 | tf_op jit(solution)/shard_map/ppermute | solution.py:458
  105.9 14.2 %collective-permute-start.33 = (bf16[256,512]{1,0:T(8,128)(2,1)S(1)}, bf16[256,512]{1,0:T(8,128)(2,1)S(1)}, u32[]{:S(2)}, u32[]{:S(2)}) collective-permute-start(bf16[256,512]{1,0:T(8,128)(2,1)S(1)} %key_backward.1.refs_4_), channel_id=1, source_target_pairs={{0,1},{1,0},{2,3},{3,2},{4,5},{5,4},{6,7},{7,6},{8,9},{9,8},{10,11... | collective-permute-start | bytes 786440 | tf_op jit(solution)/shard_map/ppermute | solution.py:458
  106.1 13.5 %collective-permute-start.31 = (bf16[256,512]{1,0:T(8,128)(2,1)S(1)}, bf16[256,512]{1,0:T(8,128)(2,1)S(1)}, u32[]{:S(2)}, u32[]{:S(2)}) collective-permute-start(bf16[256,512]{1,0:T(8,128)(2,1)S(1)} %key_backward.1.refs_4_), channel_id=1, source_target_pairs={{0,4},{1,5},{2,6},{3,7},{4,0},{5,1},{6,2},{7,3},{8,12},{9,13},{10,... | collective-permute-start | bytes 786440 | tf_op jit(solution)/shard_map/ppermute | solution.py:458
  110.3 9.3 %collective-permute-start.21 = (bf16[256,512]{1,0:T(8,128)(2,1)S(1)}, bf16[256,512]{1,0:T(8,128)(2,1)S(1)}, u32[]{:S(2)}, u32[]{:S(2)}) collective-permute-start(bf16[256,512]{1,0:T(8,128)(2,1)S(1)} %key_backward.1.refs_4_), channel_id=1, source_target_pairs={{0,2},{1,3},{2,0},{3,1},{4,6},{5,7},{6,4},{7,5},{8,10},{9,11},{10,... | collective-permute-start | bytes 786440 | tf_op jit(solution)/shard_map/ppermute | solution.py:458
  111.4 29.0 %slice-start.5 = ((s8[6291456]{0:T(1024)(128)(4,1)}), s8[2097152]{0:T(1024)(128)(4,1)S(1)}, s32[]{:S(2)}) async-start(s8[6291456]{0:T(1024)(128)(4,1)} %bitcast.56), calls=%async_computation.5 | async-start | bytes 4194304
  115.0 5.2 %collective-permute-start.35 = (bf16[256,512]{1,0:T(8,128)(2,1)S(1)}, bf16[256,512]{1,0:T(8,128)(2,1)S(1)}, u32[]{:S(2)}, u32[]{:S(2)}) collective-permute-start(bf16[256,512]{1,0:T(8,128)(2,1)S(1)} %collective-permute-done.34.refs_6_), channel_id=1, source_target_pairs={{0,1},{1,0},{2,3},{3,2},{4,5},{5,4},{6,7},{7,6},{8,9},{9,8},{10,11... | collective-permute-start | bytes 786440 | tf_op jit(solution)/shard_map/ppermute | solution.py:458
  119.7 3.7 %collective-permute-start.30 = (bf16[256,512]{1,0:T(8,128)(2,1)S(1)}, bf16[256,512]{1,0:T(8,128)(2,1)S(1)}, u32[]{:S(2)}, u32[]{:S(2)}) collective-permute-start(bf16[256,512]{1,0:T(8,128)(2,1)S(1)} %collective-permute-done.21.refs_4_), channel_id=1, source_target_pairs={{0,1},{1,0},{2,3},{3,2},{4,5},{5,4},{6,7},{7,6},{8,9},{9,8},{10,11... | collective-permute-start | bytes 786440 | tf_op jit(solution)/shard_map/ppermute | solution.py:458
  119.7 3.7 %collective-permute-start.32 = (bf16[256,512]{1,0:T(8,128)(2,1)S(1)}, bf16[256,512]{1,0:T(8,128)(2,1)S(1)}, u32[]{:S(2)}, u32[]{:S(2)}) collective-permute-start(bf16[256,512]{1,0:T(8,128)(2,1)S(1)} %collective-permute-done.31.refs_6_), channel_id=1, source_target_pairs={{0,1},{1,0},{2,3},{3,2},{4,5},{5,4},{6,7},{7,6},{8,9},{9,8},{10,11... | collective-permute-start | bytes 786440 | tf_op jit(solution)/shard_map/ppermute | solution.py:458
  120.2 20.2 %slice-start = ((s8[6291456]{0:T(1024)(128)(4,1)}), s8[4194304]{0:T(1024)(128)(4,1)S(1)}, s32[]{:S(2)}) async-start(s8[6291456]{0:T(1024)(128)(4,1)} %bitcast.40), calls=%async_computation | async-start | bytes 8388608
  120.2 20.2 %slice-start.2 = ((s8[6291456]{0:T(1024)(128)(4,1)}), s8[4194304]{0:T(1024)(128)(4,1)S(1)}, s32[]{:S(2)}) async-start(s8[6291456]{0:T(1024)(128)(4,1)} %bitcast.48), calls=%async_computation.2 | async-start | bytes 8388608
  123.4 17.0 %slice-start.1 = ((s8[6291456]{0:T(1024)(128)(4,1)}), s8[2097152]{0:T(1024)(128)(4,1)S(1)}, s32[]{:S(2)}) async-start(s8[6291456]{0:T(1024)(128)(4,1)} %bitcast.40), calls=%async_computation.1 | async-start | bytes 4194304
  123.4 17.0 %slice-start.3 = ((s8[6291456]{0:T(1024)(128)(4,1)}), s8[2097152]{0:T(1024)(128)(4,1)S(1)}, s32[]{:S(2)}) async-start(s8[6291456]{0:T(1024)(128)(4,1)} %bitcast.48), calls=%async_computation.3 | async-start | bytes 4194304
  127.0 1.2 collective-permute-start.36
  128.3 4.5 %collective-permute-start.39 = (f32[8,128]{1,0:T(8,128)S(1)}, f32[8,128]{1,0:T(8,128)S(1)}, u32[]{:S(2)}, u32[]{:S(2)}) collective-permute-start(f32[8,128]{1,0:T(8,128)S(1)} %add.32.refs_0_), channel_id=1, source_target_pairs={{0,6},{1,7},{2,4},{3,5},{4,2},{5,3},{6,0},{7,1},{8,14},{9,15},{10,... | collective-permute-start | bytes 12296 | tf_op jit(solution)/shard_map/ppermute | solution.py:458
  129.7 3.6 %collective-permute-start.38 = (f32[8,128]{1,0:T(8,128)S(1)}, f32[8,128]{1,0:T(8,128)S(1)}, u32[]{:S(2)}, u32[]{:S(2)}) collective-permute-start(f32[8,128]{1,0:T(8,128)S(1)} %add.32.refs_0_), channel_id=1, source_target_pairs={{0,4},{1,5},{2,6},{3,7},{4,0},{5,1},{6,2},{7,3},{8,12},{9,13},{10,... | collective-permute-start | bytes 12296 | tf_op jit(solution)/shard_map/ppermute | solution.py:458
  130.7 3.6 %collective-permute-start.37 = (f32[8,128]{1,0:T(8,128)S(1)}, f32[8,128]{1,0:T(8,128)S(1)}, u32[]{:S(2)}, u32[]{:S(2)}) collective-permute-start(f32[8,128]{1,0:T(8,128)S(1)} %add.32.refs_0_), channel_id=1, source_target_pairs={{0,2},{1,3},{2,0},{3,1},{4,6},{5,7},{6,4},{7,5},{8,10},{9,11},{10,... | collective-permute-start | bytes 12296 | tf_op jit(solution)/shard_map/ppermute | solution.py:458
  135.9 10.5 %collective-permute-start.40 = (bf16[384,128]{1,0:T(8,128)(2,1)S(1)}, bf16[384,128]{1,0:T(8,128)(2,1)S(1)}, u32[]{:S(2)}, u32[]{:S(2)}) collective-permute-start(bf16[384,128]{1,0:T(8,128)(2,1)S(1)} %get-tuple-element.122), channel_id=1, source_target_pairs={{0,8},{8,0},{16,24},{24,16},{1,9},{9,1},{17,25},{25,17},{2,10},{10... | collective-permute-start | bytes 294920 | tf_op jit(solution)/shard_map/ppermute | solution.py:458
  137.8 9.3 %collective-permute-start.41 = (bf16[384,128]{1,0:T(8,128)(2,1)S(1)}, bf16[384,128]{1,0:T(8,128)(2,1)S(1)}, u32[]{:S(2)}, u32[]{:S(2)}) collective-permute-start(bf16[384,128]{1,0:T(8,128)(2,1)S(1)} %get-tuple-element.123), channel_id=1, source_target_pairs={{0,16},{8,24},{16,0},{24,8},{1,17},{9,25},{17,1},{25,9},{2,18},{10... | collective-permute-start | bytes 294920 | tf_op jit(solution)/shard_map/ppermute | solution.py:458
  138.8 8.3 %collective-permute-start.42 = (bf16[384,128]{1,0:T(8,128)(2,1)S(1)}, bf16[384,128]{1,0:T(8,128)(2,1)S(1)}, u32[]{:S(2)}, u32[]{:S(2)}) collective-permute-start(bf16[384,128]{1,0:T(8,128)(2,1)S(1)} %get-tuple-element.124), channel_id=1, source_target_pairs={{0,24},{8,16},{16,8},{24,0},{1,25},{9,17},{17,9},{25,1},{2,26},{10... | collective-permute-start | bytes 294920 | tf_op jit(solution)/shard_map/ppermute | solution.py:458
  147.1 10.4 %collective-permute-start.45 = (bf16[384,128]{1,0:T(8,128)(2,1)S(1)}, bf16[384,128]{1,0:T(8,128)(2,1)S(1)}, u32[]{:S(2)}, u32[]{:S(2)}) collective-permute-start(bf16[384,128]{1,0:T(8,128)(2,1)S(1)} %convert_element_type.24.refs_7_), channel_id=1, source_target_pairs={{0,24},{8,16},{16,8},{24,0},{1,25},{9,17},{17,9},{25,1},{2,26},{10... | collective-permute-start | bytes 294920 | tf_op jit(solution)/shard_map/ppermute | solution.py:458
  149.0 8.6 %collective-permute-start.44 = (bf16[384,128]{1,0:T(8,128)(2,1)S(1)}, bf16[384,128]{1,0:T(8,128)(2,1)S(1)}, u32[]{:S(2)}, u32[]{:S(2)}) collective-permute-start(bf16[384,128]{1,0:T(8,128)(2,1)S(1)} %convert_element_type.24.refs_7_), channel_id=1, source_target_pairs={{0,16},{8,24},{16,0},{24,8},{1,17},{9,25},{17,1},{25,9},{2,18},{10... | collective-permute-start | bytes 294920 | tf_op jit(solution)/shard_map/ppermute | solution.py:458
  150.3 7.3 %collective-permute-start.43 = (bf16[384,128]{1,0:T(8,128)(2,1)S(1)}, bf16[384,128]{1,0:T(8,128)(2,1)S(1)}, u32[]{:S(2)}, u32[]{:S(2)}) collective-permute-start(bf16[384,128]{1,0:T(8,128)(2,1)S(1)} %convert_element_type.24.refs_7_), channel_id=1, source_target_pairs={{0,8},{8,0},{16,24},{24,16},{1,9},{9,1},{17,25},{25,17},{2,10},{10... | collective-permute-start | bytes 294920 | tf_op jit(solution)/shard_map/ppermute | solution.py:458
